TPU v7x, 32 devices: a whole 2x2x4 slice. The times are simulated.
32 devices in a mesh: groups: 2 (over y), row: 4 (over z), col: 4 (over x, core).
Axes of the slice: x: 2, y: 2, z: 4, core: 2. Of those that a mesh axis runs over, the one named last changes fastest.
Arguments:
- initial_rates: float32 [64, 4608], P('groups', ('row', 'col')), parts along dimension 0, may hold values from -3 to 3
- stimuli: bfloat16 [3, 64, 512], P(None, 'groups'), parts along dimension 1, may hold values from -6 to 6
- cotangent: float32 [3, 64, 4608], P(None, 'groups', ('row', 'col')), parts along dimension 1, may hold values from -0.6 to 0.6
- weight_blocks: bfloat16 [4, 4, 64, 128, 128], P('row', 'col'), may hold values from -0.09375 to 0.09375
- slot_owner: int32 [4, 4, 64], P('row', 'col'), may hold values from 0 to 1
- slot_post: int32 [4, 4, 64], P('row', 'col'), may hold values from 0 to 8
- slot_pre: int32 [4, 4, 64], P('row', 'col'), may hold values from 0 to 8
- cell_type: int32 [4608], P(('row', 'col')), may hold values from 0 to 8191
- type_gain: float32 [8192], replicated, may hold values from 0.5 to 2
- input_map: int32 [4608], P(('row', 'col')), may hold values from 0 to 512
Outputs:
- final_rates: float32 [64, 4608], P('groups', ('row', 'col')), parts along dimension 0
- weight_grads: bfloat16 [4, 4, 128, 128, 128], P('row', 'col', 'groups'), parts along dimension 2
- gain_grads: float32 [16384], P('groups'), parts along dimension 0
There are 2 independent parts, one for each index of `groups`. A program takes and returns all parts, laid end to end along the dimension named above; an argument that names none is the same for every part. Nothing has to cross between parts.
Inputs may be any that keep to these rules, and one draw needn't show every extreme that they name: `slot_owner`: 1: the block belongs to the tile whose row index differs by 2; 0: to the device's own tile. `input_map`: 512 marks a neuron without input.
All inputs are finite; a program needn't handle non-finite values.
Results may differ from a plain program's by a relative error of at most 0.006.
Values may be sent and summed in bfloat16 or wider, within the bound.
No kernel may reach another device: no remote copies, remote signals or barrier semaphores. Data moves between devices by JAX's collectives and lax.ppermute only.
A program may use at most 64 MiB of HBM per device.

v0:
```python
import jax
import jax.numpy as jnp
from jax import lax
from jax.sharding import PartitionSpec as P

BLOCK = 128


def from_partner(block, axis, distance):
    count = lax.axis_size(axis)
    route = []
    for low in range(count):
        high = low | 1 << distance
        if high != low and high < count:
            route += [(low, high), (high, low)]
    return lax.ppermute(block, axis, route)


def shards(
    initial_rates,
    stimuli,
    cotangent,
    weight_blocks,
    slot_owner,
    slot_post,
    slot_pre,
    cell_type,
    type_gain,
    input_map,
):
    row_count = lax.axis_size("row")
    col_count = lax.axis_size("col")
    batch_size = initial_rates.shape[0]
    local_rows = initial_rates.shape[1]
    step_count = cotangent.shape[0]
    slot_count = weight_blocks.shape[2]
    post_count = col_count * local_rows // BLOCK
    pre_count = row_count * local_rows // BLOCK
    half_bit = row_count.bit_length() - 2
    weights = weight_blocks.reshape(slot_count, BLOCK, BLOCK)
    owner_ids = slot_owner.reshape(slot_count)
    post_ids = slot_post.reshape(slot_count)
    pre_ids = slot_pre.reshape(slot_count)
    neuron_gain = jnp.take(type_gain, cell_type)
    channel_count = stimuli.shape[2]
    selector = (input_map[:, None] == jnp.arange(channel_count, dtype=jnp.int32)[None, :]).astype(
        jnp.bfloat16
    )
    drive_all = jnp.einsum("tbc,nc->tbn", stimuli, selector, preferred_element_type=jnp.float32)
    both_ids = owner_ids * post_count + post_ids
    state_rates = initial_rates
    gathered_list, lowered_list, current_list, activity_list = ([], [], [], [])
    for time_index in range(step_count):
        lowered = state_rates.astype(jnp.bfloat16)
        gathered = lax.all_gather(lowered, "row", axis=1, tiled=True)
        picked = gathered.reshape(batch_size, pre_count, BLOCK)[:, pre_ids]
        product = jnp.einsum("kij,bkj->bki", weights, picked, preferred_element_type=jnp.float32)
        paired = (
            jnp.zeros((batch_size, 2 * post_count, BLOCK), jnp.float32).at[:, both_ids].add(product)
        )
        own_part = paired[:, :post_count].reshape(batch_size, post_count * BLOCK)
        help_part = paired[:, post_count:].reshape(batch_size, post_count * BLOCK)
        returned = from_partner(help_part, "row", half_bit)
        current = lax.psum_scatter(own_part + returned, "col", scatter_dimension=1, tiled=True)
        current = current + drive_all[time_index]
        activity = jnp.tanh(neuron_gain[None, :] * current)
        state_rates = 0.5 * state_rates + 0.5 * activity
        gathered_list.append(gathered)
        lowered_list.append(lowered)
        current_list.append(current)
        activity_list.append(activity)
    adjoint = cotangent[step_count - 1]
    gain_sums = jnp.zeros((local_rows,), jnp.float32)
    grads = jnp.zeros((slot_count, BLOCK, BLOCK), jnp.float32)
    for time_index in reversed(range(step_count)):
        activity = activity_list[time_index]
        pressure = adjoint * 0.5 * (1.0 - activity * activity)
        delta = (pressure * neuron_gain[None, :]).astype(jnp.bfloat16)
        gain_sums = gain_sums + jnp.sum(pressure * current_list[time_index], axis=0)
        own_post = lax.all_gather(delta, "col", axis=1, tiled=True)
        help_post = from_partner(own_post, "row", half_bit)
        joined = jnp.concatenate([own_post, help_post], axis=1).reshape(
            batch_size, 2 * post_count, BLOCK
        )
        selected = joined[:, both_ids]
        gathered = lax.all_gather(lowered_list[time_index], "row", axis=1, tiled=True)
        presyn = gathered.reshape(batch_size, pre_count, BLOCK)[:, pre_ids]
        grads = grads + jnp.einsum(
            "bki,bkj->kij", selected, presyn, preferred_element_type=jnp.float32
        )
        if time_index > 0:
            backward = jnp.einsum(
                "kij,bki->bkj", weights, selected, preferred_element_type=jnp.float32
            )
            partial_sums = (
                jnp.zeros((batch_size, pre_count, BLOCK), jnp.float32).at[:, pre_ids].add(backward)
            )
            partial_sums = partial_sums.reshape(batch_size, pre_count * BLOCK)
            adjoint = (
                cotangent[time_index - 1]
                + 0.5 * adjoint
                + lax.psum_scatter(partial_sums, "row", scatter_dimension=1, tiled=True)
            )
    type_part = jax.ops.segment_sum(gain_sums, cell_type, num_segments=type_gain.shape[0])
    gain_grads = lax.psum(type_part, ("row", "col"))
    weight_grads = grads.astype(jnp.bfloat16).reshape(1, 1, slot_count, BLOCK, BLOCK)
    return (state_rates, weight_grads, gain_grads)


def solution(mesh):
    in_specs = (
        P("groups", ("row", "col")),
        P(None, "groups", None),
        P(None, "groups", ("row", "col")),
        P("row", "col", None, None, None),
        P("row", "col", None),
        P("row", "col", None),
        P("row", "col", None),
        P(("row", "col")),
        P(),
        P(("row", "col")),
    )
    out_specs = (P("groups", ("row", "col")), P("row", "col", "groups", None, None), P("groups"))
    return jax.shard_map(shards, mesh=mesh, in_specs=in_specs, out_specs=out_specs, check_vma=False)
```

profile of v0, /device:TPU:0, one launch (start us, length us, event | category | flops | bytes accessed | tf_op | source)
XLA Modules:
  0.0 357.3 jit_solution(5724663238656714592)
XLA Ops:
  7.2 0.9 convert_bitcast_fusion.1
  8.2 15.0 %all-gather = bf16[4,288,32]{1,2,0:T(8,128)(2,1)S(1)} all-gather(bf16[1,288,32]{1,2,0:T(8,128)(2,1)S(1)} %convert_bitcast_fusion.1), channel_id=1, replica_groups=mesh['groups'=2,'row'=4,'col'=4] {'row'}, dimensions={0}, use_global_device_ids=true | all-gather | bytes 92160 | tf_op jit(solution)/shard_map/all_gather | solution.py:55
  23.4 0.7 fusion.43
  24.1 0.7 fusion.42
  24.8 0.7 gather_fusion.1
  25.4 2.2 fusion.8
  27.6 6.1 %scatter_fusion = f32[32,18,128]{2,0,1:T(8,128)S(1)} fusion(f32[32,18,128]{2,0,1:T(8,128)S(1)} %broadcast.71.clone.1, s32[64]{0:T(128)S(1)} %fusion.42, f32[64,32,128]{2,1,0:T(8,128)} %fusion.8), kind=kCustom, calls=%fused_computation.7 | custom fusion | flops 262144 | bytes 3145984 | tf_op jit(solution)/shard_map/scatter-add | solution.py:59
  33.9 0.7 collective-permute-start
  34.6 2.2 gather_fusion
  36.8 4.8 %collective-permute-done = f32[32,1152]{1,0:T(8,128)S(1)} collective-permute-done((f32[32,1152]{1,0:T(8,128)S(1)}, f32[32,1152]{1,0:T(8,128)S(1)}, u32[]{:S(2)}, u32[]{:S(2)}) %collective-permute-start) | collective-permute-done | bytes 147488 | tf_op jit(solution)/shard_map/ppermute | solution.py:16
  41.6 1.1 copy.75
  43.1 21.3 %reduce-scatter.16.cloned.1.call-done = f32[288,32]{1,0:T(8,128)} async-done(((f32[1152,32]{1,0:T(8,128)}), f32[288,32]{1,0:T(8,128)}) %reduce-scatter.16.cloned.1.call-update) | async-done | bytes 36880
  64.4 1.0 copy.76
  65.4 13.4 %all-gather.1 = bf16[4,288,32]{1,2,0:T(8,128)(2,1)S(1)} all-gather(bf16[1,288,32]{1,2,0:T(8,128)(2,1)S(1)} %get-tuple-element.10), channel_id=1, replica_groups=mesh['groups'=2,'row'=4,'col'=4] {'row'}, dimensions={0}, use_global_device_ids=true | all-gather | bytes 92160 | tf_op jit(solution)/shard_map/all_gather | solution.py:55
  79.0 0.7 gather_fusion.2
  79.7 2.2 fusion.6
  81.9 6.1 %scatter_fusion.1 = f32[32,18,128]{2,0,1:T(8,128)S(1)} fusion(f32[32,18,128]{2,0,1:T(8,128)S(1)} %broadcast.71.clone, s32[64]{0:T(128)S(1)} %fusion.42, f32[64,32,128]{2,1,0:T(8,128)} %fusion.6), kind=kCustom, calls=%fused_computation.8 | custom fusion | flops 262144 | bytes 3145984 | tf_op jit(solution)/shard_map/scatter-add | solution.py:59
  88.1 0.7 collective-permute-start.1
  88.8 7.0 %collective-permute-done.1 = f32[32,1152]{1,0:T(8,128)S(1)} collective-permute-done((f32[32,1152]{1,0:T(8,128)S(1)}, f32[32,1152]{1,0:T(8,128)S(1)}, u32[]{:S(2)}, u32[]{:S(2)}) %collective-permute-start.1) | collective-permute-done | bytes 147488 | tf_op jit(solution)/shard_map/ppermute | solution.py:16
  95.8 1.1 copy.77
  97.0 20.6 %reduce-scatter.18.cloned.1.call-done = f32[288,32]{1,0:T(8,128)} async-done(((f32[1152,32]{1,0:T(8,128)}), f32[288,32]{1,0:T(8,128)}) %reduce-scatter.18.cloned.1.call-update) | async-done | bytes 36880
  117.6 1.0 copy.78
  118.6 1.5 convert_bitcast_fusion
  120.1 13.4 %all-gather.2 = bf16[4,288,32]{1,2,0:T(8,128)(2,1)S(1)} all-gather(bf16[1,288,32]{1,2,0:T(8,128)(2,1)S(1)} %get-tuple-element.8), channel_id=1, replica_groups=mesh['groups'=2,'row'=4,'col'=4] {'row'}, dimensions={0}, use_global_device_ids=true | all-gather | bytes 92160 | tf_op jit(solution)/shard_map/all_gather | solution.py:55
  133.6 1.4 gather_fusion.3
  135.1 3.2 fusion.4
  138.3 6.1 %scatter_fusion.2 = f32[32,18,128]{2,0,1:T(8,128)S(1)} fusion(f32[32,18,128]{2,0,1:T(8,128)S(1)} %broadcast.71, s32[64]{0:T(128)S(1)} %fusion.42, f32[64,32,128]{2,1,0:T(8,128)} %fusion.4), kind=kCustom, calls=%fused_computation.9 | custom fusion | flops 262144 | bytes 3145984 | tf_op jit(solution)/shard_map/scatter-add | solution.py:59
  145.2 7.0 %collective-permute-done.2 = f32[32,1152]{1,0:T(8,128)S(1)} collective-permute-done((f32[32,1152]{1,0:T(8,128)S(1)}, f32[32,1152]{1,0:T(8,128)S(1)}, u32[]{:S(2)}, u32[]{:S(2)}) %collective-permute-start.2) | collective-permute-done | bytes 147488 | tf_op jit(solution)/shard_map/ppermute | solution.py:16
  152.2 1.1 copy.79
  153.4 20.6 %reduce-scatter.20.cloned.1.call-done = f32[288,32]{1,0:T(8,128)} async-done(((f32[1152,32]{1,0:T(8,128)}), f32[288,32]{1,0:T(8,128)}) %reduce-scatter.20.cloned.1.call-update) | async-done | bytes 36880
  173.9 1.0 copy.80
  175.0 0.8 fusion.37
  175.8 5.3 %all-gather.3 = bf16[4,288,32]{1,2,0:T(8,128)(2,1)S(1)} all-gather(bf16[1,288,32]{1,2,0:T(8,128)(2,1)S(1)} %fusion.37), channel_id=1, replica_groups=mesh['groups'=2,'row'=4,'col'=4] {'col'}, dimensions={0}, use_global_device_ids=true | all-gather | bytes 92160 | tf_op jit(solution)/shard_map/all_gather | solution.py:80
  181.1 0.7 copy.67
  181.8 1.0 reshape.264
  182.9 2.5 collective-permute-start.3
  185.4 4.6 %collective-permute-done.3 = bf16[32,1152]{1,0:T(8,128)(2,1)S(1)} collective-permute-done((bf16[32,1152]{1,0:T(8,128)(2,1)S(1)}, bf16[32,1152]{1,0:T(8,128)(2,1)S(1)}, u32[]{:S(2)}, u32[]{:S(2)}) %collective-permute-start.3) | collective-permute-done | bytes 73760 | tf_op jit(solution)/shard_map/ppermute | solution.py:16
  189.9 0.9 copy_bitcast_fusion.5
  190.8 1.4 gather_fusion.4
  192.3 2.7 fusion.2
  195.0 6.2 %scatter_fusion.3 = f32[32,9,128]{2,0,1:T(8,128)S(1)} fusion(f32[32,9,128]{2,0,1:T(8,128)S(1)} %broadcast.79.clone, s32[64]{0:T(128)S(1)} %copy-done.13, f32[64,32,128]{2,1,0:T(8,128)} %fusion.2), kind=kCustom, calls=%fused_computation.10 | custom fusion | flops 262144 | bytes 3145984 | tf_op jit(solution)/shard_map/scatter-add | solution.py:96
  201.2 1.1 copy.85
  202.3 22.1 %reduce-scatter.22.cloned.1.call-done = f32[288,32]{1,0:T(8,128)} async-done(((f32[1152,32]{1,0:T(8,128)}), f32[288,32]{1,0:T(8,128)}) %reduce-scatter.22.cloned.1.call-update) | async-done | bytes 36880
  224.4 1.0 copy.82
  225.4 1.5 fusion.38
  226.9 5.5 %all-gather.4 = bf16[4,288,32]{1,2,0:T(8,128)(2,1)S(1)} all-gather(bf16[1,288,32]{1,2,0:T(8,128)(2,1)S(1)} %get-tuple-element.6), channel_id=1, replica_groups=mesh['groups'=2,'row'=4,'col'=4] {'col'}, dimensions={0}, use_global_device_ids=true | all-gather | bytes 92160 | tf_op jit(solution)/shard_map/all_gather | solution.py:80
  232.4 0.8 reshape.266
  233.2 0.8 collective-permute-start.4
  233.9 3.9 %fusion.17 = f32[64,128,128]{2,1,0:T(8,128)} fusion(bf16[64,32,128]{2,1,0:T(8,128)(2,1)} %gather_fusion.4, bf16[64,32,128]{2,1,0:T(8,128)(2,1)} %gather_fusion.3), kind=kOutput, calls=%fused_computation.32 | convolution fusion | flops 67108864 | bytes 5242880 | tf_op jit(solution)/shard_map/bki,bkj->kij/dot_general | solution.py:88
  237.8 1.0 collective-permute-done.4
  238.8 1.5 gather_fusion.5
  240.3 2.7 fusion
  243.0 6.2 %scatter_fusion.4 = f32[32,9,128]{2,0,1:T(8,128)S(1)} fusion(f32[32,9,128]{2,0,1:T(8,128)S(1)} %broadcast.79, s32[64]{0:T(128)S(1)} %copy-done.13, f32[64,32,128]{2,1,0:T(8,128)} %fusion), kind=kCustom, calls=%fused_computation.11 | custom fusion | flops 262144 | bytes 3145984 | tf_op jit(solution)/shard_map/scatter-add | solution.py:96
  249.2 1.1 copy.86
  250.3 3.8 %fusion.14 = f32[64,128,128]{2,1,0:T(8,128)} fusion(bf16[64,32,128]{2,1,0:T(8,128)(2,1)} %gather_fusion.5, bf16[64,32,128]{2,1,0:T(8,128)(2,1)S(1)} %gather_fusion.2), kind=kOutput, calls=%fused_computation.29 | convolution fusion | flops 67108864 | bytes 5242880 | tf_op jit(solution)/shard_map/bki,bkj->kij/dot_general | solution.py:88
  254.1 18.3 %reduce-scatter.24.cloned.1.call-done = f32[288,32]{1,0:T(8,128)} async-done(((f32[1152,32]{1,0:T(8,128)}), f32[288,32]{1,0:T(8,128)}) %reduce-scatter.24.cloned.1.call-update) | async-done | bytes 36880
  272.3 1.0 copy.84
  273.4 1.5 multiply_reduce_fusion.1
  274.9 5.3 %all-gather.5 = bf16[4,288,32]{1,2,0:T(8,128)(2,1)S(1)} all-gather(bf16[1,288,32]{1,2,0:T(8,128)(2,1)S(1)} %get-tuple-element.12), channel_id=1, replica_groups=mesh['groups'=2,'row'=4,'col'=4] {'col'}, dimensions={0}, use_global_device_ids=true | all-gather | bytes 92160 | tf_op jit(solution)/shard_map/all_gather | solution.py:80
  280.4 0.8 collective-permute-start.5
  281.2 3.3 scatter_custom_fusion.5
  284.5 58.9 %psum.7 = f32[8192]{0:T(1024)} all-reduce(f32[8192]{0:T(1024)S(1)} %scatter_custom_fusion.5), channel_id=1, replica_groups=mesh['groups'=2,'row'=4,'col'=4] {'row','col'}, use_global_device_ids=true, to_apply=%region_14.15 | all-reduce | flops 8192 | bytes 65536 | tf_op jit(solution)/shard_map/psum | solution.py:105
  343.5 1.5 gather_fusion.6
  345.0 5.8 %fusion.10 = bf16[1,1,64,128,128]{4,3,2,1,0:T(8,128)(2,1)} fusion(f32[64,128,128]{2,1,0:T(8,128)} %fusion.17, f32[64,128,128]{2,1,0:T(8,128)} %fusion.14, bf16[64,32,128]{2,1,0:T(8,128)(2,1)} %gather_fusion.6, bf16[64,32,128]{2,1,0:T(8,128)(2,1)S(1)} %gather_fusion.1), kind=kOutput, calls=%fused_computation.24 | convolution fusion | flops 70254592 | bytes 11534336 | tf_op jit(solution)/shard_map/bki,bkj->kij/dot_general | solution.py:88
  (80 shorter events, 2.5 us)
Async XLA Ops:
  7.2 18.3 %copy-start = (bf16[1,1,64,128,128]{4,3,2,1,0:T(8,128)(2,1)S(1)}, bf16[1,1,64,128,128]{4,3,2,1,0:T(8,128)(2,1)}, u32[]{:S(2)}) copy-start(bf16[1,1,64,128,128]{4,3,2,1,0:T(8,128)(2,1)} %param.13) | copy-start | bytes 6291460
  7.2 57.2 %reduce-scatter.16.cloned.1.call-start = ((), (), s32[]{:S(2)}) async-start(), calls=%async_computation.5 | async-start | bytes 737280
  24.1 1.4 copy-start.12
  27.6 6.9 %copy-start.11 = (s32[288]{0:T(512)S(1)}, s32[288]{0:T(512)}, u32[]{:S(2)}) copy-start(s32[288]{0:T(512)} %param.17) | copy-start | bytes 3460
  27.6 6.9 %copy-start.1 = (f32[8192]{0:T(1024)S(1)}, f32[8192]{0:T(1024)}, u32[]{:S(2)}) copy-start(f32[8192]{0:T(1024)} %param.18) | copy-start | bytes 98308
  33.8 8.9 %copy-start.14 = (bf16[3,32,512]{2,1,0:T(8,128)(2,1)S(1)}, bf16[3,32,512]{2,1,0:T(8,128)(2,1)}, u32[]{:S(2)}) copy-start(bf16[3,32,512]{2,1,0:T(8,128)(2,1)} %param.11) | copy-start | bytes 294916
  33.8 8.9 %copy-start.15 = (s32[288]{0:T(512)S(1)}, s32[288]{0:T(512)}, u32[]{:S(2)}) copy-start(s32[288]{0:T(512)} %param.19) | copy-start | bytes 3460
  33.9 7.7 %collective-permute-start = (f32[32,1152]{1,0:T(8,128)S(1)}, f32[32,1152]{1,0:T(8,128)S(1)}, u32[]{:S(2)}, u32[]{:S(2)}) collective-permute-start(f32[32,1152]{1,0:T(8,128)S(1)} %bitcast.239), channel_id=1, source_target_pairs={{0,8},{8,0},{4,12},{12,4},{1,9},{9,1},{5,13},{13,5},{2,10},{10,2},... | collective-permute-start | bytes 442376 | tf_op jit(solution)/shard_map/ppermute | solution.py:16
  34.5 30.8 %copy-start.6 = (f32[32,288]{1,0:T(8,128)S(1)}, f32[32,288]{1,0:T(8,128)}, u32[]{:S(2)}) copy-start(f32[32,288]{1,0:T(8,128)} %param.10) | copy-start | bytes 110596
  42.7 74.9 %reduce-scatter.18.cloned.1.call-start = ((), (), s32[]{:S(2)}) async-start(), calls=%async_computation.6 | async-start | bytes 737280
  43.1 35.9 %copy-start.2 = (f32[3,32,288]{2,1,0:T(8,128)}, f32[3,32,288]{2,1,0:T(8,128)S(1)}, u32[]{:S(2)}) copy-start(f32[3,32,288]{2,1,0:T(8,128)S(1)} %convolution_bitcast_fusion) | copy-start | bytes 331780
  88.1 30.5 %copy-start.7 = (f32[32,288]{1,0:T(8,128)S(1)}, f32[32,288]{1,0:T(8,128)}, u32[]{:S(2)}) copy-start(f32[32,288]{1,0:T(8,128)} %param.10) | copy-start | bytes 110596
  88.1 7.7 %collective-permute-start.1 = (f32[32,1152]{1,0:T(8,128)S(1)}, f32[32,1152]{1,0:T(8,128)S(1)}, u32[]{:S(2)}, u32[]{:S(2)}) collective-permute-start(f32[32,1152]{1,0:T(8,128)S(1)} %bitcast.240), channel_id=1, source_target_pairs={{0,8},{8,0},{4,12},{12,4},{1,9},{9,1},{5,13},{13,5},{2,10},{10,2},... | collective-permute-start | bytes 442376 | tf_op jit(solution)/shard_map/ppermute | solution.py:16
  96.9 77.0 %reduce-scatter.20.cloned.1.call-start = ((), (), s32[]{:S(2)}) async-start(), calls=%async_computation.7 | async-start | bytes 737280
  144.5 30.5 %copy-start.3 = (f32[3,32,288]{2,1,0:T(8,128)S(1)}, f32[3,32,288]{2,1,0:T(8,128)}, u32[]{:S(2)}) copy-start(f32[3,32,288]{2,1,0:T(8,128)} %copy-done.2) | copy-start | bytes 331780
  144.5 7.7 %collective-permute-start.2 = (f32[32,1152]{1,0:T(8,128)S(1)}, f32[32,1152]{1,0:T(8,128)S(1)}, u32[]{:S(2)}, u32[]{:S(2)}) collective-permute-start(f32[32,1152]{1,0:T(8,128)S(1)} %bitcast.241), channel_id=1, source_target_pairs={{0,8},{8,0},{4,12},{12,4},{1,9},{9,1},{5,13},{13,5},{2,10},{10,2},... | collective-permute-start | bytes 442376 | tf_op jit(solution)/shard_map/ppermute | solution.py:16
  153.3 71.1 %reduce-scatter.22.cloned.1.call-start = ((), (), s32[]{:S(2)}) async-start(), calls=%async_computation.8 | async-start | bytes 737280
  174.9 10.4 %copy-start.4 = (f32[32,288]{1,0:T(8,128)}, f32[32,288]{1,0:T(8,128)S(1)}, u32[]{:S(2)}) copy-start(f32[32,288]{1,0:T(8,128)S(1)} %copy.80) | copy-start | bytes 110596
  182.9 2.5 copy-start.9
  182.9 7.1 %collective-permute-start.3 = (bf16[32,1152]{1,0:T(8,128)(2,1)S(1)}, bf16[32,1152]{1,0:T(8,128)(2,1)S(1)}, u32[]{:S(2)}, u32[]{:S(2)}) collective-permute-start(bf16[32,1152]{1,0:T(8,128)(2,1)S(1)} %bitcast.232), channel_id=1, source_target_pairs={{0,8},{8,0},{4,12},{12,4},{1,9},{9,1},{5,13},{13,5},{2,10},{10,2},... | collective-permute-start | bytes 221192 | tf_op jit(solution)/shard_map/ppermute | solution.py:16
  192.3 2.7 copy-start.13
  202.3 70.1 %reduce-scatter.24.cloned.1.call-start = ((), (), s32[]{:S(2)}) async-start(), calls=%async_computation.9 | async-start | bytes 737280
  233.2 5.6 %copy-start.8 = (bf16[1152,32]{0,1:T(8,128)(2,1)S(1)}, bf16[1152,32]{0,1:T(8,128)(2,1)}, u32[]{:S(2)}) copy-start(bf16[1152,32]{0,1:T(8,128)(2,1)} %reshape.266) | copy-start | bytes 221188
  233.2 5.6 %collective-permute-start.4 = (bf16[32,1152]{1,0:T(8,128)(2,1)}, bf16[32,1152]{1,0:T(8,128)(2,1)S(1)}, u32[]{:S(2)}, u32[]{:S(2)}) collective-permute-start(bf16[32,1152]{1,0:T(8,128)(2,1)} %bitcast.230), channel_id=1, source_target_pairs={{0,8},{8,0},{4,12},{12,4},{1,9},{9,1},{5,13},{13,5},{2,10},{10,2},... | collective-permute-start | bytes 221192 | tf_op jit(solution)/shard_map/ppermute | solution.py:16
  250.3 23.1 %copy-start.5 = (f32[32,288]{1,0:T(8,128)S(1)}, f32[32,288]{1,0:T(8,128)}, u32[]{:S(2)}) copy-start(f32[32,288]{1,0:T(8,128)} %copy-done.4) | copy-start | bytes 110596
  250.3 23.1 %copy-start.10 = (f32[32,288]{1,0:T(8,128)S(1)}, f32[32,288]{1,0:T(8,128)}, u32[]{:S(2)}) copy-start(f32[32,288]{1,0:T(8,128)} %get-tuple-element.7) | copy-start | bytes 110596
  280.4 63.1 %collective-permute-start.5 = (bf16[32,1152]{1,0:T(8,128)(2,1)S(1)}, bf16[32,1152]{1,0:T(8,128)(2,1)S(1)}, u32[]{:S(2)}, u32[]{:S(2)}) collective-permute-start(bf16[32,1152]{1,0:T(8,128)(2,1)S(1)} %bitcast.228), channel_id=1, source_target_pairs={{0,8},{8,0},{4,12},{12,4},{1,9},{9,1},{5,13},{13,5},{2,10},{10,2},... | collective-permute-start | bytes 221192 | tf_op jit(solution)/shard_map/ppermute | solution.py:16
Sparse Core Ops, SparseCore 0:
  42.8 21.5 reduce-scatter.15
  97.0 20.5 reduce-scatter.17
  153.4 20.4 reduce-scatter.19
  202.4 21.9 reduce-scatter.21
  250.4 21.9 reduce-scatter.23
where the time goes:
time: 359 us; the launch traced here: 357 us
  waiting for transfers between devices  127 us (35%)
  blocking collectives  117 us (33%)
  other arithmetic  42.8 us (12%)
  matrix products  26.8 us (7%)
  local copies, waits for them, and re-layouts  23.2 us (6%)
  between operations  14.2 us (4%)
  starting transfers between devices  6.23 us (2%)
    unnamed x10, waiting for transfers between devices  103 us
    psum x1, blocking collectives, shards(): gain_grads = lax.psum(type_part, ('row', 'col'))  58.9 us
    all_gather x3, blocking collectives, shards(): gathered = lax.all_gather(lowered, 'row', axis=1, tiled=True)  41.8 us
    ppermute x6, waiting for transfers between devices, from_partner(): return lax.ppermute(block, axis, route)  24.4 us
    scatter-add x3, other arithmetic, shards(): jnp.zeros((batch_size, 2 * post_count, BLOCK), jnp.float32).at[:, both_ids]  18.4 us
    all_gather x3, blocking collectives, shards(): own_post = lax.all_gather(delta, 'col', axis=1, tiled=True)  16.2 us
    dot_general x3, matrix products, shards(): jnp.einsum('bki,bkj->kij', selected, presyn, preferred_element_type=jnp.f...  13.5 us
    unnamed x51, local copies, waits for them, and re-layouts  12.7 us
  transfers between devices with their start and end apart: 11, of which 10 were waited for; matrix products, arithmetic and copies ran while one was open for 4% of the time, Pallas kernels for 0%

commit v1 on v0

v1 whole, which is shorter than its diff:
```python
import functools

import jax
import jax.numpy as jnp
from jax import lax
from jax.experimental import pallas as pl
from jax.experimental.pallas import tpu as pltpu
from jax.sharding import PartitionSpec as P

BLOCK = 128
EXTRA = 16
F32 = jnp.float32
BF16 = jnp.bfloat16
VMEM = pl.BlockSpec(memory_space=pltpu.VMEM)
SMEM = pl.BlockSpec(memory_space=pltpu.SMEM)


class Sizes:
    def __init__(self, row_count, col_count, batch, local, slots, types, channels, steps):
        self.rows, self.cols = row_count, col_count
        self.batch, self.local, self.slots = batch, local, slots
        self.types, self.channels, self.steps = types, channels, steps
        self.post = col_count * local // BLOCK
        self.pre = row_count * local // BLOCK
        self.half = row_count // 2
        offsets = [local * i % BLOCK for i in range(max(row_count, col_count))]
        self.frame = (max(offsets) + local + BLOCK - 1) // BLOCK
        self.wide = self.frame * BLOCK

    def first(self, i):
        return lax.div(i * self.local, jnp.int32(BLOCK))

    def offset(self, i):
        return lax.rem(i * self.local, jnp.int32(BLOCK))


def call(body, outs, scratch, ins, smem=(), flops=0):
    specs = [SMEM if i in smem else VMEM for i in range(len(ins))]
    moved = sum(x.size * x.dtype.itemsize for x in ins) + sum(x.size * x.dtype.itemsize for x in outs)
    return pl.pallas_call(
        body,
        out_shape=outs,
        in_specs=specs,
        out_specs=[VMEM] * len(outs),
        scratch_shapes=scratch,
        cost_estimate=pl.CostEstimate(flops=flops, bytes_accessed=moved, transcendentals=0),
        compiler_params=pltpu.CompilerParams(vmem_limit_bytes=32 * 1024 * 1024),
    )(*ins)


def shape(dims, kind=F32):
    return jax.ShapeDtypeStruct(tuple(dims), kind)


def flip(x, axis, k):
    count = lax.axis_size(axis)
    return lax.ppermute(x, axis, [(i, i ^ k) for i in range(count)])


def few(count):
    return count <= 4


def share(x, axis):
    count = lax.axis_size(axis)
    if few(count):
        return [x] + [flip(x, axis, k) for k in range(1, count)]
    return [lax.all_gather(x, axis)]


def exchange(parts, axis):
    count = lax.axis_size(axis)
    if few(count):
        return [parts[0]] + [flip(parts[k], axis, k) for k in range(1, count)]
    return [lax.all_to_all(parts[0], axis, 0, 0, tiled=True)]


def parcel(count, dims, kind):
    if few(count):
        return [shape(dims, kind)] * count
    return [shape((count, *dims), kind)]


def slot_of(refs, count, me, k):
    return refs[k] if few(count) else refs[0].at[me ^ k]


def loop(count, body):
    lax.fori_loop(0, count, lambda i, c: (body(i), c)[1], 0, unroll=count <= 8)


def rotated(blocks, amount, z):
    whole = jnp.concatenate(blocks, axis=1)
    return pltpu.roll(whole, lax.rem(amount + z.wide, jnp.int32(z.wide)), 1)


def cut(whole, z):
    return [whole[:, i * BLOCK : (i + 1) * BLOCK] for i in range(z.frame)]


def pack_kernel(z, meta, rates, types, inputs, cots, message, own, cot_frames, pad):
    p = meta[2 * z.slots]
    offset = z.offset(p)
    pad[...] = jnp.zeros_like(pad)
    n = z.batch
    pad[0:n, 0 : z.local] = rates[...]
    t, m = types[...], inputs[...]
    pad[n : n + 1, 0 : z.local] = (lax.shift_right_logical(t, 7) + 1).astype(F32)
    pad[n + 1 : n + 2, 0 : z.local] = (t & 127).astype(F32)
    pad[n + 2 : n + 3, 0 : z.local] = (lax.shift_right_logical(m, 7) + 1).astype(F32)
    pad[n + 3 : n + 4, 0 : z.local] = (m & 127).astype(F32)
    moved = pltpu.roll(pad[...], offset, 1)
    for f, block in enumerate(cut(moved, z)):
        message[f] = block.astype(BF16)
        own[f] = block[0:n]
    pad[...] = jnp.zeros_like(pad)
    for t in range(z.steps):
        pad[0:n, 0 : z.local] = cots[t]
        moved = pltpu.roll(pad[...], offset, 1)
        for f, block in enumerate(cut(moved, z)):
            cot_frames[t, f] = block[0:n]


def prepare_kernel(z, aux, table, stimuli, gain, drive):
    highs = z.types // BLOCK
    t = jnp.transpose(table[...])
    t1 = t.astype(BF16)
    t2 = (t - t1.astype(F32)).astype(BF16)
    t3 = (t - t1.astype(F32) - t2.astype(F32)).astype(BF16)
    tables = [t1, t2, t3]
    high_ids = lax.broadcasted_iota(jnp.int32, (highs, BLOCK), 0).astype(F32) + 1.0
    low_ids = lax.broadcasted_iota(jnp.int32, (BLOCK, BLOCK), 0).astype(F32)
    channel_ids = lax.broadcasted_iota(jnp.int32, (z.channels, BLOCK), 0).astype(F32)
    stim = stimuli[...]

    def one(a):
        for f in range(z.frame):
            codes = aux[a, f].astype(F32)
            pick = (high_ids == codes[0:1]).astype(BF16)
            rows = sum(jnp.dot(x, pick, preferred_element_type=F32) for x in tables)
            mine = jnp.where(low_ids == codes[1:2], rows, 0.0)
            gain[a, f] = jnp.broadcast_to(jnp.sum(mine, axis=0, keepdims=True), (8, BLOCK))
            channel = (codes[2:3] - 1.0) * BLOCK + codes[3:4]
            chosen = (channel_ids == channel).astype(BF16)
            got = jnp.dot(stim, chosen, preferred_element_type=F32)
            for step in range(z.steps):
                drive[step, a, f] = got[step * z.batch : (step + 1) * z.batch].astype(BF16)

    loop(z.rows, one)


def multiply_forward(z, meta, weights, x, total, parts):
    c = meta[2 * z.slots + 1]
    total[...] = jnp.zeros_like(total)
    for s in range(z.slots):
        total[meta[s]] += lax.dot_general(
            x[meta[z.slots + s]], weights[s], (((1,), (1,)), ((), ())), preferred_element_type=F32
        )
    for k in range(z.cols):
        ref = slot_of(parts, z.cols, c, k)
        first = z.first(c ^ k)
        for f in range(z.frame):
            ref[0, f] = total[first + f].astype(BF16)
            ref[1, f] = total[z.post + first + f].astype(BF16)


def gather_pre(z, rates, sums, x):
    sums[...] = jnp.zeros_like(sums)

    def one(a):
        first = z.first(a)
        for f in range(z.frame):
            sums[first + f] += rates[a, f]

    loop(z.rows, one)
    x[...] = sums[...].astype(BF16)


def first_kernel(z, count, *refs):
    meta, weights, own = refs[:3]
    got = refs[3 : 3 + count]
    rates, aux, x = refs[3 + count : 6 + count]
    parts, (sums, total) = refs[6 + count : -2], refs[-2:]
    p = meta[2 * z.slots]
    for k in range(z.rows):
        ref = slot_of(got, z.rows, p, k)
        for f in range(z.frame):
            rates[p ^ k, f] = ref[f, 0 : z.batch].astype(F32)
            aux[p ^ k, f] = ref[f, z.batch :]
    rates[p] = own[...]
    gather_pre(z, rates, sums, x)
    multiply_forward(z, meta, weights, x, total, parts)


def sum_kernel(z, count, *refs):
    meta = refs[0]
    got = refs[1 : 1 + count]
    rest, out = refs[1 + count : -1], refs[-1]
    p, c = meta[2 * z.slots], meta[2 * z.slots + 1]
    begin = z.offset(c)
    lanes = lax.broadcasted_iota(jnp.int32, (z.batch, z.wide), 1)
    keep = (lanes >= begin) & (lanes < begin + z.local)
    for piece in range(2):
        blocks = []
        for f in range(z.frame):
            total = slot_of(got, z.cols, c, 0)[piece, f].astype(F32)
            for k in range(1, z.cols):
                total = total + slot_of(got, z.cols, c, k)[piece, f].astype(F32)
            blocks.append(total)
        whole = jnp.where(keep, jnp.concatenate(blocks, axis=1), 0.0)
        target = p ^ (piece * z.half)
        turned = pltpu.roll(whole, lax.rem(z.offset(target) - begin + z.wide, jnp.int32(z.wide)), 1)
        for f, block in enumerate(cut(turned, z)):
            out[piece, f] = block.astype(BF16)
    for cot in rest:
        for f in range(z.frame):
            out[2, f] = cot[f].astype(BF16)


def next_kernel(z, count, *refs):
    meta, weights, rates, gain, drive = refs[:5]
    got = refs[5 : 5 + count]
    new, act_pair, cur_pair, x = refs[5 + count : 9 + count]
    parts, (stack, acts, curs, sums, total) = refs[9 + count : -5], refs[-5:]
    p = meta[2 * z.slots]
    if few(z.rows):
        for k in range(z.rows):
            stack[p ^ k] = got[k][...]
        source = stack
    else:
        source = got[0]

    def one(a):
        for f in range(z.frame):
            current = (
                source[a, 0, f].astype(F32)
                + source[a ^ z.half, 1, f].astype(F32)
                + drive[a, f].astype(F32)
            )
            activity = jnp.tanh(gain[a, f, 0:1] * current)
            new[a, f] = 0.5 * rates[a, f] + 0.5 * activity
            curs[a, f] = current
            acts[a, f] = activity

    loop(z.rows, one)
    for piece in range(2):
        act_pair[piece] = acts[p ^ (piece * z.half)]
        cur_pair[piece] = curs[p ^ (piece * z.half)]
    gather_pre(z, new, sums, x)
    multiply_forward(z, meta, weights, x, total, parts)


def push_delta(z, p, c, piece, pressures, gain, message):
    row = p ^ (piece * z.half)
    blocks = [pressures[f] * gain[row, f, 0:1] for f in range(z.frame)]
    whole = jnp.concatenate(blocks, axis=1)
    amount = z.offset(c) - z.offset(row) + z.wide
    turned = pltpu.roll(whole, lax.rem(amount, jnp.int32(z.wide)), 1)
    for f, block in enumerate(cut(turned, z)):
        message[piece, f, 0 : z.batch] = block.astype(BF16)


def turn_kernel(z, meta, rates, gain, drive, mine, theirs, cots, final, act_pair, message, gains, base):
    p, c = meta[2 * z.slots], meta[2 * z.slots + 1]
    for piece in range(2):
        row = p ^ (piece * z.half)
        first, second = (mine, theirs) if piece == 0 else (theirs, mine)
        pressures, blocks = [], []
        for f in range(z.frame):
            current = first[0, f].astype(F32) + second[1, f].astype(F32) + drive[row, f].astype(F32)
            activity = jnp.tanh(gain[row, f, 0:1] * current)
            act_pair[piece, f] = activity
            adjoint = cots[z.steps - 1, f] if piece == 0 else theirs[2, f].astype(F32)
            pressure = adjoint * 0.5 * (1.0 - activity * activity)
            pressures.append(pressure)
            gains[piece, f] = jnp.broadcast_to(
                jnp.sum(pressure * current, axis=0, keepdims=True), (8, BLOCK)
            )
            if piece == 0:
                blocks.append(0.5 * rates[p, f] + 0.5 * activity)
                base[f] = cots[z.steps - 2, f] + 0.5 * adjoint
        push_delta(z, p, c, piece, pressures, gain, message)
        if piece == 0:
            back = pltpu.roll(
                jnp.concatenate(blocks, axis=1),
                lax.rem(z.wide - z.offset(p), jnp.int32(z.wide)),
                1,
            )
            final[...] = back[:, 0 : z.local]


def gather_post(z, c, got, sums, d):
    sums[...] = jnp.zeros_like(sums)
    for k in range(z.cols):
        ref = slot_of(got, z.cols, c, k)
        first = z.first(c ^ k)
        for f in range(z.frame):
            sums[first + f] += ref[0, f, 0 : z.batch].astype(F32)
            sums[z.post + first + f] += ref[1, f, 0 : z.batch].astype(F32)
    d[...] = sums[...].astype(BF16)


def back_kernel(z, count, *refs):
    meta, weights, base = refs[:3]
    got = refs[3 : 3 + count]
    d = refs[3 + count]
    parts, (sums, total) = refs[4 + count : -2], refs[-2:]
    p, c = meta[2 * z.slots], meta[2 * z.slots + 1]
    gather_post(z, c, got, sums, d)
    total[...] = jnp.zeros_like(total)
    for s in range(z.slots):
        total[meta[z.slots + s]] += jnp.dot(d[meta[s]], weights[s], preferred_element_type=F32)
    for k in range(z.rows):
        ref = slot_of(parts, z.rows, p, k)
        row = p ^ k
        first, other = z.first(row), z.first(row ^ z.half)
        for f in range(z.frame):
            ref[0, f] = total[first + f].astype(BF16)
            block = total[other + f]
            if k == z.half:
                block = block + base[f]
            ref[1, f] = block.astype(BF16)


def delta_kernel(z, count, last, *refs):
    meta, gain, base, act_pair, cur_pair, gains_in, tail = refs[:7]
    got = refs[7 : 7 + count]
    message, tally, base_out = refs[7 + count :]
    p, c = meta[2 * z.slots], meta[2 * z.slots + 1]
    for piece in range(2):
        row = p ^ (piece * z.half)
        pressures = []
        for f in range(z.frame):
            adjoint = slot_of(got, z.rows, p, 0)[piece, f].astype(F32)
            for k in range(1, z.rows):
                adjoint = adjoint + slot_of(got, z.rows, p, k)[piece, f].astype(F32)
            if piece == 0:
                adjoint = adjoint + base[f]
                base_out[f] = tail[f] + 0.5 * adjoint
            activity = act_pair[piece, f]
            pressure = adjoint * 0.5 * (1.0 - activity * activity)
            pressures.append(pressure)
            gained = gains_in[piece, f] + jnp.sum(
                pressure * cur_pair[piece, f], axis=0, keepdims=True
            )
            tally[piece, f] = gained
        push_delta(z, p, c, piece, pressures, gain, message)


def last_delta_kernel(z, count, *refs):
    meta, gain, base, act_pair, cur_pair, gains_in, aux = refs[:7]
    got = refs[7 : 7 + count]
    message = refs[7 + count]
    p, c = meta[2 * z.slots], meta[2 * z.slots + 1]
    rows = lax.broadcasted_iota(jnp.int32, (EXTRA, BLOCK), 0)
    for piece in range(2):
        row = p ^ (piece * z.half)
        pressures = []
        for f in range(z.frame):
            adjoint = slot_of(got, z.rows, p, 0)[piece, f].astype(F32)
            for k in range(1, z.rows):
                adjoint = adjoint + slot_of(got, z.rows, p, k)[piece, f].astype(F32)
            if piece == 0:
                adjoint = adjoint + base[f]
            activity = act_pair[piece, f]
            pressure = adjoint * 0.5 * (1.0 - activity * activity)
            pressures.append(pressure)
            sums = jnp.sum(pressure * cur_pair[piece, f], axis=0, keepdims=True)
            g = gains_in[piece, f, 0:1] + sums
            g1 = g.astype(BF16).astype(F32)
            g2 = (g - g1).astype(BF16).astype(F32)
            g3 = g - g1 - g2
            codes = aux[row, f].astype(F32)
            tail = jnp.where(rows == 2, g1, codes)
            tail = jnp.where(rows == 3, g2, tail)
            tail = jnp.where(rows == 4, g3, tail)
            message[piece, f, z.batch :] = tail.astype(BF16)
        push_delta(z, p, c, piece, pressures, gain, message)


def table_kernel(z, count, *refs):
    meta, got, out = refs[0], refs[1:-1], refs[-1]
    c = meta[2 * z.slots + 1]
    highs = z.types // BLOCK
    high_ids = lax.broadcasted_iota(jnp.int32, (highs, BLOCK), 0).astype(F32) + 1.0
    low_ids = lax.broadcasted_iota(jnp.int32, (BLOCK, BLOCK), 0).astype(F32)
    total = jnp.zeros((3 * highs, BLOCK), F32)
    for k in range(z.cols):
        ref = slot_of(got, z.cols, c, k)
        for piece in range(2):
            for f in range(z.frame):
                codes = ref[piece, f, z.batch :].astype(F32)
                hit = high_ids == codes[0:1]
                terms = [jnp.where(hit, codes[2 + i : 3 + i], 0.0) for i in range(3)]
                left = jnp.concatenate(terms, axis=0).astype(BF16)
                right = (low_ids == codes[1:2]).astype(BF16)
                total = total + lax.dot_general(
                    left, right, (((1,), (1,)), ((), ())), preferred_element_type=F32
                )
    out[...] = total[0:highs] + total[highs : 2 * highs] + total[2 * highs :]


def grad_kernel(z, count, per_step, *refs):
    meta = refs[0]
    xs = refs[1 : 1 + z.steps]
    ds = refs[1 + z.steps : z.steps + z.steps]
    got = refs[2 * z.steps : 2 * z.steps + count]
    out = refs[2 * z.steps + count]
    sums, d0, right, left = refs[2 * z.steps + count + 1 :]
    n = z.batch

    @pl.when(pl.program_id(0) == 0)
    def _():
        c = meta[2 * z.slots + 1]
        gather_post(z, c, got, sums, d0)

        def lay_right(q):
            for t in range(z.steps):
                right[q, t * n : (t + 1) * n] = xs[t][q]

        loop(z.pre, lay_right)

        def lay_left(q):
            parts = [d0[q]] + [d[q] for d in ds]
            whole = jnp.concatenate([x.astype(F32) for x in parts], axis=0)
            left[q] = jnp.transpose(whole).astype(BF16)

        loop(2 * z.post, lay_left)

    begin = pl.program_id(0) * per_step
    for s in range(per_step):
        product = jnp.dot(
            left[meta[begin + s]], right[meta[z.slots + begin + s]], preferred_element_type=F32
        )
        out[s] = product.astype(BF16)


def shards(
    initial_rates,
    stimuli,
    cotangent,
    weight_blocks,
    slot_owner,
    slot_post,
    slot_pre,
    cell_type,
    type_gain,
    input_map,
):
    batch, local = initial_rates.shape
    slots = weight_blocks.shape[2]
    steps, _, channels = stimuli.shape
    types = type_gain.shape[0]
    z = Sizes(
        lax.axis_size("row"), lax.axis_size("col"), batch, local, slots, types, channels, steps
    )
    weights = weight_blocks.reshape(slots, BLOCK, BLOCK)
    place = jnp.stack([lax.axis_index("row"), lax.axis_index("col")]).astype(jnp.int32)
    meta = jnp.concatenate(
        [slot_owner.reshape(slots) * z.post + slot_post.reshape(slots), slot_pre.reshape(slots), place]
    )
    frame = (z.frame, batch, BLOCK)
    product_flops = 2 * slots * batch * BLOCK * BLOCK

    message, own, cots = call(
        functools.partial(pack_kernel, z),
        [
            shape((z.frame, batch + EXTRA, BLOCK), BF16),
            shape(frame),
            shape((steps, *frame)),
        ],
        [pltpu.VMEM((batch + EXTRA, z.wide), F32)],
        [meta, initial_rates, cell_type.reshape(1, local), input_map.reshape(1, local), cotangent],
        smem=(0,),
    )
    got = share(message, "row")
    col_parts = parcel(z.cols, (2, *frame), BF16)
    row_parts = parcel(z.rows, (2, *frame), BF16)
    pre_sums = pltpu.VMEM((z.pre, batch, BLOCK), F32)
    post_sums = pltpu.VMEM((2 * z.post, batch, BLOCK), F32)
    rates, aux, x, *parts = call(
        functools.partial(first_kernel, z, len(got)),
        [
            shape((z.rows, *frame)),
            shape((z.rows, z.frame, EXTRA, BLOCK), BF16),
            shape((z.pre, batch, BLOCK), BF16),
            *col_parts,
        ],
        [pre_sums, post_sums],
        [meta, weights, own, *got],
        smem=(0,),
        flops=product_flops,
    )
    gain, drive = call(
        functools.partial(prepare_kernel, z),
        [shape((z.rows, z.frame, 8, BLOCK)), shape((steps, z.rows, *frame), BF16)],
        [],
        [aux, type_gain.reshape(types // BLOCK, BLOCK), stimuli.reshape(steps * batch, channels)],
    )
    xs, acts, curs = [x], [], []
    for t in range(steps):
        got = exchange(parts, "col")
        last = t == steps - 1
        tail = [cots[steps - 1]] if last else []
        (sums,) = call(
            functools.partial(sum_kernel, z, len(got)),
            [shape((2 + len(tail), *frame), BF16)],
            [],
            [meta, *got, *tail],
            smem=(0,),
        )
        if last:
            break
        got = share(sums, "row")
        rates, act, cur, x, *parts = call(
            functools.partial(next_kernel, z, len(got)),
            [
                shape((z.rows, *frame)),
                shape((2, *frame)),
                shape((2, *frame)),
                shape((z.pre, batch, BLOCK), BF16),
                *col_parts,
            ],
            [
                pltpu.VMEM((z.rows, 2, *frame), BF16),
                pltpu.VMEM((z.rows, *frame), F32),
                pltpu.VMEM((z.rows, *frame), F32),
                pre_sums,
                post_sums,
            ],
            [meta, weights, rates, gain, drive[t], *got],
            smem=(0,),
            flops=product_flops,
        )
        xs.append(x)
        acts.append(act)
        curs.append(cur)
    theirs = flip(sums, "row", z.half)
    final_rates, _, message, gains, base = call(
        functools.partial(turn_kernel, z),
        [
            shape((batch, local)),
            shape((2, *frame)),
            shape((2, *frame), BF16),
            shape((2, z.frame, 8, BLOCK)),
            shape(frame),
        ],
        [],
        [meta, rates, gain, drive[steps - 1], sums, theirs, cots],
        smem=(0,),
    )
    ds = []
    for t in reversed(range(1, steps)):
        got = share(message, "col")
        d, *parts = call(
            functools.partial(back_kernel, z, len(got)),
            [shape((2 * z.post, batch, BLOCK), BF16), *row_parts],
            [post_sums, pre_sums],
            [meta, weights, base, *got],
            smem=(0,),
            flops=product_flops,
        )
        ds.insert(0, d)
        got = exchange(parts, "row")
        before = t - 1
        if before > 0:
            message, gains, base = call(
                functools.partial(delta_kernel, z, len(got), False),
                [shape((2, *frame), BF16), shape((2, z.frame, 8, BLOCK)), shape(frame)],
                [],
                [meta, gain, base, acts[before], curs[before], gains, cots[before - 1], *got],
                smem=(0,),
            )
        else:
            (message,) = call(
                functools.partial(last_delta_kernel, z, len(got)),
                [shape((2, z.frame, batch + EXTRA, BLOCK), BF16)],
                [],
                [meta, gain, base, acts[0], curs[0], gains, aux, *got],
                smem=(0,),
            )
    got = share(message, "col")
    (table,) = call(
        functools.partial(table_kernel, z, len(got)),
        [shape((types // BLOCK, BLOCK))],
        [],
        [meta, *got],
        smem=(0,),
    )
    if z.rows == 4:
        table = table + flip(table, "row", 1)
    else:
        table = 0.5 * lax.psum(table, "row")
    gain_grads = table.reshape(types)

    grid = 4
    per_step = slots // grid
    deep = steps * batch
    ins = [meta, *xs, *ds, *got]
    weight_grads = pl.pallas_call(
        functools.partial(grad_kernel, z, len(got), per_step),
        grid=(grid,),
        out_shape=shape((slots, BLOCK, BLOCK), BF16),
        in_specs=[SMEM] + [VMEM] * (len(ins) - 1),
        out_specs=pl.BlockSpec((per_step, BLOCK, BLOCK), lambda i: (i, 0, 0)),
        scratch_shapes=[
            post_sums,
            pltpu.VMEM((2 * z.post, batch, BLOCK), BF16),
            pltpu.VMEM((z.pre, deep, BLOCK), BF16),
            pltpu.VMEM((2 * z.post, BLOCK, deep), BF16),
        ],
        cost_estimate=pl.CostEstimate(
            flops=2 * slots * deep * BLOCK * BLOCK, bytes_accessed=4 * 1024 * 1024, transcendentals=0
        ),
        compiler_params=pltpu.CompilerParams(vmem_limit_bytes=32 * 1024 * 1024),
    )(*ins)
    return (final_rates, weight_grads.reshape(1, 1, slots, BLOCK, BLOCK), gain_grads)


def solution(mesh):
    in_specs = (
        P("groups", ("row", "col")),
        P(None, "groups", None),
        P(None, "groups", ("row", "col")),
        P("row", "col", None, None, None),
        P("row", "col", None),
        P("row", "col", None),
        P("row", "col", None),
        P(("row", "col")),
        P(),
        P(("row", "col")),
    )
    out_specs = (P("groups", ("row", "col")), P("row", "col", "groups", None, None), P("groups"))
    return jax.shard_map(shards, mesh=mesh, in_specs=in_specs, out_specs=out_specs, check_vma=False)
```

time: 359 us -> 109 us (0.30)
  blocking collectives: 117 us -> 0 us
  waiting for transfers between devices: 127 us -> 45.5 us
  other arithmetic: 42.8 us -> 2.02 us
  starting transfers between devices: 6.23 us -> 35.6 us
  matrix products: 26.8 us -> 0 us
  Pallas kernels: 0 us -> 20.5 us
  local copies, waits for them, and re-layouts: 23.2 us -> 4.71 us
  between operations: 14.2 us -> 0.83 us
    unnamed x10 -> x0, waiting for transfers between devices: 103 us -> none
    psum x1 -> x0, blocking collectives: 58.9 us -> none  [shards(): gain_grads = lax.psum(type_part, ('row', 'col'))]
    all_gather x6 -> x0, blocking collectives: 57.9 us -> none  [the longest x3 41.8 us: shards(): gathered = lax.all_gather(lowered, 'row', axis=1, tiled=True)]
    scatter-add x6 -> x0, other arithmetic: 34.1 us -> none  [the longest x3 18.4 us: shards(): jnp.zeros((batch_size, 2 * post_count, BLOCK), jnp.float32).at[:, both_ids]]
    ppermute x6 -> x35, starting transfers between devices: 6.02 us -> 35.6 us  [flip(): return lax.ppermute(x, axis, [(i, i ^ k) for i in range(count)])]
    dot_general x9 -> x0, matrix products: 26.8 us -> none  [the longest x3 13.5 us: shards(): jnp.einsum('bki,bkj->kij', selected, presyn, preferred_element_type=jnp.f...]
    ppermute x6 -> x35, waiting for transfers between devices: 24.4 us -> 45.5 us  [flip(): return lax.ppermute(x, axis, [(i, i ^ k) for i in range(count)])]
    pallas_call x0 -> x15, Pallas kernels: none -> 20.5 us  [the longest x14 15.5 us: call(): pl.pallas_call(body, out_shape=outs, in_specs=specs, out_specs=[VMEM] * l...]
  transfers between devices with their start and end apart: 11 -> 35, of which waited for: 10 -> 25; matrix products, arithmetic and copies ran while one was open for 4% -> 0% of each run, Pallas kernels for 0% -> 5%
where the time goes in v1:
time: 109 us
  waiting for transfers between devices  45.5 us (42%)
  starting transfers between devices  35.6 us (33%)
  Pallas kernels  20.5 us (19%)
  local copies, waits for them, and re-layouts  4.71 us (4%)
  other arithmetic  2.02 us (2%)
    ppermute x35, waiting for transfers between devices, flip(): return lax.ppermute(x, axis, [(i, i ^ k) for i in range(count)])  45.5 us
    ppermute x35, starting transfers between devices, flip(): return lax.ppermute(x, axis, [(i, i ^ k) for i in range(count)])  35.6 us
    pallas_call x14, Pallas kernels, call(): pl.pallas_call(body, out_shape=outs, in_specs=specs, out_specs=[VMEM] * l...  15.5 us
    pallas_call x1, Pallas kernels, shards(): pl.pallas_call(functools.partial(grad_kernel, z, len(got), per_step), gri...  5.08 us
    unnamed x12, local copies, waits for them, and re-layouts  3.31 us
  transfers between devices with their start and end apart: 35, of which 25 were waited for; matrix products, arithmetic and copies ran while one was open for 0% of the time, Pallas kernels for 5%

profile of v1, /device:TPU:0, one launch (start us, length us, event | category | flops | bytes accessed | tf_op | source)
XLA Modules:
  0.0 109.2 jit_solution(17894345153891947469)
XLA Ops:
  0.6 0.7 reshape.37.types
  1.3 0.7 reshape.38.inputs
  2.0 0.7 add_bitcast_fusion.1
  2.7 0.7 pad_add_fusion.meta.refs_0_
  3.4 0.9 copy-done.2
  4.3 0.8 copy-done.4
  5.1 0.7 shard_map.121
  5.8 3.1 %collective-permute-start = (bf16[3,48,128]{2,1,0:T(8,128)(2,1)S(1)}, bf16[3,48,128]{2,1,0:T(8,128)(2,1)S(1)}, u32[]{:S(2)}, u32[]{:S(2)}) collective-permute-start(bf16[3,48,128]{2,1,0:T(8,128)(2,1)S(1)} %get-tuple-element.49.refs_3_), channel_id=1, source_target_pairs={{0,4},{4,0},{8,12},{12,8},{1,5},{5,1},{9,13},{13,9},{2,6},{6,2},{1... | collective-permute-start | bytes 110600 | tf_op jit(solution)/shard_map/ppermute | solution.py:57
  8.9 2.6 %collective-permute-start.1 = (bf16[3,48,128]{2,1,0:T(8,128)(2,1)S(1)}, bf16[3,48,128]{2,1,0:T(8,128)(2,1)S(1)}, u32[]{:S(2)}, u32[]{:S(2)}) collective-permute-start(bf16[3,48,128]{2,1,0:T(8,128)(2,1)S(1)} %get-tuple-element.49.refs_3_), channel_id=1, source_target_pairs={{0,8},{4,12},{8,0},{12,4},{1,9},{5,13},{9,1},{13,5},{2,10},{6,14},... | collective-permute-start | bytes 110600 | tf_op jit(solution)/shard_map/ppermute | solution.py:57
  11.5 2.9 %collective-permute-done.1.refs_5_ = bf16[3,48,128]{2,1,0:T(8,128)(2,1)S(1)} collective-permute-done((bf16[3,48,128]{2,1,0:T(8,128)(2,1)S(1)}, bf16[3,48,128]{2,1,0:T(8,128)(2,1)S(1)}, u32[]{:S(2)}, u32[]{:S(2)}) %collective-permute-start.1) | collective-permute-done | bytes 36896 | tf_op jit(solution)/shard_map/ppermute | solution.py:57
  14.4 2.8 %collective-permute-done.2.refs_6_ = bf16[3,48,128]{2,1,0:T(8,128)(2,1)S(1)} collective-permute-done((bf16[3,48,128]{2,1,0:T(8,128)(2,1)S(1)}, bf16[3,48,128]{2,1,0:T(8,128)(2,1)S(1)}, u32[]{:S(2)}, u32[]{:S(2)}) %collective-permute-start.2) | collective-permute-done | bytes 36896 | tf_op jit(solution)/shard_map/ppermute | solution.py:57
  17.3 1.6 %copy-done = bf16[1,1,64,128,128]{4,3,2,1,0:T(8,128)(2,1)S(1)} copy-done((bf16[1,1,64,128,128]{4,3,2,1,0:T(8,128)(2,1)S(1)}, bf16[1,1,64,128,128]{4,3,2,1,0:T(8,128)(2,1)}, u32[]{:S(2)}) %copy-start) | copy-done | bytes 2097176
  18.8 1.8 %shard_map.122 = (f32[4,3,32,128]{3,2,1,0:T(8,128)S(1)}, bf16[4,3,16,128]{3,2,1,0:T(8,128)(2,1)S(1)}, bf16[9,32,128]{2,1,0:T(8,128)(2,1)S(1)}, bf16[2,3,32,128]{...) custom-call(s32[130]{0:T(256)S(1)} %pad_add_fusion.meta.refs_0_, ...), custom_call_target="tpu_custom_call" | custom-call | flops 67108864 | bytes 2810376 | tf_op jit(solution)/shard_map/pallas_call | solution.py:40
  20.7 1.6 %collective-permute-start.4 = (bf16[2,3,32,128]{3,2,1,0:T(8,128)(2,1)S(1)}, bf16[2,3,32,128]{3,2,1,0:T(8,128)(2,1)S(1)}, u32[]{:S(2)}, u32[]{:S(2)}) collective-permute-start(bf16[2,3,32,128]{3,2,1,0:T(8,128)(2,1)S(1)} %get-tuple-element.56), channel_id=1, source_target_pairs={{0,2},{1,3},{2,0},{3,1},{4,6},{5,7},{6,4},{7,5},{8,10},{9,11},{10,... | collective-permute-start | bytes 147464 | tf_op jit(solution)/shard_map/ppermute | solution.py:57
  22.6 0.8 shard_map.123
  23.4 1.4 %collective-permute-done.4.refs_3_ = bf16[2,3,32,128]{3,2,1,0:T(8,128)(2,1)S(1)} collective-permute-done((bf16[2,3,32,128]{3,2,1,0:T(8,128)(2,1)S(1)}, bf16[2,3,32,128]{3,2,1,0:T(8,128)(2,1)S(1)}, u32[]{:S(2)}, u32[]{:S(2)}) %collective-permute-start.4) | collective-permute-done | bytes 49184 | tf_op jit(solution)/shard_map/ppermute | solution.py:57
  24.9 1.1 %collective-permute-done.5.refs_4_ = bf16[2,3,32,128]{3,2,1,0:T(8,128)(2,1)S(1)} collective-permute-done((bf16[2,3,32,128]{3,2,1,0:T(8,128)(2,1)S(1)}, bf16[2,3,32,128]{3,2,1,0:T(8,128)(2,1)S(1)}, u32[]{:S(2)}, u32[]{:S(2)}) %collective-permute-start.5) | collective-permute-done | bytes 49184 | tf_op jit(solution)/shard_map/ppermute | solution.py:57
  26.0 0.7 shard_map.124.refs_5_
  26.7 1.1 collective-permute-start.7
  27.8 3.3 %collective-permute-start.8 = (bf16[2,3,32,128]{3,2,1,0:T(8,128)(2,1)S(1)}, bf16[2,3,32,128]{3,2,1,0:T(8,128)(2,1)S(1)}, u32[]{:S(2)}, u32[]{:S(2)}) collective-permute-start(bf16[2,3,32,128]{3,2,1,0:T(8,128)(2,1)S(1)} %shard_map.124.refs_5_), channel_id=1, source_target_pairs={{0,12},{4,8},{8,4},{12,0},{1,13},{5,9},{9,5},{13,1},{2,14},{6,10},... | collective-permute-start | bytes 147464 | tf_op jit(solution)/shard_map/ppermute | solution.py:57
  31.4 2.7 %collective-permute-done.7.refs_7_ = bf16[2,3,32,128]{3,2,1,0:T(8,128)(2,1)S(1)} collective-permute-done((bf16[2,3,32,128]{3,2,1,0:T(8,128)(2,1)S(1)}, bf16[2,3,32,128]{3,2,1,0:T(8,128)(2,1)S(1)}, u32[]{:S(2)}, u32[]{:S(2)}) %collective-permute-start.7) | collective-permute-done | bytes 49184 | tf_op jit(solution)/shard_map/ppermute | solution.py:57
  34.1 1.9 %shard_map.125 = (f32[4,3,32,128]{3,2,1,0:T(8,128)S(1)}, f32[2,3,32,128]{3,2,1,0:T(8,128)S(1)}, f32[2,3,32,128]{3,2,1,0:T(8,128)S(1)}, bf16[9,32,128]{2,1,0:T(8,...) custom-call(s32[130]{0:T(256)S(1)} %pad_add_fusion.meta.refs_0_, ...), custom_call_target="tpu_custom_call" | custom-call | flops 67108864 | bytes 3301896 | tf_op jit(solution)/shard_map/pallas_call | solution.py:40
  36.1 1.2 %collective-permute-start.10 = (bf16[2,3,32,128]{3,2,1,0:T(8,128)(2,1)S(1)}, bf16[2,3,32,128]{3,2,1,0:T(8,128)(2,1)S(1)}, u32[]{:S(2)}, u32[]{:S(2)}) collective-permute-start(bf16[2,3,32,128]{3,2,1,0:T(8,128)(2,1)S(1)} %get-tuple-element.61), channel_id=1, source_target_pairs={{0,2},{1,3},{2,0},{3,1},{4,6},{5,7},{6,4},{7,5},{8,10},{9,11},{10,... | collective-permute-start | bytes 147464 | tf_op jit(solution)/shard_map/ppermute | solution.py:57
  37.3 0.7 collective-permute-start.11
  37.9 2.3 %collective-permute-done.10.refs_3_ = bf16[2,3,32,128]{3,2,1,0:T(8,128)(2,1)S(1)} collective-permute-done((bf16[2,3,32,128]{3,2,1,0:T(8,128)(2,1)S(1)}, bf16[2,3,32,128]{3,2,1,0:T(8,128)(2,1)S(1)}, u32[]{:S(2)}, u32[]{:S(2)}) %collective-permute-start.10) | collective-permute-done | bytes 49184 | tf_op jit(solution)/shard_map/ppermute | solution.py:57
  40.2 0.7 collective-permute-done.11.refs_4_
  41.0 0.7 shard_map.126.refs_5_
  41.6 1.2 %collective-permute-start.12 = (bf16[2,3,32,128]{3,2,1,0:T(8,128)(2,1)S(1)}, bf16[2,3,32,128]{3,2,1,0:T(8,128)(2,1)S(1)}, u32[]{:S(2)}, u32[]{:S(2)}) collective-permute-start(bf16[2,3,32,128]{3,2,1,0:T(8,128)(2,1)S(1)} %shard_map.126.refs_5_), channel_id=1, source_target_pairs={{0,4},{4,0},{8,12},{12,8},{1,5},{5,1},{9,13},{13,9},{2,6},{6,2},{1... | collective-permute-start | bytes 147464 | tf_op jit(solution)/shard_map/ppermute | solution.py:57
  42.8 2.4 %collective-permute-start.13 = (bf16[2,3,32,128]{3,2,1,0:T(8,128)(2,1)S(1)}, bf16[2,3,32,128]{3,2,1,0:T(8,128)(2,1)S(1)}, u32[]{:S(2)}, u32[]{:S(2)}) collective-permute-start(bf16[2,3,32,128]{3,2,1,0:T(8,128)(2,1)S(1)} %shard_map.126.refs_5_), channel_id=1, source_target_pairs={{0,8},{4,12},{8,0},{12,4},{1,9},{5,13},{9,1},{13,5},{2,10},{6,14},... | collective-permute-start | bytes 147464 | tf_op jit(solution)/shard_map/ppermute | solution.py:57
  45.2 0.9 collective-permute-start.14
  46.1 2.7 %collective-permute-done.13.refs_7_ = bf16[2,3,32,128]{3,2,1,0:T(8,128)(2,1)S(1)} collective-permute-done((bf16[2,3,32,128]{3,2,1,0:T(8,128)(2,1)S(1)}, bf16[2,3,32,128]{3,2,1,0:T(8,128)(2,1)S(1)}, u32[]{:S(2)}, u32[]{:S(2)}) %collective-permute-start.13) | collective-permute-done | bytes 49184 | tf_op jit(solution)/shard_map/ppermute | solution.py:57
  48.8 2.3 %collective-permute-done.14.refs_8_ = bf16[2,3,32,128]{3,2,1,0:T(8,128)(2,1)S(1)} collective-permute-done((bf16[2,3,32,128]{3,2,1,0:T(8,128)(2,1)S(1)}, bf16[2,3,32,128]{3,2,1,0:T(8,128)(2,1)S(1)}, u32[]{:S(2)}, u32[]{:S(2)}) %collective-permute-start.14) | collective-permute-done | bytes 49184 | tf_op jit(solution)/shard_map/ppermute | solution.py:57
  51.1 1.9 %shard_map.127 = (f32[4,3,32,128]{3,2,1,0:T(8,128)S(1)}, f32[2,3,32,128]{3,2,1,0:T(8,128)S(1)}, f32[2,3,32,128]{3,2,1,0:T(8,128)S(1)}, bf16[9,32,128]{2,1,0:T(8,...) custom-call(s32[130]{0:T(256)S(1)} %pad_add_fusion.meta.refs_0_, ...), custom_call_target="tpu_custom_call" | custom-call | flops 67108864 | bytes 3301896 | tf_op jit(solution)/shard_map/pallas_call | solution.py:40
  53.0 1.0 collective-permute-start.16
  54.0 0.8 collective-permute-start.17
  54.9 2.5 %collective-permute-done.16.refs_3_ = bf16[2,3,32,128]{3,2,1,0:T(8,128)(2,1)S(1)} collective-permute-done((bf16[2,3,32,128]{3,2,1,0:T(8,128)(2,1)S(1)}, bf16[2,3,32,128]{3,2,1,0:T(8,128)(2,1)S(1)}, u32[]{:S(2)}, u32[]{:S(2)}) %collective-permute-start.16) | collective-permute-done | bytes 49184 | tf_op jit(solution)/shard_map/ppermute | solution.py:57
  58.0 0.7 shard_map.128.mine
  59.2 5.1 %collective-permute-done.18.theirs = bf16[3,3,32,128]{3,2,1,0:T(8,128)(2,1)S(1)} collective-permute-done((bf16[3,3,32,128]{3,2,1,0:T(8,128)(2,1)S(1)}, bf16[3,3,32,128]{3,2,1,0:T(8,128)(2,1)S(1)}, u32[]{:S(2)}, u32[]{:S(2)}) %collective-permute-start.18) | collective-permute-done | bytes 73760 | tf_op jit(solution)/shard_map/ppermute | solution.py:57
  64.3 1.3 %shard_map.129 = (f32[32,288]{1,0:T(8,128)}, f32[2,3,32,128]{3,2,1,0:T(8,128)}, bf16[2,3,32,128]{3,2,1,0:T(8,128)(2,1)S(1)}, f32[2,3,8,128]{3,2,1,0:T(8,128)S(1)}, f32[3,32,128]{2,1,0:T(8,128)S(1)}) custom-call(s32[130]{0:T(256)S(1)} %pad_add_fusion.meta.refs_0_, f32[4,3,32,128]{3,2,1,0:T(8,128)S(1)} %get-tuple-element.63.rates, ...), custom_call_target="tpu_custom_call" | custom-call | bytes 897544 | tf_op jit(solution)/shard_map/pallas_call | solution.py:40
  65.6 1.2 %collective-permute-start.20 = (bf16[2,3,32,128]{3,2,1,0:T(8,128)(2,1)S(1)}, bf16[2,3,32,128]{3,2,1,0:T(8,128)(2,1)S(1)}, u32[]{:S(2)}, u32[]{:S(2)}) collective-permute-start(bf16[2,3,32,128]{3,2,1,0:T(8,128)(2,1)S(1)} %get-tuple-element.77.refs_3_), channel_id=1, source_target_pairs={{0,2},{1,3},{2,0},{3,1},{4,6},{5,7},{6,4},{7,5},{8,10},{9,11},{10,... | collective-permute-start | bytes 147464 | tf_op jit(solution)/shard_map/ppermute | solution.py:57
  66.8 0.7 collective-permute-start.21
  67.5 2.3 %collective-permute-done.20.refs_5_ = bf16[2,3,32,128]{3,2,1,0:T(8,128)(2,1)S(1)} collective-permute-done((bf16[2,3,32,128]{3,2,1,0:T(8,128)(2,1)S(1)}, bf16[2,3,32,128]{3,2,1,0:T(8,128)(2,1)S(1)}, u32[]{:S(2)}, u32[]{:S(2)}) %collective-permute-start.20) | collective-permute-done | bytes 49184 | tf_op jit(solution)/shard_map/ppermute | solution.py:57
  69.8 0.8 collective-permute-done.21.refs_6_
  70.5 1.3 %shard_map.130 = (bf16[18,32,128]{2,1,0:T(8,128)(2,1)S(1)}, bf16[2,3,32,128]{3,2,1,0:T(8,128)(2,1)S(1)}, bf16[2,3,32,128]{3,2,1,0:T(8,128)(2,1)S(1)}, bf16[2,3,3...) custom-call(s32[130]{0:T(256)S(1)} %pad_add_fusion.meta.refs_0_, bf16[64,128,128]{2,1,0:T(8,128)(2,1)S(1)} %bitcast.24, ...), custom_call_target="tpu_custom_call" | custom-call | flops 67108864 | bytes 2687496 | tf_op jit(solution)/shard_map/pallas_call | solution.py:40
  71.9 2.7 %collective-permute-start.23 = (bf16[2,3,32,128]{3,2,1,0:T(8,128)(2,1)S(1)}, bf16[2,3,32,128]{3,2,1,0:T(8,128)(2,1)S(1)}, u32[]{:S(2)}, u32[]{:S(2)}) collective-permute-start(bf16[2,3,32,128]{3,2,1,0:T(8,128)(2,1)S(1)} %get-tuple-element.80), channel_id=1, source_target_pairs={{0,8},{4,12},{8,0},{12,4},{1,9},{5,13},{9,1},{13,5},{2,10},{6,14},... | collective-permute-start | bytes 147464 | tf_op jit(solution)/shard_map/ppermute | solution.py:57
  74.7 1.6 %collective-permute-start.24 = (bf16[2,3,32,128]{3,2,1,0:T(8,128)(2,1)S(1)}, bf16[2,3,32,128]{3,2,1,0:T(8,128)(2,1)S(1)}, u32[]{:S(2)}, u32[]{:S(2)}) collective-permute-start(bf16[2,3,32,128]{3,2,1,0:T(8,128)(2,1)S(1)} %get-tuple-element.81), channel_id=1, source_target_pairs={{0,12},{4,8},{8,4},{12,0},{1,13},{5,9},{9,5},{13,1},{2,14},{6,10},... | collective-permute-start | bytes 147464 | tf_op jit(solution)/shard_map/ppermute | solution.py:57
  76.8 1.1 %collective-permute-done.23.refs_9_ = bf16[2,3,32,128]{3,2,1,0:T(8,128)(2,1)S(1)} collective-permute-done((bf16[2,3,32,128]{3,2,1,0:T(8,128)(2,1)S(1)}, bf16[2,3,32,128]{3,2,1,0:T(8,128)(2,1)S(1)}, u32[]{:S(2)}, u32[]{:S(2)}) %collective-permute-start.23) | collective-permute-done | bytes 49184 | tf_op jit(solution)/shard_map/ppermute | solution.py:57
  77.9 2.7 %collective-permute-done.24.refs_10_ = bf16[2,3,32,128]{3,2,1,0:T(8,128)(2,1)S(1)} collective-permute-done((bf16[2,3,32,128]{3,2,1,0:T(8,128)(2,1)S(1)}, bf16[2,3,32,128]{3,2,1,0:T(8,128)(2,1)S(1)}, u32[]{:S(2)}, u32[]{:S(2)}) %collective-permute-start.24) | collective-permute-done | bytes 49184 | tf_op jit(solution)/shard_map/ppermute | solution.py:57
  80.6 0.7 shard_map.131
  81.3 1.3 %collective-permute-start.26 = (bf16[2,3,32,128]{3,2,1,0:T(8,128)(2,1)S(1)}, bf16[2,3,32,128]{3,2,1,0:T(8,128)(2,1)S(1)}, u32[]{:S(2)}, u32[]{:S(2)}) collective-permute-start(bf16[2,3,32,128]{3,2,1,0:T(8,128)(2,1)S(1)} %get-tuple-element.83.refs_3_), channel_id=1, source_target_pairs={{0,2},{1,3},{2,0},{3,1},{4,6},{5,7},{6,4},{7,5},{8,10},{9,11},{10,... | collective-permute-start | bytes 147464 | tf_op jit(solution)/shard_map/ppermute | solution.py:57
  83.2 2.3 %collective-permute-done.26.refs_5_ = bf16[2,3,32,128]{3,2,1,0:T(8,128)(2,1)S(1)} collective-permute-done((bf16[2,3,32,128]{3,2,1,0:T(8,128)(2,1)S(1)}, bf16[2,3,32,128]{3,2,1,0:T(8,128)(2,1)S(1)}, u32[]{:S(2)}, u32[]{:S(2)}) %collective-permute-start.26) | collective-permute-done | bytes 49184 | tf_op jit(solution)/shard_map/ppermute | solution.py:57
  85.5 0.8 collective-permute-done.27.refs_6_
  86.3 1.3 %shard_map.132 = (bf16[18,32,128]{2,1,0:T(8,128)(2,1)S(1)}, bf16[2,3,32,128]{3,2,1,0:T(8,128)(2,1)S(1)}, bf16[2,3,32,128]{3,2,1,0:T(8,128)(2,1)S(1)}, bf16[2,3,3...) custom-call(s32[130]{0:T(256)S(1)} %pad_add_fusion.meta.refs_0_, bf16[64,128,128]{2,1,0:T(8,128)(2,1)S(1)} %bitcast.25, ...), custom_call_target="tpu_custom_call" | custom-call | flops 67108864 | bytes 2687496 | tf_op jit(solution)/shard_map/pallas_call | solution.py:40
  87.7 2.2 %collective-permute-start.29 = (bf16[2,3,32,128]{3,2,1,0:T(8,128)(2,1)S(1)}, bf16[2,3,32,128]{3,2,1,0:T(8,128)(2,1)S(1)}, u32[]{:S(2)}, u32[]{:S(2)}) collective-permute-start(bf16[2,3,32,128]{3,2,1,0:T(8,128)(2,1)S(1)} %get-tuple-element.91), channel_id=1, source_target_pairs={{0,8},{4,12},{8,0},{12,4},{1,9},{5,13},{9,1},{13,5},{2,10},{6,14},... | collective-permute-start | bytes 147464 | tf_op jit(solution)/shard_map/ppermute | solution.py:57
  89.8 2.2 %collective-permute-start.30 = (bf16[2,3,32,128]{3,2,1,0:T(8,128)(2,1)S(1)}, bf16[2,3,32,128]{3,2,1,0:T(8,128)(2,1)S(1)}, u32[]{:S(2)}, u32[]{:S(2)}) collective-permute-start(bf16[2,3,32,128]{3,2,1,0:T(8,128)(2,1)S(1)} %get-tuple-element.92), channel_id=1, source_target_pairs={{0,12},{4,8},{8,4},{12,0},{1,13},{5,9},{9,5},{13,1},{2,14},{6,10},... | collective-permute-start | bytes 147464 | tf_op jit(solution)/shard_map/ppermute | solution.py:57
  92.4 1.1 %collective-permute-done.29.refs_9_ = bf16[2,3,32,128]{3,2,1,0:T(8,128)(2,1)S(1)} collective-permute-done((bf16[2,3,32,128]{3,2,1,0:T(8,128)(2,1)S(1)}, bf16[2,3,32,128]{3,2,1,0:T(8,128)(2,1)S(1)}, u32[]{:S(2)}, u32[]{:S(2)}) %collective-permute-start.29) | collective-permute-done | bytes 49184 | tf_op jit(solution)/shard_map/ppermute | solution.py:57
  93.5 2.2 %collective-permute-done.30.refs_10_ = bf16[2,3,32,128]{3,2,1,0:T(8,128)(2,1)S(1)} collective-permute-done((bf16[2,3,32,128]{3,2,1,0:T(8,128)(2,1)S(1)}, bf16[2,3,32,128]{3,2,1,0:T(8,128)(2,1)S(1)}, u32[]{:S(2)}, u32[]{:S(2)}) %collective-permute-start.30) | collective-permute-done | bytes 49184 | tf_op jit(solution)/shard_map/ppermute | solution.py:57
  95.7 0.7 shard_map.133.refs_6_.refs_1_
  96.5 1.3 %collective-permute-start.32 = (bf16[2,3,48,128]{3,2,1,0:T(8,128)(2,1)S(1)}, bf16[2,3,48,128]{3,2,1,0:T(8,128)(2,1)S(1)}, u32[]{:S(2)}, u32[]{:S(2)}) collective-permute-start(bf16[2,3,48,128]{3,2,1,0:T(8,128)(2,1)S(1)} %shard_map.133.refs_6_.refs_1_), channel_id=1, source_target_pairs={{0,2},{1,3},{2,0},{3,1},{4,6},{5,7},{6,4},{7,5},{8,10},{9,11},{10,... | collective-permute-start | bytes 221192 | tf_op jit(solution)/shard_map/ppermute | solution.py:57
  98.4 3.3 %collective-permute-done.32.refs_8_.refs_3_ = bf16[2,3,48,128]{3,2,1,0:T(8,128)(2,1)S(1)} collective-permute-done((bf16[2,3,48,128]{3,2,1,0:T(8,128)(2,1)S(1)}, bf16[2,3,48,128]{3,2,1,0:T(8,128)(2,1)S(1)}, u32[]{:S(2)}, u32[]{:S(2)}) %collective-permute-start.32) | collective-permute-done | bytes 73760 | tf_op jit(solution)/shard_map/ppermute | solution.py:57
  101.7 0.6 collective-permute-done.33.refs_9_.refs_4_
  102.3 1.2 %shard_map.135 = f32[64,128]{1,0:T(8,128)S(1)} custom-call(s32[130]{0:T(256)S(1)} %pad_add_fusion.meta.refs_0_, bf16[2,3,48,128]{3,2,1,0:T(8,128)(2,1)S(1)} %shard_map.133.refs_6_.refs_1_, bf16[2,3,48,128]{3,2,1,0:T(8,128)(2,1)S(1)} %collective-permute-done.31.refs_7_.refs_2_, bf16[2,3,48,128]{3,2,1,0:T(8,128)(2,1)S(1)} %collective-permute-done.32.refs_8_.refs_3_, ...), custom_call_target="tpu_custom_call" | custom-call | bytes 328200 | tf_op jit(solution)/shard_map/pallas_call | solution.py:40
  103.5 5.1 %shard_map.134 = bf16[64,128,128]{2,1,0:T(8,128)(2,1)} custom-call(s32[130]{0:T(256)S(1)} %pad_add_fusion.meta.refs_0_, bf16[9,32,128]{2,1,0:T(8,128)(2,1)S(1)} %get-tuple-element.70.refs_1_, bf16[9,32,128]{2,1,0:T(8,128)(2,1)S(1)} %get-tuple-element.71.refs_2_, bf16[9,32,128]{2,1,0:T(8,128)(2,1)S(1)} %get-tuple-element.72.refs_3_, ...), custom_call_target="tpu_custom_call" | custom-call | flops 201326592 | bytes 4194304 | tf_op jit(solution)/shard_map/pallas_call | solution.py:600
  108.6 0.6 add_bitcast_fusion
  (40 shorter events, 4.4 us)
Async XLA Ops:
  3.4 0.9 copy-start.2
  4.3 0.8 copy-start.4
  5.1 17.5 %copy-start.3 = (bf16[3,32,512]{2,1,0:T(8,128)(2,1)S(1)}, bf16[3,32,512]{2,1,0:T(8,128)(2,1)}, u32[]{:S(2)}) copy-start(bf16[3,32,512]{2,1,0:T(8,128)(2,1)} %param.11) | copy-start | bytes 294916
  5.1 17.5 %copy-start.5 = (f32[8192]{0:T(1024)S(1)}, f32[8192]{0:T(1024)}, u32[]{:S(2)}) copy-start(f32[8192]{0:T(1024)} %param.18) | copy-start | bytes 98308
  5.8 5.7 %collective-permute-start = (bf16[3,48,128]{2,1,0:T(8,128)(2,1)S(1)}, bf16[3,48,128]{2,1,0:T(8,128)(2,1)S(1)}, u32[]{:S(2)}, u32[]{:S(2)}) collective-permute-start(bf16[3,48,128]{2,1,0:T(8,128)(2,1)S(1)} %get-tuple-element.49.refs_3_), channel_id=1, source_target_pairs={{0,4},{4,0},{8,12},{12,8},{1,5},{5,1},{9,13},{13,9},{2,6},{6,2},{1... | collective-permute-start | bytes 110600 | tf_op jit(solution)/shard_map/ppermute | solution.py:57
  8.9 5.5 %collective-permute-start.1 = (bf16[3,48,128]{2,1,0:T(8,128)(2,1)S(1)}, bf16[3,48,128]{2,1,0:T(8,128)(2,1)S(1)}, u32[]{:S(2)}, u32[]{:S(2)}) collective-permute-start(bf16[3,48,128]{2,1,0:T(8,128)(2,1)S(1)} %get-tuple-element.49.refs_3_), channel_id=1, source_target_pairs={{0,8},{4,12},{8,0},{12,4},{1,9},{5,13},{9,1},{13,5},{2,10},{6,14},... | collective-permute-start | bytes 110600 | tf_op jit(solution)/shard_map/ppermute | solution.py:57
  11.5 5.8 %collective-permute-start.2 = (bf16[3,48,128]{2,1,0:T(8,128)(2,1)S(1)}, bf16[3,48,128]{2,1,0:T(8,128)(2,1)S(1)}, u32[]{:S(2)}, u32[]{:S(2)}) collective-permute-start(bf16[3,48,128]{2,1,0:T(8,128)(2,1)S(1)} %get-tuple-element.49.refs_3_), channel_id=1, source_target_pairs={{0,12},{4,8},{8,4},{12,0},{1,13},{5,9},{9,5},{13,1},{2,14},{6,10},... | collective-permute-start | bytes 110600 | tf_op jit(solution)/shard_map/ppermute | solution.py:57
  17.3 1.6 %copy-start = (bf16[1,1,64,128,128]{4,3,2,1,0:T(8,128)(2,1)S(1)}, bf16[1,1,64,128,128]{4,3,2,1,0:T(8,128)(2,1)}, u32[]{:S(2)}) copy-start(bf16[1,1,64,128,128]{4,3,2,1,0:T(8,128)(2,1)} %param.13) | copy-start | bytes 6291460
  18.8 15.3 %copy-start.1 = (bf16[1,1,64,128,128]{4,3,2,1,0:T(8,128)(2,1)S(1)}, bf16[1,1,64,128,128]{4,3,2,1,0:T(8,128)(2,1)}, u32[]{:S(2)}) copy-start(bf16[1,1,64,128,128]{4,3,2,1,0:T(8,128)(2,1)} %param.13) | copy-start | bytes 6291460
  20.6 2.8 %collective-permute-start.3 = (bf16[2,3,32,128]{3,2,1,0:T(8,128)(2,1)S(1)}, bf16[2,3,32,128]{3,2,1,0:T(8,128)(2,1)S(1)}, u32[]{:S(2)}, u32[]{:S(2)}) collective-permute-start(bf16[2,3,32,128]{3,2,1,0:T(8,128)(2,1)S(1)} %get-tuple-element.55), channel_id=1, source_target_pairs={{0,1},{1,0},{2,3},{3,2},{4,5},{5,4},{6,7},{7,6},{8,9},{9,8},{10,11... | collective-permute-start | bytes 147464 | tf_op jit(solution)/shard_map/ppermute | solution.py:57
  20.7 4.2 %collective-permute-start.4 = (bf16[2,3,32,128]{3,2,1,0:T(8,128)(2,1)S(1)}, bf16[2,3,32,128]{3,2,1,0:T(8,128)(2,1)S(1)}, u32[]{:S(2)}, u32[]{:S(2)}) collective-permute-start(bf16[2,3,32,128]{3,2,1,0:T(8,128)(2,1)S(1)} %get-tuple-element.56), channel_id=1, source_target_pairs={{0,2},{1,3},{2,0},{3,1},{4,6},{5,7},{6,4},{7,5},{8,10},{9,11},{10,... | collective-permute-start | bytes 147464 | tf_op jit(solution)/shard_map/ppermute | solution.py:57
  22.3 3.7 %collective-permute-start.5 = (bf16[2,3,32,128]{3,2,1,0:T(8,128)(2,1)S(1)}, bf16[2,3,32,128]{3,2,1,0:T(8,128)(2,1)S(1)}, u32[]{:S(2)}, u32[]{:S(2)}) collective-permute-start(bf16[2,3,32,128]{3,2,1,0:T(8,128)(2,1)S(1)} %get-tuple-element.57), channel_id=1, source_target_pairs={{0,3},{1,2},{2,1},{3,0},{4,7},{5,6},{6,5},{7,4},{8,11},{9,10},{10,... | collective-permute-start | bytes 147464 | tf_op jit(solution)/shard_map/ppermute | solution.py:57
  26.6 4.8 %collective-permute-start.6 = (bf16[2,3,32,128]{3,2,1,0:T(8,128)(2,1)S(1)}, bf16[2,3,32,128]{3,2,1,0:T(8,128)(2,1)S(1)}, u32[]{:S(2)}, u32[]{:S(2)}) collective-permute-start(bf16[2,3,32,128]{3,2,1,0:T(8,128)(2,1)S(1)} %shard_map.124.refs_5_), channel_id=1, source_target_pairs={{0,4},{4,0},{8,12},{12,8},{1,5},{5,1},{9,13},{13,9},{2,6},{6,2},{1... | collective-permute-start | bytes 147464 | tf_op jit(solution)/shard_map/ppermute | solution.py:57
  26.7 7.4 %collective-permute-start.7 = (bf16[2,3,32,128]{3,2,1,0:T(8,128)(2,1)S(1)}, bf16[2,3,32,128]{3,2,1,0:T(8,128)(2,1)S(1)}, u32[]{:S(2)}, u32[]{:S(2)}) collective-permute-start(bf16[2,3,32,128]{3,2,1,0:T(8,128)(2,1)S(1)} %shard_map.124.refs_5_), channel_id=1, source_target_pairs={{0,8},{4,12},{8,0},{12,4},{1,9},{5,13},{9,1},{13,5},{2,10},{6,14},... | collective-permute-start | bytes 147464 | tf_op jit(solution)/shard_map/ppermute | solution.py:57
  27.8 6.4 %collective-permute-start.8 = (bf16[2,3,32,128]{3,2,1,0:T(8,128)(2,1)S(1)}, bf16[2,3,32,128]{3,2,1,0:T(8,128)(2,1)S(1)}, u32[]{:S(2)}, u32[]{:S(2)}) collective-permute-start(bf16[2,3,32,128]{3,2,1,0:T(8,128)(2,1)S(1)} %shard_map.124.refs_5_), channel_id=1, source_target_pairs={{0,12},{4,8},{8,4},{12,0},{1,13},{5,9},{9,5},{13,1},{2,14},{6,10},... | collective-permute-start | bytes 147464 | tf_op jit(solution)/shard_map/ppermute | solution.py:57
  36.0 1.9 %collective-permute-start.9 = (bf16[2,3,32,128]{3,2,1,0:T(8,128)(2,1)S(1)}, bf16[2,3,32,128]{3,2,1,0:T(8,128)(2,1)S(1)}, u32[]{:S(2)}, u32[]{:S(2)}) collective-permute-start(bf16[2,3,32,128]{3,2,1,0:T(8,128)(2,1)S(1)} %get-tuple-element.60), channel_id=1, source_target_pairs={{0,1},{1,0},{2,3},{3,2},{4,5},{5,4},{6,7},{7,6},{8,9},{9,8},{10,11... | collective-permute-start | bytes 147464 | tf_op jit(solution)/shard_map/ppermute | solution.py:57
  36.1 4.2 %collective-permute-start.10 = (bf16[2,3,32,128]{3,2,1,0:T(8,128)(2,1)S(1)}, bf16[2,3,32,128]{3,2,1,0:T(8,128)(2,1)S(1)}, u32[]{:S(2)}, u32[]{:S(2)}) collective-permute-start(bf16[2,3,32,128]{3,2,1,0:T(8,128)(2,1)S(1)} %get-tuple-element.61), channel_id=1, source_target_pairs={{0,2},{1,3},{2,0},{3,1},{4,6},{5,7},{6,4},{7,5},{8,10},{9,11},{10,... | collective-permute-start | bytes 147464 | tf_op jit(solution)/shard_map/ppermute | solution.py:57
  37.3 3.7 %collective-permute-start.11 = (bf16[2,3,32,128]{3,2,1,0:T(8,128)(2,1)S(1)}, bf16[2,3,32,128]{3,2,1,0:T(8,128)(2,1)S(1)}, u32[]{:S(2)}, u32[]{:S(2)}) collective-permute-start(bf16[2,3,32,128]{3,2,1,0:T(8,128)(2,1)S(1)} %get-tuple-element.62), channel_id=1, source_target_pairs={{0,3},{1,2},{2,1},{3,0},{4,7},{5,6},{6,5},{7,4},{8,11},{9,10},{10,... | collective-permute-start | bytes 147464 | tf_op jit(solution)/shard_map/ppermute | solution.py:57
  41.6 4.5 %collective-permute-start.12 = (bf16[2,3,32,128]{3,2,1,0:T(8,128)(2,1)S(1)}, bf16[2,3,32,128]{3,2,1,0:T(8,128)(2,1)S(1)}, u32[]{:S(2)}, u32[]{:S(2)}) collective-permute-start(bf16[2,3,32,128]{3,2,1,0:T(8,128)(2,1)S(1)} %shard_map.126.refs_5_), channel_id=1, source_target_pairs={{0,4},{4,0},{8,12},{12,8},{1,5},{5,1},{9,13},{13,9},{2,6},{6,2},{1... | collective-permute-start | bytes 147464 | tf_op jit(solution)/shard_map/ppermute | solution.py:57
  42.8 6.0 %collective-permute-start.13 = (bf16[2,3,32,128]{3,2,1,0:T(8,128)(2,1)S(1)}, bf16[2,3,32,128]{3,2,1,0:T(8,128)(2,1)S(1)}, u32[]{:S(2)}, u32[]{:S(2)}) collective-permute-start(bf16[2,3,32,128]{3,2,1,0:T(8,128)(2,1)S(1)} %shard_map.126.refs_5_), channel_id=1, source_target_pairs={{0,8},{4,12},{8,0},{12,4},{1,9},{5,13},{9,1},{13,5},{2,10},{6,14},... | collective-permute-start | bytes 147464 | tf_op jit(solution)/shard_map/ppermute | solution.py:57
  45.2 5.9 %collective-permute-start.14 = (bf16[2,3,32,128]{3,2,1,0:T(8,128)(2,1)S(1)}, bf16[2,3,32,128]{3,2,1,0:T(8,128)(2,1)S(1)}, u32[]{:S(2)}, u32[]{:S(2)}) collective-permute-start(bf16[2,3,32,128]{3,2,1,0:T(8,128)(2,1)S(1)} %shard_map.126.refs_5_), channel_id=1, source_target_pairs={{0,12},{4,8},{8,4},{12,0},{1,13},{5,9},{9,5},{13,1},{2,14},{6,10},... | collective-permute-start | bytes 147464 | tf_op jit(solution)/shard_map/ppermute | solution.py:57
  53.0 2.0 %collective-permute-start.15 = (bf16[2,3,32,128]{3,2,1,0:T(8,128)(2,1)S(1)}, bf16[2,3,32,128]{3,2,1,0:T(8,128)(2,1)S(1)}, u32[]{:S(2)}, u32[]{:S(2)}) collective-permute-start(bf16[2,3,32,128]{3,2,1,0:T(8,128)(2,1)S(1)} %get-tuple-element.65), channel_id=1, source_target_pairs={{0,1},{1,0},{2,3},{3,2},{4,5},{5,4},{6,7},{7,6},{8,9},{9,8},{10,11... | collective-permute-start | bytes 147464 | tf_op jit(solution)/shard_map/ppermute | solution.py:57
  53.0 4.4 %collective-permute-start.16 = (bf16[2,3,32,128]{3,2,1,0:T(8,128)(2,1)S(1)}, bf16[2,3,32,128]{3,2,1,0:T(8,128)(2,1)S(1)}, u32[]{:S(2)}, u32[]{:S(2)}) collective-permute-start(bf16[2,3,32,128]{3,2,1,0:T(8,128)(2,1)S(1)} %get-tuple-element.66), channel_id=1, source_target_pairs={{0,2},{1,3},{2,0},{3,1},{4,6},{5,7},{6,4},{7,5},{8,10},{9,11},{10,... | collective-permute-start | bytes 147464 | tf_op jit(solution)/shard_map/ppermute | solution.py:57
  54.0 3.9 %collective-permute-start.17 = (bf16[2,3,32,128]{3,2,1,0:T(8,128)(2,1)S(1)}, bf16[2,3,32,128]{3,2,1,0:T(8,128)(2,1)S(1)}, u32[]{:S(2)}, u32[]{:S(2)}) collective-permute-start(bf16[2,3,32,128]{3,2,1,0:T(8,128)(2,1)S(1)} %get-tuple-element.67), channel_id=1, source_target_pairs={{0,3},{1,2},{2,1},{3,0},{4,7},{5,6},{6,5},{7,4},{8,11},{9,10},{10,... | collective-permute-start | bytes 147464 | tf_op jit(solution)/shard_map/ppermute | solution.py:57
  58.7 5.7 %collective-permute-start.18 = (bf16[3,3,32,128]{3,2,1,0:T(8,128)(2,1)S(1)}, bf16[3,3,32,128]{3,2,1,0:T(8,128)(2,1)S(1)}, u32[]{:S(2)}, u32[]{:S(2)}) collective-permute-start(bf16[3,3,32,128]{3,2,1,0:T(8,128)(2,1)S(1)} %shard_map.128.mine), channel_id=1, source_target_pairs={{0,8},{4,12},{8,0},{12,4},{1,9},{5,13},{9,1},{13,5},{2,10},{6,14},... | collective-permute-start | bytes 221192 | tf_op jit(solution)/shard_map/ppermute | solution.py:57
  65.6 1.9 %collective-permute-start.19 = (bf16[2,3,32,128]{3,2,1,0:T(8,128)(2,1)S(1)}, bf16[2,3,32,128]{3,2,1,0:T(8,128)(2,1)S(1)}, u32[]{:S(2)}, u32[]{:S(2)}) collective-permute-start(bf16[2,3,32,128]{3,2,1,0:T(8,128)(2,1)S(1)} %get-tuple-element.77.refs_3_), channel_id=1, source_target_pairs={{0,1},{1,0},{2,3},{3,2},{4,5},{5,4},{6,7},{7,6},{8,9},{9,8},{10,11... | collective-permute-start | bytes 147464 | tf_op jit(solution)/shard_map/ppermute | solution.py:57
  65.6 4.2 %collective-permute-start.20 = (bf16[2,3,32,128]{3,2,1,0:T(8,128)(2,1)S(1)}, bf16[2,3,32,128]{3,2,1,0:T(8,128)(2,1)S(1)}, u32[]{:S(2)}, u32[]{:S(2)}) collective-permute-start(bf16[2,3,32,128]{3,2,1,0:T(8,128)(2,1)S(1)} %get-tuple-element.77.refs_3_), channel_id=1, source_target_pairs={{0,2},{1,3},{2,0},{3,1},{4,6},{5,7},{6,4},{7,5},{8,10},{9,11},{10,... | collective-permute-start | bytes 147464 | tf_op jit(solution)/shard_map/ppermute | solution.py:57
  66.8 3.7 %collective-permute-start.21 = (bf16[2,3,32,128]{3,2,1,0:T(8,128)(2,1)S(1)}, bf16[2,3,32,128]{3,2,1,0:T(8,128)(2,1)S(1)}, u32[]{:S(2)}, u32[]{:S(2)}) collective-permute-start(bf16[2,3,32,128]{3,2,1,0:T(8,128)(2,1)S(1)} %get-tuple-element.77.refs_3_), channel_id=1, source_target_pairs={{0,3},{1,2},{2,1},{3,0},{4,7},{5,6},{6,5},{7,4},{8,11},{9,10},{10,... | collective-permute-start | bytes 147464 | tf_op jit(solution)/shard_map/ppermute | solution.py:57
  71.9 4.9 %collective-permute-start.22 = (bf16[2,3,32,128]{3,2,1,0:T(8,128)(2,1)S(1)}, bf16[2,3,32,128]{3,2,1,0:T(8,128)(2,1)S(1)}, u32[]{:S(2)}, u32[]{:S(2)}) collective-permute-start(bf16[2,3,32,128]{3,2,1,0:T(8,128)(2,1)S(1)} %get-tuple-element.79), channel_id=1, source_target_pairs={{0,4},{4,0},{8,12},{12,8},{1,5},{5,1},{9,13},{13,9},{2,6},{6,2},{1... | collective-permute-start | bytes 147464 | tf_op jit(solution)/shard_map/ppermute | solution.py:57
  71.9 5.9 %collective-permute-start.23 = (bf16[2,3,32,128]{3,2,1,0:T(8,128)(2,1)S(1)}, bf16[2,3,32,128]{3,2,1,0:T(8,128)(2,1)S(1)}, u32[]{:S(2)}, u32[]{:S(2)}) collective-permute-start(bf16[2,3,32,128]{3,2,1,0:T(8,128)(2,1)S(1)} %get-tuple-element.80), channel_id=1, source_target_pairs={{0,8},{4,12},{8,0},{12,4},{1,9},{5,13},{9,1},{13,5},{2,10},{6,14},... | collective-permute-start | bytes 147464 | tf_op jit(solution)/shard_map/ppermute | solution.py:57
  74.7 5.9 %collective-permute-start.24 = (bf16[2,3,32,128]{3,2,1,0:T(8,128)(2,1)S(1)}, bf16[2,3,32,128]{3,2,1,0:T(8,128)(2,1)S(1)}, u32[]{:S(2)}, u32[]{:S(2)}) collective-permute-start(bf16[2,3,32,128]{3,2,1,0:T(8,128)(2,1)S(1)} %get-tuple-element.81), channel_id=1, source_target_pairs={{0,12},{4,8},{8,4},{12,0},{1,13},{5,9},{9,5},{13,1},{2,14},{6,10},... | collective-permute-start | bytes 147464 | tf_op jit(solution)/shard_map/ppermute | solution.py:57
  81.2 1.9 %collective-permute-start.25 = (bf16[2,3,32,128]{3,2,1,0:T(8,128)(2,1)S(1)}, bf16[2,3,32,128]{3,2,1,0:T(8,128)(2,1)S(1)}, u32[]{:S(2)}, u32[]{:S(2)}) collective-permute-start(bf16[2,3,32,128]{3,2,1,0:T(8,128)(2,1)S(1)} %get-tuple-element.83.refs_3_), channel_id=1, source_target_pairs={{0,1},{1,0},{2,3},{3,2},{4,5},{5,4},{6,7},{7,6},{8,9},{9,8},{10,11... | collective-permute-start | bytes 147464 | tf_op jit(solution)/shard_map/ppermute | solution.py:57
  81.3 4.2 %collective-permute-start.26 = (bf16[2,3,32,128]{3,2,1,0:T(8,128)(2,1)S(1)}, bf16[2,3,32,128]{3,2,1,0:T(8,128)(2,1)S(1)}, u32[]{:S(2)}, u32[]{:S(2)}) collective-permute-start(bf16[2,3,32,128]{3,2,1,0:T(8,128)(2,1)S(1)} %get-tuple-element.83.refs_3_), channel_id=1, source_target_pairs={{0,2},{1,3},{2,0},{3,1},{4,6},{5,7},{6,4},{7,5},{8,10},{9,11},{10,... | collective-permute-start | bytes 147464 | tf_op jit(solution)/shard_map/ppermute | solution.py:57
  82.6 3.7 %collective-permute-start.27 = (bf16[2,3,32,128]{3,2,1,0:T(8,128)(2,1)S(1)}, bf16[2,3,32,128]{3,2,1,0:T(8,128)(2,1)S(1)}, u32[]{:S(2)}, u32[]{:S(2)}) collective-permute-start(bf16[2,3,32,128]{3,2,1,0:T(8,128)(2,1)S(1)} %get-tuple-element.83.refs_3_), channel_id=1, source_target_pairs={{0,3},{1,2},{2,1},{3,0},{4,7},{5,6},{6,5},{7,4},{8,11},{9,10},{10,... | collective-permute-start | bytes 147464 | tf_op jit(solution)/shard_map/ppermute | solution.py:57
  87.6 4.8 %collective-permute-start.28 = (bf16[2,3,32,128]{3,2,1,0:T(8,128)(2,1)S(1)}, bf16[2,3,32,128]{3,2,1,0:T(8,128)(2,1)S(1)}, u32[]{:S(2)}, u32[]{:S(2)}) collective-permute-start(bf16[2,3,32,128]{3,2,1,0:T(8,128)(2,1)S(1)} %get-tuple-element.90), channel_id=1, source_target_pairs={{0,4},{4,0},{8,12},{12,8},{1,5},{5,1},{9,13},{13,9},{2,6},{6,2},{1... | collective-permute-start | bytes 147464 | tf_op jit(solution)/shard_map/ppermute | solution.py:57
  87.7 5.8 %collective-permute-start.29 = (bf16[2,3,32,128]{3,2,1,0:T(8,128)(2,1)S(1)}, bf16[2,3,32,128]{3,2,1,0:T(8,128)(2,1)S(1)}, u32[]{:S(2)}, u32[]{:S(2)}) collective-permute-start(bf16[2,3,32,128]{3,2,1,0:T(8,128)(2,1)S(1)} %get-tuple-element.91), channel_id=1, source_target_pairs={{0,8},{4,12},{8,0},{12,4},{1,9},{5,13},{9,1},{13,5},{2,10},{6,14},... | collective-permute-start | bytes 147464 | tf_op jit(solution)/shard_map/ppermute | solution.py:57
  89.8 5.9 %collective-permute-start.30 = (bf16[2,3,32,128]{3,2,1,0:T(8,128)(2,1)S(1)}, bf16[2,3,32,128]{3,2,1,0:T(8,128)(2,1)S(1)}, u32[]{:S(2)}, u32[]{:S(2)}) collective-permute-start(bf16[2,3,32,128]{3,2,1,0:T(8,128)(2,1)S(1)} %get-tuple-element.92), channel_id=1, source_target_pairs={{0,12},{4,8},{8,4},{12,0},{1,13},{5,9},{9,5},{13,1},{2,14},{6,10},... | collective-permute-start | bytes 147464 | tf_op jit(solution)/shard_map/ppermute | solution.py:57
  96.4 1.9 %collective-permute-start.31 = (bf16[2,3,48,128]{3,2,1,0:T(8,128)(2,1)S(1)}, bf16[2,3,48,128]{3,2,1,0:T(8,128)(2,1)S(1)}, u32[]{:S(2)}, u32[]{:S(2)}) collective-permute-start(bf16[2,3,48,128]{3,2,1,0:T(8,128)(2,1)S(1)} %shard_map.133.refs_6_.refs_1_), channel_id=1, source_target_pairs={{0,1},{1,0},{2,3},{3,2},{4,5},{5,4},{6,7},{7,6},{8,9},{9,8},{10,11... | collective-permute-start | bytes 221192 | tf_op jit(solution)/shard_map/ppermute | solution.py:57
  96.5 5.2 %collective-permute-start.32 = (bf16[2,3,48,128]{3,2,1,0:T(8,128)(2,1)S(1)}, bf16[2,3,48,128]{3,2,1,0:T(8,128)(2,1)S(1)}, u32[]{:S(2)}, u32[]{:S(2)}) collective-permute-start(bf16[2,3,48,128]{3,2,1,0:T(8,128)(2,1)S(1)} %shard_map.133.refs_6_.refs_1_), channel_id=1, source_target_pairs={{0,2},{1,3},{2,0},{3,1},{4,6},{5,7},{6,4},{7,5},{8,10},{9,11},{10,... | collective-permute-start | bytes 221192 | tf_op jit(solution)/shard_map/ppermute | solution.py:57
  97.8 4.5 %collective-permute-start.33 = (bf16[2,3,48,128]{3,2,1,0:T(8,128)(2,1)S(1)}, bf16[2,3,48,128]{3,2,1,0:T(8,128)(2,1)S(1)}, u32[]{:S(2)}, u32[]{:S(2)}) collective-permute-start(bf16[2,3,48,128]{3,2,1,0:T(8,128)(2,1)S(1)} %shard_map.133.refs_6_.refs_1_), channel_id=1, source_target_pairs={{0,3},{1,2},{2,1},{3,0},{4,7},{5,6},{6,5},{7,4},{8,11},{9,10},{10,... | collective-permute-start | bytes 221192 | tf_op jit(solution)/shard_map/ppermute | solution.py:57
  103.4 5.2 %collective-permute-start.34 = (f32[64,128]{1,0:T(8,128)S(1)}, f32[64,128]{1,0:T(8,128)S(1)}, u32[]{:S(2)}, u32[]{:S(2)}) collective-permute-start(f32[64,128]{1,0:T(8,128)S(1)} %shard_map.135), channel_id=1, source_target_pairs={{0,4},{4,0},{8,12},{12,8},{1,5},{5,1},{9,13},{13,9},{2,6},{6,2},{1... | collective-permute-start | bytes 98312 | tf_op jit(solution)/shard_map/ppermute | solution.py:57

commit v2 on v0

v2 whole, which is shorter than its diff:
```python
import functools

import jax
import jax.numpy as jnp
from jax import lax
from jax.experimental import pallas as pl
from jax.experimental.pallas import tpu as pltpu
from jax.sharding import PartitionSpec as P

BLOCK = 128
CODES = 16
F32 = jnp.float32
BF16 = jnp.bfloat16
VMEM = pl.BlockSpec(memory_space=pltpu.VMEM)
SMEM = pl.BlockSpec(memory_space=pltpu.SMEM)
ANY = pl.BlockSpec(memory_space=pl.ANY)


class Sizes:
    def __init__(self, row_count, col_count, batch, local, slots, types, channels, steps):
        self.rows, self.cols = row_count, col_count
        self.batch, self.local, self.slots = batch, local, slots
        self.types, self.channels, self.steps = types, channels, steps
        self.post = col_count * local // BLOCK
        self.pre = row_count * local // BLOCK
        self.half = row_count // 2
        self.full, self.rest = local // BLOCK, local % BLOCK
        self.groups = BLOCK // self.rest
        self.tall = batch // self.groups
        self.piece = self.full * batch + self.tall
        self.pair = 2 * self.piece
        offsets = [local * i % BLOCK for i in range(max(row_count, col_count))]
        self.frame = (max(offsets) + local + BLOCK - 1) // BLOCK
        self.wide = self.frame * BLOCK
        assert BLOCK % self.rest == 0 and batch % (8 * self.groups) == 0
        assert self.frame == self.full + 1 and self.pair % 16 == 0

    def first(self, i):
        return lax.div(i * self.local, jnp.int32(BLOCK))

    def offset(self, i):
        return lax.rem(i * self.local, jnp.int32(BLOCK))

    def pack(self, whole):
        parts = [whole[:, i * BLOCK : (i + 1) * BLOCK] for i in range(self.full)]
        tail = whole[:, self.full * BLOCK :]
        lanes = lax.broadcasted_iota(jnp.int32, (self.tall, BLOCK), 1)
        joined = tail[0 : self.tall]
        for g in range(1, self.groups):
            moved = pltpu.roll(tail[g * self.tall : (g + 1) * self.tall], g * self.rest, 1)
            joined = jnp.where(lanes < g * self.rest, joined, moved)
        return jnp.concatenate(parts + [joined], axis=0)

    def unpack(self, piece):
        parts = [piece[i * self.batch : (i + 1) * self.batch] for i in range(self.full)]
        joined = piece[self.full * self.batch :]
        lanes = lax.broadcasted_iota(jnp.int32, (self.tall, BLOCK), 1)
        tails = []
        for g in range(self.groups):
            moved = joined if g == 0 else pltpu.roll(joined, BLOCK - g * self.rest, 1)
            tails.append(jnp.where(lanes < self.rest, moved, 0.0))
        return jnp.concatenate(parts + [jnp.concatenate(tails, axis=0)], axis=1)

    def add_blocks(self, target, base, i, piece):
        turned = pltpu.roll(self.unpack(piece), self.offset(i), 1)
        first = base + self.first(i)
        for f in range(self.frame):
            target[first + f] += turned[:, f * BLOCK : (f + 1) * BLOCK]

    def take_blocks(self, source, base, i):
        first = base + self.first(i)
        whole = jnp.concatenate([source[first + f] for f in range(self.frame)], axis=1)
        back = lax.rem(self.wide - self.offset(i), jnp.int32(self.wide))
        return self.pack(pltpu.roll(whole, back, 1))


def call(body, outs, scratch, ins, places=None, flops=0, out_specs=None):
    specs = [(places or {}).get(i, VMEM) for i in range(len(ins))]
    moved = sum(x.size * x.dtype.itemsize for x in ins) + sum(x.size * x.dtype.itemsize for x in outs)
    return pl.pallas_call(
        body,
        out_shape=outs,
        in_specs=specs,
        out_specs=out_specs or [VMEM] * len(outs),
        scratch_shapes=scratch,
        cost_estimate=pl.CostEstimate(flops=flops, bytes_accessed=moved, transcendentals=0),
        compiler_params=pltpu.CompilerParams(vmem_limit_bytes=24 * 1024 * 1024),
    )(*ins)


def shape(dims, kind=F32):
    return jax.ShapeDtypeStruct(tuple(dims), kind)


def flip(x, axis, k):
    count = lax.axis_size(axis)
    return lax.ppermute(x, axis, [(i, i ^ k) for i in range(count)])


def few(count):
    return count <= 4


def near(axis, count):
    size = lax.axis_size(axis)
    return [list(range(i, i + count)) for i in range(0, size, count)]


def share(x, axis, count):
    if few(count):
        return [flip(x, axis, k) for k in range(1, count)]
    return [lax.all_gather(x, axis, axis_index_groups=near(axis, count))]


def exchange(parts, axis, count):
    if few(count):
        return [flip(parts[k - 1], axis, k) for k in range(1, count)]
    return [lax.all_to_all(parts[0], axis, 0, 0, axis_index_groups=near(axis, count), tiled=True)]


def parcel(count, dims, kind):
    if few(count):
        return [shape(dims, kind)] * (count - 1)
    return [shape((count, *dims), kind)]


def away(refs, count, me, k):
    return refs[k - 1] if few(count) else refs[0].at[(me ^ k) & (count - 1)]


def place():
    return lax.axis_index("row"), lax.axis_index("col")


def loop(count, body):
    lax.fori_loop(0, count, lambda i, c: (body(i), c)[1], 0, unroll=count <= 18)


def start_kernel(z, rates, types, inputs, message, pad, codes):
    pad[...] = jnp.zeros_like(pad)
    pad[:, 0 : z.local] = rates[...]
    codes[...] = jnp.zeros_like(codes)
    t = types[...].reshape(1, z.local)
    m = inputs[...].reshape(1, z.local)
    rows = [
        lax.shift_right_logical(t, 7) + 1,
        t & 127,
        lax.shift_right_logical(m, 7) + 1,
        m & 127,
    ]
    for r, row in enumerate(rows):
        codes[r : r + 1, 0 : z.local] = row.astype(F32)
    code = codes[...]
    blocks = [code[0:4, f * BLOCK : (f + 1) * BLOCK] for f in range(z.frame)]
    fill = message.shape[0] - z.piece - 4 * z.frame
    extra = jnp.concatenate(blocks + [jnp.zeros((fill, BLOCK), F32)], axis=0)
    message[...] = jnp.concatenate([z.pack(pad[...]), extra], axis=0).astype(BF16)


def load_kernel(z, after, owner, post, pre, weights, out, ids, sem):
    del after
    copy = pltpu.make_async_copy(weights.at[0, 0], out, sem)
    copy.start()

    def one(s, carry):
        ids[s] = owner[0, 0, s] * z.post + post[0, 0, s]
        ids[z.slots + s] = pre[0, 0, s]
        return carry

    lax.fori_loop(0, z.slots, one, 0, unroll=8)
    copy.wait()


def prepare_kernel(z, mine, theirs, rates, cots, table, stimuli, pair_rates, gain, drive, cot_out, pad):
    highs = z.types // BLOCK
    t = jnp.transpose(table[...])
    t1 = t.astype(BF16)
    t2 = (t - t1.astype(F32)).astype(BF16)
    t3 = (t - t1.astype(F32) - t2.astype(F32)).astype(BF16)
    high_ids = lax.broadcasted_iota(jnp.int32, (highs, BLOCK), 0).astype(F32) + 1.0
    low_ids = lax.broadcasted_iota(jnp.int32, (BLOCK, BLOCK), 0).astype(F32)
    channel_ids = lax.broadcasted_iota(jnp.int32, (z.channels, BLOCK), 0).astype(F32)
    stim = stimuli[...]
    for side, ref in enumerate((mine, theirs)):
        rows = slice(side * z.piece, (side + 1) * z.piece)
        message = ref[...].astype(F32)
        gains, drives = [], []
        for f in range(z.frame):
            at = z.piece + 4 * f
            codes = message[at : at + 4]
            pick = (high_ids == codes[0:1]).astype(BF16)
            got = sum(jnp.dot(x, pick, preferred_element_type=F32) for x in (t1, t2, t3))
            mine_only = jnp.where(low_ids == codes[1:2], got, 0.0)
            line = jnp.sum(mine_only, axis=0, keepdims=True)
            gains.append(jnp.broadcast_to(line, (z.batch, BLOCK)))
            channel = (codes[2:3] - 1.0) * BLOCK + codes[3:4]
            chosen = (channel_ids == channel).astype(BF16)
            drives.append(jnp.dot(stim, chosen, preferred_element_type=F32))
        gain[rows] = z.pack(jnp.concatenate(gains, axis=1))
        for step in range(z.steps):
            part = [d[step * z.batch : (step + 1) * z.batch] for d in drives]
            drive[step, rows] = z.pack(jnp.concatenate(part, axis=1))
        if side == 1:
            pair_rates[rows] = message[0 : z.piece]
    pad[...] = jnp.zeros_like(pad)
    pad[:, 0 : z.local] = rates[...]
    pair_rates[0 : z.piece] = z.pack(pad[...])
    for step in range(z.steps):
        pad[:, 0 : z.local] = cots[step]
        cot_out[step] = z.pack(pad[...])


def multiply_forward(z, c, ids, weights, x, total, own, parts):
    total[...] = jnp.zeros_like(total)
    for s in range(z.slots):
        total[ids[s]] += lax.dot_general(
            x[ids[z.slots + s]], weights[s], (((1,), (1,)), ((), ())), preferred_element_type=F32
        )
    for k in range(z.cols):
        both = jnp.concatenate(
            [z.take_blocks(total, 0, c ^ k), z.take_blocks(total, z.post, c ^ k)], axis=0
        )
        if k == 0:
            own[...] = both
        else:
            away(parts, z.cols, c, k)[...] = both.astype(BF16)


def first_kernel(z, count, *refs):
    ids, weights, mine = refs[:3]
    got = refs[3 : 3 + count]
    x, own = refs[3 + count : 5 + count]
    parts, (sums, total) = refs[5 + count : -2], refs[-2:]
    p, c = place()
    sums[...] = jnp.zeros_like(sums)
    for k in range(z.rows):
        ref = mine if k == 0 else away(got, z.rows, p, k)
        z.add_blocks(sums, 0, p ^ k, ref[...].astype(F32)[0 : z.piece])
    x[...] = sums[...].astype(BF16)
    multiply_forward(z, c, ids, weights, x, total, own, parts)


def forward_kernel(z, count, *refs):
    ids, weights, mine = refs[:3]
    got = refs[3 : 3 + count]
    x, own = refs[3 + count : 5 + count]
    parts, (sums, total) = refs[5 + count : -2], refs[-2:]
    p, c = place()
    sums[...] = jnp.zeros_like(sums)
    for k in range(z.half):
        pair = (mine if k == 0 else away(got, z.half, p, k))[...].astype(F32)
        z.add_blocks(sums, 0, p ^ k, pair[0 : z.piece])
        z.add_blocks(sums, 0, p ^ k ^ z.half, pair[z.piece :])
    x[...] = sums[...].astype(BF16)
    multiply_forward(z, c, ids, weights, x, total, own, parts)


def sum_kernel(z, count, with_cot, *refs):
    own, got = refs[0], refs[1 : 1 + count]
    kept, message = refs[-2:]
    _, c = place()
    total = own[...]
    for k in range(1, z.cols):
        total = total + away(got, z.cols, c, k)[...].astype(F32)
    kept[...] = total
    if with_cot:
        cot = refs[1 + count]
        fill = message.shape[0] - z.pair - z.piece
        parts = [total, cot[z.steps - 1], jnp.zeros((fill, BLOCK), F32)]
        total = jnp.concatenate(parts, axis=0)
    message[...] = total.astype(BF16)


def currents(z, kept, theirs, drive):
    other = theirs[...].astype(F32)
    swapped = jnp.concatenate([other[z.piece : z.pair], other[0 : z.piece]], axis=0)
    own = kept[0 : z.piece] + swapped[0 : z.piece]
    partner = kept[z.piece :] + swapped[z.piece :]
    return jnp.concatenate([own, partner], axis=0) + drive, other


def rate_kernel(z, step, kept, theirs, rates, gain, drive, new, act, cur, lowered):
    current, _ = currents(z, kept, theirs, drive[step])
    activity = jnp.tanh(gain[...] * current)
    fresh = 0.5 * rates[...] + 0.5 * activity
    new[...] = fresh
    act[...] = activity
    cur[...] = current
    lowered[...] = fresh.astype(BF16)


def turn_kernel(z, kept, theirs, rates, gain, drive, cots, final, message, tally, base):
    current, other = currents(z, kept, theirs, drive[z.steps - 1])
    activity = jnp.tanh(gain[...] * current)
    fresh = 0.5 * rates[0 : z.piece] + 0.5 * activity[0 : z.piece]
    final[...] = z.unpack(fresh)[:, 0 : z.local]
    mine = cots[z.steps - 1]
    adjoint = jnp.concatenate([mine, other[z.pair : z.pair + z.piece]], axis=0)
    pressure = adjoint * 0.5 * (1.0 - activity * activity)
    message[...] = (gain[...] * pressure).astype(BF16)
    tally[...] = pressure * current
    base[...] = cots[z.steps - 2] + 0.5 * mine


def gather_post(z, c, mine, got, sums, d):
    sums[...] = jnp.zeros_like(sums)
    for k in range(z.cols):
        pair = (mine if k == 0 else away(got, z.cols, c, k))[...].astype(F32)
        z.add_blocks(sums, 0, c ^ k, pair[0 : z.piece])
        z.add_blocks(sums, z.post, c ^ k, pair[z.piece : z.pair])
    d[...] = sums[...].astype(BF16)


def back_kernel(z, count, *refs):
    ids, weights, mine = refs[:3]
    got = refs[3 : 3 + count]
    d, own = refs[3 + count : 5 + count]
    parts, (sums, total) = refs[5 + count : -2], refs[-2:]
    p, c = place()
    gather_post(z, c, mine, got, sums, d)
    total[...] = jnp.zeros_like(total)
    for s in range(z.slots):
        total[ids[z.slots + s]] += jnp.dot(d[ids[s]], weights[s], preferred_element_type=F32)
    for k in range(z.half):
        both = jnp.concatenate(
            [z.take_blocks(total, 0, p ^ k), z.take_blocks(total, 0, p ^ k ^ z.half)], axis=0
        )
        if k == 0:
            own[...] = both
        else:
            away(parts, z.half, p, k)[...] = both.astype(BF16)


def near_kernel(z, count, *refs):
    own, base, got = refs[0], refs[1], refs[2 : 2 + count]
    kept, message = refs[-2:]
    p, _ = place()
    total = own[...]
    for k in range(1, z.half):
        total = total + away(got, z.half, p, k)[...].astype(F32)
    total = jnp.concatenate([total[0 : z.piece] + base[...], total[z.piece :]], axis=0)
    kept[...] = total
    message[...] = total.astype(BF16)


def adjoints(z, kept, theirs):
    other = theirs[...].astype(F32)
    return kept[...] + jnp.concatenate([other[z.piece :], other[0 : z.piece]], axis=0)


def delta_kernel(z, before, kept, theirs, gain, act, cur, tally_in, cots, message, tally, base):
    adjoint = adjoints(z, kept, theirs)
    activity = act[...]
    pressure = adjoint * 0.5 * (1.0 - activity * activity)
    message[...] = (gain[...] * pressure).astype(BF16)
    tally[...] = tally_in[...] + pressure * cur[...]
    base[...] = cots[before - 1] + 0.5 * adjoint[0 : z.piece]


def last_delta_kernel(z, kept, theirs, gain, act, cur, tally_in, mine, partner, message):
    adjoint = adjoints(z, kept, theirs)
    activity = act[...]
    pressure = adjoint * 0.5 * (1.0 - activity * activity)
    tally = tally_in[...] + pressure * cur[...]
    rows = [gain[...] * pressure]
    lanes = lax.broadcasted_iota(jnp.int32, (1, BLOCK), 1)
    for side, ref in enumerate((mine, partner)):
        codes = ref[...].astype(F32)[z.piece :]
        begin = side * z.piece
        for f in range(z.frame):
            if f < z.full:
                at = begin + f * z.batch
                g = jnp.sum(tally[at : at + z.batch], axis=0, keepdims=True)
            else:
                at = begin + f * z.batch
                packed = jnp.sum(tally[at : at + z.tall], axis=0, keepdims=True)
                g = packed
                for i in range(1, z.groups):
                    g = g + pltpu.roll(packed, BLOCK - i * z.rest, 1)
                g = jnp.where(lanes < z.rest, g, 0.0)
            g1 = g.astype(BF16).astype(F32)
            g2 = (g - g1).astype(BF16).astype(F32)
            rows += [codes[4 * f : 4 * f + 2], g1, g2, g - g1 - g2]
        rows.append(jnp.zeros((CODES - 5 * z.frame, BLOCK), F32))
    message[...] = jnp.concatenate(rows, axis=0).astype(BF16)


def table_kernel(z, count, *refs):
    mine, got, out = refs[0], refs[1:-1], refs[-1]
    _, c = place()
    highs = z.types // BLOCK
    high_ids = lax.broadcasted_iota(jnp.int32, (highs, BLOCK), 0).astype(F32) + 1.0
    low_ids = lax.broadcasted_iota(jnp.int32, (BLOCK, BLOCK), 0).astype(F32)
    total = jnp.zeros((3 * highs, BLOCK), F32)
    for k in range(z.cols):
        ref = mine if k == 0 else away(got, z.cols, c, k)
        extra = ref[z.pair :].astype(F32)
        for side in range(2):
            for f in range(z.frame):
                at = side * CODES + 5 * f
                hit = high_ids == extra[at : at + 1]
                terms = [jnp.where(hit, extra[at + 2 + i : at + 3 + i], 0.0) for i in range(3)]
                left = jnp.concatenate(terms, axis=0).astype(BF16)
                right = (low_ids == extra[at + 1 : at + 2]).astype(BF16)
                total = total + lax.dot_general(
                    left, right, (((1,), (1,)), ((), ())), preferred_element_type=F32
                )
    out[...] = total[0:highs] + total[highs : 2 * highs] + total[2 * highs :]


def grad_kernel(z, count, per_step, *refs):
    ids, xs, ds = refs[0], refs[1 : 1 + z.steps], refs[1 + z.steps : 2 * z.steps]
    mine, got = refs[2 * z.steps], refs[2 * z.steps + 1 : 2 * z.steps + 1 + count]
    out = refs[2 * z.steps + 1 + count]
    sums, d0, right, left = refs[2 * z.steps + 2 + count :]
    n = z.batch
    deep = right.shape[1]

    @pl.when(pl.program_id(0) == 0)
    def _():
        _, c = place()
        gather_post(z, c, mine, got, sums, d0)

        def lay_right(q):
            for t in range(z.steps):
                right[q, t * n : (t + 1) * n] = xs[t][q]
            if deep > z.steps * n:
                right[q, z.steps * n :] = jnp.zeros((deep - z.steps * n, BLOCK), BF16)

        loop(z.pre, lay_right)

        def lay_left(q):
            parts = [d0[q].astype(F32)] + [d[q].astype(F32) for d in ds]
            if deep > z.steps * n:
                parts.append(jnp.zeros((deep - z.steps * n, BLOCK), F32))
            left[q] = jnp.transpose(jnp.concatenate(parts, axis=0)).astype(BF16)

        loop(2 * z.post, lay_left)

    begin = pl.program_id(0) * per_step
    for s in range(per_step):
        product = jnp.dot(
            left[ids[begin + s]], right[ids[z.slots + begin + s]], preferred_element_type=F32
        )
        out[s] = product.astype(BF16)


def shards(
    initial_rates,
    stimuli,
    cotangent,
    weight_blocks,
    slot_owner,
    slot_post,
    slot_pre,
    cell_type,
    type_gain,
    input_map,
):
    batch, local = initial_rates.shape
    slots = weight_blocks.shape[2]
    steps, _, channels = stimuli.shape
    types = type_gain.shape[0]
    z = Sizes(
        lax.axis_size("row"), lax.axis_size("col"), batch, local, slots, types, channels, steps
    )
    pair = (z.pair, BLOCK)
    product_flops = 2 * slots * batch * BLOCK * BLOCK
    opening = (z.piece + 4 * z.frame + 15) // 16 * 16
    closing = (z.pair + z.piece + 15) // 16 * 16

    (message,) = call(
        functools.partial(start_kernel, z),
        [shape((opening, BLOCK), BF16)],
        [pltpu.VMEM((batch, z.wide), F32), pltpu.VMEM((8, z.wide), F32)],
        [initial_rates, cell_type, input_map],
    )
    got = share(message, "row", z.rows)
    weights, ids = call(
        functools.partial(load_kernel, z),
        [shape((slots, BLOCK, BLOCK), BF16), shape((2 * slots,), jnp.int32)],
        [pltpu.SemaphoreType.DMA],
        [message, slot_owner, slot_post, slot_pre, weight_blocks],
        {1: SMEM, 2: SMEM, 3: SMEM, 4: ANY},
        out_specs=[VMEM, SMEM],
    )
    if few(z.rows):
        partner_message = got[z.half - 1]
    else:
        partner_message = flip(message, "row", z.half)
    pre_sums = pltpu.VMEM((z.pre, batch, BLOCK), F32)
    post_sums = pltpu.VMEM((2 * z.post, batch, BLOCK), F32)
    x_shape = shape((z.pre, batch, BLOCK), BF16)
    col_parts = parcel(z.cols, pair, BF16)
    row_parts = parcel(z.half, pair, BF16)
    x, own, *parts = call(
        functools.partial(first_kernel, z, len(got)),
        [x_shape, shape(pair), *col_parts],
        [pre_sums, post_sums],
        [ids, weights, message, *got],
        {0: SMEM},
        flops=product_flops,
    )
    rates, gain, drive, cots = call(
        functools.partial(prepare_kernel, z),
        [shape(pair), shape(pair), shape((steps, *pair)), shape((steps, z.piece, BLOCK))],
        [pltpu.VMEM((batch, z.wide), F32)],
        [
            message,
            partner_message,
            initial_rates,
            cotangent,
            type_gain.reshape(types // BLOCK, BLOCK),
            stimuli.reshape(steps * batch, channels),
        ],
    )
    xs, acts, curs = [x], [], []
    for t in range(steps):
        last = t == steps - 1
        got = exchange(parts, "col", z.cols)
        kept, sent = call(
            functools.partial(sum_kernel, z, len(got), last),
            [shape(pair), shape((closing, BLOCK) if last else pair, BF16)],
            [],
            [own, *got] + ([cots] if last else []),
        )
        theirs = flip(sent, "row", z.half)
        if last:
            break
        rates, act, cur, lowered = call(
            functools.partial(rate_kernel, z, t),
            [shape(pair), shape(pair), shape(pair), shape(pair, BF16)],
            [],
            [kept, theirs, rates, gain, drive],
        )
        got = share(lowered, "row", z.half)
        x, own, *parts = call(
            functools.partial(forward_kernel, z, len(got)),
            [x_shape, shape(pair), *col_parts],
            [pre_sums, post_sums],
            [ids, weights, lowered, *got],
            {0: SMEM},
            flops=product_flops,
        )
        xs.append(x)
        acts.append(act)
        curs.append(cur)
    final_rates, delta, tally, base = call(
        functools.partial(turn_kernel, z),
        [shape((batch, local)), shape(pair, BF16), shape(pair), shape((z.piece, BLOCK))],
        [],
        [kept, theirs, rates, gain, drive, cots],
    )
    ds = []
    for t in reversed(range(1, steps)):
        got = share(delta, "col", z.cols)
        d, own, *parts = call(
            functools.partial(back_kernel, z, len(got)),
            [shape((2 * z.post, batch, BLOCK), BF16), shape(pair), *row_parts],
            [post_sums, pre_sums],
            [ids, weights, delta, *got],
            {0: SMEM},
            flops=product_flops,
        )
        ds.insert(0, d)
        got = exchange(parts, "row", z.half)
        kept, sent = call(
            functools.partial(near_kernel, z, len(got)),
            [shape(pair), shape(pair, BF16)],
            [],
            [own, base, *got],
        )
        theirs = flip(sent, "row", z.half)
        before = t - 1
        if before > 0:
            delta, tally, base = call(
                functools.partial(delta_kernel, z, before),
                [shape(pair, BF16), shape(pair), shape((z.piece, BLOCK))],
                [],
                [kept, theirs, gain, acts[before], curs[before], tally, cots],
            )
        else:
            (delta,) = call(
                functools.partial(last_delta_kernel, z),
                [shape((z.pair + 2 * CODES, BLOCK), BF16)],
                [],
                [kept, theirs, gain, acts[0], curs[0], tally, message, partner_message],
            )
    got = share(delta, "col", z.cols)
    (table,) = call(
        functools.partial(table_kernel, z, len(got)), [shape((types // BLOCK, BLOCK))], [], [delta, *got]
    )
    if z.half == 2:
        table = table + flip(table, "row", 1)
    else:
        table = 0.5 * lax.psum(table, "row")
    gain_grads = table.reshape(types)

    grid = 4
    per_step = slots // grid
    deep = (steps * batch + BLOCK - 1) // BLOCK * BLOCK
    ins = [ids, *xs, *ds, delta, *got]
    weight_grads = pl.pallas_call(
        functools.partial(grad_kernel, z, len(got), per_step),
        grid=(grid,),
        out_shape=shape((slots, BLOCK, BLOCK), BF16),
        in_specs=[SMEM] + [VMEM] * (len(ins) - 1),
        out_specs=pl.BlockSpec((per_step, BLOCK, BLOCK), lambda i: (i, 0, 0)),
        scratch_shapes=[
            post_sums,
            pltpu.VMEM((2 * z.post, batch, BLOCK), BF16),
            pltpu.VMEM((z.pre, deep, BLOCK), BF16),
            pltpu.VMEM((2 * z.post, BLOCK, deep), BF16),
        ],
        cost_estimate=pl.CostEstimate(
            flops=2 * slots * deep * BLOCK * BLOCK, bytes_accessed=4 * 1024 * 1024, transcendentals=0
        ),
        compiler_params=pltpu.CompilerParams(vmem_limit_bytes=24 * 1024 * 1024),
    )(*ins)
    return (final_rates, weight_grads.reshape(1, 1, slots, BLOCK, BLOCK), gain_grads)


def solution(mesh):
    in_specs = (
        P("groups", ("row", "col")),
        P(None, "groups", None),
        P(None, "groups", ("row", "col")),
        P("row", "col", None, None, None),
        P("row", "col", None),
        P("row", "col", None),
        P("row", "col", None),
        P(("row", "col")),
        P(),
        P(("row", "col")),
    )
    out_specs = (P("groups", ("row", "col")), P("row", "col", "groups", None, None), P("groups"))
    return jax.shard_map(shards, mesh=mesh, in_specs=in_specs, out_specs=out_specs, check_vma=False)
```

time: 359 us -> 101 us (0.28)
  blocking collectives: 117 us -> 0 us
  waiting for transfers between devices: 127 us -> 52 us
  other arithmetic: 42.8 us -> 0.62 us
  matrix products: 26.8 us -> 0 us
  starting transfers between devices: 6.23 us -> 24.4 us
  local copies, waits for them, and re-layouts: 23.2 us -> 5.72 us
  Pallas kernels: 0 us -> 16.9 us
  between operations: 14.2 us -> 0.81 us
    unnamed x10 -> x0, waiting for transfers between devices: 103 us -> none
    psum x1 -> x0, blocking collectives: 58.9 us -> none  [shards(): gain_grads = lax.psum(type_part, ('row', 'col'))]
    all_gather x6 -> x0, blocking collectives: 57.9 us -> none  [the longest x3 41.8 us: shards(): gathered = lax.all_gather(lowered, 'row', axis=1, tiled=True)]
    scatter-add x6 -> x0, other arithmetic: 34.1 us -> none  [the longest x3 18.4 us: shards(): jnp.zeros((batch_size, 2 * post_count, BLOCK), jnp.float32).at[:, both_ids]]
    ppermute x6 -> x31, waiting for transfers between devices: 24.4 us -> 52 us  [flip(): return lax.ppermute(x, axis, [(i, i ^ k) for i in range(count)])]
    dot_general x9 -> x0, matrix products: 26.8 us -> none  [the longest x3 13.5 us: shards(): jnp.einsum('bki,bkj->kij', selected, presyn, preferred_element_type=jnp.f...]
    ppermute x6 -> x31, starting transfers between devices: 6.02 us -> 24.4 us  [flip(): return lax.ppermute(x, axis, [(i, i ^ k) for i in range(count)])]
    pallas_call x0 -> x20, Pallas kernels: none -> 16.9 us  [the longest x19 13.4 us: call(): pl.pallas_call(body, out_shape=outs, in_specs=specs, out_specs=out_specs...]
  transfers between devices with their start and end apart: 11 -> 31, of which waited for: 10 -> 22; matrix products, arithmetic and copies ran while one was open for 4% -> 0% of each run, Pallas kernels for 0% -> 6%
where the time goes in v2:
time: 101 us; the launch traced here: 100 us
  waiting for transfers between devices  52 us (51%)
  starting transfers between devices  24.4 us (24%)
  Pallas kernels  16.9 us (17%)
  local copies, waits for them, and re-layouts  5.72 us (6%)
    ppermute x31, waiting for transfers between devices, flip(): return lax.ppermute(x, axis, [(i, i ^ k) for i in range(count)])  52 us
    ppermute x31, starting transfers between devices, flip(): return lax.ppermute(x, axis, [(i, i ^ k) for i in range(count)])  24.4 us
    pallas_call x19, Pallas kernels, call(): pl.pallas_call(body, out_shape=outs, in_specs=specs, out_specs=out_specs...  13.4 us
    unnamed x22, local copies, waits for them, and re-layouts  5.72 us
    pallas_call x1, Pallas kernels, shards(): pl.pallas_call(functools.partial(grad_kernel, z, len(got), per_step), gri...  3.56 us
  transfers between devices with their start and end apart: 31, of which 22 were waited for; matrix products, arithmetic and copies ran while one was open for 0% of the time, Pallas kernels for 6%

profile of v2, /device:TPU:0, one launch (start us, length us, event | category | flops | bytes accessed | tf_op | source)
XLA Modules:
  0.0 100.4 jit_solution(1400240492359650373)
XLA Ops:
  0.6 0.8 copy-done.1
  1.4 0.7 copy-done.6
  2.1 0.7 copy-done.7
  2.8 0.1 shard_map.121.after.refs_2_.mine
  2.9 5.1 %collective-permute-start.2 = (bf16[96,128]{1,0:T(8,128)(2,1)S(1)}, bf16[96,128]{1,0:T(8,128)(2,1)S(1)}, u32[]{:S(2)}, u32[]{:S(2)}) collective-permute-start(bf16[96,128]{1,0:T(8,128)(2,1)S(1)} %shard_map.121.after.refs_2_.mine), channel_id=1, source_target_pairs={{0,12},{4,8},{8,4},{12,0},{1,13},{5,9},{9,5},{13,1},{2,14},{6,10},... | collective-permute-start | bytes 73736 | tf_op jit(solution)/shard_map/ppermute | solution.py:97
  7.9 0.6 collective-permute-start
  8.6 1.6 %copy-done = bf16[1,1,64,128,128]{4,3,2,1,0:T(8,128)(2,1)S(1)} copy-done((bf16[1,1,64,128,128]{4,3,2,1,0:T(8,128)(2,1)S(1)}, bf16[1,1,64,128,128]{4,3,2,1,0:T(8,128)(2,1)}, u32[]{:S(2)}) %copy-start) | copy-done | bytes 2097176
  10.2 0.7 copy-done.8
  10.8 0.7 copy-done.9
  11.5 0.7 copy-done.10
  12.1 1.5 %shard_map.122 = (bf16[64,128,128]{2,1,0:T(8,128)(2,1)S(1)}, s32[128]{0:T(128)S(1)}) custom-call(bf16[96,128]{1,0:T(8,128)(2,1)S(1)} %shard_map.121.after.refs_2_.mine, s32[1,1,64]{2,1,0:T(1,128)S(1)} %copy-done.8, s32[1,1,64]{2,1,0:T(1,128)S(1)} %copy-done.9, s32[1,1,64]{2,1,0:T(1,128)S(1)} %copy-done.10, bf16[1,1,64,128,128]{4,3,2,1,0:T(8,128)(2,1)S(1)} %copy-done), custom_call_target="tpu_custom_call" | custom-call | bytes 4220160 | tf_op jit(solution)/shard_map/pallas_call | solution.py:80
  13.7 2.1 %shard_map.123 = (bf16[9,32,128]{2,1,0:T(8,128)(2,1)S(1)}, f32[144,128]{1,0:T(8,128)S(1)}, bf16[144,128]{1,0:T(8,128)(2,1)S(1)}, bf16[144,128]{1,0:T(8,128)(2,1)S(1)}, bf16[144,128]{1,0:T(8,128)(2,1)S(1)}) custom-call(s32[128]{0:T(128)S(1)} %get-tuple-element.55.refs_0_, bf16[64,128,128]{2,1,0:T(8,128)(2,1)S(1)} %get-tuple-element.56.refs_1_, ...), custom_call_target="tpu_custom_call" | custom-call | flops 67108864 | bytes 2454016 | tf_op jit(solution)/shard_map/pallas_call | solution.py:80
  15.9 1.7 %collective-permute-start.4 = (bf16[144,128]{1,0:T(8,128)(2,1)S(1)}, bf16[144,128]{1,0:T(8,128)(2,1)S(1)}, u32[]{:S(2)}, u32[]{:S(2)}) collective-permute-start(bf16[144,128]{1,0:T(8,128)(2,1)S(1)} %get-tuple-element.59), channel_id=1, source_target_pairs={{0,2},{1,3},{2,0},{3,1},{4,6},{5,7},{6,4},{7,5},{8,10},{9,11},{10,... | collective-permute-start | bytes 110600 | tf_op jit(solution)/shard_map/ppermute | solution.py:97
  17.6 0.2 collective-permute-start.5
  17.7 2.2 %collective-permute-done.4.refs_2_ = bf16[144,128]{1,0:T(8,128)(2,1)S(1)} collective-permute-done((bf16[144,128]{1,0:T(8,128)(2,1)S(1)}, bf16[144,128]{1,0:T(8,128)(2,1)S(1)}, u32[]{:S(2)}, u32[]{:S(2)}) %collective-permute-start.4) | collective-permute-done | bytes 36896 | tf_op jit(solution)/shard_map/ppermute | solution.py:97
  19.9 1.1 %collective-permute-done.5.refs_3_ = bf16[144,128]{1,0:T(8,128)(2,1)S(1)} collective-permute-done((bf16[144,128]{1,0:T(8,128)(2,1)S(1)}, bf16[144,128]{1,0:T(8,128)(2,1)S(1)}, u32[]{:S(2)}, u32[]{:S(2)}) %collective-permute-start.5) | collective-permute-done | bytes 36896 | tf_op jit(solution)/shard_map/ppermute | solution.py:97
  21.0 2.2 %collective-permute-start.6 = (bf16[144,128]{1,0:T(8,128)(2,1)S(1)}, bf16[144,128]{1,0:T(8,128)(2,1)S(1)}, u32[]{:S(2)}, u32[]{:S(2)}) collective-permute-start(bf16[144,128]{1,0:T(8,128)(2,1)S(1)} %get-tuple-element.62), channel_id=1, source_target_pairs={{0,8},{4,12},{8,0},{12,4},{1,9},{5,13},{9,1},{13,5},{2,10},{6,14},... | collective-permute-start | bytes 110600 | tf_op jit(solution)/shard_map/ppermute | solution.py:97
  23.2 0.6 shard_map.125
  23.8 2.9 %collective-permute-done.6.theirs = bf16[144,128]{1,0:T(8,128)(2,1)S(1)} collective-permute-done((bf16[144,128]{1,0:T(8,128)(2,1)S(1)}, bf16[144,128]{1,0:T(8,128)(2,1)S(1)}, u32[]{:S(2)}, u32[]{:S(2)}) %collective-permute-start.6) | collective-permute-done | bytes 36896 | tf_op jit(solution)/shard_map/ppermute | solution.py:97
  26.8 0.5 collective-permute-start.7
  27.3 3.5 %collective-permute-done.7.refs_3_ = bf16[144,128]{1,0:T(8,128)(2,1)S(1)} collective-permute-done((bf16[144,128]{1,0:T(8,128)(2,1)S(1)}, bf16[144,128]{1,0:T(8,128)(2,1)S(1)}, u32[]{:S(2)}, u32[]{:S(2)}) %collective-permute-start.7) | collective-permute-done | bytes 36896 | tf_op jit(solution)/shard_map/ppermute | solution.py:97
  30.8 2.1 %shard_map.127 = (bf16[9,32,128]{2,1,0:T(8,128)(2,1)S(1)}, f32[144,128]{1,0:T(8,128)S(1)}, bf16[144,128]{1,0:T(8,128)(2,1)S(1)}, bf16[144,128]{1,0:T(8,128)(2,1)S(1)}, bf16[144,128]{1,0:T(8,128)(2,1)S(1)}) custom-call(s32[128]{0:T(128)S(1)} %get-tuple-element.55.refs_0_, bf16[64,128,128]{2,1,0:T(8,128)(2,1)S(1)} %get-tuple-element.56.refs_1_, ...), custom_call_target="tpu_custom_call" | custom-call | flops 67108864 | bytes 2429440 | tf_op jit(solution)/shard_map/pallas_call | solution.py:80
  33.0 0.9 collective-permute-start.9
  33.8 1.0 %collective-permute-start.10 = (bf16[144,128]{1,0:T(8,128)(2,1)S(1)}, bf16[144,128]{1,0:T(8,128)(2,1)S(1)}, u32[]{:S(2)}, u32[]{:S(2)}) collective-permute-start(bf16[144,128]{1,0:T(8,128)(2,1)S(1)} %get-tuple-element.70), channel_id=1, source_target_pairs={{0,3},{1,2},{2,1},{3,0},{4,7},{5,6},{6,5},{7,4},{8,11},{9,10},{10,... | collective-permute-start | bytes 110600 | tf_op jit(solution)/shard_map/ppermute | solution.py:97
  34.8 2.3 %collective-permute-done.9.refs_2_ = bf16[144,128]{1,0:T(8,128)(2,1)S(1)} collective-permute-done((bf16[144,128]{1,0:T(8,128)(2,1)S(1)}, bf16[144,128]{1,0:T(8,128)(2,1)S(1)}, u32[]{:S(2)}, u32[]{:S(2)}) %collective-permute-start.9) | collective-permute-done | bytes 36896 | tf_op jit(solution)/shard_map/ppermute | solution.py:97
  37.2 0.4 collective-permute-done.10.refs_3_
  37.6 1.4 %collective-permute-start.11 = (bf16[144,128]{1,0:T(8,128)(2,1)S(1)}, bf16[144,128]{1,0:T(8,128)(2,1)S(1)}, u32[]{:S(2)}, u32[]{:S(2)}) collective-permute-start(bf16[144,128]{1,0:T(8,128)(2,1)S(1)} %get-tuple-element.72), channel_id=1, source_target_pairs={{0,8},{4,12},{8,0},{12,4},{1,9},{5,13},{9,1},{13,5},{2,10},{6,14},... | collective-permute-start | bytes 110600 | tf_op jit(solution)/shard_map/ppermute | solution.py:97
  39.1 3.8 %collective-permute-done.11.theirs = bf16[144,128]{1,0:T(8,128)(2,1)S(1)} collective-permute-done((bf16[144,128]{1,0:T(8,128)(2,1)S(1)}, bf16[144,128]{1,0:T(8,128)(2,1)S(1)}, u32[]{:S(2)}, u32[]{:S(2)}) %collective-permute-start.11) | collective-permute-done | bytes 36896 | tf_op jit(solution)/shard_map/ppermute | solution.py:97
  42.9 0.1 collective-permute-start.12
  43.0 3.9 %collective-permute-done.12.refs_3_ = bf16[144,128]{1,0:T(8,128)(2,1)S(1)} collective-permute-done((bf16[144,128]{1,0:T(8,128)(2,1)S(1)}, bf16[144,128]{1,0:T(8,128)(2,1)S(1)}, u32[]{:S(2)}, u32[]{:S(2)}) %collective-permute-start.12) | collective-permute-done | bytes 36896 | tf_op jit(solution)/shard_map/ppermute | solution.py:97
  47.0 2.1 %shard_map.130 = (bf16[9,32,128]{2,1,0:T(8,128)(2,1)S(1)}, f32[144,128]{1,0:T(8,128)S(1)}, bf16[144,128]{1,0:T(8,128)(2,1)S(1)}, bf16[144,128]{1,0:T(8,128)(2,1)S(1)}, bf16[144,128]{1,0:T(8,128)(2,1)S(1)}) custom-call(s32[128]{0:T(128)S(1)} %get-tuple-element.55.refs_0_, bf16[64,128,128]{2,1,0:T(8,128)(2,1)S(1)} %get-tuple-element.56.refs_1_, ...), custom_call_target="tpu_custom_call" | custom-call | flops 67108864 | bytes 2429440 | tf_op jit(solution)/shard_map/pallas_call | solution.py:80
  49.1 1.0 %collective-permute-start.14 = (bf16[144,128]{1,0:T(8,128)(2,1)S(1)}, bf16[144,128]{1,0:T(8,128)(2,1)S(1)}, u32[]{:S(2)}, u32[]{:S(2)}) collective-permute-start(bf16[144,128]{1,0:T(8,128)(2,1)S(1)} %get-tuple-element.77), channel_id=1, source_target_pairs={{0,2},{1,3},{2,0},{3,1},{4,6},{5,7},{6,4},{7,5},{8,10},{9,11},{10,... | collective-permute-start | bytes 110600 | tf_op jit(solution)/shard_map/ppermute | solution.py:97
  50.1 0.9 collective-permute-start.15
  51.0 2.3 %collective-permute-done.14.refs_2_ = bf16[144,128]{1,0:T(8,128)(2,1)S(1)} collective-permute-done((bf16[144,128]{1,0:T(8,128)(2,1)S(1)}, bf16[144,128]{1,0:T(8,128)(2,1)S(1)}, u32[]{:S(2)}, u32[]{:S(2)}) %collective-permute-start.14) | collective-permute-done | bytes 36896 | tf_op jit(solution)/shard_map/ppermute | solution.py:97
  53.3 0.4 collective-permute-done.15.refs_3_
  53.7 1.1 %collective-permute-start.16 = (bf16[224,128]{1,0:T(8,128)(2,1)S(1)}, bf16[224,128]{1,0:T(8,128)(2,1)S(1)}, u32[]{:S(2)}, u32[]{:S(2)}) collective-permute-start(bf16[224,128]{1,0:T(8,128)(2,1)S(1)} %get-tuple-element.81), channel_id=1, source_target_pairs={{0,8},{4,12},{8,0},{12,4},{1,9},{5,13},{9,1},{13,5},{2,10},{6,14},... | collective-permute-start | bytes 172040 | tf_op jit(solution)/shard_map/ppermute | solution.py:97
  54.8 4.8 %collective-permute-done.16.theirs = bf16[224,128]{1,0:T(8,128)(2,1)S(1)} collective-permute-done((bf16[224,128]{1,0:T(8,128)(2,1)S(1)}, bf16[224,128]{1,0:T(8,128)(2,1)S(1)}, u32[]{:S(2)}, u32[]{:S(2)}) %collective-permute-start.16) | collective-permute-done | bytes 57376 | tf_op jit(solution)/shard_map/ppermute | solution.py:97
  59.6 0.7 shard_map.132
  60.3 0.7 collective-permute-start.19
  61.0 1.0 %collective-permute-start.18 = (bf16[144,128]{1,0:T(8,128)(2,1)S(1)}, bf16[144,128]{1,0:T(8,128)(2,1)S(1)}, u32[]{:S(2)}, u32[]{:S(2)}) collective-permute-start(bf16[144,128]{1,0:T(8,128)(2,1)S(1)} %get-tuple-element.87.refs_2_), channel_id=1, source_target_pairs={{0,2},{1,3},{2,0},{3,1},{4,6},{5,7},{6,4},{7,5},{8,10},{9,11},{10,... | collective-permute-start | bytes 110600 | tf_op jit(solution)/shard_map/ppermute | solution.py:97
  62.0 0.2 collective-permute-start.17
  62.2 1.7 %collective-permute-done.19.refs_5_ = bf16[144,128]{1,0:T(8,128)(2,1)S(1)} collective-permute-done((bf16[144,128]{1,0:T(8,128)(2,1)S(1)}, bf16[144,128]{1,0:T(8,128)(2,1)S(1)}, u32[]{:S(2)}, u32[]{:S(2)}) %collective-permute-start.19) | collective-permute-done | bytes 36896 | tf_op jit(solution)/shard_map/ppermute | solution.py:97
  63.9 1.1 %collective-permute-done.18.refs_4_ = bf16[144,128]{1,0:T(8,128)(2,1)S(1)} collective-permute-done((bf16[144,128]{1,0:T(8,128)(2,1)S(1)}, bf16[144,128]{1,0:T(8,128)(2,1)S(1)}, u32[]{:S(2)}, u32[]{:S(2)}) %collective-permute-start.18) | collective-permute-done | bytes 36896 | tf_op jit(solution)/shard_map/ppermute | solution.py:97
  64.9 1.6 %shard_map.133 = (bf16[18,32,128]{2,1,0:T(8,128)(2,1)S(1)}, f32[144,128]{1,0:T(8,128)S(1)}, bf16[144,128]{1,0:T(8,128)(2,1)S(1)}) custom-call(s32[128]{0:T(128)S(1)} %get-tuple-element.55.refs_0_, bf16[64,128,128]{2,1,0:T(8,128)(2,1)S(1)} %get-tuple-element.56.refs_1_, bf16[144,128]{1,0:T(8,128)(2,1)S(1)} %get-tuple-element.87.refs_2_, ...), custom_call_target="tpu_custom_call" | custom-call | flops 67108864 | bytes 2503168 | tf_op jit(solution)/shard_map/pallas_call | solution.py:80
  66.6 3.9 %collective-permute-done.20.refs_2_ = bf16[144,128]{1,0:T(8,128)(2,1)S(1)} collective-permute-done((bf16[144,128]{1,0:T(8,128)(2,1)S(1)}, bf16[144,128]{1,0:T(8,128)(2,1)S(1)}, u32[]{:S(2)}, u32[]{:S(2)}) %collective-permute-start.20) | collective-permute-done | bytes 36896 | tf_op jit(solution)/shard_map/ppermute | solution.py:97
  70.6 0.8 collective-permute-start.21
  71.4 4.1 %collective-permute-done.21.theirs = bf16[144,128]{1,0:T(8,128)(2,1)S(1)} collective-permute-done((bf16[144,128]{1,0:T(8,128)(2,1)S(1)}, bf16[144,128]{1,0:T(8,128)(2,1)S(1)}, u32[]{:S(2)}, u32[]{:S(2)}) %collective-permute-start.21) | collective-permute-done | bytes 36896 | tf_op jit(solution)/shard_map/ppermute | solution.py:97
  75.6 1.1 %collective-permute-start.23 = (bf16[144,128]{1,0:T(8,128)(2,1)S(1)}, bf16[144,128]{1,0:T(8,128)(2,1)S(1)}, u32[]{:S(2)}, u32[]{:S(2)}) collective-permute-start(bf16[144,128]{1,0:T(8,128)(2,1)S(1)} %get-tuple-element.96.refs_2_), channel_id=1, source_target_pairs={{0,2},{1,3},{2,0},{3,1},{4,6},{5,7},{6,4},{7,5},{8,10},{9,11},{10,... | collective-permute-start | bytes 110600 | tf_op jit(solution)/shard_map/ppermute | solution.py:97
  76.7 0.8 collective-permute-start.22
  77.5 1.5 %collective-permute-done.24.refs_5_ = bf16[144,128]{1,0:T(8,128)(2,1)S(1)} collective-permute-done((bf16[144,128]{1,0:T(8,128)(2,1)S(1)}, bf16[144,128]{1,0:T(8,128)(2,1)S(1)}, u32[]{:S(2)}, u32[]{:S(2)}) %collective-permute-start.24) | collective-permute-done | bytes 36896 | tf_op jit(solution)/shard_map/ppermute | solution.py:97
  79.0 1.0 collective-permute-done.23.refs_4_
  79.9 1.6 %shard_map.136 = (bf16[18,32,128]{2,1,0:T(8,128)(2,1)S(1)}, f32[144,128]{1,0:T(8,128)S(1)}, bf16[144,128]{1,0:T(8,128)(2,1)S(1)}) custom-call(s32[128]{0:T(128)S(1)} %get-tuple-element.55.refs_0_, bf16[64,128,128]{2,1,0:T(8,128)(2,1)S(1)} %get-tuple-element.56.refs_1_, bf16[144,128]{1,0:T(8,128)(2,1)S(1)} %get-tuple-element.96.refs_2_, ...), custom_call_target="tpu_custom_call" | custom-call | flops 67108864 | bytes 2503168 | tf_op jit(solution)/shard_map/pallas_call | solution.py:80
  81.6 3.9 %collective-permute-done.25.refs_2_ = bf16[144,128]{1,0:T(8,128)(2,1)S(1)} collective-permute-done((bf16[144,128]{1,0:T(8,128)(2,1)S(1)}, bf16[144,128]{1,0:T(8,128)(2,1)S(1)}, u32[]{:S(2)}, u32[]{:S(2)}) %collective-permute-start.25) | collective-permute-done | bytes 36896 | tf_op jit(solution)/shard_map/ppermute | solution.py:97
  85.6 0.8 collective-permute-start.26
  86.4 4.1 %collective-permute-done.26.theirs = bf16[144,128]{1,0:T(8,128)(2,1)S(1)} collective-permute-done((bf16[144,128]{1,0:T(8,128)(2,1)S(1)}, bf16[144,128]{1,0:T(8,128)(2,1)S(1)}, u32[]{:S(2)}, u32[]{:S(2)}) %collective-permute-start.26) | collective-permute-done | bytes 36896 | tf_op jit(solution)/shard_map/ppermute | solution.py:97
  90.5 0.1 shard_map.138.refs_6_.refs_0_
  90.7 1.1 %collective-permute-start.28 = (bf16[176,128]{1,0:T(8,128)(2,1)S(1)}, bf16[176,128]{1,0:T(8,128)(2,1)S(1)}, u32[]{:S(2)}, u32[]{:S(2)}) collective-permute-start(bf16[176,128]{1,0:T(8,128)(2,1)S(1)} %shard_map.138.refs_6_.refs_0_), channel_id=1, source_target_pairs={{0,2},{1,3},{2,0},{3,1},{4,6},{5,7},{6,4},{7,5},{8,10},{9,11},{10,... | collective-permute-start | bytes 135176 | tf_op jit(solution)/shard_map/ppermute | solution.py:97
  91.8 0.8 collective-permute-start.27
  92.5 1.7 %collective-permute-done.29.refs_9_.refs_3_ = bf16[176,128]{1,0:T(8,128)(2,1)S(1)} collective-permute-done((bf16[176,128]{1,0:T(8,128)(2,1)S(1)}, bf16[176,128]{1,0:T(8,128)(2,1)S(1)}, u32[]{:S(2)}, u32[]{:S(2)}) %collective-permute-start.29) | collective-permute-done | bytes 45088 | tf_op jit(solution)/shard_map/ppermute | solution.py:97
  94.2 1.0 collective-permute-done.28.refs_8_.refs_2_
  95.2 0.6 shard_map.140
  95.9 3.6 %shard_map.139 = bf16[64,128,128]{2,1,0:T(8,128)(2,1)} custom-call(s32[128]{0:T(128)S(1)} %get-tuple-element.55.refs_0_, bf16[9,32,128]{2,1,0:T(8,128)(2,1)S(1)} %get-tuple-element.84.refs_1_, bf16[9,32,128]{2,1,0:T(8,128)(2,1)S(1)} %get-tuple-element.85.refs_2_, bf16[9,32,128]{2,1,0:T(8,128)(2,1)S(1)} %get-tuple-element.86.refs_3_, ...), custom_call_target="tpu_custom_call" | custom-call | flops 268435456 | bytes 4194304 | tf_op jit(solution)/shard_map/pallas_call | solution.py:603
  99.4 0.3 collective-permute-done.30
  99.8 0.6 add_bitcast_fusion
  (41 shorter events, 0.8 us)
Async XLA Ops:
  0.6 0.8 copy-start.1
  1.4 0.7 copy-start.6
  2.1 0.7 copy-start.7
  2.8 20.4 %copy-start.2 = (f32[32,288]{1,0:T(8,128)S(1)}, f32[32,288]{1,0:T(8,128)}, u32[]{:S(2)}) copy-start(f32[32,288]{1,0:T(8,128)} %rates.3) | copy-start | bytes 110596
  2.9 10.8 %collective-permute-start.2 = (bf16[96,128]{1,0:T(8,128)(2,1)S(1)}, bf16[96,128]{1,0:T(8,128)(2,1)S(1)}, u32[]{:S(2)}, u32[]{:S(2)}) collective-permute-start(bf16[96,128]{1,0:T(8,128)(2,1)S(1)} %shard_map.121.after.refs_2_.mine), channel_id=1, source_target_pairs={{0,12},{4,8},{8,4},{12,0},{1,13},{5,9},{9,5},{13,1},{2,14},{6,10},... | collective-permute-start | bytes 73736 | tf_op jit(solution)/shard_map/ppermute | solution.py:97
  7.9 5.7 %collective-permute-start.1 = (bf16[96,128]{1,0:T(8,128)(2,1)S(1)}, bf16[96,128]{1,0:T(8,128)(2,1)S(1)}, u32[]{:S(2)}, u32[]{:S(2)}) collective-permute-start(bf16[96,128]{1,0:T(8,128)(2,1)S(1)} %shard_map.121.after.refs_2_.mine), channel_id=1, source_target_pairs={{0,8},{4,12},{8,0},{12,4},{1,9},{5,13},{9,1},{13,5},{2,10},{6,14},... | collective-permute-start | bytes 73736 | tf_op jit(solution)/shard_map/ppermute | solution.py:97
  7.9 5.7 %collective-permute-start = (bf16[96,128]{1,0:T(8,128)(2,1)S(1)}, bf16[96,128]{1,0:T(8,128)(2,1)S(1)}, u32[]{:S(2)}, u32[]{:S(2)}) collective-permute-start(bf16[96,128]{1,0:T(8,128)(2,1)S(1)} %shard_map.121.after.refs_2_.mine), channel_id=1, source_target_pairs={{0,4},{4,0},{8,12},{12,8},{1,5},{5,1},{9,13},{13,9},{2,6},{6,2},{1... | collective-permute-start | bytes 73736 | tf_op jit(solution)/shard_map/ppermute | solution.py:97
  8.6 1.6 %copy-start = (bf16[1,1,64,128,128]{4,3,2,1,0:T(8,128)(2,1)S(1)}, bf16[1,1,64,128,128]{4,3,2,1,0:T(8,128)(2,1)}, u32[]{:S(2)}) copy-start(bf16[1,1,64,128,128]{4,3,2,1,0:T(8,128)(2,1)} %weights.1) | copy-start | bytes 6291460
  10.2 0.7 copy-start.8
  10.8 0.7 copy-start.9
  11.5 0.7 copy-start.10
  12.1 11.1 %copy-start.3 = (f32[3,32,288]{2,1,0:T(8,128)S(1)}, f32[3,32,288]{2,1,0:T(8,128)}, u32[]{:S(2)}) copy-start(f32[3,32,288]{2,1,0:T(8,128)} %cots.1) | copy-start | bytes 331780
  12.1 11.1 %copy-start.4 = (bf16[3,32,512]{2,1,0:T(8,128)(2,1)S(1)}, bf16[3,32,512]{2,1,0:T(8,128)(2,1)}, u32[]{:S(2)}) copy-start(bf16[3,32,512]{2,1,0:T(8,128)(2,1)} %param.11) | copy-start | bytes 294916
  12.1 11.1 %copy-start.5 = (f32[8192]{0:T(1024)S(1)}, f32[8192]{0:T(1024)}, u32[]{:S(2)}) copy-start(f32[8192]{0:T(1024)} %param.18) | copy-start | bytes 98308
  15.8 1.9 %collective-permute-start.3 = (bf16[144,128]{1,0:T(8,128)(2,1)S(1)}, bf16[144,128]{1,0:T(8,128)(2,1)S(1)}, u32[]{:S(2)}, u32[]{:S(2)}) collective-permute-start(bf16[144,128]{1,0:T(8,128)(2,1)S(1)} %get-tuple-element.58), channel_id=1, source_target_pairs={{0,1},{1,0},{2,3},{3,2},{4,5},{5,4},{6,7},{7,6},{8,9},{9,8},{10,11... | collective-permute-start | bytes 110600 | tf_op jit(solution)/shard_map/ppermute | solution.py:97
  15.9 4.0 %collective-permute-start.4 = (bf16[144,128]{1,0:T(8,128)(2,1)S(1)}, bf16[144,128]{1,0:T(8,128)(2,1)S(1)}, u32[]{:S(2)}, u32[]{:S(2)}) collective-permute-start(bf16[144,128]{1,0:T(8,128)(2,1)S(1)} %get-tuple-element.59), channel_id=1, source_target_pairs={{0,2},{1,3},{2,0},{3,1},{4,6},{5,7},{6,4},{7,5},{8,10},{9,11},{10,... | collective-permute-start | bytes 110600 | tf_op jit(solution)/shard_map/ppermute | solution.py:97
  17.6 3.4 %collective-permute-start.5 = (bf16[144,128]{1,0:T(8,128)(2,1)S(1)}, bf16[144,128]{1,0:T(8,128)(2,1)S(1)}, u32[]{:S(2)}, u32[]{:S(2)}) collective-permute-start(bf16[144,128]{1,0:T(8,128)(2,1)S(1)} %get-tuple-element.60), channel_id=1, source_target_pairs={{0,3},{1,2},{2,1},{3,0},{4,7},{5,6},{6,5},{7,4},{8,11},{9,10},{10,... | collective-permute-start | bytes 110600 | tf_op jit(solution)/shard_map/ppermute | solution.py:97
  21.0 5.7 %collective-permute-start.6 = (bf16[144,128]{1,0:T(8,128)(2,1)S(1)}, bf16[144,128]{1,0:T(8,128)(2,1)S(1)}, u32[]{:S(2)}, u32[]{:S(2)}) collective-permute-start(bf16[144,128]{1,0:T(8,128)(2,1)S(1)} %get-tuple-element.62), channel_id=1, source_target_pairs={{0,8},{4,12},{8,0},{12,4},{1,9},{5,13},{9,1},{13,5},{2,10},{6,14},... | collective-permute-start | bytes 110600 | tf_op jit(solution)/shard_map/ppermute | solution.py:97
  26.8 4.0 %collective-permute-start.7 = (bf16[144,128]{1,0:T(8,128)(2,1)S(1)}, bf16[144,128]{1,0:T(8,128)(2,1)S(1)}, u32[]{:S(2)}, u32[]{:S(2)}) collective-permute-start(bf16[144,128]{1,0:T(8,128)(2,1)S(1)} %get-tuple-element.66.refs_2_), channel_id=1, source_target_pairs={{0,4},{4,0},{8,12},{12,8},{1,5},{5,1},{9,13},{13,9},{2,6},{6,2},{1... | collective-permute-start | bytes 110600 | tf_op jit(solution)/shard_map/ppermute | solution.py:97
  32.9 1.9 %collective-permute-start.8 = (bf16[144,128]{1,0:T(8,128)(2,1)S(1)}, bf16[144,128]{1,0:T(8,128)(2,1)S(1)}, u32[]{:S(2)}, u32[]{:S(2)}) collective-permute-start(bf16[144,128]{1,0:T(8,128)(2,1)S(1)} %get-tuple-element.68), channel_id=1, source_target_pairs={{0,1},{1,0},{2,3},{3,2},{4,5},{5,4},{6,7},{7,6},{8,9},{9,8},{10,11... | collective-permute-start | bytes 110600 | tf_op jit(solution)/shard_map/ppermute | solution.py:97
  33.0 4.2 %collective-permute-start.9 = (bf16[144,128]{1,0:T(8,128)(2,1)S(1)}, bf16[144,128]{1,0:T(8,128)(2,1)S(1)}, u32[]{:S(2)}, u32[]{:S(2)}) collective-permute-start(bf16[144,128]{1,0:T(8,128)(2,1)S(1)} %get-tuple-element.69), channel_id=1, source_target_pairs={{0,2},{1,3},{2,0},{3,1},{4,6},{5,7},{6,4},{7,5},{8,10},{9,11},{10,... | collective-permute-start | bytes 110600 | tf_op jit(solution)/shard_map/ppermute | solution.py:97
  33.8 3.8 %collective-permute-start.10 = (bf16[144,128]{1,0:T(8,128)(2,1)S(1)}, bf16[144,128]{1,0:T(8,128)(2,1)S(1)}, u32[]{:S(2)}, u32[]{:S(2)}) collective-permute-start(bf16[144,128]{1,0:T(8,128)(2,1)S(1)} %get-tuple-element.70), channel_id=1, source_target_pairs={{0,3},{1,2},{2,1},{3,0},{4,7},{5,6},{6,5},{7,4},{8,11},{9,10},{10,... | collective-permute-start | bytes 110600 | tf_op jit(solution)/shard_map/ppermute | solution.py:97
  37.6 5.3 %collective-permute-start.11 = (bf16[144,128]{1,0:T(8,128)(2,1)S(1)}, bf16[144,128]{1,0:T(8,128)(2,1)S(1)}, u32[]{:S(2)}, u32[]{:S(2)}) collective-permute-start(bf16[144,128]{1,0:T(8,128)(2,1)S(1)} %get-tuple-element.72), channel_id=1, source_target_pairs={{0,8},{4,12},{8,0},{12,4},{1,9},{5,13},{9,1},{13,5},{2,10},{6,14},... | collective-permute-start | bytes 110600 | tf_op jit(solution)/shard_map/ppermute | solution.py:97
  42.9 4.0 %collective-permute-start.12 = (bf16[144,128]{1,0:T(8,128)(2,1)S(1)}, bf16[144,128]{1,0:T(8,128)(2,1)S(1)}, u32[]{:S(2)}, u32[]{:S(2)}) collective-permute-start(bf16[144,128]{1,0:T(8,128)(2,1)S(1)} %get-tuple-element.74.refs_2_), channel_id=1, source_target_pairs={{0,4},{4,0},{8,12},{12,8},{1,5},{5,1},{9,13},{13,9},{2,6},{6,2},{1... | collective-permute-start | bytes 110600 | tf_op jit(solution)/shard_map/ppermute | solution.py:97
  49.1 1.9 %collective-permute-start.13 = (bf16[144,128]{1,0:T(8,128)(2,1)S(1)}, bf16[144,128]{1,0:T(8,128)(2,1)S(1)}, u32[]{:S(2)}, u32[]{:S(2)}) collective-permute-start(bf16[144,128]{1,0:T(8,128)(2,1)S(1)} %get-tuple-element.76), channel_id=1, source_target_pairs={{0,1},{1,0},{2,3},{3,2},{4,5},{5,4},{6,7},{7,6},{8,9},{9,8},{10,11... | collective-permute-start | bytes 110600 | tf_op jit(solution)/shard_map/ppermute | solution.py:97
  49.1 4.1 %collective-permute-start.14 = (bf16[144,128]{1,0:T(8,128)(2,1)S(1)}, bf16[144,128]{1,0:T(8,128)(2,1)S(1)}, u32[]{:S(2)}, u32[]{:S(2)}) collective-permute-start(bf16[144,128]{1,0:T(8,128)(2,1)S(1)} %get-tuple-element.77), channel_id=1, source_target_pairs={{0,2},{1,3},{2,0},{3,1},{4,6},{5,7},{6,4},{7,5},{8,10},{9,11},{10,... | collective-permute-start | bytes 110600 | tf_op jit(solution)/shard_map/ppermute | solution.py:97
  50.1 3.5 %collective-permute-start.15 = (bf16[144,128]{1,0:T(8,128)(2,1)S(1)}, bf16[144,128]{1,0:T(8,128)(2,1)S(1)}, u32[]{:S(2)}, u32[]{:S(2)}) collective-permute-start(bf16[144,128]{1,0:T(8,128)(2,1)S(1)} %get-tuple-element.78), channel_id=1, source_target_pairs={{0,3},{1,2},{2,1},{3,0},{4,7},{5,6},{6,5},{7,4},{8,11},{9,10},{10,... | collective-permute-start | bytes 110600 | tf_op jit(solution)/shard_map/ppermute | solution.py:97
  53.7 5.9 %collective-permute-start.16 = (bf16[224,128]{1,0:T(8,128)(2,1)S(1)}, bf16[224,128]{1,0:T(8,128)(2,1)S(1)}, u32[]{:S(2)}, u32[]{:S(2)}) collective-permute-start(bf16[224,128]{1,0:T(8,128)(2,1)S(1)} %get-tuple-element.81), channel_id=1, source_target_pairs={{0,8},{4,12},{8,0},{12,4},{1,9},{5,13},{9,1},{13,5},{2,10},{6,14},... | collective-permute-start | bytes 172040 | tf_op jit(solution)/shard_map/ppermute | solution.py:97
  60.3 3.6 %collective-permute-start.19 = (bf16[144,128]{1,0:T(8,128)(2,1)S(1)}, bf16[144,128]{1,0:T(8,128)(2,1)S(1)}, u32[]{:S(2)}, u32[]{:S(2)}) collective-permute-start(bf16[144,128]{1,0:T(8,128)(2,1)S(1)} %get-tuple-element.87.refs_2_), channel_id=1, source_target_pairs={{0,3},{1,2},{2,1},{3,0},{4,7},{5,6},{6,5},{7,4},{8,11},{9,10},{10,... | collective-permute-start | bytes 110600 | tf_op jit(solution)/shard_map/ppermute | solution.py:97
  61.0 4.0 %collective-permute-start.18 = (bf16[144,128]{1,0:T(8,128)(2,1)S(1)}, bf16[144,128]{1,0:T(8,128)(2,1)S(1)}, u32[]{:S(2)}, u32[]{:S(2)}) collective-permute-start(bf16[144,128]{1,0:T(8,128)(2,1)S(1)} %get-tuple-element.87.refs_2_), channel_id=1, source_target_pairs={{0,2},{1,3},{2,0},{3,1},{4,6},{5,7},{6,4},{7,5},{8,10},{9,11},{10,... | collective-permute-start | bytes 110600 | tf_op jit(solution)/shard_map/ppermute | solution.py:97
  62.0 3.0 %collective-permute-start.17 = (bf16[144,128]{1,0:T(8,128)(2,1)S(1)}, bf16[144,128]{1,0:T(8,128)(2,1)S(1)}, u32[]{:S(2)}, u32[]{:S(2)}) collective-permute-start(bf16[144,128]{1,0:T(8,128)(2,1)S(1)} %get-tuple-element.87.refs_2_), channel_id=1, source_target_pairs={{0,1},{1,0},{2,3},{3,2},{4,5},{5,4},{6,7},{7,6},{8,9},{9,8},{10,11... | collective-permute-start | bytes 110600 | tf_op jit(solution)/shard_map/ppermute | solution.py:97
  66.5 4.0 %collective-permute-start.20 = (bf16[144,128]{1,0:T(8,128)(2,1)S(1)}, bf16[144,128]{1,0:T(8,128)(2,1)S(1)}, u32[]{:S(2)}, u32[]{:S(2)}) collective-permute-start(bf16[144,128]{1,0:T(8,128)(2,1)S(1)} %get-tuple-element.90), channel_id=1, source_target_pairs={{0,4},{4,0},{8,12},{12,8},{1,5},{5,1},{9,13},{13,9},{2,6},{6,2},{1... | collective-permute-start | bytes 110600 | tf_op jit(solution)/shard_map/ppermute | solution.py:97
  70.6 4.9 %collective-permute-start.21 = (bf16[144,128]{1,0:T(8,128)(2,1)S(1)}, bf16[144,128]{1,0:T(8,128)(2,1)S(1)}, u32[]{:S(2)}, u32[]{:S(2)}) collective-permute-start(bf16[144,128]{1,0:T(8,128)(2,1)S(1)} %get-tuple-element.92), channel_id=1, source_target_pairs={{0,8},{4,12},{8,0},{12,4},{1,9},{5,13},{9,1},{13,5},{2,10},{6,14},... | collective-permute-start | bytes 110600 | tf_op jit(solution)/shard_map/ppermute | solution.py:97
  75.5 3.4 %collective-permute-start.24 = (bf16[144,128]{1,0:T(8,128)(2,1)S(1)}, bf16[144,128]{1,0:T(8,128)(2,1)S(1)}, u32[]{:S(2)}, u32[]{:S(2)}) collective-permute-start(bf16[144,128]{1,0:T(8,128)(2,1)S(1)} %get-tuple-element.96.refs_2_), channel_id=1, source_target_pairs={{0,3},{1,2},{2,1},{3,0},{4,7},{5,6},{6,5},{7,4},{8,11},{9,10},{10,... | collective-permute-start | bytes 110600 | tf_op jit(solution)/shard_map/ppermute | solution.py:97
  75.6 4.3 %collective-permute-start.23 = (bf16[144,128]{1,0:T(8,128)(2,1)S(1)}, bf16[144,128]{1,0:T(8,128)(2,1)S(1)}, u32[]{:S(2)}, u32[]{:S(2)}) collective-permute-start(bf16[144,128]{1,0:T(8,128)(2,1)S(1)} %get-tuple-element.96.refs_2_), channel_id=1, source_target_pairs={{0,2},{1,3},{2,0},{3,1},{4,6},{5,7},{6,4},{7,5},{8,10},{9,11},{10,... | collective-permute-start | bytes 110600 | tf_op jit(solution)/shard_map/ppermute | solution.py:97
  76.7 3.3 %collective-permute-start.22 = (bf16[144,128]{1,0:T(8,128)(2,1)S(1)}, bf16[144,128]{1,0:T(8,128)(2,1)S(1)}, u32[]{:S(2)}, u32[]{:S(2)}) collective-permute-start(bf16[144,128]{1,0:T(8,128)(2,1)S(1)} %get-tuple-element.96.refs_2_), channel_id=1, source_target_pairs={{0,1},{1,0},{2,3},{3,2},{4,5},{5,4},{6,7},{7,6},{8,9},{9,8},{10,11... | collective-permute-start | bytes 110600 | tf_op jit(solution)/shard_map/ppermute | solution.py:97
  81.6 4.0 %collective-permute-start.25 = (bf16[144,128]{1,0:T(8,128)(2,1)S(1)}, bf16[144,128]{1,0:T(8,128)(2,1)S(1)}, u32[]{:S(2)}, u32[]{:S(2)}) collective-permute-start(bf16[144,128]{1,0:T(8,128)(2,1)S(1)} %get-tuple-element.101), channel_id=1, source_target_pairs={{0,4},{4,0},{8,12},{12,8},{1,5},{5,1},{9,13},{13,9},{2,6},{6,2},{1... | collective-permute-start | bytes 110600 | tf_op jit(solution)/shard_map/ppermute | solution.py:97
  85.6 4.9 %collective-permute-start.26 = (bf16[144,128]{1,0:T(8,128)(2,1)S(1)}, bf16[144,128]{1,0:T(8,128)(2,1)S(1)}, u32[]{:S(2)}, u32[]{:S(2)}) collective-permute-start(bf16[144,128]{1,0:T(8,128)(2,1)S(1)} %get-tuple-element.103), channel_id=1, source_target_pairs={{0,8},{4,12},{8,0},{12,4},{1,9},{5,13},{9,1},{13,5},{2,10},{6,14},... | collective-permute-start | bytes 110600 | tf_op jit(solution)/shard_map/ppermute | solution.py:97
  90.6 3.6 %collective-permute-start.29 = (bf16[176,128]{1,0:T(8,128)(2,1)S(1)}, bf16[176,128]{1,0:T(8,128)(2,1)S(1)}, u32[]{:S(2)}, u32[]{:S(2)}) collective-permute-start(bf16[176,128]{1,0:T(8,128)(2,1)S(1)} %shard_map.138.refs_6_.refs_0_), channel_id=1, source_target_pairs={{0,3},{1,2},{2,1},{3,0},{4,7},{5,6},{6,5},{7,4},{8,11},{9,10},{10,... | collective-permute-start | bytes 135176 | tf_op jit(solution)/shard_map/ppermute | solution.py:97
  90.7 4.5 %collective-permute-start.28 = (bf16[176,128]{1,0:T(8,128)(2,1)S(1)}, bf16[176,128]{1,0:T(8,128)(2,1)S(1)}, u32[]{:S(2)}, u32[]{:S(2)}) collective-permute-start(bf16[176,128]{1,0:T(8,128)(2,1)S(1)} %shard_map.138.refs_6_.refs_0_), channel_id=1, source_target_pairs={{0,2},{1,3},{2,0},{3,1},{4,6},{5,7},{6,4},{7,5},{8,10},{9,11},{10,... | collective-permute-start | bytes 135176 | tf_op jit(solution)/shard_map/ppermute | solution.py:97
  91.8 3.4 %collective-permute-start.27 = (bf16[176,128]{1,0:T(8,128)(2,1)S(1)}, bf16[176,128]{1,0:T(8,128)(2,1)S(1)}, u32[]{:S(2)}, u32[]{:S(2)}) collective-permute-start(bf16[176,128]{1,0:T(8,128)(2,1)S(1)} %shard_map.138.refs_6_.refs_0_), channel_id=1, source_target_pairs={{0,1},{1,0},{2,3},{3,2},{4,5},{5,4},{6,7},{7,6},{8,9},{9,8},{10,11... | collective-permute-start | bytes 135176 | tf_op jit(solution)/shard_map/ppermute | solution.py:97
  95.8 4.0 %collective-permute-start.30 = (f32[64,128]{1,0:T(8,128)S(1)}, f32[64,128]{1,0:T(8,128)S(1)}, u32[]{:S(2)}, u32[]{:S(2)}) collective-permute-start(f32[64,128]{1,0:T(8,128)S(1)} %shard_map.140), channel_id=1, source_target_pairs={{0,4},{4,0},{8,12},{12,8},{1,5},{5,1},{9,13},{13,9},{2,6},{6,2},{1... | collective-permute-start | bytes 98312 | tf_op jit(solution)/shard_map/ppermute | solution.py:97

commit v3 on v2

--- a/solution.py
+++ b/solution.py
@@ -13,7 +13,7 @@
 BF16 = jnp.bfloat16
 VMEM = pl.BlockSpec(memory_space=pltpu.VMEM)
 SMEM = pl.BlockSpec(memory_space=pltpu.SMEM)
-ANY = pl.BlockSpec(memory_space=pl.ANY)
+HBM = pl.BlockSpec(memory_space=pltpu.HBM)
 
 
 class Sizes:
@@ -101,31 +101,28 @@
     return count <= 4
 
 
-def near(axis, count):
-    size = lax.axis_size(axis)
-    return [list(range(i, i + count)) for i in range(0, size, count)]
-
-
-def share(x, axis, count):
+def share(x, axis):
+    count = lax.axis_size(axis)
     if few(count):
-        return [flip(x, axis, k) for k in range(1, count)]
-    return [lax.all_gather(x, axis, axis_index_groups=near(axis, count))]
-
-
-def exchange(parts, axis, count):
-    if few(count):
-        return [flip(parts[k - 1], axis, k) for k in range(1, count)]
-    return [lax.all_to_all(parts[0], axis, 0, 0, axis_index_groups=near(axis, count), tiled=True)]
-
-
-def parcel(count, dims, kind):
-    if few(count):
+        return [flip(x, axis, k) for k in reversed(range(1, count))][::-1]
+    return [lax.all_gather(x, axis)]
+
+
+def exchange(parts, axis):
+    count = lax.axis_size(axis)
+    if len(parts) == count - 1:
+        return [flip(parts[k - 1], axis, k) for k in reversed(range(1, count))][::-1]
+    return [lax.all_to_all(parts[0], axis, 0, 0, tiled=True)]
+
+
+def parcel(count, dims, kind, whole=False):
+    if few(count) and not whole:
         return [shape(dims, kind)] * (count - 1)
     return [shape((count, *dims), kind)]
 
 
 def away(refs, count, me, k):
-    return refs[k - 1] if few(count) else refs[0].at[(me ^ k) & (count - 1)]
+    return refs[k - 1] if len(refs) == count - 1 else refs[0].at[me ^ k]
 
 
 def place():
@@ -136,10 +133,20 @@
     lax.fori_loop(0, count, lambda i, c: (body(i), c)[1], 0, unroll=count <= 18)
 
 
-def start_kernel(z, rates, types, inputs, message, pad, codes):
+def fetch(pairs, sems):
+    copies = [pltpu.make_async_copy(a, b, sems.at[i]) for i, (a, b) in enumerate(pairs)]
+    for copy in copies:
+        copy.start()
+    return copies
+
+
+def start_kernel(z, rates_in, types_in, inputs_in, message, own, rates, types, inputs, pad, codes, sems):
+    copies = fetch([(rates_in, rates), (types_in, types), (inputs_in, inputs)], sems)
     pad[...] = jnp.zeros_like(pad)
+    codes[...] = jnp.zeros_like(codes)
+    for copy in copies:
+        copy.wait()
     pad[:, 0 : z.local] = rates[...]
-    codes[...] = jnp.zeros_like(codes)
     t = types[...].reshape(1, z.local)
     m = inputs[...].reshape(1, z.local)
     rows = [
@@ -154,13 +161,18 @@
     blocks = [code[0:4, f * BLOCK : (f + 1) * BLOCK] for f in range(z.frame)]
     fill = message.shape[0] - z.piece - 4 * z.frame
     extra = jnp.concatenate(blocks + [jnp.zeros((fill, BLOCK), F32)], axis=0)
-    message[...] = jnp.concatenate([z.pack(pad[...]), extra], axis=0).astype(BF16)
-
-
-def load_kernel(z, after, owner, post, pre, weights, out, ids, sem):
+    packed = z.pack(pad[...])
+    own[...] = packed
+    message[...] = jnp.concatenate([packed, extra], axis=0).astype(BF16)
+
+
+def load_kernel(z, after, owner_in, post_in, pre_in, weights, out, ids, owner, post, pre, sems):
     del after
-    copy = pltpu.make_async_copy(weights.at[0, 0], out, sem)
-    copy.start()
+    copies = fetch(
+        [(owner_in, owner), (post_in, post), (pre_in, pre), (weights.at[0, 0], out)], sems
+    )
+    for copy in copies[:3]:
+        copy.wait()
 
     def one(s, carry):
         ids[s] = owner[0, 0, s] * z.post + post[0, 0, s]
@@ -168,10 +180,14 @@
         return carry
 
     lax.fori_loop(0, z.slots, one, 0, unroll=8)
-    copy.wait()
-
-
-def prepare_kernel(z, mine, theirs, rates, cots, table, stimuli, pair_rates, gain, drive, cot_out, pad):
+    copies[3].wait()
+
+
+def prepare_kernel(z, count, *refs):
+    mine, own, cots, table, stimuli = refs[:5]
+    got = refs[5 : 5 + count]
+    rates, gain, drive, cot_out, pad = refs[5 + count :]
+    p, _ = place()
     highs = z.types // BLOCK
     t = jnp.transpose(table[...])
     t1 = t.astype(BF16)
@@ -181,17 +197,17 @@
     low_ids = lax.broadcasted_iota(jnp.int32, (BLOCK, BLOCK), 0).astype(F32)
     channel_ids = lax.broadcasted_iota(jnp.int32, (z.channels, BLOCK), 0).astype(F32)
     stim = stimuli[...]
-    for side, ref in enumerate((mine, theirs)):
-        rows = slice(side * z.piece, (side + 1) * z.piece)
+    for k in range(z.rows):
+        ref = mine if k == 0 else away(got, z.rows, p, k)
+        rows = slice(k * z.piece, (k + 1) * z.piece)
         message = ref[...].astype(F32)
         gains, drives = [], []
         for f in range(z.frame):
             at = z.piece + 4 * f
             codes = message[at : at + 4]
             pick = (high_ids == codes[0:1]).astype(BF16)
-            got = sum(jnp.dot(x, pick, preferred_element_type=F32) for x in (t1, t2, t3))
-            mine_only = jnp.where(low_ids == codes[1:2], got, 0.0)
-            line = jnp.sum(mine_only, axis=0, keepdims=True)
+            found = sum(jnp.dot(x, pick, preferred_element_type=F32) for x in (t1, t2, t3))
+            line = jnp.sum(jnp.where(low_ids == codes[1:2], found, 0.0), axis=0, keepdims=True)
             gains.append(jnp.broadcast_to(line, (z.batch, BLOCK)))
             channel = (codes[2:3] - 1.0) * BLOCK + codes[3:4]
             chosen = (channel_ids == channel).astype(BF16)
@@ -200,11 +216,8 @@
         for step in range(z.steps):
             part = [d[step * z.batch : (step + 1) * z.batch] for d in drives]
             drive[step, rows] = z.pack(jnp.concatenate(part, axis=1))
-        if side == 1:
-            pair_rates[rows] = message[0 : z.piece]
+        rates[rows] = own[...] if k == 0 else message[0 : z.piece]
     pad[...] = jnp.zeros_like(pad)
-    pad[:, 0 : z.local] = rates[...]
-    pair_rates[0 : z.piece] = z.pack(pad[...])
     for step in range(z.steps):
         pad[:, 0 : z.local] = cots[step]
         cot_out[step] = z.pack(pad[...])
@@ -240,17 +253,29 @@
     multiply_forward(z, c, ids, weights, x, total, own, parts)
 
 
-def forward_kernel(z, count, *refs):
-    ids, weights, mine = refs[:3]
-    got = refs[3 : 3 + count]
-    x, own = refs[3 + count : 5 + count]
-    parts, (sums, total) = refs[5 + count : -2], refs[-2:]
+def forward_kernel(z, step, count, *refs):
+    ids, weights, kept, rates, gain, drive = refs[:6]
+    got = refs[6 : 6 + count]
+    new, act_pair, cur_pair, x, own = refs[6 + count : 11 + count]
+    parts, (sums, total) = refs[11 + count : -2], refs[-2:]
     p, c = place()
     sums[...] = jnp.zeros_like(sums)
-    for k in range(z.half):
-        pair = (mine if k == 0 else away(got, z.half, p, k))[...].astype(F32)
-        z.add_blocks(sums, 0, p ^ k, pair[0 : z.piece])
-        z.add_blocks(sums, 0, p ^ k ^ z.half, pair[z.piece :])
+
+    def sent(k, side):
+        ref = kept if k == 0 else away(got, z.rows, p, k)
+        return ref[side * z.piece : (side + 1) * z.piece].astype(F32)
+
+    for k in range(z.rows):
+        rows = slice(k * z.piece, (k + 1) * z.piece)
+        current = sent(k, 0) + sent(k ^ z.half, 1) + drive[step, rows]
+        activity = jnp.tanh(gain[rows] * current)
+        fresh = 0.5 * rates[rows] + 0.5 * activity
+        new[rows] = fresh
+        if k % z.half == 0:
+            at = k // z.half * z.piece
+            act_pair[at : at + z.piece] = activity
+            cur_pair[at : at + z.piece] = current
+        z.add_blocks(sums, 0, p ^ k, fresh)
     x[...] = sums[...].astype(BF16)
     multiply_forward(z, c, ids, weights, x, total, own, parts)
 
@@ -271,33 +296,24 @@
     message[...] = total.astype(BF16)
 
 
-def currents(z, kept, theirs, drive):
+def pair_of(z, ref):
+    at = z.half * z.piece
+    return jnp.concatenate([ref[0 : z.piece], ref[at : at + z.piece]], axis=0)
+
+
+def turn_kernel(z, kept, theirs, rates, gain, drive, cots, final, message, gain_pair, tally, base):
     other = theirs[...].astype(F32)
     swapped = jnp.concatenate([other[z.piece : z.pair], other[0 : z.piece]], axis=0)
-    own = kept[0 : z.piece] + swapped[0 : z.piece]
-    partner = kept[z.piece :] + swapped[z.piece :]
-    return jnp.concatenate([own, partner], axis=0) + drive, other
-
-
-def rate_kernel(z, step, kept, theirs, rates, gain, drive, new, act, cur, lowered):
-    current, _ = currents(z, kept, theirs, drive[step])
-    activity = jnp.tanh(gain[...] * current)
-    fresh = 0.5 * rates[...] + 0.5 * activity
-    new[...] = fresh
-    act[...] = activity
-    cur[...] = current
-    lowered[...] = fresh.astype(BF16)
-
-
-def turn_kernel(z, kept, theirs, rates, gain, drive, cots, final, message, tally, base):
-    current, other = currents(z, kept, theirs, drive[z.steps - 1])
-    activity = jnp.tanh(gain[...] * current)
+    gains = pair_of(z, gain)
+    current = kept[...] + swapped + pair_of(z, drive.at[z.steps - 1])
+    activity = jnp.tanh(gains * current)
     fresh = 0.5 * rates[0 : z.piece] + 0.5 * activity[0 : z.piece]
     final[...] = z.unpack(fresh)[:, 0 : z.local]
     mine = cots[z.steps - 1]
     adjoint = jnp.concatenate([mine, other[z.pair : z.pair + z.piece]], axis=0)
     pressure = adjoint * 0.5 * (1.0 - activity * activity)
-    message[...] = (gain[...] * pressure).astype(BF16)
+    message[...] = (gains * pressure).astype(BF16)
+    gain_pair[...] = gains
     tally[...] = pressure * current
     base[...] = cots[z.steps - 2] + 0.5 * mine
 
@@ -312,44 +328,38 @@
 
 
 def back_kernel(z, count, *refs):
-    ids, weights, mine = refs[:3]
-    got = refs[3 : 3 + count]
-    d, own = refs[3 + count : 5 + count]
-    parts, (sums, total) = refs[5 + count : -2], refs[-2:]
+    ids, weights, base, mine = refs[:4]
+    got = refs[4 : 4 + count]
+    d, own = refs[4 + count : 6 + count]
+    parts, (sums, total) = refs[6 + count : -2], refs[-2:]
     p, c = place()
     gather_post(z, c, mine, got, sums, d)
     total[...] = jnp.zeros_like(total)
     for s in range(z.slots):
         total[ids[z.slots + s]] += jnp.dot(d[ids[s]], weights[s], preferred_element_type=F32)
-    for k in range(z.half):
-        both = jnp.concatenate(
-            [z.take_blocks(total, 0, p ^ k), z.take_blocks(total, 0, p ^ k ^ z.half)], axis=0
-        )
+    pieces = [z.take_blocks(total, 0, p ^ k) for k in range(z.rows)]
+    for k in range(z.rows):
+        other = pieces[k ^ z.half]
         if k == 0:
-            own[...] = both
+            own[...] = jnp.concatenate([pieces[0] + base[...], other], axis=0)
         else:
-            away(parts, z.half, p, k)[...] = both.astype(BF16)
-
-
-def near_kernel(z, count, *refs):
-    own, base, got = refs[0], refs[1], refs[2 : 2 + count]
-    kept, message = refs[-2:]
+            if k == z.half:
+                other = other + base[...]
+            both = jnp.concatenate([pieces[k], other], axis=0)
+            away(parts, z.rows, p, k)[...] = both.astype(BF16)
+
+
+def adjoints(z, own, got):
     p, _ = place()
     total = own[...]
-    for k in range(1, z.half):
-        total = total + away(got, z.half, p, k)[...].astype(F32)
-    total = jnp.concatenate([total[0 : z.piece] + base[...], total[z.piece :]], axis=0)
-    kept[...] = total
-    message[...] = total.astype(BF16)
-
-
-def adjoints(z, kept, theirs):
-    other = theirs[...].astype(F32)
-    return kept[...] + jnp.concatenate([other[z.piece :], other[0 : z.piece]], axis=0)
-
-
-def delta_kernel(z, before, kept, theirs, gain, act, cur, tally_in, cots, message, tally, base):
-    adjoint = adjoints(z, kept, theirs)
+    for k in range(1, z.rows):
+        total = total + away(got, z.rows, p, k)[...].astype(F32)
+    return total
+
+
+def delta_kernel(z, before, count, own, gain, act, cur, tally_in, cots, *refs):
+    got, (message, tally, base) = refs[:count], refs[count:]
+    adjoint = adjoints(z, own, got)
     activity = act[...]
     pressure = adjoint * 0.5 * (1.0 - activity * activity)
     message[...] = (gain[...] * pressure).astype(BF16)
@@ -357,8 +367,9 @@
     base[...] = cots[before - 1] + 0.5 * adjoint[0 : z.piece]
 
 
-def last_delta_kernel(z, kept, theirs, gain, act, cur, tally_in, mine, partner, message):
-    adjoint = adjoints(z, kept, theirs)
+def last_delta_kernel(z, count, own, gain, act, cur, tally_in, mine, partner, *refs):
+    got, message = refs[:count], refs[count]
+    adjoint = adjoints(z, own, got)
     activity = act[...]
     pressure = adjoint * 0.5 * (1.0 - activity * activity)
     tally = tally_in[...] + pressure * cur[...]
@@ -368,11 +379,10 @@
         codes = ref[...].astype(F32)[z.piece :]
         begin = side * z.piece
         for f in range(z.frame):
+            at = begin + f * z.batch
             if f < z.full:
-                at = begin + f * z.batch
                 g = jnp.sum(tally[at : at + z.batch], axis=0, keepdims=True)
             else:
-                at = begin + f * z.batch
                 packed = jnp.sum(tally[at : at + z.tall], axis=0, keepdims=True)
                 g = packed
                 for i in range(1, z.groups):
@@ -469,19 +479,27 @@
     opening = (z.piece + 4 * z.frame + 15) // 16 * 16
     closing = (z.pair + z.piece + 15) // 16 * 16
 
-    (message,) = call(
+    message, own_rates = call(
         functools.partial(start_kernel, z),
-        [shape((opening, BLOCK), BF16)],
-        [pltpu.VMEM((batch, z.wide), F32), pltpu.VMEM((8, z.wide), F32)],
+        [shape((opening, BLOCK), BF16), shape((z.piece, BLOCK))],
+        [
+            pltpu.VMEM((batch, local), F32),
+            pltpu.VMEM((local,), jnp.int32),
+            pltpu.VMEM((local,), jnp.int32),
+            pltpu.VMEM((batch, z.wide), F32),
+            pltpu.VMEM((8, z.wide), F32),
+            pltpu.SemaphoreType.DMA((3,)),
+        ],
         [initial_rates, cell_type, input_map],
-    )
-    got = share(message, "row", z.rows)
+        {0: HBM, 1: HBM, 2: HBM},
+    )
+    got = share(message, "row")
     weights, ids = call(
         functools.partial(load_kernel, z),
         [shape((slots, BLOCK, BLOCK), BF16), shape((2 * slots,), jnp.int32)],
-        [pltpu.SemaphoreType.DMA],
+        [pltpu.SMEM((1, 1, slots), jnp.int32)] * 3 + [pltpu.SemaphoreType.DMA((4,))],
         [message, slot_owner, slot_post, slot_pre, weight_blocks],
-        {1: SMEM, 2: SMEM, 3: SMEM, 4: ANY},
+        {1: HBM, 2: HBM, 3: HBM, 4: HBM},
         out_specs=[VMEM, SMEM],
     )
     if few(z.rows):
@@ -491,102 +509,96 @@
     pre_sums = pltpu.VMEM((z.pre, batch, BLOCK), F32)
     post_sums = pltpu.VMEM((2 * z.post, batch, BLOCK), F32)
     x_shape = shape((z.pre, batch, BLOCK), BF16)
-    col_parts = parcel(z.cols, pair, BF16)
-    row_parts = parcel(z.half, pair, BF16)
+    row_parts = parcel(z.rows, pair, BF16)
     x, own, *parts = call(
         functools.partial(first_kernel, z, len(got)),
-        [x_shape, shape(pair), *col_parts],
+        [x_shape, shape(pair), *parcel(z.cols, pair, BF16, True)],
         [pre_sums, post_sums],
         [ids, weights, message, *got],
         {0: SMEM},
         flops=product_flops,
     )
+    every = (z.rows * z.piece, BLOCK)
     rates, gain, drive, cots = call(
-        functools.partial(prepare_kernel, z),
-        [shape(pair), shape(pair), shape((steps, *pair)), shape((steps, z.piece, BLOCK))],
+        functools.partial(prepare_kernel, z, len(got)),
+        [shape(every), shape(every), shape((steps, *every)), shape((steps, z.piece, BLOCK))],
         [pltpu.VMEM((batch, z.wide), F32)],
         [
             message,
-            partner_message,
-            initial_rates,
+            own_rates,
             cotangent,
             type_gain.reshape(types // BLOCK, BLOCK),
             stimuli.reshape(steps * batch, channels),
+            *got,
         ],
     )
     xs, acts, curs = [x], [], []
     for t in range(steps):
         last = t == steps - 1
-        got = exchange(parts, "col", z.cols)
+        got = exchange(parts, "col")
         kept, sent = call(
             functools.partial(sum_kernel, z, len(got), last),
             [shape(pair), shape((closing, BLOCK) if last else pair, BF16)],
             [],
             [own, *got] + ([cots] if last else []),
         )
-        theirs = flip(sent, "row", z.half)
         if last:
             break
-        rates, act, cur, lowered = call(
-            functools.partial(rate_kernel, z, t),
-            [shape(pair), shape(pair), shape(pair), shape(pair, BF16)],
-            [],
-            [kept, theirs, rates, gain, drive],
-        )
-        got = share(lowered, "row", z.half)
-        x, own, *parts = call(
-            functools.partial(forward_kernel, z, len(got)),
-            [x_shape, shape(pair), *col_parts],
+        got = share(sent, "row")
+        rates, act, cur, x, own, *parts = call(
+            functools.partial(forward_kernel, z, t, len(got)),
+            [shape(every), shape(pair), shape(pair), x_shape, shape(pair)]
+            + parcel(z.cols, pair, BF16),
             [pre_sums, post_sums],
-            [ids, weights, lowered, *got],
+            [ids, weights, kept, rates, gain, drive, *got],
             {0: SMEM},
             flops=product_flops,
         )
         xs.append(x)
         acts.append(act)
         curs.append(cur)
-    final_rates, delta, tally, base = call(
+    theirs = flip(sent, "row", z.half)
+    final_rates, delta, gain, tally, base = call(
         functools.partial(turn_kernel, z),
-        [shape((batch, local)), shape(pair, BF16), shape(pair), shape((z.piece, BLOCK))],
+        [
+            shape((batch, local)),
+            shape(pair, BF16),
+            shape(pair),
+            shape(pair),
+            shape((z.piece, BLOCK)),
+        ],
         [],
         [kept, theirs, rates, gain, drive, cots],
     )
     ds = []
     for t in reversed(range(1, steps)):
-        got = share(delta, "col", z.cols)
+        got = share(delta, "col")
         d, own, *parts = call(
             functools.partial(back_kernel, z, len(got)),
             [shape((2 * z.post, batch, BLOCK), BF16), shape(pair), *row_parts],
             [post_sums, pre_sums],
-            [ids, weights, delta, *got],
+            [ids, weights, base, delta, *got],
             {0: SMEM},
             flops=product_flops,
         )
         ds.insert(0, d)
-        got = exchange(parts, "row", z.half)
-        kept, sent = call(
-            functools.partial(near_kernel, z, len(got)),
-            [shape(pair), shape(pair, BF16)],
-            [],
-            [own, base, *got],
-        )
-        theirs = flip(sent, "row", z.half)
+        got = exchange(parts, "row")
         before = t - 1
         if before > 0:
             delta, tally, base = call(
-                functools.partial(delta_kernel, z, before),
+                functools.partial(delta_kernel, z, before, len(got)),
                 [shape(pair, BF16), shape(pair), shape((z.piece, BLOCK))],
                 [],
-                [kept, theirs, gain, acts[before], curs[before], tally, cots],
+                [own, gain, acts[before], curs[before], tally, cots, *got],
             )
         else:
             (delta,) = call(
-                functools.partial(last_delta_kernel, z),
+                functools.partial(last_delta_kernel, z, len(got)),
                 [shape((z.pair + 2 * CODES, BLOCK), BF16)],
                 [],
-                [kept, theirs, gain, acts[0], curs[0], tally, message, partner_message],
+                [own, gain, acts[0], curs[0], tally, message, partner_message, *got],
             )
-    got = share(delta, "col", z.cols)
+    got = share(delta, "col")
     (table,) = call(
         functools.partial(table_kernel, z, len(got)), [shape((types // BLOCK, BLOCK))], [], [delta, *got]
     )

time: 101 us -> 98 us (0.970)
  waiting for transfers between devices: 52 us -> 31.2 us
  starting transfers between devices: 24.4 us -> 34.7 us
  blocking collectives: 0 us -> 7.52 us
    ppermute x31 -> x32, waiting for transfers between devices: 52 us -> 31.2 us  [flip(): return lax.ppermute(x, axis, [(i, i ^ k) for i in range(count)])]
    ppermute x31 -> x32, starting transfers between devices: 24.4 us -> 34.7 us  [flip(): return lax.ppermute(x, axis, [(i, i ^ k) for i in range(count)])]
    all_to_all x0 -> x1, blocking collectives: none -> 7.52 us  [exchange(): return [lax.all_to_all(parts[0], axis, 0, 0, tiled=True)]]
    pallas_call x19 -> x15, Pallas kernels: 13.4 us -> 13.6 us  [call(): pl.pallas_call(body, out_shape=outs, in_specs=specs, out_specs=out_specs...]
    unnamed x22 -> x20, local copies, waits for them, and re-layouts: 5.72 us -> 5.72 us
  transfers between devices with their start and end apart: 31 -> 32, of which waited for: 22 -> 19; matrix products, arithmetic and copies ran while one was open for 0% -> 0% of each run, Pallas kernels for 6% -> 6%
where the time goes in v3:
time: 98 us; the launch traced here: 97.7 us
  starting transfers between devices  34.7 us (35%)
  waiting for transfers between devices  31.2 us (32%)
  Pallas kernels  17.2 us (18%)
  blocking collectives  7.52 us (8%)
  local copies, waits for them, and re-layouts  5.72 us (6%)
    ppermute x32, starting transfers between devices, flip(): return lax.ppermute(x, axis, [(i, i ^ k) for i in range(count)])  34.7 us
    ppermute x32, waiting for transfers between devices, flip(): return lax.ppermute(x, axis, [(i, i ^ k) for i in range(count)])  31.2 us
    pallas_call x15, Pallas kernels, call(): pl.pallas_call(body, out_shape=outs, in_specs=specs, out_specs=out_specs...  13.6 us
    all_to_all x1, blocking collectives, exchange(): return [lax.all_to_all(parts[0], axis, 0, 0, tiled=True)]  7.52 us
    unnamed x20, local copies, waits for them, and re-layouts  5.72 us
    pallas_call x1, Pallas kernels, shards(): pl.pallas_call(functools.partial(grad_kernel, z, len(got), per_step), gri...  3.56 us
  transfers between devices with their start and end apart: 32, of which 19 were waited for; matrix products, arithmetic and copies ran while one was open for 0% of the time, Pallas kernels for 6%

profile of v3, /device:TPU:0, one launch (start us, length us, event | category | flops | bytes accessed | tf_op | source)
XLA Modules:
  0.0 97.7 jit_solution(8580164250014374249)
XLA Ops:
  0.6 0.8 copy-done.3
  1.4 0.7 copy-done.5
  2.1 0.7 copy-done.6
  2.8 0.2 shard_map.121
  3.0 5.1 %collective-permute-start.2 = (bf16[96,128]{1,0:T(8,128)(2,1)S(1)}, bf16[96,128]{1,0:T(8,128)(2,1)S(1)}, u32[]{:S(2)}, u32[]{:S(2)}) collective-permute-start(bf16[96,128]{1,0:T(8,128)(2,1)S(1)} %get-tuple-element.54.after.refs_2_.refs_0_.mine), channel_id=1, source_target_pairs={{0,12},{4,8},{8,4},{12,0},{1,13},{5,9},{9,5},{13,1},{2,14},{6,10},... | collective-permute-start | bytes 73736 | tf_op jit(solution)/shard_map/ppermute | solution.py:97
  8.1 0.6 collective-permute-start
  8.7 1.6 %copy-done = bf16[1,1,64,128,128]{4,3,2,1,0:T(8,128)(2,1)S(1)} copy-done((bf16[1,1,64,128,128]{4,3,2,1,0:T(8,128)(2,1)S(1)}, bf16[1,1,64,128,128]{4,3,2,1,0:T(8,128)(2,1)}, u32[]{:S(2)}) %copy-start) | copy-done | bytes 2097176
  10.3 0.7 copy-done.7
  11.0 0.7 copy-done.8
  11.6 0.7 copy-done.9
  12.3 1.4 %shard_map.122 = (bf16[64,128,128]{2,1,0:T(8,128)(2,1)S(1)}, s32[128]{0:T(128)S(1)}) custom-call(bf16[96,128]{1,0:T(8,128)(2,1)S(1)} %get-tuple-element.54.after.refs_2_.refs_0_.mine, s32[1,1,64]{2,1,0:T(1,128)S(1)} %copy-done.7, s32[1,1,64]{2,1,0:T(1,128)S(1)} %copy-done.8, s32[1,1,64]{2,1,0:T(1,128)S(1)} %copy-done.9, bf16[1,1,64,128,128]{4,3,2,1,0:T(8,128)(2,1)S(1)} %copy-done), custom_call_target="tpu_custom_call" | custom-call | bytes 4220160 | tf_op jit(solution)/shard_map/pallas_call | solution.py:80
  13.7 2.1 %shard_map.123 = (bf16[9,32,128]{2,1,0:T(8,128)(2,1)S(1)}, f32[144,128]{1,0:T(8,128)S(1)}, bf16[4,144,128]{2,1,0:T(8,128)(2,1)S(1)}) custom-call(s32[128]{0:T(128)S(1)} %get-tuple-element.55.refs_0_, bf16[64,128,128]{2,1,0:T(8,128)(2,1)S(1)} %get-tuple-element.56.refs_1_, bf16[96,128]{1,0:T(8,128)(2,1)S(1)} %get-tuple-element.54.after.refs_2_.refs_0_.mine, ...), custom_call_target="tpu_custom_call" | custom-call | flops 67108864 | bytes 2490880 | tf_op jit(solution)/shard_map/pallas_call | solution.py:80
  15.8 7.5 %all_to_all.5.refs_1_ = bf16[4,144,128]{2,1,0:T(8,128)(2,1)S(1)} all-to-all(bf16[4,144,128]{2,1,0:T(8,128)(2,1)S(1)} %get-tuple-element.58), channel_id=1, replica_groups=mesh['groups'=2,'row'=4,'col'=4] {'col'}, dimensions={0} | all-to-all | bytes 294912 | tf_op jit(solution)/shard_map/all_to_all | solution.py:115
  23.4 3.7 %collective-permute-start.5 = (bf16[144,128]{1,0:T(8,128)(2,1)S(1)}, bf16[144,128]{1,0:T(8,128)(2,1)S(1)}, u32[]{:S(2)}, u32[]{:S(2)}) collective-permute-start(bf16[144,128]{1,0:T(8,128)(2,1)S(1)} %get-tuple-element.64), channel_id=1, source_target_pairs={{0,12},{4,8},{8,4},{12,0},{1,13},{5,9},{9,5},{13,1},{2,14},{6,10},... | collective-permute-start | bytes 110600 | tf_op jit(solution)/shard_map/ppermute | solution.py:97
  27.0 0.8 collective-permute-start.3
  27.8 0.9 shard_map.125
  28.8 0.8 collective-permute-done.5.refs_8_
  29.6 2.3 %collective-permute-done.4.refs_7_ = bf16[144,128]{1,0:T(8,128)(2,1)S(1)} collective-permute-done((bf16[144,128]{1,0:T(8,128)(2,1)S(1)}, bf16[144,128]{1,0:T(8,128)(2,1)S(1)}, u32[]{:S(2)}, u32[]{:S(2)}) %collective-permute-start.4) | collective-permute-done | bytes 36896 | tf_op jit(solution)/shard_map/ppermute | solution.py:97
  31.9 2.1 %shard_map.126 = (f32[288,128]{1,0:T(8,128)S(1)}, f32[144,128]{1,0:T(8,128)S(1)}, f32[144,128]{1,0:T(8,128)S(1)}, bf16[9,32,128]{2,1,0:T(8,128)(2,1)S(1)}, f32[1...) custom-call(s32[128]{0:T(128)S(1)} %get-tuple-element.55.refs_0_, ...), custom_call_target="tpu_custom_call" | custom-call | flops 67108864 | bytes 3572224 | tf_op jit(solution)/shard_map/pallas_call | solution.py:80
  34.1 0.4 collective-permute-start.7
  34.5 1.4 %collective-permute-start.8 = (bf16[144,128]{1,0:T(8,128)(2,1)S(1)}, bf16[144,128]{1,0:T(8,128)(2,1)S(1)}, u32[]{:S(2)}, u32[]{:S(2)}) collective-permute-start(bf16[144,128]{1,0:T(8,128)(2,1)S(1)} %get-tuple-element.68), channel_id=1, source_target_pairs={{0,3},{1,2},{2,1},{3,0},{4,7},{5,6},{6,5},{7,4},{8,11},{9,10},{10,... | collective-permute-start | bytes 110600 | tf_op jit(solution)/shard_map/ppermute | solution.py:97
  36.0 2.4 %collective-permute-done.7.refs_2_ = bf16[144,128]{1,0:T(8,128)(2,1)S(1)} collective-permute-done((bf16[144,128]{1,0:T(8,128)(2,1)S(1)}, bf16[144,128]{1,0:T(8,128)(2,1)S(1)}, u32[]{:S(2)}, u32[]{:S(2)}) %collective-permute-start.7) | collective-permute-done | bytes 36896 | tf_op jit(solution)/shard_map/ppermute | solution.py:97
  38.4 1.6 %collective-permute-start.11 = (bf16[144,128]{1,0:T(8,128)(2,1)S(1)}, bf16[144,128]{1,0:T(8,128)(2,1)S(1)}, u32[]{:S(2)}, u32[]{:S(2)}) collective-permute-start(bf16[144,128]{1,0:T(8,128)(2,1)S(1)} %get-tuple-element.71), channel_id=1, source_target_pairs={{0,12},{4,8},{8,4},{12,0},{1,13},{5,9},{9,5},{13,1},{2,14},{6,10},... | collective-permute-start | bytes 110600 | tf_op jit(solution)/shard_map/ppermute | solution.py:97
  40.0 0.6 collective-permute-start.10
  40.6 2.3 %collective-permute-start.9 = (bf16[144,128]{1,0:T(8,128)(2,1)S(1)}, bf16[144,128]{1,0:T(8,128)(2,1)S(1)}, u32[]{:S(2)}, u32[]{:S(2)}) collective-permute-start(bf16[144,128]{1,0:T(8,128)(2,1)S(1)} %get-tuple-element.71), channel_id=1, source_target_pairs={{0,4},{4,0},{8,12},{12,8},{1,5},{5,1},{9,13},{13,9},{2,6},{6,2},{1... | collective-permute-start | bytes 110600 | tf_op jit(solution)/shard_map/ppermute | solution.py:97
  42.9 1.7 %collective-permute-done.11.refs_8_ = bf16[144,128]{1,0:T(8,128)(2,1)S(1)} collective-permute-done((bf16[144,128]{1,0:T(8,128)(2,1)S(1)}, bf16[144,128]{1,0:T(8,128)(2,1)S(1)}, u32[]{:S(2)}, u32[]{:S(2)}) %collective-permute-start.11) | collective-permute-done | bytes 36896 | tf_op jit(solution)/shard_map/ppermute | solution.py:97
  44.5 0.9 collective-permute-done.10.refs_7_
  45.5 2.1 %shard_map.128 = (f32[288,128]{1,0:T(8,128)S(1)}, f32[144,128]{1,0:T(8,128)S(1)}, f32[144,128]{1,0:T(8,128)S(1)}, bf16[9,32,128]{2,1,0:T(8,128)(2,1)S(1)}, f32[1...) custom-call(s32[128]{0:T(128)S(1)} %get-tuple-element.55.refs_0_, ...), custom_call_target="tpu_custom_call" | custom-call | flops 67108864 | bytes 3572224 | tf_op jit(solution)/shard_map/pallas_call | solution.py:80
  47.7 1.2 %collective-permute-start.13 = (bf16[144,128]{1,0:T(8,128)(2,1)S(1)}, bf16[144,128]{1,0:T(8,128)(2,1)S(1)}, u32[]{:S(2)}, u32[]{:S(2)}) collective-permute-start(bf16[144,128]{1,0:T(8,128)(2,1)S(1)} %get-tuple-element.74), channel_id=1, source_target_pairs={{0,2},{1,3},{2,0},{3,1},{4,6},{5,7},{6,4},{7,5},{8,10},{9,11},{10,... | collective-permute-start | bytes 110600 | tf_op jit(solution)/shard_map/ppermute | solution.py:97
  48.9 0.6 collective-permute-start.14
  49.5 2.2 %collective-permute-done.13.refs_2_ = bf16[144,128]{1,0:T(8,128)(2,1)S(1)} collective-permute-done((bf16[144,128]{1,0:T(8,128)(2,1)S(1)}, bf16[144,128]{1,0:T(8,128)(2,1)S(1)}, u32[]{:S(2)}, u32[]{:S(2)}) %collective-permute-start.13) | collective-permute-done | bytes 36896 | tf_op jit(solution)/shard_map/ppermute | solution.py:97
  51.7 0.7 collective-permute-done.14.refs_3_
  52.4 1.6 %collective-permute-start.15 = (bf16[224,128]{1,0:T(8,128)(2,1)S(1)}, bf16[224,128]{1,0:T(8,128)(2,1)S(1)}, u32[]{:S(2)}, u32[]{:S(2)}) collective-permute-start(bf16[224,128]{1,0:T(8,128)(2,1)S(1)} %get-tuple-element.78), channel_id=1, source_target_pairs={{0,8},{4,12},{8,0},{12,4},{1,9},{5,13},{9,1},{13,5},{2,10},{6,14},... | collective-permute-start | bytes 172040 | tf_op jit(solution)/shard_map/ppermute | solution.py:97
  53.9 4.8 %collective-permute-done.15.theirs = bf16[224,128]{1,0:T(8,128)(2,1)S(1)} collective-permute-done((bf16[224,128]{1,0:T(8,128)(2,1)S(1)}, bf16[224,128]{1,0:T(8,128)(2,1)S(1)}, u32[]{:S(2)}, u32[]{:S(2)}) %collective-permute-start.15) | collective-permute-done | bytes 57376 | tf_op jit(solution)/shard_map/ppermute | solution.py:97
  58.7 0.7 shard_map.130
  59.5 1.1 %collective-permute-start.17 = (bf16[144,128]{1,0:T(8,128)(2,1)S(1)}, bf16[144,128]{1,0:T(8,128)(2,1)S(1)}, u32[]{:S(2)}, u32[]{:S(2)}) collective-permute-start(bf16[144,128]{1,0:T(8,128)(2,1)S(1)} %get-tuple-element.85.refs_3_), channel_id=1, source_target_pairs={{0,2},{1,3},{2,0},{3,1},{4,6},{5,7},{6,4},{7,5},{8,10},{9,11},{10,... | collective-permute-start | bytes 110600 | tf_op jit(solution)/shard_map/ppermute | solution.py:97
  60.6 0.7 collective-permute-start.16
  61.3 1.6 %collective-permute-done.18.refs_6_ = bf16[144,128]{1,0:T(8,128)(2,1)S(1)} collective-permute-done((bf16[144,128]{1,0:T(8,128)(2,1)S(1)}, bf16[144,128]{1,0:T(8,128)(2,1)S(1)}, u32[]{:S(2)}, u32[]{:S(2)}) %collective-permute-start.18) | collective-permute-done | bytes 36896 | tf_op jit(solution)/shard_map/ppermute | solution.py:97
  62.9 0.8 collective-permute-done.17.refs_5_
  63.6 1.6 %shard_map.131 = (bf16[18,32,128]{2,1,0:T(8,128)(2,1)S(1)}, f32[144,128]{1,0:T(8,128)S(1)}, bf16[144,128]{1,0:T(8,128)(2,1)S(1)}, bf16[144,128]{1,0:T(8,128)(2,1)S(1)}, bf16[144,128]{1,0:T(8,128)(2,1)S(1)}) custom-call(s32[128]{0:T(128)S(1)} %get-tuple-element.55.refs_0_, bf16[64,128,128]{2,1,0:T(8,128)(2,1)S(1)} %get-tuple-element.56.refs_1_, ...), custom_call_target="tpu_custom_call" | custom-call | flops 67108864 | bytes 2613760 | tf_op jit(solution)/shard_map/pallas_call | solution.py:80
  65.2 0.2 collective-permute-start.19
  65.5 3.0 %collective-permute-start.20 = (bf16[144,128]{1,0:T(8,128)(2,1)S(1)}, bf16[144,128]{1,0:T(8,128)(2,1)S(1)}, u32[]{:S(2)}, u32[]{:S(2)}) collective-permute-start(bf16[144,128]{1,0:T(8,128)(2,1)S(1)} %get-tuple-element.92), channel_id=1, source_target_pairs={{0,8},{4,12},{8,0},{12,4},{1,9},{5,13},{9,1},{13,5},{2,10},{6,14},... | collective-permute-start | bytes 110600 | tf_op jit(solution)/shard_map/ppermute | solution.py:97
  68.4 1.3 %collective-permute-start.21 = (bf16[144,128]{1,0:T(8,128)(2,1)S(1)}, bf16[144,128]{1,0:T(8,128)(2,1)S(1)}, u32[]{:S(2)}, u32[]{:S(2)}) collective-permute-start(bf16[144,128]{1,0:T(8,128)(2,1)S(1)} %get-tuple-element.93), channel_id=1, source_target_pairs={{0,12},{4,8},{8,4},{12,0},{1,13},{5,9},{9,5},{13,1},{2,14},{6,10},... | collective-permute-start | bytes 110600 | tf_op jit(solution)/shard_map/ppermute | solution.py:97
  69.7 1.4 %collective-permute-done.20.refs_1_ = bf16[144,128]{1,0:T(8,128)(2,1)S(1)} collective-permute-done((bf16[144,128]{1,0:T(8,128)(2,1)S(1)}, bf16[144,128]{1,0:T(8,128)(2,1)S(1)}, u32[]{:S(2)}, u32[]{:S(2)}) %collective-permute-start.20) | collective-permute-done | bytes 36896 | tf_op jit(solution)/shard_map/ppermute | solution.py:97
  71.1 3.1 %collective-permute-done.21.refs_2_ = bf16[144,128]{1,0:T(8,128)(2,1)S(1)} collective-permute-done((bf16[144,128]{1,0:T(8,128)(2,1)S(1)}, bf16[144,128]{1,0:T(8,128)(2,1)S(1)}, u32[]{:S(2)}, u32[]{:S(2)}) %collective-permute-start.21) | collective-permute-done | bytes 36896 | tf_op jit(solution)/shard_map/ppermute | solution.py:97
  74.2 0.1 collective-permute-start.24
  74.3 1.1 %collective-permute-start.23 = (bf16[144,128]{1,0:T(8,128)(2,1)S(1)}, bf16[144,128]{1,0:T(8,128)(2,1)S(1)}, u32[]{:S(2)}, u32[]{:S(2)}) collective-permute-start(bf16[144,128]{1,0:T(8,128)(2,1)S(1)} %get-tuple-element.95.refs_3_), channel_id=1, source_target_pairs={{0,2},{1,3},{2,0},{3,1},{4,6},{5,7},{6,4},{7,5},{8,10},{9,11},{10,... | collective-permute-start | bytes 110600 | tf_op jit(solution)/shard_map/ppermute | solution.py:97
  75.4 0.7 collective-permute-start.22
  76.2 1.5 %collective-permute-done.24.refs_6_ = bf16[144,128]{1,0:T(8,128)(2,1)S(1)} collective-permute-done((bf16[144,128]{1,0:T(8,128)(2,1)S(1)}, bf16[144,128]{1,0:T(8,128)(2,1)S(1)}, u32[]{:S(2)}, u32[]{:S(2)}) %collective-permute-start.24) | collective-permute-done | bytes 36896 | tf_op jit(solution)/shard_map/ppermute | solution.py:97
  77.7 0.9 collective-permute-done.23.refs_5_
  78.6 1.6 %shard_map.133 = (bf16[18,32,128]{2,1,0:T(8,128)(2,1)S(1)}, f32[144,128]{1,0:T(8,128)S(1)}, bf16[144,128]{1,0:T(8,128)(2,1)S(1)}, bf16[144,128]{1,0:T(8,128)(2,1)S(1)}, bf16[144,128]{1,0:T(8,128)(2,1)S(1)}) custom-call(s32[128]{0:T(128)S(1)} %get-tuple-element.55.refs_0_, bf16[64,128,128]{2,1,0:T(8,128)(2,1)S(1)} %get-tuple-element.56.refs_1_, ...), custom_call_target="tpu_custom_call" | custom-call | flops 67108864 | bytes 2613760 | tf_op jit(solution)/shard_map/pallas_call | solution.py:80
  80.3 1.6 %collective-permute-start.26 = (bf16[144,128]{1,0:T(8,128)(2,1)S(1)}, bf16[144,128]{1,0:T(8,128)(2,1)S(1)}, u32[]{:S(2)}, u32[]{:S(2)}) collective-permute-start(bf16[144,128]{1,0:T(8,128)(2,1)S(1)} %get-tuple-element.103), channel_id=1, source_target_pairs={{0,8},{4,12},{8,0},{12,4},{1,9},{5,13},{9,1},{13,5},{2,10},{6,14},... | collective-permute-start | bytes 110600 | tf_op jit(solution)/shard_map/ppermute | solution.py:97
  81.9 2.7 %collective-permute-start.27 = (bf16[144,128]{1,0:T(8,128)(2,1)S(1)}, bf16[144,128]{1,0:T(8,128)(2,1)S(1)}, u32[]{:S(2)}, u32[]{:S(2)}) collective-permute-start(bf16[144,128]{1,0:T(8,128)(2,1)S(1)} %get-tuple-element.104), channel_id=1, source_target_pairs={{0,12},{4,8},{8,4},{12,0},{1,13},{5,9},{9,5},{13,1},{2,14},{6,10},... | collective-permute-start | bytes 110600 | tf_op jit(solution)/shard_map/ppermute | solution.py:97
  84.7 0.9 collective-permute-done.26.refs_1_
  85.6 2.1 %collective-permute-done.27.refs_2_ = bf16[144,128]{1,0:T(8,128)(2,1)S(1)} collective-permute-done((bf16[144,128]{1,0:T(8,128)(2,1)S(1)}, bf16[144,128]{1,0:T(8,128)(2,1)S(1)}, u32[]{:S(2)}, u32[]{:S(2)}) %collective-permute-start.27) | collective-permute-done | bytes 36896 | tf_op jit(solution)/shard_map/ppermute | solution.py:97
  87.7 0.1 shard_map.134.refs_6_.refs_0_
  87.9 1.5 %collective-permute-start.29 = (bf16[176,128]{1,0:T(8,128)(2,1)S(1)}, bf16[176,128]{1,0:T(8,128)(2,1)S(1)}, u32[]{:S(2)}, u32[]{:S(2)}) collective-permute-start(bf16[176,128]{1,0:T(8,128)(2,1)S(1)} %shard_map.134.refs_6_.refs_0_), channel_id=1, source_target_pairs={{0,2},{1,3},{2,0},{3,1},{4,6},{5,7},{6,4},{7,5},{8,10},{9,11},{10,... | collective-permute-start | bytes 135176 | tf_op jit(solution)/shard_map/ppermute | solution.py:97
  89.4 0.4 collective-permute-start.28
  89.7 2.1 %collective-permute-done.30.refs_9_.refs_3_ = bf16[176,128]{1,0:T(8,128)(2,1)S(1)} collective-permute-done((bf16[176,128]{1,0:T(8,128)(2,1)S(1)}, bf16[176,128]{1,0:T(8,128)(2,1)S(1)}, u32[]{:S(2)}, u32[]{:S(2)}) %collective-permute-start.30) | collective-permute-done | bytes 45088 | tf_op jit(solution)/shard_map/ppermute | solution.py:97
  91.8 0.7 collective-permute-done.29.refs_8_.refs_2_
  92.5 0.6 shard_map.136
  93.2 3.6 %shard_map.135 = bf16[64,128,128]{2,1,0:T(8,128)(2,1)} custom-call(s32[128]{0:T(128)S(1)} %get-tuple-element.55.refs_0_, bf16[9,32,128]{2,1,0:T(8,128)(2,1)S(1)} %get-tuple-element.81.refs_1_, bf16[9,32,128]{2,1,0:T(8,128)(2,1)S(1)} %get-tuple-element.82.refs_2_, bf16[9,32,128]{2,1,0:T(8,128)(2,1)S(1)} %get-tuple-element.83.refs_3_, ...), custom_call_target="tpu_custom_call" | custom-call | flops 268435456 | bytes 4194304 | tf_op jit(solution)/shard_map/pallas_call | solution.py:615
  96.8 0.3 collective-permute-done.31
  97.1 0.6 add_bitcast_fusion
  (38 shorter events, 0.5 us)
Async XLA Ops:
  0.6 0.8 copy-start.3
  1.4 0.7 copy-start.5
  2.1 0.7 copy-start.6
  2.8 25.0 %copy-start.4 = (f32[8192]{0:T(1024)S(1)}, f32[8192]{0:T(1024)}, u32[]{:S(2)}) copy-start(f32[8192]{0:T(1024)} %param.18) | copy-start | bytes 98308
  3.0 10.7 %collective-permute-start.2 = (bf16[96,128]{1,0:T(8,128)(2,1)S(1)}, bf16[96,128]{1,0:T(8,128)(2,1)S(1)}, u32[]{:S(2)}, u32[]{:S(2)}) collective-permute-start(bf16[96,128]{1,0:T(8,128)(2,1)S(1)} %get-tuple-element.54.after.refs_2_.refs_0_.mine), channel_id=1, source_target_pairs={{0,12},{4,8},{8,4},{12,0},{1,13},{5,9},{9,5},{13,1},{2,14},{6,10},... | collective-permute-start | bytes 73736 | tf_op jit(solution)/shard_map/ppermute | solution.py:97
  8.1 5.6 %collective-permute-start.1 = (bf16[96,128]{1,0:T(8,128)(2,1)S(1)}, bf16[96,128]{1,0:T(8,128)(2,1)S(1)}, u32[]{:S(2)}, u32[]{:S(2)}) collective-permute-start(bf16[96,128]{1,0:T(8,128)(2,1)S(1)} %get-tuple-element.54.after.refs_2_.refs_0_.mine), channel_id=1, source_target_pairs={{0,8},{4,12},{8,0},{12,4},{1,9},{5,13},{9,1},{13,5},{2,10},{6,14},... | collective-permute-start | bytes 73736 | tf_op jit(solution)/shard_map/ppermute | solution.py:97
  8.1 5.6 %collective-permute-start = (bf16[96,128]{1,0:T(8,128)(2,1)S(1)}, bf16[96,128]{1,0:T(8,128)(2,1)S(1)}, u32[]{:S(2)}, u32[]{:S(2)}) collective-permute-start(bf16[96,128]{1,0:T(8,128)(2,1)S(1)} %get-tuple-element.54.after.refs_2_.refs_0_.mine), channel_id=1, source_target_pairs={{0,4},{4,0},{8,12},{12,8},{1,5},{5,1},{9,13},{13,9},{2,6},{6,2},{1... | collective-permute-start | bytes 73736 | tf_op jit(solution)/shard_map/ppermute | solution.py:97
  8.7 1.6 %copy-start = (bf16[1,1,64,128,128]{4,3,2,1,0:T(8,128)(2,1)S(1)}, bf16[1,1,64,128,128]{4,3,2,1,0:T(8,128)(2,1)}, u32[]{:S(2)}) copy-start(bf16[1,1,64,128,128]{4,3,2,1,0:T(8,128)(2,1)} %weights.1) | copy-start | bytes 6291460
  10.3 0.7 copy-start.7
  11.0 0.7 copy-start.8
  11.6 0.7 copy-start.9
  12.3 15.5 %copy-start.1 = (f32[3,32,288]{2,1,0:T(8,128)S(1)}, f32[3,32,288]{2,1,0:T(8,128)}, u32[]{:S(2)}) copy-start(f32[3,32,288]{2,1,0:T(8,128)} %refs_2_.1) | copy-start | bytes 331780
  12.3 15.5 %copy-start.2 = (bf16[3,32,512]{2,1,0:T(8,128)(2,1)S(1)}, bf16[3,32,512]{2,1,0:T(8,128)(2,1)}, u32[]{:S(2)}) copy-start(bf16[3,32,512]{2,1,0:T(8,128)(2,1)} %param.11) | copy-start | bytes 294916
  23.4 6.2 %collective-permute-start.5 = (bf16[144,128]{1,0:T(8,128)(2,1)S(1)}, bf16[144,128]{1,0:T(8,128)(2,1)S(1)}, u32[]{:S(2)}, u32[]{:S(2)}) collective-permute-start(bf16[144,128]{1,0:T(8,128)(2,1)S(1)} %get-tuple-element.64), channel_id=1, source_target_pairs={{0,12},{4,8},{8,4},{12,0},{1,13},{5,9},{9,5},{13,1},{2,14},{6,10},... | collective-permute-start | bytes 110600 | tf_op jit(solution)/shard_map/ppermute | solution.py:97
  27.0 4.9 %collective-permute-start.4 = (bf16[144,128]{1,0:T(8,128)(2,1)S(1)}, bf16[144,128]{1,0:T(8,128)(2,1)S(1)}, u32[]{:S(2)}, u32[]{:S(2)}) collective-permute-start(bf16[144,128]{1,0:T(8,128)(2,1)S(1)} %get-tuple-element.64), channel_id=1, source_target_pairs={{0,8},{4,12},{8,0},{12,4},{1,9},{5,13},{9,1},{13,5},{2,10},{6,14},... | collective-permute-start | bytes 110600 | tf_op jit(solution)/shard_map/ppermute | solution.py:97
  27.0 4.9 %collective-permute-start.3 = (bf16[144,128]{1,0:T(8,128)(2,1)S(1)}, bf16[144,128]{1,0:T(8,128)(2,1)S(1)}, u32[]{:S(2)}, u32[]{:S(2)}) collective-permute-start(bf16[144,128]{1,0:T(8,128)(2,1)S(1)} %get-tuple-element.64), channel_id=1, source_target_pairs={{0,4},{4,0},{8,12},{12,8},{1,5},{5,1},{9,13},{13,9},{2,6},{6,2},{1... | collective-permute-start | bytes 110600 | tf_op jit(solution)/shard_map/ppermute | solution.py:97
  34.0 1.9 %collective-permute-start.6 = (bf16[144,128]{1,0:T(8,128)(2,1)S(1)}, bf16[144,128]{1,0:T(8,128)(2,1)S(1)}, u32[]{:S(2)}, u32[]{:S(2)}) collective-permute-start(bf16[144,128]{1,0:T(8,128)(2,1)S(1)} %get-tuple-element.66), channel_id=1, source_target_pairs={{0,1},{1,0},{2,3},{3,2},{4,5},{5,4},{6,7},{7,6},{8,9},{9,8},{10,11... | collective-permute-start | bytes 110600 | tf_op jit(solution)/shard_map/ppermute | solution.py:97
  34.1 4.3 %collective-permute-start.7 = (bf16[144,128]{1,0:T(8,128)(2,1)S(1)}, bf16[144,128]{1,0:T(8,128)(2,1)S(1)}, u32[]{:S(2)}, u32[]{:S(2)}) collective-permute-start(bf16[144,128]{1,0:T(8,128)(2,1)S(1)} %get-tuple-element.67), channel_id=1, source_target_pairs={{0,2},{1,3},{2,0},{3,1},{4,6},{5,7},{6,4},{7,5},{8,10},{9,11},{10,... | collective-permute-start | bytes 110600 | tf_op jit(solution)/shard_map/ppermute | solution.py:97
  34.5 3.9 %collective-permute-start.8 = (bf16[144,128]{1,0:T(8,128)(2,1)S(1)}, bf16[144,128]{1,0:T(8,128)(2,1)S(1)}, u32[]{:S(2)}, u32[]{:S(2)}) collective-permute-start(bf16[144,128]{1,0:T(8,128)(2,1)S(1)} %get-tuple-element.68), channel_id=1, source_target_pairs={{0,3},{1,2},{2,1},{3,0},{4,7},{5,6},{6,5},{7,4},{8,11},{9,10},{10,... | collective-permute-start | bytes 110600 | tf_op jit(solution)/shard_map/ppermute | solution.py:97
  38.4 6.1 %collective-permute-start.11 = (bf16[144,128]{1,0:T(8,128)(2,1)S(1)}, bf16[144,128]{1,0:T(8,128)(2,1)S(1)}, u32[]{:S(2)}, u32[]{:S(2)}) collective-permute-start(bf16[144,128]{1,0:T(8,128)(2,1)S(1)} %get-tuple-element.71), channel_id=1, source_target_pairs={{0,12},{4,8},{8,4},{12,0},{1,13},{5,9},{9,5},{13,1},{2,14},{6,10},... | collective-permute-start | bytes 110600 | tf_op jit(solution)/shard_map/ppermute | solution.py:97
  40.0 5.4 %collective-permute-start.10 = (bf16[144,128]{1,0:T(8,128)(2,1)S(1)}, bf16[144,128]{1,0:T(8,128)(2,1)S(1)}, u32[]{:S(2)}, u32[]{:S(2)}) collective-permute-start(bf16[144,128]{1,0:T(8,128)(2,1)S(1)} %get-tuple-element.71), channel_id=1, source_target_pairs={{0,8},{4,12},{8,0},{12,4},{1,9},{5,13},{9,1},{13,5},{2,10},{6,14},... | collective-permute-start | bytes 110600 | tf_op jit(solution)/shard_map/ppermute | solution.py:97
  40.6 4.9 %collective-permute-start.9 = (bf16[144,128]{1,0:T(8,128)(2,1)S(1)}, bf16[144,128]{1,0:T(8,128)(2,1)S(1)}, u32[]{:S(2)}, u32[]{:S(2)}) collective-permute-start(bf16[144,128]{1,0:T(8,128)(2,1)S(1)} %get-tuple-element.71), channel_id=1, source_target_pairs={{0,4},{4,0},{8,12},{12,8},{1,5},{5,1},{9,13},{13,9},{2,6},{6,2},{1... | collective-permute-start | bytes 110600 | tf_op jit(solution)/shard_map/ppermute | solution.py:97
  47.6 1.9 %collective-permute-start.12 = (bf16[144,128]{1,0:T(8,128)(2,1)S(1)}, bf16[144,128]{1,0:T(8,128)(2,1)S(1)}, u32[]{:S(2)}, u32[]{:S(2)}) collective-permute-start(bf16[144,128]{1,0:T(8,128)(2,1)S(1)} %get-tuple-element.73), channel_id=1, source_target_pairs={{0,1},{1,0},{2,3},{3,2},{4,5},{5,4},{6,7},{7,6},{8,9},{9,8},{10,11... | collective-permute-start | bytes 110600 | tf_op jit(solution)/shard_map/ppermute | solution.py:97
  47.7 4.0 %collective-permute-start.13 = (bf16[144,128]{1,0:T(8,128)(2,1)S(1)}, bf16[144,128]{1,0:T(8,128)(2,1)S(1)}, u32[]{:S(2)}, u32[]{:S(2)}) collective-permute-start(bf16[144,128]{1,0:T(8,128)(2,1)S(1)} %get-tuple-element.74), channel_id=1, source_target_pairs={{0,2},{1,3},{2,0},{3,1},{4,6},{5,7},{6,4},{7,5},{8,10},{9,11},{10,... | collective-permute-start | bytes 110600 | tf_op jit(solution)/shard_map/ppermute | solution.py:97
  48.9 3.4 %collective-permute-start.14 = (bf16[144,128]{1,0:T(8,128)(2,1)S(1)}, bf16[144,128]{1,0:T(8,128)(2,1)S(1)}, u32[]{:S(2)}, u32[]{:S(2)}) collective-permute-start(bf16[144,128]{1,0:T(8,128)(2,1)S(1)} %get-tuple-element.75), channel_id=1, source_target_pairs={{0,3},{1,2},{2,1},{3,0},{4,7},{5,6},{6,5},{7,4},{8,11},{9,10},{10,... | collective-permute-start | bytes 110600 | tf_op jit(solution)/shard_map/ppermute | solution.py:97
  52.4 6.4 %collective-permute-start.15 = (bf16[224,128]{1,0:T(8,128)(2,1)S(1)}, bf16[224,128]{1,0:T(8,128)(2,1)S(1)}, u32[]{:S(2)}, u32[]{:S(2)}) collective-permute-start(bf16[224,128]{1,0:T(8,128)(2,1)S(1)} %get-tuple-element.78), channel_id=1, source_target_pairs={{0,8},{4,12},{8,0},{12,4},{1,9},{5,13},{9,1},{13,5},{2,10},{6,14},... | collective-permute-start | bytes 172040 | tf_op jit(solution)/shard_map/ppermute | solution.py:97
  59.5 3.4 %collective-permute-start.18 = (bf16[144,128]{1,0:T(8,128)(2,1)S(1)}, bf16[144,128]{1,0:T(8,128)(2,1)S(1)}, u32[]{:S(2)}, u32[]{:S(2)}) collective-permute-start(bf16[144,128]{1,0:T(8,128)(2,1)S(1)} %get-tuple-element.85.refs_3_), channel_id=1, source_target_pairs={{0,3},{1,2},{2,1},{3,0},{4,7},{5,6},{6,5},{7,4},{8,11},{9,10},{10,... | collective-permute-start | bytes 110600 | tf_op jit(solution)/shard_map/ppermute | solution.py:97
  59.5 4.2 %collective-permute-start.17 = (bf16[144,128]{1,0:T(8,128)(2,1)S(1)}, bf16[144,128]{1,0:T(8,128)(2,1)S(1)}, u32[]{:S(2)}, u32[]{:S(2)}) collective-permute-start(bf16[144,128]{1,0:T(8,128)(2,1)S(1)} %get-tuple-element.85.refs_3_), channel_id=1, source_target_pairs={{0,2},{1,3},{2,0},{3,1},{4,6},{5,7},{6,4},{7,5},{8,10},{9,11},{10,... | collective-permute-start | bytes 110600 | tf_op jit(solution)/shard_map/ppermute | solution.py:97
  60.6 3.1 %collective-permute-start.16 = (bf16[144,128]{1,0:T(8,128)(2,1)S(1)}, bf16[144,128]{1,0:T(8,128)(2,1)S(1)}, u32[]{:S(2)}, u32[]{:S(2)}) collective-permute-start(bf16[144,128]{1,0:T(8,128)(2,1)S(1)} %get-tuple-element.85.refs_3_), channel_id=1, source_target_pairs={{0,1},{1,0},{2,3},{3,2},{4,5},{5,4},{6,7},{7,6},{8,9},{9,8},{10,11... | collective-permute-start | bytes 110600 | tf_op jit(solution)/shard_map/ppermute | solution.py:97
  65.2 4.5 %collective-permute-start.19 = (bf16[144,128]{1,0:T(8,128)(2,1)S(1)}, bf16[144,128]{1,0:T(8,128)(2,1)S(1)}, u32[]{:S(2)}, u32[]{:S(2)}) collective-permute-start(bf16[144,128]{1,0:T(8,128)(2,1)S(1)} %get-tuple-element.91), channel_id=1, source_target_pairs={{0,4},{4,0},{8,12},{12,8},{1,5},{5,1},{9,13},{13,9},{2,6},{6,2},{1... | collective-permute-start | bytes 110600 | tf_op jit(solution)/shard_map/ppermute | solution.py:97
  65.5 5.6 %collective-permute-start.20 = (bf16[144,128]{1,0:T(8,128)(2,1)S(1)}, bf16[144,128]{1,0:T(8,128)(2,1)S(1)}, u32[]{:S(2)}, u32[]{:S(2)}) collective-permute-start(bf16[144,128]{1,0:T(8,128)(2,1)S(1)} %get-tuple-element.92), channel_id=1, source_target_pairs={{0,8},{4,12},{8,0},{12,4},{1,9},{5,13},{9,1},{13,5},{2,10},{6,14},... | collective-permute-start | bytes 110600 | tf_op jit(solution)/shard_map/ppermute | solution.py:97
  68.4 5.8 %collective-permute-start.21 = (bf16[144,128]{1,0:T(8,128)(2,1)S(1)}, bf16[144,128]{1,0:T(8,128)(2,1)S(1)}, u32[]{:S(2)}, u32[]{:S(2)}) collective-permute-start(bf16[144,128]{1,0:T(8,128)(2,1)S(1)} %get-tuple-element.93), channel_id=1, source_target_pairs={{0,12},{4,8},{8,4},{12,0},{1,13},{5,9},{9,5},{13,1},{2,14},{6,10},... | collective-permute-start | bytes 110600 | tf_op jit(solution)/shard_map/ppermute | solution.py:97
  74.2 3.5 %collective-permute-start.24 = (bf16[144,128]{1,0:T(8,128)(2,1)S(1)}, bf16[144,128]{1,0:T(8,128)(2,1)S(1)}, u32[]{:S(2)}, u32[]{:S(2)}) collective-permute-start(bf16[144,128]{1,0:T(8,128)(2,1)S(1)} %get-tuple-element.95.refs_3_), channel_id=1, source_target_pairs={{0,3},{1,2},{2,1},{3,0},{4,7},{5,6},{6,5},{7,4},{8,11},{9,10},{10,... | collective-permute-start | bytes 110600 | tf_op jit(solution)/shard_map/ppermute | solution.py:97
  74.3 4.3 %collective-permute-start.23 = (bf16[144,128]{1,0:T(8,128)(2,1)S(1)}, bf16[144,128]{1,0:T(8,128)(2,1)S(1)}, u32[]{:S(2)}, u32[]{:S(2)}) collective-permute-start(bf16[144,128]{1,0:T(8,128)(2,1)S(1)} %get-tuple-element.95.refs_3_), channel_id=1, source_target_pairs={{0,2},{1,3},{2,0},{3,1},{4,6},{5,7},{6,4},{7,5},{8,10},{9,11},{10,... | collective-permute-start | bytes 110600 | tf_op jit(solution)/shard_map/ppermute | solution.py:97
  75.4 3.2 %collective-permute-start.22 = (bf16[144,128]{1,0:T(8,128)(2,1)S(1)}, bf16[144,128]{1,0:T(8,128)(2,1)S(1)}, u32[]{:S(2)}, u32[]{:S(2)}) collective-permute-start(bf16[144,128]{1,0:T(8,128)(2,1)S(1)} %get-tuple-element.95.refs_3_), channel_id=1, source_target_pairs={{0,1},{1,0},{2,3},{3,2},{4,5},{5,4},{6,7},{7,6},{8,9},{9,8},{10,11... | collective-permute-start | bytes 110600 | tf_op jit(solution)/shard_map/ppermute | solution.py:97
  80.2 4.5 %collective-permute-start.25 = (bf16[144,128]{1,0:T(8,128)(2,1)S(1)}, bf16[144,128]{1,0:T(8,128)(2,1)S(1)}, u32[]{:S(2)}, u32[]{:S(2)}) collective-permute-start(bf16[144,128]{1,0:T(8,128)(2,1)S(1)} %get-tuple-element.102), channel_id=1, source_target_pairs={{0,4},{4,0},{8,12},{12,8},{1,5},{5,1},{9,13},{13,9},{2,6},{6,2},{1... | collective-permute-start | bytes 110600 | tf_op jit(solution)/shard_map/ppermute | solution.py:97
  80.3 5.3 %collective-permute-start.26 = (bf16[144,128]{1,0:T(8,128)(2,1)S(1)}, bf16[144,128]{1,0:T(8,128)(2,1)S(1)}, u32[]{:S(2)}, u32[]{:S(2)}) collective-permute-start(bf16[144,128]{1,0:T(8,128)(2,1)S(1)} %get-tuple-element.103), channel_id=1, source_target_pairs={{0,8},{4,12},{8,0},{12,4},{1,9},{5,13},{9,1},{13,5},{2,10},{6,14},... | collective-permute-start | bytes 110600 | tf_op jit(solution)/shard_map/ppermute | solution.py:97
  81.9 5.8 %collective-permute-start.27 = (bf16[144,128]{1,0:T(8,128)(2,1)S(1)}, bf16[144,128]{1,0:T(8,128)(2,1)S(1)}, u32[]{:S(2)}, u32[]{:S(2)}) collective-permute-start(bf16[144,128]{1,0:T(8,128)(2,1)S(1)} %get-tuple-element.104), channel_id=1, source_target_pairs={{0,12},{4,8},{8,4},{12,0},{1,13},{5,9},{9,5},{13,1},{2,14},{6,10},... | collective-permute-start | bytes 110600 | tf_op jit(solution)/shard_map/ppermute | solution.py:97
  87.8 4.0 %collective-permute-start.30 = (bf16[176,128]{1,0:T(8,128)(2,1)S(1)}, bf16[176,128]{1,0:T(8,128)(2,1)S(1)}, u32[]{:S(2)}, u32[]{:S(2)}) collective-permute-start(bf16[176,128]{1,0:T(8,128)(2,1)S(1)} %shard_map.134.refs_6_.refs_0_), channel_id=1, source_target_pairs={{0,3},{1,2},{2,1},{3,0},{4,7},{5,6},{6,5},{7,4},{8,11},{9,10},{10,... | collective-permute-start | bytes 135176 | tf_op jit(solution)/shard_map/ppermute | solution.py:97
  87.9 4.7 %collective-permute-start.29 = (bf16[176,128]{1,0:T(8,128)(2,1)S(1)}, bf16[176,128]{1,0:T(8,128)(2,1)S(1)}, u32[]{:S(2)}, u32[]{:S(2)}) collective-permute-start(bf16[176,128]{1,0:T(8,128)(2,1)S(1)} %shard_map.134.refs_6_.refs_0_), channel_id=1, source_target_pairs={{0,2},{1,3},{2,0},{3,1},{4,6},{5,7},{6,4},{7,5},{8,10},{9,11},{10,... | collective-permute-start | bytes 135176 | tf_op jit(solution)/shard_map/ppermute | solution.py:97
  89.4 3.2 %collective-permute-start.28 = (bf16[176,128]{1,0:T(8,128)(2,1)S(1)}, bf16[176,128]{1,0:T(8,128)(2,1)S(1)}, u32[]{:S(2)}, u32[]{:S(2)}) collective-permute-start(bf16[176,128]{1,0:T(8,128)(2,1)S(1)} %shard_map.134.refs_6_.refs_0_), channel_id=1, source_target_pairs={{0,1},{1,0},{2,3},{3,2},{4,5},{5,4},{6,7},{7,6},{8,9},{9,8},{10,11... | collective-permute-start | bytes 135176 | tf_op jit(solution)/shard_map/ppermute | solution.py:97
  93.1 4.0 %collective-permute-start.31 = (f32[64,128]{1,0:T(8,128)S(1)}, f32[64,128]{1,0:T(8,128)S(1)}, u32[]{:S(2)}, u32[]{:S(2)}) collective-permute-start(f32[64,128]{1,0:T(8,128)S(1)} %shard_map.136), channel_id=1, source_target_pairs={{0,4},{4,0},{8,12},{12,8},{1,5},{5,1},{9,13},{13,9},{2,6},{6,2},{1... | collective-permute-start | bytes 98312 | tf_op jit(solution)/shard_map/ppermute | solution.py:97

commit v4 on v3

--- a/solution.py
+++ b/solution.py
@@ -13,7 +13,6 @@
 BF16 = jnp.bfloat16
 VMEM = pl.BlockSpec(memory_space=pltpu.VMEM)
 SMEM = pl.BlockSpec(memory_space=pltpu.SMEM)
-HBM = pl.BlockSpec(memory_space=pltpu.HBM)
 
 
 class Sizes:
@@ -74,7 +73,7 @@
         return self.pack(pltpu.roll(whole, back, 1))
 
 
-def call(body, outs, scratch, ins, places=None, flops=0, out_specs=None):
+def call(body, outs, scratch, ins, places=None, flops=0, out_specs=None, aliases=None):
     specs = [(places or {}).get(i, VMEM) for i in range(len(ins))]
     moved = sum(x.size * x.dtype.itemsize for x in ins) + sum(x.size * x.dtype.itemsize for x in outs)
     return pl.pallas_call(
@@ -85,6 +84,7 @@
         scratch_shapes=scratch,
         cost_estimate=pl.CostEstimate(flops=flops, bytes_accessed=moved, transcendentals=0),
         compiler_params=pltpu.CompilerParams(vmem_limit_bytes=24 * 1024 * 1024),
+        input_output_aliases=aliases or {},
     )(*ins)
 
 
@@ -101,8 +101,15 @@
     return count <= 4
 
 
+def paired(axis):
+    return axis == "col" and lax.axis_size(axis) == 4
+
+
 def share(x, axis):
     count = lax.axis_size(axis)
+    if paired(axis):
+        far = flip(x, axis, 2)
+        return [flip(x, axis, 1), far, flip(far, axis, 1)]
     if few(count):
         return [flip(x, axis, k) for k in reversed(range(1, count))][::-1]
     return [lax.all_gather(x, axis)]
@@ -115,8 +122,8 @@
     return [lax.all_to_all(parts[0], axis, 0, 0, tiled=True)]
 
 
-def parcel(count, dims, kind, whole=False):
-    if few(count) and not whole:
+def parcel(count, dims, kind):
+    if few(count):
         return [shape(dims, kind)] * (count - 1)
     return [shape((count, *dims), kind)]
 
@@ -133,46 +140,25 @@
     lax.fori_loop(0, count, lambda i, c: (body(i), c)[1], 0, unroll=count <= 18)
 
 
-def fetch(pairs, sems):
-    copies = [pltpu.make_async_copy(a, b, sems.at[i]) for i, (a, b) in enumerate(pairs)]
-    for copy in copies:
-        copy.start()
-    return copies
-
-
-def start_kernel(z, rates_in, types_in, inputs_in, message, own, rates, types, inputs, pad, codes, sems):
-    copies = fetch([(rates_in, rates), (types_in, types), (inputs_in, inputs)], sems)
+def start_kernel(z, rates, numbers, message, own, pad):
     pad[...] = jnp.zeros_like(pad)
-    codes[...] = jnp.zeros_like(codes)
-    for copy in copies:
-        copy.wait()
     pad[:, 0 : z.local] = rates[...]
-    t = types[...].reshape(1, z.local)
-    m = inputs[...].reshape(1, z.local)
-    rows = [
-        lax.shift_right_logical(t, 7) + 1,
-        t & 127,
-        lax.shift_right_logical(m, 7) + 1,
-        m & 127,
-    ]
-    for r, row in enumerate(rows):
-        codes[r : r + 1, 0 : z.local] = row.astype(F32)
-    code = codes[...]
-    blocks = [code[0:4, f * BLOCK : (f + 1) * BLOCK] for f in range(z.frame)]
+    packed = z.pack(pad[...])
+    own[...] = packed
+    number = numbers[...]
+    high = (lax.shift_right_arithmetic(number, 7) + 1).astype(F32)
+    low = (number & 127).astype(F32)
+    blocks = []
+    for f in range(z.frame):
+        for r in (f, z.frame + f):
+            blocks += [high[r : r + 1], low[r : r + 1]]
     fill = message.shape[0] - z.piece - 4 * z.frame
     extra = jnp.concatenate(blocks + [jnp.zeros((fill, BLOCK), F32)], axis=0)
-    packed = z.pack(pad[...])
-    own[...] = packed
     message[...] = jnp.concatenate([packed, extra], axis=0).astype(BF16)
 
 
-def load_kernel(z, after, owner_in, post_in, pre_in, weights, out, ids, owner, post, pre, sems):
-    del after
-    copies = fetch(
-        [(owner_in, owner), (post_in, post), (pre_in, pre), (weights.at[0, 0], out)], sems
-    )
-    for copy in copies[:3]:
-        copy.wait()
+def load_kernel(z, after, owner, post, pre, weights, ids):
+    del after, weights
 
     def one(s, carry):
         ids[s] = owner[0, 0, s] * z.post + post[0, 0, s]
@@ -180,7 +166,6 @@
         return carry
 
     lax.fori_loop(0, z.slots, one, 0, unroll=8)
-    copies[3].wait()
 
 
 def prepare_kernel(z, count, *refs):
@@ -233,7 +218,13 @@
         both = jnp.concatenate(
             [z.take_blocks(total, 0, c ^ k), z.take_blocks(total, z.post, c ^ k)], axis=0
         )
-        if k == 0:
+        if z.cols == 4:
+            rows = slice(k // 2 * z.pair, (k // 2 + 1) * z.pair)
+            if k % 2 == 0:
+                own[rows] = both
+            else:
+                parts[0][rows] = both.astype(BF16)
+        elif k == 0:
             own[...] = both
         else:
             away(parts, z.cols, c, k)[...] = both.astype(BF16)
@@ -280,13 +271,22 @@
     multiply_forward(z, c, ids, weights, x, total, own, parts)
 
 
+def half_kernel(z, own, got, kept, message):
+    total = own[...] + got[...].astype(F32)
+    kept[...] = total[0 : z.pair]
+    message[...] = total[z.pair :].astype(BF16)
+
+
 def sum_kernel(z, count, with_cot, *refs):
     own, got = refs[0], refs[1 : 1 + count]
     kept, message = refs[-2:]
     _, c = place()
     total = own[...]
-    for k in range(1, z.cols):
-        total = total + away(got, z.cols, c, k)[...].astype(F32)
+    if z.cols == 4:
+        total = total + got[0][...].astype(F32)
+    else:
+        for k in range(1, z.cols):
+            total = total + away(got, z.cols, c, k)[...].astype(F32)
     kept[...] = total
     if with_cot:
         cot = refs[1 + count]
@@ -479,28 +479,23 @@
     opening = (z.piece + 4 * z.frame + 15) // 16 * 16
     closing = (z.pair + z.piece + 15) // 16 * 16
 
+    fill = jnp.full((z.wide - local,), -BLOCK, jnp.int32)
+    numbers = jnp.concatenate([cell_type, fill, input_map, fill])
     message, own_rates = call(
         functools.partial(start_kernel, z),
         [shape((opening, BLOCK), BF16), shape((z.piece, BLOCK))],
-        [
-            pltpu.VMEM((batch, local), F32),
-            pltpu.VMEM((local,), jnp.int32),
-            pltpu.VMEM((local,), jnp.int32),
-            pltpu.VMEM((batch, z.wide), F32),
-            pltpu.VMEM((8, z.wide), F32),
-            pltpu.SemaphoreType.DMA((3,)),
-        ],
-        [initial_rates, cell_type, input_map],
-        {0: HBM, 1: HBM, 2: HBM},
+        [pltpu.VMEM((batch, z.wide), F32)],
+        [initial_rates, numbers.reshape(2 * z.frame, BLOCK)],
     )
     got = share(message, "row")
-    weights, ids = call(
+    weights = weight_blocks.reshape(slots, BLOCK, BLOCK)
+    (ids,) = call(
         functools.partial(load_kernel, z),
-        [shape((slots, BLOCK, BLOCK), BF16), shape((2 * slots,), jnp.int32)],
-        [pltpu.SMEM((1, 1, slots), jnp.int32)] * 3 + [pltpu.SemaphoreType.DMA((4,))],
-        [message, slot_owner, slot_post, slot_pre, weight_blocks],
-        {1: HBM, 2: HBM, 3: HBM, 4: HBM},
-        out_specs=[VMEM, SMEM],
+        [shape((2 * slots,), jnp.int32)],
+        [],
+        [message, slot_owner, slot_post, slot_pre, weights],
+        {1: SMEM, 2: SMEM, 3: SMEM},
+        out_specs=[SMEM],
     )
     if few(z.rows):
         partner_message = got[z.half - 1]
@@ -510,9 +505,14 @@
     post_sums = pltpu.VMEM((2 * z.post, batch, BLOCK), F32)
     x_shape = shape((z.pre, batch, BLOCK), BF16)
     row_parts = parcel(z.rows, pair, BF16)
+    two = paired("col")
+    if two:
+        col_parts = [shape((2 * z.pair, BLOCK)), shape((2 * z.pair, BLOCK), BF16)]
+    else:
+        col_parts = [shape(pair), *parcel(z.cols, pair, BF16)]
     x, own, *parts = call(
         functools.partial(first_kernel, z, len(got)),
-        [x_shape, shape(pair), *parcel(z.cols, pair, BF16, True)],
+        [x_shape, *col_parts],
         [pre_sums, post_sums],
         [ids, weights, message, *got],
         {0: SMEM},
@@ -535,7 +535,14 @@
     xs, acts, curs = [x], [], []
     for t in range(steps):
         last = t == steps - 1
-        got = exchange(parts, "col")
+        if two:
+            near = flip(parts[0], "col", 1)
+            own, far = call(
+                functools.partial(half_kernel, z), [shape(pair), shape(pair, BF16)], [], [own, near]
+            )
+            got = [flip(far, "col", 2)]
+        else:
+            got = exchange(parts, "col")
         kept, sent = call(
             functools.partial(sum_kernel, z, len(got), last),
             [shape(pair), shape((closing, BLOCK) if last else pair, BF16)],
@@ -547,8 +554,7 @@
         got = share(sent, "row")
         rates, act, cur, x, own, *parts = call(
             functools.partial(forward_kernel, z, t, len(got)),
-            [shape(every), shape(pair), shape(pair), x_shape, shape(pair)]
-            + parcel(z.cols, pair, BF16),
+            [shape(every), shape(pair), shape(pair), x_shape, *col_parts],
             [pre_sums, post_sums],
             [ids, weights, kept, rates, gain, drive, *got],
             {0: SMEM},

time: 98 us -> 100 us (1.020)
  waiting for transfers between devices: 31.2 us -> 43.1 us
  blocking collectives: 7.52 us -> 0 us
  local copies, waits for them, and re-layouts: 5.72 us -> 4.37 us
  starting transfers between devices: 34.7 us -> 33.4 us
    ppermute x32, waiting for transfers between devices: 31.2 us -> 43.1 us  [flip(): return lax.ppermute(x, axis, [(i, i ^ k) for i in range(count)])]
    all_to_all x1 -> x0, blocking collectives: 7.52 us -> none  [exchange(): return [lax.all_to_all(parts[0], axis, 0, 0, tiled=True)]]
    unnamed x20 -> x18, local copies, waits for them, and re-layouts: 5.72 us -> 4.37 us
    ppermute x32, starting transfers between devices: 34.7 us -> 33.4 us  [flip(): return lax.ppermute(x, axis, [(i, i ^ k) for i in range(count)])]
    pallas_call x15 -> x18, Pallas kernels: 13.6 us -> 13.5 us  [call(): pl.pallas_call(body, out_shape=outs, in_specs=specs, out_specs=out_specs...]
  transfers between devices with their start and end apart: 32 -> 32, of which waited for: 19 -> 23; matrix products, arithmetic and copies ran while one was open for 0% -> 0% of each run, Pallas kernels for 6% -> 6%
where the time goes in v4:
time: 100 us
  waiting for transfers between devices  43.1 us (43%)
  starting transfers between devices  33.4 us (33%)
  Pallas kernels  17.1 us (17%)
  local copies, waits for them, and re-layouts  4.37 us (4%)
  other arithmetic  1.4 us (1%)
    ppermute x32, waiting for transfers between devices, flip(): return lax.ppermute(x, axis, [(i, i ^ k) for i in range(count)])  43.1 us
    ppermute x32, starting transfers between devices, flip(): return lax.ppermute(x, axis, [(i, i ^ k) for i in range(count)])  33.4 us
    pallas_call x18, Pallas kernels, call(): pl.pallas_call(body, out_shape=outs, in_specs=specs, out_specs=out_specs...  13.5 us
    unnamed x18, local copies, waits for them, and re-layouts  4.37 us
    pallas_call x1, Pallas kernels, shards(): pl.pallas_call(functools.partial(grad_kernel, z, len(got), per_step), gri...  3.56 us
  transfers between devices with their start and end apart: 32, of which 23 were waited for; matrix products, arithmetic and copies ran while one was open for 0% of the time, Pallas kernels for 6%

profile of v4, /device:TPU:0, one launch (start us, length us, event | category | flops | bytes accessed | tf_op | source)
XLA Modules:
  0.0 100.0 jit_solution(3662673178358591853)
XLA Ops:
  0.6 0.8 add_bitcast_fusion.1.numbers
  1.4 0.8 copy-done.4
  2.2 0.1 shard_map.121
  2.3 3.0 %collective-permute-start = (bf16[96,128]{1,0:T(8,128)(2,1)S(1)}, bf16[96,128]{1,0:T(8,128)(2,1)S(1)}, u32[]{:S(2)}, u32[]{:S(2)}) collective-permute-start(bf16[96,128]{1,0:T(8,128)(2,1)S(1)} %get-tuple-element.54.after.refs_2_.refs_0_.mine), channel_id=1, source_target_pairs={{0,4},{4,0},{8,12},{12,8},{1,5},{5,1},{9,13},{13,9},{2,6},{6,2},{1... | collective-permute-start | bytes 73736 | tf_op jit(solution)/shard_map/ppermute | solution.py:97
  5.3 2.6 %collective-permute-start.1 = (bf16[96,128]{1,0:T(8,128)(2,1)S(1)}, bf16[96,128]{1,0:T(8,128)(2,1)S(1)}, u32[]{:S(2)}, u32[]{:S(2)}) collective-permute-start(bf16[96,128]{1,0:T(8,128)(2,1)S(1)} %get-tuple-element.54.after.refs_2_.refs_0_.mine), channel_id=1, source_target_pairs={{0,8},{4,12},{8,0},{12,4},{1,9},{5,13},{9,1},{13,5},{2,10},{6,14},... | collective-permute-start | bytes 73736 | tf_op jit(solution)/shard_map/ppermute | solution.py:97
  7.9 1.6 %copy-done = bf16[1,1,64,128,128]{4,3,2,1,0:T(8,128)(2,1)S(1)} copy-done((bf16[1,1,64,128,128]{4,3,2,1,0:T(8,128)(2,1)S(1)}, bf16[1,1,64,128,128]{4,3,2,1,0:T(8,128)(2,1)}, u32[]{:S(2)}) %copy-start) | copy-done | bytes 2097176
  9.5 0.7 copy-done.6
  10.2 0.7 copy-done.7
  10.8 0.7 copy-done.8
  11.5 1.3 %shard_map.122.refs_0_ = s32[128]{0:T(128)S(1)} custom-call(bf16[96,128]{1,0:T(8,128)(2,1)S(1)} %get-tuple-element.54.after.refs_2_.refs_0_.mine, s32[1,1,64]{2,1,0:T(1,128)S(1)} %copy-done.6, s32[1,1,64]{2,1,0:T(1,128)S(1)} %copy-done.7, s32[1,1,64]{2,1,0:T(1,128)S(1)} %copy-done.8, bf16[64,128,128]{2,1,0:T(8,128)(2,1)S(1)} %bitcast.8), custom_call_target="tpu_custom_call" | custom-call | bytes 2123008 | tf_op jit(solution)/shard_map/pallas_call | solution.py:79
  12.8 0.7 collective-permute-done.2.refs_5_.refs_7_
  13.5 2.1 %shard_map.123 = (bf16[9,32,128]{2,1,0:T(8,128)(2,1)S(1)}, f32[288,128]{1,0:T(8,128)S(1)}, bf16[288,128]{1,0:T(8,128)(2,1)S(1)}) custom-call(s32[128]{0:T(128)S(1)} %shard_map.122.refs_0_, bf16[64,128,128]{2,1,0:T(8,128)(2,1)S(1)} %bitcast.9, bf16[96,128]{1,0:T(8,128)(2,1)S(1)} %get-tuple-element.54.after.refs_2_.refs_0_.mine, ...), custom_call_target="tpu_custom_call" | custom-call | flops 67108864 | bytes 2490880 | tf_op jit(solution)/shard_map/pallas_call | solution.py:79
  15.7 1.3 %collective-permute-done.3.got = bf16[288,128]{1,0:T(8,128)(2,1)S(1)} collective-permute-done((bf16[288,128]{1,0:T(8,128)(2,1)S(1)}, bf16[288,128]{1,0:T(8,128)(2,1)S(1)}, u32[]{:S(2)}, u32[]{:S(2)}) %collective-permute-start.3) | collective-permute-done | bytes 73760 | tf_op jit(solution)/shard_map/ppermute | solution.py:97
  17.0 1.6 %collective-permute-start.4 = (bf16[144,128]{1,0:T(8,128)(2,1)S(1)}, bf16[144,128]{1,0:T(8,128)(2,1)S(1)}, u32[]{:S(2)}, u32[]{:S(2)}) collective-permute-start(bf16[144,128]{1,0:T(8,128)(2,1)S(1)} %get-tuple-element.58), channel_id=1, source_target_pairs={{0,2},{1,3},{2,0},{3,1},{4,6},{5,7},{6,4},{7,5},{8,10},{9,11},{10,... | collective-permute-start | bytes 110600 | tf_op jit(solution)/shard_map/ppermute | solution.py:97
  18.6 2.5 %collective-permute-done.4.refs_1_ = bf16[144,128]{1,0:T(8,128)(2,1)S(1)} collective-permute-done((bf16[144,128]{1,0:T(8,128)(2,1)S(1)}, bf16[144,128]{1,0:T(8,128)(2,1)S(1)}, u32[]{:S(2)}, u32[]{:S(2)}) %collective-permute-start.4) | collective-permute-done | bytes 36896 | tf_op jit(solution)/shard_map/ppermute | solution.py:97
  21.0 0.5 collective-permute-start.5
  21.5 3.5 %collective-permute-start.6 = (bf16[144,128]{1,0:T(8,128)(2,1)S(1)}, bf16[144,128]{1,0:T(8,128)(2,1)S(1)}, u32[]{:S(2)}, u32[]{:S(2)}) collective-permute-start(bf16[144,128]{1,0:T(8,128)(2,1)S(1)} %get-tuple-element.64), channel_id=1, source_target_pairs={{0,8},{4,12},{8,0},{12,4},{1,9},{5,13},{9,1},{13,5},{2,10},{6,14},... | collective-permute-start | bytes 110600 | tf_op jit(solution)/shard_map/ppermute | solution.py:97
  25.0 0.5 collective-permute-start.7
  25.5 0.9 shard_map.126
  26.4 0.5 collective-permute-done.6.refs_7_
  27.0 3.8 %collective-permute-done.7.refs_8_ = bf16[144,128]{1,0:T(8,128)(2,1)S(1)} collective-permute-done((bf16[144,128]{1,0:T(8,128)(2,1)S(1)}, bf16[144,128]{1,0:T(8,128)(2,1)S(1)}, u32[]{:S(2)}, u32[]{:S(2)}) %collective-permute-start.7) | collective-permute-done | bytes 36896 | tf_op jit(solution)/shard_map/ppermute | solution.py:97
  30.8 2.1 %shard_map.127 = (f32[288,128]{1,0:T(8,128)S(1)}, f32[144,128]{1,0:T(8,128)S(1)}, f32[144,128]{1,0:T(8,128)S(1)}, bf16[9,32,128]{2,1,0:T(8,128)(2,1)S(1)}, f32[2...) custom-call(s32[128]{0:T(128)S(1)} %shard_map.122.refs_0_, bf16[64,128,128]{2,1,0:T(8,128)(2,1)S(1)} %bitcast.10, ...), custom_call_target="tpu_custom_call" | custom-call | flops 67108864 | bytes 3609088 | tf_op jit(solution)/shard_map/pallas_call | solution.py:79
  32.9 0.1 collective-permute-start.8
  33.0 1.3 %collective-permute-done.8.got = bf16[288,128]{1,0:T(8,128)(2,1)S(1)} collective-permute-done((bf16[288,128]{1,0:T(8,128)(2,1)S(1)}, bf16[288,128]{1,0:T(8,128)(2,1)S(1)}, u32[]{:S(2)}, u32[]{:S(2)}) %collective-permute-start.8) | collective-permute-done | bytes 73760 | tf_op jit(solution)/shard_map/ppermute | solution.py:97
  34.3 1.6 %collective-permute-start.9 = (bf16[144,128]{1,0:T(8,128)(2,1)S(1)}, bf16[144,128]{1,0:T(8,128)(2,1)S(1)}, u32[]{:S(2)}, u32[]{:S(2)}) collective-permute-start(bf16[144,128]{1,0:T(8,128)(2,1)S(1)} %get-tuple-element.68), channel_id=1, source_target_pairs={{0,2},{1,3},{2,0},{3,1},{4,6},{5,7},{6,4},{7,5},{8,10},{9,11},{10,... | collective-permute-start | bytes 110600 | tf_op jit(solution)/shard_map/ppermute | solution.py:97
  35.8 2.5 %collective-permute-done.9.refs_1_ = bf16[144,128]{1,0:T(8,128)(2,1)S(1)} collective-permute-done((bf16[144,128]{1,0:T(8,128)(2,1)S(1)}, bf16[144,128]{1,0:T(8,128)(2,1)S(1)}, u32[]{:S(2)}, u32[]{:S(2)}) %collective-permute-start.9) | collective-permute-done | bytes 36896 | tf_op jit(solution)/shard_map/ppermute | solution.py:97
  38.3 0.1 collective-permute-start.10
  38.4 1.0 %collective-permute-start.11 = (bf16[144,128]{1,0:T(8,128)(2,1)S(1)}, bf16[144,128]{1,0:T(8,128)(2,1)S(1)}, u32[]{:S(2)}, u32[]{:S(2)}) collective-permute-start(bf16[144,128]{1,0:T(8,128)(2,1)S(1)} %get-tuple-element.71), channel_id=1, source_target_pairs={{0,8},{4,12},{8,0},{12,4},{1,9},{5,13},{9,1},{13,5},{2,10},{6,14},... | collective-permute-start | bytes 110600 | tf_op jit(solution)/shard_map/ppermute | solution.py:97
  39.4 3.3 %collective-permute-start.12 = (bf16[144,128]{1,0:T(8,128)(2,1)S(1)}, bf16[144,128]{1,0:T(8,128)(2,1)S(1)}, u32[]{:S(2)}, u32[]{:S(2)}) collective-permute-start(bf16[144,128]{1,0:T(8,128)(2,1)S(1)} %get-tuple-element.71), channel_id=1, source_target_pairs={{0,12},{4,8},{8,4},{12,0},{1,13},{5,9},{9,5},{13,1},{2,14},{6,10},... | collective-permute-start | bytes 110600 | tf_op jit(solution)/shard_map/ppermute | solution.py:97
  42.8 0.5 collective-permute-done.11.refs_7_
  43.3 1.9 %collective-permute-done.12.refs_8_ = bf16[144,128]{1,0:T(8,128)(2,1)S(1)} collective-permute-done((bf16[144,128]{1,0:T(8,128)(2,1)S(1)}, bf16[144,128]{1,0:T(8,128)(2,1)S(1)}, u32[]{:S(2)}, u32[]{:S(2)}) %collective-permute-start.12) | collective-permute-done | bytes 36896 | tf_op jit(solution)/shard_map/ppermute | solution.py:97
  45.2 2.1 %shard_map.130 = (f32[288,128]{1,0:T(8,128)S(1)}, f32[144,128]{1,0:T(8,128)S(1)}, f32[144,128]{1,0:T(8,128)S(1)}, bf16[9,32,128]{2,1,0:T(8,128)(2,1)S(1)}, f32[2...) custom-call(s32[128]{0:T(128)S(1)} %shard_map.122.refs_0_, bf16[64,128,128]{2,1,0:T(8,128)(2,1)S(1)} %bitcast.11, ...), custom_call_target="tpu_custom_call" | custom-call | flops 67108864 | bytes 3609088 | tf_op jit(solution)/shard_map/pallas_call | solution.py:79
  47.4 1.3 %collective-permute-done.13.got = bf16[288,128]{1,0:T(8,128)(2,1)S(1)} collective-permute-done((bf16[288,128]{1,0:T(8,128)(2,1)S(1)}, bf16[288,128]{1,0:T(8,128)(2,1)S(1)}, u32[]{:S(2)}, u32[]{:S(2)}) %collective-permute-start.13) | collective-permute-done | bytes 73760 | tf_op jit(solution)/shard_map/ppermute | solution.py:97
  48.6 1.6 %collective-permute-start.14 = (bf16[144,128]{1,0:T(8,128)(2,1)S(1)}, bf16[144,128]{1,0:T(8,128)(2,1)S(1)}, u32[]{:S(2)}, u32[]{:S(2)}) collective-permute-start(bf16[144,128]{1,0:T(8,128)(2,1)S(1)} %get-tuple-element.75), channel_id=1, source_target_pairs={{0,2},{1,3},{2,0},{3,1},{4,6},{5,7},{6,4},{7,5},{8,10},{9,11},{10,... | collective-permute-start | bytes 110600 | tf_op jit(solution)/shard_map/ppermute | solution.py:97
  50.2 2.5 %collective-permute-done.14.refs_1_ = bf16[144,128]{1,0:T(8,128)(2,1)S(1)} collective-permute-done((bf16[144,128]{1,0:T(8,128)(2,1)S(1)}, bf16[144,128]{1,0:T(8,128)(2,1)S(1)}, u32[]{:S(2)}, u32[]{:S(2)}) %collective-permute-start.14) | collective-permute-done | bytes 36896 | tf_op jit(solution)/shard_map/ppermute | solution.py:97
  52.7 0.4 collective-permute-start.15
  53.1 5.4 %collective-permute-done.15.theirs = bf16[224,128]{1,0:T(8,128)(2,1)S(1)} collective-permute-done((bf16[224,128]{1,0:T(8,128)(2,1)S(1)}, bf16[224,128]{1,0:T(8,128)(2,1)S(1)}, u32[]{:S(2)}, u32[]{:S(2)}) %collective-permute-start.15) | collective-permute-done | bytes 57376 | tf_op jit(solution)/shard_map/ppermute | solution.py:97
  58.4 0.7 shard_map.133
  59.1 1.5 %collective-permute-start.17 = (bf16[144,128]{1,0:T(8,128)(2,1)S(1)}, bf16[144,128]{1,0:T(8,128)(2,1)S(1)}, u32[]{:S(2)}, u32[]{:S(2)}) collective-permute-start(bf16[144,128]{1,0:T(8,128)(2,1)S(1)} %get-tuple-element.85.refs_3_), channel_id=1, source_target_pairs={{0,2},{1,3},{2,0},{3,1},{4,6},{5,7},{6,4},{7,5},{8,10},{9,11},{10,... | collective-permute-start | bytes 110600 | tf_op jit(solution)/shard_map/ppermute | solution.py:97
  60.7 2.5 %collective-permute-done.17.refs_5_ = bf16[144,128]{1,0:T(8,128)(2,1)S(1)} collective-permute-done((bf16[144,128]{1,0:T(8,128)(2,1)S(1)}, bf16[144,128]{1,0:T(8,128)(2,1)S(1)}, u32[]{:S(2)}, u32[]{:S(2)}) %collective-permute-start.17) | collective-permute-done | bytes 36896 | tf_op jit(solution)/shard_map/ppermute | solution.py:97
  63.1 1.2 %collective-permute-done.18.refs_6_ = bf16[144,128]{1,0:T(8,128)(2,1)S(1)} collective-permute-done((bf16[144,128]{1,0:T(8,128)(2,1)S(1)}, bf16[144,128]{1,0:T(8,128)(2,1)S(1)}, u32[]{:S(2)}, u32[]{:S(2)}) %collective-permute-start.18) | collective-permute-done | bytes 36896 | tf_op jit(solution)/shard_map/ppermute | solution.py:97
  64.3 1.6 %shard_map.134 = (bf16[18,32,128]{2,1,0:T(8,128)(2,1)S(1)}, f32[144,128]{1,0:T(8,128)S(1)}, bf16[144,128]{1,0:T(8,128)(2,1)S(1)}, bf16[144,128]{1,0:T(8,128)(2,1)S(1)}, bf16[144,128]{1,0:T(8,128)(2,1)S(1)}) custom-call(s32[128]{0:T(128)S(1)} %shard_map.122.refs_0_, bf16[64,128,128]{2,1,0:T(8,128)(2,1)S(1)} %bitcast.12, ...), custom_call_target="tpu_custom_call" | custom-call | flops 67108864 | bytes 2613760 | tf_op jit(solution)/shard_map/pallas_call | solution.py:79
  65.9 0.5 collective-permute-start.19
  66.5 2.8 %collective-permute-start.20 = (bf16[144,128]{1,0:T(8,128)(2,1)S(1)}, bf16[144,128]{1,0:T(8,128)(2,1)S(1)}, u32[]{:S(2)}, u32[]{:S(2)}) collective-permute-start(bf16[144,128]{1,0:T(8,128)(2,1)S(1)} %get-tuple-element.92), channel_id=1, source_target_pairs={{0,8},{4,12},{8,0},{12,4},{1,9},{5,13},{9,1},{13,5},{2,10},{6,14},... | collective-permute-start | bytes 110600 | tf_op jit(solution)/shard_map/ppermute | solution.py:97
  69.3 1.1 %collective-permute-start.21 = (bf16[144,128]{1,0:T(8,128)(2,1)S(1)}, bf16[144,128]{1,0:T(8,128)(2,1)S(1)}, u32[]{:S(2)}, u32[]{:S(2)}) collective-permute-start(bf16[144,128]{1,0:T(8,128)(2,1)S(1)} %get-tuple-element.93), channel_id=1, source_target_pairs={{0,12},{4,8},{8,4},{12,0},{1,13},{5,9},{9,5},{13,1},{2,14},{6,10},... | collective-permute-start | bytes 110600 | tf_op jit(solution)/shard_map/ppermute | solution.py:97
  70.4 1.6 %collective-permute-done.20.refs_1_ = bf16[144,128]{1,0:T(8,128)(2,1)S(1)} collective-permute-done((bf16[144,128]{1,0:T(8,128)(2,1)S(1)}, bf16[144,128]{1,0:T(8,128)(2,1)S(1)}, u32[]{:S(2)}, u32[]{:S(2)}) %collective-permute-start.20) | collective-permute-done | bytes 36896 | tf_op jit(solution)/shard_map/ppermute | solution.py:97
  72.0 3.0 %collective-permute-done.21.refs_2_ = bf16[144,128]{1,0:T(8,128)(2,1)S(1)} collective-permute-done((bf16[144,128]{1,0:T(8,128)(2,1)S(1)}, bf16[144,128]{1,0:T(8,128)(2,1)S(1)}, u32[]{:S(2)}, u32[]{:S(2)}) %collective-permute-start.21) | collective-permute-done | bytes 36896 | tf_op jit(solution)/shard_map/ppermute | solution.py:97
  75.1 1.6 %collective-permute-start.23 = (bf16[144,128]{1,0:T(8,128)(2,1)S(1)}, bf16[144,128]{1,0:T(8,128)(2,1)S(1)}, u32[]{:S(2)}, u32[]{:S(2)}) collective-permute-start(bf16[144,128]{1,0:T(8,128)(2,1)S(1)} %get-tuple-element.95.refs_3_), channel_id=1, source_target_pairs={{0,2},{1,3},{2,0},{3,1},{4,6},{5,7},{6,4},{7,5},{8,10},{9,11},{10,... | collective-permute-start | bytes 110600 | tf_op jit(solution)/shard_map/ppermute | solution.py:97
  76.7 2.5 %collective-permute-done.23.refs_5_ = bf16[144,128]{1,0:T(8,128)(2,1)S(1)} collective-permute-done((bf16[144,128]{1,0:T(8,128)(2,1)S(1)}, bf16[144,128]{1,0:T(8,128)(2,1)S(1)}, u32[]{:S(2)}, u32[]{:S(2)}) %collective-permute-start.23) | collective-permute-done | bytes 36896 | tf_op jit(solution)/shard_map/ppermute | solution.py:97
  79.1 1.2 %collective-permute-done.24.refs_6_ = bf16[144,128]{1,0:T(8,128)(2,1)S(1)} collective-permute-done((bf16[144,128]{1,0:T(8,128)(2,1)S(1)}, bf16[144,128]{1,0:T(8,128)(2,1)S(1)}, u32[]{:S(2)}, u32[]{:S(2)}) %collective-permute-start.24) | collective-permute-done | bytes 36896 | tf_op jit(solution)/shard_map/ppermute | solution.py:97
  80.3 1.6 %shard_map.136 = (bf16[18,32,128]{2,1,0:T(8,128)(2,1)S(1)}, f32[144,128]{1,0:T(8,128)S(1)}, bf16[144,128]{1,0:T(8,128)(2,1)S(1)}, bf16[144,128]{1,0:T(8,128)(2,1)S(1)}, bf16[144,128]{1,0:T(8,128)(2,1)S(1)}) custom-call(s32[128]{0:T(128)S(1)} %shard_map.122.refs_0_, bf16[64,128,128]{2,1,0:T(8,128)(2,1)S(1)} %bitcast.13, ...), custom_call_target="tpu_custom_call" | custom-call | flops 67108864 | bytes 2613760 | tf_op jit(solution)/shard_map/pallas_call | solution.py:79
  81.9 0.1 collective-permute-start.25
  82.0 1.6 %collective-permute-start.26 = (bf16[144,128]{1,0:T(8,128)(2,1)S(1)}, bf16[144,128]{1,0:T(8,128)(2,1)S(1)}, u32[]{:S(2)}, u32[]{:S(2)}) collective-permute-start(bf16[144,128]{1,0:T(8,128)(2,1)S(1)} %get-tuple-element.103), channel_id=1, source_target_pairs={{0,8},{4,12},{8,0},{12,4},{1,9},{5,13},{9,1},{13,5},{2,10},{6,14},... | collective-permute-start | bytes 110600 | tf_op jit(solution)/shard_map/ppermute | solution.py:97
  83.7 2.7 %collective-permute-start.27 = (bf16[144,128]{1,0:T(8,128)(2,1)S(1)}, bf16[144,128]{1,0:T(8,128)(2,1)S(1)}, u32[]{:S(2)}, u32[]{:S(2)}) collective-permute-start(bf16[144,128]{1,0:T(8,128)(2,1)S(1)} %get-tuple-element.104), channel_id=1, source_target_pairs={{0,12},{4,8},{8,4},{12,0},{1,13},{5,9},{9,5},{13,1},{2,14},{6,10},... | collective-permute-start | bytes 110600 | tf_op jit(solution)/shard_map/ppermute | solution.py:97
  86.4 0.6 collective-permute-done.26.refs_1_
  87.0 2.5 %collective-permute-done.27.refs_2_ = bf16[144,128]{1,0:T(8,128)(2,1)S(1)} collective-permute-done((bf16[144,128]{1,0:T(8,128)(2,1)S(1)}, bf16[144,128]{1,0:T(8,128)(2,1)S(1)}, u32[]{:S(2)}, u32[]{:S(2)}) %collective-permute-start.27) | collective-permute-done | bytes 36896 | tf_op jit(solution)/shard_map/ppermute | solution.py:97
  89.4 0.1 shard_map.137.refs_6_.refs_0_
  89.5 1.6 %collective-permute-start.29 = (bf16[176,128]{1,0:T(8,128)(2,1)S(1)}, bf16[176,128]{1,0:T(8,128)(2,1)S(1)}, u32[]{:S(2)}, u32[]{:S(2)}) collective-permute-start(bf16[176,128]{1,0:T(8,128)(2,1)S(1)} %shard_map.137.refs_6_.refs_0_), channel_id=1, source_target_pairs={{0,2},{1,3},{2,0},{3,1},{4,6},{5,7},{6,4},{7,5},{8,10},{9,11},{10,... | collective-permute-start | bytes 135176 | tf_op jit(solution)/shard_map/ppermute | solution.py:97
  91.1 2.5 %collective-permute-done.29.refs_8_.refs_2_ = bf16[176,128]{1,0:T(8,128)(2,1)S(1)} collective-permute-done((bf16[176,128]{1,0:T(8,128)(2,1)S(1)}, bf16[176,128]{1,0:T(8,128)(2,1)S(1)}, u32[]{:S(2)}, u32[]{:S(2)}) %collective-permute-start.29) | collective-permute-done | bytes 45088 | tf_op jit(solution)/shard_map/ppermute | solution.py:97
  93.7 1.2 %collective-permute-done.30.refs_9_.refs_3_ = bf16[176,128]{1,0:T(8,128)(2,1)S(1)} collective-permute-done((bf16[176,128]{1,0:T(8,128)(2,1)S(1)}, bf16[176,128]{1,0:T(8,128)(2,1)S(1)}, u32[]{:S(2)}, u32[]{:S(2)}) %collective-permute-start.30) | collective-permute-done | bytes 45088 | tf_op jit(solution)/shard_map/ppermute | solution.py:97
  94.9 0.6 shard_map.139
  95.5 3.6 %shard_map.138 = bf16[64,128,128]{2,1,0:T(8,128)(2,1)} custom-call(s32[128]{0:T(128)S(1)} %shard_map.122.refs_0_, bf16[9,32,128]{2,1,0:T(8,128)(2,1)S(1)} %get-tuple-element.81.refs_1_, bf16[9,32,128]{2,1,0:T(8,128)(2,1)S(1)} %get-tuple-element.82.refs_2_, bf16[9,32,128]{2,1,0:T(8,128)(2,1)S(1)} %get-tuple-element.83.refs_3_, ...), custom_call_target="tpu_custom_call" | custom-call | flops 268435456 | bytes 4194304 | tf_op jit(solution)/shard_map/pallas_call | solution.py:621
  99.1 0.3 collective-permute-done.31
  99.4 0.6 add_bitcast_fusion
  (40 shorter events, 0.4 us)
Async XLA Ops:
  1.4 0.8 copy-start.4
  2.3 10.5 %collective-permute-start = (bf16[96,128]{1,0:T(8,128)(2,1)S(1)}, bf16[96,128]{1,0:T(8,128)(2,1)S(1)}, u32[]{:S(2)}, u32[]{:S(2)}) collective-permute-start(bf16[96,128]{1,0:T(8,128)(2,1)S(1)} %get-tuple-element.54.after.refs_2_.refs_0_.mine), channel_id=1, source_target_pairs={{0,4},{4,0},{8,12},{12,8},{1,5},{5,1},{9,13},{13,9},{2,6},{6,2},{1... | collective-permute-start | bytes 73736 | tf_op jit(solution)/shard_map/ppermute | solution.py:97
  5.3 7.5 %collective-permute-start.1 = (bf16[96,128]{1,0:T(8,128)(2,1)S(1)}, bf16[96,128]{1,0:T(8,128)(2,1)S(1)}, u32[]{:S(2)}, u32[]{:S(2)}) collective-permute-start(bf16[96,128]{1,0:T(8,128)(2,1)S(1)} %get-tuple-element.54.after.refs_2_.refs_0_.mine), channel_id=1, source_target_pairs={{0,8},{4,12},{8,0},{12,4},{1,9},{5,13},{9,1},{13,5},{2,10},{6,14},... | collective-permute-start | bytes 73736 | tf_op jit(solution)/shard_map/ppermute | solution.py:97
  7.9 5.6 %collective-permute-start.2 = (bf16[96,128]{1,0:T(8,128)(2,1)S(1)}, bf16[96,128]{1,0:T(8,128)(2,1)S(1)}, u32[]{:S(2)}, u32[]{:S(2)}) collective-permute-start(bf16[96,128]{1,0:T(8,128)(2,1)S(1)} %get-tuple-element.54.after.refs_2_.refs_0_.mine), channel_id=1, source_target_pairs={{0,12},{4,8},{8,4},{12,0},{1,13},{5,9},{9,5},{13,1},{2,14},{6,10},... | collective-permute-start | bytes 73736 | tf_op jit(solution)/shard_map/ppermute | solution.py:97
  7.9 1.6 %copy-start = (bf16[1,1,64,128,128]{4,3,2,1,0:T(8,128)(2,1)S(1)}, bf16[1,1,64,128,128]{4,3,2,1,0:T(8,128)(2,1)}, u32[]{:S(2)}) copy-start(bf16[1,1,64,128,128]{4,3,2,1,0:T(8,128)(2,1)} %param.13) | copy-start | bytes 6291460
  9.5 0.7 copy-start.6
  10.2 0.7 copy-start.7
  10.8 0.7 copy-start.8
  11.5 2.1 %copy-start.1 = (bf16[1,1,64,128,128]{4,3,2,1,0:T(8,128)(2,1)S(1)}, bf16[1,1,64,128,128]{4,3,2,1,0:T(8,128)(2,1)}, u32[]{:S(2)}) copy-start(bf16[1,1,64,128,128]{4,3,2,1,0:T(8,128)(2,1)} %param.13) | copy-start | bytes 6291460
  11.5 14.0 %copy-start.2 = (f32[3,32,288]{2,1,0:T(8,128)S(1)}, f32[3,32,288]{2,1,0:T(8,128)}, u32[]{:S(2)}) copy-start(f32[3,32,288]{2,1,0:T(8,128)} %refs_2_.1) | copy-start | bytes 331780
  11.5 14.0 %copy-start.3 = (bf16[3,32,512]{2,1,0:T(8,128)(2,1)S(1)}, bf16[3,32,512]{2,1,0:T(8,128)(2,1)}, u32[]{:S(2)}) copy-start(bf16[3,32,512]{2,1,0:T(8,128)(2,1)} %param.11) | copy-start | bytes 294916
  11.5 14.0 %copy-start.5 = (f32[8192]{0:T(1024)S(1)}, f32[8192]{0:T(1024)}, u32[]{:S(2)}) copy-start(f32[8192]{0:T(1024)} %param.18) | copy-start | bytes 98308
  15.7 1.3 %collective-permute-start.3 = (bf16[288,128]{1,0:T(8,128)(2,1)S(1)}, bf16[288,128]{1,0:T(8,128)(2,1)S(1)}, u32[]{:S(2)}, u32[]{:S(2)}) collective-permute-start(bf16[288,128]{1,0:T(8,128)(2,1)S(1)} %get-tuple-element.56), channel_id=1, source_target_pairs={{0,1},{1,0},{2,3},{3,2},{4,5},{5,4},{6,7},{7,6},{8,9},{9,8},{10,11... | collective-permute-start | bytes 221192 | tf_op jit(solution)/shard_map/ppermute | solution.py:97
  17.0 4.0 %collective-permute-start.4 = (bf16[144,128]{1,0:T(8,128)(2,1)S(1)}, bf16[144,128]{1,0:T(8,128)(2,1)S(1)}, u32[]{:S(2)}, u32[]{:S(2)}) collective-permute-start(bf16[144,128]{1,0:T(8,128)(2,1)S(1)} %get-tuple-element.58), channel_id=1, source_target_pairs={{0,2},{1,3},{2,0},{3,1},{4,6},{5,7},{6,4},{7,5},{8,10},{9,11},{10,... | collective-permute-start | bytes 110600 | tf_op jit(solution)/shard_map/ppermute | solution.py:97
  21.0 5.4 %collective-permute-start.5 = (bf16[144,128]{1,0:T(8,128)(2,1)S(1)}, bf16[144,128]{1,0:T(8,128)(2,1)S(1)}, u32[]{:S(2)}, u32[]{:S(2)}) collective-permute-start(bf16[144,128]{1,0:T(8,128)(2,1)S(1)} %get-tuple-element.64), channel_id=1, source_target_pairs={{0,4},{4,0},{8,12},{12,8},{1,5},{5,1},{9,13},{13,9},{2,6},{6,2},{1... | collective-permute-start | bytes 110600 | tf_op jit(solution)/shard_map/ppermute | solution.py:97
  21.5 5.4 %collective-permute-start.6 = (bf16[144,128]{1,0:T(8,128)(2,1)S(1)}, bf16[144,128]{1,0:T(8,128)(2,1)S(1)}, u32[]{:S(2)}, u32[]{:S(2)}) collective-permute-start(bf16[144,128]{1,0:T(8,128)(2,1)S(1)} %get-tuple-element.64), channel_id=1, source_target_pairs={{0,8},{4,12},{8,0},{12,4},{1,9},{5,13},{9,1},{13,5},{2,10},{6,14},... | collective-permute-start | bytes 110600 | tf_op jit(solution)/shard_map/ppermute | solution.py:97
  25.0 5.8 %collective-permute-start.7 = (bf16[144,128]{1,0:T(8,128)(2,1)S(1)}, bf16[144,128]{1,0:T(8,128)(2,1)S(1)}, u32[]{:S(2)}, u32[]{:S(2)}) collective-permute-start(bf16[144,128]{1,0:T(8,128)(2,1)S(1)} %get-tuple-element.64), channel_id=1, source_target_pairs={{0,12},{4,8},{8,4},{12,0},{1,13},{5,9},{9,5},{13,1},{2,14},{6,10},... | collective-permute-start | bytes 110600 | tf_op jit(solution)/shard_map/ppermute | solution.py:97
  32.9 1.3 %collective-permute-start.8 = (bf16[288,128]{1,0:T(8,128)(2,1)S(1)}, bf16[288,128]{1,0:T(8,128)(2,1)S(1)}, u32[]{:S(2)}, u32[]{:S(2)}) collective-permute-start(bf16[288,128]{1,0:T(8,128)(2,1)S(1)} %get-tuple-element.66), channel_id=1, source_target_pairs={{0,1},{1,0},{2,3},{3,2},{4,5},{5,4},{6,7},{7,6},{8,9},{9,8},{10,11... | collective-permute-start | bytes 221192 | tf_op jit(solution)/shard_map/ppermute | solution.py:97
  34.3 4.0 %collective-permute-start.9 = (bf16[144,128]{1,0:T(8,128)(2,1)S(1)}, bf16[144,128]{1,0:T(8,128)(2,1)S(1)}, u32[]{:S(2)}, u32[]{:S(2)}) collective-permute-start(bf16[144,128]{1,0:T(8,128)(2,1)S(1)} %get-tuple-element.68), channel_id=1, source_target_pairs={{0,2},{1,3},{2,0},{3,1},{4,6},{5,7},{6,4},{7,5},{8,10},{9,11},{10,... | collective-permute-start | bytes 110600 | tf_op jit(solution)/shard_map/ppermute | solution.py:97
  38.3 4.5 %collective-permute-start.10 = (bf16[144,128]{1,0:T(8,128)(2,1)S(1)}, bf16[144,128]{1,0:T(8,128)(2,1)S(1)}, u32[]{:S(2)}, u32[]{:S(2)}) collective-permute-start(bf16[144,128]{1,0:T(8,128)(2,1)S(1)} %get-tuple-element.71), channel_id=1, source_target_pairs={{0,4},{4,0},{8,12},{12,8},{1,5},{5,1},{9,13},{13,9},{2,6},{6,2},{1... | collective-permute-start | bytes 110600 | tf_op jit(solution)/shard_map/ppermute | solution.py:97
  38.4 4.9 %collective-permute-start.11 = (bf16[144,128]{1,0:T(8,128)(2,1)S(1)}, bf16[144,128]{1,0:T(8,128)(2,1)S(1)}, u32[]{:S(2)}, u32[]{:S(2)}) collective-permute-start(bf16[144,128]{1,0:T(8,128)(2,1)S(1)} %get-tuple-element.71), channel_id=1, source_target_pairs={{0,8},{4,12},{8,0},{12,4},{1,9},{5,13},{9,1},{13,5},{2,10},{6,14},... | collective-permute-start | bytes 110600 | tf_op jit(solution)/shard_map/ppermute | solution.py:97
  39.4 5.8 %collective-permute-start.12 = (bf16[144,128]{1,0:T(8,128)(2,1)S(1)}, bf16[144,128]{1,0:T(8,128)(2,1)S(1)}, u32[]{:S(2)}, u32[]{:S(2)}) collective-permute-start(bf16[144,128]{1,0:T(8,128)(2,1)S(1)} %get-tuple-element.71), channel_id=1, source_target_pairs={{0,12},{4,8},{8,4},{12,0},{1,13},{5,9},{9,5},{13,1},{2,14},{6,10},... | collective-permute-start | bytes 110600 | tf_op jit(solution)/shard_map/ppermute | solution.py:97
  47.3 1.3 %collective-permute-start.13 = (bf16[288,128]{1,0:T(8,128)(2,1)S(1)}, bf16[288,128]{1,0:T(8,128)(2,1)S(1)}, u32[]{:S(2)}, u32[]{:S(2)}) collective-permute-start(bf16[288,128]{1,0:T(8,128)(2,1)S(1)} %get-tuple-element.73), channel_id=1, source_target_pairs={{0,1},{1,0},{2,3},{3,2},{4,5},{5,4},{6,7},{7,6},{8,9},{9,8},{10,11... | collective-permute-start | bytes 221192 | tf_op jit(solution)/shard_map/ppermute | solution.py:97
  48.6 4.0 %collective-permute-start.14 = (bf16[144,128]{1,0:T(8,128)(2,1)S(1)}, bf16[144,128]{1,0:T(8,128)(2,1)S(1)}, u32[]{:S(2)}, u32[]{:S(2)}) collective-permute-start(bf16[144,128]{1,0:T(8,128)(2,1)S(1)} %get-tuple-element.75), channel_id=1, source_target_pairs={{0,2},{1,3},{2,0},{3,1},{4,6},{5,7},{6,4},{7,5},{8,10},{9,11},{10,... | collective-permute-start | bytes 110600 | tf_op jit(solution)/shard_map/ppermute | solution.py:97
  52.7 5.8 %collective-permute-start.15 = (bf16[224,128]{1,0:T(8,128)(2,1)S(1)}, bf16[224,128]{1,0:T(8,128)(2,1)S(1)}, u32[]{:S(2)}, u32[]{:S(2)}) collective-permute-start(bf16[224,128]{1,0:T(8,128)(2,1)S(1)} %get-tuple-element.78), channel_id=1, source_target_pairs={{0,8},{4,12},{8,0},{12,4},{1,9},{5,13},{9,1},{13,5},{2,10},{6,14},... | collective-permute-start | bytes 172040 | tf_op jit(solution)/shard_map/ppermute | solution.py:97
  59.1 4.0 %collective-permute-start.17 = (bf16[144,128]{1,0:T(8,128)(2,1)S(1)}, bf16[144,128]{1,0:T(8,128)(2,1)S(1)}, u32[]{:S(2)}, u32[]{:S(2)}) collective-permute-start(bf16[144,128]{1,0:T(8,128)(2,1)S(1)} %get-tuple-element.85.refs_3_), channel_id=1, source_target_pairs={{0,2},{1,3},{2,0},{3,1},{4,6},{5,7},{6,4},{7,5},{8,10},{9,11},{10,... | collective-permute-start | bytes 110600 | tf_op jit(solution)/shard_map/ppermute | solution.py:97
  60.6 2.5 %collective-permute-start.16 = (bf16[144,128]{1,0:T(8,128)(2,1)S(1)}, bf16[144,128]{1,0:T(8,128)(2,1)S(1)}, u32[]{:S(2)}, u32[]{:S(2)}) collective-permute-start(bf16[144,128]{1,0:T(8,128)(2,1)S(1)} %get-tuple-element.85.refs_3_), channel_id=1, source_target_pairs={{0,1},{1,0},{2,3},{3,2},{4,5},{5,4},{6,7},{7,6},{8,9},{9,8},{10,11... | collective-permute-start | bytes 110600 | tf_op jit(solution)/shard_map/ppermute | solution.py:97
  63.1 1.2 %collective-permute-start.18 = (bf16[144,128]{1,0:T(8,128)(2,1)S(1)}, bf16[144,128]{1,0:T(8,128)(2,1)S(1)}, u32[]{:S(2)}, u32[]{:S(2)}) collective-permute-start(bf16[144,128]{1,0:T(8,128)(2,1)S(1)} %collective-permute-done.17.refs_5_), channel_id=1, source_target_pairs={{0,1},{1,0},{2,3},{3,2},{4,5},{5,4},{6,7},{7,6},{8,9},{9,8},{10,11... | collective-permute-start | bytes 110600 | tf_op jit(solution)/shard_map/ppermute | solution.py:97
  65.9 4.5 %collective-permute-start.19 = (bf16[144,128]{1,0:T(8,128)(2,1)S(1)}, bf16[144,128]{1,0:T(8,128)(2,1)S(1)}, u32[]{:S(2)}, u32[]{:S(2)}) collective-permute-start(bf16[144,128]{1,0:T(8,128)(2,1)S(1)} %get-tuple-element.91), channel_id=1, source_target_pairs={{0,4},{4,0},{8,12},{12,8},{1,5},{5,1},{9,13},{13,9},{2,6},{6,2},{1... | collective-permute-start | bytes 110600 | tf_op jit(solution)/shard_map/ppermute | solution.py:97
  66.5 5.5 %collective-permute-start.20 = (bf16[144,128]{1,0:T(8,128)(2,1)S(1)}, bf16[144,128]{1,0:T(8,128)(2,1)S(1)}, u32[]{:S(2)}, u32[]{:S(2)}) collective-permute-start(bf16[144,128]{1,0:T(8,128)(2,1)S(1)} %get-tuple-element.92), channel_id=1, source_target_pairs={{0,8},{4,12},{8,0},{12,4},{1,9},{5,13},{9,1},{13,5},{2,10},{6,14},... | collective-permute-start | bytes 110600 | tf_op jit(solution)/shard_map/ppermute | solution.py:97
  69.3 5.8 %collective-permute-start.21 = (bf16[144,128]{1,0:T(8,128)(2,1)S(1)}, bf16[144,128]{1,0:T(8,128)(2,1)S(1)}, u32[]{:S(2)}, u32[]{:S(2)}) collective-permute-start(bf16[144,128]{1,0:T(8,128)(2,1)S(1)} %get-tuple-element.93), channel_id=1, source_target_pairs={{0,12},{4,8},{8,4},{12,0},{1,13},{5,9},{9,5},{13,1},{2,14},{6,10},... | collective-permute-start | bytes 110600 | tf_op jit(solution)/shard_map/ppermute | solution.py:97
  75.1 4.0 %collective-permute-start.23 = (bf16[144,128]{1,0:T(8,128)(2,1)S(1)}, bf16[144,128]{1,0:T(8,128)(2,1)S(1)}, u32[]{:S(2)}, u32[]{:S(2)}) collective-permute-start(bf16[144,128]{1,0:T(8,128)(2,1)S(1)} %get-tuple-element.95.refs_3_), channel_id=1, source_target_pairs={{0,2},{1,3},{2,0},{3,1},{4,6},{5,7},{6,4},{7,5},{8,10},{9,11},{10,... | collective-permute-start | bytes 110600 | tf_op jit(solution)/shard_map/ppermute | solution.py:97
  76.7 2.5 %collective-permute-start.22 = (bf16[144,128]{1,0:T(8,128)(2,1)S(1)}, bf16[144,128]{1,0:T(8,128)(2,1)S(1)}, u32[]{:S(2)}, u32[]{:S(2)}) collective-permute-start(bf16[144,128]{1,0:T(8,128)(2,1)S(1)} %get-tuple-element.95.refs_3_), channel_id=1, source_target_pairs={{0,1},{1,0},{2,3},{3,2},{4,5},{5,4},{6,7},{7,6},{8,9},{9,8},{10,11... | collective-permute-start | bytes 110600 | tf_op jit(solution)/shard_map/ppermute | solution.py:97
  79.1 1.2 %collective-permute-start.24 = (bf16[144,128]{1,0:T(8,128)(2,1)S(1)}, bf16[144,128]{1,0:T(8,128)(2,1)S(1)}, u32[]{:S(2)}, u32[]{:S(2)}) collective-permute-start(bf16[144,128]{1,0:T(8,128)(2,1)S(1)} %collective-permute-done.23.refs_5_), channel_id=1, source_target_pairs={{0,1},{1,0},{2,3},{3,2},{4,5},{5,4},{6,7},{7,6},{8,9},{9,8},{10,11... | collective-permute-start | bytes 110600 | tf_op jit(solution)/shard_map/ppermute | solution.py:97
  81.9 4.5 %collective-permute-start.25 = (bf16[144,128]{1,0:T(8,128)(2,1)S(1)}, bf16[144,128]{1,0:T(8,128)(2,1)S(1)}, u32[]{:S(2)}, u32[]{:S(2)}) collective-permute-start(bf16[144,128]{1,0:T(8,128)(2,1)S(1)} %get-tuple-element.102), channel_id=1, source_target_pairs={{0,4},{4,0},{8,12},{12,8},{1,5},{5,1},{9,13},{13,9},{2,6},{6,2},{1... | collective-permute-start | bytes 110600 | tf_op jit(solution)/shard_map/ppermute | solution.py:97
  82.0 4.9 %collective-permute-start.26 = (bf16[144,128]{1,0:T(8,128)(2,1)S(1)}, bf16[144,128]{1,0:T(8,128)(2,1)S(1)}, u32[]{:S(2)}, u32[]{:S(2)}) collective-permute-start(bf16[144,128]{1,0:T(8,128)(2,1)S(1)} %get-tuple-element.103), channel_id=1, source_target_pairs={{0,8},{4,12},{8,0},{12,4},{1,9},{5,13},{9,1},{13,5},{2,10},{6,14},... | collective-permute-start | bytes 110600 | tf_op jit(solution)/shard_map/ppermute | solution.py:97
  83.7 5.8 %collective-permute-start.27 = (bf16[144,128]{1,0:T(8,128)(2,1)S(1)}, bf16[144,128]{1,0:T(8,128)(2,1)S(1)}, u32[]{:S(2)}, u32[]{:S(2)}) collective-permute-start(bf16[144,128]{1,0:T(8,128)(2,1)S(1)} %get-tuple-element.104), channel_id=1, source_target_pairs={{0,12},{4,8},{8,4},{12,0},{1,13},{5,9},{9,5},{13,1},{2,14},{6,10},... | collective-permute-start | bytes 110600 | tf_op jit(solution)/shard_map/ppermute | solution.py:97
  89.5 4.1 %collective-permute-start.29 = (bf16[176,128]{1,0:T(8,128)(2,1)S(1)}, bf16[176,128]{1,0:T(8,128)(2,1)S(1)}, u32[]{:S(2)}, u32[]{:S(2)}) collective-permute-start(bf16[176,128]{1,0:T(8,128)(2,1)S(1)} %shard_map.137.refs_6_.refs_0_), channel_id=1, source_target_pairs={{0,2},{1,3},{2,0},{3,1},{4,6},{5,7},{6,4},{7,5},{8,10},{9,11},{10,... | collective-permute-start | bytes 135176 | tf_op jit(solution)/shard_map/ppermute | solution.py:97
  91.1 2.6 %collective-permute-start.28 = (bf16[176,128]{1,0:T(8,128)(2,1)S(1)}, bf16[176,128]{1,0:T(8,128)(2,1)S(1)}, u32[]{:S(2)}, u32[]{:S(2)}) collective-permute-start(bf16[176,128]{1,0:T(8,128)(2,1)S(1)} %shard_map.137.refs_6_.refs_0_), channel_id=1, source_target_pairs={{0,1},{1,0},{2,3},{3,2},{4,5},{5,4},{6,7},{7,6},{8,9},{9,8},{10,11... | collective-permute-start | bytes 135176 | tf_op jit(solution)/shard_map/ppermute | solution.py:97
  93.6 1.2 %collective-permute-start.30 = (bf16[176,128]{1,0:T(8,128)(2,1)S(1)}, bf16[176,128]{1,0:T(8,128)(2,1)S(1)}, u32[]{:S(2)}, u32[]{:S(2)}) collective-permute-start(bf16[176,128]{1,0:T(8,128)(2,1)S(1)} %collective-permute-done.29.refs_8_.refs_2_), channel_id=1, source_target_pairs={{0,1},{1,0},{2,3},{3,2},{4,5},{5,4},{6,7},{7,6},{8,9},{9,8},{10,11... | collective-permute-start | bytes 135176 | tf_op jit(solution)/shard_map/ppermute | solution.py:97
  95.5 4.0 %collective-permute-start.31 = (f32[64,128]{1,0:T(8,128)S(1)}, f32[64,128]{1,0:T(8,128)S(1)}, u32[]{:S(2)}, u32[]{:S(2)}) collective-permute-start(f32[64,128]{1,0:T(8,128)S(1)} %shard_map.139), channel_id=1, source_target_pairs={{0,4},{4,0},{8,12},{12,8},{1,5},{5,1},{9,13},{13,9},{2,6},{6,2},{1... | collective-permute-start | bytes 98312 | tf_op jit(solution)/shard_map/ppermute | solution.py:97

commit v5 on v4

--- a/solution.py
+++ b/solution.py
@@ -12,7 +12,6 @@
 F32 = jnp.float32
 BF16 = jnp.bfloat16
 VMEM = pl.BlockSpec(memory_space=pltpu.VMEM)
-SMEM = pl.BlockSpec(memory_space=pltpu.SMEM)
 
 
 class Sizes:
@@ -101,24 +100,17 @@
     return count <= 4
 
 
-def paired(axis):
-    return axis == "col" and lax.axis_size(axis) == 4
-
-
 def share(x, axis):
     count = lax.axis_size(axis)
-    if paired(axis):
-        far = flip(x, axis, 2)
-        return [flip(x, axis, 1), far, flip(far, axis, 1)]
     if few(count):
-        return [flip(x, axis, k) for k in reversed(range(1, count))][::-1]
+        return [flip(x, axis, k) for k in reversed(range(1, count))]
     return [lax.all_gather(x, axis)]
 
 
 def exchange(parts, axis):
     count = lax.axis_size(axis)
     if len(parts) == count - 1:
-        return [flip(parts[k - 1], axis, k) for k in reversed(range(1, count))][::-1]
+        return [flip(part, axis, count - 1 - i) for i, part in enumerate(parts)]
     return [lax.all_to_all(parts[0], axis, 0, 0, tiled=True)]
 
 
@@ -129,7 +121,7 @@
 
 
 def away(refs, count, me, k):
-    return refs[k - 1] if len(refs) == count - 1 else refs[0].at[me ^ k]
+    return refs[count - 1 - k] if len(refs) == count - 1 else refs[0].at[me ^ k]
 
 
 def place():
@@ -157,15 +149,9 @@
     message[...] = jnp.concatenate([packed, extra], axis=0).astype(BF16)
 
 
-def load_kernel(z, after, owner, post, pre, weights, ids):
+def list_kernel(z, after, owner, post, pre, weights, ids):
     del after, weights
-
-    def one(s, carry):
-        ids[s] = owner[0, 0, s] * z.post + post[0, 0, s]
-        ids[z.slots + s] = pre[0, 0, s]
-        return carry
-
-    lax.fori_loop(0, z.slots, one, 0, unroll=8)
+    ids[...] = jnp.concatenate([owner[0] * z.post + post[0], pre[0]], axis=1)
 
 
 def prepare_kernel(z, count, *refs):
@@ -211,44 +197,43 @@
 def multiply_forward(z, c, ids, weights, x, total, own, parts):
     total[...] = jnp.zeros_like(total)
     for s in range(z.slots):
-        total[ids[s]] += lax.dot_general(
-            x[ids[z.slots + s]], weights[s], (((1,), (1,)), ((), ())), preferred_element_type=F32
+        total[ids[0, s]] += lax.dot_general(
+            x[ids[0, z.slots + s]], weights[s], (((1,), (1,)), ((), ())), preferred_element_type=F32
         )
     for k in range(z.cols):
         both = jnp.concatenate(
             [z.take_blocks(total, 0, c ^ k), z.take_blocks(total, z.post, c ^ k)], axis=0
         )
-        if z.cols == 4:
-            rows = slice(k // 2 * z.pair, (k // 2 + 1) * z.pair)
-            if k % 2 == 0:
-                own[rows] = both
-            else:
-                parts[0][rows] = both.astype(BF16)
-        elif k == 0:
+        if k == 0:
             own[...] = both
         else:
             away(parts, z.cols, c, k)[...] = both.astype(BF16)
 
 
 def first_kernel(z, count, *refs):
-    ids, weights, mine = refs[:3]
+    near_ids, weights, mine = refs[:3]
     got = refs[3 : 3 + count]
     x, own = refs[3 + count : 5 + count]
-    parts, (sums, total) = refs[5 + count : -2], refs[-2:]
+    parts, (sums, total, ids, sem) = refs[5 + count : -4], refs[-4:]
+    bring = pltpu.make_async_copy(near_ids, ids, sem)
+    bring.start()
     p, c = place()
     sums[...] = jnp.zeros_like(sums)
     for k in range(z.rows):
         ref = mine if k == 0 else away(got, z.rows, p, k)
         z.add_blocks(sums, 0, p ^ k, ref[...].astype(F32)[0 : z.piece])
     x[...] = sums[...].astype(BF16)
+    bring.wait()
     multiply_forward(z, c, ids, weights, x, total, own, parts)
 
 
 def forward_kernel(z, step, count, *refs):
-    ids, weights, kept, rates, gain, drive = refs[:6]
+    near_ids, weights, kept, rates, gain, drive = refs[:6]
     got = refs[6 : 6 + count]
     new, act_pair, cur_pair, x, own = refs[6 + count : 11 + count]
-    parts, (sums, total) = refs[11 + count : -2], refs[-2:]
+    parts, (sums, total, ids, sem) = refs[11 + count : -4], refs[-4:]
+    bring = pltpu.make_async_copy(near_ids, ids, sem)
+    bring.start()
     p, c = place()
     sums[...] = jnp.zeros_like(sums)
 
@@ -268,13 +253,8 @@
             cur_pair[at : at + z.piece] = current
         z.add_blocks(sums, 0, p ^ k, fresh)
     x[...] = sums[...].astype(BF16)
+    bring.wait()
     multiply_forward(z, c, ids, weights, x, total, own, parts)
-
-
-def half_kernel(z, own, got, kept, message):
-    total = own[...] + got[...].astype(F32)
-    kept[...] = total[0 : z.pair]
-    message[...] = total[z.pair :].astype(BF16)
 
 
 def sum_kernel(z, count, with_cot, *refs):
@@ -282,11 +262,8 @@
     kept, message = refs[-2:]
     _, c = place()
     total = own[...]
-    if z.cols == 4:
-        total = total + got[0][...].astype(F32)
-    else:
-        for k in range(1, z.cols):
-            total = total + away(got, z.cols, c, k)[...].astype(F32)
+    for k in range(1, z.cols):
+        total = total + away(got, z.cols, c, k)[...].astype(F32)
     kept[...] = total
     if with_cot:
         cot = refs[1 + count]
@@ -308,7 +285,7 @@
     current = kept[...] + swapped + pair_of(z, drive.at[z.steps - 1])
     activity = jnp.tanh(gains * current)
     fresh = 0.5 * rates[0 : z.piece] + 0.5 * activity[0 : z.piece]
-    final[...] = z.unpack(fresh)[:, 0 : z.local]
+    final[...] = fresh
     mine = cots[z.steps - 1]
     adjoint = jnp.concatenate([mine, other[z.pair : z.pair + z.piece]], axis=0)
     pressure = adjoint * 0.5 * (1.0 - activity * activity)
@@ -328,15 +305,18 @@
 
 
 def back_kernel(z, count, *refs):
-    ids, weights, base, mine = refs[:4]
+    near_ids, weights, base, mine = refs[:4]
     got = refs[4 : 4 + count]
     d, own = refs[4 + count : 6 + count]
-    parts, (sums, total) = refs[6 + count : -2], refs[-2:]
+    parts, (sums, total, ids, sem) = refs[6 + count : -4], refs[-4:]
+    bring = pltpu.make_async_copy(near_ids, ids, sem)
+    bring.start()
     p, c = place()
     gather_post(z, c, mine, got, sums, d)
     total[...] = jnp.zeros_like(total)
+    bring.wait()
     for s in range(z.slots):
-        total[ids[z.slots + s]] += jnp.dot(d[ids[s]], weights[s], preferred_element_type=F32)
+        total[ids[0, z.slots + s]] += jnp.dot(d[ids[0, s]], weights[s], preferred_element_type=F32)
     pieces = [z.take_blocks(total, 0, p ^ k) for k in range(z.rows)]
     for k in range(z.rows):
         other = pieces[k ^ z.half]
@@ -396,7 +376,7 @@
 
 
 def table_kernel(z, count, *refs):
-    mine, got, out = refs[0], refs[1:-1], refs[-1]
+    mine, got, out = refs[1], refs[2:-1], refs[-1]
     _, c = place()
     highs = z.types // BLOCK
     high_ids = lax.broadcasted_iota(jnp.int32, (highs, BLOCK), 0).astype(F32) + 1.0
@@ -418,41 +398,72 @@
     out[...] = total[0:highs] + total[highs : 2 * highs] + total[2 * highs :]
 
 
-def grad_kernel(z, count, per_step, *refs):
-    ids, xs, ds = refs[0], refs[1 : 1 + z.steps], refs[1 + z.steps : 2 * z.steps]
-    mine, got = refs[2 * z.steps], refs[2 * z.steps + 1 : 2 * z.steps + 1 + count]
-    out = refs[2 * z.steps + 1 + count]
-    sums, d0, right, left = refs[2 * z.steps + 2 + count :]
+def lay_kernel(z, *refs):
+    xs, ds = refs[: z.steps], refs[z.steps : 2 * z.steps - 1]
+    last_rates, right, left, final = refs[2 * z.steps - 1 :]
+    final[...] = z.unpack(last_rates[...])[:, 0 : z.local]
     n = z.batch
     deep = right.shape[1]
+    rest = deep - z.steps * n
+
+    def lay_right(q):
+        for t in range(z.steps):
+            right[q, t * n : (t + 1) * n] = xs[t][q]
+        if rest:
+            right[q, z.steps * n :] = jnp.zeros((rest, BLOCK), BF16)
+
+    loop(z.pre, lay_right)
+
+    def lay_left(q):
+        parts = [jnp.zeros((n, BLOCK), F32)] + [d[q].astype(F32) for d in ds]
+        if rest:
+            parts.append(jnp.zeros((rest, BLOCK), F32))
+        left[q] = jnp.transpose(jnp.concatenate(parts, axis=0)).astype(BF16)
+
+    loop(2 * z.post, lay_left)
+
+
+def grad_kernel(z, count, per_step, *refs):
+    near_ids, right, later, mine = refs[:4]
+    got = refs[4 : 4 + count]
+    left, out, sums, d0, ids, sem = refs[4 + count :]
+    n = z.batch
+    deep = right.shape[1]
 
     @pl.when(pl.program_id(0) == 0)
     def _():
+        bring = pltpu.make_async_copy(near_ids, ids, sem)
+        bring.start()
         _, c = place()
         gather_post(z, c, mine, got, sums, d0)
-
-        def lay_right(q):
-            for t in range(z.steps):
-                right[q, t * n : (t + 1) * n] = xs[t][q]
-            if deep > z.steps * n:
-                right[q, z.steps * n :] = jnp.zeros((deep - z.steps * n, BLOCK), BF16)
-
-        loop(z.pre, lay_right)
+        lanes = lax.broadcasted_iota(jnp.int32, (BLOCK, deep), 1)
 
         def lay_left(q):
-            parts = [d0[q].astype(F32)] + [d[q].astype(F32) for d in ds]
-            if deep > z.steps * n:
-                parts.append(jnp.zeros((deep - z.steps * n, BLOCK), F32))
-            left[q] = jnp.transpose(jnp.concatenate(parts, axis=0)).astype(BF16)
+            whole = jnp.concatenate([sums[q], jnp.zeros((deep - n, BLOCK), F32)], axis=0)
+            turned = jnp.transpose(whole)
+            left[q] = jnp.where(lanes < n, turned, later[q].astype(F32)).astype(BF16)
 
         loop(2 * z.post, lay_left)
-
-    begin = pl.program_id(0) * per_step
-    for s in range(per_step):
+        bring.wait()
+
+    products(z, pl.program_id(0) * per_step, per_step, ids, left, right, out)
+
+
+def products(z, begin, count, ids, left, right, out):
+    for s in range(count):
         product = jnp.dot(
-            left[ids[begin + s]], right[ids[z.slots + begin + s]], preferred_element_type=F32
+            left[ids[0, begin + s]], right[ids[0, z.slots + begin + s]], preferred_element_type=F32
         )
         out[s] = product.astype(BF16)
+
+
+def rest_kernel(z, begin, per_step, near_ids, left, right, table, other, grads, out, sums, ids, sem):
+    del grads
+    bring = pltpu.make_async_copy(near_ids, ids, sem)
+    bring.start()
+    sums[...] = table[...] + other[...]
+    bring.wait()
+    products(z, begin + pl.program_id(0) * per_step, per_step, ids, left, right, out)
 
 
 def shards(
@@ -490,32 +501,26 @@
     got = share(message, "row")
     weights = weight_blocks.reshape(slots, BLOCK, BLOCK)
     (ids,) = call(
-        functools.partial(load_kernel, z),
-        [shape((2 * slots,), jnp.int32)],
+        functools.partial(list_kernel, z),
+        [shape((1, 2 * slots), jnp.int32)],
         [],
         [message, slot_owner, slot_post, slot_pre, weights],
-        {1: SMEM, 2: SMEM, 3: SMEM},
-        out_specs=[SMEM],
-    )
+    )
+    held_ids = [pltpu.SMEM((1, 2 * slots), jnp.int32), pltpu.SemaphoreType.DMA]
     if few(z.rows):
-        partner_message = got[z.half - 1]
+        partner_message = got[z.rows - 1 - z.half]
     else:
         partner_message = flip(message, "row", z.half)
     pre_sums = pltpu.VMEM((z.pre, batch, BLOCK), F32)
     post_sums = pltpu.VMEM((2 * z.post, batch, BLOCK), F32)
     x_shape = shape((z.pre, batch, BLOCK), BF16)
     row_parts = parcel(z.rows, pair, BF16)
-    two = paired("col")
-    if two:
-        col_parts = [shape((2 * z.pair, BLOCK)), shape((2 * z.pair, BLOCK), BF16)]
-    else:
-        col_parts = [shape(pair), *parcel(z.cols, pair, BF16)]
+    col_parts = [shape(pair), *parcel(z.cols, pair, BF16)]
     x, own, *parts = call(
         functools.partial(first_kernel, z, len(got)),
         [x_shape, *col_parts],
-        [pre_sums, post_sums],
+        [pre_sums, post_sums, *held_ids],
         [ids, weights, message, *got],
-        {0: SMEM},
         flops=product_flops,
     )
     every = (z.rows * z.piece, BLOCK)
@@ -535,14 +540,7 @@
     xs, acts, curs = [x], [], []
     for t in range(steps):
         last = t == steps - 1
-        if two:
-            near = flip(parts[0], "col", 1)
-            own, far = call(
-                functools.partial(half_kernel, z), [shape(pair), shape(pair, BF16)], [], [own, near]
-            )
-            got = [flip(far, "col", 2)]
-        else:
-            got = exchange(parts, "col")
+        got = exchange(parts, "col")
         kept, sent = call(
             functools.partial(sum_kernel, z, len(got), last),
             [shape(pair), shape((closing, BLOCK) if last else pair, BF16)],
@@ -555,19 +553,18 @@
         rates, act, cur, x, own, *parts = call(
             functools.partial(forward_kernel, z, t, len(got)),
             [shape(every), shape(pair), shape(pair), x_shape, *col_parts],
-            [pre_sums, post_sums],
+            [pre_sums, post_sums, *held_ids],
             [ids, weights, kept, rates, gain, drive, *got],
-            {0: SMEM},
             flops=product_flops,
         )
         xs.append(x)
         acts.append(act)
         curs.append(cur)
     theirs = flip(sent, "row", z.half)
-    final_rates, delta, gain, tally, base = call(
+    last_rates, delta, gain, tally, base = call(
         functools.partial(turn_kernel, z),
         [
-            shape((batch, local)),
+            shape((z.piece, BLOCK)),
             shape(pair, BF16),
             shape(pair),
             shape(pair),
@@ -582,9 +579,8 @@
         d, own, *parts = call(
             functools.partial(back_kernel, z, len(got)),
             [shape((2 * z.post, batch, BLOCK), BF16), shape(pair), *row_parts],
-            [post_sums, pre_sums],
+            [post_sums, pre_sums, *held_ids],
             [ids, weights, base, delta, *got],
-            {0: SMEM},
             flops=product_flops,
         )
         ds.insert(0, d)
@@ -605,36 +601,54 @@
                 [own, gain, acts[0], curs[0], tally, message, partner_message, *got],
             )
     got = share(delta, "col")
-    (table,) = call(
-        functools.partial(table_kernel, z, len(got)), [shape((types // BLOCK, BLOCK))], [], [delta, *got]
-    )
-    if z.half == 2:
-        table = table + flip(table, "row", 1)
-    else:
-        table = 0.5 * lax.psum(table, "row")
-    gain_grads = table.reshape(types)
-
     grid = 4
     per_step = slots // grid
     deep = (steps * batch + BLOCK - 1) // BLOCK * BLOCK
-    ins = [ids, *xs, *ds, delta, *got]
-    weight_grads = pl.pallas_call(
+    left_shape = shape((2 * z.post, BLOCK, deep), BF16)
+    right, later, final_rates = call(
+        functools.partial(lay_kernel, z),
+        [shape((z.pre, deep, BLOCK), BF16), left_shape, shape((batch, local))],
+        [],
+        [*xs, *ds, last_rates],
+    )
+    (table,) = call(
+        functools.partial(table_kernel, z, len(got)), [shape((types // BLOCK, BLOCK))], [], [right, delta, *got]
+    )
+    if z.half == 2:
+        other = flip(table, "row", 1)
+    else:
+        total = lax.psum(table, "row")
+        other = 0.5 * total - table
+
+    ins = [ids, right, later, delta, *got]
+    cost = pl.CostEstimate(
+        flops=2 * slots * deep * BLOCK * BLOCK, bytes_accessed=4 * 1024 * 1024, transcendentals=0
+    )
+    grads = shape((slots, BLOCK, BLOCK), BF16)
+    limit = pltpu.CompilerParams(vmem_limit_bytes=24 * 1024 * 1024)
+    left, weight_grads = pl.pallas_call(
         functools.partial(grad_kernel, z, len(got), per_step),
-        grid=(grid,),
-        out_shape=shape((slots, BLOCK, BLOCK), BF16),
-        in_specs=[SMEM] + [VMEM] * (len(ins) - 1),
-        out_specs=pl.BlockSpec((per_step, BLOCK, BLOCK), lambda i: (i, 0, 0)),
-        scratch_shapes=[
-            post_sums,
-            pltpu.VMEM((2 * z.post, batch, BLOCK), BF16),
-            pltpu.VMEM((z.pre, deep, BLOCK), BF16),
-            pltpu.VMEM((2 * z.post, BLOCK, deep), BF16),
-        ],
-        cost_estimate=pl.CostEstimate(
-            flops=2 * slots * deep * BLOCK * BLOCK, bytes_accessed=4 * 1024 * 1024, transcendentals=0
-        ),
-        compiler_params=pltpu.CompilerParams(vmem_limit_bytes=24 * 1024 * 1024),
+        grid=(grid - 1,),
+        out_shape=[left_shape, grads],
+        in_specs=[VMEM] * len(ins),
+        out_specs=[VMEM, pl.BlockSpec((per_step, BLOCK, BLOCK), lambda i: (i, 0, 0))],
+        scratch_shapes=[post_sums, pltpu.VMEM((2 * z.post, batch, BLOCK), BF16), *held_ids],
+        cost_estimate=cost,
+        compiler_params=limit,
     )(*ins)
+    ins = [ids, left, right, table, other, weight_grads]
+    weight_grads, table = pl.pallas_call(
+        functools.partial(rest_kernel, z, slots - per_step, per_step),
+        grid=(1,),
+        out_shape=[grads, shape(table.shape)],
+        in_specs=[VMEM] * 5 + [pl.BlockSpec(memory_space=pl.ANY)],
+        out_specs=[pl.BlockSpec((per_step, BLOCK, BLOCK), lambda i: (i + grid - 1, 0, 0)), VMEM],
+        scratch_shapes=held_ids,
+        input_output_aliases={5: 0},
+        cost_estimate=cost,
+        compiler_params=limit,
+    )(*ins)
+    gain_grads = table.reshape(types)
     return (final_rates, weight_grads.reshape(1, 1, slots, BLOCK, BLOCK), gain_grads)
 
 

time: 100 us -> 94.3 us (0.943)
  waiting for transfers between devices: 43.1 us -> 35.3 us
  starting transfers between devices: 33.4 us -> 36.2 us
    ppermute x32 -> x35, waiting for transfers between devices: 43.1 us -> 35.3 us  [flip(): return lax.ppermute(x, axis, [(i, i ^ k) for i in range(count)])]
    ppermute x32 -> x35, starting transfers between devices: 33.4 us -> 36.2 us  [flip(): return lax.ppermute(x, axis, [(i, i ^ k) for i in range(count)])]
    pallas_call x0 -> x1, Pallas kernels: none -> 1.65 us  [shards(): pl.pallas_call(functools.partial(rest_kernel, z, slots - per_step, per_st...]
    pallas_call x18 -> x16, Pallas kernels: 13.5 us -> 12 us  [call(): pl.pallas_call(body, out_shape=outs, in_specs=specs, out_specs=out_specs...]
  transfers between devices with their start and end apart: 32 -> 35, of which waited for: 23 -> 22; matrix products, arithmetic and copies ran while one was open for 0% -> 0% of each run, Pallas kernels for 6% -> 5%
where the time goes in v5:
time: 94.3 us; the launch traced here: 94 us
  starting transfers between devices  36.2 us (38%)
  waiting for transfers between devices  35.3 us (37%)
  Pallas kernels  16.5 us (17%)
  local copies, waits for them, and re-layouts  4.37 us (5%)
    ppermute x35, starting transfers between devices, flip(): return lax.ppermute(x, axis, [(i, i ^ k) for i in range(count)])  36.2 us
    ppermute x35, waiting for transfers between devices, flip(): return lax.ppermute(x, axis, [(i, i ^ k) for i in range(count)])  35.3 us
    pallas_call x16, Pallas kernels, call(): pl.pallas_call(body, out_shape=outs, in_specs=specs, out_specs=out_specs...  12 us
    unnamed x18, local copies, waits for them, and re-layouts  4.37 us
    pallas_call x1, Pallas kernels, shards(): pl.pallas_call(functools.partial(grad_kernel, z, len(got), per_step), gri...  2.9 us
  transfers between devices with their start and end apart: 35, of which 22 were waited for; matrix products, arithmetic and copies ran while one was open for 0% of the time, Pallas kernels for 5%

profile of v5, /device:TPU:0, one launch (start us, length us, event | category | flops | bytes accessed | tf_op | source)
XLA Modules:
  0.0 94.0 jit_solution(4510080081597070654)
XLA Ops:
  0.6 0.8 add_bitcast_fusion.numbers
  1.4 0.8 copy-done.4
  2.3 3.0 %collective-permute-start.2 = (bf16[96,128]{1,0:T(8,128)(2,1)S(1)}, bf16[96,128]{1,0:T(8,128)(2,1)S(1)}, u32[]{:S(2)}, u32[]{:S(2)}) collective-permute-start(bf16[96,128]{1,0:T(8,128)(2,1)S(1)} %get-tuple-element.61.after.refs_2_.refs_0_.mine), channel_id=1, source_target_pairs={{0,4},{4,0},{8,12},{12,8},{1,5},{5,1},{9,13},{13,9},{2,6},{6,2},{1... | collective-permute-start | bytes 73736 | tf_op jit(solution)/shard_map/ppermute | solution.py:96
  5.3 2.6 %collective-permute-start.1 = (bf16[96,128]{1,0:T(8,128)(2,1)S(1)}, bf16[96,128]{1,0:T(8,128)(2,1)S(1)}, u32[]{:S(2)}, u32[]{:S(2)}) collective-permute-start(bf16[96,128]{1,0:T(8,128)(2,1)S(1)} %get-tuple-element.61.after.refs_2_.refs_0_.mine), channel_id=1, source_target_pairs={{0,8},{4,12},{8,0},{12,4},{1,9},{5,13},{9,1},{13,5},{2,10},{6,14},... | collective-permute-start | bytes 73736 | tf_op jit(solution)/shard_map/ppermute | solution.py:96
  7.9 1.6 %copy-done = bf16[1,1,64,128,128]{4,3,2,1,0:T(8,128)(2,1)S(1)} copy-done((bf16[1,1,64,128,128]{4,3,2,1,0:T(8,128)(2,1)S(1)}, bf16[1,1,64,128,128]{4,3,2,1,0:T(8,128)(2,1)}, u32[]{:S(2)}) %copy-start) | copy-done | bytes 2097176
  9.5 0.7 copy-done.6
  10.2 0.7 copy-done.7
  10.8 0.7 copy-done.8
  11.6 2.0 %collective-permute-done.refs_3_.refs_5_ = bf16[96,128]{1,0:T(8,128)(2,1)S(1)} collective-permute-done((bf16[96,128]{1,0:T(8,128)(2,1)S(1)}, bf16[96,128]{1,0:T(8,128)(2,1)S(1)}, u32[]{:S(2)}, u32[]{:S(2)}) %collective-permute-start) | collective-permute-done | bytes 24608 | tf_op jit(solution)/shard_map/ppermute | solution.py:96
  13.5 2.0 %shard_map.123 = (bf16[9,32,128]{2,1,0:T(8,128)(2,1)S(1)}, f32[144,128]{1,0:T(8,128)S(1)}, bf16[144,128]{1,0:T(8,128)(2,1)S(1)}, bf16[144,128]{1,0:T(8,128)(2,1)S(1)}, bf16[144,128]{1,0:T(8,128)(2,1)S(1)}) custom-call(s32[1,128]{1,0:T(1,128)S(1)} %shard_map.122.refs_0_.near_ids, bf16[64,128,128]{2,1,0:T(8,128)(2,1)S(1)} %bitcast.8, ...), custom_call_target="tpu_custom_call" | custom-call | flops 67108864 | bytes 2454016 | tf_op jit(solution)/shard_map/pallas_call | solution.py:78
  15.6 1.6 %collective-permute-start.4 = (bf16[144,128]{1,0:T(8,128)(2,1)S(1)}, bf16[144,128]{1,0:T(8,128)(2,1)S(1)}, u32[]{:S(2)}, u32[]{:S(2)}) collective-permute-start(bf16[144,128]{1,0:T(8,128)(2,1)S(1)} %get-tuple-element.65), channel_id=1, source_target_pairs={{0,2},{1,3},{2,0},{3,1},{4,6},{5,7},{6,4},{7,5},{8,10},{9,11},{10,... | collective-permute-start | bytes 110600 | tf_op jit(solution)/shard_map/ppermute | solution.py:96
  17.2 0.3 collective-permute-start.5
  17.5 1.9 %collective-permute-done.3.refs_1_ = bf16[144,128]{1,0:T(8,128)(2,1)S(1)} collective-permute-done((bf16[144,128]{1,0:T(8,128)(2,1)S(1)}, bf16[144,128]{1,0:T(8,128)(2,1)S(1)}, u32[]{:S(2)}, u32[]{:S(2)}) %collective-permute-start.3) | collective-permute-done | bytes 36896 | tf_op jit(solution)/shard_map/ppermute | solution.py:96
  19.3 0.4 collective-permute-done.4.refs_2_
  19.8 0.5 collective-permute-start.8
  20.3 3.5 %collective-permute-start.7 = (bf16[144,128]{1,0:T(8,128)(2,1)S(1)}, bf16[144,128]{1,0:T(8,128)(2,1)S(1)}, u32[]{:S(2)}, u32[]{:S(2)}) collective-permute-start(bf16[144,128]{1,0:T(8,128)(2,1)S(1)} %get-tuple-element.72), channel_id=1, source_target_pairs={{0,8},{4,12},{8,0},{12,4},{1,9},{5,13},{9,1},{13,5},{2,10},{6,14},... | collective-permute-start | bytes 110600 | tf_op jit(solution)/shard_map/ppermute | solution.py:96
  23.8 0.5 collective-permute-start.6
  24.3 0.9 shard_map.125
  25.2 1.1 %collective-permute-done.7.refs_7_ = bf16[144,128]{1,0:T(8,128)(2,1)S(1)} collective-permute-done((bf16[144,128]{1,0:T(8,128)(2,1)S(1)}, bf16[144,128]{1,0:T(8,128)(2,1)S(1)}, u32[]{:S(2)}, u32[]{:S(2)}) %collective-permute-start.7) | collective-permute-done | bytes 36896 | tf_op jit(solution)/shard_map/ppermute | solution.py:96
  26.3 3.3 %collective-permute-done.6.refs_6_ = bf16[144,128]{1,0:T(8,128)(2,1)S(1)} collective-permute-done((bf16[144,128]{1,0:T(8,128)(2,1)S(1)}, bf16[144,128]{1,0:T(8,128)(2,1)S(1)}, u32[]{:S(2)}, u32[]{:S(2)}) %collective-permute-start.6) | collective-permute-done | bytes 36896 | tf_op jit(solution)/shard_map/ppermute | solution.py:96
  29.6 2.1 %shard_map.126 = (f32[288,128]{1,0:T(8,128)S(1)}, f32[144,128]{1,0:T(8,128)S(1)}, f32[144,128]{1,0:T(8,128)S(1)}, bf16[9,32,128]{2,1,0:T(8,128)(2,1)S(1)}, f32[1...) custom-call(s32[1,128]{1,0:T(1,128)S(1)} %shard_map.122.refs_0_.near, ...), custom_call_target="tpu_custom_call" | custom-call | flops 67108864 | bytes 3572224 | tf_op jit(solution)/shard_map/pallas_call | solution.py:78
  31.7 1.6 %collective-permute-start.10 = (bf16[144,128]{1,0:T(8,128)(2,1)S(1)}, bf16[144,128]{1,0:T(8,128)(2,1)S(1)}, u32[]{:S(2)}, u32[]{:S(2)}) collective-permute-start(bf16[144,128]{1,0:T(8,128)(2,1)S(1)} %get-tuple-element.76), channel_id=1, source_target_pairs={{0,2},{1,3},{2,0},{3,1},{4,6},{5,7},{6,4},{7,5},{8,10},{9,11},{10,... | collective-permute-start | bytes 110600 | tf_op jit(solution)/shard_map/ppermute | solution.py:96
  33.3 0.3 collective-permute-start.11
  33.6 1.9 %collective-permute-done.9.refs_1_ = bf16[144,128]{1,0:T(8,128)(2,1)S(1)} collective-permute-done((bf16[144,128]{1,0:T(8,128)(2,1)S(1)}, bf16[144,128]{1,0:T(8,128)(2,1)S(1)}, u32[]{:S(2)}, u32[]{:S(2)}) %collective-permute-start.9) | collective-permute-done | bytes 36896 | tf_op jit(solution)/shard_map/ppermute | solution.py:96
  35.4 0.4 collective-permute-done.10.refs_2_
  36.0 1.1 %collective-permute-start.13 = (bf16[144,128]{1,0:T(8,128)(2,1)S(1)}, bf16[144,128]{1,0:T(8,128)(2,1)S(1)}, u32[]{:S(2)}, u32[]{:S(2)}) collective-permute-start(bf16[144,128]{1,0:T(8,128)(2,1)S(1)} %get-tuple-element.80), channel_id=1, source_target_pairs={{0,8},{4,12},{8,0},{12,4},{1,9},{5,13},{9,1},{13,5},{2,10},{6,14},... | collective-permute-start | bytes 110600 | tf_op jit(solution)/shard_map/ppermute | solution.py:96
  37.1 3.3 %collective-permute-start.12 = (bf16[144,128]{1,0:T(8,128)(2,1)S(1)}, bf16[144,128]{1,0:T(8,128)(2,1)S(1)}, u32[]{:S(2)}, u32[]{:S(2)}) collective-permute-start(bf16[144,128]{1,0:T(8,128)(2,1)S(1)} %get-tuple-element.80), channel_id=1, source_target_pairs={{0,12},{4,8},{8,4},{12,0},{1,13},{5,9},{9,5},{13,1},{2,14},{6,10},... | collective-permute-start | bytes 110600 | tf_op jit(solution)/shard_map/ppermute | solution.py:96
  40.4 0.6 collective-permute-done.13.refs_7_
  41.0 1.9 %collective-permute-done.12.refs_6_ = bf16[144,128]{1,0:T(8,128)(2,1)S(1)} collective-permute-done((bf16[144,128]{1,0:T(8,128)(2,1)S(1)}, bf16[144,128]{1,0:T(8,128)(2,1)S(1)}, u32[]{:S(2)}, u32[]{:S(2)}) %collective-permute-start.12) | collective-permute-done | bytes 36896 | tf_op jit(solution)/shard_map/ppermute | solution.py:96
  42.9 2.1 %shard_map.128 = (f32[288,128]{1,0:T(8,128)S(1)}, f32[144,128]{1,0:T(8,128)S(1)}, f32[144,128]{1,0:T(8,128)S(1)}, bf16[9,32,128]{2,1,0:T(8,128)(2,1)S(1)}, f32[1...) custom-call(s32[1,128]{1,0:T(1,128)S(1)} %shard_map.122.refs_0_.near, ...), custom_call_target="tpu_custom_call" | custom-call | flops 67108864 | bytes 3572224 | tf_op jit(solution)/shard_map/pallas_call | solution.py:78
  45.0 1.6 %collective-permute-start.16 = (bf16[144,128]{1,0:T(8,128)(2,1)S(1)}, bf16[144,128]{1,0:T(8,128)(2,1)S(1)}, u32[]{:S(2)}, u32[]{:S(2)}) collective-permute-start(bf16[144,128]{1,0:T(8,128)(2,1)S(1)} %get-tuple-element.84), channel_id=1, source_target_pairs={{0,2},{1,3},{2,0},{3,1},{4,6},{5,7},{6,4},{7,5},{8,10},{9,11},{10,... | collective-permute-start | bytes 110600 | tf_op jit(solution)/shard_map/ppermute | solution.py:96
  46.6 0.3 collective-permute-start.17
  46.9 1.9 %collective-permute-done.15.refs_1_ = bf16[144,128]{1,0:T(8,128)(2,1)S(1)} collective-permute-done((bf16[144,128]{1,0:T(8,128)(2,1)S(1)}, bf16[144,128]{1,0:T(8,128)(2,1)S(1)}, u32[]{:S(2)}, u32[]{:S(2)}) %collective-permute-start.15) | collective-permute-done | bytes 36896 | tf_op jit(solution)/shard_map/ppermute | solution.py:96
  48.7 0.4 collective-permute-done.16.refs_2_
  49.2 0.1 collective-permute-start.18
  49.4 6.1 %collective-permute-done.18.theirs = bf16[224,128]{1,0:T(8,128)(2,1)S(1)} collective-permute-done((bf16[224,128]{1,0:T(8,128)(2,1)S(1)}, bf16[224,128]{1,0:T(8,128)(2,1)S(1)}, u32[]{:S(2)}, u32[]{:S(2)}) %collective-permute-start.18) | collective-permute-done | bytes 57376 | tf_op jit(solution)/shard_map/ppermute | solution.py:96
  55.6 1.2 %collective-permute-start.20 = (bf16[144,128]{1,0:T(8,128)(2,1)S(1)}, bf16[144,128]{1,0:T(8,128)(2,1)S(1)}, u32[]{:S(2)}, u32[]{:S(2)}) collective-permute-start(bf16[144,128]{1,0:T(8,128)(2,1)S(1)} %get-tuple-element.91.refs_3_), channel_id=1, source_target_pairs={{0,2},{1,3},{2,0},{3,1},{4,6},{5,7},{6,4},{7,5},{8,10},{9,11},{10,... | collective-permute-start | bytes 110600 | tf_op jit(solution)/shard_map/ppermute | solution.py:96
  56.8 0.6 collective-permute-start.19
  57.5 2.2 %collective-permute-done.20.refs_5_ = bf16[144,128]{1,0:T(8,128)(2,1)S(1)} collective-permute-done((bf16[144,128]{1,0:T(8,128)(2,1)S(1)}, bf16[144,128]{1,0:T(8,128)(2,1)S(1)}, u32[]{:S(2)}, u32[]{:S(2)}) %collective-permute-start.20) | collective-permute-done | bytes 36896 | tf_op jit(solution)/shard_map/ppermute | solution.py:96
  59.6 0.6 collective-permute-done.19.refs_4_
  60.3 1.5 %shard_map.131 = (bf16[18,32,128]{2,1,0:T(8,128)(2,1)S(1)}, f32[144,128]{1,0:T(8,128)S(1)}, bf16[144,128]{1,0:T(8,128)(2,1)S(1)}, bf16[144,128]{1,0:T(8,128)(2,1)S(1)}, bf16[144,128]{1,0:T(8,128)(2,1)S(1)}) custom-call(s32[1,128]{1,0:T(1,128)S(1)} %shard_map.122.refs_0_.near_ids, bf16[64,128,128]{2,1,0:T(8,128)(2,1)S(1)} %bitcast.11, ...), custom_call_target="tpu_custom_call" | custom-call | flops 67108864 | bytes 2613760 | tf_op jit(solution)/shard_map/pallas_call | solution.py:78
  61.8 2.6 %collective-permute-start.22 = (bf16[144,128]{1,0:T(8,128)(2,1)S(1)}, bf16[144,128]{1,0:T(8,128)(2,1)S(1)}, u32[]{:S(2)}, u32[]{:S(2)}) collective-permute-start(bf16[144,128]{1,0:T(8,128)(2,1)S(1)} %get-tuple-element.97), channel_id=1, source_target_pairs={{0,12},{4,8},{8,4},{12,0},{1,13},{5,9},{9,5},{13,1},{2,14},{6,10},... | collective-permute-start | bytes 110600 | tf_op jit(solution)/shard_map/ppermute | solution.py:96
  64.4 1.9 %collective-permute-start.24 = (bf16[144,128]{1,0:T(8,128)(2,1)S(1)}, bf16[144,128]{1,0:T(8,128)(2,1)S(1)}, u32[]{:S(2)}, u32[]{:S(2)}) collective-permute-start(bf16[144,128]{1,0:T(8,128)(2,1)S(1)} %get-tuple-element.99), channel_id=1, source_target_pairs={{0,4},{4,0},{8,12},{12,8},{1,5},{5,1},{9,13},{13,9},{2,6},{6,2},{1... | collective-permute-start | bytes 110600 | tf_op jit(solution)/shard_map/ppermute | solution.py:96
  66.3 1.4 %collective-permute-done.22.refs_0_ = bf16[144,128]{1,0:T(8,128)(2,1)S(1)} collective-permute-done((bf16[144,128]{1,0:T(8,128)(2,1)S(1)}, bf16[144,128]{1,0:T(8,128)(2,1)S(1)}, u32[]{:S(2)}, u32[]{:S(2)}) %collective-permute-start.22) | collective-permute-done | bytes 36896 | tf_op jit(solution)/shard_map/ppermute | solution.py:96
  67.6 1.6 %collective-permute-done.23.refs_1_ = bf16[144,128]{1,0:T(8,128)(2,1)S(1)} collective-permute-done((bf16[144,128]{1,0:T(8,128)(2,1)S(1)}, bf16[144,128]{1,0:T(8,128)(2,1)S(1)}, u32[]{:S(2)}, u32[]{:S(2)}) %collective-permute-start.23) | collective-permute-done | bytes 36896 | tf_op jit(solution)/shard_map/ppermute | solution.py:96
  69.4 0.9 %collective-permute-start.26 = (bf16[144,128]{1,0:T(8,128)(2,1)S(1)}, bf16[144,128]{1,0:T(8,128)(2,1)S(1)}, u32[]{:S(2)}, u32[]{:S(2)}) collective-permute-start(bf16[144,128]{1,0:T(8,128)(2,1)S(1)} %get-tuple-element.101.refs_3_), channel_id=1, source_target_pairs={{0,2},{1,3},{2,0},{3,1},{4,6},{5,7},{6,4},{7,5},{8,10},{9,11},{10,... | collective-permute-start | bytes 110600 | tf_op jit(solution)/shard_map/ppermute | solution.py:96
  70.3 0.9 collective-permute-start.25
  71.2 2.2 %collective-permute-done.26.refs_5_ = bf16[144,128]{1,0:T(8,128)(2,1)S(1)} collective-permute-done((bf16[144,128]{1,0:T(8,128)(2,1)S(1)}, bf16[144,128]{1,0:T(8,128)(2,1)S(1)}, u32[]{:S(2)}, u32[]{:S(2)}) %collective-permute-start.26) | collective-permute-done | bytes 36896 | tf_op jit(solution)/shard_map/ppermute | solution.py:96
  73.5 0.4 collective-permute-done.25.refs_4_
  73.9 1.5 %shard_map.133 = (bf16[18,32,128]{2,1,0:T(8,128)(2,1)S(1)}, f32[144,128]{1,0:T(8,128)S(1)}, bf16[144,128]{1,0:T(8,128)(2,1)S(1)}, bf16[144,128]{1,0:T(8,128)(2,1)S(1)}, bf16[144,128]{1,0:T(8,128)(2,1)S(1)}) custom-call(s32[1,128]{1,0:T(1,128)S(1)} %shard_map.122.refs_0_.near_ids, bf16[64,128,128]{2,1,0:T(8,128)(2,1)S(1)} %bitcast.12, ...), custom_call_target="tpu_custom_call" | custom-call | flops 67108864 | bytes 2613760 | tf_op jit(solution)/shard_map/pallas_call | solution.py:78
  75.4 2.2 %collective-permute-start.28 = (bf16[144,128]{1,0:T(8,128)(2,1)S(1)}, bf16[144,128]{1,0:T(8,128)(2,1)S(1)}, u32[]{:S(2)}, u32[]{:S(2)}) collective-permute-start(bf16[144,128]{1,0:T(8,128)(2,1)S(1)} %get-tuple-element.112), channel_id=1, source_target_pairs={{0,12},{4,8},{8,4},{12,0},{1,13},{5,9},{9,5},{13,1},{2,14},{6,10},... | collective-permute-start | bytes 110600 | tf_op jit(solution)/shard_map/ppermute | solution.py:96
  77.6 0.3 collective-permute-start.29
  78.0 1.9 %collective-permute-start.30 = (bf16[144,128]{1,0:T(8,128)(2,1)S(1)}, bf16[144,128]{1,0:T(8,128)(2,1)S(1)}, u32[]{:S(2)}, u32[]{:S(2)}) collective-permute-start(bf16[144,128]{1,0:T(8,128)(2,1)S(1)} %get-tuple-element.114), channel_id=1, source_target_pairs={{0,4},{4,0},{8,12},{12,8},{1,5},{5,1},{9,13},{13,9},{2,6},{6,2},{1... | collective-permute-start | bytes 110600 | tf_op jit(solution)/shard_map/ppermute | solution.py:96
  79.9 1.9 %collective-permute-done.28.refs_0_ = bf16[144,128]{1,0:T(8,128)(2,1)S(1)} collective-permute-done((bf16[144,128]{1,0:T(8,128)(2,1)S(1)}, bf16[144,128]{1,0:T(8,128)(2,1)S(1)}, u32[]{:S(2)}, u32[]{:S(2)}) %collective-permute-start.28) | collective-permute-done | bytes 36896 | tf_op jit(solution)/shard_map/ppermute | solution.py:96
  81.8 1.1 %collective-permute-done.29.refs_1_ = bf16[144,128]{1,0:T(8,128)(2,1)S(1)} collective-permute-done((bf16[144,128]{1,0:T(8,128)(2,1)S(1)}, bf16[144,128]{1,0:T(8,128)(2,1)S(1)}, u32[]{:S(2)}, u32[]{:S(2)}) %collective-permute-start.29) | collective-permute-done | bytes 36896 | tf_op jit(solution)/shard_map/ppermute | solution.py:96
  83.0 1.1 %collective-permute-start.32 = (bf16[176,128]{1,0:T(8,128)(2,1)S(1)}, bf16[176,128]{1,0:T(8,128)(2,1)S(1)}, u32[]{:S(2)}, u32[]{:S(2)}) collective-permute-start(bf16[176,128]{1,0:T(8,128)(2,1)S(1)} %shard_map.135.refs_3_.refs_1_), channel_id=1, source_target_pairs={{0,2},{1,3},{2,0},{3,1},{4,6},{5,7},{6,4},{7,5},{8,10},{9,11},{10,... | collective-permute-start | bytes 135176 | tf_op jit(solution)/shard_map/ppermute | solution.py:96
  84.1 0.8 collective-permute-start.31
  84.9 0.8 shard_map.134
  85.7 1.6 %collective-permute-done.32.refs_5_.refs_3_ = bf16[176,128]{1,0:T(8,128)(2,1)S(1)} collective-permute-done((bf16[176,128]{1,0:T(8,128)(2,1)S(1)}, bf16[176,128]{1,0:T(8,128)(2,1)S(1)}, u32[]{:S(2)}, u32[]{:S(2)}) %collective-permute-start.32) | collective-permute-done | bytes 45088 | tf_op jit(solution)/shard_map/ppermute | solution.py:96
  87.3 0.5 collective-permute-done.31.refs_4_.refs_2_
  87.8 0.6 shard_map.137.table
  88.4 1.1 %collective-permute-start.34 = (f32[64,128]{1,0:T(8,128)S(1)}, f32[64,128]{1,0:T(8,128)S(1)}, u32[]{:S(2)}, u32[]{:S(2)}) collective-permute-start(f32[64,128]{1,0:T(8,128)S(1)} %shard_map.137.table), channel_id=1, source_target_pairs={{0,4},{4,0},{8,12},{12,8},{1,5},{5,1},{9,13},{13,9},{2,6},{6,2},{1... | collective-permute-start | bytes 98312 | tf_op jit(solution)/shard_map/ppermute | solution.py:96
  89.5 2.9 %shard_map.136 = (bf16[18,128,128]{2,1,0:T(8,128)(2,1)S(1)}, bf16[64,128,128]{2,1,0:T(8,128)(2,1)}) custom-call(s32[1,128]{1,0:T(1,128)S(1)} %shard_map.122.refs_0_.near_ids, bf16[9,128,128]{2,1,0:T(8,128)(2,1)S(1)} %get-tuple-element.106.refs_1_.refs_0_.right, bf16[18,128,128]{2,1,0:T(8,128)(2,1)S(1)} %get-tuple-element.107.refs_2_, ...), custom_call_target="tpu_custom_call" | custom-call | flops 268435456 | bytes 4194304 | tf_op jit(solution)/shard_map/pallas_call | solution.py:629
  92.4 1.6 %shard_map.138 = (bf16[64,128,128]{2,1,0:T(8,128)(2,1)}, f32[64,128]{1,0:T(8,128)}) custom-call(s32[1,128]{1,0:T(1,128)S(1)} %shard_map.122.refs_0_.near_ids, bf16[18,128,128]{2,1,0:T(8,128)(2,1)S(1)} %get-tuple-element.115.left, bf16[9,128,128]{2,1,0:T(8,128)(2,1)S(1)} %get-tuple-element.106.refs_1_.refs_0_.right, ...), custom_call_target="tpu_custom_call", output_to_operand_aliasing={{0}: (5, {})} | custom-call | flops 268435456 | bytes 4194304 | tf_op jit(solution)/shard_map/pallas_call | solution.py:640
  (44 shorter events, 1.0 us)
Async XLA Ops:
  1.4 0.8 copy-start.4
  2.3 9.3 %collective-permute-start.2 = (bf16[96,128]{1,0:T(8,128)(2,1)S(1)}, bf16[96,128]{1,0:T(8,128)(2,1)S(1)}, u32[]{:S(2)}, u32[]{:S(2)}) collective-permute-start(bf16[96,128]{1,0:T(8,128)(2,1)S(1)} %get-tuple-element.61.after.refs_2_.refs_0_.mine), channel_id=1, source_target_pairs={{0,4},{4,0},{8,12},{12,8},{1,5},{5,1},{9,13},{13,9},{2,6},{6,2},{1... | collective-permute-start | bytes 73736 | tf_op jit(solution)/shard_map/ppermute | solution.py:96
  5.3 6.2 %collective-permute-start.1 = (bf16[96,128]{1,0:T(8,128)(2,1)S(1)}, bf16[96,128]{1,0:T(8,128)(2,1)S(1)}, u32[]{:S(2)}, u32[]{:S(2)}) collective-permute-start(bf16[96,128]{1,0:T(8,128)(2,1)S(1)} %get-tuple-element.61.after.refs_2_.refs_0_.mine), channel_id=1, source_target_pairs={{0,8},{4,12},{8,0},{12,4},{1,9},{5,13},{9,1},{13,5},{2,10},{6,14},... | collective-permute-start | bytes 73736 | tf_op jit(solution)/shard_map/ppermute | solution.py:96
  7.9 5.6 %collective-permute-start = (bf16[96,128]{1,0:T(8,128)(2,1)S(1)}, bf16[96,128]{1,0:T(8,128)(2,1)S(1)}, u32[]{:S(2)}, u32[]{:S(2)}) collective-permute-start(bf16[96,128]{1,0:T(8,128)(2,1)S(1)} %get-tuple-element.61.after.refs_2_.refs_0_.mine), channel_id=1, source_target_pairs={{0,12},{4,8},{8,4},{12,0},{1,13},{5,9},{9,5},{13,1},{2,14},{6,10},... | collective-permute-start | bytes 73736 | tf_op jit(solution)/shard_map/ppermute | solution.py:96
  7.9 1.6 %copy-start = (bf16[1,1,64,128,128]{4,3,2,1,0:T(8,128)(2,1)S(1)}, bf16[1,1,64,128,128]{4,3,2,1,0:T(8,128)(2,1)}, u32[]{:S(2)}) copy-start(bf16[1,1,64,128,128]{4,3,2,1,0:T(8,128)(2,1)} %param.13) | copy-start | bytes 6291460
  9.5 0.7 copy-start.6
  10.2 0.7 copy-start.7
  10.8 0.7 copy-start.8
  11.5 2.1 %copy-start.1 = (bf16[1,1,64,128,128]{4,3,2,1,0:T(8,128)(2,1)S(1)}, bf16[1,1,64,128,128]{4,3,2,1,0:T(8,128)(2,1)}, u32[]{:S(2)}) copy-start(bf16[1,1,64,128,128]{4,3,2,1,0:T(8,128)(2,1)} %param.13) | copy-start | bytes 6291460
  11.5 12.8 %copy-start.2 = (f32[3,32,288]{2,1,0:T(8,128)S(1)}, f32[3,32,288]{2,1,0:T(8,128)}, u32[]{:S(2)}) copy-start(f32[3,32,288]{2,1,0:T(8,128)} %refs_2_.1) | copy-start | bytes 331780
  11.5 12.8 %copy-start.3 = (bf16[3,32,512]{2,1,0:T(8,128)(2,1)S(1)}, bf16[3,32,512]{2,1,0:T(8,128)(2,1)}, u32[]{:S(2)}) copy-start(bf16[3,32,512]{2,1,0:T(8,128)(2,1)} %param.11) | copy-start | bytes 294916
  11.5 12.8 %copy-start.5 = (f32[8192]{0:T(1024)S(1)}, f32[8192]{0:T(1024)}, u32[]{:S(2)}) copy-start(f32[8192]{0:T(1024)} %param.18) | copy-start | bytes 98308
  15.5 3.8 %collective-permute-start.3 = (bf16[144,128]{1,0:T(8,128)(2,1)S(1)}, bf16[144,128]{1,0:T(8,128)(2,1)S(1)}, u32[]{:S(2)}, u32[]{:S(2)}) collective-permute-start(bf16[144,128]{1,0:T(8,128)(2,1)S(1)} %get-tuple-element.64), channel_id=1, source_target_pairs={{0,3},{1,2},{2,1},{3,0},{4,7},{5,6},{6,5},{7,4},{8,11},{9,10},{10,... | collective-permute-start | bytes 110600 | tf_op jit(solution)/shard_map/ppermute | solution.py:96
  15.6 4.2 %collective-permute-start.4 = (bf16[144,128]{1,0:T(8,128)(2,1)S(1)}, bf16[144,128]{1,0:T(8,128)(2,1)S(1)}, u32[]{:S(2)}, u32[]{:S(2)}) collective-permute-start(bf16[144,128]{1,0:T(8,128)(2,1)S(1)} %get-tuple-element.65), channel_id=1, source_target_pairs={{0,2},{1,3},{2,0},{3,1},{4,6},{5,7},{6,4},{7,5},{8,10},{9,11},{10,... | collective-permute-start | bytes 110600 | tf_op jit(solution)/shard_map/ppermute | solution.py:96
  17.2 2.6 %collective-permute-start.5 = (bf16[144,128]{1,0:T(8,128)(2,1)S(1)}, bf16[144,128]{1,0:T(8,128)(2,1)S(1)}, u32[]{:S(2)}, u32[]{:S(2)}) collective-permute-start(bf16[144,128]{1,0:T(8,128)(2,1)S(1)} %get-tuple-element.66), channel_id=1, source_target_pairs={{0,1},{1,0},{2,3},{3,2},{4,5},{5,4},{6,7},{7,6},{8,9},{9,8},{10,11... | collective-permute-start | bytes 110600 | tf_op jit(solution)/shard_map/ppermute | solution.py:96
  19.8 5.4 %collective-permute-start.8 = (bf16[144,128]{1,0:T(8,128)(2,1)S(1)}, bf16[144,128]{1,0:T(8,128)(2,1)S(1)}, u32[]{:S(2)}, u32[]{:S(2)}) collective-permute-start(bf16[144,128]{1,0:T(8,128)(2,1)S(1)} %get-tuple-element.72), channel_id=1, source_target_pairs={{0,4},{4,0},{8,12},{12,8},{1,5},{5,1},{9,13},{13,9},{2,6},{6,2},{1... | collective-permute-start | bytes 110600 | tf_op jit(solution)/shard_map/ppermute | solution.py:96
  20.3 6.0 %collective-permute-start.7 = (bf16[144,128]{1,0:T(8,128)(2,1)S(1)}, bf16[144,128]{1,0:T(8,128)(2,1)S(1)}, u32[]{:S(2)}, u32[]{:S(2)}) collective-permute-start(bf16[144,128]{1,0:T(8,128)(2,1)S(1)} %get-tuple-element.72), channel_id=1, source_target_pairs={{0,8},{4,12},{8,0},{12,4},{1,9},{5,13},{9,1},{13,5},{2,10},{6,14},... | collective-permute-start | bytes 110600 | tf_op jit(solution)/shard_map/ppermute | solution.py:96
  23.8 5.8 %collective-permute-start.6 = (bf16[144,128]{1,0:T(8,128)(2,1)S(1)}, bf16[144,128]{1,0:T(8,128)(2,1)S(1)}, u32[]{:S(2)}, u32[]{:S(2)}) collective-permute-start(bf16[144,128]{1,0:T(8,128)(2,1)S(1)} %get-tuple-element.72), channel_id=1, source_target_pairs={{0,12},{4,8},{8,4},{12,0},{1,13},{5,9},{9,5},{13,1},{2,14},{6,10},... | collective-permute-start | bytes 110600 | tf_op jit(solution)/shard_map/ppermute | solution.py:96
  31.6 3.8 %collective-permute-start.9 = (bf16[144,128]{1,0:T(8,128)(2,1)S(1)}, bf16[144,128]{1,0:T(8,128)(2,1)S(1)}, u32[]{:S(2)}, u32[]{:S(2)}) collective-permute-start(bf16[144,128]{1,0:T(8,128)(2,1)S(1)} %get-tuple-element.75), channel_id=1, source_target_pairs={{0,3},{1,2},{2,1},{3,0},{4,7},{5,6},{6,5},{7,4},{8,11},{9,10},{10,... | collective-permute-start | bytes 110600 | tf_op jit(solution)/shard_map/ppermute | solution.py:96
  31.7 4.2 %collective-permute-start.10 = (bf16[144,128]{1,0:T(8,128)(2,1)S(1)}, bf16[144,128]{1,0:T(8,128)(2,1)S(1)}, u32[]{:S(2)}, u32[]{:S(2)}) collective-permute-start(bf16[144,128]{1,0:T(8,128)(2,1)S(1)} %get-tuple-element.76), channel_id=1, source_target_pairs={{0,2},{1,3},{2,0},{3,1},{4,6},{5,7},{6,4},{7,5},{8,10},{9,11},{10,... | collective-permute-start | bytes 110600 | tf_op jit(solution)/shard_map/ppermute | solution.py:96
  33.3 2.6 %collective-permute-start.11 = (bf16[144,128]{1,0:T(8,128)(2,1)S(1)}, bf16[144,128]{1,0:T(8,128)(2,1)S(1)}, u32[]{:S(2)}, u32[]{:S(2)}) collective-permute-start(bf16[144,128]{1,0:T(8,128)(2,1)S(1)} %get-tuple-element.77), channel_id=1, source_target_pairs={{0,1},{1,0},{2,3},{3,2},{4,5},{5,4},{6,7},{7,6},{8,9},{9,8},{10,11... | collective-permute-start | bytes 110600 | tf_op jit(solution)/shard_map/ppermute | solution.py:96
  35.9 4.5 %collective-permute-start.14 = (bf16[144,128]{1,0:T(8,128)(2,1)S(1)}, bf16[144,128]{1,0:T(8,128)(2,1)S(1)}, u32[]{:S(2)}, u32[]{:S(2)}) collective-permute-start(bf16[144,128]{1,0:T(8,128)(2,1)S(1)} %get-tuple-element.80), channel_id=1, source_target_pairs={{0,4},{4,0},{8,12},{12,8},{1,5},{5,1},{9,13},{13,9},{2,6},{6,2},{1... | collective-permute-start | bytes 110600 | tf_op jit(solution)/shard_map/ppermute | solution.py:96
  36.0 5.0 %collective-permute-start.13 = (bf16[144,128]{1,0:T(8,128)(2,1)S(1)}, bf16[144,128]{1,0:T(8,128)(2,1)S(1)}, u32[]{:S(2)}, u32[]{:S(2)}) collective-permute-start(bf16[144,128]{1,0:T(8,128)(2,1)S(1)} %get-tuple-element.80), channel_id=1, source_target_pairs={{0,8},{4,12},{8,0},{12,4},{1,9},{5,13},{9,1},{13,5},{2,10},{6,14},... | collective-permute-start | bytes 110600 | tf_op jit(solution)/shard_map/ppermute | solution.py:96
  37.1 5.8 %collective-permute-start.12 = (bf16[144,128]{1,0:T(8,128)(2,1)S(1)}, bf16[144,128]{1,0:T(8,128)(2,1)S(1)}, u32[]{:S(2)}, u32[]{:S(2)}) collective-permute-start(bf16[144,128]{1,0:T(8,128)(2,1)S(1)} %get-tuple-element.80), channel_id=1, source_target_pairs={{0,12},{4,8},{8,4},{12,0},{1,13},{5,9},{9,5},{13,1},{2,14},{6,10},... | collective-permute-start | bytes 110600 | tf_op jit(solution)/shard_map/ppermute | solution.py:96
  45.0 3.8 %collective-permute-start.15 = (bf16[144,128]{1,0:T(8,128)(2,1)S(1)}, bf16[144,128]{1,0:T(8,128)(2,1)S(1)}, u32[]{:S(2)}, u32[]{:S(2)}) collective-permute-start(bf16[144,128]{1,0:T(8,128)(2,1)S(1)} %get-tuple-element.83), channel_id=1, source_target_pairs={{0,3},{1,2},{2,1},{3,0},{4,7},{5,6},{6,5},{7,4},{8,11},{9,10},{10,... | collective-permute-start | bytes 110600 | tf_op jit(solution)/shard_map/ppermute | solution.py:96
  45.0 4.2 %collective-permute-start.16 = (bf16[144,128]{1,0:T(8,128)(2,1)S(1)}, bf16[144,128]{1,0:T(8,128)(2,1)S(1)}, u32[]{:S(2)}, u32[]{:S(2)}) collective-permute-start(bf16[144,128]{1,0:T(8,128)(2,1)S(1)} %get-tuple-element.84), channel_id=1, source_target_pairs={{0,2},{1,3},{2,0},{3,1},{4,6},{5,7},{6,4},{7,5},{8,10},{9,11},{10,... | collective-permute-start | bytes 110600 | tf_op jit(solution)/shard_map/ppermute | solution.py:96
  46.6 2.6 %collective-permute-start.17 = (bf16[144,128]{1,0:T(8,128)(2,1)S(1)}, bf16[144,128]{1,0:T(8,128)(2,1)S(1)}, u32[]{:S(2)}, u32[]{:S(2)}) collective-permute-start(bf16[144,128]{1,0:T(8,128)(2,1)S(1)} %get-tuple-element.85), channel_id=1, source_target_pairs={{0,1},{1,0},{2,3},{3,2},{4,5},{5,4},{6,7},{7,6},{8,9},{9,8},{10,11... | collective-permute-start | bytes 110600 | tf_op jit(solution)/shard_map/ppermute | solution.py:96
  49.2 6.3 %collective-permute-start.18 = (bf16[224,128]{1,0:T(8,128)(2,1)S(1)}, bf16[224,128]{1,0:T(8,128)(2,1)S(1)}, u32[]{:S(2)}, u32[]{:S(2)}) collective-permute-start(bf16[224,128]{1,0:T(8,128)(2,1)S(1)} %get-tuple-element.88), channel_id=1, source_target_pairs={{0,8},{4,12},{8,0},{12,4},{1,9},{5,13},{9,1},{13,5},{2,10},{6,14},... | collective-permute-start | bytes 172040 | tf_op jit(solution)/shard_map/ppermute | solution.py:96
  55.5 1.9 %collective-permute-start.21 = (bf16[144,128]{1,0:T(8,128)(2,1)S(1)}, bf16[144,128]{1,0:T(8,128)(2,1)S(1)}, u32[]{:S(2)}, u32[]{:S(2)}) collective-permute-start(bf16[144,128]{1,0:T(8,128)(2,1)S(1)} %get-tuple-element.91.refs_3_), channel_id=1, source_target_pairs={{0,1},{1,0},{2,3},{3,2},{4,5},{5,4},{6,7},{7,6},{8,9},{9,8},{10,11... | collective-permute-start | bytes 110600 | tf_op jit(solution)/shard_map/ppermute | solution.py:96
  55.6 4.0 %collective-permute-start.20 = (bf16[144,128]{1,0:T(8,128)(2,1)S(1)}, bf16[144,128]{1,0:T(8,128)(2,1)S(1)}, u32[]{:S(2)}, u32[]{:S(2)}) collective-permute-start(bf16[144,128]{1,0:T(8,128)(2,1)S(1)} %get-tuple-element.91.refs_3_), channel_id=1, source_target_pairs={{0,2},{1,3},{2,0},{3,1},{4,6},{5,7},{6,4},{7,5},{8,10},{9,11},{10,... | collective-permute-start | bytes 110600 | tf_op jit(solution)/shard_map/ppermute | solution.py:96
  56.8 3.4 %collective-permute-start.19 = (bf16[144,128]{1,0:T(8,128)(2,1)S(1)}, bf16[144,128]{1,0:T(8,128)(2,1)S(1)}, u32[]{:S(2)}, u32[]{:S(2)}) collective-permute-start(bf16[144,128]{1,0:T(8,128)(2,1)S(1)} %get-tuple-element.91.refs_3_), channel_id=1, source_target_pairs={{0,3},{1,2},{2,1},{3,0},{4,7},{5,6},{6,5},{7,4},{8,11},{9,10},{10,... | collective-permute-start | bytes 110600 | tf_op jit(solution)/shard_map/ppermute | solution.py:96
  61.8 5.8 %collective-permute-start.22 = (bf16[144,128]{1,0:T(8,128)(2,1)S(1)}, bf16[144,128]{1,0:T(8,128)(2,1)S(1)}, u32[]{:S(2)}, u32[]{:S(2)}) collective-permute-start(bf16[144,128]{1,0:T(8,128)(2,1)S(1)} %get-tuple-element.97), channel_id=1, source_target_pairs={{0,12},{4,8},{8,4},{12,0},{1,13},{5,9},{9,5},{13,1},{2,14},{6,10},... | collective-permute-start | bytes 110600 | tf_op jit(solution)/shard_map/ppermute | solution.py:96
  64.4 4.9 %collective-permute-start.23 = (bf16[144,128]{1,0:T(8,128)(2,1)S(1)}, bf16[144,128]{1,0:T(8,128)(2,1)S(1)}, u32[]{:S(2)}, u32[]{:S(2)}) collective-permute-start(bf16[144,128]{1,0:T(8,128)(2,1)S(1)} %get-tuple-element.98), channel_id=1, source_target_pairs={{0,8},{4,12},{8,0},{12,4},{1,9},{5,13},{9,1},{13,5},{2,10},{6,14},... | collective-permute-start | bytes 110600 | tf_op jit(solution)/shard_map/ppermute | solution.py:96
  64.4 4.9 %collective-permute-start.24 = (bf16[144,128]{1,0:T(8,128)(2,1)S(1)}, bf16[144,128]{1,0:T(8,128)(2,1)S(1)}, u32[]{:S(2)}, u32[]{:S(2)}) collective-permute-start(bf16[144,128]{1,0:T(8,128)(2,1)S(1)} %get-tuple-element.99), channel_id=1, source_target_pairs={{0,4},{4,0},{8,12},{12,8},{1,5},{5,1},{9,13},{13,9},{2,6},{6,2},{1... | collective-permute-start | bytes 110600 | tf_op jit(solution)/shard_map/ppermute | solution.py:96
  69.3 1.9 %collective-permute-start.27 = (bf16[144,128]{1,0:T(8,128)(2,1)S(1)}, bf16[144,128]{1,0:T(8,128)(2,1)S(1)}, u32[]{:S(2)}, u32[]{:S(2)}) collective-permute-start(bf16[144,128]{1,0:T(8,128)(2,1)S(1)} %get-tuple-element.101.refs_3_), channel_id=1, source_target_pairs={{0,1},{1,0},{2,3},{3,2},{4,5},{5,4},{6,7},{7,6},{8,9},{9,8},{10,11... | collective-permute-start | bytes 110600 | tf_op jit(solution)/shard_map/ppermute | solution.py:96
  69.4 4.1 %collective-permute-start.26 = (bf16[144,128]{1,0:T(8,128)(2,1)S(1)}, bf16[144,128]{1,0:T(8,128)(2,1)S(1)}, u32[]{:S(2)}, u32[]{:S(2)}) collective-permute-start(bf16[144,128]{1,0:T(8,128)(2,1)S(1)} %get-tuple-element.101.refs_3_), channel_id=1, source_target_pairs={{0,2},{1,3},{2,0},{3,1},{4,6},{5,7},{6,4},{7,5},{8,10},{9,11},{10,... | collective-permute-start | bytes 110600 | tf_op jit(solution)/shard_map/ppermute | solution.py:96
  70.3 3.6 %collective-permute-start.25 = (bf16[144,128]{1,0:T(8,128)(2,1)S(1)}, bf16[144,128]{1,0:T(8,128)(2,1)S(1)}, u32[]{:S(2)}, u32[]{:S(2)}) collective-permute-start(bf16[144,128]{1,0:T(8,128)(2,1)S(1)} %get-tuple-element.101.refs_3_), channel_id=1, source_target_pairs={{0,3},{1,2},{2,1},{3,0},{4,7},{5,6},{6,5},{7,4},{8,11},{9,10},{10,... | collective-permute-start | bytes 110600 | tf_op jit(solution)/shard_map/ppermute | solution.py:96
  75.4 6.3 %collective-permute-start.28 = (bf16[144,128]{1,0:T(8,128)(2,1)S(1)}, bf16[144,128]{1,0:T(8,128)(2,1)S(1)}, u32[]{:S(2)}, u32[]{:S(2)}) collective-permute-start(bf16[144,128]{1,0:T(8,128)(2,1)S(1)} %get-tuple-element.112), channel_id=1, source_target_pairs={{0,12},{4,8},{8,4},{12,0},{1,13},{5,9},{9,5},{13,1},{2,14},{6,10},... | collective-permute-start | bytes 110600 | tf_op jit(solution)/shard_map/ppermute | solution.py:96
  77.6 5.2 %collective-permute-start.29 = (bf16[144,128]{1,0:T(8,128)(2,1)S(1)}, bf16[144,128]{1,0:T(8,128)(2,1)S(1)}, u32[]{:S(2)}, u32[]{:S(2)}) collective-permute-start(bf16[144,128]{1,0:T(8,128)(2,1)S(1)} %get-tuple-element.113), channel_id=1, source_target_pairs={{0,8},{4,12},{8,0},{12,4},{1,9},{5,13},{9,1},{13,5},{2,10},{6,14},... | collective-permute-start | bytes 110600 | tf_op jit(solution)/shard_map/ppermute | solution.py:96
  78.0 4.8 %collective-permute-start.30 = (bf16[144,128]{1,0:T(8,128)(2,1)S(1)}, bf16[144,128]{1,0:T(8,128)(2,1)S(1)}, u32[]{:S(2)}, u32[]{:S(2)}) collective-permute-start(bf16[144,128]{1,0:T(8,128)(2,1)S(1)} %get-tuple-element.114), channel_id=1, source_target_pairs={{0,4},{4,0},{8,12},{12,8},{1,5},{5,1},{9,13},{13,9},{2,6},{6,2},{1... | collective-permute-start | bytes 110600 | tf_op jit(solution)/shard_map/ppermute | solution.py:96
  82.9 2.8 %collective-permute-start.33 = (bf16[176,128]{1,0:T(8,128)(2,1)S(1)}, bf16[176,128]{1,0:T(8,128)(2,1)S(1)}, u32[]{:S(2)}, u32[]{:S(2)}) collective-permute-start(bf16[176,128]{1,0:T(8,128)(2,1)S(1)} %shard_map.135.refs_3_.refs_1_), channel_id=1, source_target_pairs={{0,1},{1,0},{2,3},{3,2},{4,5},{5,4},{6,7},{7,6},{8,9},{9,8},{10,11... | collective-permute-start | bytes 135176 | tf_op jit(solution)/shard_map/ppermute | solution.py:96
  83.0 4.3 %collective-permute-start.32 = (bf16[176,128]{1,0:T(8,128)(2,1)S(1)}, bf16[176,128]{1,0:T(8,128)(2,1)S(1)}, u32[]{:S(2)}, u32[]{:S(2)}) collective-permute-start(bf16[176,128]{1,0:T(8,128)(2,1)S(1)} %shard_map.135.refs_3_.refs_1_), channel_id=1, source_target_pairs={{0,2},{1,3},{2,0},{3,1},{4,6},{5,7},{6,4},{7,5},{8,10},{9,11},{10,... | collective-permute-start | bytes 135176 | tf_op jit(solution)/shard_map/ppermute | solution.py:96
  84.1 3.7 %collective-permute-start.31 = (bf16[176,128]{1,0:T(8,128)(2,1)S(1)}, bf16[176,128]{1,0:T(8,128)(2,1)S(1)}, u32[]{:S(2)}, u32[]{:S(2)}) collective-permute-start(bf16[176,128]{1,0:T(8,128)(2,1)S(1)} %shard_map.135.refs_3_.refs_1_), channel_id=1, source_target_pairs={{0,3},{1,2},{2,1},{3,0},{4,7},{5,6},{6,5},{7,4},{8,11},{9,10},{10,... | collective-permute-start | bytes 135176 | tf_op jit(solution)/shard_map/ppermute | solution.py:96
  88.4 4.0 %collective-permute-start.34 = (f32[64,128]{1,0:T(8,128)S(1)}, f32[64,128]{1,0:T(8,128)S(1)}, u32[]{:S(2)}, u32[]{:S(2)}) collective-permute-start(f32[64,128]{1,0:T(8,128)S(1)} %shard_map.137.table), channel_id=1, source_target_pairs={{0,4},{4,0},{8,12},{12,8},{1,5},{5,1},{9,13},{13,9},{2,6},{6,2},{1... | collective-permute-start | bytes 98312 | tf_op jit(solution)/shard_map/ppermute | solution.py:96

commit v6 on v5

--- a/solution.py
+++ b/solution.py
@@ -30,7 +30,7 @@
         offsets = [local * i % BLOCK for i in range(max(row_count, col_count))]
         self.frame = (max(offsets) + local + BLOCK - 1) // BLOCK
         self.wide = self.frame * BLOCK
-        assert BLOCK % self.rest == 0 and batch % (8 * self.groups) == 0
+        assert 2 * slots == BLOCK and BLOCK % self.rest == 0 and batch % (8 * self.groups) == 0
         assert self.frame == self.full + 1 and self.pair % 16 == 0
 
     def first(self, i):
@@ -132,12 +132,17 @@
     lax.fori_loop(0, count, lambda i, c: (body(i), c)[1], 0, unroll=count <= 18)
 
 
-def start_kernel(z, rates, numbers, message, own, pad):
+def start_kernel(z, rates, numbers, message, own, ids, pad):
     pad[...] = jnp.zeros_like(pad)
     pad[:, 0 : z.local] = rates[...]
     packed = z.pack(pad[...])
     own[...] = packed
     number = numbers[...]
+    at = 2 * z.frame
+    lists = [number[at + r : at + r + 1] for r in range(3)]
+    pre_lanes = pltpu.roll(lists[2], z.slots, 1)
+    lanes = lax.broadcasted_iota(jnp.int32, (1, BLOCK), 1)
+    ids[...] = jnp.where(lanes < z.slots, lists[0] * z.post + lists[1], pre_lanes)
     high = (lax.shift_right_arithmetic(number, 7) + 1).astype(F32)
     low = (number & 127).astype(F32)
     blocks = []
@@ -149,9 +154,13 @@
     message[...] = jnp.concatenate([packed, extra], axis=0).astype(BF16)
 
 
-def list_kernel(z, after, owner, post, pre, weights, ids):
-    del after, weights
-    ids[...] = jnp.concatenate([owner[0] * z.post + post[0], pre[0]], axis=1)
+def turn_weights_kernel(z, after, weights, out):
+    del after
+
+    def one(s):
+        out[s] = jnp.transpose(weights[s])
+
+    lax.fori_loop(0, z.slots, lambda i, c: (one(i), c)[1], 0, unroll=8)
 
 
 def prepare_kernel(z, count, *refs):
@@ -197,9 +206,7 @@
 def multiply_forward(z, c, ids, weights, x, total, own, parts):
     total[...] = jnp.zeros_like(total)
     for s in range(z.slots):
-        total[ids[0, s]] += lax.dot_general(
-            x[ids[0, z.slots + s]], weights[s], (((1,), (1,)), ((), ())), preferred_element_type=F32
-        )
+        total[ids[0, s]] += jnp.dot(x[ids[0, z.slots + s]], weights[s], preferred_element_type=F32)
     for k in range(z.cols):
         both = jnp.concatenate(
             [z.take_blocks(total, 0, c ^ k), z.take_blocks(total, z.post, c ^ k)], axis=0
@@ -375,19 +382,25 @@
     message[...] = jnp.concatenate(rows, axis=0).astype(BF16)
 
 
-def table_kernel(z, count, *refs):
-    mine, got, out = refs[1], refs[2:-1], refs[-1]
+def extras_kernel(z, count, right, mine, *refs):
+    del right
+    got, out = refs[:-1], refs[-1]
     _, c = place()
+    for k in range(z.cols):
+        ref = mine if k == 0 else away(got, z.cols, c, k)
+        out[2 * CODES * k : 2 * CODES * (k + 1)] = ref[z.pair :]
+
+
+def add_table(z, extras, out):
     highs = z.types // BLOCK
     high_ids = lax.broadcasted_iota(jnp.int32, (highs, BLOCK), 0).astype(F32) + 1.0
     low_ids = lax.broadcasted_iota(jnp.int32, (BLOCK, BLOCK), 0).astype(F32)
     total = jnp.zeros((3 * highs, BLOCK), F32)
-    for k in range(z.cols):
-        ref = mine if k == 0 else away(got, z.cols, c, k)
-        extra = ref[z.pair :].astype(F32)
-        for side in range(2):
+    for ref in extras:
+        for side in range(2 * z.cols):
+            extra = ref[side * CODES : (side + 1) * CODES].astype(F32)
             for f in range(z.frame):
-                at = side * CODES + 5 * f
+                at = 5 * f
                 hit = high_ids == extra[at : at + 1]
                 terms = [jnp.where(hit, extra[at + 2 + i : at + 3 + i], 0.0) for i in range(3)]
                 left = jnp.concatenate(terms, axis=0).astype(BF16)
@@ -457,11 +470,13 @@
         out[s] = product.astype(BF16)
 
 
-def rest_kernel(z, begin, per_step, near_ids, left, right, table, other, grads, out, sums, ids, sem):
+def rest_kernel(z, count, begin, per_step, near_ids, left, right, grads, *refs):
     del grads
+    extras = refs[:count]
+    out, table, ids, sem = refs[count:]
     bring = pltpu.make_async_copy(near_ids, ids, sem)
     bring.start()
-    sums[...] = table[...] + other[...]
+    add_table(z, extras, table)
     bring.wait()
     products(z, begin + pl.program_id(0) * per_step, per_step, ids, left, right, out)
 
@@ -491,20 +506,28 @@
     closing = (z.pair + z.piece + 15) // 16 * 16
 
     fill = jnp.full((z.wide - local,), -BLOCK, jnp.int32)
-    numbers = jnp.concatenate([cell_type, fill, input_map, fill])
-    message, own_rates = call(
+    blank = jnp.zeros((BLOCK - slots,), jnp.int32)
+    lists = [cell_type, fill, input_map, fill]
+    for x in (slot_owner, slot_post, slot_pre):
+        lists += [x.reshape(slots), blank]
+    numbers = jnp.concatenate(lists)
+    message, own_rates, ids = call(
         functools.partial(start_kernel, z),
-        [shape((opening, BLOCK), BF16), shape((z.piece, BLOCK))],
+        [
+            shape((opening, BLOCK), BF16),
+            shape((z.piece, BLOCK)),
+            shape((1, 2 * slots), jnp.int32),
+        ],
         [pltpu.VMEM((batch, z.wide), F32)],
-        [initial_rates, numbers.reshape(2 * z.frame, BLOCK)],
+        [initial_rates, numbers.reshape(numbers.size // BLOCK, BLOCK)],
     )
     got = share(message, "row")
     weights = weight_blocks.reshape(slots, BLOCK, BLOCK)
-    (ids,) = call(
-        functools.partial(list_kernel, z),
-        [shape((1, 2 * slots), jnp.int32)],
+    (turned,) = call(
+        functools.partial(turn_weights_kernel, z),
+        [shape((slots, BLOCK, BLOCK), BF16)],
         [],
-        [message, slot_owner, slot_post, slot_pre, weights],
+        [message, weights],
     )
     held_ids = [pltpu.SMEM((1, 2 * slots), jnp.int32), pltpu.SemaphoreType.DMA]
     if few(z.rows):
@@ -520,7 +543,7 @@
         functools.partial(first_kernel, z, len(got)),
         [x_shape, *col_parts],
         [pre_sums, post_sums, *held_ids],
-        [ids, weights, message, *got],
+        [ids, turned, message, *got],
         flops=product_flops,
     )
     every = (z.rows * z.piece, BLOCK)
@@ -554,7 +577,7 @@
             functools.partial(forward_kernel, z, t, len(got)),
             [shape(every), shape(pair), shape(pair), x_shape, *col_parts],
             [pre_sums, post_sums, *held_ids],
-            [ids, weights, kept, rates, gain, drive, *got],
+            [ids, turned, kept, rates, gain, drive, *got],
             flops=product_flops,
         )
         xs.append(x)
@@ -611,15 +634,13 @@
         [],
         [*xs, *ds, last_rates],
     )
-    (table,) = call(
-        functools.partial(table_kernel, z, len(got)), [shape((types // BLOCK, BLOCK))], [], [right, delta, *got]
-    )
-    if z.half == 2:
-        other = flip(table, "row", 1)
-    else:
-        total = lax.psum(table, "row")
-        other = 0.5 * total - table
-
+    (extras,) = call(
+        functools.partial(extras_kernel, z, len(got)),
+        [shape((2 * CODES * z.cols, BLOCK), BF16)],
+        [],
+        [right, delta, *got],
+    )
+    all_extras = [extras, flip(extras, "row", 1)] if z.half == 2 else [extras]
     ins = [ids, right, later, delta, *got]
     cost = pl.CostEstimate(
         flops=2 * slots * deep * BLOCK * BLOCK, bytes_accessed=4 * 1024 * 1024, transcendentals=0
@@ -636,18 +657,20 @@
         cost_estimate=cost,
         compiler_params=limit,
     )(*ins)
-    ins = [ids, left, right, table, other, weight_grads]
+    ins = [ids, left, right, weight_grads, *all_extras]
     weight_grads, table = pl.pallas_call(
-        functools.partial(rest_kernel, z, slots - per_step, per_step),
+        functools.partial(rest_kernel, z, len(all_extras), slots - per_step, per_step),
         grid=(1,),
-        out_shape=[grads, shape(table.shape)],
-        in_specs=[VMEM] * 5 + [pl.BlockSpec(memory_space=pl.ANY)],
+        out_shape=[grads, shape((types // BLOCK, BLOCK))],
+        in_specs=[VMEM] * 3 + [pl.BlockSpec(memory_space=pl.ANY)] + [VMEM] * len(all_extras),
         out_specs=[pl.BlockSpec((per_step, BLOCK, BLOCK), lambda i: (i + grid - 1, 0, 0)), VMEM],
         scratch_shapes=held_ids,
-        input_output_aliases={5: 0},
+        input_output_aliases={3: 0},
         cost_estimate=cost,
         compiler_params=limit,
     )(*ins)
+    if z.half != 2:
+        table = 0.5 * lax.psum(table, "row")
     gain_grads = table.reshape(types)
     return (final_rates, weight_grads.reshape(1, 1, slots, BLOCK, BLOCK), gain_grads)
 

time: 94.3 us -> 91.8 us (0.973)
  local copies, waits for them, and re-layouts: 4.37 us -> 3.22 us
    unnamed x18 -> x12, local copies, waits for them, and re-layouts: 4.37 us -> 2.41 us
    pallas_call x16, Pallas kernels: 12 us -> 10.7 us  [call(): pl.pallas_call(body, out_shape=outs, in_specs=specs, out_specs=out_specs...]
  transfers between devices with their start and end apart: 35 -> 35, of which waited for: 22 -> 23; matrix products, arithmetic and copies ran while one was open for 0% -> 0% of each run, Pallas kernels for 5% -> 6%
where the time goes in v6:
time: 91.8 us; the launch traced here: 91.6 us
  starting transfers between devices  35.9 us (39%)
  waiting for transfers between devices  35.5 us (39%)
  Pallas kernels  16.1 us (18%)
  local copies, waits for them, and re-layouts  3.22 us (4%)
    ppermute x35, starting transfers between devices, flip(): return lax.ppermute(x, axis, [(i, i ^ k) for i in range(count)])  35.9 us
    ppermute x35, waiting for transfers between devices, flip(): return lax.ppermute(x, axis, [(i, i ^ k) for i in range(count)])  35.5 us
    pallas_call x16, Pallas kernels, call(): pl.pallas_call(body, out_shape=outs, in_specs=specs, out_specs=out_specs...  10.7 us
    pallas_call x1, Pallas kernels, shards(): pl.pallas_call(functools.partial(grad_kernel, z, len(got), per_step), gri...  2.9 us
    pallas_call x1, Pallas kernels, shards(): pl.pallas_call(functools.partial(rest_kernel, z, len(all_extras), slots -...  2.48 us
    unnamed x12, local copies, waits for them, and re-layouts  2.41 us
  transfers between devices with their start and end apart: 35, of which 23 were waited for; matrix products, arithmetic and copies ran while one was open for 0% of the time, Pallas kernels for 6%

profile of v6, /device:TPU:0, one launch (start us, length us, event | category | flops | bytes accessed | tf_op | source)
XLA Modules:
  0.0 91.6 jit_solution(2470696666233302976)
XLA Ops:
  0.7 0.8 concatenate.3
  1.5 0.8 copy-done.4
  2.3 0.1 shard_map.121
  2.3 3.0 %collective-permute-start.2 = (bf16[96,128]{1,0:T(8,128)(2,1)S(1)}, bf16[96,128]{1,0:T(8,128)(2,1)S(1)}, u32[]{:S(2)}, u32[]{:S(2)}) collective-permute-start(bf16[96,128]{1,0:T(8,128)(2,1)S(1)} %get-tuple-element.63.after.refs_2_.refs_0_.mine), channel_id=1, source_target_pairs={{0,4},{4,0},{8,12},{12,8},{1,5},{5,1},{9,13},{13,9},{2,6},{6,2},{1... | collective-permute-start | bytes 73736 | tf_op jit(solution)/shard_map/ppermute | solution.py:96
  5.4 2.6 %collective-permute-start.1 = (bf16[96,128]{1,0:T(8,128)(2,1)S(1)}, bf16[96,128]{1,0:T(8,128)(2,1)S(1)}, u32[]{:S(2)}, u32[]{:S(2)}) collective-permute-start(bf16[96,128]{1,0:T(8,128)(2,1)S(1)} %get-tuple-element.63.after.refs_2_.refs_0_.mine), channel_id=1, source_target_pairs={{0,8},{4,12},{8,0},{12,4},{1,9},{5,13},{9,1},{13,5},{2,10},{6,14},... | collective-permute-start | bytes 73736 | tf_op jit(solution)/shard_map/ppermute | solution.py:96
  8.0 1.6 %copy-done = bf16[1,1,64,128,128]{4,3,2,1,0:T(8,128)(2,1)S(1)} copy-done((bf16[1,1,64,128,128]{4,3,2,1,0:T(8,128)(2,1)S(1)}, bf16[1,1,64,128,128]{4,3,2,1,0:T(8,128)(2,1)}, u32[]{:S(2)}) %copy-start) | copy-done | bytes 2097176
  9.5 1.0 %shard_map.122.refs_1_ = bf16[64,128,128]{2,1,0:T(8,128)(2,1)S(1)} custom-call(bf16[96,128]{1,0:T(8,128)(2,1)S(1)} %get-tuple-element.63.after.refs_2_.refs_0_.mine, bf16[64,128,128]{2,1,0:T(8,128)(2,1)S(1)} %bitcast.9), custom_call_target="tpu_custom_call" | custom-call | bytes 4218880 | tf_op jit(solution)/shard_map/pallas_call | solution.py:78
  10.6 3.0 %collective-permute-done.refs_3_.refs_5_ = bf16[96,128]{1,0:T(8,128)(2,1)S(1)} collective-permute-done((bf16[96,128]{1,0:T(8,128)(2,1)S(1)}, bf16[96,128]{1,0:T(8,128)(2,1)S(1)}, u32[]{:S(2)}, u32[]{:S(2)}) %collective-permute-start) | collective-permute-done | bytes 24608 | tf_op jit(solution)/shard_map/ppermute | solution.py:96
  13.6 1.5 %shard_map.123 = (bf16[9,32,128]{2,1,0:T(8,128)(2,1)S(1)}, f32[144,128]{1,0:T(8,128)S(1)}, bf16[144,128]{1,0:T(8,128)(2,1)S(1)}, bf16[144,128]{1,0:T(8,128)(2,1)S(1)}, bf16[144,128]{1,0:T(8,128)(2,1)S(1)}) custom-call(s32[1,128]{1,0:T(1,128)S(1)} %get-tuple-element.62.refs_0_.near_ids, bf16[64,128,128]{2,1,0:T(8,128)(2,1)S(1)} %shard_map.122.refs_1_, ...), custom_call_target="tpu_custom_call" | custom-call | flops 67108864 | bytes 2454016 | tf_op jit(solution)/shard_map/pallas_call | solution.py:78
  15.1 1.6 %collective-permute-start.4 = (bf16[144,128]{1,0:T(8,128)(2,1)S(1)}, bf16[144,128]{1,0:T(8,128)(2,1)S(1)}, u32[]{:S(2)}, u32[]{:S(2)}) collective-permute-start(bf16[144,128]{1,0:T(8,128)(2,1)S(1)} %get-tuple-element.67), channel_id=1, source_target_pairs={{0,2},{1,3},{2,0},{3,1},{4,6},{5,7},{6,4},{7,5},{8,10},{9,11},{10,... | collective-permute-start | bytes 110600 | tf_op jit(solution)/shard_map/ppermute | solution.py:96
  16.7 0.3 collective-permute-start.5
  17.0 1.9 %collective-permute-done.3.refs_1_ = bf16[144,128]{1,0:T(8,128)(2,1)S(1)} collective-permute-done((bf16[144,128]{1,0:T(8,128)(2,1)S(1)}, bf16[144,128]{1,0:T(8,128)(2,1)S(1)}, u32[]{:S(2)}, u32[]{:S(2)}) %collective-permute-start.3) | collective-permute-done | bytes 36896 | tf_op jit(solution)/shard_map/ppermute | solution.py:96
  18.8 0.4 collective-permute-done.4.refs_2_
  19.4 1.4 %collective-permute-start.7 = (bf16[144,128]{1,0:T(8,128)(2,1)S(1)}, bf16[144,128]{1,0:T(8,128)(2,1)S(1)}, u32[]{:S(2)}, u32[]{:S(2)}) collective-permute-start(bf16[144,128]{1,0:T(8,128)(2,1)S(1)} %get-tuple-element.74), channel_id=1, source_target_pairs={{0,8},{4,12},{8,0},{12,4},{1,9},{5,13},{9,1},{13,5},{2,10},{6,14},... | collective-permute-start | bytes 110600 | tf_op jit(solution)/shard_map/ppermute | solution.py:96
  20.8 3.0 %collective-permute-start.6 = (bf16[144,128]{1,0:T(8,128)(2,1)S(1)}, bf16[144,128]{1,0:T(8,128)(2,1)S(1)}, u32[]{:S(2)}, u32[]{:S(2)}) collective-permute-start(bf16[144,128]{1,0:T(8,128)(2,1)S(1)} %get-tuple-element.74), channel_id=1, source_target_pairs={{0,12},{4,8},{8,4},{12,0},{1,13},{5,9},{9,5},{13,1},{2,14},{6,10},... | collective-permute-start | bytes 110600 | tf_op jit(solution)/shard_map/ppermute | solution.py:96
  23.8 0.9 %shard_map.125 = (f32[288,128]{1,0:T(8,128)S(1)}, f32[288,128]{1,0:T(8,128)S(1)}, f32[3,288,128]{2,1,0:T(8,128)S(1)}, f32[3,72,128]{2,1,0:T(8,128)S(1)}) custom-call(bf16[96,128]{1,0:T(8,128)(2,1)S(1)} %get-tuple-element.63.after.refs_2_.refs_0_.mine, f32[72,128]{1,0:T(8,128)S(1)} %get-tuple-element.70.refs_1_, f32[3,32,288]{2,1,0:T(8,128)S(1)} %copy-done.2, ...), custom_call_target="tpu_custom_call" | custom-call | bytes 1224704 | tf_op jit(solution)/shard_map/pallas_call | solution.py:78
  24.7 1.8 %collective-permute-done.6.refs_6_ = bf16[144,128]{1,0:T(8,128)(2,1)S(1)} collective-permute-done((bf16[144,128]{1,0:T(8,128)(2,1)S(1)}, bf16[144,128]{1,0:T(8,128)(2,1)S(1)}, u32[]{:S(2)}, u32[]{:S(2)}) %collective-permute-start.6) | collective-permute-done | bytes 36896 | tf_op jit(solution)/shard_map/ppermute | solution.py:96
  26.5 1.5 %shard_map.126 = (f32[288,128]{1,0:T(8,128)S(1)}, f32[144,128]{1,0:T(8,128)S(1)}, f32[144,128]{1,0:T(8,128)S(1)}, bf16[9,32,128]{2,1,0:T(8,128)(2,1)S(1)}, f32[1...) custom-call(s32[1,128]{1,0:T(1,128)S(1)} %get-tuple-element.62.refs_, ...), custom_call_target="tpu_custom_call" | custom-call | flops 67108864 | bytes 3572224 | tf_op jit(solution)/shard_map/pallas_call | solution.py:78
  28.2 1.6 %collective-permute-start.10 = (bf16[144,128]{1,0:T(8,128)(2,1)S(1)}, bf16[144,128]{1,0:T(8,128)(2,1)S(1)}, u32[]{:S(2)}, u32[]{:S(2)}) collective-permute-start(bf16[144,128]{1,0:T(8,128)(2,1)S(1)} %get-tuple-element.78), channel_id=1, source_target_pairs={{0,2},{1,3},{2,0},{3,1},{4,6},{5,7},{6,4},{7,5},{8,10},{9,11},{10,... | collective-permute-start | bytes 110600 | tf_op jit(solution)/shard_map/ppermute | solution.py:96
  29.7 0.3 collective-permute-start.11
  30.0 1.9 %collective-permute-done.9.refs_1_ = bf16[144,128]{1,0:T(8,128)(2,1)S(1)} collective-permute-done((bf16[144,128]{1,0:T(8,128)(2,1)S(1)}, bf16[144,128]{1,0:T(8,128)(2,1)S(1)}, u32[]{:S(2)}, u32[]{:S(2)}) %collective-permute-start.9) | collective-permute-done | bytes 36896 | tf_op jit(solution)/shard_map/ppermute | solution.py:96
  31.9 0.4 collective-permute-done.10.refs_2_
  32.4 0.1 collective-permute-start.14
  32.4 3.5 %collective-permute-start.13 = (bf16[144,128]{1,0:T(8,128)(2,1)S(1)}, bf16[144,128]{1,0:T(8,128)(2,1)S(1)}, u32[]{:S(2)}, u32[]{:S(2)}) collective-permute-start(bf16[144,128]{1,0:T(8,128)(2,1)S(1)} %get-tuple-element.82), channel_id=1, source_target_pairs={{0,8},{4,12},{8,0},{12,4},{1,9},{5,13},{9,1},{13,5},{2,10},{6,14},... | collective-permute-start | bytes 110600 | tf_op jit(solution)/shard_map/ppermute | solution.py:96
  36.0 0.8 collective-permute-start.12
  36.8 1.4 %collective-permute-done.13.refs_7_ = bf16[144,128]{1,0:T(8,128)(2,1)S(1)} collective-permute-done((bf16[144,128]{1,0:T(8,128)(2,1)S(1)}, bf16[144,128]{1,0:T(8,128)(2,1)S(1)}, u32[]{:S(2)}, u32[]{:S(2)}) %collective-permute-start.13) | collective-permute-done | bytes 36896 | tf_op jit(solution)/shard_map/ppermute | solution.py:96
  38.2 3.5 %collective-permute-done.12.refs_6_ = bf16[144,128]{1,0:T(8,128)(2,1)S(1)} collective-permute-done((bf16[144,128]{1,0:T(8,128)(2,1)S(1)}, bf16[144,128]{1,0:T(8,128)(2,1)S(1)}, u32[]{:S(2)}, u32[]{:S(2)}) %collective-permute-start.12) | collective-permute-done | bytes 36896 | tf_op jit(solution)/shard_map/ppermute | solution.py:96
  41.7 1.6 %shard_map.128 = (f32[288,128]{1,0:T(8,128)S(1)}, f32[144,128]{1,0:T(8,128)S(1)}, f32[144,128]{1,0:T(8,128)S(1)}, bf16[9,32,128]{2,1,0:T(8,128)(2,1)S(1)}, f32[1...) custom-call(s32[1,128]{1,0:T(1,128)S(1)} %get-tuple-element.62.refs_, ...), custom_call_target="tpu_custom_call" | custom-call | flops 67108864 | bytes 3572224 | tf_op jit(solution)/shard_map/pallas_call | solution.py:78
  43.3 0.1 collective-permute-start.15
  43.4 1.6 %collective-permute-start.16 = (bf16[144,128]{1,0:T(8,128)(2,1)S(1)}, bf16[144,128]{1,0:T(8,128)(2,1)S(1)}, u32[]{:S(2)}, u32[]{:S(2)}) collective-permute-start(bf16[144,128]{1,0:T(8,128)(2,1)S(1)} %get-tuple-element.86), channel_id=1, source_target_pairs={{0,2},{1,3},{2,0},{3,1},{4,6},{5,7},{6,4},{7,5},{8,10},{9,11},{10,... | collective-permute-start | bytes 110600 | tf_op jit(solution)/shard_map/ppermute | solution.py:96
  44.9 0.3 collective-permute-start.17
  45.2 1.9 %collective-permute-done.15.refs_1_ = bf16[144,128]{1,0:T(8,128)(2,1)S(1)} collective-permute-done((bf16[144,128]{1,0:T(8,128)(2,1)S(1)}, bf16[144,128]{1,0:T(8,128)(2,1)S(1)}, u32[]{:S(2)}, u32[]{:S(2)}) %collective-permute-start.15) | collective-permute-done | bytes 36896 | tf_op jit(solution)/shard_map/ppermute | solution.py:96
  47.1 0.5 collective-permute-done.16.refs_2_
  47.6 5.1 %collective-permute-done.18.theirs = bf16[224,128]{1,0:T(8,128)(2,1)S(1)} collective-permute-done((bf16[224,128]{1,0:T(8,128)(2,1)S(1)}, bf16[224,128]{1,0:T(8,128)(2,1)S(1)}, u32[]{:S(2)}, u32[]{:S(2)}) %collective-permute-start.18) | collective-permute-done | bytes 57376 | tf_op jit(solution)/shard_map/ppermute | solution.py:96
  52.8 1.6 %collective-permute-start.20 = (bf16[144,128]{1,0:T(8,128)(2,1)S(1)}, bf16[144,128]{1,0:T(8,128)(2,1)S(1)}, u32[]{:S(2)}, u32[]{:S(2)}) collective-permute-start(bf16[144,128]{1,0:T(8,128)(2,1)S(1)} %get-tuple-element.93.refs_3_), channel_id=1, source_target_pairs={{0,2},{1,3},{2,0},{3,1},{4,6},{5,7},{6,4},{7,5},{8,10},{9,11},{10,... | collective-permute-start | bytes 110600 | tf_op jit(solution)/shard_map/ppermute | solution.py:96
  54.4 0.3 collective-permute-start.19
  54.7 2.2 %collective-permute-done.20.refs_5_ = bf16[144,128]{1,0:T(8,128)(2,1)S(1)} collective-permute-done((bf16[144,128]{1,0:T(8,128)(2,1)S(1)}, bf16[144,128]{1,0:T(8,128)(2,1)S(1)}, u32[]{:S(2)}, u32[]{:S(2)}) %collective-permute-start.20) | collective-permute-done | bytes 36896 | tf_op jit(solution)/shard_map/ppermute | solution.py:96
  56.9 1.0 %collective-permute-done.19.refs_4_ = bf16[144,128]{1,0:T(8,128)(2,1)S(1)} collective-permute-done((bf16[144,128]{1,0:T(8,128)(2,1)S(1)}, bf16[144,128]{1,0:T(8,128)(2,1)S(1)}, u32[]{:S(2)}, u32[]{:S(2)}) %collective-permute-start.19) | collective-permute-done | bytes 36896 | tf_op jit(solution)/shard_map/ppermute | solution.py:96
  57.8 1.5 %shard_map.131 = (bf16[18,32,128]{2,1,0:T(8,128)(2,1)S(1)}, f32[144,128]{1,0:T(8,128)S(1)}, bf16[144,128]{1,0:T(8,128)(2,1)S(1)}, bf16[144,128]{1,0:T(8,128)(2,1)S(1)}, bf16[144,128]{1,0:T(8,128)(2,1)S(1)}) custom-call(s32[1,128]{1,0:T(1,128)S(1)} %get-tuple-element.62.refs_0_.near_ids, bf16[64,128,128]{2,1,0:T(8,128)(2,1)S(1)} %bitcast.10, ...), custom_call_target="tpu_custom_call" | custom-call | flops 67108864 | bytes 2613760 | tf_op jit(solution)/shard_map/pallas_call | solution.py:78
  59.4 1.7 %collective-permute-start.22 = (bf16[144,128]{1,0:T(8,128)(2,1)S(1)}, bf16[144,128]{1,0:T(8,128)(2,1)S(1)}, u32[]{:S(2)}, u32[]{:S(2)}) collective-permute-start(bf16[144,128]{1,0:T(8,128)(2,1)S(1)} %get-tuple-element.99), channel_id=1, source_target_pairs={{0,12},{4,8},{8,4},{12,0},{1,13},{5,9},{9,5},{13,1},{2,14},{6,10},... | collective-permute-start | bytes 110600 | tf_op jit(solution)/shard_map/ppermute | solution.py:96
  61.1 2.8 %collective-permute-start.24 = (bf16[144,128]{1,0:T(8,128)(2,1)S(1)}, bf16[144,128]{1,0:T(8,128)(2,1)S(1)}, u32[]{:S(2)}, u32[]{:S(2)}) collective-permute-start(bf16[144,128]{1,0:T(8,128)(2,1)S(1)} %get-tuple-element.101), channel_id=1, source_target_pairs={{0,4},{4,0},{8,12},{12,8},{1,5},{5,1},{9,13},{13,9},{2,6},{6,2},{1... | collective-permute-start | bytes 110600 | tf_op jit(solution)/shard_map/ppermute | solution.py:96
  63.8 1.4 %collective-permute-done.22.refs_0_ = bf16[144,128]{1,0:T(8,128)(2,1)S(1)} collective-permute-done((bf16[144,128]{1,0:T(8,128)(2,1)S(1)}, bf16[144,128]{1,0:T(8,128)(2,1)S(1)}, u32[]{:S(2)}, u32[]{:S(2)}) %collective-permute-start.22) | collective-permute-done | bytes 36896 | tf_op jit(solution)/shard_map/ppermute | solution.py:96
  65.3 1.2 %collective-permute-done.23.refs_1_ = bf16[144,128]{1,0:T(8,128)(2,1)S(1)} collective-permute-done((bf16[144,128]{1,0:T(8,128)(2,1)S(1)}, bf16[144,128]{1,0:T(8,128)(2,1)S(1)}, u32[]{:S(2)}, u32[]{:S(2)}) %collective-permute-start.23) | collective-permute-done | bytes 36896 | tf_op jit(solution)/shard_map/ppermute | solution.py:96
  66.6 0.9 %collective-permute-start.26 = (bf16[144,128]{1,0:T(8,128)(2,1)S(1)}, bf16[144,128]{1,0:T(8,128)(2,1)S(1)}, u32[]{:S(2)}, u32[]{:S(2)}) collective-permute-start(bf16[144,128]{1,0:T(8,128)(2,1)S(1)} %get-tuple-element.103.refs_3_), channel_id=1, source_target_pairs={{0,2},{1,3},{2,0},{3,1},{4,6},{5,7},{6,4},{7,5},{8,10},{9,11},{10,... | collective-permute-start | bytes 110600 | tf_op jit(solution)/shard_map/ppermute | solution.py:96
  67.5 0.9 %collective-permute-start.25 = (bf16[144,128]{1,0:T(8,128)(2,1)S(1)}, bf16[144,128]{1,0:T(8,128)(2,1)S(1)}, u32[]{:S(2)}, u32[]{:S(2)}) collective-permute-start(bf16[144,128]{1,0:T(8,128)(2,1)S(1)} %get-tuple-element.103.refs_3_), channel_id=1, source_target_pairs={{0,3},{1,2},{2,1},{3,0},{4,7},{5,6},{6,5},{7,4},{8,11},{9,10},{10,... | collective-permute-start | bytes 110600 | tf_op jit(solution)/shard_map/ppermute | solution.py:96
  68.5 2.2 %collective-permute-done.26.refs_5_ = bf16[144,128]{1,0:T(8,128)(2,1)S(1)} collective-permute-done((bf16[144,128]{1,0:T(8,128)(2,1)S(1)}, bf16[144,128]{1,0:T(8,128)(2,1)S(1)}, u32[]{:S(2)}, u32[]{:S(2)}) %collective-permute-start.26) | collective-permute-done | bytes 36896 | tf_op jit(solution)/shard_map/ppermute | solution.py:96
  70.7 0.4 collective-permute-done.25.refs_4_
  71.2 1.5 %shard_map.133 = (bf16[18,32,128]{2,1,0:T(8,128)(2,1)S(1)}, f32[144,128]{1,0:T(8,128)S(1)}, bf16[144,128]{1,0:T(8,128)(2,1)S(1)}, bf16[144,128]{1,0:T(8,128)(2,1)S(1)}, bf16[144,128]{1,0:T(8,128)(2,1)S(1)}) custom-call(s32[1,128]{1,0:T(1,128)S(1)} %get-tuple-element.62.refs_0_.near_ids, bf16[64,128,128]{2,1,0:T(8,128)(2,1)S(1)} %bitcast.11, ...), custom_call_target="tpu_custom_call" | custom-call | flops 67108864 | bytes 2613760 | tf_op jit(solution)/shard_map/pallas_call | solution.py:78
  72.7 1.7 %collective-permute-start.28 = (bf16[144,128]{1,0:T(8,128)(2,1)S(1)}, bf16[144,128]{1,0:T(8,128)(2,1)S(1)}, u32[]{:S(2)}, u32[]{:S(2)}) collective-permute-start(bf16[144,128]{1,0:T(8,128)(2,1)S(1)} %get-tuple-element.114), channel_id=1, source_target_pairs={{0,12},{4,8},{8,4},{12,0},{1,13},{5,9},{9,5},{13,1},{2,14},{6,10},... | collective-permute-start | bytes 110600 | tf_op jit(solution)/shard_map/ppermute | solution.py:96
  74.4 1.1 %collective-permute-start.29 = (bf16[144,128]{1,0:T(8,128)(2,1)S(1)}, bf16[144,128]{1,0:T(8,128)(2,1)S(1)}, u32[]{:S(2)}, u32[]{:S(2)}) collective-permute-start(bf16[144,128]{1,0:T(8,128)(2,1)S(1)} %get-tuple-element.115), channel_id=1, source_target_pairs={{0,8},{4,12},{8,0},{12,4},{1,9},{5,13},{9,1},{13,5},{2,10},{6,14},... | collective-permute-start | bytes 110600 | tf_op jit(solution)/shard_map/ppermute | solution.py:96
  75.6 1.6 %collective-permute-start.30 = (bf16[144,128]{1,0:T(8,128)(2,1)S(1)}, bf16[144,128]{1,0:T(8,128)(2,1)S(1)}, u32[]{:S(2)}, u32[]{:S(2)}) collective-permute-start(bf16[144,128]{1,0:T(8,128)(2,1)S(1)} %get-tuple-element.116), channel_id=1, source_target_pairs={{0,4},{4,0},{8,12},{12,8},{1,5},{5,1},{9,13},{13,9},{2,6},{6,2},{1... | collective-permute-start | bytes 110600 | tf_op jit(solution)/shard_map/ppermute | solution.py:96
  77.1 1.4 %collective-permute-done.28.refs_0_ = bf16[144,128]{1,0:T(8,128)(2,1)S(1)} collective-permute-done((bf16[144,128]{1,0:T(8,128)(2,1)S(1)}, bf16[144,128]{1,0:T(8,128)(2,1)S(1)}, u32[]{:S(2)}, u32[]{:S(2)}) %collective-permute-start.28) | collective-permute-done | bytes 36896 | tf_op jit(solution)/shard_map/ppermute | solution.py:96
  78.6 1.4 %collective-permute-done.29.refs_1_ = bf16[144,128]{1,0:T(8,128)(2,1)S(1)} collective-permute-done((bf16[144,128]{1,0:T(8,128)(2,1)S(1)}, bf16[144,128]{1,0:T(8,128)(2,1)S(1)}, u32[]{:S(2)}, u32[]{:S(2)}) %collective-permute-start.29) | collective-permute-done | bytes 36896 | tf_op jit(solution)/shard_map/ppermute | solution.py:96
  79.9 0.3 collective-permute-done.30.refs_2_
  80.2 0.1 shard_map.135.refs_3_.mine
  80.4 1.0 %collective-permute-start.32 = (bf16[176,128]{1,0:T(8,128)(2,1)S(1)}, bf16[176,128]{1,0:T(8,128)(2,1)S(1)}, u32[]{:S(2)}, u32[]{:S(2)}) collective-permute-start(bf16[176,128]{1,0:T(8,128)(2,1)S(1)} %shard_map.135.refs_3_.mine), channel_id=1, source_target_pairs={{0,2},{1,3},{2,0},{3,1},{4,6},{5,7},{6,4},{7,5},{8,10},{9,11},{10,... | collective-permute-start | bytes 135176 | tf_op jit(solution)/shard_map/ppermute | solution.py:96
  81.4 0.8 collective-permute-start.31
  82.2 0.8 shard_map.134
  83.1 1.6 %collective-permute-done.32.refs_5_.refs_1_ = bf16[176,128]{1,0:T(8,128)(2,1)S(1)} collective-permute-done((bf16[176,128]{1,0:T(8,128)(2,1)S(1)}, bf16[176,128]{1,0:T(8,128)(2,1)S(1)}, u32[]{:S(2)}, u32[]{:S(2)}) %collective-permute-start.32) | collective-permute-done | bytes 45088 | tf_op jit(solution)/shard_map/ppermute | solution.py:96
  84.7 0.5 collective-permute-done.31.refs_4_.refs_0_
  85.2 0.9 collective-permute-start.34
  86.1 2.9 %shard_map.136 = (bf16[18,128,128]{2,1,0:T(8,128)(2,1)S(1)}, bf16[64,128,128]{2,1,0:T(8,128)(2,1)}) custom-call(s32[1,128]{1,0:T(1,128)S(1)} %get-tuple-element.62.refs_0_.near_ids, bf16[9,128,128]{2,1,0:T(8,128)(2,1)S(1)} %get-tuple-element.108.refs_1_.right, bf16[18,128,128]{2,1,0:T(8,128)(2,1)S(1)} %get-tuple-element.109.refs_2_, ...), custom_call_target="tpu_custom_call" | custom-call | flops 268435456 | bytes 4194304 | tf_op jit(solution)/shard_map/pallas_call | solution.py:650
  89.0 0.1 collective-permute-done.34.refs_1_
  89.1 2.5 %shard_map.138 = (bf16[64,128,128]{2,1,0:T(8,128)(2,1)}, f32[64,128]{1,0:T(8,128)}) custom-call(s32[1,128]{1,0:T(1,128)S(1)} %get-tuple-element.62.refs_0_.near_ids, bf16[18,128,128]{2,1,0:T(8,128)(2,1)S(1)} %get-tuple-element.117.left, bf16[9,128,128]{2,1,0:T(8,128)(2,1)S(1)} %get-tuple-element.108.refs_1_.right, ...), custom_call_target="tpu_custom_call", output_to_operand_aliasing={{0}: (3, {})} | custom-call | flops 268435456 | bytes 4194304 | tf_op jit(solution)/shard_map/pallas_call | solution.py:661
  (39 shorter events, 0.8 us)
Async XLA Ops:
  1.5 0.8 copy-start.4
  2.3 8.2 %collective-permute-start.2 = (bf16[96,128]{1,0:T(8,128)(2,1)S(1)}, bf16[96,128]{1,0:T(8,128)(2,1)S(1)}, u32[]{:S(2)}, u32[]{:S(2)}) collective-permute-start(bf16[96,128]{1,0:T(8,128)(2,1)S(1)} %get-tuple-element.63.after.refs_2_.refs_0_.mine), channel_id=1, source_target_pairs={{0,4},{4,0},{8,12},{12,8},{1,5},{5,1},{9,13},{13,9},{2,6},{6,2},{1... | collective-permute-start | bytes 73736 | tf_op jit(solution)/shard_map/ppermute | solution.py:96
  5.4 5.2 %collective-permute-start.1 = (bf16[96,128]{1,0:T(8,128)(2,1)S(1)}, bf16[96,128]{1,0:T(8,128)(2,1)S(1)}, u32[]{:S(2)}, u32[]{:S(2)}) collective-permute-start(bf16[96,128]{1,0:T(8,128)(2,1)S(1)} %get-tuple-element.63.after.refs_2_.refs_0_.mine), channel_id=1, source_target_pairs={{0,8},{4,12},{8,0},{12,4},{1,9},{5,13},{9,1},{13,5},{2,10},{6,14},... | collective-permute-start | bytes 73736 | tf_op jit(solution)/shard_map/ppermute | solution.py:96
  7.9 5.6 %collective-permute-start = (bf16[96,128]{1,0:T(8,128)(2,1)S(1)}, bf16[96,128]{1,0:T(8,128)(2,1)S(1)}, u32[]{:S(2)}, u32[]{:S(2)}) collective-permute-start(bf16[96,128]{1,0:T(8,128)(2,1)S(1)} %get-tuple-element.63.after.refs_2_.refs_0_.mine), channel_id=1, source_target_pairs={{0,12},{4,8},{8,4},{12,0},{1,13},{5,9},{9,5},{13,1},{2,14},{6,10},... | collective-permute-start | bytes 73736 | tf_op jit(solution)/shard_map/ppermute | solution.py:96
  8.0 1.6 %copy-start = (bf16[1,1,64,128,128]{4,3,2,1,0:T(8,128)(2,1)S(1)}, bf16[1,1,64,128,128]{4,3,2,1,0:T(8,128)(2,1)}, u32[]{:S(2)}) copy-start(bf16[1,1,64,128,128]{4,3,2,1,0:T(8,128)(2,1)} %param.13) | copy-start | bytes 6291460
  10.5 13.2 %copy-start.2 = (f32[3,32,288]{2,1,0:T(8,128)S(1)}, f32[3,32,288]{2,1,0:T(8,128)}, u32[]{:S(2)}) copy-start(f32[3,32,288]{2,1,0:T(8,128)} %refs_2_.1) | copy-start | bytes 331780
  10.5 13.2 %copy-start.3 = (bf16[3,32,512]{2,1,0:T(8,128)(2,1)S(1)}, bf16[3,32,512]{2,1,0:T(8,128)(2,1)}, u32[]{:S(2)}) copy-start(bf16[3,32,512]{2,1,0:T(8,128)(2,1)} %param.11) | copy-start | bytes 294916
  10.5 13.2 %copy-start.5 = (f32[8192]{0:T(1024)S(1)}, f32[8192]{0:T(1024)}, u32[]{:S(2)}) copy-start(f32[8192]{0:T(1024)} %param.18) | copy-start | bytes 98308
  15.0 3.8 %collective-permute-start.3 = (bf16[144,128]{1,0:T(8,128)(2,1)S(1)}, bf16[144,128]{1,0:T(8,128)(2,1)S(1)}, u32[]{:S(2)}, u32[]{:S(2)}) collective-permute-start(bf16[144,128]{1,0:T(8,128)(2,1)S(1)} %get-tuple-element.66), channel_id=1, source_target_pairs={{0,3},{1,2},{2,1},{3,0},{4,7},{5,6},{6,5},{7,4},{8,11},{9,10},{10,... | collective-permute-start | bytes 110600 | tf_op jit(solution)/shard_map/ppermute | solution.py:96
  15.1 4.2 %collective-permute-start.4 = (bf16[144,128]{1,0:T(8,128)(2,1)S(1)}, bf16[144,128]{1,0:T(8,128)(2,1)S(1)}, u32[]{:S(2)}, u32[]{:S(2)}) collective-permute-start(bf16[144,128]{1,0:T(8,128)(2,1)S(1)} %get-tuple-element.67), channel_id=1, source_target_pairs={{0,2},{1,3},{2,0},{3,1},{4,6},{5,7},{6,4},{7,5},{8,10},{9,11},{10,... | collective-permute-start | bytes 110600 | tf_op jit(solution)/shard_map/ppermute | solution.py:96
  16.7 2.6 %collective-permute-start.5 = (bf16[144,128]{1,0:T(8,128)(2,1)S(1)}, bf16[144,128]{1,0:T(8,128)(2,1)S(1)}, u32[]{:S(2)}, u32[]{:S(2)}) collective-permute-start(bf16[144,128]{1,0:T(8,128)(2,1)S(1)} %get-tuple-element.68), channel_id=1, source_target_pairs={{0,1},{1,0},{2,3},{3,2},{4,5},{5,4},{6,7},{7,6},{8,9},{9,8},{10,11... | collective-permute-start | bytes 110600 | tf_op jit(solution)/shard_map/ppermute | solution.py:96
  19.3 5.4 %collective-permute-start.8 = (bf16[144,128]{1,0:T(8,128)(2,1)S(1)}, bf16[144,128]{1,0:T(8,128)(2,1)S(1)}, u32[]{:S(2)}, u32[]{:S(2)}) collective-permute-start(bf16[144,128]{1,0:T(8,128)(2,1)S(1)} %get-tuple-element.74), channel_id=1, source_target_pairs={{0,4},{4,0},{8,12},{12,8},{1,5},{5,1},{9,13},{13,9},{2,6},{6,2},{1... | collective-permute-start | bytes 110600 | tf_op jit(solution)/shard_map/ppermute | solution.py:96
  19.4 5.3 %collective-permute-start.7 = (bf16[144,128]{1,0:T(8,128)(2,1)S(1)}, bf16[144,128]{1,0:T(8,128)(2,1)S(1)}, u32[]{:S(2)}, u32[]{:S(2)}) collective-permute-start(bf16[144,128]{1,0:T(8,128)(2,1)S(1)} %get-tuple-element.74), channel_id=1, source_target_pairs={{0,8},{4,12},{8,0},{12,4},{1,9},{5,13},{9,1},{13,5},{2,10},{6,14},... | collective-permute-start | bytes 110600 | tf_op jit(solution)/shard_map/ppermute | solution.py:96
  20.8 5.8 %collective-permute-start.6 = (bf16[144,128]{1,0:T(8,128)(2,1)S(1)}, bf16[144,128]{1,0:T(8,128)(2,1)S(1)}, u32[]{:S(2)}, u32[]{:S(2)}) collective-permute-start(bf16[144,128]{1,0:T(8,128)(2,1)S(1)} %get-tuple-element.74), channel_id=1, source_target_pairs={{0,12},{4,8},{8,4},{12,0},{1,13},{5,9},{9,5},{13,1},{2,14},{6,10},... | collective-permute-start | bytes 110600 | tf_op jit(solution)/shard_map/ppermute | solution.py:96
  28.1 3.8 %collective-permute-start.9 = (bf16[144,128]{1,0:T(8,128)(2,1)S(1)}, bf16[144,128]{1,0:T(8,128)(2,1)S(1)}, u32[]{:S(2)}, u32[]{:S(2)}) collective-permute-start(bf16[144,128]{1,0:T(8,128)(2,1)S(1)} %get-tuple-element.77), channel_id=1, source_target_pairs={{0,3},{1,2},{2,1},{3,0},{4,7},{5,6},{6,5},{7,4},{8,11},{9,10},{10,... | collective-permute-start | bytes 110600 | tf_op jit(solution)/shard_map/ppermute | solution.py:96
  28.2 4.2 %collective-permute-start.10 = (bf16[144,128]{1,0:T(8,128)(2,1)S(1)}, bf16[144,128]{1,0:T(8,128)(2,1)S(1)}, u32[]{:S(2)}, u32[]{:S(2)}) collective-permute-start(bf16[144,128]{1,0:T(8,128)(2,1)S(1)} %get-tuple-element.78), channel_id=1, source_target_pairs={{0,2},{1,3},{2,0},{3,1},{4,6},{5,7},{6,4},{7,5},{8,10},{9,11},{10,... | collective-permute-start | bytes 110600 | tf_op jit(solution)/shard_map/ppermute | solution.py:96
  29.7 2.6 %collective-permute-start.11 = (bf16[144,128]{1,0:T(8,128)(2,1)S(1)}, bf16[144,128]{1,0:T(8,128)(2,1)S(1)}, u32[]{:S(2)}, u32[]{:S(2)}) collective-permute-start(bf16[144,128]{1,0:T(8,128)(2,1)S(1)} %get-tuple-element.79), channel_id=1, source_target_pairs={{0,1},{1,0},{2,3},{3,2},{4,5},{5,4},{6,7},{7,6},{8,9},{9,8},{10,11... | collective-permute-start | bytes 110600 | tf_op jit(solution)/shard_map/ppermute | solution.py:96
  32.4 4.5 %collective-permute-start.14 = (bf16[144,128]{1,0:T(8,128)(2,1)S(1)}, bf16[144,128]{1,0:T(8,128)(2,1)S(1)}, u32[]{:S(2)}, u32[]{:S(2)}) collective-permute-start(bf16[144,128]{1,0:T(8,128)(2,1)S(1)} %get-tuple-element.82), channel_id=1, source_target_pairs={{0,4},{4,0},{8,12},{12,8},{1,5},{5,1},{9,13},{13,9},{2,6},{6,2},{1... | collective-permute-start | bytes 110600 | tf_op jit(solution)/shard_map/ppermute | solution.py:96
  32.4 5.8 %collective-permute-start.13 = (bf16[144,128]{1,0:T(8,128)(2,1)S(1)}, bf16[144,128]{1,0:T(8,128)(2,1)S(1)}, u32[]{:S(2)}, u32[]{:S(2)}) collective-permute-start(bf16[144,128]{1,0:T(8,128)(2,1)S(1)} %get-tuple-element.82), channel_id=1, source_target_pairs={{0,8},{4,12},{8,0},{12,4},{1,9},{5,13},{9,1},{13,5},{2,10},{6,14},... | collective-permute-start | bytes 110600 | tf_op jit(solution)/shard_map/ppermute | solution.py:96
  36.0 5.8 %collective-permute-start.12 = (bf16[144,128]{1,0:T(8,128)(2,1)S(1)}, bf16[144,128]{1,0:T(8,128)(2,1)S(1)}, u32[]{:S(2)}, u32[]{:S(2)}) collective-permute-start(bf16[144,128]{1,0:T(8,128)(2,1)S(1)} %get-tuple-element.82), channel_id=1, source_target_pairs={{0,12},{4,8},{8,4},{12,0},{1,13},{5,9},{9,5},{13,1},{2,14},{6,10},... | collective-permute-start | bytes 110600 | tf_op jit(solution)/shard_map/ppermute | solution.py:96
  41.7 16.1 %copy-start.1 = (bf16[1,1,64,128,128]{4,3,2,1,0:T(8,128)(2,1)S(1)}, bf16[1,1,64,128,128]{4,3,2,1,0:T(8,128)(2,1)}, u32[]{:S(2)}) copy-start(bf16[1,1,64,128,128]{4,3,2,1,0:T(8,128)(2,1)} %param.13) | copy-start | bytes 6291460
  43.3 3.8 %collective-permute-start.15 = (bf16[144,128]{1,0:T(8,128)(2,1)S(1)}, bf16[144,128]{1,0:T(8,128)(2,1)S(1)}, u32[]{:S(2)}, u32[]{:S(2)}) collective-permute-start(bf16[144,128]{1,0:T(8,128)(2,1)S(1)} %get-tuple-element.85), channel_id=1, source_target_pairs={{0,3},{1,2},{2,1},{3,0},{4,7},{5,6},{6,5},{7,4},{8,11},{9,10},{10,... | collective-permute-start | bytes 110600 | tf_op jit(solution)/shard_map/ppermute | solution.py:96
  43.4 4.2 %collective-permute-start.16 = (bf16[144,128]{1,0:T(8,128)(2,1)S(1)}, bf16[144,128]{1,0:T(8,128)(2,1)S(1)}, u32[]{:S(2)}, u32[]{:S(2)}) collective-permute-start(bf16[144,128]{1,0:T(8,128)(2,1)S(1)} %get-tuple-element.86), channel_id=1, source_target_pairs={{0,2},{1,3},{2,0},{3,1},{4,6},{5,7},{6,4},{7,5},{8,10},{9,11},{10,... | collective-permute-start | bytes 110600 | tf_op jit(solution)/shard_map/ppermute | solution.py:96
  44.9 2.6 %collective-permute-start.17 = (bf16[144,128]{1,0:T(8,128)(2,1)S(1)}, bf16[144,128]{1,0:T(8,128)(2,1)S(1)}, u32[]{:S(2)}, u32[]{:S(2)}) collective-permute-start(bf16[144,128]{1,0:T(8,128)(2,1)S(1)} %get-tuple-element.87), channel_id=1, source_target_pairs={{0,1},{1,0},{2,3},{3,2},{4,5},{5,4},{6,7},{7,6},{8,9},{9,8},{10,11... | collective-permute-start | bytes 110600 | tf_op jit(solution)/shard_map/ppermute | solution.py:96
  47.6 5.1 %collective-permute-start.18 = (bf16[224,128]{1,0:T(8,128)(2,1)S(1)}, bf16[224,128]{1,0:T(8,128)(2,1)S(1)}, u32[]{:S(2)}, u32[]{:S(2)}) collective-permute-start(bf16[224,128]{1,0:T(8,128)(2,1)S(1)} %get-tuple-element.90), channel_id=1, source_target_pairs={{0,8},{4,12},{8,0},{12,4},{1,9},{5,13},{9,1},{13,5},{2,10},{6,14},... | collective-permute-start | bytes 172040 | tf_op jit(solution)/shard_map/ppermute | solution.py:96
  52.8 1.9 %collective-permute-start.21 = (bf16[144,128]{1,0:T(8,128)(2,1)S(1)}, bf16[144,128]{1,0:T(8,128)(2,1)S(1)}, u32[]{:S(2)}, u32[]{:S(2)}) collective-permute-start(bf16[144,128]{1,0:T(8,128)(2,1)S(1)} %get-tuple-element.93.refs_3_), channel_id=1, source_target_pairs={{0,1},{1,0},{2,3},{3,2},{4,5},{5,4},{6,7},{7,6},{8,9},{9,8},{10,11... | collective-permute-start | bytes 110600 | tf_op jit(solution)/shard_map/ppermute | solution.py:96
  52.8 4.0 %collective-permute-start.20 = (bf16[144,128]{1,0:T(8,128)(2,1)S(1)}, bf16[144,128]{1,0:T(8,128)(2,1)S(1)}, u32[]{:S(2)}, u32[]{:S(2)}) collective-permute-start(bf16[144,128]{1,0:T(8,128)(2,1)S(1)} %get-tuple-element.93.refs_3_), channel_id=1, source_target_pairs={{0,2},{1,3},{2,0},{3,1},{4,6},{5,7},{6,4},{7,5},{8,10},{9,11},{10,... | collective-permute-start | bytes 110600 | tf_op jit(solution)/shard_map/ppermute | solution.py:96
  54.4 3.4 %collective-permute-start.19 = (bf16[144,128]{1,0:T(8,128)(2,1)S(1)}, bf16[144,128]{1,0:T(8,128)(2,1)S(1)}, u32[]{:S(2)}, u32[]{:S(2)}) collective-permute-start(bf16[144,128]{1,0:T(8,128)(2,1)S(1)} %get-tuple-element.93.refs_3_), channel_id=1, source_target_pairs={{0,3},{1,2},{2,1},{3,0},{4,7},{5,6},{6,5},{7,4},{8,11},{9,10},{10,... | collective-permute-start | bytes 110600 | tf_op jit(solution)/shard_map/ppermute | solution.py:96
  59.4 5.9 %collective-permute-start.22 = (bf16[144,128]{1,0:T(8,128)(2,1)S(1)}, bf16[144,128]{1,0:T(8,128)(2,1)S(1)}, u32[]{:S(2)}, u32[]{:S(2)}) collective-permute-start(bf16[144,128]{1,0:T(8,128)(2,1)S(1)} %get-tuple-element.99), channel_id=1, source_target_pairs={{0,12},{4,8},{8,4},{12,0},{1,13},{5,9},{9,5},{13,1},{2,14},{6,10},... | collective-permute-start | bytes 110600 | tf_op jit(solution)/shard_map/ppermute | solution.py:96
  61.1 5.4 %collective-permute-start.23 = (bf16[144,128]{1,0:T(8,128)(2,1)S(1)}, bf16[144,128]{1,0:T(8,128)(2,1)S(1)}, u32[]{:S(2)}, u32[]{:S(2)}) collective-permute-start(bf16[144,128]{1,0:T(8,128)(2,1)S(1)} %get-tuple-element.100), channel_id=1, source_target_pairs={{0,8},{4,12},{8,0},{12,4},{1,9},{5,13},{9,1},{13,5},{2,10},{6,14},... | collective-permute-start | bytes 110600 | tf_op jit(solution)/shard_map/ppermute | solution.py:96
  61.1 5.4 %collective-permute-start.24 = (bf16[144,128]{1,0:T(8,128)(2,1)S(1)}, bf16[144,128]{1,0:T(8,128)(2,1)S(1)}, u32[]{:S(2)}, u32[]{:S(2)}) collective-permute-start(bf16[144,128]{1,0:T(8,128)(2,1)S(1)} %get-tuple-element.101), channel_id=1, source_target_pairs={{0,4},{4,0},{8,12},{12,8},{1,5},{5,1},{9,13},{13,9},{2,6},{6,2},{1... | collective-permute-start | bytes 110600 | tf_op jit(solution)/shard_map/ppermute | solution.py:96
  66.5 1.9 %collective-permute-start.27 = (bf16[144,128]{1,0:T(8,128)(2,1)S(1)}, bf16[144,128]{1,0:T(8,128)(2,1)S(1)}, u32[]{:S(2)}, u32[]{:S(2)}) collective-permute-start(bf16[144,128]{1,0:T(8,128)(2,1)S(1)} %get-tuple-element.103.refs_3_), channel_id=1, source_target_pairs={{0,1},{1,0},{2,3},{3,2},{4,5},{5,4},{6,7},{7,6},{8,9},{9,8},{10,11... | collective-permute-start | bytes 110600 | tf_op jit(solution)/shard_map/ppermute | solution.py:96
  66.6 4.1 %collective-permute-start.26 = (bf16[144,128]{1,0:T(8,128)(2,1)S(1)}, bf16[144,128]{1,0:T(8,128)(2,1)S(1)}, u32[]{:S(2)}, u32[]{:S(2)}) collective-permute-start(bf16[144,128]{1,0:T(8,128)(2,1)S(1)} %get-tuple-element.103.refs_3_), channel_id=1, source_target_pairs={{0,2},{1,3},{2,0},{3,1},{4,6},{5,7},{6,4},{7,5},{8,10},{9,11},{10,... | collective-permute-start | bytes 110600 | tf_op jit(solution)/shard_map/ppermute | solution.py:96
  67.5 3.6 %collective-permute-start.25 = (bf16[144,128]{1,0:T(8,128)(2,1)S(1)}, bf16[144,128]{1,0:T(8,128)(2,1)S(1)}, u32[]{:S(2)}, u32[]{:S(2)}) collective-permute-start(bf16[144,128]{1,0:T(8,128)(2,1)S(1)} %get-tuple-element.103.refs_3_), channel_id=1, source_target_pairs={{0,3},{1,2},{2,1},{3,0},{4,7},{5,6},{6,5},{7,4},{8,11},{9,10},{10,... | collective-permute-start | bytes 110600 | tf_op jit(solution)/shard_map/ppermute | solution.py:96
  72.7 5.9 %collective-permute-start.28 = (bf16[144,128]{1,0:T(8,128)(2,1)S(1)}, bf16[144,128]{1,0:T(8,128)(2,1)S(1)}, u32[]{:S(2)}, u32[]{:S(2)}) collective-permute-start(bf16[144,128]{1,0:T(8,128)(2,1)S(1)} %get-tuple-element.114), channel_id=1, source_target_pairs={{0,12},{4,8},{8,4},{12,0},{1,13},{5,9},{9,5},{13,1},{2,14},{6,10},... | collective-permute-start | bytes 110600 | tf_op jit(solution)/shard_map/ppermute | solution.py:96
  74.4 5.5 %collective-permute-start.29 = (bf16[144,128]{1,0:T(8,128)(2,1)S(1)}, bf16[144,128]{1,0:T(8,128)(2,1)S(1)}, u32[]{:S(2)}, u32[]{:S(2)}) collective-permute-start(bf16[144,128]{1,0:T(8,128)(2,1)S(1)} %get-tuple-element.115), channel_id=1, source_target_pairs={{0,8},{4,12},{8,0},{12,4},{1,9},{5,13},{9,1},{13,5},{2,10},{6,14},... | collective-permute-start | bytes 110600 | tf_op jit(solution)/shard_map/ppermute | solution.py:96
  75.6 4.6 %collective-permute-start.30 = (bf16[144,128]{1,0:T(8,128)(2,1)S(1)}, bf16[144,128]{1,0:T(8,128)(2,1)S(1)}, u32[]{:S(2)}, u32[]{:S(2)}) collective-permute-start(bf16[144,128]{1,0:T(8,128)(2,1)S(1)} %get-tuple-element.116), channel_id=1, source_target_pairs={{0,4},{4,0},{8,12},{12,8},{1,5},{5,1},{9,13},{13,9},{2,6},{6,2},{1... | collective-permute-start | bytes 110600 | tf_op jit(solution)/shard_map/ppermute | solution.py:96
  80.3 2.8 %collective-permute-start.33 = (bf16[176,128]{1,0:T(8,128)(2,1)S(1)}, bf16[176,128]{1,0:T(8,128)(2,1)S(1)}, u32[]{:S(2)}, u32[]{:S(2)}) collective-permute-start(bf16[176,128]{1,0:T(8,128)(2,1)S(1)} %shard_map.135.refs_3_.mine), channel_id=1, source_target_pairs={{0,1},{1,0},{2,3},{3,2},{4,5},{5,4},{6,7},{7,6},{8,9},{9,8},{10,11... | collective-permute-start | bytes 135176 | tf_op jit(solution)/shard_map/ppermute | solution.py:96
  80.4 4.3 %collective-permute-start.32 = (bf16[176,128]{1,0:T(8,128)(2,1)S(1)}, bf16[176,128]{1,0:T(8,128)(2,1)S(1)}, u32[]{:S(2)}, u32[]{:S(2)}) collective-permute-start(bf16[176,128]{1,0:T(8,128)(2,1)S(1)} %shard_map.135.refs_3_.mine), channel_id=1, source_target_pairs={{0,2},{1,3},{2,0},{3,1},{4,6},{5,7},{6,4},{7,5},{8,10},{9,11},{10,... | collective-permute-start | bytes 135176 | tf_op jit(solution)/shard_map/ppermute | solution.py:96
  81.4 3.8 %collective-permute-start.31 = (bf16[176,128]{1,0:T(8,128)(2,1)S(1)}, bf16[176,128]{1,0:T(8,128)(2,1)S(1)}, u32[]{:S(2)}, u32[]{:S(2)}) collective-permute-start(bf16[176,128]{1,0:T(8,128)(2,1)S(1)} %shard_map.135.refs_3_.mine), channel_id=1, source_target_pairs={{0,3},{1,2},{2,1},{3,0},{4,7},{5,6},{6,5},{7,4},{8,11},{9,10},{10,... | collective-permute-start | bytes 135176 | tf_op jit(solution)/shard_map/ppermute | solution.py:96
  85.2 3.9 %collective-permute-start.34 = (bf16[128,128]{1,0:T(8,128)(2,1)S(1)}, bf16[128,128]{1,0:T(8,128)(2,1)S(1)}, u32[]{:S(2)}, u32[]{:S(2)}) collective-permute-start(bf16[128,128]{1,0:T(8,128)(2,1)S(1)} %shard_map.137.refs_0_), channel_id=1, source_target_pairs={{0,4},{4,0},{8,12},{12,8},{1,5},{5,1},{9,13},{13,9},{2,6},{6,2},{1... | collective-permute-start | bytes 98312 | tf_op jit(solution)/shard_map/ppermute | solution.py:96

commit v7 on v6

--- a/solution.py
+++ b/solution.py
@@ -103,7 +103,7 @@
 def share(x, axis):
     count = lax.axis_size(axis)
     if few(count):
-        return [flip(x, axis, k) for k in reversed(range(1, count))]
+        return [flip(x, axis, k) for k in range(1, count)]
     return [lax.all_gather(x, axis)]
 
 
@@ -121,6 +121,10 @@
 
 
 def away(refs, count, me, k):
+    return refs[k - 1] if len(refs) == count - 1 else refs[0].at[me ^ k]
+
+
+def parted(refs, count, me, k):
     return refs[count - 1 - k] if len(refs) == count - 1 else refs[0].at[me ^ k]
 
 
@@ -214,7 +218,7 @@
         if k == 0:
             own[...] = both
         else:
-            away(parts, z.cols, c, k)[...] = both.astype(BF16)
+            parted(parts, z.cols, c, k)[...] = both.astype(BF16)
 
 
 def first_kernel(z, count, *refs):
@@ -270,7 +274,7 @@
     _, c = place()
     total = own[...]
     for k in range(1, z.cols):
-        total = total + away(got, z.cols, c, k)[...].astype(F32)
+        total = total + parted(got, z.cols, c, k)[...].astype(F32)
     kept[...] = total
     if with_cot:
         cot = refs[1 + count]
@@ -333,14 +337,14 @@
             if k == z.half:
                 other = other + base[...]
             both = jnp.concatenate([pieces[k], other], axis=0)
-            away(parts, z.rows, p, k)[...] = both.astype(BF16)
+            parted(parts, z.rows, p, k)[...] = both.astype(BF16)
 
 
 def adjoints(z, own, got):
     p, _ = place()
     total = own[...]
     for k in range(1, z.rows):
-        total = total + away(got, z.rows, p, k)[...].astype(F32)
+        total = total + parted(got, z.rows, p, k)[...].astype(F32)
     return total
 
 
@@ -531,7 +535,7 @@
     )
     held_ids = [pltpu.SMEM((1, 2 * slots), jnp.int32), pltpu.SemaphoreType.DMA]
     if few(z.rows):
-        partner_message = got[z.rows - 1 - z.half]
+        partner_message = got[z.half - 1]
     else:
         partner_message = flip(message, "row", z.half)
     pre_sums = pltpu.VMEM((z.pre, batch, BLOCK), F32)

time: 91.8 us -> 89.2 us (0.972)
  waiting for transfers between devices: 35.5 us -> 30.5 us
  starting transfers between devices: 35.9 us -> 38.3 us
    ppermute x35, waiting for transfers between devices: 35.5 us -> 30.5 us  [flip(): return lax.ppermute(x, axis, [(i, i ^ k) for i in range(count)])]
    ppermute x35, starting transfers between devices: 35.9 us -> 38.3 us  [flip(): return lax.ppermute(x, axis, [(i, i ^ k) for i in range(count)])]
  transfers between devices with their start and end apart: 35 -> 35, of which waited for: 23 -> 22; matrix products, arithmetic and copies ran while one was open for 0% -> 0% of each run, Pallas kernels for 6% -> 6%
where the time goes in v7:
time: 89.2 us; the launch traced here: 89 us
  starting transfers between devices  38.3 us (43%)
  waiting for transfers between devices  30.5 us (34%)
  Pallas kernels  16.1 us (18%)
  local copies, waits for them, and re-layouts  3.22 us (4%)
    ppermute x35, starting transfers between devices, flip(): return lax.ppermute(x, axis, [(i, i ^ k) for i in range(count)])  38.3 us
    ppermute x35, waiting for transfers between devices, flip(): return lax.ppermute(x, axis, [(i, i ^ k) for i in range(count)])  30.5 us
    pallas_call x16, Pallas kernels, call(): pl.pallas_call(body, out_shape=outs, in_specs=specs, out_specs=out_specs...  10.7 us
    pallas_call x1, Pallas kernels, shards(): pl.pallas_call(functools.partial(grad_kernel, z, len(got), per_step), gri...  2.9 us
    pallas_call x1, Pallas kernels, shards(): pl.pallas_call(functools.partial(rest_kernel, z, len(all_extras), slots -...  2.49 us
    unnamed x12, local copies, waits for them, and re-layouts  2.41 us
  transfers between devices with their start and end apart: 35, of which 22 were waited for; matrix products, arithmetic and copies ran while one was open for 0% of the time, Pallas kernels for 6%

profile of v7, /device:TPU:0, one launch (start us, length us, event | category | flops | bytes accessed | tf_op | source)
XLA Modules:
  0.0 89.0 jit_solution(15979102370312781864)
XLA Ops:
  0.7 0.8 concatenate.3
  1.5 0.8 copy-done.4
  2.3 0.1 shard_map.121
  2.3 5.1 %collective-permute-start.2 = (bf16[96,128]{1,0:T(8,128)(2,1)S(1)}, bf16[96,128]{1,0:T(8,128)(2,1)S(1)}, u32[]{:S(2)}, u32[]{:S(2)}) collective-permute-start(bf16[96,128]{1,0:T(8,128)(2,1)S(1)} %get-tuple-element.63.after.refs_2_.refs_0_.mine), channel_id=1, source_target_pairs={{0,12},{4,8},{8,4},{12,0},{1,13},{5,9},{9,5},{13,1},{2,14},{6,10},... | collective-permute-start | bytes 73736 | tf_op jit(solution)/shard_map/ppermute | solution.py:96
  7.4 0.6 collective-permute-start
  8.0 1.6 %copy-done = bf16[1,1,64,128,128]{4,3,2,1,0:T(8,128)(2,1)S(1)} copy-done((bf16[1,1,64,128,128]{4,3,2,1,0:T(8,128)(2,1)S(1)}, bf16[1,1,64,128,128]{4,3,2,1,0:T(8,128)(2,1)}, u32[]{:S(2)}) %copy-start) | copy-done | bytes 2097176
  9.6 1.0 %shard_map.122.refs_1_ = bf16[64,128,128]{2,1,0:T(8,128)(2,1)S(1)} custom-call(bf16[96,128]{1,0:T(8,128)(2,1)S(1)} %get-tuple-element.63.after.refs_2_.refs_0_.mine, bf16[64,128,128]{2,1,0:T(8,128)(2,1)S(1)} %bitcast.9), custom_call_target="tpu_custom_call" | custom-call | bytes 4218880 | tf_op jit(solution)/shard_map/pallas_call | solution.py:78
  10.6 1.5 %collective-permute-done.1.refs_4_.refs_6_.partner = bf16[96,128]{1,0:T(8,128)(2,1)S(1)} collective-permute-done((bf16[96,128]{1,0:T(8,128)(2,1)S(1)}, bf16[96,128]{1,0:T(8,128)(2,1)S(1)}, u32[]{:S(2)}, u32[]{:S(2)}) %collective-permute-start.1) | collective-permute-done | bytes 24608 | tf_op jit(solution)/shard_map/ppermute | solution.py:96
  12.1 1.5 %shard_map.123 = (bf16[9,32,128]{2,1,0:T(8,128)(2,1)S(1)}, f32[144,128]{1,0:T(8,128)S(1)}, bf16[144,128]{1,0:T(8,128)(2,1)S(1)}, bf16[144,128]{1,0:T(8,128)(2,1)S(1)}, bf16[144,128]{1,0:T(8,128)(2,1)S(1)}) custom-call(s32[1,128]{1,0:T(1,128)S(1)} %get-tuple-element.62.refs_0_.near_ids, bf16[64,128,128]{2,1,0:T(8,128)(2,1)S(1)} %shard_map.122.refs_1_, ...), custom_call_target="tpu_custom_call" | custom-call | flops 67108864 | bytes 2454016 | tf_op jit(solution)/shard_map/pallas_call | solution.py:78
  13.7 1.6 %collective-permute-start.4 = (bf16[144,128]{1,0:T(8,128)(2,1)S(1)}, bf16[144,128]{1,0:T(8,128)(2,1)S(1)}, u32[]{:S(2)}, u32[]{:S(2)}) collective-permute-start(bf16[144,128]{1,0:T(8,128)(2,1)S(1)} %get-tuple-element.67), channel_id=1, source_target_pairs={{0,2},{1,3},{2,0},{3,1},{4,6},{5,7},{6,4},{7,5},{8,10},{9,11},{10,... | collective-permute-start | bytes 110600 | tf_op jit(solution)/shard_map/ppermute | solution.py:96
  15.2 0.3 collective-permute-start.5
  15.5 1.9 %collective-permute-done.3.refs_1_ = bf16[144,128]{1,0:T(8,128)(2,1)S(1)} collective-permute-done((bf16[144,128]{1,0:T(8,128)(2,1)S(1)}, bf16[144,128]{1,0:T(8,128)(2,1)S(1)}, u32[]{:S(2)}, u32[]{:S(2)}) %collective-permute-start.3) | collective-permute-done | bytes 36896 | tf_op jit(solution)/shard_map/ppermute | solution.py:96
  17.4 0.4 collective-permute-done.4.refs_2_
  17.9 2.4 %collective-permute-start.8 = (bf16[144,128]{1,0:T(8,128)(2,1)S(1)}, bf16[144,128]{1,0:T(8,128)(2,1)S(1)}, u32[]{:S(2)}, u32[]{:S(2)}) collective-permute-start(bf16[144,128]{1,0:T(8,128)(2,1)S(1)} %get-tuple-element.74), channel_id=1, source_target_pairs={{0,12},{4,8},{8,4},{12,0},{1,13},{5,9},{9,5},{13,1},{2,14},{6,10},... | collective-permute-start | bytes 110600 | tf_op jit(solution)/shard_map/ppermute | solution.py:96
  20.2 2.1 %collective-permute-start.6 = (bf16[144,128]{1,0:T(8,128)(2,1)S(1)}, bf16[144,128]{1,0:T(8,128)(2,1)S(1)}, u32[]{:S(2)}, u32[]{:S(2)}) collective-permute-start(bf16[144,128]{1,0:T(8,128)(2,1)S(1)} %get-tuple-element.74), channel_id=1, source_target_pairs={{0,4},{4,0},{8,12},{12,8},{1,5},{5,1},{9,13},{13,9},{2,6},{6,2},{1... | collective-permute-start | bytes 110600 | tf_op jit(solution)/shard_map/ppermute | solution.py:96
  22.3 0.9 %shard_map.125 = (f32[288,128]{1,0:T(8,128)S(1)}, f32[288,128]{1,0:T(8,128)S(1)}, f32[3,288,128]{2,1,0:T(8,128)S(1)}, f32[3,72,128]{2,1,0:T(8,128)S(1)}) custom-call(bf16[96,128]{1,0:T(8,128)(2,1)S(1)} %get-tuple-element.63.after.refs_2_.refs_0_.mine, f32[72,128]{1,0:T(8,128)S(1)} %get-tuple-element.70.refs_1_, f32[3,32,288]{2,1,0:T(8,128)S(1)} %copy-done.2, ...), custom_call_target="tpu_custom_call" | custom-call | bytes 1224704 | tf_op jit(solution)/shard_map/pallas_call | solution.py:78
  23.2 0.7 collective-permute-done.8.refs_8_
  24.0 1.3 %collective-permute-done.7.refs_7_ = bf16[144,128]{1,0:T(8,128)(2,1)S(1)} collective-permute-done((bf16[144,128]{1,0:T(8,128)(2,1)S(1)}, bf16[144,128]{1,0:T(8,128)(2,1)S(1)}, u32[]{:S(2)}, u32[]{:S(2)}) %collective-permute-start.7) | collective-permute-done | bytes 36896 | tf_op jit(solution)/shard_map/ppermute | solution.py:96
  25.3 1.6 %shard_map.126 = (f32[288,128]{1,0:T(8,128)S(1)}, f32[144,128]{1,0:T(8,128)S(1)}, f32[144,128]{1,0:T(8,128)S(1)}, bf16[9,32,128]{2,1,0:T(8,128)(2,1)S(1)}, f32[1...) custom-call(s32[1,128]{1,0:T(1,128)S(1)} %get-tuple-element.62.refs_, ...), custom_call_target="tpu_custom_call" | custom-call | flops 67108864 | bytes 3572224 | tf_op jit(solution)/shard_map/pallas_call | solution.py:78
  26.9 1.6 %collective-permute-start.10 = (bf16[144,128]{1,0:T(8,128)(2,1)S(1)}, bf16[144,128]{1,0:T(8,128)(2,1)S(1)}, u32[]{:S(2)}, u32[]{:S(2)}) collective-permute-start(bf16[144,128]{1,0:T(8,128)(2,1)S(1)} %get-tuple-element.78), channel_id=1, source_target_pairs={{0,2},{1,3},{2,0},{3,1},{4,6},{5,7},{6,4},{7,5},{8,10},{9,11},{10,... | collective-permute-start | bytes 110600 | tf_op jit(solution)/shard_map/ppermute | solution.py:96
  28.5 0.3 collective-permute-start.11
  28.7 1.9 %collective-permute-done.9.refs_1_ = bf16[144,128]{1,0:T(8,128)(2,1)S(1)} collective-permute-done((bf16[144,128]{1,0:T(8,128)(2,1)S(1)}, bf16[144,128]{1,0:T(8,128)(2,1)S(1)}, u32[]{:S(2)}, u32[]{:S(2)}) %collective-permute-start.9) | collective-permute-done | bytes 36896 | tf_op jit(solution)/shard_map/ppermute | solution.py:96
  30.6 0.5 collective-permute-done.10.refs_2_
  31.1 3.0 %collective-permute-start.14 = (bf16[144,128]{1,0:T(8,128)(2,1)S(1)}, bf16[144,128]{1,0:T(8,128)(2,1)S(1)}, u32[]{:S(2)}, u32[]{:S(2)}) collective-permute-start(bf16[144,128]{1,0:T(8,128)(2,1)S(1)} %get-tuple-element.82), channel_id=1, source_target_pairs={{0,12},{4,8},{8,4},{12,0},{1,13},{5,9},{9,5},{13,1},{2,14},{6,10},... | collective-permute-start | bytes 110600 | tf_op jit(solution)/shard_map/ppermute | solution.py:96
  34.1 1.4 %collective-permute-start.12 = (bf16[144,128]{1,0:T(8,128)(2,1)S(1)}, bf16[144,128]{1,0:T(8,128)(2,1)S(1)}, u32[]{:S(2)}, u32[]{:S(2)}) collective-permute-start(bf16[144,128]{1,0:T(8,128)(2,1)S(1)} %get-tuple-element.82), channel_id=1, source_target_pairs={{0,4},{4,0},{8,12},{12,8},{1,5},{5,1},{9,13},{13,9},{2,6},{6,2},{1... | collective-permute-start | bytes 110600 | tf_op jit(solution)/shard_map/ppermute | solution.py:96
  35.5 1.7 %collective-permute-done.14.refs_8_ = bf16[144,128]{1,0:T(8,128)(2,1)S(1)} collective-permute-done((bf16[144,128]{1,0:T(8,128)(2,1)S(1)}, bf16[144,128]{1,0:T(8,128)(2,1)S(1)}, u32[]{:S(2)}, u32[]{:S(2)}) %collective-permute-start.14) | collective-permute-done | bytes 36896 | tf_op jit(solution)/shard_map/ppermute | solution.py:96
  37.2 1.7 %collective-permute-done.13.refs_7_ = bf16[144,128]{1,0:T(8,128)(2,1)S(1)} collective-permute-done((bf16[144,128]{1,0:T(8,128)(2,1)S(1)}, bf16[144,128]{1,0:T(8,128)(2,1)S(1)}, u32[]{:S(2)}, u32[]{:S(2)}) %collective-permute-start.13) | collective-permute-done | bytes 36896 | tf_op jit(solution)/shard_map/ppermute | solution.py:96
  39.0 1.6 %shard_map.128 = (f32[288,128]{1,0:T(8,128)S(1)}, f32[144,128]{1,0:T(8,128)S(1)}, f32[144,128]{1,0:T(8,128)S(1)}, bf16[9,32,128]{2,1,0:T(8,128)(2,1)S(1)}, f32[1...) custom-call(s32[1,128]{1,0:T(1,128)S(1)} %get-tuple-element.62.refs_, ...), custom_call_target="tpu_custom_call" | custom-call | flops 67108864 | bytes 3572224 | tf_op jit(solution)/shard_map/pallas_call | solution.py:78
  40.6 1.0 %collective-permute-start.16 = (bf16[144,128]{1,0:T(8,128)(2,1)S(1)}, bf16[144,128]{1,0:T(8,128)(2,1)S(1)}, u32[]{:S(2)}, u32[]{:S(2)}) collective-permute-start(bf16[144,128]{1,0:T(8,128)(2,1)S(1)} %get-tuple-element.86), channel_id=1, source_target_pairs={{0,2},{1,3},{2,0},{3,1},{4,6},{5,7},{6,4},{7,5},{8,10},{9,11},{10,... | collective-permute-start | bytes 110600 | tf_op jit(solution)/shard_map/ppermute | solution.py:96
  41.5 0.9 %collective-permute-start.17 = (bf16[144,128]{1,0:T(8,128)(2,1)S(1)}, bf16[144,128]{1,0:T(8,128)(2,1)S(1)}, u32[]{:S(2)}, u32[]{:S(2)}) collective-permute-start(bf16[144,128]{1,0:T(8,128)(2,1)S(1)} %get-tuple-element.87), channel_id=1, source_target_pairs={{0,1},{1,0},{2,3},{3,2},{4,5},{5,4},{6,7},{7,6},{8,9},{9,8},{10,11... | collective-permute-start | bytes 110600 | tf_op jit(solution)/shard_map/ppermute | solution.py:96
  42.4 1.5 %collective-permute-done.15.refs_1_ = bf16[144,128]{1,0:T(8,128)(2,1)S(1)} collective-permute-done((bf16[144,128]{1,0:T(8,128)(2,1)S(1)}, bf16[144,128]{1,0:T(8,128)(2,1)S(1)}, u32[]{:S(2)}, u32[]{:S(2)}) %collective-permute-start.15) | collective-permute-done | bytes 36896 | tf_op jit(solution)/shard_map/ppermute | solution.py:96
  44.0 1.0 %collective-permute-done.16.refs_2_ = bf16[144,128]{1,0:T(8,128)(2,1)S(1)} collective-permute-done((bf16[144,128]{1,0:T(8,128)(2,1)S(1)}, bf16[144,128]{1,0:T(8,128)(2,1)S(1)}, u32[]{:S(2)}, u32[]{:S(2)}) %collective-permute-start.16) | collective-permute-done | bytes 36896 | tf_op jit(solution)/shard_map/ppermute | solution.py:96
  45.0 2.1 %collective-permute-start.18 = (bf16[224,128]{1,0:T(8,128)(2,1)S(1)}, bf16[224,128]{1,0:T(8,128)(2,1)S(1)}, u32[]{:S(2)}, u32[]{:S(2)}) collective-permute-start(bf16[224,128]{1,0:T(8,128)(2,1)S(1)} %get-tuple-element.90), channel_id=1, source_target_pairs={{0,8},{4,12},{8,0},{12,4},{1,9},{5,13},{9,1},{13,5},{2,10},{6,14},... | collective-permute-start | bytes 172040 | tf_op jit(solution)/shard_map/ppermute | solution.py:96
  47.1 4.0 %collective-permute-done.18.theirs = bf16[224,128]{1,0:T(8,128)(2,1)S(1)} collective-permute-done((bf16[224,128]{1,0:T(8,128)(2,1)S(1)}, bf16[224,128]{1,0:T(8,128)(2,1)S(1)}, u32[]{:S(2)}, u32[]{:S(2)}) %collective-permute-start.18) | collective-permute-done | bytes 57376 | tf_op jit(solution)/shard_map/ppermute | solution.py:96
  51.1 0.2 collective-permute-start.21
  51.3 1.5 %collective-permute-start.20 = (bf16[144,128]{1,0:T(8,128)(2,1)S(1)}, bf16[144,128]{1,0:T(8,128)(2,1)S(1)}, u32[]{:S(2)}, u32[]{:S(2)}) collective-permute-start(bf16[144,128]{1,0:T(8,128)(2,1)S(1)} %get-tuple-element.93.refs_3_), channel_id=1, source_target_pairs={{0,2},{1,3},{2,0},{3,1},{4,6},{5,7},{6,4},{7,5},{8,10},{9,11},{10,... | collective-permute-start | bytes 110600 | tf_op jit(solution)/shard_map/ppermute | solution.py:96
  52.8 0.2 collective-permute-start.19
  53.0 1.7 %collective-permute-done.21.refs_6_ = bf16[144,128]{1,0:T(8,128)(2,1)S(1)} collective-permute-done((bf16[144,128]{1,0:T(8,128)(2,1)S(1)}, bf16[144,128]{1,0:T(8,128)(2,1)S(1)}, u32[]{:S(2)}, u32[]{:S(2)}) %collective-permute-start.21) | collective-permute-done | bytes 36896 | tf_op jit(solution)/shard_map/ppermute | solution.py:96
  54.7 1.0 %collective-permute-done.20.refs_5_ = bf16[144,128]{1,0:T(8,128)(2,1)S(1)} collective-permute-done((bf16[144,128]{1,0:T(8,128)(2,1)S(1)}, bf16[144,128]{1,0:T(8,128)(2,1)S(1)}, u32[]{:S(2)}, u32[]{:S(2)}) %collective-permute-start.20) | collective-permute-done | bytes 36896 | tf_op jit(solution)/shard_map/ppermute | solution.py:96
  55.7 1.5 %shard_map.131 = (bf16[18,32,128]{2,1,0:T(8,128)(2,1)S(1)}, f32[144,128]{1,0:T(8,128)S(1)}, bf16[144,128]{1,0:T(8,128)(2,1)S(1)}, bf16[144,128]{1,0:T(8,128)(2,1)S(1)}, bf16[144,128]{1,0:T(8,128)(2,1)S(1)}) custom-call(s32[1,128]{1,0:T(1,128)S(1)} %get-tuple-element.62.refs_0_.near_ids, bf16[64,128,128]{2,1,0:T(8,128)(2,1)S(1)} %bitcast.10, ...), custom_call_target="tpu_custom_call" | custom-call | flops 67108864 | bytes 2613760 | tf_op jit(solution)/shard_map/pallas_call | solution.py:78
  57.3 2.3 %collective-permute-start.22 = (bf16[144,128]{1,0:T(8,128)(2,1)S(1)}, bf16[144,128]{1,0:T(8,128)(2,1)S(1)}, u32[]{:S(2)}, u32[]{:S(2)}) collective-permute-start(bf16[144,128]{1,0:T(8,128)(2,1)S(1)} %get-tuple-element.99), channel_id=1, source_target_pairs={{0,12},{4,8},{8,4},{12,0},{1,13},{5,9},{9,5},{13,1},{2,14},{6,10},... | collective-permute-start | bytes 110600 | tf_op jit(solution)/shard_map/ppermute | solution.py:96
  59.5 2.2 %collective-permute-start.24 = (bf16[144,128]{1,0:T(8,128)(2,1)S(1)}, bf16[144,128]{1,0:T(8,128)(2,1)S(1)}, u32[]{:S(2)}, u32[]{:S(2)}) collective-permute-start(bf16[144,128]{1,0:T(8,128)(2,1)S(1)} %get-tuple-element.101), channel_id=1, source_target_pairs={{0,4},{4,0},{8,12},{12,8},{1,5},{5,1},{9,13},{13,9},{2,6},{6,2},{1... | collective-permute-start | bytes 110600 | tf_op jit(solution)/shard_map/ppermute | solution.py:96
  61.7 1.4 %collective-permute-done.22.refs_0_ = bf16[144,128]{1,0:T(8,128)(2,1)S(1)} collective-permute-done((bf16[144,128]{1,0:T(8,128)(2,1)S(1)}, bf16[144,128]{1,0:T(8,128)(2,1)S(1)}, u32[]{:S(2)}, u32[]{:S(2)}) %collective-permute-start.22) | collective-permute-done | bytes 36896 | tf_op jit(solution)/shard_map/ppermute | solution.py:96
  63.1 1.3 %collective-permute-done.23.refs_1_ = bf16[144,128]{1,0:T(8,128)(2,1)S(1)} collective-permute-done((bf16[144,128]{1,0:T(8,128)(2,1)S(1)}, bf16[144,128]{1,0:T(8,128)(2,1)S(1)}, u32[]{:S(2)}, u32[]{:S(2)}) %collective-permute-start.23) | collective-permute-done | bytes 36896 | tf_op jit(solution)/shard_map/ppermute | solution.py:96
  64.5 0.2 collective-permute-start.27
  64.7 0.9 collective-permute-start.26
  65.6 0.8 collective-permute-start.25
  66.4 1.5 %collective-permute-done.27.refs_6_ = bf16[144,128]{1,0:T(8,128)(2,1)S(1)} collective-permute-done((bf16[144,128]{1,0:T(8,128)(2,1)S(1)}, bf16[144,128]{1,0:T(8,128)(2,1)S(1)}, u32[]{:S(2)}, u32[]{:S(2)}) %collective-permute-start.27) | collective-permute-done | bytes 36896 | tf_op jit(solution)/shard_map/ppermute | solution.py:96
  67.9 1.0 %collective-permute-done.26.refs_5_ = bf16[144,128]{1,0:T(8,128)(2,1)S(1)} collective-permute-done((bf16[144,128]{1,0:T(8,128)(2,1)S(1)}, bf16[144,128]{1,0:T(8,128)(2,1)S(1)}, u32[]{:S(2)}, u32[]{:S(2)}) %collective-permute-start.26) | collective-permute-done | bytes 36896 | tf_op jit(solution)/shard_map/ppermute | solution.py:96
  68.9 1.5 %shard_map.133 = (bf16[18,32,128]{2,1,0:T(8,128)(2,1)S(1)}, f32[144,128]{1,0:T(8,128)S(1)}, bf16[144,128]{1,0:T(8,128)(2,1)S(1)}, bf16[144,128]{1,0:T(8,128)(2,1)S(1)}, bf16[144,128]{1,0:T(8,128)(2,1)S(1)}) custom-call(s32[1,128]{1,0:T(1,128)S(1)} %get-tuple-element.62.refs_0_.near_ids, bf16[64,128,128]{2,1,0:T(8,128)(2,1)S(1)} %bitcast.11, ...), custom_call_target="tpu_custom_call" | custom-call | flops 67108864 | bytes 2613760 | tf_op jit(solution)/shard_map/pallas_call | solution.py:78
  70.4 2.3 %collective-permute-start.28 = (bf16[144,128]{1,0:T(8,128)(2,1)S(1)}, bf16[144,128]{1,0:T(8,128)(2,1)S(1)}, u32[]{:S(2)}, u32[]{:S(2)}) collective-permute-start(bf16[144,128]{1,0:T(8,128)(2,1)S(1)} %get-tuple-element.114), channel_id=1, source_target_pairs={{0,12},{4,8},{8,4},{12,0},{1,13},{5,9},{9,5},{13,1},{2,14},{6,10},... | collective-permute-start | bytes 110600 | tf_op jit(solution)/shard_map/ppermute | solution.py:96
  72.8 0.4 collective-permute-start.29
  73.2 1.7 %collective-permute-start.30 = (bf16[144,128]{1,0:T(8,128)(2,1)S(1)}, bf16[144,128]{1,0:T(8,128)(2,1)S(1)}, u32[]{:S(2)}, u32[]{:S(2)}) collective-permute-start(bf16[144,128]{1,0:T(8,128)(2,1)S(1)} %get-tuple-element.116), channel_id=1, source_target_pairs={{0,4},{4,0},{8,12},{12,8},{1,5},{5,1},{9,13},{13,9},{2,6},{6,2},{1... | collective-permute-start | bytes 110600 | tf_op jit(solution)/shard_map/ppermute | solution.py:96
  74.9 1.4 %collective-permute-done.28.refs_0_ = bf16[144,128]{1,0:T(8,128)(2,1)S(1)} collective-permute-done((bf16[144,128]{1,0:T(8,128)(2,1)S(1)}, bf16[144,128]{1,0:T(8,128)(2,1)S(1)}, u32[]{:S(2)}, u32[]{:S(2)}) %collective-permute-start.28) | collective-permute-done | bytes 36896 | tf_op jit(solution)/shard_map/ppermute | solution.py:96
  76.3 1.3 %collective-permute-done.29.refs_1_ = bf16[144,128]{1,0:T(8,128)(2,1)S(1)} collective-permute-done((bf16[144,128]{1,0:T(8,128)(2,1)S(1)}, bf16[144,128]{1,0:T(8,128)(2,1)S(1)}, u32[]{:S(2)}, u32[]{:S(2)}) %collective-permute-start.29) | collective-permute-done | bytes 36896 | tf_op jit(solution)/shard_map/ppermute | solution.py:96
  77.6 0.1 shard_map.135.refs_3_.mine
  77.8 1.3 %collective-permute-start.32 = (bf16[176,128]{1,0:T(8,128)(2,1)S(1)}, bf16[176,128]{1,0:T(8,128)(2,1)S(1)}, u32[]{:S(2)}, u32[]{:S(2)}) collective-permute-start(bf16[176,128]{1,0:T(8,128)(2,1)S(1)} %shard_map.135.refs_3_.mine), channel_id=1, source_target_pairs={{0,2},{1,3},{2,0},{3,1},{4,6},{5,7},{6,4},{7,5},{8,10},{9,11},{10,... | collective-permute-start | bytes 135176 | tf_op jit(solution)/shard_map/ppermute | solution.py:96
  79.1 0.5 collective-permute-start.31
  79.7 0.8 shard_map.134
  80.5 1.2 %collective-permute-done.33.refs_6_.refs_2_ = bf16[176,128]{1,0:T(8,128)(2,1)S(1)} collective-permute-done((bf16[176,128]{1,0:T(8,128)(2,1)S(1)}, bf16[176,128]{1,0:T(8,128)(2,1)S(1)}, u32[]{:S(2)}, u32[]{:S(2)}) %collective-permute-start.33) | collective-permute-done | bytes 45088 | tf_op jit(solution)/shard_map/ppermute | solution.py:96
  81.7 0.6 collective-permute-done.32.refs_5_.refs_1_
  82.3 1.2 %collective-permute-start.34 = (bf16[128,128]{1,0:T(8,128)(2,1)S(1)}, bf16[128,128]{1,0:T(8,128)(2,1)S(1)}, u32[]{:S(2)}, u32[]{:S(2)}) collective-permute-start(bf16[128,128]{1,0:T(8,128)(2,1)S(1)} %shard_map.137.refs_0_), channel_id=1, source_target_pairs={{0,4},{4,0},{8,12},{12,8},{1,5},{5,1},{9,13},{13,9},{2,6},{6,2},{1... | collective-permute-start | bytes 98312 | tf_op jit(solution)/shard_map/ppermute | solution.py:96
  83.6 2.9 %shard_map.136 = (bf16[18,128,128]{2,1,0:T(8,128)(2,1)S(1)}, bf16[64,128,128]{2,1,0:T(8,128)(2,1)}) custom-call(s32[1,128]{1,0:T(1,128)S(1)} %get-tuple-element.62.refs_0_.near_ids, bf16[9,128,128]{2,1,0:T(8,128)(2,1)S(1)} %get-tuple-element.108.refs_1_.right, bf16[18,128,128]{2,1,0:T(8,128)(2,1)S(1)} %get-tuple-element.109.refs_2_, ...), custom_call_target="tpu_custom_call" | custom-call | flops 268435456 | bytes 4194304 | tf_op jit(solution)/shard_map/pallas_call | solution.py:654
  86.5 2.5 %shard_map.138 = (bf16[64,128,128]{2,1,0:T(8,128)(2,1)}, f32[64,128]{1,0:T(8,128)}) custom-call(s32[1,128]{1,0:T(1,128)S(1)} %get-tuple-element.62.refs_0_.near_ids, bf16[18,128,128]{2,1,0:T(8,128)(2,1)S(1)} %get-tuple-element.117.left, bf16[9,128,128]{2,1,0:T(8,128)(2,1)S(1)} %get-tuple-element.108.refs_1_.right, ...), custom_call_target="tpu_custom_call", output_to_operand_aliasing={{0}: (3, {})} | custom-call | flops 268435456 | bytes 4194304 | tf_op jit(solution)/shard_map/pallas_call | solution.py:665
  (39 shorter events, 0.5 us)
Async XLA Ops:
  1.5 0.8 copy-start.4
  2.3 8.3 %collective-permute-start.2 = (bf16[96,128]{1,0:T(8,128)(2,1)S(1)}, bf16[96,128]{1,0:T(8,128)(2,1)S(1)}, u32[]{:S(2)}, u32[]{:S(2)}) collective-permute-start(bf16[96,128]{1,0:T(8,128)(2,1)S(1)} %get-tuple-element.63.after.refs_2_.refs_0_.mine), channel_id=1, source_target_pairs={{0,12},{4,8},{8,4},{12,0},{1,13},{5,9},{9,5},{13,1},{2,14},{6,10},... | collective-permute-start | bytes 73736 | tf_op jit(solution)/shard_map/ppermute | solution.py:96
  7.4 4.7 %collective-permute-start.1 = (bf16[96,128]{1,0:T(8,128)(2,1)S(1)}, bf16[96,128]{1,0:T(8,128)(2,1)S(1)}, u32[]{:S(2)}, u32[]{:S(2)}) collective-permute-start(bf16[96,128]{1,0:T(8,128)(2,1)S(1)} %get-tuple-element.63.after.refs_2_.refs_0_.mine), channel_id=1, source_target_pairs={{0,8},{4,12},{8,0},{12,4},{1,9},{5,13},{9,1},{13,5},{2,10},{6,14},... | collective-permute-start | bytes 73736 | tf_op jit(solution)/shard_map/ppermute | solution.py:96
  7.4 4.7 %collective-permute-start = (bf16[96,128]{1,0:T(8,128)(2,1)S(1)}, bf16[96,128]{1,0:T(8,128)(2,1)S(1)}, u32[]{:S(2)}, u32[]{:S(2)}) collective-permute-start(bf16[96,128]{1,0:T(8,128)(2,1)S(1)} %get-tuple-element.63.after.refs_2_.refs_0_.mine), channel_id=1, source_target_pairs={{0,4},{4,0},{8,12},{12,8},{1,5},{5,1},{9,13},{13,9},{2,6},{6,2},{1... | collective-permute-start | bytes 73736 | tf_op jit(solution)/shard_map/ppermute | solution.py:96
  8.0 1.6 %copy-start = (bf16[1,1,64,128,128]{4,3,2,1,0:T(8,128)(2,1)S(1)}, bf16[1,1,64,128,128]{4,3,2,1,0:T(8,128)(2,1)}, u32[]{:S(2)}) copy-start(bf16[1,1,64,128,128]{4,3,2,1,0:T(8,128)(2,1)} %param.13) | copy-start | bytes 6291460
  10.6 11.7 %copy-start.2 = (f32[3,32,288]{2,1,0:T(8,128)S(1)}, f32[3,32,288]{2,1,0:T(8,128)}, u32[]{:S(2)}) copy-start(f32[3,32,288]{2,1,0:T(8,128)} %refs_2_.1) | copy-start | bytes 331780
  10.6 11.7 %copy-start.3 = (bf16[3,32,512]{2,1,0:T(8,128)(2,1)S(1)}, bf16[3,32,512]{2,1,0:T(8,128)(2,1)}, u32[]{:S(2)}) copy-start(bf16[3,32,512]{2,1,0:T(8,128)(2,1)} %param.11) | copy-start | bytes 294916
  10.6 11.7 %copy-start.5 = (f32[8192]{0:T(1024)S(1)}, f32[8192]{0:T(1024)}, u32[]{:S(2)}) copy-start(f32[8192]{0:T(1024)} %param.18) | copy-start | bytes 98308
  13.6 3.8 %collective-permute-start.3 = (bf16[144,128]{1,0:T(8,128)(2,1)S(1)}, bf16[144,128]{1,0:T(8,128)(2,1)S(1)}, u32[]{:S(2)}, u32[]{:S(2)}) collective-permute-start(bf16[144,128]{1,0:T(8,128)(2,1)S(1)} %get-tuple-element.66), channel_id=1, source_target_pairs={{0,3},{1,2},{2,1},{3,0},{4,7},{5,6},{6,5},{7,4},{8,11},{9,10},{10,... | collective-permute-start | bytes 110600 | tf_op jit(solution)/shard_map/ppermute | solution.py:96
  13.7 4.2 %collective-permute-start.4 = (bf16[144,128]{1,0:T(8,128)(2,1)S(1)}, bf16[144,128]{1,0:T(8,128)(2,1)S(1)}, u32[]{:S(2)}, u32[]{:S(2)}) collective-permute-start(bf16[144,128]{1,0:T(8,128)(2,1)S(1)} %get-tuple-element.67), channel_id=1, source_target_pairs={{0,2},{1,3},{2,0},{3,1},{4,6},{5,7},{6,4},{7,5},{8,10},{9,11},{10,... | collective-permute-start | bytes 110600 | tf_op jit(solution)/shard_map/ppermute | solution.py:96
  15.2 2.6 %collective-permute-start.5 = (bf16[144,128]{1,0:T(8,128)(2,1)S(1)}, bf16[144,128]{1,0:T(8,128)(2,1)S(1)}, u32[]{:S(2)}, u32[]{:S(2)}) collective-permute-start(bf16[144,128]{1,0:T(8,128)(2,1)S(1)} %get-tuple-element.68), channel_id=1, source_target_pairs={{0,1},{1,0},{2,3},{3,2},{4,5},{5,4},{6,7},{7,6},{8,9},{9,8},{10,11... | collective-permute-start | bytes 110600 | tf_op jit(solution)/shard_map/ppermute | solution.py:96
  17.9 6.1 %collective-permute-start.8 = (bf16[144,128]{1,0:T(8,128)(2,1)S(1)}, bf16[144,128]{1,0:T(8,128)(2,1)S(1)}, u32[]{:S(2)}, u32[]{:S(2)}) collective-permute-start(bf16[144,128]{1,0:T(8,128)(2,1)S(1)} %get-tuple-element.74), channel_id=1, source_target_pairs={{0,12},{4,8},{8,4},{12,0},{1,13},{5,9},{9,5},{13,1},{2,14},{6,10},... | collective-permute-start | bytes 110600 | tf_op jit(solution)/shard_map/ppermute | solution.py:96
  20.2 5.0 %collective-permute-start.7 = (bf16[144,128]{1,0:T(8,128)(2,1)S(1)}, bf16[144,128]{1,0:T(8,128)(2,1)S(1)}, u32[]{:S(2)}, u32[]{:S(2)}) collective-permute-start(bf16[144,128]{1,0:T(8,128)(2,1)S(1)} %get-tuple-element.74), channel_id=1, source_target_pairs={{0,8},{4,12},{8,0},{12,4},{1,9},{5,13},{9,1},{13,5},{2,10},{6,14},... | collective-permute-start | bytes 110600 | tf_op jit(solution)/shard_map/ppermute | solution.py:96
  20.2 5.0 %collective-permute-start.6 = (bf16[144,128]{1,0:T(8,128)(2,1)S(1)}, bf16[144,128]{1,0:T(8,128)(2,1)S(1)}, u32[]{:S(2)}, u32[]{:S(2)}) collective-permute-start(bf16[144,128]{1,0:T(8,128)(2,1)S(1)} %get-tuple-element.74), channel_id=1, source_target_pairs={{0,4},{4,0},{8,12},{12,8},{1,5},{5,1},{9,13},{13,9},{2,6},{6,2},{1... | collective-permute-start | bytes 110600 | tf_op jit(solution)/shard_map/ppermute | solution.py:96
  26.8 3.8 %collective-permute-start.9 = (bf16[144,128]{1,0:T(8,128)(2,1)S(1)}, bf16[144,128]{1,0:T(8,128)(2,1)S(1)}, u32[]{:S(2)}, u32[]{:S(2)}) collective-permute-start(bf16[144,128]{1,0:T(8,128)(2,1)S(1)} %get-tuple-element.77), channel_id=1, source_target_pairs={{0,3},{1,2},{2,1},{3,0},{4,7},{5,6},{6,5},{7,4},{8,11},{9,10},{10,... | collective-permute-start | bytes 110600 | tf_op jit(solution)/shard_map/ppermute | solution.py:96
  26.9 4.2 %collective-permute-start.10 = (bf16[144,128]{1,0:T(8,128)(2,1)S(1)}, bf16[144,128]{1,0:T(8,128)(2,1)S(1)}, u32[]{:S(2)}, u32[]{:S(2)}) collective-permute-start(bf16[144,128]{1,0:T(8,128)(2,1)S(1)} %get-tuple-element.78), channel_id=1, source_target_pairs={{0,2},{1,3},{2,0},{3,1},{4,6},{5,7},{6,4},{7,5},{8,10},{9,11},{10,... | collective-permute-start | bytes 110600 | tf_op jit(solution)/shard_map/ppermute | solution.py:96
  28.5 2.6 %collective-permute-start.11 = (bf16[144,128]{1,0:T(8,128)(2,1)S(1)}, bf16[144,128]{1,0:T(8,128)(2,1)S(1)}, u32[]{:S(2)}, u32[]{:S(2)}) collective-permute-start(bf16[144,128]{1,0:T(8,128)(2,1)S(1)} %get-tuple-element.79), channel_id=1, source_target_pairs={{0,1},{1,0},{2,3},{3,2},{4,5},{5,4},{6,7},{7,6},{8,9},{9,8},{10,11... | collective-permute-start | bytes 110600 | tf_op jit(solution)/shard_map/ppermute | solution.py:96
  31.1 6.2 %collective-permute-start.14 = (bf16[144,128]{1,0:T(8,128)(2,1)S(1)}, bf16[144,128]{1,0:T(8,128)(2,1)S(1)}, u32[]{:S(2)}, u32[]{:S(2)}) collective-permute-start(bf16[144,128]{1,0:T(8,128)(2,1)S(1)} %get-tuple-element.82), channel_id=1, source_target_pairs={{0,12},{4,8},{8,4},{12,0},{1,13},{5,9},{9,5},{13,1},{2,14},{6,10},... | collective-permute-start | bytes 110600 | tf_op jit(solution)/shard_map/ppermute | solution.py:96
  34.1 4.9 %collective-permute-start.13 = (bf16[144,128]{1,0:T(8,128)(2,1)S(1)}, bf16[144,128]{1,0:T(8,128)(2,1)S(1)}, u32[]{:S(2)}, u32[]{:S(2)}) collective-permute-start(bf16[144,128]{1,0:T(8,128)(2,1)S(1)} %get-tuple-element.82), channel_id=1, source_target_pairs={{0,8},{4,12},{8,0},{12,4},{1,9},{5,13},{9,1},{13,5},{2,10},{6,14},... | collective-permute-start | bytes 110600 | tf_op jit(solution)/shard_map/ppermute | solution.py:96
  34.1 4.9 %collective-permute-start.12 = (bf16[144,128]{1,0:T(8,128)(2,1)S(1)}, bf16[144,128]{1,0:T(8,128)(2,1)S(1)}, u32[]{:S(2)}, u32[]{:S(2)}) collective-permute-start(bf16[144,128]{1,0:T(8,128)(2,1)S(1)} %get-tuple-element.82), channel_id=1, source_target_pairs={{0,4},{4,0},{8,12},{12,8},{1,5},{5,1},{9,13},{13,9},{2,6},{6,2},{1... | collective-permute-start | bytes 110600 | tf_op jit(solution)/shard_map/ppermute | solution.py:96
  38.9 16.8 %copy-start.1 = (bf16[1,1,64,128,128]{4,3,2,1,0:T(8,128)(2,1)S(1)}, bf16[1,1,64,128,128]{4,3,2,1,0:T(8,128)(2,1)}, u32[]{:S(2)}) copy-start(bf16[1,1,64,128,128]{4,3,2,1,0:T(8,128)(2,1)} %param.13) | copy-start | bytes 6291460
  40.5 3.4 %collective-permute-start.15 = (bf16[144,128]{1,0:T(8,128)(2,1)S(1)}, bf16[144,128]{1,0:T(8,128)(2,1)S(1)}, u32[]{:S(2)}, u32[]{:S(2)}) collective-permute-start(bf16[144,128]{1,0:T(8,128)(2,1)S(1)} %get-tuple-element.85), channel_id=1, source_target_pairs={{0,3},{1,2},{2,1},{3,0},{4,7},{5,6},{6,5},{7,4},{8,11},{9,10},{10,... | collective-permute-start | bytes 110600 | tf_op jit(solution)/shard_map/ppermute | solution.py:96
  40.6 4.4 %collective-permute-start.16 = (bf16[144,128]{1,0:T(8,128)(2,1)S(1)}, bf16[144,128]{1,0:T(8,128)(2,1)S(1)}, u32[]{:S(2)}, u32[]{:S(2)}) collective-permute-start(bf16[144,128]{1,0:T(8,128)(2,1)S(1)} %get-tuple-element.86), channel_id=1, source_target_pairs={{0,2},{1,3},{2,0},{3,1},{4,6},{5,7},{6,4},{7,5},{8,10},{9,11},{10,... | collective-permute-start | bytes 110600 | tf_op jit(solution)/shard_map/ppermute | solution.py:96
  41.5 3.4 %collective-permute-start.17 = (bf16[144,128]{1,0:T(8,128)(2,1)S(1)}, bf16[144,128]{1,0:T(8,128)(2,1)S(1)}, u32[]{:S(2)}, u32[]{:S(2)}) collective-permute-start(bf16[144,128]{1,0:T(8,128)(2,1)S(1)} %get-tuple-element.87), channel_id=1, source_target_pairs={{0,1},{1,0},{2,3},{3,2},{4,5},{5,4},{6,7},{7,6},{8,9},{9,8},{10,11... | collective-permute-start | bytes 110600 | tf_op jit(solution)/shard_map/ppermute | solution.py:96
  45.0 6.0 %collective-permute-start.18 = (bf16[224,128]{1,0:T(8,128)(2,1)S(1)}, bf16[224,128]{1,0:T(8,128)(2,1)S(1)}, u32[]{:S(2)}, u32[]{:S(2)}) collective-permute-start(bf16[224,128]{1,0:T(8,128)(2,1)S(1)} %get-tuple-element.90), channel_id=1, source_target_pairs={{0,8},{4,12},{8,0},{12,4},{1,9},{5,13},{9,1},{13,5},{2,10},{6,14},... | collective-permute-start | bytes 172040 | tf_op jit(solution)/shard_map/ppermute | solution.py:96
  51.1 3.6 %collective-permute-start.21 = (bf16[144,128]{1,0:T(8,128)(2,1)S(1)}, bf16[144,128]{1,0:T(8,128)(2,1)S(1)}, u32[]{:S(2)}, u32[]{:S(2)}) collective-permute-start(bf16[144,128]{1,0:T(8,128)(2,1)S(1)} %get-tuple-element.93.refs_3_), channel_id=1, source_target_pairs={{0,3},{1,2},{2,1},{3,0},{4,7},{5,6},{6,5},{7,4},{8,11},{9,10},{10,... | collective-permute-start | bytes 110600 | tf_op jit(solution)/shard_map/ppermute | solution.py:96
  51.3 4.5 %collective-permute-start.20 = (bf16[144,128]{1,0:T(8,128)(2,1)S(1)}, bf16[144,128]{1,0:T(8,128)(2,1)S(1)}, u32[]{:S(2)}, u32[]{:S(2)}) collective-permute-start(bf16[144,128]{1,0:T(8,128)(2,1)S(1)} %get-tuple-element.93.refs_3_), channel_id=1, source_target_pairs={{0,2},{1,3},{2,0},{3,1},{4,6},{5,7},{6,4},{7,5},{8,10},{9,11},{10,... | collective-permute-start | bytes 110600 | tf_op jit(solution)/shard_map/ppermute | solution.py:96
  52.8 2.9 %collective-permute-start.19 = (bf16[144,128]{1,0:T(8,128)(2,1)S(1)}, bf16[144,128]{1,0:T(8,128)(2,1)S(1)}, u32[]{:S(2)}, u32[]{:S(2)}) collective-permute-start(bf16[144,128]{1,0:T(8,128)(2,1)S(1)} %get-tuple-element.93.refs_3_), channel_id=1, source_target_pairs={{0,1},{1,0},{2,3},{3,2},{4,5},{5,4},{6,7},{7,6},{8,9},{9,8},{10,11... | collective-permute-start | bytes 110600 | tf_op jit(solution)/shard_map/ppermute | solution.py:96
  57.3 5.8 %collective-permute-start.22 = (bf16[144,128]{1,0:T(8,128)(2,1)S(1)}, bf16[144,128]{1,0:T(8,128)(2,1)S(1)}, u32[]{:S(2)}, u32[]{:S(2)}) collective-permute-start(bf16[144,128]{1,0:T(8,128)(2,1)S(1)} %get-tuple-element.99), channel_id=1, source_target_pairs={{0,12},{4,8},{8,4},{12,0},{1,13},{5,9},{9,5},{13,1},{2,14},{6,10},... | collective-permute-start | bytes 110600 | tf_op jit(solution)/shard_map/ppermute | solution.py:96
  59.5 4.9 %collective-permute-start.23 = (bf16[144,128]{1,0:T(8,128)(2,1)S(1)}, bf16[144,128]{1,0:T(8,128)(2,1)S(1)}, u32[]{:S(2)}, u32[]{:S(2)}) collective-permute-start(bf16[144,128]{1,0:T(8,128)(2,1)S(1)} %get-tuple-element.100), channel_id=1, source_target_pairs={{0,8},{4,12},{8,0},{12,4},{1,9},{5,13},{9,1},{13,5},{2,10},{6,14},... | collective-permute-start | bytes 110600 | tf_op jit(solution)/shard_map/ppermute | solution.py:96
  59.5 4.9 %collective-permute-start.24 = (bf16[144,128]{1,0:T(8,128)(2,1)S(1)}, bf16[144,128]{1,0:T(8,128)(2,1)S(1)}, u32[]{:S(2)}, u32[]{:S(2)}) collective-permute-start(bf16[144,128]{1,0:T(8,128)(2,1)S(1)} %get-tuple-element.101), channel_id=1, source_target_pairs={{0,4},{4,0},{8,12},{12,8},{1,5},{5,1},{9,13},{13,9},{2,6},{6,2},{1... | collective-permute-start | bytes 110600 | tf_op jit(solution)/shard_map/ppermute | solution.py:96
  64.5 3.4 %collective-permute-start.27 = (bf16[144,128]{1,0:T(8,128)(2,1)S(1)}, bf16[144,128]{1,0:T(8,128)(2,1)S(1)}, u32[]{:S(2)}, u32[]{:S(2)}) collective-permute-start(bf16[144,128]{1,0:T(8,128)(2,1)S(1)} %get-tuple-element.103.refs_3_), channel_id=1, source_target_pairs={{0,3},{1,2},{2,1},{3,0},{4,7},{5,6},{6,5},{7,4},{8,11},{9,10},{10,... | collective-permute-start | bytes 110600 | tf_op jit(solution)/shard_map/ppermute | solution.py:96
  64.7 4.2 %collective-permute-start.26 = (bf16[144,128]{1,0:T(8,128)(2,1)S(1)}, bf16[144,128]{1,0:T(8,128)(2,1)S(1)}, u32[]{:S(2)}, u32[]{:S(2)}) collective-permute-start(bf16[144,128]{1,0:T(8,128)(2,1)S(1)} %get-tuple-element.103.refs_3_), channel_id=1, source_target_pairs={{0,2},{1,3},{2,0},{3,1},{4,6},{5,7},{6,4},{7,5},{8,10},{9,11},{10,... | collective-permute-start | bytes 110600 | tf_op jit(solution)/shard_map/ppermute | solution.py:96
  65.6 3.3 %collective-permute-start.25 = (bf16[144,128]{1,0:T(8,128)(2,1)S(1)}, bf16[144,128]{1,0:T(8,128)(2,1)S(1)}, u32[]{:S(2)}, u32[]{:S(2)}) collective-permute-start(bf16[144,128]{1,0:T(8,128)(2,1)S(1)} %get-tuple-element.103.refs_3_), channel_id=1, source_target_pairs={{0,1},{1,0},{2,3},{3,2},{4,5},{5,4},{6,7},{7,6},{8,9},{9,8},{10,11... | collective-permute-start | bytes 110600 | tf_op jit(solution)/shard_map/ppermute | solution.py:96
  70.4 5.9 %collective-permute-start.28 = (bf16[144,128]{1,0:T(8,128)(2,1)S(1)}, bf16[144,128]{1,0:T(8,128)(2,1)S(1)}, u32[]{:S(2)}, u32[]{:S(2)}) collective-permute-start(bf16[144,128]{1,0:T(8,128)(2,1)S(1)} %get-tuple-element.114), channel_id=1, source_target_pairs={{0,12},{4,8},{8,4},{12,0},{1,13},{5,9},{9,5},{13,1},{2,14},{6,10},... | collective-permute-start | bytes 110600 | tf_op jit(solution)/shard_map/ppermute | solution.py:96
  72.8 4.9 %collective-permute-start.29 = (bf16[144,128]{1,0:T(8,128)(2,1)S(1)}, bf16[144,128]{1,0:T(8,128)(2,1)S(1)}, u32[]{:S(2)}, u32[]{:S(2)}) collective-permute-start(bf16[144,128]{1,0:T(8,128)(2,1)S(1)} %get-tuple-element.115), channel_id=1, source_target_pairs={{0,8},{4,12},{8,0},{12,4},{1,9},{5,13},{9,1},{13,5},{2,10},{6,14},... | collective-permute-start | bytes 110600 | tf_op jit(solution)/shard_map/ppermute | solution.py:96
  73.2 4.5 %collective-permute-start.30 = (bf16[144,128]{1,0:T(8,128)(2,1)S(1)}, bf16[144,128]{1,0:T(8,128)(2,1)S(1)}, u32[]{:S(2)}, u32[]{:S(2)}) collective-permute-start(bf16[144,128]{1,0:T(8,128)(2,1)S(1)} %get-tuple-element.116), channel_id=1, source_target_pairs={{0,4},{4,0},{8,12},{12,8},{1,5},{5,1},{9,13},{13,9},{2,6},{6,2},{1... | collective-permute-start | bytes 110600 | tf_op jit(solution)/shard_map/ppermute | solution.py:96
  77.8 4.0 %collective-permute-start.33 = (bf16[176,128]{1,0:T(8,128)(2,1)S(1)}, bf16[176,128]{1,0:T(8,128)(2,1)S(1)}, u32[]{:S(2)}, u32[]{:S(2)}) collective-permute-start(bf16[176,128]{1,0:T(8,128)(2,1)S(1)} %shard_map.135.refs_3_.mine), channel_id=1, source_target_pairs={{0,3},{1,2},{2,1},{3,0},{4,7},{5,6},{6,5},{7,4},{8,11},{9,10},{10,... | collective-permute-start | bytes 135176 | tf_op jit(solution)/shard_map/ppermute | solution.py:96
  77.8 4.5 %collective-permute-start.32 = (bf16[176,128]{1,0:T(8,128)(2,1)S(1)}, bf16[176,128]{1,0:T(8,128)(2,1)S(1)}, u32[]{:S(2)}, u32[]{:S(2)}) collective-permute-start(bf16[176,128]{1,0:T(8,128)(2,1)S(1)} %shard_map.135.refs_3_.mine), channel_id=1, source_target_pairs={{0,2},{1,3},{2,0},{3,1},{4,6},{5,7},{6,4},{7,5},{8,10},{9,11},{10,... | collective-permute-start | bytes 135176 | tf_op jit(solution)/shard_map/ppermute | solution.py:96
  79.1 3.2 %collective-permute-start.31 = (bf16[176,128]{1,0:T(8,128)(2,1)S(1)}, bf16[176,128]{1,0:T(8,128)(2,1)S(1)}, u32[]{:S(2)}, u32[]{:S(2)}) collective-permute-start(bf16[176,128]{1,0:T(8,128)(2,1)S(1)} %shard_map.135.refs_3_.mine), channel_id=1, source_target_pairs={{0,1},{1,0},{2,3},{3,2},{4,5},{5,4},{6,7},{7,6},{8,9},{9,8},{10,11... | collective-permute-start | bytes 135176 | tf_op jit(solution)/shard_map/ppermute | solution.py:96
  82.3 4.1 %collective-permute-start.34 = (bf16[128,128]{1,0:T(8,128)(2,1)S(1)}, bf16[128,128]{1,0:T(8,128)(2,1)S(1)}, u32[]{:S(2)}, u32[]{:S(2)}) collective-permute-start(bf16[128,128]{1,0:T(8,128)(2,1)S(1)} %shard_map.137.refs_0_), channel_id=1, source_target_pairs={{0,4},{4,0},{8,12},{12,8},{1,5},{5,1},{9,13},{13,9},{2,6},{6,2},{1... | collective-permute-start | bytes 98312 | tf_op jit(solution)/shard_map/ppermute | solution.py:96

commit v8 on v6

--- a/solution.py
+++ b/solution.py
@@ -100,17 +100,21 @@
     return count <= 4
 
 
+def order(axis, count):
+    return (3, 1, 2) if axis == "row" and count == 4 else tuple(range(count - 1, 0, -1))
+
+
 def share(x, axis):
     count = lax.axis_size(axis)
     if few(count):
-        return [flip(x, axis, k) for k in reversed(range(1, count))]
+        return [flip(x, axis, k) for k in order(axis, count)[::-1]]
     return [lax.all_gather(x, axis)]
 
 
 def exchange(parts, axis):
     count = lax.axis_size(axis)
     if len(parts) == count - 1:
-        return [flip(part, axis, count - 1 - i) for i, part in enumerate(parts)]
+        return [flip(part, axis, k) for part, k in zip(parts, order(axis, count))]
     return [lax.all_to_all(parts[0], axis, 0, 0, tiled=True)]
 
 
@@ -120,8 +124,16 @@
     return [shape((count, *dims), kind)]
 
 
-def away(refs, count, me, k):
-    return refs[count - 1 - k] if len(refs) == count - 1 else refs[0].at[me ^ k]
+def away(refs, axis, count, me, k):
+    if few(count):
+        return refs[order(axis, count)[::-1].index(k)]
+    return refs[0].at[me ^ k]
+
+
+def parted(refs, axis, count, me, k):
+    if few(count):
+        return refs[order(axis, count).index(k)]
+    return refs[0].at[me ^ k]
 
 
 def place():
@@ -178,7 +190,7 @@
     channel_ids = lax.broadcasted_iota(jnp.int32, (z.channels, BLOCK), 0).astype(F32)
     stim = stimuli[...]
     for k in range(z.rows):
-        ref = mine if k == 0 else away(got, z.rows, p, k)
+        ref = mine if k == 0 else away(got, "row", z.rows, p, k)
         rows = slice(k * z.piece, (k + 1) * z.piece)
         message = ref[...].astype(F32)
         gains, drives = [], []
@@ -214,7 +226,7 @@
         if k == 0:
             own[...] = both
         else:
-            away(parts, z.cols, c, k)[...] = both.astype(BF16)
+            parted(parts, "col", z.cols, c, k)[...] = both.astype(BF16)
 
 
 def first_kernel(z, count, *refs):
@@ -227,7 +239,7 @@
     p, c = place()
     sums[...] = jnp.zeros_like(sums)
     for k in range(z.rows):
-        ref = mine if k == 0 else away(got, z.rows, p, k)
+        ref = mine if k == 0 else away(got, "row", z.rows, p, k)
         z.add_blocks(sums, 0, p ^ k, ref[...].astype(F32)[0 : z.piece])
     x[...] = sums[...].astype(BF16)
     bring.wait()
@@ -245,7 +257,7 @@
     sums[...] = jnp.zeros_like(sums)
 
     def sent(k, side):
-        ref = kept if k == 0 else away(got, z.rows, p, k)
+        ref = kept if k == 0 else away(got, "row", z.rows, p, k)
         return ref[side * z.piece : (side + 1) * z.piece].astype(F32)
 
     for k in range(z.rows):
@@ -270,7 +282,7 @@
     _, c = place()
     total = own[...]
     for k in range(1, z.cols):
-        total = total + away(got, z.cols, c, k)[...].astype(F32)
+        total = total + parted(got, "col", z.cols, c, k)[...].astype(F32)
     kept[...] = total
     if with_cot:
         cot = refs[1 + count]
@@ -305,7 +317,7 @@
 def gather_post(z, c, mine, got, sums, d):
     sums[...] = jnp.zeros_like(sums)
     for k in range(z.cols):
-        pair = (mine if k == 0 else away(got, z.cols, c, k))[...].astype(F32)
+        pair = (mine if k == 0 else away(got, "col", z.cols, c, k))[...].astype(F32)
         z.add_blocks(sums, 0, c ^ k, pair[0 : z.piece])
         z.add_blocks(sums, z.post, c ^ k, pair[z.piece : z.pair])
     d[...] = sums[...].astype(BF16)
@@ -333,14 +345,14 @@
             if k == z.half:
                 other = other + base[...]
             both = jnp.concatenate([pieces[k], other], axis=0)
-            away(parts, z.rows, p, k)[...] = both.astype(BF16)
+            parted(parts, "row", z.rows, p, k)[...] = both.astype(BF16)
 
 
 def adjoints(z, own, got):
     p, _ = place()
     total = own[...]
     for k in range(1, z.rows):
-        total = total + away(got, z.rows, p, k)[...].astype(F32)
+        total = total + parted(got, "row", z.rows, p, k)[...].astype(F32)
     return total
 
 
@@ -387,27 +399,28 @@
     got, out = refs[:-1], refs[-1]
     _, c = place()
     for k in range(z.cols):
-        ref = mine if k == 0 else away(got, z.cols, c, k)
+        ref = mine if k == 0 else away(got, "col", z.cols, c, k)
         out[2 * CODES * k : 2 * CODES * (k + 1)] = ref[z.pair :]
 
 
 def add_table(z, extras, out):
     highs = z.types // BLOCK
     high_ids = lax.broadcasted_iota(jnp.int32, (highs, BLOCK), 0).astype(F32) + 1.0
-    low_ids = lax.broadcasted_iota(jnp.int32, (BLOCK, BLOCK), 0).astype(F32)
+    low_ids = lax.broadcasted_iota(jnp.int32, (BLOCK, BLOCK), 1).astype(F32)
     total = jnp.zeros((3 * highs, BLOCK), F32)
     for ref in extras:
+        everything = ref[...].astype(F32)
+        down = jnp.transpose(everything)
         for side in range(2 * z.cols):
-            extra = ref[side * CODES : (side + 1) * CODES].astype(F32)
+            extra = everything[side * CODES : (side + 1) * CODES]
             for f in range(z.frame):
                 at = 5 * f
+                low = side * CODES + at + 1
                 hit = high_ids == extra[at : at + 1]
                 terms = [jnp.where(hit, extra[at + 2 + i : at + 3 + i], 0.0) for i in range(3)]
                 left = jnp.concatenate(terms, axis=0).astype(BF16)
-                right = (low_ids == extra[at + 1 : at + 2]).astype(BF16)
-                total = total + lax.dot_general(
-                    left, right, (((1,), (1,)), ((), ())), preferred_element_type=F32
-                )
+                right = (low_ids == down[:, low : low + 1]).astype(BF16)
+                total = total + jnp.dot(left, right, preferred_element_type=F32)
     out[...] = total[0:highs] + total[highs : 2 * highs] + total[2 * highs :]
 
 
@@ -520,6 +533,7 @@
         ],
         [pltpu.VMEM((batch, z.wide), F32)],
         [initial_rates, numbers.reshape(numbers.size // BLOCK, BLOCK)],
+        flops=4_000_000_000,
     )
     got = share(message, "row")
     weights = weight_blocks.reshape(slots, BLOCK, BLOCK)
@@ -531,7 +545,7 @@
     )
     held_ids = [pltpu.SMEM((1, 2 * slots), jnp.int32), pltpu.SemaphoreType.DMA]
     if few(z.rows):
-        partner_message = got[z.rows - 1 - z.half]
+        partner_message = away(got, "row", z.rows, None, z.half)
     else:
         partner_message = flip(message, "row", z.half)
     pre_sums = pltpu.VMEM((z.pre, batch, BLOCK), F32)

time: 91.8 us -> 89.2 us (0.972)
  waiting for transfers between devices: 35.5 us -> 32.1 us
  starting transfers between devices: 35.9 us -> 38.3 us
  local copies, waits for them, and re-layouts: 3.22 us -> 1.63 us
    ppermute x35, waiting for transfers between devices: 35.5 us -> 32.1 us  [flip(): return lax.ppermute(x, axis, [(i, i ^ k) for i in range(count)])]
    ppermute x35, starting transfers between devices: 35.9 us -> 38.3 us  [flip(): return lax.ppermute(x, axis, [(i, i ^ k) for i in range(count)])]
    unnamed x12 -> x10, local copies, waits for them, and re-layouts: 2.41 us -> 0.82 us
  transfers between devices with their start and end apart: 35 -> 35, of which waited for: 23 -> 28; matrix products, arithmetic and copies ran while one was open for 0% -> 0% of each run, Pallas kernels for 6% -> 6%
where the time goes in v8:
time: 89.2 us; the launch traced here: 89 us
  starting transfers between devices  38.3 us (43%)
  waiting for transfers between devices  32.1 us (36%)
  Pallas kernels  16.1 us (18%)
  local copies, waits for them, and re-layouts  1.63 us (2%)
    ppermute x35, starting transfers between devices, flip(): return lax.ppermute(x, axis, [(i, i ^ k) for i in range(count)])  38.3 us
    ppermute x35, waiting for transfers between devices, flip(): return lax.ppermute(x, axis, [(i, i ^ k) for i in range(count)])  32.1 us
    pallas_call x16, Pallas kernels, call(): pl.pallas_call(body, out_shape=outs, in_specs=specs, out_specs=out_specs...  10.7 us
    pallas_call x1, Pallas kernels, shards(): pl.pallas_call(functools.partial(grad_kernel, z, len(got), per_step), gri...  2.9 us
    pallas_call x1, Pallas kernels, shards(): pl.pallas_call(functools.partial(rest_kernel, z, len(all_extras), slots -...  2.5 us
  transfers between devices with their start and end apart: 35, of which 28 were waited for; matrix products, arithmetic and copies ran while one was open for 0% of the time, Pallas kernels for 6%

profile of v8, /device:TPU:0, one launch (start us, length us, event | category | flops | bytes accessed | tf_op | source)
XLA Modules:
  0.0 89.0 jit_solution(1726486542859543466)
XLA Ops:
  0.7 0.8 concatenate.3
  1.5 0.8 copy-done.4
  2.3 5.1 %collective-permute-start.2 = (bf16[96,128]{1,0:T(8,128)(2,1)S(1)}, bf16[96,128]{1,0:T(8,128)(2,1)S(1)}, u32[]{:S(2)}, u32[]{:S(2)}) collective-permute-start(bf16[96,128]{1,0:T(8,128)(2,1)S(1)} %get-tuple-element.63.after.refs_2_.refs_0_.mine), channel_id=1, source_target_pairs={{0,12},{4,8},{8,4},{12,0},{1,13},{5,9},{9,5},{13,1},{2,14},{6,10},... | collective-permute-start | bytes 73736 | tf_op jit(solution)/shard_map/ppermute | solution.py:96
  7.4 0.6 collective-permute-start
  8.0 1.0 %shard_map.122.refs_1_ = bf16[64,128,128]{2,1,0:T(8,128)(2,1)S(1)} custom-call(bf16[96,128]{1,0:T(8,128)(2,1)S(1)} %get-tuple-element.63.after.refs_2_.refs_0_.mine, bf16[64,128,128]{2,1,0:T(8,128)(2,1)S(1)} %bitcast.9), custom_call_target="tpu_custom_call" | custom-call | bytes 4218880 | tf_op jit(solution)/shard_map/pallas_call | solution.py:78
  9.2 2.0 %collective-permute-done.1.refs_4_.refs_6_ = bf16[96,128]{1,0:T(8,128)(2,1)S(1)} collective-permute-done((bf16[96,128]{1,0:T(8,128)(2,1)S(1)}, bf16[96,128]{1,0:T(8,128)(2,1)S(1)}, u32[]{:S(2)}, u32[]{:S(2)}) %collective-permute-start.1) | collective-permute-done | bytes 24608 | tf_op jit(solution)/shard_map/ppermute | solution.py:96
  11.2 0.9 %collective-permute-done.refs_3_.refs_5_.partner = bf16[96,128]{1,0:T(8,128)(2,1)S(1)} collective-permute-done((bf16[96,128]{1,0:T(8,128)(2,1)S(1)}, bf16[96,128]{1,0:T(8,128)(2,1)S(1)}, u32[]{:S(2)}, u32[]{:S(2)}) %collective-permute-start) | collective-permute-done | bytes 24608 | tf_op jit(solution)/shard_map/ppermute | solution.py:96
  12.1 1.5 %shard_map.123 = (bf16[9,32,128]{2,1,0:T(8,128)(2,1)S(1)}, f32[144,128]{1,0:T(8,128)S(1)}, bf16[144,128]{1,0:T(8,128)(2,1)S(1)}, bf16[144,128]{1,0:T(8,128)(2,1)S(1)}, bf16[144,128]{1,0:T(8,128)(2,1)S(1)}) custom-call(s32[1,128]{1,0:T(1,128)S(1)} %get-tuple-element.62.refs_0_.near_ids, bf16[64,128,128]{2,1,0:T(8,128)(2,1)S(1)} %shard_map.122.refs_1_, ...), custom_call_target="tpu_custom_call" | custom-call | flops 67108864 | bytes 2454016 | tf_op jit(solution)/shard_map/pallas_call | solution.py:78
  13.7 1.6 %collective-permute-start.4 = (bf16[144,128]{1,0:T(8,128)(2,1)S(1)}, bf16[144,128]{1,0:T(8,128)(2,1)S(1)}, u32[]{:S(2)}, u32[]{:S(2)}) collective-permute-start(bf16[144,128]{1,0:T(8,128)(2,1)S(1)} %get-tuple-element.67), channel_id=1, source_target_pairs={{0,2},{1,3},{2,0},{3,1},{4,6},{5,7},{6,4},{7,5},{8,10},{9,11},{10,... | collective-permute-start | bytes 110600 | tf_op jit(solution)/shard_map/ppermute | solution.py:96
  15.5 1.9 %collective-permute-done.3.refs_1_ = bf16[144,128]{1,0:T(8,128)(2,1)S(1)} collective-permute-done((bf16[144,128]{1,0:T(8,128)(2,1)S(1)}, bf16[144,128]{1,0:T(8,128)(2,1)S(1)}, u32[]{:S(2)}, u32[]{:S(2)}) %collective-permute-start.3) | collective-permute-done | bytes 36896 | tf_op jit(solution)/shard_map/ppermute | solution.py:96
  17.4 0.4 collective-permute-done.4.refs_2_
  17.9 1.7 %collective-permute-start.8 = (bf16[144,128]{1,0:T(8,128)(2,1)S(1)}, bf16[144,128]{1,0:T(8,128)(2,1)S(1)}, u32[]{:S(2)}, u32[]{:S(2)}) collective-permute-start(bf16[144,128]{1,0:T(8,128)(2,1)S(1)} %get-tuple-element.74), channel_id=1, source_target_pairs={{0,12},{4,8},{8,4},{12,0},{1,13},{5,9},{9,5},{13,1},{2,14},{6,10},... | collective-permute-start | bytes 110600 | tf_op jit(solution)/shard_map/ppermute | solution.py:96
  19.6 0.4 collective-permute-start.7
  20.0 2.3 %collective-permute-start.6 = (bf16[144,128]{1,0:T(8,128)(2,1)S(1)}, bf16[144,128]{1,0:T(8,128)(2,1)S(1)}, u32[]{:S(2)}, u32[]{:S(2)}) collective-permute-start(bf16[144,128]{1,0:T(8,128)(2,1)S(1)} %get-tuple-element.74), channel_id=1, source_target_pairs={{0,8},{4,12},{8,0},{12,4},{1,9},{5,13},{9,1},{13,5},{2,10},{6,14},... | collective-permute-start | bytes 110600 | tf_op jit(solution)/shard_map/ppermute | solution.py:96
  22.3 0.9 %shard_map.125 = (f32[288,128]{1,0:T(8,128)S(1)}, f32[288,128]{1,0:T(8,128)S(1)}, f32[3,288,128]{2,1,0:T(8,128)S(1)}, f32[3,72,128]{2,1,0:T(8,128)S(1)}) custom-call(bf16[96,128]{1,0:T(8,128)(2,1)S(1)} %get-tuple-element.63.after.refs_2_.refs_0_.mine, f32[72,128]{1,0:T(8,128)S(1)} %get-tuple-element.70.refs_1_, f32[3,32,288]{2,1,0:T(8,128)S(1)} %copy-done.1, ...), custom_call_target="tpu_custom_call" | custom-call | bytes 1224704 | tf_op jit(solution)/shard_map/pallas_call | solution.py:78
  23.3 0.8 collective-permute-done.8.refs_8_
  24.3 0.7 collective-permute-done.6.refs_6_
  25.0 1.5 %shard_map.126 = (f32[288,128]{1,0:T(8,128)S(1)}, f32[144,128]{1,0:T(8,128)S(1)}, f32[144,128]{1,0:T(8,128)S(1)}, bf16[9,32,128]{2,1,0:T(8,128)(2,1)S(1)}, f32[1...) custom-call(s32[1,128]{1,0:T(1,128)S(1)} %get-tuple-element.62.refs_, ...), custom_call_target="tpu_custom_call" | custom-call | flops 67108864 | bytes 3572224 | tf_op jit(solution)/shard_map/pallas_call | solution.py:78
  26.5 0.5 collective-permute-start.9
  27.1 1.0 %collective-permute-start.10 = (bf16[144,128]{1,0:T(8,128)(2,1)S(1)}, bf16[144,128]{1,0:T(8,128)(2,1)S(1)}, u32[]{:S(2)}, u32[]{:S(2)}) collective-permute-start(bf16[144,128]{1,0:T(8,128)(2,1)S(1)} %get-tuple-element.78), channel_id=1, source_target_pairs={{0,2},{1,3},{2,0},{3,1},{4,6},{5,7},{6,4},{7,5},{8,10},{9,11},{10,... | collective-permute-start | bytes 110600 | tf_op jit(solution)/shard_map/ppermute | solution.py:96
  28.1 0.4 collective-permute-start.11
  28.5 1.9 %collective-permute-done.9.refs_1_ = bf16[144,128]{1,0:T(8,128)(2,1)S(1)} collective-permute-done((bf16[144,128]{1,0:T(8,128)(2,1)S(1)}, bf16[144,128]{1,0:T(8,128)(2,1)S(1)}, u32[]{:S(2)}, u32[]{:S(2)}) %collective-permute-start.9) | collective-permute-done | bytes 36896 | tf_op jit(solution)/shard_map/ppermute | solution.py:96
  30.4 0.9 %collective-permute-done.10.refs_2_ = bf16[144,128]{1,0:T(8,128)(2,1)S(1)} collective-permute-done((bf16[144,128]{1,0:T(8,128)(2,1)S(1)}, bf16[144,128]{1,0:T(8,128)(2,1)S(1)}, u32[]{:S(2)}, u32[]{:S(2)}) %collective-permute-start.10) | collective-permute-done | bytes 36896 | tf_op jit(solution)/shard_map/ppermute | solution.py:96
  31.3 2.3 %collective-permute-start.14 = (bf16[144,128]{1,0:T(8,128)(2,1)S(1)}, bf16[144,128]{1,0:T(8,128)(2,1)S(1)}, u32[]{:S(2)}, u32[]{:S(2)}) collective-permute-start(bf16[144,128]{1,0:T(8,128)(2,1)S(1)} %get-tuple-element.82), channel_id=1, source_target_pairs={{0,12},{4,8},{8,4},{12,0},{1,13},{5,9},{9,5},{13,1},{2,14},{6,10},... | collective-permute-start | bytes 110600 | tf_op jit(solution)/shard_map/ppermute | solution.py:96
  33.7 2.1 %collective-permute-start.12 = (bf16[144,128]{1,0:T(8,128)(2,1)S(1)}, bf16[144,128]{1,0:T(8,128)(2,1)S(1)}, u32[]{:S(2)}, u32[]{:S(2)}) collective-permute-start(bf16[144,128]{1,0:T(8,128)(2,1)S(1)} %get-tuple-element.82), channel_id=1, source_target_pairs={{0,8},{4,12},{8,0},{12,4},{1,9},{5,13},{9,1},{13,5},{2,10},{6,14},... | collective-permute-start | bytes 110600 | tf_op jit(solution)/shard_map/ppermute | solution.py:96
  35.8 1.4 %collective-permute-done.14.refs_8_ = bf16[144,128]{1,0:T(8,128)(2,1)S(1)} collective-permute-done((bf16[144,128]{1,0:T(8,128)(2,1)S(1)}, bf16[144,128]{1,0:T(8,128)(2,1)S(1)}, u32[]{:S(2)}, u32[]{:S(2)}) %collective-permute-start.14) | collective-permute-done | bytes 36896 | tf_op jit(solution)/shard_map/ppermute | solution.py:96
  37.2 0.8 collective-permute-done.13.refs_7_
  37.9 1.0 %collective-permute-done.12.refs_6_ = bf16[144,128]{1,0:T(8,128)(2,1)S(1)} collective-permute-done((bf16[144,128]{1,0:T(8,128)(2,1)S(1)}, bf16[144,128]{1,0:T(8,128)(2,1)S(1)}, u32[]{:S(2)}, u32[]{:S(2)}) %collective-permute-start.12) | collective-permute-done | bytes 36896 | tf_op jit(solution)/shard_map/ppermute | solution.py:96
  38.9 1.6 %shard_map.128 = (f32[288,128]{1,0:T(8,128)S(1)}, f32[144,128]{1,0:T(8,128)S(1)}, f32[144,128]{1,0:T(8,128)S(1)}, bf16[9,32,128]{2,1,0:T(8,128)(2,1)S(1)}, f32[1...) custom-call(s32[1,128]{1,0:T(1,128)S(1)} %get-tuple-element.62.refs_, ...), custom_call_target="tpu_custom_call" | custom-call | flops 67108864 | bytes 3572224 | tf_op jit(solution)/shard_map/pallas_call | solution.py:78
  40.6 1.3 %collective-permute-start.16 = (bf16[144,128]{1,0:T(8,128)(2,1)S(1)}, bf16[144,128]{1,0:T(8,128)(2,1)S(1)}, u32[]{:S(2)}, u32[]{:S(2)}) collective-permute-start(bf16[144,128]{1,0:T(8,128)(2,1)S(1)} %get-tuple-element.86), channel_id=1, source_target_pairs={{0,2},{1,3},{2,0},{3,1},{4,6},{5,7},{6,4},{7,5},{8,10},{9,11},{10,... | collective-permute-start | bytes 110600 | tf_op jit(solution)/shard_map/ppermute | solution.py:96
  41.9 0.5 collective-permute-start.17
  42.4 1.7 %collective-permute-done.15.refs_1_ = bf16[144,128]{1,0:T(8,128)(2,1)S(1)} collective-permute-done((bf16[144,128]{1,0:T(8,128)(2,1)S(1)}, bf16[144,128]{1,0:T(8,128)(2,1)S(1)}, u32[]{:S(2)}, u32[]{:S(2)}) %collective-permute-start.15) | collective-permute-done | bytes 36896 | tf_op jit(solution)/shard_map/ppermute | solution.py:96
  44.2 0.5 collective-permute-done.16.refs_2_
  44.7 2.1 %collective-permute-start.18 = (bf16[224,128]{1,0:T(8,128)(2,1)S(1)}, bf16[224,128]{1,0:T(8,128)(2,1)S(1)}, u32[]{:S(2)}, u32[]{:S(2)}) collective-permute-start(bf16[224,128]{1,0:T(8,128)(2,1)S(1)} %get-tuple-element.90), channel_id=1, source_target_pairs={{0,8},{4,12},{8,0},{12,4},{1,9},{5,13},{9,1},{13,5},{2,10},{6,14},... | collective-permute-start | bytes 172040 | tf_op jit(solution)/shard_map/ppermute | solution.py:96
  46.8 4.3 %collective-permute-done.18.theirs = bf16[224,128]{1,0:T(8,128)(2,1)S(1)} collective-permute-done((bf16[224,128]{1,0:T(8,128)(2,1)S(1)}, bf16[224,128]{1,0:T(8,128)(2,1)S(1)}, u32[]{:S(2)}, u32[]{:S(2)}) %collective-permute-start.18) | collective-permute-done | bytes 57376 | tf_op jit(solution)/shard_map/ppermute | solution.py:96
  51.2 1.5 %collective-permute-start.20 = (bf16[144,128]{1,0:T(8,128)(2,1)S(1)}, bf16[144,128]{1,0:T(8,128)(2,1)S(1)}, u32[]{:S(2)}, u32[]{:S(2)}) collective-permute-start(bf16[144,128]{1,0:T(8,128)(2,1)S(1)} %get-tuple-element.93.refs_3_), channel_id=1, source_target_pairs={{0,2},{1,3},{2,0},{3,1},{4,6},{5,7},{6,4},{7,5},{8,10},{9,11},{10,... | collective-permute-start | bytes 110600 | tf_op jit(solution)/shard_map/ppermute | solution.py:96
  52.7 0.3 collective-permute-start.19
  53.0 1.9 %collective-permute-done.21.refs_6_ = bf16[144,128]{1,0:T(8,128)(2,1)S(1)} collective-permute-done((bf16[144,128]{1,0:T(8,128)(2,1)S(1)}, bf16[144,128]{1,0:T(8,128)(2,1)S(1)}, u32[]{:S(2)}, u32[]{:S(2)}) %collective-permute-start.21) | collective-permute-done | bytes 36896 | tf_op jit(solution)/shard_map/ppermute | solution.py:96
  54.9 0.4 collective-permute-done.20.refs_5_
  55.3 1.5 %shard_map.131 = (bf16[18,32,128]{2,1,0:T(8,128)(2,1)S(1)}, f32[144,128]{1,0:T(8,128)S(1)}, bf16[144,128]{1,0:T(8,128)(2,1)S(1)}, bf16[144,128]{1,0:T(8,128)(2,1)S(1)}, bf16[144,128]{1,0:T(8,128)(2,1)S(1)}) custom-call(s32[1,128]{1,0:T(1,128)S(1)} %get-tuple-element.62.refs_0_.near_ids, bf16[64,128,128]{2,1,0:T(8,128)(2,1)S(1)} %bitcast.10, ...), custom_call_target="tpu_custom_call" | custom-call | flops 67108864 | bytes 2613760 | tf_op jit(solution)/shard_map/pallas_call | solution.py:78
  56.9 1.9 %collective-permute-start.22 = (bf16[144,128]{1,0:T(8,128)(2,1)S(1)}, bf16[144,128]{1,0:T(8,128)(2,1)S(1)}, u32[]{:S(2)}, u32[]{:S(2)}) collective-permute-start(bf16[144,128]{1,0:T(8,128)(2,1)S(1)} %get-tuple-element.99), channel_id=1, source_target_pairs={{0,12},{4,8},{8,4},{12,0},{1,13},{5,9},{9,5},{13,1},{2,14},{6,10},... | collective-permute-start | bytes 110600 | tf_op jit(solution)/shard_map/ppermute | solution.py:96
  58.8 2.5 %collective-permute-start.24 = (bf16[144,128]{1,0:T(8,128)(2,1)S(1)}, bf16[144,128]{1,0:T(8,128)(2,1)S(1)}, u32[]{:S(2)}, u32[]{:S(2)}) collective-permute-start(bf16[144,128]{1,0:T(8,128)(2,1)S(1)} %get-tuple-element.101), channel_id=1, source_target_pairs={{0,8},{4,12},{8,0},{12,4},{1,9},{5,13},{9,1},{13,5},{2,10},{6,14},... | collective-permute-start | bytes 110600 | tf_op jit(solution)/shard_map/ppermute | solution.py:96
  61.3 1.5 %collective-permute-done.22.refs_0_ = bf16[144,128]{1,0:T(8,128)(2,1)S(1)} collective-permute-done((bf16[144,128]{1,0:T(8,128)(2,1)S(1)}, bf16[144,128]{1,0:T(8,128)(2,1)S(1)}, u32[]{:S(2)}, u32[]{:S(2)}) %collective-permute-start.22) | collective-permute-done | bytes 36896 | tf_op jit(solution)/shard_map/ppermute | solution.py:96
  62.8 0.6 collective-permute-done.23.refs_1_
  63.5 0.6 collective-permute-done.24.refs_2_
  64.2 1.3 %collective-permute-start.26 = (bf16[144,128]{1,0:T(8,128)(2,1)S(1)}, bf16[144,128]{1,0:T(8,128)(2,1)S(1)}, u32[]{:S(2)}, u32[]{:S(2)}) collective-permute-start(bf16[144,128]{1,0:T(8,128)(2,1)S(1)} %get-tuple-element.103.refs_3_), channel_id=1, source_target_pairs={{0,2},{1,3},{2,0},{3,1},{4,6},{5,7},{6,4},{7,5},{8,10},{9,11},{10,... | collective-permute-start | bytes 110600 | tf_op jit(solution)/shard_map/ppermute | solution.py:96
  65.4 0.6 collective-permute-start.25
  66.0 1.7 %collective-permute-done.27.refs_6_ = bf16[144,128]{1,0:T(8,128)(2,1)S(1)} collective-permute-done((bf16[144,128]{1,0:T(8,128)(2,1)S(1)}, bf16[144,128]{1,0:T(8,128)(2,1)S(1)}, u32[]{:S(2)}, u32[]{:S(2)}) %collective-permute-start.27) | collective-permute-done | bytes 36896 | tf_op jit(solution)/shard_map/ppermute | solution.py:96
  67.7 0.6 collective-permute-done.26.refs_5_
  68.3 1.5 %shard_map.133 = (bf16[18,32,128]{2,1,0:T(8,128)(2,1)S(1)}, f32[144,128]{1,0:T(8,128)S(1)}, bf16[144,128]{1,0:T(8,128)(2,1)S(1)}, bf16[144,128]{1,0:T(8,128)(2,1)S(1)}, bf16[144,128]{1,0:T(8,128)(2,1)S(1)}) custom-call(s32[1,128]{1,0:T(1,128)S(1)} %get-tuple-element.62.refs_0_.near_ids, bf16[64,128,128]{2,1,0:T(8,128)(2,1)S(1)} %bitcast.11, ...), custom_call_target="tpu_custom_call" | custom-call | flops 67108864 | bytes 2613760 | tf_op jit(solution)/shard_map/pallas_call | solution.py:78
  69.9 2.0 %collective-permute-start.28 = (bf16[144,128]{1,0:T(8,128)(2,1)S(1)}, bf16[144,128]{1,0:T(8,128)(2,1)S(1)}, u32[]{:S(2)}, u32[]{:S(2)}) collective-permute-start(bf16[144,128]{1,0:T(8,128)(2,1)S(1)} %get-tuple-element.114), channel_id=1, source_target_pairs={{0,12},{4,8},{8,4},{12,0},{1,13},{5,9},{9,5},{13,1},{2,14},{6,10},... | collective-permute-start | bytes 110600 | tf_op jit(solution)/shard_map/ppermute | solution.py:96
  71.8 0.8 collective-permute-start.29
  72.6 1.7 %collective-permute-start.30 = (bf16[144,128]{1,0:T(8,128)(2,1)S(1)}, bf16[144,128]{1,0:T(8,128)(2,1)S(1)}, u32[]{:S(2)}, u32[]{:S(2)}) collective-permute-start(bf16[144,128]{1,0:T(8,128)(2,1)S(1)} %get-tuple-element.116), channel_id=1, source_target_pairs={{0,8},{4,12},{8,0},{12,4},{1,9},{5,13},{9,1},{13,5},{2,10},{6,14},... | collective-permute-start | bytes 110600 | tf_op jit(solution)/shard_map/ppermute | solution.py:96
  74.3 1.4 %collective-permute-done.28.refs_0_ = bf16[144,128]{1,0:T(8,128)(2,1)S(1)} collective-permute-done((bf16[144,128]{1,0:T(8,128)(2,1)S(1)}, bf16[144,128]{1,0:T(8,128)(2,1)S(1)}, u32[]{:S(2)}, u32[]{:S(2)}) %collective-permute-start.28) | collective-permute-done | bytes 36896 | tf_op jit(solution)/shard_map/ppermute | solution.py:96
  75.7 0.8 collective-permute-done.29.refs_1_
  76.5 1.0 %collective-permute-done.30.refs_2_ = bf16[144,128]{1,0:T(8,128)(2,1)S(1)} collective-permute-done((bf16[144,128]{1,0:T(8,128)(2,1)S(1)}, bf16[144,128]{1,0:T(8,128)(2,1)S(1)}, u32[]{:S(2)}, u32[]{:S(2)}) %collective-permute-start.30) | collective-permute-done | bytes 36896 | tf_op jit(solution)/shard_map/ppermute | solution.py:96
  77.7 1.5 %collective-permute-start.32 = (bf16[176,128]{1,0:T(8,128)(2,1)S(1)}, bf16[176,128]{1,0:T(8,128)(2,1)S(1)}, u32[]{:S(2)}, u32[]{:S(2)}) collective-permute-start(bf16[176,128]{1,0:T(8,128)(2,1)S(1)} %shard_map.135.refs_3_.mine), channel_id=1, source_target_pairs={{0,2},{1,3},{2,0},{3,1},{4,6},{5,7},{6,4},{7,5},{8,10},{9,11},{10,... | collective-permute-start | bytes 135176 | tf_op jit(solution)/shard_map/ppermute | solution.py:96
  79.2 0.3 collective-permute-start.31
  79.5 0.8 shard_map.134
  80.4 1.3 %collective-permute-done.33.refs_6_.refs_2_ = bf16[176,128]{1,0:T(8,128)(2,1)S(1)} collective-permute-done((bf16[176,128]{1,0:T(8,128)(2,1)S(1)}, bf16[176,128]{1,0:T(8,128)(2,1)S(1)}, u32[]{:S(2)}, u32[]{:S(2)}) %collective-permute-start.33) | collective-permute-done | bytes 45088 | tf_op jit(solution)/shard_map/ppermute | solution.py:96
  81.6 0.7 collective-permute-done.32.refs_5_.refs_1_
  82.4 1.2 %collective-permute-start.34 = (bf16[128,128]{1,0:T(8,128)(2,1)S(1)}, bf16[128,128]{1,0:T(8,128)(2,1)S(1)}, u32[]{:S(2)}, u32[]{:S(2)}) collective-permute-start(bf16[128,128]{1,0:T(8,128)(2,1)S(1)} %shard_map.137.refs_0_), channel_id=1, source_target_pairs={{0,4},{4,0},{8,12},{12,8},{1,5},{5,1},{9,13},{13,9},{2,6},{6,2},{1... | collective-permute-start | bytes 98312 | tf_op jit(solution)/shard_map/ppermute | solution.py:96
  83.6 2.9 %shard_map.136 = (bf16[18,128,128]{2,1,0:T(8,128)(2,1)S(1)}, bf16[64,128,128]{2,1,0:T(8,128)(2,1)}) custom-call(s32[1,128]{1,0:T(1,128)S(1)} %get-tuple-element.62.refs_0_.near_ids, bf16[9,128,128]{2,1,0:T(8,128)(2,1)S(1)} %get-tuple-element.108.refs_1_.right, bf16[18,128,128]{2,1,0:T(8,128)(2,1)S(1)} %get-tuple-element.109.refs_2_, ...), custom_call_target="tpu_custom_call" | custom-call | flops 268435456 | bytes 4194304 | tf_op jit(solution)/shard_map/pallas_call | solution.py:664
  86.5 2.5 %shard_map.138 = (bf16[64,128,128]{2,1,0:T(8,128)(2,1)}, f32[64,128]{1,0:T(8,128)}) custom-call(s32[1,128]{1,0:T(1,128)S(1)} %get-tuple-element.62.refs_0_.near_ids, bf16[18,128,128]{2,1,0:T(8,128)(2,1)S(1)} %get-tuple-element.117.left, bf16[9,128,128]{2,1,0:T(8,128)(2,1)S(1)} %get-tuple-element.108.refs_1_.right, ...), custom_call_target="tpu_custom_call", output_to_operand_aliasing={{0}: (3, {})} | custom-call | flops 268435456 | bytes 4194304 | tf_op jit(solution)/shard_map/pallas_call | solution.py:675
  (37 shorter events, 1.5 us)
Async XLA Ops:
  1.5 0.8 copy-start.4
  2.3 5.8 %copy-start = (bf16[1,1,64,128,128]{4,3,2,1,0:T(8,128)(2,1)S(1)}, bf16[1,1,64,128,128]{4,3,2,1,0:T(8,128)(2,1)}, u32[]{:S(2)}) copy-start(bf16[1,1,64,128,128]{4,3,2,1,0:T(8,128)(2,1)} %param.13) | copy-start | bytes 6291460
  2.3 6.9 %collective-permute-start.2 = (bf16[96,128]{1,0:T(8,128)(2,1)S(1)}, bf16[96,128]{1,0:T(8,128)(2,1)S(1)}, u32[]{:S(2)}, u32[]{:S(2)}) collective-permute-start(bf16[96,128]{1,0:T(8,128)(2,1)S(1)} %get-tuple-element.63.after.refs_2_.refs_0_.mine), channel_id=1, source_target_pairs={{0,12},{4,8},{8,4},{12,0},{1,13},{5,9},{9,5},{13,1},{2,14},{6,10},... | collective-permute-start | bytes 73736 | tf_op jit(solution)/shard_map/ppermute | solution.py:96
  7.4 3.8 %collective-permute-start.1 = (bf16[96,128]{1,0:T(8,128)(2,1)S(1)}, bf16[96,128]{1,0:T(8,128)(2,1)S(1)}, u32[]{:S(2)}, u32[]{:S(2)}) collective-permute-start(bf16[96,128]{1,0:T(8,128)(2,1)S(1)} %get-tuple-element.63.after.refs_2_.refs_0_.mine), channel_id=1, source_target_pairs={{0,4},{4,0},{8,12},{12,8},{1,5},{5,1},{9,13},{13,9},{2,6},{6,2},{1... | collective-permute-start | bytes 73736 | tf_op jit(solution)/shard_map/ppermute | solution.py:96
  7.4 4.8 %collective-permute-start = (bf16[96,128]{1,0:T(8,128)(2,1)S(1)}, bf16[96,128]{1,0:T(8,128)(2,1)S(1)}, u32[]{:S(2)}, u32[]{:S(2)}) collective-permute-start(bf16[96,128]{1,0:T(8,128)(2,1)S(1)} %get-tuple-element.63.after.refs_2_.refs_0_.mine), channel_id=1, source_target_pairs={{0,8},{4,12},{8,0},{12,4},{1,9},{5,13},{9,1},{13,5},{2,10},{6,14},... | collective-permute-start | bytes 73736 | tf_op jit(solution)/shard_map/ppermute | solution.py:96
  9.0 13.3 %copy-start.1 = (f32[3,32,288]{2,1,0:T(8,128)S(1)}, f32[3,32,288]{2,1,0:T(8,128)}, u32[]{:S(2)}) copy-start(f32[3,32,288]{2,1,0:T(8,128)} %refs_2_.1) | copy-start | bytes 331780
  9.0 13.3 %copy-start.2 = (bf16[3,32,512]{2,1,0:T(8,128)(2,1)S(1)}, bf16[3,32,512]{2,1,0:T(8,128)(2,1)}, u32[]{:S(2)}) copy-start(bf16[3,32,512]{2,1,0:T(8,128)(2,1)} %param.11) | copy-start | bytes 294916
  9.0 13.3 %copy-start.3 = (f32[8192]{0:T(1024)S(1)}, f32[8192]{0:T(1024)}, u32[]{:S(2)}) copy-start(f32[8192]{0:T(1024)} %param.18) | copy-start | bytes 98308
  13.6 3.8 %collective-permute-start.3 = (bf16[144,128]{1,0:T(8,128)(2,1)S(1)}, bf16[144,128]{1,0:T(8,128)(2,1)S(1)}, u32[]{:S(2)}, u32[]{:S(2)}) collective-permute-start(bf16[144,128]{1,0:T(8,128)(2,1)S(1)} %get-tuple-element.66), channel_id=1, source_target_pairs={{0,3},{1,2},{2,1},{3,0},{4,7},{5,6},{6,5},{7,4},{8,11},{9,10},{10,... | collective-permute-start | bytes 110600 | tf_op jit(solution)/shard_map/ppermute | solution.py:96
  13.7 4.2 %collective-permute-start.4 = (bf16[144,128]{1,0:T(8,128)(2,1)S(1)}, bf16[144,128]{1,0:T(8,128)(2,1)S(1)}, u32[]{:S(2)}, u32[]{:S(2)}) collective-permute-start(bf16[144,128]{1,0:T(8,128)(2,1)S(1)} %get-tuple-element.67), channel_id=1, source_target_pairs={{0,2},{1,3},{2,0},{3,1},{4,6},{5,7},{6,4},{7,5},{8,10},{9,11},{10,... | collective-permute-start | bytes 110600 | tf_op jit(solution)/shard_map/ppermute | solution.py:96
  15.2 2.6 %collective-permute-start.5 = (bf16[144,128]{1,0:T(8,128)(2,1)S(1)}, bf16[144,128]{1,0:T(8,128)(2,1)S(1)}, u32[]{:S(2)}, u32[]{:S(2)}) collective-permute-start(bf16[144,128]{1,0:T(8,128)(2,1)S(1)} %get-tuple-element.68), channel_id=1, source_target_pairs={{0,1},{1,0},{2,3},{3,2},{4,5},{5,4},{6,7},{7,6},{8,9},{9,8},{10,11... | collective-permute-start | bytes 110600 | tf_op jit(solution)/shard_map/ppermute | solution.py:96
  17.9 6.2 %collective-permute-start.8 = (bf16[144,128]{1,0:T(8,128)(2,1)S(1)}, bf16[144,128]{1,0:T(8,128)(2,1)S(1)}, u32[]{:S(2)}, u32[]{:S(2)}) collective-permute-start(bf16[144,128]{1,0:T(8,128)(2,1)S(1)} %get-tuple-element.74), channel_id=1, source_target_pairs={{0,12},{4,8},{8,4},{12,0},{1,13},{5,9},{9,5},{13,1},{2,14},{6,10},... | collective-permute-start | bytes 110600 | tf_op jit(solution)/shard_map/ppermute | solution.py:96
  19.6 4.7 %collective-permute-start.7 = (bf16[144,128]{1,0:T(8,128)(2,1)S(1)}, bf16[144,128]{1,0:T(8,128)(2,1)S(1)}, u32[]{:S(2)}, u32[]{:S(2)}) collective-permute-start(bf16[144,128]{1,0:T(8,128)(2,1)S(1)} %get-tuple-element.74), channel_id=1, source_target_pairs={{0,4},{4,0},{8,12},{12,8},{1,5},{5,1},{9,13},{13,9},{2,6},{6,2},{1... | collective-permute-start | bytes 110600 | tf_op jit(solution)/shard_map/ppermute | solution.py:96
  20.0 5.0 %collective-permute-start.6 = (bf16[144,128]{1,0:T(8,128)(2,1)S(1)}, bf16[144,128]{1,0:T(8,128)(2,1)S(1)}, u32[]{:S(2)}, u32[]{:S(2)}) collective-permute-start(bf16[144,128]{1,0:T(8,128)(2,1)S(1)} %get-tuple-element.74), channel_id=1, source_target_pairs={{0,8},{4,12},{8,0},{12,4},{1,9},{5,13},{9,1},{13,5},{2,10},{6,14},... | collective-permute-start | bytes 110600 | tf_op jit(solution)/shard_map/ppermute | solution.py:96
  26.5 3.8 %collective-permute-start.9 = (bf16[144,128]{1,0:T(8,128)(2,1)S(1)}, bf16[144,128]{1,0:T(8,128)(2,1)S(1)}, u32[]{:S(2)}, u32[]{:S(2)}) collective-permute-start(bf16[144,128]{1,0:T(8,128)(2,1)S(1)} %get-tuple-element.77), channel_id=1, source_target_pairs={{0,3},{1,2},{2,1},{3,0},{4,7},{5,6},{6,5},{7,4},{8,11},{9,10},{10,... | collective-permute-start | bytes 110600 | tf_op jit(solution)/shard_map/ppermute | solution.py:96
  27.1 4.2 %collective-permute-start.10 = (bf16[144,128]{1,0:T(8,128)(2,1)S(1)}, bf16[144,128]{1,0:T(8,128)(2,1)S(1)}, u32[]{:S(2)}, u32[]{:S(2)}) collective-permute-start(bf16[144,128]{1,0:T(8,128)(2,1)S(1)} %get-tuple-element.78), channel_id=1, source_target_pairs={{0,2},{1,3},{2,0},{3,1},{4,6},{5,7},{6,4},{7,5},{8,10},{9,11},{10,... | collective-permute-start | bytes 110600 | tf_op jit(solution)/shard_map/ppermute | solution.py:96
  28.1 3.2 %collective-permute-start.11 = (bf16[144,128]{1,0:T(8,128)(2,1)S(1)}, bf16[144,128]{1,0:T(8,128)(2,1)S(1)}, u32[]{:S(2)}, u32[]{:S(2)}) collective-permute-start(bf16[144,128]{1,0:T(8,128)(2,1)S(1)} %get-tuple-element.79), channel_id=1, source_target_pairs={{0,1},{1,0},{2,3},{3,2},{4,5},{5,4},{6,7},{7,6},{8,9},{9,8},{10,11... | collective-permute-start | bytes 110600 | tf_op jit(solution)/shard_map/ppermute | solution.py:96
  31.3 5.8 %collective-permute-start.14 = (bf16[144,128]{1,0:T(8,128)(2,1)S(1)}, bf16[144,128]{1,0:T(8,128)(2,1)S(1)}, u32[]{:S(2)}, u32[]{:S(2)}) collective-permute-start(bf16[144,128]{1,0:T(8,128)(2,1)S(1)} %get-tuple-element.82), channel_id=1, source_target_pairs={{0,12},{4,8},{8,4},{12,0},{1,13},{5,9},{9,5},{13,1},{2,14},{6,10},... | collective-permute-start | bytes 110600 | tf_op jit(solution)/shard_map/ppermute | solution.py:96
  33.6 4.3 %collective-permute-start.13 = (bf16[144,128]{1,0:T(8,128)(2,1)S(1)}, bf16[144,128]{1,0:T(8,128)(2,1)S(1)}, u32[]{:S(2)}, u32[]{:S(2)}) collective-permute-start(bf16[144,128]{1,0:T(8,128)(2,1)S(1)} %get-tuple-element.82), channel_id=1, source_target_pairs={{0,4},{4,0},{8,12},{12,8},{1,5},{5,1},{9,13},{13,9},{2,6},{6,2},{1... | collective-permute-start | bytes 110600 | tf_op jit(solution)/shard_map/ppermute | solution.py:96
  33.7 5.3 %collective-permute-start.12 = (bf16[144,128]{1,0:T(8,128)(2,1)S(1)}, bf16[144,128]{1,0:T(8,128)(2,1)S(1)}, u32[]{:S(2)}, u32[]{:S(2)}) collective-permute-start(bf16[144,128]{1,0:T(8,128)(2,1)S(1)} %get-tuple-element.82), channel_id=1, source_target_pairs={{0,8},{4,12},{8,0},{12,4},{1,9},{5,13},{9,1},{13,5},{2,10},{6,14},... | collective-permute-start | bytes 110600 | tf_op jit(solution)/shard_map/ppermute | solution.py:96
  40.5 3.7 %collective-permute-start.15 = (bf16[144,128]{1,0:T(8,128)(2,1)S(1)}, bf16[144,128]{1,0:T(8,128)(2,1)S(1)}, u32[]{:S(2)}, u32[]{:S(2)}) collective-permute-start(bf16[144,128]{1,0:T(8,128)(2,1)S(1)} %get-tuple-element.85), channel_id=1, source_target_pairs={{0,3},{1,2},{2,1},{3,0},{4,7},{5,6},{6,5},{7,4},{8,11},{9,10},{10,... | collective-permute-start | bytes 110600 | tf_op jit(solution)/shard_map/ppermute | solution.py:96
  40.6 4.1 %collective-permute-start.16 = (bf16[144,128]{1,0:T(8,128)(2,1)S(1)}, bf16[144,128]{1,0:T(8,128)(2,1)S(1)}, u32[]{:S(2)}, u32[]{:S(2)}) collective-permute-start(bf16[144,128]{1,0:T(8,128)(2,1)S(1)} %get-tuple-element.86), channel_id=1, source_target_pairs={{0,2},{1,3},{2,0},{3,1},{4,6},{5,7},{6,4},{7,5},{8,10},{9,11},{10,... | collective-permute-start | bytes 110600 | tf_op jit(solution)/shard_map/ppermute | solution.py:96
  41.9 2.7 %collective-permute-start.17 = (bf16[144,128]{1,0:T(8,128)(2,1)S(1)}, bf16[144,128]{1,0:T(8,128)(2,1)S(1)}, u32[]{:S(2)}, u32[]{:S(2)}) collective-permute-start(bf16[144,128]{1,0:T(8,128)(2,1)S(1)} %get-tuple-element.87), channel_id=1, source_target_pairs={{0,1},{1,0},{2,3},{3,2},{4,5},{5,4},{6,7},{7,6},{8,9},{9,8},{10,11... | collective-permute-start | bytes 110600 | tf_op jit(solution)/shard_map/ppermute | solution.py:96
  44.7 6.4 %collective-permute-start.18 = (bf16[224,128]{1,0:T(8,128)(2,1)S(1)}, bf16[224,128]{1,0:T(8,128)(2,1)S(1)}, u32[]{:S(2)}, u32[]{:S(2)}) collective-permute-start(bf16[224,128]{1,0:T(8,128)(2,1)S(1)} %get-tuple-element.90), channel_id=1, source_target_pairs={{0,8},{4,12},{8,0},{12,4},{1,9},{5,13},{9,1},{13,5},{2,10},{6,14},... | collective-permute-start | bytes 172040 | tf_op jit(solution)/shard_map/ppermute | solution.py:96
  51.1 3.8 %collective-permute-start.21 = (bf16[144,128]{1,0:T(8,128)(2,1)S(1)}, bf16[144,128]{1,0:T(8,128)(2,1)S(1)}, u32[]{:S(2)}, u32[]{:S(2)}) collective-permute-start(bf16[144,128]{1,0:T(8,128)(2,1)S(1)} %get-tuple-element.93.refs_3_), channel_id=1, source_target_pairs={{0,3},{1,2},{2,1},{3,0},{4,7},{5,6},{6,5},{7,4},{8,11},{9,10},{10,... | collective-permute-start | bytes 110600 | tf_op jit(solution)/shard_map/ppermute | solution.py:96
  51.2 4.1 %collective-permute-start.20 = (bf16[144,128]{1,0:T(8,128)(2,1)S(1)}, bf16[144,128]{1,0:T(8,128)(2,1)S(1)}, u32[]{:S(2)}, u32[]{:S(2)}) collective-permute-start(bf16[144,128]{1,0:T(8,128)(2,1)S(1)} %get-tuple-element.93.refs_3_), channel_id=1, source_target_pairs={{0,2},{1,3},{2,0},{3,1},{4,6},{5,7},{6,4},{7,5},{8,10},{9,11},{10,... | collective-permute-start | bytes 110600 | tf_op jit(solution)/shard_map/ppermute | solution.py:96
  52.7 2.7 %collective-permute-start.19 = (bf16[144,128]{1,0:T(8,128)(2,1)S(1)}, bf16[144,128]{1,0:T(8,128)(2,1)S(1)}, u32[]{:S(2)}, u32[]{:S(2)}) collective-permute-start(bf16[144,128]{1,0:T(8,128)(2,1)S(1)} %get-tuple-element.93.refs_3_), channel_id=1, source_target_pairs={{0,1},{1,0},{2,3},{3,2},{4,5},{5,4},{6,7},{7,6},{8,9},{9,8},{10,11... | collective-permute-start | bytes 110600 | tf_op jit(solution)/shard_map/ppermute | solution.py:96
  56.9 6.0 %collective-permute-start.22 = (bf16[144,128]{1,0:T(8,128)(2,1)S(1)}, bf16[144,128]{1,0:T(8,128)(2,1)S(1)}, u32[]{:S(2)}, u32[]{:S(2)}) collective-permute-start(bf16[144,128]{1,0:T(8,128)(2,1)S(1)} %get-tuple-element.99), channel_id=1, source_target_pairs={{0,12},{4,8},{8,4},{12,0},{1,13},{5,9},{9,5},{13,1},{2,14},{6,10},... | collective-permute-start | bytes 110600 | tf_op jit(solution)/shard_map/ppermute | solution.py:96
  58.8 4.7 %collective-permute-start.23 = (bf16[144,128]{1,0:T(8,128)(2,1)S(1)}, bf16[144,128]{1,0:T(8,128)(2,1)S(1)}, u32[]{:S(2)}, u32[]{:S(2)}) collective-permute-start(bf16[144,128]{1,0:T(8,128)(2,1)S(1)} %get-tuple-element.100), channel_id=1, source_target_pairs={{0,4},{4,0},{8,12},{12,8},{1,5},{5,1},{9,13},{13,9},{2,6},{6,2},{1... | collective-permute-start | bytes 110600 | tf_op jit(solution)/shard_map/ppermute | solution.py:96
  58.8 5.3 %collective-permute-start.24 = (bf16[144,128]{1,0:T(8,128)(2,1)S(1)}, bf16[144,128]{1,0:T(8,128)(2,1)S(1)}, u32[]{:S(2)}, u32[]{:S(2)}) collective-permute-start(bf16[144,128]{1,0:T(8,128)(2,1)S(1)} %get-tuple-element.101), channel_id=1, source_target_pairs={{0,8},{4,12},{8,0},{12,4},{1,9},{5,13},{9,1},{13,5},{2,10},{6,14},... | collective-permute-start | bytes 110600 | tf_op jit(solution)/shard_map/ppermute | solution.py:96
  64.1 3.6 %collective-permute-start.27 = (bf16[144,128]{1,0:T(8,128)(2,1)S(1)}, bf16[144,128]{1,0:T(8,128)(2,1)S(1)}, u32[]{:S(2)}, u32[]{:S(2)}) collective-permute-start(bf16[144,128]{1,0:T(8,128)(2,1)S(1)} %get-tuple-element.103.refs_3_), channel_id=1, source_target_pairs={{0,3},{1,2},{2,1},{3,0},{4,7},{5,6},{6,5},{7,4},{8,11},{9,10},{10,... | collective-permute-start | bytes 110600 | tf_op jit(solution)/shard_map/ppermute | solution.py:96
  64.2 4.1 %collective-permute-start.26 = (bf16[144,128]{1,0:T(8,128)(2,1)S(1)}, bf16[144,128]{1,0:T(8,128)(2,1)S(1)}, u32[]{:S(2)}, u32[]{:S(2)}) collective-permute-start(bf16[144,128]{1,0:T(8,128)(2,1)S(1)} %get-tuple-element.103.refs_3_), channel_id=1, source_target_pairs={{0,2},{1,3},{2,0},{3,1},{4,6},{5,7},{6,4},{7,5},{8,10},{9,11},{10,... | collective-permute-start | bytes 110600 | tf_op jit(solution)/shard_map/ppermute | solution.py:96
  65.4 2.9 %collective-permute-start.25 = (bf16[144,128]{1,0:T(8,128)(2,1)S(1)}, bf16[144,128]{1,0:T(8,128)(2,1)S(1)}, u32[]{:S(2)}, u32[]{:S(2)}) collective-permute-start(bf16[144,128]{1,0:T(8,128)(2,1)S(1)} %get-tuple-element.103.refs_3_), channel_id=1, source_target_pairs={{0,1},{1,0},{2,3},{3,2},{4,5},{5,4},{6,7},{7,6},{8,9},{9,8},{10,11... | collective-permute-start | bytes 110600 | tf_op jit(solution)/shard_map/ppermute | solution.py:96
  69.9 5.8 %collective-permute-start.28 = (bf16[144,128]{1,0:T(8,128)(2,1)S(1)}, bf16[144,128]{1,0:T(8,128)(2,1)S(1)}, u32[]{:S(2)}, u32[]{:S(2)}) collective-permute-start(bf16[144,128]{1,0:T(8,128)(2,1)S(1)} %get-tuple-element.114), channel_id=1, source_target_pairs={{0,12},{4,8},{8,4},{12,0},{1,13},{5,9},{9,5},{13,1},{2,14},{6,10},... | collective-permute-start | bytes 110600 | tf_op jit(solution)/shard_map/ppermute | solution.py:96
  71.8 4.6 %collective-permute-start.29 = (bf16[144,128]{1,0:T(8,128)(2,1)S(1)}, bf16[144,128]{1,0:T(8,128)(2,1)S(1)}, u32[]{:S(2)}, u32[]{:S(2)}) collective-permute-start(bf16[144,128]{1,0:T(8,128)(2,1)S(1)} %get-tuple-element.115), channel_id=1, source_target_pairs={{0,4},{4,0},{8,12},{12,8},{1,5},{5,1},{9,13},{13,9},{2,6},{6,2},{1... | collective-permute-start | bytes 110600 | tf_op jit(solution)/shard_map/ppermute | solution.py:96
  72.6 4.9 %collective-permute-start.30 = (bf16[144,128]{1,0:T(8,128)(2,1)S(1)}, bf16[144,128]{1,0:T(8,128)(2,1)S(1)}, u32[]{:S(2)}, u32[]{:S(2)}) collective-permute-start(bf16[144,128]{1,0:T(8,128)(2,1)S(1)} %get-tuple-element.116), channel_id=1, source_target_pairs={{0,8},{4,12},{8,0},{12,4},{1,9},{5,13},{9,1},{13,5},{2,10},{6,14},... | collective-permute-start | bytes 110600 | tf_op jit(solution)/shard_map/ppermute | solution.py:96
  77.6 4.0 %collective-permute-start.33 = (bf16[176,128]{1,0:T(8,128)(2,1)S(1)}, bf16[176,128]{1,0:T(8,128)(2,1)S(1)}, u32[]{:S(2)}, u32[]{:S(2)}) collective-permute-start(bf16[176,128]{1,0:T(8,128)(2,1)S(1)} %shard_map.135.refs_3_.mine), channel_id=1, source_target_pairs={{0,3},{1,2},{2,1},{3,0},{4,7},{5,6},{6,5},{7,4},{8,11},{9,10},{10,... | collective-permute-start | bytes 135176 | tf_op jit(solution)/shard_map/ppermute | solution.py:96
  77.7 4.7 %collective-permute-start.32 = (bf16[176,128]{1,0:T(8,128)(2,1)S(1)}, bf16[176,128]{1,0:T(8,128)(2,1)S(1)}, u32[]{:S(2)}, u32[]{:S(2)}) collective-permute-start(bf16[176,128]{1,0:T(8,128)(2,1)S(1)} %shard_map.135.refs_3_.mine), channel_id=1, source_target_pairs={{0,2},{1,3},{2,0},{3,1},{4,6},{5,7},{6,4},{7,5},{8,10},{9,11},{10,... | collective-permute-start | bytes 135176 | tf_op jit(solution)/shard_map/ppermute | solution.py:96
  79.2 3.2 %collective-permute-start.31 = (bf16[176,128]{1,0:T(8,128)(2,1)S(1)}, bf16[176,128]{1,0:T(8,128)(2,1)S(1)}, u32[]{:S(2)}, u32[]{:S(2)}) collective-permute-start(bf16[176,128]{1,0:T(8,128)(2,1)S(1)} %shard_map.135.refs_3_.mine), channel_id=1, source_target_pairs={{0,1},{1,0},{2,3},{3,2},{4,5},{5,4},{6,7},{7,6},{8,9},{9,8},{10,11... | collective-permute-start | bytes 135176 | tf_op jit(solution)/shard_map/ppermute | solution.py:96
  82.4 4.1 %collective-permute-start.34 = (bf16[128,128]{1,0:T(8,128)(2,1)S(1)}, bf16[128,128]{1,0:T(8,128)(2,1)S(1)}, u32[]{:S(2)}, u32[]{:S(2)}) collective-permute-start(bf16[128,128]{1,0:T(8,128)(2,1)S(1)} %shard_map.137.refs_0_), channel_id=1, source_target_pairs={{0,4},{4,0},{8,12},{12,8},{1,5},{5,1},{9,13},{13,9},{2,6},{6,2},{1... | collective-permute-start | bytes 98312 | tf_op jit(solution)/shard_map/ppermute | solution.py:96

commit v9 on v8

--- a/solution.py
+++ b/solution.py
@@ -67,7 +67,8 @@
 
     def take_blocks(self, source, base, i):
         first = base + self.first(i)
-        whole = jnp.concatenate([source[first + f] for f in range(self.frame)], axis=1)
+        blocks = [source[0, first + f] + source[1, first + f] for f in range(self.frame)]
+        whole = jnp.concatenate(blocks, axis=1)
         back = lax.rem(self.wide - self.offset(i), jnp.int32(self.wide))
         return self.pack(pltpu.roll(whole, back, 1))
 
@@ -144,23 +145,28 @@
     lax.fori_loop(0, count, lambda i, c: (body(i), c)[1], 0, unroll=count <= 18)
 
 
-def start_kernel(z, rates, numbers, message, own, ids, pad):
+def open_kernel(out):
+    out[...] = jnp.zeros_like(out)
+
+
+def start_kernel(z, after, rates, types, inputs, owner, post, pre, message, own, ids, pad, codes):
     pad[...] = jnp.zeros_like(pad)
     pad[:, 0 : z.local] = rates[...]
     packed = z.pack(pad[...])
     own[...] = packed
-    number = numbers[...]
-    at = 2 * z.frame
-    lists = [number[at + r : at + r + 1] for r in range(3)]
-    pre_lanes = pltpu.roll(lists[2], z.slots, 1)
-    lanes = lax.broadcasted_iota(jnp.int32, (1, BLOCK), 1)
-    ids[...] = jnp.where(lanes < z.slots, lists[0] * z.post + lists[1], pre_lanes)
+    del after
+    ids[...] = jnp.concatenate([owner[0] * z.post + post[0], pre[0]], axis=1)
+    codes[...] = jnp.full(codes.shape, -BLOCK, jnp.int32)
+    codes[0:1, 0 : z.local] = types[...].reshape(1, z.local)
+    codes[1:2, 0 : z.local] = inputs[...].reshape(1, z.local)
+    number = codes[...]
     high = (lax.shift_right_arithmetic(number, 7) + 1).astype(F32)
     low = (number & 127).astype(F32)
     blocks = []
     for f in range(z.frame):
-        for r in (f, z.frame + f):
-            blocks += [high[r : r + 1], low[r : r + 1]]
+        for r in range(2):
+            lanes = slice(f * BLOCK, (f + 1) * BLOCK)
+            blocks += [high[r : r + 1, lanes], low[r : r + 1, lanes]]
     fill = message.shape[0] - z.piece - 4 * z.frame
     extra = jnp.concatenate(blocks + [jnp.zeros((fill, BLOCK), F32)], axis=0)
     message[...] = jnp.concatenate([packed, extra], axis=0).astype(BF16)
@@ -218,7 +224,8 @@
 def multiply_forward(z, c, ids, weights, x, total, own, parts):
     total[...] = jnp.zeros_like(total)
     for s in range(z.slots):
-        total[ids[0, s]] += jnp.dot(x[ids[0, z.slots + s]], weights[s], preferred_element_type=F32)
+        product = jnp.dot(x[ids[0, z.slots + s]], weights[s], preferred_element_type=F32)
+        total[s % 2, ids[0, s]] += product
     for k in range(z.cols):
         both = jnp.concatenate(
             [z.take_blocks(total, 0, c ^ k), z.take_blocks(total, z.post, c ^ k)], axis=0
@@ -335,7 +342,8 @@
     total[...] = jnp.zeros_like(total)
     bring.wait()
     for s in range(z.slots):
-        total[ids[0, z.slots + s]] += jnp.dot(d[ids[0, s]], weights[s], preferred_element_type=F32)
+        product = jnp.dot(d[ids[0, s]], weights[s], preferred_element_type=F32)
+        total[s % 2, ids[0, z.slots + s]] += product
     pieces = [z.take_blocks(total, 0, p ^ k) for k in range(z.rows)]
     for k in range(z.rows):
         other = pieces[k ^ z.half]
@@ -472,7 +480,7 @@
         loop(2 * z.post, lay_left)
         bring.wait()
 
-    products(z, pl.program_id(0) * per_step, per_step, ids, left, right, out)
+    paired_products(z, pl.program_id(0) * per_step, per_step, ids, left, right, out)
 
 
 def products(z, begin, count, ids, left, right, out):
@@ -481,6 +489,20 @@
             left[ids[0, begin + s]], right[ids[0, z.slots + begin + s]], preferred_element_type=F32
         )
         out[s] = product.astype(BF16)
+
+
+def paired_products(z, begin, count, ids, left, right, out):
+    for s in range(0, count, 2):
+        a, b = begin + s, begin + s + 1
+        deltas = jnp.concatenate([left[ids[0, a]], left[ids[0, b]]], axis=1)
+        one, two = right[ids[0, z.slots + a]], right[ids[0, z.slots + b]]
+        none = jnp.zeros_like(one)
+        rates = jnp.concatenate(
+            [jnp.concatenate([one, none], axis=1), jnp.concatenate([none, two], axis=1)], axis=0
+        )
+        product = jnp.dot(deltas, rates, preferred_element_type=F32)
+        out[s] = product[:, 0:BLOCK].astype(BF16)
+        out[s + 1] = product[:, BLOCK:].astype(BF16)
 
 
 def rest_kernel(z, count, begin, per_step, near_ids, left, right, grads, *refs):
@@ -518,12 +540,7 @@
     opening = (z.piece + 4 * z.frame + 15) // 16 * 16
     closing = (z.pair + z.piece + 15) // 16 * 16
 
-    fill = jnp.full((z.wide - local,), -BLOCK, jnp.int32)
-    blank = jnp.zeros((BLOCK - slots,), jnp.int32)
-    lists = [cell_type, fill, input_map, fill]
-    for x in (slot_owner, slot_post, slot_pre):
-        lists += [x.reshape(slots), blank]
-    numbers = jnp.concatenate(lists)
+    (opened,) = call(open_kernel, [shape((8, BLOCK))], [], [], flops=4_000_000_000)
     message, own_rates, ids = call(
         functools.partial(start_kernel, z),
         [
@@ -531,9 +548,8 @@
             shape((z.piece, BLOCK)),
             shape((1, 2 * slots), jnp.int32),
         ],
-        [pltpu.VMEM((batch, z.wide), F32)],
-        [initial_rates, numbers.reshape(numbers.size // BLOCK, BLOCK)],
-        flops=4_000_000_000,
+        [pltpu.VMEM((batch, z.wide), F32), pltpu.VMEM((8, z.wide), jnp.int32)],
+        [opened, initial_rates, cell_type, input_map, slot_owner, slot_post, slot_pre],
     )
     got = share(message, "row")
     weights = weight_blocks.reshape(slots, BLOCK, BLOCK)
@@ -550,13 +566,15 @@
         partner_message = flip(message, "row", z.half)
     pre_sums = pltpu.VMEM((z.pre, batch, BLOCK), F32)
     post_sums = pltpu.VMEM((2 * z.post, batch, BLOCK), F32)
+    pre_totals = pltpu.VMEM((2, z.pre, batch, BLOCK), F32)
+    post_totals = pltpu.VMEM((2, 2 * z.post, batch, BLOCK), F32)
     x_shape = shape((z.pre, batch, BLOCK), BF16)
     row_parts = parcel(z.rows, pair, BF16)
     col_parts = [shape(pair), *parcel(z.cols, pair, BF16)]
     x, own, *parts = call(
         functools.partial(first_kernel, z, len(got)),
         [x_shape, *col_parts],
-        [pre_sums, post_sums, *held_ids],
+        [pre_sums, post_totals, *held_ids],
         [ids, turned, message, *got],
         flops=product_flops,
     )
@@ -590,7 +608,7 @@
         rates, act, cur, x, own, *parts = call(
             functools.partial(forward_kernel, z, t, len(got)),
             [shape(every), shape(pair), shape(pair), x_shape, *col_parts],
-            [pre_sums, post_sums, *held_ids],
+            [pre_sums, post_totals, *held_ids],
             [ids, turned, kept, rates, gain, drive, *got],
             flops=product_flops,
         )
@@ -616,7 +634,7 @@
         d, own, *parts = call(
             functools.partial(back_kernel, z, len(got)),
             [shape((2 * z.post, batch, BLOCK), BF16), shape(pair), *row_parts],
-            [post_sums, pre_sums, *held_ids],
+            [post_sums, pre_totals, *held_ids],
             [ids, weights, base, delta, *got],
             flops=product_flops,
         )

time: 89.2 us -> 88.6 us (level)
    pallas_call x16 -> x17, Pallas kernels: 10.7 us -> 10.7 us  [call(): pl.pallas_call(body, out_shape=outs, in_specs=specs, out_specs=out_specs...]
where the time goes in v9:
time: 88.6 us; the launch traced here: 88.4 us
  starting transfers between devices  38.3 us (43%)
  waiting for transfers between devices  32.2 us (36%)
  Pallas kernels  16.2 us (18%)
    ppermute x35, starting transfers between devices, flip(): return lax.ppermute(x, axis, [(i, i ^ k) for i in range(count)])  38.3 us
    ppermute x35, waiting for transfers between devices, flip(): return lax.ppermute(x, axis, [(i, i ^ k) for i in range(count)])  32.2 us
    pallas_call x17, Pallas kernels, call(): pl.pallas_call(body, out_shape=outs, in_specs=specs, out_specs=out_specs...  10.7 us
    pallas_call x1, Pallas kernels, shards(): pl.pallas_call(functools.partial(grad_kernel, z, len(got), per_step), gri...  2.93 us
    pallas_call x1, Pallas kernels, shards(): pl.pallas_call(functools.partial(rest_kernel, z, len(all_extras), slots -...  2.5 us
  transfers between devices with their start and end apart: 35, of which 28 were waited for; matrix products, arithmetic and copies ran while one was open for 0% of the time, Pallas kernels for 6%

profile of v9, /device:TPU:0, one launch (start us, length us, event | category | flops | bytes accessed | tf_op | source)
XLA Modules:
  0.0 88.4 jit_solution(6845096164511882362)
XLA Ops:
  0.7 0.6 copy-done.6
  1.6 5.1 %collective-permute-start.2 = (bf16[96,128]{1,0:T(8,128)(2,1)S(1)}, bf16[96,128]{1,0:T(8,128)(2,1)S(1)}, u32[]{:S(2)}, u32[]{:S(2)}) collective-permute-start(bf16[96,128]{1,0:T(8,128)(2,1)S(1)} %get-tuple-element.63.after.refs_2_.refs_0_.mine), channel_id=1, source_target_pairs={{0,12},{4,8},{8,4},{12,0},{1,13},{5,9},{9,5},{13,1},{2,14},{6,10},... | collective-permute-start | bytes 73736 | tf_op jit(solution)/shard_map/ppermute | solution.py:97
  6.7 0.6 collective-permute-start
  7.3 1.0 %shard_map.123.refs_1_ = bf16[64,128,128]{2,1,0:T(8,128)(2,1)S(1)} custom-call(bf16[96,128]{1,0:T(8,128)(2,1)S(1)} %get-tuple-element.63.after.refs_2_.refs_0_.mine, bf16[64,128,128]{2,1,0:T(8,128)(2,1)S(1)} %bitcast.5), custom_call_target="tpu_custom_call" | custom-call | bytes 4218880 | tf_op jit(solution)/shard_map/pallas_call | solution.py:79
  8.5 2.0 %collective-permute-done.1.refs_4_.refs_6_ = bf16[96,128]{1,0:T(8,128)(2,1)S(1)} collective-permute-done((bf16[96,128]{1,0:T(8,128)(2,1)S(1)}, bf16[96,128]{1,0:T(8,128)(2,1)S(1)}, u32[]{:S(2)}, u32[]{:S(2)}) %collective-permute-start.1) | collective-permute-done | bytes 24608 | tf_op jit(solution)/shard_map/ppermute | solution.py:97
  10.5 0.9 %collective-permute-done.refs_3_.refs_5_.partner = bf16[96,128]{1,0:T(8,128)(2,1)S(1)} collective-permute-done((bf16[96,128]{1,0:T(8,128)(2,1)S(1)}, bf16[96,128]{1,0:T(8,128)(2,1)S(1)}, u32[]{:S(2)}, u32[]{:S(2)}) %collective-permute-start) | collective-permute-done | bytes 24608 | tf_op jit(solution)/shard_map/ppermute | solution.py:97
  11.4 1.5 %shard_map.124 = (bf16[9,32,128]{2,1,0:T(8,128)(2,1)S(1)}, f32[144,128]{1,0:T(8,128)S(1)}, bf16[144,128]{1,0:T(8,128)(2,1)S(1)}, bf16[144,128]{1,0:T(8,128)(2,1)S(1)}, bf16[144,128]{1,0:T(8,128)(2,1)S(1)}) custom-call(s32[1,128]{1,0:T(1,128)S(1)} %get-tuple-element.62.refs_0_.near_ids, bf16[64,128,128]{2,1,0:T(8,128)(2,1)S(1)} %shard_map.123.refs_1_, ...), custom_call_target="tpu_custom_call" | custom-call | flops 67108864 | bytes 2454016 | tf_op jit(solution)/shard_map/pallas_call | solution.py:79
  13.0 1.6 %collective-permute-start.4 = (bf16[144,128]{1,0:T(8,128)(2,1)S(1)}, bf16[144,128]{1,0:T(8,128)(2,1)S(1)}, u32[]{:S(2)}, u32[]{:S(2)}) collective-permute-start(bf16[144,128]{1,0:T(8,128)(2,1)S(1)} %get-tuple-element.67), channel_id=1, source_target_pairs={{0,2},{1,3},{2,0},{3,1},{4,6},{5,7},{6,4},{7,5},{8,10},{9,11},{10,... | collective-permute-start | bytes 110600 | tf_op jit(solution)/shard_map/ppermute | solution.py:97
  14.5 0.3 collective-permute-start.5
  14.8 1.9 %collective-permute-done.3.refs_1_ = bf16[144,128]{1,0:T(8,128)(2,1)S(1)} collective-permute-done((bf16[144,128]{1,0:T(8,128)(2,1)S(1)}, bf16[144,128]{1,0:T(8,128)(2,1)S(1)}, u32[]{:S(2)}, u32[]{:S(2)}) %collective-permute-start.3) | collective-permute-done | bytes 36896 | tf_op jit(solution)/shard_map/ppermute | solution.py:97
  16.7 0.4 collective-permute-done.4.refs_2_
  17.2 1.7 %collective-permute-start.8 = (bf16[144,128]{1,0:T(8,128)(2,1)S(1)}, bf16[144,128]{1,0:T(8,128)(2,1)S(1)}, u32[]{:S(2)}, u32[]{:S(2)}) collective-permute-start(bf16[144,128]{1,0:T(8,128)(2,1)S(1)} %get-tuple-element.74), channel_id=1, source_target_pairs={{0,12},{4,8},{8,4},{12,0},{1,13},{5,9},{9,5},{13,1},{2,14},{6,10},... | collective-permute-start | bytes 110600 | tf_op jit(solution)/shard_map/ppermute | solution.py:97
  18.9 0.4 collective-permute-start.7
  19.3 2.3 %collective-permute-start.6 = (bf16[144,128]{1,0:T(8,128)(2,1)S(1)}, bf16[144,128]{1,0:T(8,128)(2,1)S(1)}, u32[]{:S(2)}, u32[]{:S(2)}) collective-permute-start(bf16[144,128]{1,0:T(8,128)(2,1)S(1)} %get-tuple-element.74), channel_id=1, source_target_pairs={{0,8},{4,12},{8,0},{12,4},{1,9},{5,13},{9,1},{13,5},{2,10},{6,14},... | collective-permute-start | bytes 110600 | tf_op jit(solution)/shard_map/ppermute | solution.py:97
  21.6 0.9 %shard_map.126 = (f32[288,128]{1,0:T(8,128)S(1)}, f32[288,128]{1,0:T(8,128)S(1)}, f32[3,288,128]{2,1,0:T(8,128)S(1)}, f32[3,72,128]{2,1,0:T(8,128)S(1)}) custom-call(bf16[96,128]{1,0:T(8,128)(2,1)S(1)} %get-tuple-element.63.after.refs_2_.refs_0_.mine, f32[72,128]{1,0:T(8,128)S(1)} %get-tuple-element.70.refs_1_, f32[3,32,288]{2,1,0:T(8,128)S(1)} %copy-done.1, ...), custom_call_target="tpu_custom_call" | custom-call | bytes 1224704 | tf_op jit(solution)/shard_map/pallas_call | solution.py:79
  22.5 0.8 collective-permute-done.8.refs_8_
  23.6 0.7 collective-permute-done.6.refs_6_
  24.3 1.6 %shard_map.127 = (f32[288,128]{1,0:T(8,128)S(1)}, f32[144,128]{1,0:T(8,128)S(1)}, f32[144,128]{1,0:T(8,128)S(1)}, bf16[9,32,128]{2,1,0:T(8,128)(2,1)S(1)}, f32[1...) custom-call(s32[1,128]{1,0:T(1,128)S(1)} %get-tuple-element.62.refs_, ...), custom_call_target="tpu_custom_call" | custom-call | flops 67108864 | bytes 3572224 | tf_op jit(solution)/shard_map/pallas_call | solution.py:79
  25.8 0.5 collective-permute-start.9
  26.3 1.0 %collective-permute-start.10 = (bf16[144,128]{1,0:T(8,128)(2,1)S(1)}, bf16[144,128]{1,0:T(8,128)(2,1)S(1)}, u32[]{:S(2)}, u32[]{:S(2)}) collective-permute-start(bf16[144,128]{1,0:T(8,128)(2,1)S(1)} %get-tuple-element.78), channel_id=1, source_target_pairs={{0,2},{1,3},{2,0},{3,1},{4,6},{5,7},{6,4},{7,5},{8,10},{9,11},{10,... | collective-permute-start | bytes 110600 | tf_op jit(solution)/shard_map/ppermute | solution.py:97
  27.4 0.4 collective-permute-start.11
  27.7 1.9 %collective-permute-done.9.refs_1_ = bf16[144,128]{1,0:T(8,128)(2,1)S(1)} collective-permute-done((bf16[144,128]{1,0:T(8,128)(2,1)S(1)}, bf16[144,128]{1,0:T(8,128)(2,1)S(1)}, u32[]{:S(2)}, u32[]{:S(2)}) %collective-permute-start.9) | collective-permute-done | bytes 36896 | tf_op jit(solution)/shard_map/ppermute | solution.py:97
  29.6 0.9 %collective-permute-done.10.refs_2_ = bf16[144,128]{1,0:T(8,128)(2,1)S(1)} collective-permute-done((bf16[144,128]{1,0:T(8,128)(2,1)S(1)}, bf16[144,128]{1,0:T(8,128)(2,1)S(1)}, u32[]{:S(2)}, u32[]{:S(2)}) %collective-permute-start.10) | collective-permute-done | bytes 36896 | tf_op jit(solution)/shard_map/ppermute | solution.py:97
  30.6 2.3 %collective-permute-start.14 = (bf16[144,128]{1,0:T(8,128)(2,1)S(1)}, bf16[144,128]{1,0:T(8,128)(2,1)S(1)}, u32[]{:S(2)}, u32[]{:S(2)}) collective-permute-start(bf16[144,128]{1,0:T(8,128)(2,1)S(1)} %get-tuple-element.82), channel_id=1, source_target_pairs={{0,12},{4,8},{8,4},{12,0},{1,13},{5,9},{9,5},{13,1},{2,14},{6,10},... | collective-permute-start | bytes 110600 | tf_op jit(solution)/shard_map/ppermute | solution.py:97
  33.0 2.1 %collective-permute-start.12 = (bf16[144,128]{1,0:T(8,128)(2,1)S(1)}, bf16[144,128]{1,0:T(8,128)(2,1)S(1)}, u32[]{:S(2)}, u32[]{:S(2)}) collective-permute-start(bf16[144,128]{1,0:T(8,128)(2,1)S(1)} %get-tuple-element.82), channel_id=1, source_target_pairs={{0,8},{4,12},{8,0},{12,4},{1,9},{5,13},{9,1},{13,5},{2,10},{6,14},... | collective-permute-start | bytes 110600 | tf_op jit(solution)/shard_map/ppermute | solution.py:97
  35.1 1.4 %collective-permute-done.14.refs_8_ = bf16[144,128]{1,0:T(8,128)(2,1)S(1)} collective-permute-done((bf16[144,128]{1,0:T(8,128)(2,1)S(1)}, bf16[144,128]{1,0:T(8,128)(2,1)S(1)}, u32[]{:S(2)}, u32[]{:S(2)}) %collective-permute-start.14) | collective-permute-done | bytes 36896 | tf_op jit(solution)/shard_map/ppermute | solution.py:97
  36.4 0.8 collective-permute-done.13.refs_7_
  37.2 1.0 %collective-permute-done.12.refs_6_ = bf16[144,128]{1,0:T(8,128)(2,1)S(1)} collective-permute-done((bf16[144,128]{1,0:T(8,128)(2,1)S(1)}, bf16[144,128]{1,0:T(8,128)(2,1)S(1)}, u32[]{:S(2)}, u32[]{:S(2)}) %collective-permute-start.12) | collective-permute-done | bytes 36896 | tf_op jit(solution)/shard_map/ppermute | solution.py:97
  38.2 1.6 %shard_map.129 = (f32[288,128]{1,0:T(8,128)S(1)}, f32[144,128]{1,0:T(8,128)S(1)}, f32[144,128]{1,0:T(8,128)S(1)}, bf16[9,32,128]{2,1,0:T(8,128)(2,1)S(1)}, f32[1...) custom-call(s32[1,128]{1,0:T(1,128)S(1)} %get-tuple-element.62.refs_, ...), custom_call_target="tpu_custom_call" | custom-call | flops 67108864 | bytes 3572224 | tf_op jit(solution)/shard_map/pallas_call | solution.py:79
  39.9 1.3 %collective-permute-start.16 = (bf16[144,128]{1,0:T(8,128)(2,1)S(1)}, bf16[144,128]{1,0:T(8,128)(2,1)S(1)}, u32[]{:S(2)}, u32[]{:S(2)}) collective-permute-start(bf16[144,128]{1,0:T(8,128)(2,1)S(1)} %get-tuple-element.86), channel_id=1, source_target_pairs={{0,2},{1,3},{2,0},{3,1},{4,6},{5,7},{6,4},{7,5},{8,10},{9,11},{10,... | collective-permute-start | bytes 110600 | tf_op jit(solution)/shard_map/ppermute | solution.py:97
  41.2 0.5 collective-permute-start.17
  41.7 1.8 %collective-permute-done.15.refs_1_ = bf16[144,128]{1,0:T(8,128)(2,1)S(1)} collective-permute-done((bf16[144,128]{1,0:T(8,128)(2,1)S(1)}, bf16[144,128]{1,0:T(8,128)(2,1)S(1)}, u32[]{:S(2)}, u32[]{:S(2)}) %collective-permute-start.15) | collective-permute-done | bytes 36896 | tf_op jit(solution)/shard_map/ppermute | solution.py:97
  43.5 0.6 collective-permute-done.16.refs_2_
  44.1 2.0 %collective-permute-start.18 = (bf16[224,128]{1,0:T(8,128)(2,1)S(1)}, bf16[224,128]{1,0:T(8,128)(2,1)S(1)}, u32[]{:S(2)}, u32[]{:S(2)}) collective-permute-start(bf16[224,128]{1,0:T(8,128)(2,1)S(1)} %get-tuple-element.90), channel_id=1, source_target_pairs={{0,8},{4,12},{8,0},{12,4},{1,9},{5,13},{9,1},{13,5},{2,10},{6,14},... | collective-permute-start | bytes 172040 | tf_op jit(solution)/shard_map/ppermute | solution.py:97
  46.1 4.4 %collective-permute-done.18.theirs = bf16[224,128]{1,0:T(8,128)(2,1)S(1)} collective-permute-done((bf16[224,128]{1,0:T(8,128)(2,1)S(1)}, bf16[224,128]{1,0:T(8,128)(2,1)S(1)}, u32[]{:S(2)}, u32[]{:S(2)}) %collective-permute-start.18) | collective-permute-done | bytes 57376 | tf_op jit(solution)/shard_map/ppermute | solution.py:97
  50.6 1.4 %collective-permute-start.20 = (bf16[144,128]{1,0:T(8,128)(2,1)S(1)}, bf16[144,128]{1,0:T(8,128)(2,1)S(1)}, u32[]{:S(2)}, u32[]{:S(2)}) collective-permute-start(bf16[144,128]{1,0:T(8,128)(2,1)S(1)} %get-tuple-element.93.refs_3_), channel_id=1, source_target_pairs={{0,2},{1,3},{2,0},{3,1},{4,6},{5,7},{6,4},{7,5},{8,10},{9,11},{10,... | collective-permute-start | bytes 110600 | tf_op jit(solution)/shard_map/ppermute | solution.py:97
  52.0 0.4 collective-permute-start.19
  52.4 1.9 %collective-permute-done.21.refs_6_ = bf16[144,128]{1,0:T(8,128)(2,1)S(1)} collective-permute-done((bf16[144,128]{1,0:T(8,128)(2,1)S(1)}, bf16[144,128]{1,0:T(8,128)(2,1)S(1)}, u32[]{:S(2)}, u32[]{:S(2)}) %collective-permute-start.21) | collective-permute-done | bytes 36896 | tf_op jit(solution)/shard_map/ppermute | solution.py:97
  54.3 0.4 collective-permute-done.20.refs_5_
  54.7 1.5 %shard_map.132 = (bf16[18,32,128]{2,1,0:T(8,128)(2,1)S(1)}, f32[144,128]{1,0:T(8,128)S(1)}, bf16[144,128]{1,0:T(8,128)(2,1)S(1)}, bf16[144,128]{1,0:T(8,128)(2,1)S(1)}, bf16[144,128]{1,0:T(8,128)(2,1)S(1)}) custom-call(s32[1,128]{1,0:T(1,128)S(1)} %get-tuple-element.62.refs_0_.near_ids, bf16[64,128,128]{2,1,0:T(8,128)(2,1)S(1)} %bitcast.6, ...), custom_call_target="tpu_custom_call" | custom-call | flops 67108864 | bytes 2613760 | tf_op jit(solution)/shard_map/pallas_call | solution.py:79
  56.3 1.9 %collective-permute-start.22 = (bf16[144,128]{1,0:T(8,128)(2,1)S(1)}, bf16[144,128]{1,0:T(8,128)(2,1)S(1)}, u32[]{:S(2)}, u32[]{:S(2)}) collective-permute-start(bf16[144,128]{1,0:T(8,128)(2,1)S(1)} %get-tuple-element.99), channel_id=1, source_target_pairs={{0,12},{4,8},{8,4},{12,0},{1,13},{5,9},{9,5},{13,1},{2,14},{6,10},... | collective-permute-start | bytes 110600 | tf_op jit(solution)/shard_map/ppermute | solution.py:97
  58.1 2.6 %collective-permute-start.24 = (bf16[144,128]{1,0:T(8,128)(2,1)S(1)}, bf16[144,128]{1,0:T(8,128)(2,1)S(1)}, u32[]{:S(2)}, u32[]{:S(2)}) collective-permute-start(bf16[144,128]{1,0:T(8,128)(2,1)S(1)} %get-tuple-element.101), channel_id=1, source_target_pairs={{0,8},{4,12},{8,0},{12,4},{1,9},{5,13},{9,1},{13,5},{2,10},{6,14},... | collective-permute-start | bytes 110600 | tf_op jit(solution)/shard_map/ppermute | solution.py:97
  60.7 1.5 %collective-permute-done.22.refs_0_ = bf16[144,128]{1,0:T(8,128)(2,1)S(1)} collective-permute-done((bf16[144,128]{1,0:T(8,128)(2,1)S(1)}, bf16[144,128]{1,0:T(8,128)(2,1)S(1)}, u32[]{:S(2)}, u32[]{:S(2)}) %collective-permute-start.22) | collective-permute-done | bytes 36896 | tf_op jit(solution)/shard_map/ppermute | solution.py:97
  62.2 0.5 collective-permute-done.23.refs_1_
  62.8 0.6 collective-permute-done.24.refs_2_
  63.5 1.2 %collective-permute-start.26 = (bf16[144,128]{1,0:T(8,128)(2,1)S(1)}, bf16[144,128]{1,0:T(8,128)(2,1)S(1)}, u32[]{:S(2)}, u32[]{:S(2)}) collective-permute-start(bf16[144,128]{1,0:T(8,128)(2,1)S(1)} %get-tuple-element.103.refs_3_), channel_id=1, source_target_pairs={{0,2},{1,3},{2,0},{3,1},{4,6},{5,7},{6,4},{7,5},{8,10},{9,11},{10,... | collective-permute-start | bytes 110600 | tf_op jit(solution)/shard_map/ppermute | solution.py:97
  64.7 0.6 collective-permute-start.25
  65.3 1.7 %collective-permute-done.27.refs_6_ = bf16[144,128]{1,0:T(8,128)(2,1)S(1)} collective-permute-done((bf16[144,128]{1,0:T(8,128)(2,1)S(1)}, bf16[144,128]{1,0:T(8,128)(2,1)S(1)}, u32[]{:S(2)}, u32[]{:S(2)}) %collective-permute-start.27) | collective-permute-done | bytes 36896 | tf_op jit(solution)/shard_map/ppermute | solution.py:97
  67.0 0.7 collective-permute-done.26.refs_5_
  67.7 1.5 %shard_map.134 = (bf16[18,32,128]{2,1,0:T(8,128)(2,1)S(1)}, f32[144,128]{1,0:T(8,128)S(1)}, bf16[144,128]{1,0:T(8,128)(2,1)S(1)}, bf16[144,128]{1,0:T(8,128)(2,1)S(1)}, bf16[144,128]{1,0:T(8,128)(2,1)S(1)}) custom-call(s32[1,128]{1,0:T(1,128)S(1)} %get-tuple-element.62.refs_0_.near_ids, bf16[64,128,128]{2,1,0:T(8,128)(2,1)S(1)} %bitcast.7, ...), custom_call_target="tpu_custom_call" | custom-call | flops 67108864 | bytes 2613760 | tf_op jit(solution)/shard_map/pallas_call | solution.py:79
  69.2 2.1 %collective-permute-start.28 = (bf16[144,128]{1,0:T(8,128)(2,1)S(1)}, bf16[144,128]{1,0:T(8,128)(2,1)S(1)}, u32[]{:S(2)}, u32[]{:S(2)}) collective-permute-start(bf16[144,128]{1,0:T(8,128)(2,1)S(1)} %get-tuple-element.114), channel_id=1, source_target_pairs={{0,12},{4,8},{8,4},{12,0},{1,13},{5,9},{9,5},{13,1},{2,14},{6,10},... | collective-permute-start | bytes 110600 | tf_op jit(solution)/shard_map/ppermute | solution.py:97
  71.3 0.7 collective-permute-start.29
  72.0 1.6 %collective-permute-start.30 = (bf16[144,128]{1,0:T(8,128)(2,1)S(1)}, bf16[144,128]{1,0:T(8,128)(2,1)S(1)}, u32[]{:S(2)}, u32[]{:S(2)}) collective-permute-start(bf16[144,128]{1,0:T(8,128)(2,1)S(1)} %get-tuple-element.116), channel_id=1, source_target_pairs={{0,8},{4,12},{8,0},{12,4},{1,9},{5,13},{9,1},{13,5},{2,10},{6,14},... | collective-permute-start | bytes 110600 | tf_op jit(solution)/shard_map/ppermute | solution.py:97
  73.6 1.4 %collective-permute-done.28.refs_0_ = bf16[144,128]{1,0:T(8,128)(2,1)S(1)} collective-permute-done((bf16[144,128]{1,0:T(8,128)(2,1)S(1)}, bf16[144,128]{1,0:T(8,128)(2,1)S(1)}, u32[]{:S(2)}, u32[]{:S(2)}) %collective-permute-start.28) | collective-permute-done | bytes 36896 | tf_op jit(solution)/shard_map/ppermute | solution.py:97
  75.0 0.8 collective-permute-done.29.refs_1_
  75.8 1.1 %collective-permute-done.30.refs_2_ = bf16[144,128]{1,0:T(8,128)(2,1)S(1)} collective-permute-done((bf16[144,128]{1,0:T(8,128)(2,1)S(1)}, bf16[144,128]{1,0:T(8,128)(2,1)S(1)}, u32[]{:S(2)}, u32[]{:S(2)}) %collective-permute-start.30) | collective-permute-done | bytes 36896 | tf_op jit(solution)/shard_map/ppermute | solution.py:97
  77.1 1.4 %collective-permute-start.32 = (bf16[176,128]{1,0:T(8,128)(2,1)S(1)}, bf16[176,128]{1,0:T(8,128)(2,1)S(1)}, u32[]{:S(2)}, u32[]{:S(2)}) collective-permute-start(bf16[176,128]{1,0:T(8,128)(2,1)S(1)} %shard_map.136.refs_3_.mine), channel_id=1, source_target_pairs={{0,2},{1,3},{2,0},{3,1},{4,6},{5,7},{6,4},{7,5},{8,10},{9,11},{10,... | collective-permute-start | bytes 135176 | tf_op jit(solution)/shard_map/ppermute | solution.py:97
  78.5 0.4 collective-permute-start.31
  78.9 0.8 shard_map.135
  79.7 1.3 %collective-permute-done.33.refs_6_.refs_2_ = bf16[176,128]{1,0:T(8,128)(2,1)S(1)} collective-permute-done((bf16[176,128]{1,0:T(8,128)(2,1)S(1)}, bf16[176,128]{1,0:T(8,128)(2,1)S(1)}, u32[]{:S(2)}, u32[]{:S(2)}) %collective-permute-start.33) | collective-permute-done | bytes 45088 | tf_op jit(solution)/shard_map/ppermute | solution.py:97
  81.0 0.6 collective-permute-done.32.refs_5_.refs_1_
  81.7 1.3 %collective-permute-start.34 = (bf16[128,128]{1,0:T(8,128)(2,1)S(1)}, bf16[128,128]{1,0:T(8,128)(2,1)S(1)}, u32[]{:S(2)}, u32[]{:S(2)}) collective-permute-start(bf16[128,128]{1,0:T(8,128)(2,1)S(1)} %shard_map.138.refs_0_), channel_id=1, source_target_pairs={{0,4},{4,0},{8,12},{12,8},{1,5},{5,1},{9,13},{13,9},{2,6},{6,2},{1... | collective-permute-start | bytes 98312 | tf_op jit(solution)/shard_map/ppermute | solution.py:97
  83.0 2.9 %shard_map.137 = (bf16[18,128,128]{2,1,0:T(8,128)(2,1)S(1)}, bf16[64,128,128]{2,1,0:T(8,128)(2,1)}) custom-call(s32[1,128]{1,0:T(1,128)S(1)} %get-tuple-element.62.refs_0_.near_ids, bf16[9,128,128]{2,1,0:T(8,128)(2,1)S(1)} %get-tuple-element.108.refs_1_.right, bf16[18,128,128]{2,1,0:T(8,128)(2,1)S(1)} %get-tuple-element.109.refs_2_, ...), custom_call_target="tpu_custom_call" | custom-call | flops 268435456 | bytes 4194304 | tf_op jit(solution)/shard_map/pallas_call | solution.py:682
  85.9 2.5 %shard_map.139 = (bf16[64,128,128]{2,1,0:T(8,128)(2,1)}, f32[64,128]{1,0:T(8,128)}) custom-call(s32[1,128]{1,0:T(1,128)S(1)} %get-tuple-element.62.refs_0_.near_ids, bf16[18,128,128]{2,1,0:T(8,128)(2,1)S(1)} %get-tuple-element.117.left, bf16[9,128,128]{2,1,0:T(8,128)(2,1)S(1)} %get-tuple-element.108.refs_1_.right, ...), custom_call_target="tpu_custom_call", output_to_operand_aliasing={{0}: (3, {})} | custom-call | flops 268435456 | bytes 4194304 | tf_op jit(solution)/shard_map/pallas_call | solution.py:693
  (45 shorter events, 1.4 us)
Async XLA Ops:
  0.6 0.7 copy-start.6
  0.6 0.7 copy-start.5
  0.7 0.7 copy-start.9
  0.7 0.7 copy-start.8
  0.7 0.7 copy-start.7
  0.7 0.8 copy-start.3
  0.7 6.6 %copy-start = (bf16[1,1,64,128,128]{4,3,2,1,0:T(8,128)(2,1)S(1)}, bf16[1,1,64,128,128]{4,3,2,1,0:T(8,128)(2,1)}, u32[]{:S(2)}) copy-start(bf16[1,1,64,128,128]{4,3,2,1,0:T(8,128)(2,1)} %param.13) | copy-start | bytes 6291460
  1.6 6.9 %collective-permute-start.2 = (bf16[96,128]{1,0:T(8,128)(2,1)S(1)}, bf16[96,128]{1,0:T(8,128)(2,1)S(1)}, u32[]{:S(2)}, u32[]{:S(2)}) collective-permute-start(bf16[96,128]{1,0:T(8,128)(2,1)S(1)} %get-tuple-element.63.after.refs_2_.refs_0_.mine), channel_id=1, source_target_pairs={{0,12},{4,8},{8,4},{12,0},{1,13},{5,9},{9,5},{13,1},{2,14},{6,10},... | collective-permute-start | bytes 73736 | tf_op jit(solution)/shard_map/ppermute | solution.py:97
  6.6 3.8 %collective-permute-start.1 = (bf16[96,128]{1,0:T(8,128)(2,1)S(1)}, bf16[96,128]{1,0:T(8,128)(2,1)S(1)}, u32[]{:S(2)}, u32[]{:S(2)}) collective-permute-start(bf16[96,128]{1,0:T(8,128)(2,1)S(1)} %get-tuple-element.63.after.refs_2_.refs_0_.mine), channel_id=1, source_target_pairs={{0,4},{4,0},{8,12},{12,8},{1,5},{5,1},{9,13},{13,9},{2,6},{6,2},{1... | collective-permute-start | bytes 73736 | tf_op jit(solution)/shard_map/ppermute | solution.py:97
  6.7 4.8 %collective-permute-start = (bf16[96,128]{1,0:T(8,128)(2,1)S(1)}, bf16[96,128]{1,0:T(8,128)(2,1)S(1)}, u32[]{:S(2)}, u32[]{:S(2)}) collective-permute-start(bf16[96,128]{1,0:T(8,128)(2,1)S(1)} %get-tuple-element.63.after.refs_2_.refs_0_.mine), channel_id=1, source_target_pairs={{0,8},{4,12},{8,0},{12,4},{1,9},{5,13},{9,1},{13,5},{2,10},{6,14},... | collective-permute-start | bytes 73736 | tf_op jit(solution)/shard_map/ppermute | solution.py:97
  8.3 13.3 %copy-start.1 = (f32[3,32,288]{2,1,0:T(8,128)S(1)}, f32[3,32,288]{2,1,0:T(8,128)}, u32[]{:S(2)}) copy-start(f32[3,32,288]{2,1,0:T(8,128)} %refs_2_.1) | copy-start | bytes 331780
  8.3 13.3 %copy-start.2 = (bf16[3,32,512]{2,1,0:T(8,128)(2,1)S(1)}, bf16[3,32,512]{2,1,0:T(8,128)(2,1)}, u32[]{:S(2)}) copy-start(bf16[3,32,512]{2,1,0:T(8,128)(2,1)} %param.11) | copy-start | bytes 294916
  8.3 13.3 %copy-start.4 = (f32[8192]{0:T(1024)S(1)}, f32[8192]{0:T(1024)}, u32[]{:S(2)}) copy-start(f32[8192]{0:T(1024)} %param.18) | copy-start | bytes 98308
  12.9 3.8 %collective-permute-start.3 = (bf16[144,128]{1,0:T(8,128)(2,1)S(1)}, bf16[144,128]{1,0:T(8,128)(2,1)S(1)}, u32[]{:S(2)}, u32[]{:S(2)}) collective-permute-start(bf16[144,128]{1,0:T(8,128)(2,1)S(1)} %get-tuple-element.66), channel_id=1, source_target_pairs={{0,3},{1,2},{2,1},{3,0},{4,7},{5,6},{6,5},{7,4},{8,11},{9,10},{10,... | collective-permute-start | bytes 110600 | tf_op jit(solution)/shard_map/ppermute | solution.py:97
  13.0 4.2 %collective-permute-start.4 = (bf16[144,128]{1,0:T(8,128)(2,1)S(1)}, bf16[144,128]{1,0:T(8,128)(2,1)S(1)}, u32[]{:S(2)}, u32[]{:S(2)}) collective-permute-start(bf16[144,128]{1,0:T(8,128)(2,1)S(1)} %get-tuple-element.67), channel_id=1, source_target_pairs={{0,2},{1,3},{2,0},{3,1},{4,6},{5,7},{6,4},{7,5},{8,10},{9,11},{10,... | collective-permute-start | bytes 110600 | tf_op jit(solution)/shard_map/ppermute | solution.py:97
  14.5 2.6 %collective-permute-start.5 = (bf16[144,128]{1,0:T(8,128)(2,1)S(1)}, bf16[144,128]{1,0:T(8,128)(2,1)S(1)}, u32[]{:S(2)}, u32[]{:S(2)}) collective-permute-start(bf16[144,128]{1,0:T(8,128)(2,1)S(1)} %get-tuple-element.68), channel_id=1, source_target_pairs={{0,1},{1,0},{2,3},{3,2},{4,5},{5,4},{6,7},{7,6},{8,9},{9,8},{10,11... | collective-permute-start | bytes 110600 | tf_op jit(solution)/shard_map/ppermute | solution.py:97
  17.2 6.2 %collective-permute-start.8 = (bf16[144,128]{1,0:T(8,128)(2,1)S(1)}, bf16[144,128]{1,0:T(8,128)(2,1)S(1)}, u32[]{:S(2)}, u32[]{:S(2)}) collective-permute-start(bf16[144,128]{1,0:T(8,128)(2,1)S(1)} %get-tuple-element.74), channel_id=1, source_target_pairs={{0,12},{4,8},{8,4},{12,0},{1,13},{5,9},{9,5},{13,1},{2,14},{6,10},... | collective-permute-start | bytes 110600 | tf_op jit(solution)/shard_map/ppermute | solution.py:97
  18.9 4.7 %collective-permute-start.7 = (bf16[144,128]{1,0:T(8,128)(2,1)S(1)}, bf16[144,128]{1,0:T(8,128)(2,1)S(1)}, u32[]{:S(2)}, u32[]{:S(2)}) collective-permute-start(bf16[144,128]{1,0:T(8,128)(2,1)S(1)} %get-tuple-element.74), channel_id=1, source_target_pairs={{0,4},{4,0},{8,12},{12,8},{1,5},{5,1},{9,13},{13,9},{2,6},{6,2},{1... | collective-permute-start | bytes 110600 | tf_op jit(solution)/shard_map/ppermute | solution.py:97
  19.3 5.0 %collective-permute-start.6 = (bf16[144,128]{1,0:T(8,128)(2,1)S(1)}, bf16[144,128]{1,0:T(8,128)(2,1)S(1)}, u32[]{:S(2)}, u32[]{:S(2)}) collective-permute-start(bf16[144,128]{1,0:T(8,128)(2,1)S(1)} %get-tuple-element.74), channel_id=1, source_target_pairs={{0,8},{4,12},{8,0},{12,4},{1,9},{5,13},{9,1},{13,5},{2,10},{6,14},... | collective-permute-start | bytes 110600 | tf_op jit(solution)/shard_map/ppermute | solution.py:97
  25.8 3.8 %collective-permute-start.9 = (bf16[144,128]{1,0:T(8,128)(2,1)S(1)}, bf16[144,128]{1,0:T(8,128)(2,1)S(1)}, u32[]{:S(2)}, u32[]{:S(2)}) collective-permute-start(bf16[144,128]{1,0:T(8,128)(2,1)S(1)} %get-tuple-element.77), channel_id=1, source_target_pairs={{0,3},{1,2},{2,1},{3,0},{4,7},{5,6},{6,5},{7,4},{8,11},{9,10},{10,... | collective-permute-start | bytes 110600 | tf_op jit(solution)/shard_map/ppermute | solution.py:97
  26.3 4.2 %collective-permute-start.10 = (bf16[144,128]{1,0:T(8,128)(2,1)S(1)}, bf16[144,128]{1,0:T(8,128)(2,1)S(1)}, u32[]{:S(2)}, u32[]{:S(2)}) collective-permute-start(bf16[144,128]{1,0:T(8,128)(2,1)S(1)} %get-tuple-element.78), channel_id=1, source_target_pairs={{0,2},{1,3},{2,0},{3,1},{4,6},{5,7},{6,4},{7,5},{8,10},{9,11},{10,... | collective-permute-start | bytes 110600 | tf_op jit(solution)/shard_map/ppermute | solution.py:97
  27.4 3.2 %collective-permute-start.11 = (bf16[144,128]{1,0:T(8,128)(2,1)S(1)}, bf16[144,128]{1,0:T(8,128)(2,1)S(1)}, u32[]{:S(2)}, u32[]{:S(2)}) collective-permute-start(bf16[144,128]{1,0:T(8,128)(2,1)S(1)} %get-tuple-element.79), channel_id=1, source_target_pairs={{0,1},{1,0},{2,3},{3,2},{4,5},{5,4},{6,7},{7,6},{8,9},{9,8},{10,11... | collective-permute-start | bytes 110600 | tf_op jit(solution)/shard_map/ppermute | solution.py:97
  30.6 5.8 %collective-permute-start.14 = (bf16[144,128]{1,0:T(8,128)(2,1)S(1)}, bf16[144,128]{1,0:T(8,128)(2,1)S(1)}, u32[]{:S(2)}, u32[]{:S(2)}) collective-permute-start(bf16[144,128]{1,0:T(8,128)(2,1)S(1)} %get-tuple-element.82), channel_id=1, source_target_pairs={{0,12},{4,8},{8,4},{12,0},{1,13},{5,9},{9,5},{13,1},{2,14},{6,10},... | collective-permute-start | bytes 110600 | tf_op jit(solution)/shard_map/ppermute | solution.py:97
  32.9 4.3 %collective-permute-start.13 = (bf16[144,128]{1,0:T(8,128)(2,1)S(1)}, bf16[144,128]{1,0:T(8,128)(2,1)S(1)}, u32[]{:S(2)}, u32[]{:S(2)}) collective-permute-start(bf16[144,128]{1,0:T(8,128)(2,1)S(1)} %get-tuple-element.82), channel_id=1, source_target_pairs={{0,4},{4,0},{8,12},{12,8},{1,5},{5,1},{9,13},{13,9},{2,6},{6,2},{1... | collective-permute-start | bytes 110600 | tf_op jit(solution)/shard_map/ppermute | solution.py:97
  33.0 5.3 %collective-permute-start.12 = (bf16[144,128]{1,0:T(8,128)(2,1)S(1)}, bf16[144,128]{1,0:T(8,128)(2,1)S(1)}, u32[]{:S(2)}, u32[]{:S(2)}) collective-permute-start(bf16[144,128]{1,0:T(8,128)(2,1)S(1)} %get-tuple-element.82), channel_id=1, source_target_pairs={{0,8},{4,12},{8,0},{12,4},{1,9},{5,13},{9,1},{13,5},{2,10},{6,14},... | collective-permute-start | bytes 110600 | tf_op jit(solution)/shard_map/ppermute | solution.py:97
  39.8 3.7 %collective-permute-start.15 = (bf16[144,128]{1,0:T(8,128)(2,1)S(1)}, bf16[144,128]{1,0:T(8,128)(2,1)S(1)}, u32[]{:S(2)}, u32[]{:S(2)}) collective-permute-start(bf16[144,128]{1,0:T(8,128)(2,1)S(1)} %get-tuple-element.85), channel_id=1, source_target_pairs={{0,3},{1,2},{2,1},{3,0},{4,7},{5,6},{6,5},{7,4},{8,11},{9,10},{10,... | collective-permute-start | bytes 110600 | tf_op jit(solution)/shard_map/ppermute | solution.py:97
  39.9 4.2 %collective-permute-start.16 = (bf16[144,128]{1,0:T(8,128)(2,1)S(1)}, bf16[144,128]{1,0:T(8,128)(2,1)S(1)}, u32[]{:S(2)}, u32[]{:S(2)}) collective-permute-start(bf16[144,128]{1,0:T(8,128)(2,1)S(1)} %get-tuple-element.86), channel_id=1, source_target_pairs={{0,2},{1,3},{2,0},{3,1},{4,6},{5,7},{6,4},{7,5},{8,10},{9,11},{10,... | collective-permute-start | bytes 110600 | tf_op jit(solution)/shard_map/ppermute | solution.py:97
  41.2 2.8 %collective-permute-start.17 = (bf16[144,128]{1,0:T(8,128)(2,1)S(1)}, bf16[144,128]{1,0:T(8,128)(2,1)S(1)}, u32[]{:S(2)}, u32[]{:S(2)}) collective-permute-start(bf16[144,128]{1,0:T(8,128)(2,1)S(1)} %get-tuple-element.87), channel_id=1, source_target_pairs={{0,1},{1,0},{2,3},{3,2},{4,5},{5,4},{6,7},{7,6},{8,9},{9,8},{10,11... | collective-permute-start | bytes 110600 | tf_op jit(solution)/shard_map/ppermute | solution.py:97
  44.1 6.4 %collective-permute-start.18 = (bf16[224,128]{1,0:T(8,128)(2,1)S(1)}, bf16[224,128]{1,0:T(8,128)(2,1)S(1)}, u32[]{:S(2)}, u32[]{:S(2)}) collective-permute-start(bf16[224,128]{1,0:T(8,128)(2,1)S(1)} %get-tuple-element.90), channel_id=1, source_target_pairs={{0,8},{4,12},{8,0},{12,4},{1,9},{5,13},{9,1},{13,5},{2,10},{6,14},... | collective-permute-start | bytes 172040 | tf_op jit(solution)/shard_map/ppermute | solution.py:97
  50.5 3.8 %collective-permute-start.21 = (bf16[144,128]{1,0:T(8,128)(2,1)S(1)}, bf16[144,128]{1,0:T(8,128)(2,1)S(1)}, u32[]{:S(2)}, u32[]{:S(2)}) collective-permute-start(bf16[144,128]{1,0:T(8,128)(2,1)S(1)} %get-tuple-element.93.refs_3_), channel_id=1, source_target_pairs={{0,3},{1,2},{2,1},{3,0},{4,7},{5,6},{6,5},{7,4},{8,11},{9,10},{10,... | collective-permute-start | bytes 110600 | tf_op jit(solution)/shard_map/ppermute | solution.py:97
  50.6 4.2 %collective-permute-start.20 = (bf16[144,128]{1,0:T(8,128)(2,1)S(1)}, bf16[144,128]{1,0:T(8,128)(2,1)S(1)}, u32[]{:S(2)}, u32[]{:S(2)}) collective-permute-start(bf16[144,128]{1,0:T(8,128)(2,1)S(1)} %get-tuple-element.93.refs_3_), channel_id=1, source_target_pairs={{0,2},{1,3},{2,0},{3,1},{4,6},{5,7},{6,4},{7,5},{8,10},{9,11},{10,... | collective-permute-start | bytes 110600 | tf_op jit(solution)/shard_map/ppermute | solution.py:97
  52.0 2.8 %collective-permute-start.19 = (bf16[144,128]{1,0:T(8,128)(2,1)S(1)}, bf16[144,128]{1,0:T(8,128)(2,1)S(1)}, u32[]{:S(2)}, u32[]{:S(2)}) collective-permute-start(bf16[144,128]{1,0:T(8,128)(2,1)S(1)} %get-tuple-element.93.refs_3_), channel_id=1, source_target_pairs={{0,1},{1,0},{2,3},{3,2},{4,5},{5,4},{6,7},{7,6},{8,9},{9,8},{10,11... | collective-permute-start | bytes 110600 | tf_op jit(solution)/shard_map/ppermute | solution.py:97
  56.3 6.0 %collective-permute-start.22 = (bf16[144,128]{1,0:T(8,128)(2,1)S(1)}, bf16[144,128]{1,0:T(8,128)(2,1)S(1)}, u32[]{:S(2)}, u32[]{:S(2)}) collective-permute-start(bf16[144,128]{1,0:T(8,128)(2,1)S(1)} %get-tuple-element.99), channel_id=1, source_target_pairs={{0,12},{4,8},{8,4},{12,0},{1,13},{5,9},{9,5},{13,1},{2,14},{6,10},... | collective-permute-start | bytes 110600 | tf_op jit(solution)/shard_map/ppermute | solution.py:97
  58.1 4.7 %collective-permute-start.23 = (bf16[144,128]{1,0:T(8,128)(2,1)S(1)}, bf16[144,128]{1,0:T(8,128)(2,1)S(1)}, u32[]{:S(2)}, u32[]{:S(2)}) collective-permute-start(bf16[144,128]{1,0:T(8,128)(2,1)S(1)} %get-tuple-element.100), channel_id=1, source_target_pairs={{0,4},{4,0},{8,12},{12,8},{1,5},{5,1},{9,13},{13,9},{2,6},{6,2},{1... | collective-permute-start | bytes 110600 | tf_op jit(solution)/shard_map/ppermute | solution.py:97
  58.1 5.3 %collective-permute-start.24 = (bf16[144,128]{1,0:T(8,128)(2,1)S(1)}, bf16[144,128]{1,0:T(8,128)(2,1)S(1)}, u32[]{:S(2)}, u32[]{:S(2)}) collective-permute-start(bf16[144,128]{1,0:T(8,128)(2,1)S(1)} %get-tuple-element.101), channel_id=1, source_target_pairs={{0,8},{4,12},{8,0},{12,4},{1,9},{5,13},{9,1},{13,5},{2,10},{6,14},... | collective-permute-start | bytes 110600 | tf_op jit(solution)/shard_map/ppermute | solution.py:97
  63.4 3.6 %collective-permute-start.27 = (bf16[144,128]{1,0:T(8,128)(2,1)S(1)}, bf16[144,128]{1,0:T(8,128)(2,1)S(1)}, u32[]{:S(2)}, u32[]{:S(2)}) collective-permute-start(bf16[144,128]{1,0:T(8,128)(2,1)S(1)} %get-tuple-element.103.refs_3_), channel_id=1, source_target_pairs={{0,3},{1,2},{2,1},{3,0},{4,7},{5,6},{6,5},{7,4},{8,11},{9,10},{10,... | collective-permute-start | bytes 110600 | tf_op jit(solution)/shard_map/ppermute | solution.py:97
  63.5 4.2 %collective-permute-start.26 = (bf16[144,128]{1,0:T(8,128)(2,1)S(1)}, bf16[144,128]{1,0:T(8,128)(2,1)S(1)}, u32[]{:S(2)}, u32[]{:S(2)}) collective-permute-start(bf16[144,128]{1,0:T(8,128)(2,1)S(1)} %get-tuple-element.103.refs_3_), channel_id=1, source_target_pairs={{0,2},{1,3},{2,0},{3,1},{4,6},{5,7},{6,4},{7,5},{8,10},{9,11},{10,... | collective-permute-start | bytes 110600 | tf_op jit(solution)/shard_map/ppermute | solution.py:97
  64.7 2.9 %collective-permute-start.25 = (bf16[144,128]{1,0:T(8,128)(2,1)S(1)}, bf16[144,128]{1,0:T(8,128)(2,1)S(1)}, u32[]{:S(2)}, u32[]{:S(2)}) collective-permute-start(bf16[144,128]{1,0:T(8,128)(2,1)S(1)} %get-tuple-element.103.refs_3_), channel_id=1, source_target_pairs={{0,1},{1,0},{2,3},{3,2},{4,5},{5,4},{6,7},{7,6},{8,9},{9,8},{10,11... | collective-permute-start | bytes 110600 | tf_op jit(solution)/shard_map/ppermute | solution.py:97
  69.2 5.8 %collective-permute-start.28 = (bf16[144,128]{1,0:T(8,128)(2,1)S(1)}, bf16[144,128]{1,0:T(8,128)(2,1)S(1)}, u32[]{:S(2)}, u32[]{:S(2)}) collective-permute-start(bf16[144,128]{1,0:T(8,128)(2,1)S(1)} %get-tuple-element.114), channel_id=1, source_target_pairs={{0,12},{4,8},{8,4},{12,0},{1,13},{5,9},{9,5},{13,1},{2,14},{6,10},... | collective-permute-start | bytes 110600 | tf_op jit(solution)/shard_map/ppermute | solution.py:97
  71.3 4.5 %collective-permute-start.29 = (bf16[144,128]{1,0:T(8,128)(2,1)S(1)}, bf16[144,128]{1,0:T(8,128)(2,1)S(1)}, u32[]{:S(2)}, u32[]{:S(2)}) collective-permute-start(bf16[144,128]{1,0:T(8,128)(2,1)S(1)} %get-tuple-element.115), channel_id=1, source_target_pairs={{0,4},{4,0},{8,12},{12,8},{1,5},{5,1},{9,13},{13,9},{2,6},{6,2},{1... | collective-permute-start | bytes 110600 | tf_op jit(solution)/shard_map/ppermute | solution.py:97
  72.0 4.9 %collective-permute-start.30 = (bf16[144,128]{1,0:T(8,128)(2,1)S(1)}, bf16[144,128]{1,0:T(8,128)(2,1)S(1)}, u32[]{:S(2)}, u32[]{:S(2)}) collective-permute-start(bf16[144,128]{1,0:T(8,128)(2,1)S(1)} %get-tuple-element.116), channel_id=1, source_target_pairs={{0,8},{4,12},{8,0},{12,4},{1,9},{5,13},{9,1},{13,5},{2,10},{6,14},... | collective-permute-start | bytes 110600 | tf_op jit(solution)/shard_map/ppermute | solution.py:97
  77.0 4.0 %collective-permute-start.33 = (bf16[176,128]{1,0:T(8,128)(2,1)S(1)}, bf16[176,128]{1,0:T(8,128)(2,1)S(1)}, u32[]{:S(2)}, u32[]{:S(2)}) collective-permute-start(bf16[176,128]{1,0:T(8,128)(2,1)S(1)} %shard_map.136.refs_3_.mine), channel_id=1, source_target_pairs={{0,3},{1,2},{2,1},{3,0},{4,7},{5,6},{6,5},{7,4},{8,11},{9,10},{10,... | collective-permute-start | bytes 135176 | tf_op jit(solution)/shard_map/ppermute | solution.py:97
  77.1 4.6 %collective-permute-start.32 = (bf16[176,128]{1,0:T(8,128)(2,1)S(1)}, bf16[176,128]{1,0:T(8,128)(2,1)S(1)}, u32[]{:S(2)}, u32[]{:S(2)}) collective-permute-start(bf16[176,128]{1,0:T(8,128)(2,1)S(1)} %shard_map.136.refs_3_.mine), channel_id=1, source_target_pairs={{0,2},{1,3},{2,0},{3,1},{4,6},{5,7},{6,4},{7,5},{8,10},{9,11},{10,... | collective-permute-start | bytes 135176 | tf_op jit(solution)/shard_map/ppermute | solution.py:97
  78.5 3.2 %collective-permute-start.31 = (bf16[176,128]{1,0:T(8,128)(2,1)S(1)}, bf16[176,128]{1,0:T(8,128)(2,1)S(1)}, u32[]{:S(2)}, u32[]{:S(2)}) collective-permute-start(bf16[176,128]{1,0:T(8,128)(2,1)S(1)} %shard_map.136.refs_3_.mine), channel_id=1, source_target_pairs={{0,1},{1,0},{2,3},{3,2},{4,5},{5,4},{6,7},{7,6},{8,9},{9,8},{10,11... | collective-permute-start | bytes 135176 | tf_op jit(solution)/shard_map/ppermute | solution.py:97
  81.7 4.2 %collective-permute-start.34 = (bf16[128,128]{1,0:T(8,128)(2,1)S(1)}, bf16[128,128]{1,0:T(8,128)(2,1)S(1)}, u32[]{:S(2)}, u32[]{:S(2)}) collective-permute-start(bf16[128,128]{1,0:T(8,128)(2,1)S(1)} %shard_map.138.refs_0_), channel_id=1, source_target_pairs={{0,4},{4,0},{8,12},{12,8},{1,5},{5,1},{9,13},{13,9},{2,6},{6,2},{1... | collective-permute-start | bytes 98312 | tf_op jit(solution)/shard_map/ppermute | solution.py:97

commit v10 on v9

--- a/solution.py
+++ b/solution.py
@@ -67,8 +67,7 @@
 
     def take_blocks(self, source, base, i):
         first = base + self.first(i)
-        blocks = [source[0, first + f] + source[1, first + f] for f in range(self.frame)]
-        whole = jnp.concatenate(blocks, axis=1)
+        whole = jnp.concatenate([source[first + f] for f in range(self.frame)], axis=1)
         back = lax.rem(self.wide - self.offset(i), jnp.int32(self.wide))
         return self.pack(pltpu.roll(whole, back, 1))
 
@@ -224,8 +223,7 @@
 def multiply_forward(z, c, ids, weights, x, total, own, parts):
     total[...] = jnp.zeros_like(total)
     for s in range(z.slots):
-        product = jnp.dot(x[ids[0, z.slots + s]], weights[s], preferred_element_type=F32)
-        total[s % 2, ids[0, s]] += product
+        total[ids[0, s]] += jnp.dot(x[ids[0, z.slots + s]], weights[s], preferred_element_type=F32)
     for k in range(z.cols):
         both = jnp.concatenate(
             [z.take_blocks(total, 0, c ^ k), z.take_blocks(total, z.post, c ^ k)], axis=0
@@ -342,8 +340,7 @@
     total[...] = jnp.zeros_like(total)
     bring.wait()
     for s in range(z.slots):
-        product = jnp.dot(d[ids[0, s]], weights[s], preferred_element_type=F32)
-        total[s % 2, ids[0, z.slots + s]] += product
+        total[ids[0, z.slots + s]] += jnp.dot(d[ids[0, s]], weights[s], preferred_element_type=F32)
     pieces = [z.take_blocks(total, 0, p ^ k) for k in range(z.rows)]
     for k in range(z.rows):
         other = pieces[k ^ z.half]
@@ -416,19 +413,18 @@
     high_ids = lax.broadcasted_iota(jnp.int32, (highs, BLOCK), 0).astype(F32) + 1.0
     low_ids = lax.broadcasted_iota(jnp.int32, (BLOCK, BLOCK), 1).astype(F32)
     total = jnp.zeros((3 * highs, BLOCK), F32)
-    for ref in extras:
-        everything = ref[...].astype(F32)
-        down = jnp.transpose(everything)
-        for side in range(2 * z.cols):
-            extra = everything[side * CODES : (side + 1) * CODES]
-            for f in range(z.frame):
-                at = 5 * f
-                low = side * CODES + at + 1
-                hit = high_ids == extra[at : at + 1]
-                terms = [jnp.where(hit, extra[at + 2 + i : at + 3 + i], 0.0) for i in range(3)]
-                left = jnp.concatenate(terms, axis=0).astype(BF16)
-                right = (low_ids == down[:, low : low + 1]).astype(BF16)
-                total = total + jnp.dot(left, right, preferred_element_type=F32)
+    everything = extras[...].astype(F32)
+    down = jnp.transpose(everything)
+    for side in range(2 * z.cols):
+        extra = everything[side * CODES : (side + 1) * CODES]
+        for f in range(z.frame):
+            at = 5 * f
+            low = side * CODES + at + 1
+            hit = high_ids == extra[at : at + 1]
+            terms = [jnp.where(hit, extra[at + 2 + i : at + 3 + i], 0.0) for i in range(3)]
+            left = jnp.concatenate(terms, axis=0).astype(BF16)
+            right = (low_ids == down[:, low : low + 1]).astype(BF16)
+            total = total + jnp.dot(left, right, preferred_element_type=F32)
     out[...] = total[0:highs] + total[highs : 2 * highs] + total[2 * highs :]
 
 
@@ -458,9 +454,9 @@
 
 
 def grad_kernel(z, count, per_step, *refs):
-    near_ids, right, later, mine = refs[:4]
-    got = refs[4 : 4 + count]
-    left, out, sums, d0, ids, sem = refs[4 + count :]
+    near_ids, right, later, extras, mine = refs[:5]
+    got = refs[5 : 5 + count]
+    table, out, left, sums, d0, ids, sem = refs[5 + count :]
     n = z.batch
     deep = right.shape[1]
 
@@ -469,6 +465,7 @@
         bring = pltpu.make_async_copy(near_ids, ids, sem)
         bring.start()
         _, c = place()
+        add_table(z, extras, table)
         gather_post(z, c, mine, got, sums, d0)
         lanes = lax.broadcasted_iota(jnp.int32, (BLOCK, deep), 1)
 
@@ -480,7 +477,7 @@
         loop(2 * z.post, lay_left)
         bring.wait()
 
-    paired_products(z, pl.program_id(0) * per_step, per_step, ids, left, right, out)
+    products(z, pl.program_id(0) * per_step, per_step, ids, left, right, out)
 
 
 def products(z, begin, count, ids, left, right, out):
@@ -491,29 +488,9 @@
         out[s] = product.astype(BF16)
 
 
-def paired_products(z, begin, count, ids, left, right, out):
-    for s in range(0, count, 2):
-        a, b = begin + s, begin + s + 1
-        deltas = jnp.concatenate([left[ids[0, a]], left[ids[0, b]]], axis=1)
-        one, two = right[ids[0, z.slots + a]], right[ids[0, z.slots + b]]
-        none = jnp.zeros_like(one)
-        rates = jnp.concatenate(
-            [jnp.concatenate([one, none], axis=1), jnp.concatenate([none, two], axis=1)], axis=0
-        )
-        product = jnp.dot(deltas, rates, preferred_element_type=F32)
-        out[s] = product[:, 0:BLOCK].astype(BF16)
-        out[s + 1] = product[:, BLOCK:].astype(BF16)
-
-
-def rest_kernel(z, count, begin, per_step, near_ids, left, right, grads, *refs):
-    del grads
-    extras = refs[:count]
-    out, table, ids, sem = refs[count:]
-    bring = pltpu.make_async_copy(near_ids, ids, sem)
-    bring.start()
+def finish_kernel(z, own, extras, table):
     add_table(z, extras, table)
-    bring.wait()
-    products(z, begin + pl.program_id(0) * per_step, per_step, ids, left, right, out)
+    table[...] += own[...]
 
 
 def shards(
@@ -566,15 +543,13 @@
         partner_message = flip(message, "row", z.half)
     pre_sums = pltpu.VMEM((z.pre, batch, BLOCK), F32)
     post_sums = pltpu.VMEM((2 * z.post, batch, BLOCK), F32)
-    pre_totals = pltpu.VMEM((2, z.pre, batch, BLOCK), F32)
-    post_totals = pltpu.VMEM((2, 2 * z.post, batch, BLOCK), F32)
     x_shape = shape((z.pre, batch, BLOCK), BF16)
     row_parts = parcel(z.rows, pair, BF16)
     col_parts = [shape(pair), *parcel(z.cols, pair, BF16)]
     x, own, *parts = call(
         functools.partial(first_kernel, z, len(got)),
         [x_shape, *col_parts],
-        [pre_sums, post_totals, *held_ids],
+        [pre_sums, post_sums, *held_ids],
         [ids, turned, message, *got],
         flops=product_flops,
     )
@@ -608,7 +583,7 @@
         rates, act, cur, x, own, *parts = call(
             functools.partial(forward_kernel, z, t, len(got)),
             [shape(every), shape(pair), shape(pair), x_shape, *col_parts],
-            [pre_sums, post_totals, *held_ids],
+            [pre_sums, post_sums, *held_ids],
             [ids, turned, kept, rates, gain, drive, *got],
             flops=product_flops,
         )
@@ -634,7 +609,7 @@
         d, own, *parts = call(
             functools.partial(back_kernel, z, len(got)),
             [shape((2 * z.post, batch, BLOCK), BF16), shape(pair), *row_parts],
-            [post_sums, pre_totals, *held_ids],
+            [post_sums, pre_sums, *held_ids],
             [ids, weights, base, delta, *got],
             flops=product_flops,
         )
@@ -672,36 +647,33 @@
         [],
         [right, delta, *got],
     )
-    all_extras = [extras, flip(extras, "row", 1)] if z.half == 2 else [extras]
-    ins = [ids, right, later, delta, *got]
+    if z.half == 2:
+        their_extras = flip(extras, "row", 1)
+    ins = [ids, right, later, extras, delta, *got]
     cost = pl.CostEstimate(
         flops=2 * slots * deep * BLOCK * BLOCK, bytes_accessed=4 * 1024 * 1024, transcendentals=0
     )
     grads = shape((slots, BLOCK, BLOCK), BF16)
     limit = pltpu.CompilerParams(vmem_limit_bytes=24 * 1024 * 1024)
-    left, weight_grads = pl.pallas_call(
+    table_shape = shape((types // BLOCK, BLOCK))
+    table, weight_grads = pl.pallas_call(
         functools.partial(grad_kernel, z, len(got), per_step),
-        grid=(grid - 1,),
-        out_shape=[left_shape, grads],
+        grid=(grid,),
+        out_shape=[table_shape, grads],
         in_specs=[VMEM] * len(ins),
         out_specs=[VMEM, pl.BlockSpec((per_step, BLOCK, BLOCK), lambda i: (i, 0, 0))],
-        scratch_shapes=[post_sums, pltpu.VMEM((2 * z.post, batch, BLOCK), BF16), *held_ids],
+        scratch_shapes=[
+            pltpu.VMEM(left_shape.shape, BF16),
+            post_sums,
+            pltpu.VMEM((2 * z.post, batch, BLOCK), BF16),
+            *held_ids,
+        ],
         cost_estimate=cost,
         compiler_params=limit,
     )(*ins)
-    ins = [ids, left, right, weight_grads, *all_extras]
-    weight_grads, table = pl.pallas_call(
-        functools.partial(rest_kernel, z, len(all_extras), slots - per_step, per_step),
-        grid=(1,),
-        out_shape=[grads, shape((types // BLOCK, BLOCK))],
-        in_specs=[VMEM] * 3 + [pl.BlockSpec(memory_space=pl.ANY)] + [VMEM] * len(all_extras),
-        out_specs=[pl.BlockSpec((per_step, BLOCK, BLOCK), lambda i: (i + grid - 1, 0, 0)), VMEM],
-        scratch_shapes=held_ids,
-        input_output_aliases={3: 0},
-        cost_estimate=cost,
-        compiler_params=limit,
-    )(*ins)
-    if z.half != 2:
+    if z.half == 2:
+        (table,) = call(functools.partial(finish_kernel, z), [table_shape], [], [table, their_extras])
+    else:
         table = 0.5 * lax.psum(table, "row")
     gain_grads = table.reshape(types)
     return (final_rates, weight_grads.reshape(1, 1, slots, BLOCK, BLOCK), gain_grads)

time: 88.6 us -> 88.1 us (level)
    pallas_call x1 -> x0, Pallas kernels: 2.5 us -> none  [shards(): pl.pallas_call(functools.partial(rest_kernel, z, len(all_extras), slots -...]
    pallas_call x17 -> x18, Pallas kernels: 10.7 us -> 12.1 us  [call(): pl.pallas_call(body, out_shape=outs, in_specs=specs, out_specs=out_specs...]
  transfers between devices with their start and end apart: 35 -> 35, of which waited for: 28 -> 28; matrix products, arithmetic and copies ran while one was open for 0% -> 0% of each run, Pallas kernels for 6% -> 7%
where the time goes in v10:
time: 88.1 us; the launch traced here: 88 us
  starting transfers between devices  38.3 us (43%)
  waiting for transfers between devices  32.1 us (36%)
  Pallas kernels  15.8 us (18%)
    ppermute x35, starting transfers between devices, flip(): return lax.ppermute(x, axis, [(i, i ^ k) for i in range(count)])  38.3 us
    ppermute x35, waiting for transfers between devices, flip(): return lax.ppermute(x, axis, [(i, i ^ k) for i in range(count)])  32.1 us
    pallas_call x18, Pallas kernels, call(): pl.pallas_call(body, out_shape=outs, in_specs=specs, out_specs=out_specs...  12.1 us
    pallas_call x1, Pallas kernels, shards(): pl.pallas_call(functools.partial(grad_kernel, z, len(got), per_step), gri...  3.72 us
  transfers between devices with their start and end apart: 35, of which 28 were waited for; matrix products, arithmetic and copies ran while one was open for 0% of the time, Pallas kernels for 7%

profile of v10, /device:TPU:0, one launch (start us, length us, event | category | flops | bytes accessed | tf_op | source)
XLA Modules:
  0.0 88.0 jit_solution(13418144399629483023)
XLA Ops:
  0.7 0.6 copy-done.6
  1.6 5.1 %collective-permute-start.2 = (bf16[96,128]{1,0:T(8,128)(2,1)S(1)}, bf16[96,128]{1,0:T(8,128)(2,1)S(1)}, u32[]{:S(2)}, u32[]{:S(2)}) collective-permute-start(bf16[96,128]{1,0:T(8,128)(2,1)S(1)} %get-tuple-element.61.after.refs_2_.refs_0_.mine), channel_id=1, source_target_pairs={{0,12},{4,8},{8,4},{12,0},{1,13},{5,9},{9,5},{13,1},{2,14},{6,10},... | collective-permute-start | bytes 73736 | tf_op jit(solution)/shard_map/ppermute | solution.py:96
  6.7 0.6 collective-permute-start
  7.3 1.0 %shard_map.123.refs_1_ = bf16[64,128,128]{2,1,0:T(8,128)(2,1)S(1)} custom-call(bf16[96,128]{1,0:T(8,128)(2,1)S(1)} %get-tuple-element.61.after.refs_2_.refs_0_.mine, bf16[64,128,128]{2,1,0:T(8,128)(2,1)S(1)} %bitcast.5), custom_call_target="tpu_custom_call" | custom-call | bytes 4218880 | tf_op jit(solution)/shard_map/pallas_call | solution.py:78
  8.5 2.0 %collective-permute-done.1.refs_4_.refs_6_ = bf16[96,128]{1,0:T(8,128)(2,1)S(1)} collective-permute-done((bf16[96,128]{1,0:T(8,128)(2,1)S(1)}, bf16[96,128]{1,0:T(8,128)(2,1)S(1)}, u32[]{:S(2)}, u32[]{:S(2)}) %collective-permute-start.1) | collective-permute-done | bytes 24608 | tf_op jit(solution)/shard_map/ppermute | solution.py:96
  10.5 0.9 %collective-permute-done.refs_3_.refs_5_.partner = bf16[96,128]{1,0:T(8,128)(2,1)S(1)} collective-permute-done((bf16[96,128]{1,0:T(8,128)(2,1)S(1)}, bf16[96,128]{1,0:T(8,128)(2,1)S(1)}, u32[]{:S(2)}, u32[]{:S(2)}) %collective-permute-start) | collective-permute-done | bytes 24608 | tf_op jit(solution)/shard_map/ppermute | solution.py:96
  11.4 1.5 %shard_map.124 = (bf16[9,32,128]{2,1,0:T(8,128)(2,1)S(1)}, f32[144,128]{1,0:T(8,128)S(1)}, bf16[144,128]{1,0:T(8,128)(2,1)S(1)}, bf16[144,128]{1,0:T(8,128)(2,1)S(1)}, bf16[144,128]{1,0:T(8,128)(2,1)S(1)}) custom-call(s32[1,128]{1,0:T(1,128)S(1)} %get-tuple-element.60.refs_0_, bf16[64,128,128]{2,1,0:T(8,128)(2,1)S(1)} %shard_map.123.refs_1_, ...), custom_call_target="tpu_custom_call" | custom-call | flops 67108864 | bytes 2454016 | tf_op jit(solution)/shard_map/pallas_call | solution.py:78
  13.0 1.6 %collective-permute-start.4 = (bf16[144,128]{1,0:T(8,128)(2,1)S(1)}, bf16[144,128]{1,0:T(8,128)(2,1)S(1)}, u32[]{:S(2)}, u32[]{:S(2)}) collective-permute-start(bf16[144,128]{1,0:T(8,128)(2,1)S(1)} %get-tuple-element.65), channel_id=1, source_target_pairs={{0,2},{1,3},{2,0},{3,1},{4,6},{5,7},{6,4},{7,5},{8,10},{9,11},{10,... | collective-permute-start | bytes 110600 | tf_op jit(solution)/shard_map/ppermute | solution.py:96
  14.5 0.3 collective-permute-start.5
  14.8 1.9 %collective-permute-done.3.refs_1_ = bf16[144,128]{1,0:T(8,128)(2,1)S(1)} collective-permute-done((bf16[144,128]{1,0:T(8,128)(2,1)S(1)}, bf16[144,128]{1,0:T(8,128)(2,1)S(1)}, u32[]{:S(2)}, u32[]{:S(2)}) %collective-permute-start.3) | collective-permute-done | bytes 36896 | tf_op jit(solution)/shard_map/ppermute | solution.py:96
  16.7 0.4 collective-permute-done.4.refs_2_
  17.2 1.7 %collective-permute-start.8 = (bf16[144,128]{1,0:T(8,128)(2,1)S(1)}, bf16[144,128]{1,0:T(8,128)(2,1)S(1)}, u32[]{:S(2)}, u32[]{:S(2)}) collective-permute-start(bf16[144,128]{1,0:T(8,128)(2,1)S(1)} %get-tuple-element.72), channel_id=1, source_target_pairs={{0,12},{4,8},{8,4},{12,0},{1,13},{5,9},{9,5},{13,1},{2,14},{6,10},... | collective-permute-start | bytes 110600 | tf_op jit(solution)/shard_map/ppermute | solution.py:96
  18.9 0.4 collective-permute-start.7
  19.3 2.3 %collective-permute-start.6 = (bf16[144,128]{1,0:T(8,128)(2,1)S(1)}, bf16[144,128]{1,0:T(8,128)(2,1)S(1)}, u32[]{:S(2)}, u32[]{:S(2)}) collective-permute-start(bf16[144,128]{1,0:T(8,128)(2,1)S(1)} %get-tuple-element.72), channel_id=1, source_target_pairs={{0,8},{4,12},{8,0},{12,4},{1,9},{5,13},{9,1},{13,5},{2,10},{6,14},... | collective-permute-start | bytes 110600 | tf_op jit(solution)/shard_map/ppermute | solution.py:96
  21.6 0.9 %shard_map.126 = (f32[288,128]{1,0:T(8,128)S(1)}, f32[288,128]{1,0:T(8,128)S(1)}, f32[3,288,128]{2,1,0:T(8,128)S(1)}, f32[3,72,128]{2,1,0:T(8,128)S(1)}) custom-call(bf16[96,128]{1,0:T(8,128)(2,1)S(1)} %get-tuple-element.61.after.refs_2_.refs_0_.mine, f32[72,128]{1,0:T(8,128)S(1)} %get-tuple-element.68.refs_1_, f32[3,32,288]{2,1,0:T(8,128)S(1)} %copy-done.1, ...), custom_call_target="tpu_custom_call" | custom-call | bytes 1224704 | tf_op jit(solution)/shard_map/pallas_call | solution.py:78
  22.6 0.8 collective-permute-done.8.refs_8_
  23.6 0.7 collective-permute-done.6.refs_6_
  24.3 1.5 %shard_map.127 = (f32[288,128]{1,0:T(8,128)S(1)}, f32[144,128]{1,0:T(8,128)S(1)}, f32[144,128]{1,0:T(8,128)S(1)}, bf16[9,32,128]{2,1,0:T(8,128)(2,1)S(1)}, f32[1...) custom-call(s32[1,128]{1,0:T(1,128)S(1)} %get-tuple-element.60.refs_, ...), custom_call_target="tpu_custom_call" | custom-call | flops 67108864 | bytes 3572224 | tf_op jit(solution)/shard_map/pallas_call | solution.py:78
  25.8 0.5 collective-permute-start.9
  26.3 1.0 %collective-permute-start.10 = (bf16[144,128]{1,0:T(8,128)(2,1)S(1)}, bf16[144,128]{1,0:T(8,128)(2,1)S(1)}, u32[]{:S(2)}, u32[]{:S(2)}) collective-permute-start(bf16[144,128]{1,0:T(8,128)(2,1)S(1)} %get-tuple-element.76), channel_id=1, source_target_pairs={{0,2},{1,3},{2,0},{3,1},{4,6},{5,7},{6,4},{7,5},{8,10},{9,11},{10,... | collective-permute-start | bytes 110600 | tf_op jit(solution)/shard_map/ppermute | solution.py:96
  27.4 0.4 collective-permute-start.11
  27.7 1.9 %collective-permute-done.9.refs_1_ = bf16[144,128]{1,0:T(8,128)(2,1)S(1)} collective-permute-done((bf16[144,128]{1,0:T(8,128)(2,1)S(1)}, bf16[144,128]{1,0:T(8,128)(2,1)S(1)}, u32[]{:S(2)}, u32[]{:S(2)}) %collective-permute-start.9) | collective-permute-done | bytes 36896 | tf_op jit(solution)/shard_map/ppermute | solution.py:96
  29.6 0.9 %collective-permute-done.10.refs_2_ = bf16[144,128]{1,0:T(8,128)(2,1)S(1)} collective-permute-done((bf16[144,128]{1,0:T(8,128)(2,1)S(1)}, bf16[144,128]{1,0:T(8,128)(2,1)S(1)}, u32[]{:S(2)}, u32[]{:S(2)}) %collective-permute-start.10) | collective-permute-done | bytes 36896 | tf_op jit(solution)/shard_map/ppermute | solution.py:96
  30.6 2.3 %collective-permute-start.14 = (bf16[144,128]{1,0:T(8,128)(2,1)S(1)}, bf16[144,128]{1,0:T(8,128)(2,1)S(1)}, u32[]{:S(2)}, u32[]{:S(2)}) collective-permute-start(bf16[144,128]{1,0:T(8,128)(2,1)S(1)} %get-tuple-element.80), channel_id=1, source_target_pairs={{0,12},{4,8},{8,4},{12,0},{1,13},{5,9},{9,5},{13,1},{2,14},{6,10},... | collective-permute-start | bytes 110600 | tf_op jit(solution)/shard_map/ppermute | solution.py:96
  33.0 2.1 %collective-permute-start.12 = (bf16[144,128]{1,0:T(8,128)(2,1)S(1)}, bf16[144,128]{1,0:T(8,128)(2,1)S(1)}, u32[]{:S(2)}, u32[]{:S(2)}) collective-permute-start(bf16[144,128]{1,0:T(8,128)(2,1)S(1)} %get-tuple-element.80), channel_id=1, source_target_pairs={{0,8},{4,12},{8,0},{12,4},{1,9},{5,13},{9,1},{13,5},{2,10},{6,14},... | collective-permute-start | bytes 110600 | tf_op jit(solution)/shard_map/ppermute | solution.py:96
  35.1 1.4 %collective-permute-done.14.refs_8_ = bf16[144,128]{1,0:T(8,128)(2,1)S(1)} collective-permute-done((bf16[144,128]{1,0:T(8,128)(2,1)S(1)}, bf16[144,128]{1,0:T(8,128)(2,1)S(1)}, u32[]{:S(2)}, u32[]{:S(2)}) %collective-permute-start.14) | collective-permute-done | bytes 36896 | tf_op jit(solution)/shard_map/ppermute | solution.py:96
  36.4 0.8 collective-permute-done.13.refs_7_
  37.2 1.0 %collective-permute-done.12.refs_6_ = bf16[144,128]{1,0:T(8,128)(2,1)S(1)} collective-permute-done((bf16[144,128]{1,0:T(8,128)(2,1)S(1)}, bf16[144,128]{1,0:T(8,128)(2,1)S(1)}, u32[]{:S(2)}, u32[]{:S(2)}) %collective-permute-start.12) | collective-permute-done | bytes 36896 | tf_op jit(solution)/shard_map/ppermute | solution.py:96
  38.2 1.6 %shard_map.129 = (f32[288,128]{1,0:T(8,128)S(1)}, f32[144,128]{1,0:T(8,128)S(1)}, f32[144,128]{1,0:T(8,128)S(1)}, bf16[9,32,128]{2,1,0:T(8,128)(2,1)S(1)}, f32[1...) custom-call(s32[1,128]{1,0:T(1,128)S(1)} %get-tuple-element.60.refs_, ...), custom_call_target="tpu_custom_call" | custom-call | flops 67108864 | bytes 3572224 | tf_op jit(solution)/shard_map/pallas_call | solution.py:78
  39.9 1.3 %collective-permute-start.16 = (bf16[144,128]{1,0:T(8,128)(2,1)S(1)}, bf16[144,128]{1,0:T(8,128)(2,1)S(1)}, u32[]{:S(2)}, u32[]{:S(2)}) collective-permute-start(bf16[144,128]{1,0:T(8,128)(2,1)S(1)} %get-tuple-element.84), channel_id=1, source_target_pairs={{0,2},{1,3},{2,0},{3,1},{4,6},{5,7},{6,4},{7,5},{8,10},{9,11},{10,... | collective-permute-start | bytes 110600 | tf_op jit(solution)/shard_map/ppermute | solution.py:96
  41.2 0.5 collective-permute-start.17
  41.7 1.7 %collective-permute-done.15.refs_1_ = bf16[144,128]{1,0:T(8,128)(2,1)S(1)} collective-permute-done((bf16[144,128]{1,0:T(8,128)(2,1)S(1)}, bf16[144,128]{1,0:T(8,128)(2,1)S(1)}, u32[]{:S(2)}, u32[]{:S(2)}) %collective-permute-start.15) | collective-permute-done | bytes 36896 | tf_op jit(solution)/shard_map/ppermute | solution.py:96
  43.4 0.5 collective-permute-done.16.refs_2_
  44.0 2.1 %collective-permute-start.18 = (bf16[224,128]{1,0:T(8,128)(2,1)S(1)}, bf16[224,128]{1,0:T(8,128)(2,1)S(1)}, u32[]{:S(2)}, u32[]{:S(2)}) collective-permute-start(bf16[224,128]{1,0:T(8,128)(2,1)S(1)} %get-tuple-element.88), channel_id=1, source_target_pairs={{0,8},{4,12},{8,0},{12,4},{1,9},{5,13},{9,1},{13,5},{2,10},{6,14},... | collective-permute-start | bytes 172040 | tf_op jit(solution)/shard_map/ppermute | solution.py:96
  46.1 4.3 %collective-permute-done.18.theirs = bf16[224,128]{1,0:T(8,128)(2,1)S(1)} collective-permute-done((bf16[224,128]{1,0:T(8,128)(2,1)S(1)}, bf16[224,128]{1,0:T(8,128)(2,1)S(1)}, u32[]{:S(2)}, u32[]{:S(2)}) %collective-permute-start.18) | collective-permute-done | bytes 57376 | tf_op jit(solution)/shard_map/ppermute | solution.py:96
  50.5 1.5 %collective-permute-start.20 = (bf16[144,128]{1,0:T(8,128)(2,1)S(1)}, bf16[144,128]{1,0:T(8,128)(2,1)S(1)}, u32[]{:S(2)}, u32[]{:S(2)}) collective-permute-start(bf16[144,128]{1,0:T(8,128)(2,1)S(1)} %get-tuple-element.91.refs_3_), channel_id=1, source_target_pairs={{0,2},{1,3},{2,0},{3,1},{4,6},{5,7},{6,4},{7,5},{8,10},{9,11},{10,... | collective-permute-start | bytes 110600 | tf_op jit(solution)/shard_map/ppermute | solution.py:96
  52.0 0.3 collective-permute-start.19
  52.3 1.9 %collective-permute-done.21.refs_6_ = bf16[144,128]{1,0:T(8,128)(2,1)S(1)} collective-permute-done((bf16[144,128]{1,0:T(8,128)(2,1)S(1)}, bf16[144,128]{1,0:T(8,128)(2,1)S(1)}, u32[]{:S(2)}, u32[]{:S(2)}) %collective-permute-start.21) | collective-permute-done | bytes 36896 | tf_op jit(solution)/shard_map/ppermute | solution.py:96
  54.2 0.4 collective-permute-done.20.refs_5_
  54.6 1.5 %shard_map.132 = (bf16[18,32,128]{2,1,0:T(8,128)(2,1)S(1)}, f32[144,128]{1,0:T(8,128)S(1)}, bf16[144,128]{1,0:T(8,128)(2,1)S(1)}, bf16[144,128]{1,0:T(8,128)(2,1)S(1)}, bf16[144,128]{1,0:T(8,128)(2,1)S(1)}) custom-call(s32[1,128]{1,0:T(1,128)S(1)} %get-tuple-element.60.refs_0_, bf16[64,128,128]{2,1,0:T(8,128)(2,1)S(1)} %bitcast.6, ...), custom_call_target="tpu_custom_call" | custom-call | flops 67108864 | bytes 2613760 | tf_op jit(solution)/shard_map/pallas_call | solution.py:78
  56.2 1.9 %collective-permute-start.22 = (bf16[144,128]{1,0:T(8,128)(2,1)S(1)}, bf16[144,128]{1,0:T(8,128)(2,1)S(1)}, u32[]{:S(2)}, u32[]{:S(2)}) collective-permute-start(bf16[144,128]{1,0:T(8,128)(2,1)S(1)} %get-tuple-element.97), channel_id=1, source_target_pairs={{0,12},{4,8},{8,4},{12,0},{1,13},{5,9},{9,5},{13,1},{2,14},{6,10},... | collective-permute-start | bytes 110600 | tf_op jit(solution)/shard_map/ppermute | solution.py:96
  58.1 2.5 %collective-permute-start.24 = (bf16[144,128]{1,0:T(8,128)(2,1)S(1)}, bf16[144,128]{1,0:T(8,128)(2,1)S(1)}, u32[]{:S(2)}, u32[]{:S(2)}) collective-permute-start(bf16[144,128]{1,0:T(8,128)(2,1)S(1)} %get-tuple-element.99), channel_id=1, source_target_pairs={{0,8},{4,12},{8,0},{12,4},{1,9},{5,13},{9,1},{13,5},{2,10},{6,14},... | collective-permute-start | bytes 110600 | tf_op jit(solution)/shard_map/ppermute | solution.py:96
  60.6 1.5 %collective-permute-done.22.refs_0_ = bf16[144,128]{1,0:T(8,128)(2,1)S(1)} collective-permute-done((bf16[144,128]{1,0:T(8,128)(2,1)S(1)}, bf16[144,128]{1,0:T(8,128)(2,1)S(1)}, u32[]{:S(2)}, u32[]{:S(2)}) %collective-permute-start.22) | collective-permute-done | bytes 36896 | tf_op jit(solution)/shard_map/ppermute | solution.py:96
  62.1 0.6 collective-permute-done.23.refs_1_
  62.8 0.6 collective-permute-done.24.refs_2_
  63.5 1.3 %collective-permute-start.26 = (bf16[144,128]{1,0:T(8,128)(2,1)S(1)}, bf16[144,128]{1,0:T(8,128)(2,1)S(1)}, u32[]{:S(2)}, u32[]{:S(2)}) collective-permute-start(bf16[144,128]{1,0:T(8,128)(2,1)S(1)} %get-tuple-element.101.refs_3_), channel_id=1, source_target_pairs={{0,2},{1,3},{2,0},{3,1},{4,6},{5,7},{6,4},{7,5},{8,10},{9,11},{10,... | collective-permute-start | bytes 110600 | tf_op jit(solution)/shard_map/ppermute | solution.py:96
  64.7 0.6 collective-permute-start.25
  65.3 1.7 %collective-permute-done.27.refs_6_ = bf16[144,128]{1,0:T(8,128)(2,1)S(1)} collective-permute-done((bf16[144,128]{1,0:T(8,128)(2,1)S(1)}, bf16[144,128]{1,0:T(8,128)(2,1)S(1)}, u32[]{:S(2)}, u32[]{:S(2)}) %collective-permute-start.27) | collective-permute-done | bytes 36896 | tf_op jit(solution)/shard_map/ppermute | solution.py:96
  67.0 0.6 collective-permute-done.26.refs_5_
  67.6 1.5 %shard_map.134 = (bf16[18,32,128]{2,1,0:T(8,128)(2,1)S(1)}, f32[144,128]{1,0:T(8,128)S(1)}, bf16[144,128]{1,0:T(8,128)(2,1)S(1)}, bf16[144,128]{1,0:T(8,128)(2,1)S(1)}, bf16[144,128]{1,0:T(8,128)(2,1)S(1)}) custom-call(s32[1,128]{1,0:T(1,128)S(1)} %get-tuple-element.60.refs_0_, bf16[64,128,128]{2,1,0:T(8,128)(2,1)S(1)} %bitcast.7, ...), custom_call_target="tpu_custom_call" | custom-call | flops 67108864 | bytes 2613760 | tf_op jit(solution)/shard_map/pallas_call | solution.py:78
  69.2 1.9 %collective-permute-start.28 = (bf16[144,128]{1,0:T(8,128)(2,1)S(1)}, bf16[144,128]{1,0:T(8,128)(2,1)S(1)}, u32[]{:S(2)}, u32[]{:S(2)}) collective-permute-start(bf16[144,128]{1,0:T(8,128)(2,1)S(1)} %get-tuple-element.112), channel_id=1, source_target_pairs={{0,12},{4,8},{8,4},{12,0},{1,13},{5,9},{9,5},{13,1},{2,14},{6,10},... | collective-permute-start | bytes 110600 | tf_op jit(solution)/shard_map/ppermute | solution.py:96
  71.1 0.8 collective-permute-start.29
  71.9 1.7 %collective-permute-start.30 = (bf16[144,128]{1,0:T(8,128)(2,1)S(1)}, bf16[144,128]{1,0:T(8,128)(2,1)S(1)}, u32[]{:S(2)}, u32[]{:S(2)}) collective-permute-start(bf16[144,128]{1,0:T(8,128)(2,1)S(1)} %get-tuple-element.114), channel_id=1, source_target_pairs={{0,8},{4,12},{8,0},{12,4},{1,9},{5,13},{9,1},{13,5},{2,10},{6,14},... | collective-permute-start | bytes 110600 | tf_op jit(solution)/shard_map/ppermute | solution.py:96
  73.6 1.4 %collective-permute-done.28.refs_0_ = bf16[144,128]{1,0:T(8,128)(2,1)S(1)} collective-permute-done((bf16[144,128]{1,0:T(8,128)(2,1)S(1)}, bf16[144,128]{1,0:T(8,128)(2,1)S(1)}, u32[]{:S(2)}, u32[]{:S(2)}) %collective-permute-start.28) | collective-permute-done | bytes 36896 | tf_op jit(solution)/shard_map/ppermute | solution.py:96
  75.0 0.8 collective-permute-done.29.refs_1_
  75.8 1.0 %collective-permute-done.30.refs_2_ = bf16[144,128]{1,0:T(8,128)(2,1)S(1)} collective-permute-done((bf16[144,128]{1,0:T(8,128)(2,1)S(1)}, bf16[144,128]{1,0:T(8,128)(2,1)S(1)}, u32[]{:S(2)}, u32[]{:S(2)}) %collective-permute-start.30) | collective-permute-done | bytes 36896 | tf_op jit(solution)/shard_map/ppermute | solution.py:96
  77.0 1.5 %collective-permute-start.32 = (bf16[176,128]{1,0:T(8,128)(2,1)S(1)}, bf16[176,128]{1,0:T(8,128)(2,1)S(1)}, u32[]{:S(2)}, u32[]{:S(2)}) collective-permute-start(bf16[176,128]{1,0:T(8,128)(2,1)S(1)} %shard_map.136.mine.refs_4_), channel_id=1, source_target_pairs={{0,2},{1,3},{2,0},{3,1},{4,6},{5,7},{6,4},{7,5},{8,10},{9,11},{10,... | collective-permute-start | bytes 135176 | tf_op jit(solution)/shard_map/ppermute | solution.py:96
  78.5 0.3 collective-permute-start.31
  78.8 0.8 shard_map.135
  79.6 1.3 %collective-permute-done.33.refs_2_.refs_7_ = bf16[176,128]{1,0:T(8,128)(2,1)S(1)} collective-permute-done((bf16[176,128]{1,0:T(8,128)(2,1)S(1)}, bf16[176,128]{1,0:T(8,128)(2,1)S(1)}, u32[]{:S(2)}, u32[]{:S(2)}) %collective-permute-start.33) | collective-permute-done | bytes 45088 | tf_op jit(solution)/shard_map/ppermute | solution.py:96
  80.9 0.7 collective-permute-done.32.refs_1_.refs_6_
  81.6 1.2 %collective-permute-start.34 = (bf16[128,128]{1,0:T(8,128)(2,1)S(1)}, bf16[128,128]{1,0:T(8,128)(2,1)S(1)}, u32[]{:S(2)}, u32[]{:S(2)}) collective-permute-start(bf16[128,128]{1,0:T(8,128)(2,1)S(1)} %shard_map.137.refs_3_), channel_id=1, source_target_pairs={{0,4},{4,0},{8,12},{12,8},{1,5},{5,1},{9,13},{13,9},{2,6},{6,2},{1... | collective-permute-start | bytes 98312 | tf_op jit(solution)/shard_map/ppermute | solution.py:96
  82.9 3.7 %shard_map.138 = (f32[64,128]{1,0:T(8,128)S(1)}, bf16[64,128,128]{2,1,0:T(8,128)(2,1)}) custom-call(s32[1,128]{1,0:T(1,128)S(1)} %get-tuple-element.60.refs_0_, bf16[9,128,128]{2,1,0:T(8,128)(2,1)S(1)} %get-tuple-element.106.right.refs_1_, bf16[18,128,128]{2,1,0:T(8,128)(2,1)S(1)} %get-tuple-element.107.refs_2_, bf16[128,128]{1,0:T(8,128)(2,1)S(1)} %shard_map.137.refs_3_, ...), custom_call_target="tpu_custom_call" | custom-call | flops 268435456 | bytes 4194304 | tf_op jit(solution)/shard_map/pallas_call | solution.py:659
  86.6 1.4 %shard_map.139 = f32[64,128]{1,0:T(8,128)} custom-call(f32[64,128]{1,0:T(8,128)S(1)} %get-tuple-element.116.own, bf16[128,128]{1,0:T(8,128)(2,1)S(1)} %collective-permute-done.34.extras), custom_call_target="tpu_custom_call" | custom-call | bytes 98304 | tf_op jit(solution)/shard_map/pallas_call | solution.py:78
  (45 shorter events, 1.4 us)
Async XLA Ops:
  0.6 0.7 copy-start.6
  0.6 0.7 copy-start.5
  0.7 0.7 copy-start.9
  0.7 0.7 copy-start.8
  0.7 0.7 copy-start.7
  0.7 0.8 copy-start.3
  0.7 6.6 %copy-start = (bf16[1,1,64,128,128]{4,3,2,1,0:T(8,128)(2,1)S(1)}, bf16[1,1,64,128,128]{4,3,2,1,0:T(8,128)(2,1)}, u32[]{:S(2)}) copy-start(bf16[1,1,64,128,128]{4,3,2,1,0:T(8,128)(2,1)} %param.13) | copy-start | bytes 6291460
  1.6 6.9 %collective-permute-start.2 = (bf16[96,128]{1,0:T(8,128)(2,1)S(1)}, bf16[96,128]{1,0:T(8,128)(2,1)S(1)}, u32[]{:S(2)}, u32[]{:S(2)}) collective-permute-start(bf16[96,128]{1,0:T(8,128)(2,1)S(1)} %get-tuple-element.61.after.refs_2_.refs_0_.mine), channel_id=1, source_target_pairs={{0,12},{4,8},{8,4},{12,0},{1,13},{5,9},{9,5},{13,1},{2,14},{6,10},... | collective-permute-start | bytes 73736 | tf_op jit(solution)/shard_map/ppermute | solution.py:96
  6.6 3.8 %collective-permute-start.1 = (bf16[96,128]{1,0:T(8,128)(2,1)S(1)}, bf16[96,128]{1,0:T(8,128)(2,1)S(1)}, u32[]{:S(2)}, u32[]{:S(2)}) collective-permute-start(bf16[96,128]{1,0:T(8,128)(2,1)S(1)} %get-tuple-element.61.after.refs_2_.refs_0_.mine), channel_id=1, source_target_pairs={{0,4},{4,0},{8,12},{12,8},{1,5},{5,1},{9,13},{13,9},{2,6},{6,2},{1... | collective-permute-start | bytes 73736 | tf_op jit(solution)/shard_map/ppermute | solution.py:96
  6.7 4.8 %collective-permute-start = (bf16[96,128]{1,0:T(8,128)(2,1)S(1)}, bf16[96,128]{1,0:T(8,128)(2,1)S(1)}, u32[]{:S(2)}, u32[]{:S(2)}) collective-permute-start(bf16[96,128]{1,0:T(8,128)(2,1)S(1)} %get-tuple-element.61.after.refs_2_.refs_0_.mine), channel_id=1, source_target_pairs={{0,8},{4,12},{8,0},{12,4},{1,9},{5,13},{9,1},{13,5},{2,10},{6,14},... | collective-permute-start | bytes 73736 | tf_op jit(solution)/shard_map/ppermute | solution.py:96
  8.3 13.3 %copy-start.1 = (f32[3,32,288]{2,1,0:T(8,128)S(1)}, f32[3,32,288]{2,1,0:T(8,128)}, u32[]{:S(2)}) copy-start(f32[3,32,288]{2,1,0:T(8,128)} %refs_2_.1) | copy-start | bytes 331780
  8.3 13.3 %copy-start.2 = (bf16[3,32,512]{2,1,0:T(8,128)(2,1)S(1)}, bf16[3,32,512]{2,1,0:T(8,128)(2,1)}, u32[]{:S(2)}) copy-start(bf16[3,32,512]{2,1,0:T(8,128)(2,1)} %param.11) | copy-start | bytes 294916
  8.3 13.3 %copy-start.4 = (f32[8192]{0:T(1024)S(1)}, f32[8192]{0:T(1024)}, u32[]{:S(2)}) copy-start(f32[8192]{0:T(1024)} %param.18) | copy-start | bytes 98308
  12.9 3.8 %collective-permute-start.3 = (bf16[144,128]{1,0:T(8,128)(2,1)S(1)}, bf16[144,128]{1,0:T(8,128)(2,1)S(1)}, u32[]{:S(2)}, u32[]{:S(2)}) collective-permute-start(bf16[144,128]{1,0:T(8,128)(2,1)S(1)} %get-tuple-element.64), channel_id=1, source_target_pairs={{0,3},{1,2},{2,1},{3,0},{4,7},{5,6},{6,5},{7,4},{8,11},{9,10},{10,... | collective-permute-start | bytes 110600 | tf_op jit(solution)/shard_map/ppermute | solution.py:96
  13.0 4.2 %collective-permute-start.4 = (bf16[144,128]{1,0:T(8,128)(2,1)S(1)}, bf16[144,128]{1,0:T(8,128)(2,1)S(1)}, u32[]{:S(2)}, u32[]{:S(2)}) collective-permute-start(bf16[144,128]{1,0:T(8,128)(2,1)S(1)} %get-tuple-element.65), channel_id=1, source_target_pairs={{0,2},{1,3},{2,0},{3,1},{4,6},{5,7},{6,4},{7,5},{8,10},{9,11},{10,... | collective-permute-start | bytes 110600 | tf_op jit(solution)/shard_map/ppermute | solution.py:96
  14.5 2.6 %collective-permute-start.5 = (bf16[144,128]{1,0:T(8,128)(2,1)S(1)}, bf16[144,128]{1,0:T(8,128)(2,1)S(1)}, u32[]{:S(2)}, u32[]{:S(2)}) collective-permute-start(bf16[144,128]{1,0:T(8,128)(2,1)S(1)} %get-tuple-element.66), channel_id=1, source_target_pairs={{0,1},{1,0},{2,3},{3,2},{4,5},{5,4},{6,7},{7,6},{8,9},{9,8},{10,11... | collective-permute-start | bytes 110600 | tf_op jit(solution)/shard_map/ppermute | solution.py:96
  17.2 6.2 %collective-permute-start.8 = (bf16[144,128]{1,0:T(8,128)(2,1)S(1)}, bf16[144,128]{1,0:T(8,128)(2,1)S(1)}, u32[]{:S(2)}, u32[]{:S(2)}) collective-permute-start(bf16[144,128]{1,0:T(8,128)(2,1)S(1)} %get-tuple-element.72), channel_id=1, source_target_pairs={{0,12},{4,8},{8,4},{12,0},{1,13},{5,9},{9,5},{13,1},{2,14},{6,10},... | collective-permute-start | bytes 110600 | tf_op jit(solution)/shard_map/ppermute | solution.py:96
  18.9 4.7 %collective-permute-start.7 = (bf16[144,128]{1,0:T(8,128)(2,1)S(1)}, bf16[144,128]{1,0:T(8,128)(2,1)S(1)}, u32[]{:S(2)}, u32[]{:S(2)}) collective-permute-start(bf16[144,128]{1,0:T(8,128)(2,1)S(1)} %get-tuple-element.72), channel_id=1, source_target_pairs={{0,4},{4,0},{8,12},{12,8},{1,5},{5,1},{9,13},{13,9},{2,6},{6,2},{1... | collective-permute-start | bytes 110600 | tf_op jit(solution)/shard_map/ppermute | solution.py:96
  19.3 5.0 %collective-permute-start.6 = (bf16[144,128]{1,0:T(8,128)(2,1)S(1)}, bf16[144,128]{1,0:T(8,128)(2,1)S(1)}, u32[]{:S(2)}, u32[]{:S(2)}) collective-permute-start(bf16[144,128]{1,0:T(8,128)(2,1)S(1)} %get-tuple-element.72), channel_id=1, source_target_pairs={{0,8},{4,12},{8,0},{12,4},{1,9},{5,13},{9,1},{13,5},{2,10},{6,14},... | collective-permute-start | bytes 110600 | tf_op jit(solution)/shard_map/ppermute | solution.py:96
  25.8 3.8 %collective-permute-start.9 = (bf16[144,128]{1,0:T(8,128)(2,1)S(1)}, bf16[144,128]{1,0:T(8,128)(2,1)S(1)}, u32[]{:S(2)}, u32[]{:S(2)}) collective-permute-start(bf16[144,128]{1,0:T(8,128)(2,1)S(1)} %get-tuple-element.75), channel_id=1, source_target_pairs={{0,3},{1,2},{2,1},{3,0},{4,7},{5,6},{6,5},{7,4},{8,11},{9,10},{10,... | collective-permute-start | bytes 110600 | tf_op jit(solution)/shard_map/ppermute | solution.py:96
  26.3 4.2 %collective-permute-start.10 = (bf16[144,128]{1,0:T(8,128)(2,1)S(1)}, bf16[144,128]{1,0:T(8,128)(2,1)S(1)}, u32[]{:S(2)}, u32[]{:S(2)}) collective-permute-start(bf16[144,128]{1,0:T(8,128)(2,1)S(1)} %get-tuple-element.76), channel_id=1, source_target_pairs={{0,2},{1,3},{2,0},{3,1},{4,6},{5,7},{6,4},{7,5},{8,10},{9,11},{10,... | collective-permute-start | bytes 110600 | tf_op jit(solution)/shard_map/ppermute | solution.py:96
  27.4 3.2 %collective-permute-start.11 = (bf16[144,128]{1,0:T(8,128)(2,1)S(1)}, bf16[144,128]{1,0:T(8,128)(2,1)S(1)}, u32[]{:S(2)}, u32[]{:S(2)}) collective-permute-start(bf16[144,128]{1,0:T(8,128)(2,1)S(1)} %get-tuple-element.77), channel_id=1, source_target_pairs={{0,1},{1,0},{2,3},{3,2},{4,5},{5,4},{6,7},{7,6},{8,9},{9,8},{10,11... | collective-permute-start | bytes 110600 | tf_op jit(solution)/shard_map/ppermute | solution.py:96
  30.6 5.8 %collective-permute-start.14 = (bf16[144,128]{1,0:T(8,128)(2,1)S(1)}, bf16[144,128]{1,0:T(8,128)(2,1)S(1)}, u32[]{:S(2)}, u32[]{:S(2)}) collective-permute-start(bf16[144,128]{1,0:T(8,128)(2,1)S(1)} %get-tuple-element.80), channel_id=1, source_target_pairs={{0,12},{4,8},{8,4},{12,0},{1,13},{5,9},{9,5},{13,1},{2,14},{6,10},... | collective-permute-start | bytes 110600 | tf_op jit(solution)/shard_map/ppermute | solution.py:96
  32.9 4.3 %collective-permute-start.13 = (bf16[144,128]{1,0:T(8,128)(2,1)S(1)}, bf16[144,128]{1,0:T(8,128)(2,1)S(1)}, u32[]{:S(2)}, u32[]{:S(2)}) collective-permute-start(bf16[144,128]{1,0:T(8,128)(2,1)S(1)} %get-tuple-element.80), channel_id=1, source_target_pairs={{0,4},{4,0},{8,12},{12,8},{1,5},{5,1},{9,13},{13,9},{2,6},{6,2},{1... | collective-permute-start | bytes 110600 | tf_op jit(solution)/shard_map/ppermute | solution.py:96
  33.0 5.3 %collective-permute-start.12 = (bf16[144,128]{1,0:T(8,128)(2,1)S(1)}, bf16[144,128]{1,0:T(8,128)(2,1)S(1)}, u32[]{:S(2)}, u32[]{:S(2)}) collective-permute-start(bf16[144,128]{1,0:T(8,128)(2,1)S(1)} %get-tuple-element.80), channel_id=1, source_target_pairs={{0,8},{4,12},{8,0},{12,4},{1,9},{5,13},{9,1},{13,5},{2,10},{6,14},... | collective-permute-start | bytes 110600 | tf_op jit(solution)/shard_map/ppermute | solution.py:96
  39.8 3.7 %collective-permute-start.15 = (bf16[144,128]{1,0:T(8,128)(2,1)S(1)}, bf16[144,128]{1,0:T(8,128)(2,1)S(1)}, u32[]{:S(2)}, u32[]{:S(2)}) collective-permute-start(bf16[144,128]{1,0:T(8,128)(2,1)S(1)} %get-tuple-element.83), channel_id=1, source_target_pairs={{0,3},{1,2},{2,1},{3,0},{4,7},{5,6},{6,5},{7,4},{8,11},{9,10},{10,... | collective-permute-start | bytes 110600 | tf_op jit(solution)/shard_map/ppermute | solution.py:96
  39.9 4.1 %collective-permute-start.16 = (bf16[144,128]{1,0:T(8,128)(2,1)S(1)}, bf16[144,128]{1,0:T(8,128)(2,1)S(1)}, u32[]{:S(2)}, u32[]{:S(2)}) collective-permute-start(bf16[144,128]{1,0:T(8,128)(2,1)S(1)} %get-tuple-element.84), channel_id=1, source_target_pairs={{0,2},{1,3},{2,0},{3,1},{4,6},{5,7},{6,4},{7,5},{8,10},{9,11},{10,... | collective-permute-start | bytes 110600 | tf_op jit(solution)/shard_map/ppermute | solution.py:96
  41.2 2.7 %collective-permute-start.17 = (bf16[144,128]{1,0:T(8,128)(2,1)S(1)}, bf16[144,128]{1,0:T(8,128)(2,1)S(1)}, u32[]{:S(2)}, u32[]{:S(2)}) collective-permute-start(bf16[144,128]{1,0:T(8,128)(2,1)S(1)} %get-tuple-element.85), channel_id=1, source_target_pairs={{0,1},{1,0},{2,3},{3,2},{4,5},{5,4},{6,7},{7,6},{8,9},{9,8},{10,11... | collective-permute-start | bytes 110600 | tf_op jit(solution)/shard_map/ppermute | solution.py:96
  44.0 6.4 %collective-permute-start.18 = (bf16[224,128]{1,0:T(8,128)(2,1)S(1)}, bf16[224,128]{1,0:T(8,128)(2,1)S(1)}, u32[]{:S(2)}, u32[]{:S(2)}) collective-permute-start(bf16[224,128]{1,0:T(8,128)(2,1)S(1)} %get-tuple-element.88), channel_id=1, source_target_pairs={{0,8},{4,12},{8,0},{12,4},{1,9},{5,13},{9,1},{13,5},{2,10},{6,14},... | collective-permute-start | bytes 172040 | tf_op jit(solution)/shard_map/ppermute | solution.py:96
  50.4 3.8 %collective-permute-start.21 = (bf16[144,128]{1,0:T(8,128)(2,1)S(1)}, bf16[144,128]{1,0:T(8,128)(2,1)S(1)}, u32[]{:S(2)}, u32[]{:S(2)}) collective-permute-start(bf16[144,128]{1,0:T(8,128)(2,1)S(1)} %get-tuple-element.91.refs_3_), channel_id=1, source_target_pairs={{0,3},{1,2},{2,1},{3,0},{4,7},{5,6},{6,5},{7,4},{8,11},{9,10},{10,... | collective-permute-start | bytes 110600 | tf_op jit(solution)/shard_map/ppermute | solution.py:96
  50.5 4.2 %collective-permute-start.20 = (bf16[144,128]{1,0:T(8,128)(2,1)S(1)}, bf16[144,128]{1,0:T(8,128)(2,1)S(1)}, u32[]{:S(2)}, u32[]{:S(2)}) collective-permute-start(bf16[144,128]{1,0:T(8,128)(2,1)S(1)} %get-tuple-element.91.refs_3_), channel_id=1, source_target_pairs={{0,2},{1,3},{2,0},{3,1},{4,6},{5,7},{6,4},{7,5},{8,10},{9,11},{10,... | collective-permute-start | bytes 110600 | tf_op jit(solution)/shard_map/ppermute | solution.py:96
  52.0 2.7 %collective-permute-start.19 = (bf16[144,128]{1,0:T(8,128)(2,1)S(1)}, bf16[144,128]{1,0:T(8,128)(2,1)S(1)}, u32[]{:S(2)}, u32[]{:S(2)}) collective-permute-start(bf16[144,128]{1,0:T(8,128)(2,1)S(1)} %get-tuple-element.91.refs_3_), channel_id=1, source_target_pairs={{0,1},{1,0},{2,3},{3,2},{4,5},{5,4},{6,7},{7,6},{8,9},{9,8},{10,11... | collective-permute-start | bytes 110600 | tf_op jit(solution)/shard_map/ppermute | solution.py:96
  56.2 6.0 %collective-permute-start.22 = (bf16[144,128]{1,0:T(8,128)(2,1)S(1)}, bf16[144,128]{1,0:T(8,128)(2,1)S(1)}, u32[]{:S(2)}, u32[]{:S(2)}) collective-permute-start(bf16[144,128]{1,0:T(8,128)(2,1)S(1)} %get-tuple-element.97), channel_id=1, source_target_pairs={{0,12},{4,8},{8,4},{12,0},{1,13},{5,9},{9,5},{13,1},{2,14},{6,10},... | collective-permute-start | bytes 110600 | tf_op jit(solution)/shard_map/ppermute | solution.py:96
  58.1 4.7 %collective-permute-start.23 = (bf16[144,128]{1,0:T(8,128)(2,1)S(1)}, bf16[144,128]{1,0:T(8,128)(2,1)S(1)}, u32[]{:S(2)}, u32[]{:S(2)}) collective-permute-start(bf16[144,128]{1,0:T(8,128)(2,1)S(1)} %get-tuple-element.98), channel_id=1, source_target_pairs={{0,4},{4,0},{8,12},{12,8},{1,5},{5,1},{9,13},{13,9},{2,6},{6,2},{1... | collective-permute-start | bytes 110600 | tf_op jit(solution)/shard_map/ppermute | solution.py:96
  58.1 5.3 %collective-permute-start.24 = (bf16[144,128]{1,0:T(8,128)(2,1)S(1)}, bf16[144,128]{1,0:T(8,128)(2,1)S(1)}, u32[]{:S(2)}, u32[]{:S(2)}) collective-permute-start(bf16[144,128]{1,0:T(8,128)(2,1)S(1)} %get-tuple-element.99), channel_id=1, source_target_pairs={{0,8},{4,12},{8,0},{12,4},{1,9},{5,13},{9,1},{13,5},{2,10},{6,14},... | collective-permute-start | bytes 110600 | tf_op jit(solution)/shard_map/ppermute | solution.py:96
  63.4 3.6 %collective-permute-start.27 = (bf16[144,128]{1,0:T(8,128)(2,1)S(1)}, bf16[144,128]{1,0:T(8,128)(2,1)S(1)}, u32[]{:S(2)}, u32[]{:S(2)}) collective-permute-start(bf16[144,128]{1,0:T(8,128)(2,1)S(1)} %get-tuple-element.101.refs_3_), channel_id=1, source_target_pairs={{0,3},{1,2},{2,1},{3,0},{4,7},{5,6},{6,5},{7,4},{8,11},{9,10},{10,... | collective-permute-start | bytes 110600 | tf_op jit(solution)/shard_map/ppermute | solution.py:96
  63.5 4.2 %collective-permute-start.26 = (bf16[144,128]{1,0:T(8,128)(2,1)S(1)}, bf16[144,128]{1,0:T(8,128)(2,1)S(1)}, u32[]{:S(2)}, u32[]{:S(2)}) collective-permute-start(bf16[144,128]{1,0:T(8,128)(2,1)S(1)} %get-tuple-element.101.refs_3_), channel_id=1, source_target_pairs={{0,2},{1,3},{2,0},{3,1},{4,6},{5,7},{6,4},{7,5},{8,10},{9,11},{10,... | collective-permute-start | bytes 110600 | tf_op jit(solution)/shard_map/ppermute | solution.py:96
  64.7 2.9 %collective-permute-start.25 = (bf16[144,128]{1,0:T(8,128)(2,1)S(1)}, bf16[144,128]{1,0:T(8,128)(2,1)S(1)}, u32[]{:S(2)}, u32[]{:S(2)}) collective-permute-start(bf16[144,128]{1,0:T(8,128)(2,1)S(1)} %get-tuple-element.101.refs_3_), channel_id=1, source_target_pairs={{0,1},{1,0},{2,3},{3,2},{4,5},{5,4},{6,7},{7,6},{8,9},{9,8},{10,11... | collective-permute-start | bytes 110600 | tf_op jit(solution)/shard_map/ppermute | solution.py:96
  69.2 5.9 %collective-permute-start.28 = (bf16[144,128]{1,0:T(8,128)(2,1)S(1)}, bf16[144,128]{1,0:T(8,128)(2,1)S(1)}, u32[]{:S(2)}, u32[]{:S(2)}) collective-permute-start(bf16[144,128]{1,0:T(8,128)(2,1)S(1)} %get-tuple-element.112), channel_id=1, source_target_pairs={{0,12},{4,8},{8,4},{12,0},{1,13},{5,9},{9,5},{13,1},{2,14},{6,10},... | collective-permute-start | bytes 110600 | tf_op jit(solution)/shard_map/ppermute | solution.py:96
  71.1 4.7 %collective-permute-start.29 = (bf16[144,128]{1,0:T(8,128)(2,1)S(1)}, bf16[144,128]{1,0:T(8,128)(2,1)S(1)}, u32[]{:S(2)}, u32[]{:S(2)}) collective-permute-start(bf16[144,128]{1,0:T(8,128)(2,1)S(1)} %get-tuple-element.113), channel_id=1, source_target_pairs={{0,4},{4,0},{8,12},{12,8},{1,5},{5,1},{9,13},{13,9},{2,6},{6,2},{1... | collective-permute-start | bytes 110600 | tf_op jit(solution)/shard_map/ppermute | solution.py:96
  71.9 4.9 %collective-permute-start.30 = (bf16[144,128]{1,0:T(8,128)(2,1)S(1)}, bf16[144,128]{1,0:T(8,128)(2,1)S(1)}, u32[]{:S(2)}, u32[]{:S(2)}) collective-permute-start(bf16[144,128]{1,0:T(8,128)(2,1)S(1)} %get-tuple-element.114), channel_id=1, source_target_pairs={{0,8},{4,12},{8,0},{12,4},{1,9},{5,13},{9,1},{13,5},{2,10},{6,14},... | collective-permute-start | bytes 110600 | tf_op jit(solution)/shard_map/ppermute | solution.py:96
  76.9 4.0 %collective-permute-start.33 = (bf16[176,128]{1,0:T(8,128)(2,1)S(1)}, bf16[176,128]{1,0:T(8,128)(2,1)S(1)}, u32[]{:S(2)}, u32[]{:S(2)}) collective-permute-start(bf16[176,128]{1,0:T(8,128)(2,1)S(1)} %shard_map.136.mine.refs_4_), channel_id=1, source_target_pairs={{0,3},{1,2},{2,1},{3,0},{4,7},{5,6},{6,5},{7,4},{8,11},{9,10},{10,... | collective-permute-start | bytes 135176 | tf_op jit(solution)/shard_map/ppermute | solution.py:96
  77.0 4.7 %collective-permute-start.32 = (bf16[176,128]{1,0:T(8,128)(2,1)S(1)}, bf16[176,128]{1,0:T(8,128)(2,1)S(1)}, u32[]{:S(2)}, u32[]{:S(2)}) collective-permute-start(bf16[176,128]{1,0:T(8,128)(2,1)S(1)} %shard_map.136.mine.refs_4_), channel_id=1, source_target_pairs={{0,2},{1,3},{2,0},{3,1},{4,6},{5,7},{6,4},{7,5},{8,10},{9,11},{10,... | collective-permute-start | bytes 135176 | tf_op jit(solution)/shard_map/ppermute | solution.py:96
  78.5 3.2 %collective-permute-start.31 = (bf16[176,128]{1,0:T(8,128)(2,1)S(1)}, bf16[176,128]{1,0:T(8,128)(2,1)S(1)}, u32[]{:S(2)}, u32[]{:S(2)}) collective-permute-start(bf16[176,128]{1,0:T(8,128)(2,1)S(1)} %shard_map.136.mine.refs_4_), channel_id=1, source_target_pairs={{0,1},{1,0},{2,3},{3,2},{4,5},{5,4},{6,7},{7,6},{8,9},{9,8},{10,11... | collective-permute-start | bytes 135176 | tf_op jit(solution)/shard_map/ppermute | solution.py:96
  81.6 5.0 %collective-permute-start.34 = (bf16[128,128]{1,0:T(8,128)(2,1)S(1)}, bf16[128,128]{1,0:T(8,128)(2,1)S(1)}, u32[]{:S(2)}, u32[]{:S(2)}) collective-permute-start(bf16[128,128]{1,0:T(8,128)(2,1)S(1)} %shard_map.137.refs_3_), channel_id=1, source_target_pairs={{0,4},{4,0},{8,12},{12,8},{1,5},{5,1},{9,13},{13,9},{2,6},{6,2},{1... | collective-permute-start | bytes 98312 | tf_op jit(solution)/shard_map/ppermute | solution.py:96

commit v11 on v10

--- a/solution.py
+++ b/solution.py
@@ -399,32 +399,27 @@
     message[...] = jnp.concatenate(rows, axis=0).astype(BF16)
 
 
-def extras_kernel(z, count, right, mine, *refs):
+def table_kernel(z, count, right, mine, *refs):
     del right
     got, out = refs[:-1], refs[-1]
     _, c = place()
+    highs = z.types // BLOCK
+    high_ids = lax.broadcasted_iota(jnp.int32, (highs, BLOCK), 0).astype(F32) + 1.0
+    low_ids = lax.broadcasted_iota(jnp.int32, (BLOCK, BLOCK), 0).astype(F32)
+    total = jnp.zeros((3 * highs, BLOCK), F32)
     for k in range(z.cols):
         ref = mine if k == 0 else away(got, "col", z.cols, c, k)
-        out[2 * CODES * k : 2 * CODES * (k + 1)] = ref[z.pair :]
-
-
-def add_table(z, extras, out):
-    highs = z.types // BLOCK
-    high_ids = lax.broadcasted_iota(jnp.int32, (highs, BLOCK), 0).astype(F32) + 1.0
-    low_ids = lax.broadcasted_iota(jnp.int32, (BLOCK, BLOCK), 1).astype(F32)
-    total = jnp.zeros((3 * highs, BLOCK), F32)
-    everything = extras[...].astype(F32)
-    down = jnp.transpose(everything)
-    for side in range(2 * z.cols):
-        extra = everything[side * CODES : (side + 1) * CODES]
-        for f in range(z.frame):
-            at = 5 * f
-            low = side * CODES + at + 1
-            hit = high_ids == extra[at : at + 1]
-            terms = [jnp.where(hit, extra[at + 2 + i : at + 3 + i], 0.0) for i in range(3)]
-            left = jnp.concatenate(terms, axis=0).astype(BF16)
-            right = (low_ids == down[:, low : low + 1]).astype(BF16)
-            total = total + jnp.dot(left, right, preferred_element_type=F32)
+        extra = ref[z.pair :].astype(F32)
+        for side in range(2):
+            for f in range(z.frame):
+                at = side * CODES + 5 * f
+                hit = high_ids == extra[at : at + 1]
+                terms = [jnp.where(hit, extra[at + 2 + i : at + 3 + i], 0.0) for i in range(3)]
+                left = jnp.concatenate(terms, axis=0).astype(BF16)
+                right_side = (low_ids == extra[at + 1 : at + 2]).astype(BF16)
+                total = total + lax.dot_general(
+                    left, right_side, (((1,), (1,)), ((), ())), preferred_element_type=F32
+                )
     out[...] = total[0:highs] + total[highs : 2 * highs] + total[2 * highs :]
 
 
@@ -454,9 +449,9 @@
 
 
 def grad_kernel(z, count, per_step, *refs):
-    near_ids, right, later, extras, mine = refs[:5]
-    got = refs[5 : 5 + count]
-    table, out, left, sums, d0, ids, sem = refs[5 + count :]
+    near_ids, right, later, mine = refs[:4]
+    got = refs[4 : 4 + count]
+    out, left, sums, d0, ids, sem = refs[4 + count :]
     n = z.batch
     deep = right.shape[1]
 
@@ -465,7 +460,6 @@
         bring = pltpu.make_async_copy(near_ids, ids, sem)
         bring.start()
         _, c = place()
-        add_table(z, extras, table)
         gather_post(z, c, mine, got, sums, d0)
         lanes = lax.broadcasted_iota(jnp.int32, (BLOCK, deep), 1)
 
@@ -486,11 +480,6 @@
             left[ids[0, begin + s]], right[ids[0, z.slots + begin + s]], preferred_element_type=F32
         )
         out[s] = product.astype(BF16)
-
-
-def finish_kernel(z, own, extras, table):
-    add_table(z, extras, table)
-    table[...] += own[...]
 
 
 def shards(
@@ -641,27 +630,28 @@
         [],
         [*xs, *ds, last_rates],
     )
-    (extras,) = call(
-        functools.partial(extras_kernel, z, len(got)),
-        [shape((2 * CODES * z.cols, BLOCK), BF16)],
+    (table,) = call(
+        functools.partial(table_kernel, z, len(got)),
+        [shape((types // BLOCK, BLOCK))],
         [],
         [right, delta, *got],
     )
     if z.half == 2:
-        their_extras = flip(extras, "row", 1)
-    ins = [ids, right, later, extras, delta, *got]
+        table = table + flip(table, "row", 1)
+    else:
+        table = 0.5 * lax.psum(table, "row")
+    ins = [ids, right, later, delta, *got]
     cost = pl.CostEstimate(
         flops=2 * slots * deep * BLOCK * BLOCK, bytes_accessed=4 * 1024 * 1024, transcendentals=0
     )
     grads = shape((slots, BLOCK, BLOCK), BF16)
     limit = pltpu.CompilerParams(vmem_limit_bytes=24 * 1024 * 1024)
-    table_shape = shape((types // BLOCK, BLOCK))
-    table, weight_grads = pl.pallas_call(
+    weight_grads = pl.pallas_call(
         functools.partial(grad_kernel, z, len(got), per_step),
         grid=(grid,),
-        out_shape=[table_shape, grads],
+        out_shape=grads,
         in_specs=[VMEM] * len(ins),
-        out_specs=[VMEM, pl.BlockSpec((per_step, BLOCK, BLOCK), lambda i: (i, 0, 0))],
+        out_specs=pl.BlockSpec((per_step, BLOCK, BLOCK), lambda i: (i, 0, 0)),
         scratch_shapes=[
             pltpu.VMEM(left_shape.shape, BF16),
             post_sums,
@@ -671,10 +661,6 @@
         cost_estimate=cost,
         compiler_params=limit,
     )(*ins)
-    if z.half == 2:
-        (table,) = call(functools.partial(finish_kernel, z), [table_shape], [], [table, their_extras])
-    else:
-        table = 0.5 * lax.psum(table, "row")
     gain_grads = table.reshape(types)
     return (final_rates, weight_grads.reshape(1, 1, slots, BLOCK, BLOCK), gain_grads)
 

time: 88.1 us -> 87.6 us (level)
  Pallas kernels: 15.8 us -> 14.6 us
    pallas_call x18 -> x17, Pallas kernels: 12.1 us -> 11.3 us  [call(): pl.pallas_call(body, out_shape=outs, in_specs=specs, out_specs=out_specs...]
where the time goes in v11:
time: 87.6 us; the launch traced here: 87.4 us
  starting transfers between devices  38.4 us (44%)
  waiting for transfers between devices  32.1 us (37%)
  Pallas kernels  14.6 us (17%)
  between operations  0.88 us (1%)
    ppermute x35, starting transfers between devices, flip(): return lax.ppermute(x, axis, [(i, i ^ k) for i in range(count)])  38.4 us
    ppermute x35, waiting for transfers between devices, flip(): return lax.ppermute(x, axis, [(i, i ^ k) for i in range(count)])  32.1 us
    pallas_call x17, Pallas kernels, call(): pl.pallas_call(body, out_shape=outs, in_specs=specs, out_specs=out_specs...  11.3 us
    pallas_call x1, Pallas kernels, shards(): pl.pallas_call(functools.partial(grad_kernel, z, len(got), per_step), gri...  3.23 us
  transfers between devices with their start and end apart: 35, of which 28 were waited for; matrix products, arithmetic and copies ran while one was open for 0% of the time, Pallas kernels for 7%

profile of v11, /device:TPU:0, one launch (start us, length us, event | category | flops | bytes accessed | tf_op | source)
XLA Modules:
  0.0 87.4 jit_solution(3519270078599431194)
XLA Ops:
  0.7 0.6 copy-done.6
  1.6 5.1 %collective-permute-start.2 = (bf16[96,128]{1,0:T(8,128)(2,1)S(1)}, bf16[96,128]{1,0:T(8,128)(2,1)S(1)}, u32[]{:S(2)}, u32[]{:S(2)}) collective-permute-start(bf16[96,128]{1,0:T(8,128)(2,1)S(1)} %get-tuple-element.59.after.refs_2_.refs_0_.mine), channel_id=1, source_target_pairs={{0,12},{4,8},{8,4},{12,0},{1,13},{5,9},{9,5},{13,1},{2,14},{6,10},... | collective-permute-start | bytes 73736 | tf_op jit(solution)/shard_map/ppermute | solution.py:96
  6.7 0.6 collective-permute-start
  7.3 1.0 %shard_map.123.refs_1_ = bf16[64,128,128]{2,1,0:T(8,128)(2,1)S(1)} custom-call(bf16[96,128]{1,0:T(8,128)(2,1)S(1)} %get-tuple-element.59.after.refs_2_.refs_0_.mine, bf16[64,128,128]{2,1,0:T(8,128)(2,1)S(1)} %bitcast.6), custom_call_target="tpu_custom_call" | custom-call | bytes 4218880 | tf_op jit(solution)/shard_map/pallas_call | solution.py:78
  8.5 2.0 %collective-permute-done.1.refs_4_.refs_6_ = bf16[96,128]{1,0:T(8,128)(2,1)S(1)} collective-permute-done((bf16[96,128]{1,0:T(8,128)(2,1)S(1)}, bf16[96,128]{1,0:T(8,128)(2,1)S(1)}, u32[]{:S(2)}, u32[]{:S(2)}) %collective-permute-start.1) | collective-permute-done | bytes 24608 | tf_op jit(solution)/shard_map/ppermute | solution.py:96
  10.5 0.9 %collective-permute-done.refs_3_.refs_5_.partner = bf16[96,128]{1,0:T(8,128)(2,1)S(1)} collective-permute-done((bf16[96,128]{1,0:T(8,128)(2,1)S(1)}, bf16[96,128]{1,0:T(8,128)(2,1)S(1)}, u32[]{:S(2)}, u32[]{:S(2)}) %collective-permute-start) | collective-permute-done | bytes 24608 | tf_op jit(solution)/shard_map/ppermute | solution.py:96
  11.4 1.5 %shard_map.124 = (bf16[9,32,128]{2,1,0:T(8,128)(2,1)S(1)}, f32[144,128]{1,0:T(8,128)S(1)}, bf16[144,128]{1,0:T(8,128)(2,1)S(1)}, bf16[144,128]{1,0:T(8,128)(2,1)S(1)}, bf16[144,128]{1,0:T(8,128)(2,1)S(1)}) custom-call(s32[1,128]{1,0:T(1,128)S(1)} %get-tuple-element.58.refs_0_, bf16[64,128,128]{2,1,0:T(8,128)(2,1)S(1)} %shard_map.123.refs_1_, ...), custom_call_target="tpu_custom_call" | custom-call | flops 67108864 | bytes 2454016 | tf_op jit(solution)/shard_map/pallas_call | solution.py:78
  13.0 1.6 %collective-permute-start.4 = (bf16[144,128]{1,0:T(8,128)(2,1)S(1)}, bf16[144,128]{1,0:T(8,128)(2,1)S(1)}, u32[]{:S(2)}, u32[]{:S(2)}) collective-permute-start(bf16[144,128]{1,0:T(8,128)(2,1)S(1)} %get-tuple-element.63), channel_id=1, source_target_pairs={{0,2},{1,3},{2,0},{3,1},{4,6},{5,7},{6,4},{7,5},{8,10},{9,11},{10,... | collective-permute-start | bytes 110600 | tf_op jit(solution)/shard_map/ppermute | solution.py:96
  14.8 1.9 %collective-permute-done.3.refs_1_ = bf16[144,128]{1,0:T(8,128)(2,1)S(1)} collective-permute-done((bf16[144,128]{1,0:T(8,128)(2,1)S(1)}, bf16[144,128]{1,0:T(8,128)(2,1)S(1)}, u32[]{:S(2)}, u32[]{:S(2)}) %collective-permute-start.3) | collective-permute-done | bytes 36896 | tf_op jit(solution)/shard_map/ppermute | solution.py:96
  16.7 0.4 collective-permute-done.4.refs_2_
  17.1 1.7 %collective-permute-start.8 = (bf16[144,128]{1,0:T(8,128)(2,1)S(1)}, bf16[144,128]{1,0:T(8,128)(2,1)S(1)}, u32[]{:S(2)}, u32[]{:S(2)}) collective-permute-start(bf16[144,128]{1,0:T(8,128)(2,1)S(1)} %get-tuple-element.70), channel_id=1, source_target_pairs={{0,12},{4,8},{8,4},{12,0},{1,13},{5,9},{9,5},{13,1},{2,14},{6,10},... | collective-permute-start | bytes 110600 | tf_op jit(solution)/shard_map/ppermute | solution.py:96
  18.9 0.4 collective-permute-start.7
  19.3 2.3 %collective-permute-start.6 = (bf16[144,128]{1,0:T(8,128)(2,1)S(1)}, bf16[144,128]{1,0:T(8,128)(2,1)S(1)}, u32[]{:S(2)}, u32[]{:S(2)}) collective-permute-start(bf16[144,128]{1,0:T(8,128)(2,1)S(1)} %get-tuple-element.70), channel_id=1, source_target_pairs={{0,8},{4,12},{8,0},{12,4},{1,9},{5,13},{9,1},{13,5},{2,10},{6,14},... | collective-permute-start | bytes 110600 | tf_op jit(solution)/shard_map/ppermute | solution.py:96
  21.6 0.9 %shard_map.126 = (f32[288,128]{1,0:T(8,128)S(1)}, f32[288,128]{1,0:T(8,128)S(1)}, f32[3,288,128]{2,1,0:T(8,128)S(1)}, f32[3,72,128]{2,1,0:T(8,128)S(1)}) custom-call(bf16[96,128]{1,0:T(8,128)(2,1)S(1)} %get-tuple-element.59.after.refs_2_.refs_0_.mine, f32[72,128]{1,0:T(8,128)S(1)} %get-tuple-element.66.refs_1_, f32[3,32,288]{2,1,0:T(8,128)S(1)} %copy-done.1, ...), custom_call_target="tpu_custom_call" | custom-call | bytes 1224704 | tf_op jit(solution)/shard_map/pallas_call | solution.py:78
  22.5 0.8 collective-permute-done.8.refs_8_
  23.5 0.7 collective-permute-done.6.refs_6_
  24.2 1.6 %shard_map.127 = (f32[288,128]{1,0:T(8,128)S(1)}, f32[144,128]{1,0:T(8,128)S(1)}, f32[144,128]{1,0:T(8,128)S(1)}, bf16[9,32,128]{2,1,0:T(8,128)(2,1)S(1)}, f32[1...) custom-call(s32[1,128]{1,0:T(1,128)S(1)} %get-tuple-element.58.refs_, ...), custom_call_target="tpu_custom_call" | custom-call | flops 67108864 | bytes 3572224 | tf_op jit(solution)/shard_map/pallas_call | solution.py:78
  25.8 0.5 collective-permute-start.9
  26.3 1.0 %collective-permute-start.10 = (bf16[144,128]{1,0:T(8,128)(2,1)S(1)}, bf16[144,128]{1,0:T(8,128)(2,1)S(1)}, u32[]{:S(2)}, u32[]{:S(2)}) collective-permute-start(bf16[144,128]{1,0:T(8,128)(2,1)S(1)} %get-tuple-element.74), channel_id=1, source_target_pairs={{0,2},{1,3},{2,0},{3,1},{4,6},{5,7},{6,4},{7,5},{8,10},{9,11},{10,... | collective-permute-start | bytes 110600 | tf_op jit(solution)/shard_map/ppermute | solution.py:96
  27.4 0.4 collective-permute-start.11
  27.7 1.9 %collective-permute-done.9.refs_1_ = bf16[144,128]{1,0:T(8,128)(2,1)S(1)} collective-permute-done((bf16[144,128]{1,0:T(8,128)(2,1)S(1)}, bf16[144,128]{1,0:T(8,128)(2,1)S(1)}, u32[]{:S(2)}, u32[]{:S(2)}) %collective-permute-start.9) | collective-permute-done | bytes 36896 | tf_op jit(solution)/shard_map/ppermute | solution.py:96
  29.6 0.9 %collective-permute-done.10.refs_2_ = bf16[144,128]{1,0:T(8,128)(2,1)S(1)} collective-permute-done((bf16[144,128]{1,0:T(8,128)(2,1)S(1)}, bf16[144,128]{1,0:T(8,128)(2,1)S(1)}, u32[]{:S(2)}, u32[]{:S(2)}) %collective-permute-start.10) | collective-permute-done | bytes 36896 | tf_op jit(solution)/shard_map/ppermute | solution.py:96
  30.6 2.3 %collective-permute-start.14 = (bf16[144,128]{1,0:T(8,128)(2,1)S(1)}, bf16[144,128]{1,0:T(8,128)(2,1)S(1)}, u32[]{:S(2)}, u32[]{:S(2)}) collective-permute-start(bf16[144,128]{1,0:T(8,128)(2,1)S(1)} %get-tuple-element.78), channel_id=1, source_target_pairs={{0,12},{4,8},{8,4},{12,0},{1,13},{5,9},{9,5},{13,1},{2,14},{6,10},... | collective-permute-start | bytes 110600 | tf_op jit(solution)/shard_map/ppermute | solution.py:96
  32.9 2.1 %collective-permute-start.12 = (bf16[144,128]{1,0:T(8,128)(2,1)S(1)}, bf16[144,128]{1,0:T(8,128)(2,1)S(1)}, u32[]{:S(2)}, u32[]{:S(2)}) collective-permute-start(bf16[144,128]{1,0:T(8,128)(2,1)S(1)} %get-tuple-element.78), channel_id=1, source_target_pairs={{0,8},{4,12},{8,0},{12,4},{1,9},{5,13},{9,1},{13,5},{2,10},{6,14},... | collective-permute-start | bytes 110600 | tf_op jit(solution)/shard_map/ppermute | solution.py:96
  35.1 1.4 %collective-permute-done.14.refs_8_ = bf16[144,128]{1,0:T(8,128)(2,1)S(1)} collective-permute-done((bf16[144,128]{1,0:T(8,128)(2,1)S(1)}, bf16[144,128]{1,0:T(8,128)(2,1)S(1)}, u32[]{:S(2)}, u32[]{:S(2)}) %collective-permute-start.14) | collective-permute-done | bytes 36896 | tf_op jit(solution)/shard_map/ppermute | solution.py:96
  36.4 0.8 collective-permute-done.13.refs_7_
  37.2 1.0 %collective-permute-done.12.refs_6_ = bf16[144,128]{1,0:T(8,128)(2,1)S(1)} collective-permute-done((bf16[144,128]{1,0:T(8,128)(2,1)S(1)}, bf16[144,128]{1,0:T(8,128)(2,1)S(1)}, u32[]{:S(2)}, u32[]{:S(2)}) %collective-permute-start.12) | collective-permute-done | bytes 36896 | tf_op jit(solution)/shard_map/ppermute | solution.py:96
  38.2 1.6 %shard_map.129 = (f32[288,128]{1,0:T(8,128)S(1)}, f32[144,128]{1,0:T(8,128)S(1)}, f32[144,128]{1,0:T(8,128)S(1)}, bf16[9,32,128]{2,1,0:T(8,128)(2,1)S(1)}, f32[1...) custom-call(s32[1,128]{1,0:T(1,128)S(1)} %get-tuple-element.58.refs_, ...), custom_call_target="tpu_custom_call" | custom-call | flops 67108864 | bytes 3572224 | tf_op jit(solution)/shard_map/pallas_call | solution.py:78
  39.8 1.3 %collective-permute-start.16 = (bf16[144,128]{1,0:T(8,128)(2,1)S(1)}, bf16[144,128]{1,0:T(8,128)(2,1)S(1)}, u32[]{:S(2)}, u32[]{:S(2)}) collective-permute-start(bf16[144,128]{1,0:T(8,128)(2,1)S(1)} %get-tuple-element.82), channel_id=1, source_target_pairs={{0,2},{1,3},{2,0},{3,1},{4,6},{5,7},{6,4},{7,5},{8,10},{9,11},{10,... | collective-permute-start | bytes 110600 | tf_op jit(solution)/shard_map/ppermute | solution.py:96
  41.2 0.5 collective-permute-start.17
  41.7 1.7 %collective-permute-done.15.refs_1_ = bf16[144,128]{1,0:T(8,128)(2,1)S(1)} collective-permute-done((bf16[144,128]{1,0:T(8,128)(2,1)S(1)}, bf16[144,128]{1,0:T(8,128)(2,1)S(1)}, u32[]{:S(2)}, u32[]{:S(2)}) %collective-permute-start.15) | collective-permute-done | bytes 36896 | tf_op jit(solution)/shard_map/ppermute | solution.py:96
  43.4 0.5 collective-permute-done.16.refs_2_
  44.0 2.1 %collective-permute-start.18 = (bf16[224,128]{1,0:T(8,128)(2,1)S(1)}, bf16[224,128]{1,0:T(8,128)(2,1)S(1)}, u32[]{:S(2)}, u32[]{:S(2)}) collective-permute-start(bf16[224,128]{1,0:T(8,128)(2,1)S(1)} %get-tuple-element.86), channel_id=1, source_target_pairs={{0,8},{4,12},{8,0},{12,4},{1,9},{5,13},{9,1},{13,5},{2,10},{6,14},... | collective-permute-start | bytes 172040 | tf_op jit(solution)/shard_map/ppermute | solution.py:96
  46.0 4.3 %collective-permute-done.18.theirs = bf16[224,128]{1,0:T(8,128)(2,1)S(1)} collective-permute-done((bf16[224,128]{1,0:T(8,128)(2,1)S(1)}, bf16[224,128]{1,0:T(8,128)(2,1)S(1)}, u32[]{:S(2)}, u32[]{:S(2)}) %collective-permute-start.18) | collective-permute-done | bytes 57376 | tf_op jit(solution)/shard_map/ppermute | solution.py:96
  50.5 1.5 %collective-permute-start.20 = (bf16[144,128]{1,0:T(8,128)(2,1)S(1)}, bf16[144,128]{1,0:T(8,128)(2,1)S(1)}, u32[]{:S(2)}, u32[]{:S(2)}) collective-permute-start(bf16[144,128]{1,0:T(8,128)(2,1)S(1)} %get-tuple-element.89.refs_3_), channel_id=1, source_target_pairs={{0,2},{1,3},{2,0},{3,1},{4,6},{5,7},{6,4},{7,5},{8,10},{9,11},{10,... | collective-permute-start | bytes 110600 | tf_op jit(solution)/shard_map/ppermute | solution.py:96
  52.0 0.3 collective-permute-start.19
  52.3 1.9 %collective-permute-done.21.refs_6_ = bf16[144,128]{1,0:T(8,128)(2,1)S(1)} collective-permute-done((bf16[144,128]{1,0:T(8,128)(2,1)S(1)}, bf16[144,128]{1,0:T(8,128)(2,1)S(1)}, u32[]{:S(2)}, u32[]{:S(2)}) %collective-permute-start.21) | collective-permute-done | bytes 36896 | tf_op jit(solution)/shard_map/ppermute | solution.py:96
  54.2 0.4 collective-permute-done.20.refs_5_
  54.6 1.5 %shard_map.132 = (bf16[18,32,128]{2,1,0:T(8,128)(2,1)S(1)}, f32[144,128]{1,0:T(8,128)S(1)}, bf16[144,128]{1,0:T(8,128)(2,1)S(1)}, bf16[144,128]{1,0:T(8,128)(2,1)S(1)}, bf16[144,128]{1,0:T(8,128)(2,1)S(1)}) custom-call(s32[1,128]{1,0:T(1,128)S(1)} %get-tuple-element.58.refs_0_, bf16[64,128,128]{2,1,0:T(8,128)(2,1)S(1)} %bitcast.7, ...), custom_call_target="tpu_custom_call" | custom-call | flops 67108864 | bytes 2613760 | tf_op jit(solution)/shard_map/pallas_call | solution.py:78
  56.1 1.9 %collective-permute-start.22 = (bf16[144,128]{1,0:T(8,128)(2,1)S(1)}, bf16[144,128]{1,0:T(8,128)(2,1)S(1)}, u32[]{:S(2)}, u32[]{:S(2)}) collective-permute-start(bf16[144,128]{1,0:T(8,128)(2,1)S(1)} %get-tuple-element.95), channel_id=1, source_target_pairs={{0,12},{4,8},{8,4},{12,0},{1,13},{5,9},{9,5},{13,1},{2,14},{6,10},... | collective-permute-start | bytes 110600 | tf_op jit(solution)/shard_map/ppermute | solution.py:96
  58.0 2.6 %collective-permute-start.24 = (bf16[144,128]{1,0:T(8,128)(2,1)S(1)}, bf16[144,128]{1,0:T(8,128)(2,1)S(1)}, u32[]{:S(2)}, u32[]{:S(2)}) collective-permute-start(bf16[144,128]{1,0:T(8,128)(2,1)S(1)} %get-tuple-element.97), channel_id=1, source_target_pairs={{0,8},{4,12},{8,0},{12,4},{1,9},{5,13},{9,1},{13,5},{2,10},{6,14},... | collective-permute-start | bytes 110600 | tf_op jit(solution)/shard_map/ppermute | solution.py:96
  60.6 1.5 %collective-permute-done.22.refs_0_ = bf16[144,128]{1,0:T(8,128)(2,1)S(1)} collective-permute-done((bf16[144,128]{1,0:T(8,128)(2,1)S(1)}, bf16[144,128]{1,0:T(8,128)(2,1)S(1)}, u32[]{:S(2)}, u32[]{:S(2)}) %collective-permute-start.22) | collective-permute-done | bytes 36896 | tf_op jit(solution)/shard_map/ppermute | solution.py:96
  62.1 0.6 collective-permute-done.23.refs_1_
  62.7 0.6 collective-permute-done.24.refs_2_
  63.4 1.3 %collective-permute-start.26 = (bf16[144,128]{1,0:T(8,128)(2,1)S(1)}, bf16[144,128]{1,0:T(8,128)(2,1)S(1)}, u32[]{:S(2)}, u32[]{:S(2)}) collective-permute-start(bf16[144,128]{1,0:T(8,128)(2,1)S(1)} %get-tuple-element.99.refs_3_), channel_id=1, source_target_pairs={{0,2},{1,3},{2,0},{3,1},{4,6},{5,7},{6,4},{7,5},{8,10},{9,11},{10,... | collective-permute-start | bytes 110600 | tf_op jit(solution)/shard_map/ppermute | solution.py:96
  64.7 0.5 collective-permute-start.25
  65.3 1.7 %collective-permute-done.27.refs_6_ = bf16[144,128]{1,0:T(8,128)(2,1)S(1)} collective-permute-done((bf16[144,128]{1,0:T(8,128)(2,1)S(1)}, bf16[144,128]{1,0:T(8,128)(2,1)S(1)}, u32[]{:S(2)}, u32[]{:S(2)}) %collective-permute-start.27) | collective-permute-done | bytes 36896 | tf_op jit(solution)/shard_map/ppermute | solution.py:96
  67.0 0.5 collective-permute-done.26.refs_5_
  67.5 1.5 %shard_map.134 = (bf16[18,32,128]{2,1,0:T(8,128)(2,1)S(1)}, f32[144,128]{1,0:T(8,128)S(1)}, bf16[144,128]{1,0:T(8,128)(2,1)S(1)}, bf16[144,128]{1,0:T(8,128)(2,1)S(1)}, bf16[144,128]{1,0:T(8,128)(2,1)S(1)}) custom-call(s32[1,128]{1,0:T(1,128)S(1)} %get-tuple-element.58.refs_0_, bf16[64,128,128]{2,1,0:T(8,128)(2,1)S(1)} %bitcast.8, ...), custom_call_target="tpu_custom_call" | custom-call | flops 67108864 | bytes 2613760 | tf_op jit(solution)/shard_map/pallas_call | solution.py:78
  69.0 2.1 %collective-permute-start.28 = (bf16[144,128]{1,0:T(8,128)(2,1)S(1)}, bf16[144,128]{1,0:T(8,128)(2,1)S(1)}, u32[]{:S(2)}, u32[]{:S(2)}) collective-permute-start(bf16[144,128]{1,0:T(8,128)(2,1)S(1)} %get-tuple-element.110), channel_id=1, source_target_pairs={{0,12},{4,8},{8,4},{12,0},{1,13},{5,9},{9,5},{13,1},{2,14},{6,10},... | collective-permute-start | bytes 110600 | tf_op jit(solution)/shard_map/ppermute | solution.py:96
  71.1 0.8 collective-permute-start.29
  71.9 1.6 %collective-permute-start.30 = (bf16[144,128]{1,0:T(8,128)(2,1)S(1)}, bf16[144,128]{1,0:T(8,128)(2,1)S(1)}, u32[]{:S(2)}, u32[]{:S(2)}) collective-permute-start(bf16[144,128]{1,0:T(8,128)(2,1)S(1)} %get-tuple-element.112), channel_id=1, source_target_pairs={{0,8},{4,12},{8,0},{12,4},{1,9},{5,13},{9,1},{13,5},{2,10},{6,14},... | collective-permute-start | bytes 110600 | tf_op jit(solution)/shard_map/ppermute | solution.py:96
  73.5 1.4 %collective-permute-done.28.refs_0_ = bf16[144,128]{1,0:T(8,128)(2,1)S(1)} collective-permute-done((bf16[144,128]{1,0:T(8,128)(2,1)S(1)}, bf16[144,128]{1,0:T(8,128)(2,1)S(1)}, u32[]{:S(2)}, u32[]{:S(2)}) %collective-permute-start.28) | collective-permute-done | bytes 36896 | tf_op jit(solution)/shard_map/ppermute | solution.py:96
  74.9 0.8 collective-permute-done.29.refs_1_
  75.7 1.1 %collective-permute-done.30.refs_2_ = bf16[144,128]{1,0:T(8,128)(2,1)S(1)} collective-permute-done((bf16[144,128]{1,0:T(8,128)(2,1)S(1)}, bf16[144,128]{1,0:T(8,128)(2,1)S(1)}, u32[]{:S(2)}, u32[]{:S(2)}) %collective-permute-start.30) | collective-permute-done | bytes 36896 | tf_op jit(solution)/shard_map/ppermute | solution.py:96
  76.9 1.5 %collective-permute-start.32 = (bf16[176,128]{1,0:T(8,128)(2,1)S(1)}, bf16[176,128]{1,0:T(8,128)(2,1)S(1)}, u32[]{:S(2)}, u32[]{:S(2)}) collective-permute-start(bf16[176,128]{1,0:T(8,128)(2,1)S(1)} %shard_map.136.refs_3_.mine), channel_id=1, source_target_pairs={{0,2},{1,3},{2,0},{3,1},{4,6},{5,7},{6,4},{7,5},{8,10},{9,11},{10,... | collective-permute-start | bytes 135176 | tf_op jit(solution)/shard_map/ppermute | solution.py:96
  78.5 0.3 collective-permute-start.31
  78.8 0.8 shard_map.135
  79.6 1.3 %collective-permute-done.33.refs_6_.refs_2_ = bf16[176,128]{1,0:T(8,128)(2,1)S(1)} collective-permute-done((bf16[176,128]{1,0:T(8,128)(2,1)S(1)}, bf16[176,128]{1,0:T(8,128)(2,1)S(1)}, u32[]{:S(2)}, u32[]{:S(2)}) %collective-permute-start.33) | collective-permute-done | bytes 45088 | tf_op jit(solution)/shard_map/ppermute | solution.py:96
  80.9 0.7 collective-permute-done.32.refs_5_.refs_1_
  81.6 0.6 shard_map.138
  82.2 1.2 %collective-permute-start.34 = (f32[64,128]{1,0:T(8,128)S(1)}, f32[64,128]{1,0:T(8,128)S(1)}, u32[]{:S(2)}, u32[]{:S(2)}) collective-permute-start(f32[64,128]{1,0:T(8,128)S(1)} %shard_map.138), channel_id=1, source_target_pairs={{0,4},{4,0},{8,12},{12,8},{1,5},{5,1},{9,13},{13,9},{2,6},{6,2},{1... | collective-permute-start | bytes 98312 | tf_op jit(solution)/shard_map/ppermute | solution.py:96
  83.5 3.2 %shard_map.137 = bf16[64,128,128]{2,1,0:T(8,128)(2,1)} custom-call(s32[1,128]{1,0:T(1,128)S(1)} %get-tuple-element.58.refs_0_, bf16[9,128,128]{2,1,0:T(8,128)(2,1)S(1)} %get-tuple-element.104.refs_1_.right, bf16[18,128,128]{2,1,0:T(8,128)(2,1)S(1)} %get-tuple-element.105.refs_2_, bf16[176,128]{1,0:T(8,128)(2,1)S(1)} %shard_map.136.refs_3_.mine, ...), custom_call_target="tpu_custom_call" | custom-call | flops 268435456 | bytes 4194304 | tf_op jit(solution)/shard_map/pallas_call | solution.py:649
  86.7 0.6 add_bitcast_fusion
  (45 shorter events, 1.6 us)
Async XLA Ops:
  0.6 0.7 copy-start.6
  0.6 0.7 copy-start.5
  0.7 0.7 copy-start.9
  0.7 0.7 copy-start.8
  0.7 0.7 copy-start.7
  0.7 0.8 copy-start.3
  0.7 6.6 %copy-start = (bf16[1,1,64,128,128]{4,3,2,1,0:T(8,128)(2,1)S(1)}, bf16[1,1,64,128,128]{4,3,2,1,0:T(8,128)(2,1)}, u32[]{:S(2)}) copy-start(bf16[1,1,64,128,128]{4,3,2,1,0:T(8,128)(2,1)} %param.13) | copy-start | bytes 6291460
  1.6 6.9 %collective-permute-start.2 = (bf16[96,128]{1,0:T(8,128)(2,1)S(1)}, bf16[96,128]{1,0:T(8,128)(2,1)S(1)}, u32[]{:S(2)}, u32[]{:S(2)}) collective-permute-start(bf16[96,128]{1,0:T(8,128)(2,1)S(1)} %get-tuple-element.59.after.refs_2_.refs_0_.mine), channel_id=1, source_target_pairs={{0,12},{4,8},{8,4},{12,0},{1,13},{5,9},{9,5},{13,1},{2,14},{6,10},... | collective-permute-start | bytes 73736 | tf_op jit(solution)/shard_map/ppermute | solution.py:96
  6.6 3.8 %collective-permute-start.1 = (bf16[96,128]{1,0:T(8,128)(2,1)S(1)}, bf16[96,128]{1,0:T(8,128)(2,1)S(1)}, u32[]{:S(2)}, u32[]{:S(2)}) collective-permute-start(bf16[96,128]{1,0:T(8,128)(2,1)S(1)} %get-tuple-element.59.after.refs_2_.refs_0_.mine), channel_id=1, source_target_pairs={{0,4},{4,0},{8,12},{12,8},{1,5},{5,1},{9,13},{13,9},{2,6},{6,2},{1... | collective-permute-start | bytes 73736 | tf_op jit(solution)/shard_map/ppermute | solution.py:96
  6.7 4.8 %collective-permute-start = (bf16[96,128]{1,0:T(8,128)(2,1)S(1)}, bf16[96,128]{1,0:T(8,128)(2,1)S(1)}, u32[]{:S(2)}, u32[]{:S(2)}) collective-permute-start(bf16[96,128]{1,0:T(8,128)(2,1)S(1)} %get-tuple-element.59.after.refs_2_.refs_0_.mine), channel_id=1, source_target_pairs={{0,8},{4,12},{8,0},{12,4},{1,9},{5,13},{9,1},{13,5},{2,10},{6,14},... | collective-permute-start | bytes 73736 | tf_op jit(solution)/shard_map/ppermute | solution.py:96
  8.3 13.3 %copy-start.1 = (f32[3,32,288]{2,1,0:T(8,128)S(1)}, f32[3,32,288]{2,1,0:T(8,128)}, u32[]{:S(2)}) copy-start(f32[3,32,288]{2,1,0:T(8,128)} %refs_2_.1) | copy-start | bytes 331780
  8.3 13.3 %copy-start.2 = (bf16[3,32,512]{2,1,0:T(8,128)(2,1)S(1)}, bf16[3,32,512]{2,1,0:T(8,128)(2,1)}, u32[]{:S(2)}) copy-start(bf16[3,32,512]{2,1,0:T(8,128)(2,1)} %param.11) | copy-start | bytes 294916
  8.3 13.3 %copy-start.4 = (f32[8192]{0:T(1024)S(1)}, f32[8192]{0:T(1024)}, u32[]{:S(2)}) copy-start(f32[8192]{0:T(1024)} %param.18) | copy-start | bytes 98308
  12.9 3.8 %collective-permute-start.3 = (bf16[144,128]{1,0:T(8,128)(2,1)S(1)}, bf16[144,128]{1,0:T(8,128)(2,1)S(1)}, u32[]{:S(2)}, u32[]{:S(2)}) collective-permute-start(bf16[144,128]{1,0:T(8,128)(2,1)S(1)} %get-tuple-element.62), channel_id=1, source_target_pairs={{0,3},{1,2},{2,1},{3,0},{4,7},{5,6},{6,5},{7,4},{8,11},{9,10},{10,... | collective-permute-start | bytes 110600 | tf_op jit(solution)/shard_map/ppermute | solution.py:96
  13.0 4.2 %collective-permute-start.4 = (bf16[144,128]{1,0:T(8,128)(2,1)S(1)}, bf16[144,128]{1,0:T(8,128)(2,1)S(1)}, u32[]{:S(2)}, u32[]{:S(2)}) collective-permute-start(bf16[144,128]{1,0:T(8,128)(2,1)S(1)} %get-tuple-element.63), channel_id=1, source_target_pairs={{0,2},{1,3},{2,0},{3,1},{4,6},{5,7},{6,4},{7,5},{8,10},{9,11},{10,... | collective-permute-start | bytes 110600 | tf_op jit(solution)/shard_map/ppermute | solution.py:96
  14.5 2.6 %collective-permute-start.5 = (bf16[144,128]{1,0:T(8,128)(2,1)S(1)}, bf16[144,128]{1,0:T(8,128)(2,1)S(1)}, u32[]{:S(2)}, u32[]{:S(2)}) collective-permute-start(bf16[144,128]{1,0:T(8,128)(2,1)S(1)} %get-tuple-element.64), channel_id=1, source_target_pairs={{0,1},{1,0},{2,3},{3,2},{4,5},{5,4},{6,7},{7,6},{8,9},{9,8},{10,11... | collective-permute-start | bytes 110600 | tf_op jit(solution)/shard_map/ppermute | solution.py:96
  17.1 6.2 %collective-permute-start.8 = (bf16[144,128]{1,0:T(8,128)(2,1)S(1)}, bf16[144,128]{1,0:T(8,128)(2,1)S(1)}, u32[]{:S(2)}, u32[]{:S(2)}) collective-permute-start(bf16[144,128]{1,0:T(8,128)(2,1)S(1)} %get-tuple-element.70), channel_id=1, source_target_pairs={{0,12},{4,8},{8,4},{12,0},{1,13},{5,9},{9,5},{13,1},{2,14},{6,10},... | collective-permute-start | bytes 110600 | tf_op jit(solution)/shard_map/ppermute | solution.py:96
  18.9 4.7 %collective-permute-start.7 = (bf16[144,128]{1,0:T(8,128)(2,1)S(1)}, bf16[144,128]{1,0:T(8,128)(2,1)S(1)}, u32[]{:S(2)}, u32[]{:S(2)}) collective-permute-start(bf16[144,128]{1,0:T(8,128)(2,1)S(1)} %get-tuple-element.70), channel_id=1, source_target_pairs={{0,4},{4,0},{8,12},{12,8},{1,5},{5,1},{9,13},{13,9},{2,6},{6,2},{1... | collective-permute-start | bytes 110600 | tf_op jit(solution)/shard_map/ppermute | solution.py:96
  19.3 5.0 %collective-permute-start.6 = (bf16[144,128]{1,0:T(8,128)(2,1)S(1)}, bf16[144,128]{1,0:T(8,128)(2,1)S(1)}, u32[]{:S(2)}, u32[]{:S(2)}) collective-permute-start(bf16[144,128]{1,0:T(8,128)(2,1)S(1)} %get-tuple-element.70), channel_id=1, source_target_pairs={{0,8},{4,12},{8,0},{12,4},{1,9},{5,13},{9,1},{13,5},{2,10},{6,14},... | collective-permute-start | bytes 110600 | tf_op jit(solution)/shard_map/ppermute | solution.py:96
  25.8 3.8 %collective-permute-start.9 = (bf16[144,128]{1,0:T(8,128)(2,1)S(1)}, bf16[144,128]{1,0:T(8,128)(2,1)S(1)}, u32[]{:S(2)}, u32[]{:S(2)}) collective-permute-start(bf16[144,128]{1,0:T(8,128)(2,1)S(1)} %get-tuple-element.73), channel_id=1, source_target_pairs={{0,3},{1,2},{2,1},{3,0},{4,7},{5,6},{6,5},{7,4},{8,11},{9,10},{10,... | collective-permute-start | bytes 110600 | tf_op jit(solution)/shard_map/ppermute | solution.py:96
  26.3 4.2 %collective-permute-start.10 = (bf16[144,128]{1,0:T(8,128)(2,1)S(1)}, bf16[144,128]{1,0:T(8,128)(2,1)S(1)}, u32[]{:S(2)}, u32[]{:S(2)}) collective-permute-start(bf16[144,128]{1,0:T(8,128)(2,1)S(1)} %get-tuple-element.74), channel_id=1, source_target_pairs={{0,2},{1,3},{2,0},{3,1},{4,6},{5,7},{6,4},{7,5},{8,10},{9,11},{10,... | collective-permute-start | bytes 110600 | tf_op jit(solution)/shard_map/ppermute | solution.py:96
  27.4 3.2 %collective-permute-start.11 = (bf16[144,128]{1,0:T(8,128)(2,1)S(1)}, bf16[144,128]{1,0:T(8,128)(2,1)S(1)}, u32[]{:S(2)}, u32[]{:S(2)}) collective-permute-start(bf16[144,128]{1,0:T(8,128)(2,1)S(1)} %get-tuple-element.75), channel_id=1, source_target_pairs={{0,1},{1,0},{2,3},{3,2},{4,5},{5,4},{6,7},{7,6},{8,9},{9,8},{10,11... | collective-permute-start | bytes 110600 | tf_op jit(solution)/shard_map/ppermute | solution.py:96
  30.6 5.8 %collective-permute-start.14 = (bf16[144,128]{1,0:T(8,128)(2,1)S(1)}, bf16[144,128]{1,0:T(8,128)(2,1)S(1)}, u32[]{:S(2)}, u32[]{:S(2)}) collective-permute-start(bf16[144,128]{1,0:T(8,128)(2,1)S(1)} %get-tuple-element.78), channel_id=1, source_target_pairs={{0,12},{4,8},{8,4},{12,0},{1,13},{5,9},{9,5},{13,1},{2,14},{6,10},... | collective-permute-start | bytes 110600 | tf_op jit(solution)/shard_map/ppermute | solution.py:96
  32.9 4.3 %collective-permute-start.13 = (bf16[144,128]{1,0:T(8,128)(2,1)S(1)}, bf16[144,128]{1,0:T(8,128)(2,1)S(1)}, u32[]{:S(2)}, u32[]{:S(2)}) collective-permute-start(bf16[144,128]{1,0:T(8,128)(2,1)S(1)} %get-tuple-element.78), channel_id=1, source_target_pairs={{0,4},{4,0},{8,12},{12,8},{1,5},{5,1},{9,13},{13,9},{2,6},{6,2},{1... | collective-permute-start | bytes 110600 | tf_op jit(solution)/shard_map/ppermute | solution.py:96
  32.9 5.3 %collective-permute-start.12 = (bf16[144,128]{1,0:T(8,128)(2,1)S(1)}, bf16[144,128]{1,0:T(8,128)(2,1)S(1)}, u32[]{:S(2)}, u32[]{:S(2)}) collective-permute-start(bf16[144,128]{1,0:T(8,128)(2,1)S(1)} %get-tuple-element.78), channel_id=1, source_target_pairs={{0,8},{4,12},{8,0},{12,4},{1,9},{5,13},{9,1},{13,5},{2,10},{6,14},... | collective-permute-start | bytes 110600 | tf_op jit(solution)/shard_map/ppermute | solution.py:96
  39.8 3.7 %collective-permute-start.15 = (bf16[144,128]{1,0:T(8,128)(2,1)S(1)}, bf16[144,128]{1,0:T(8,128)(2,1)S(1)}, u32[]{:S(2)}, u32[]{:S(2)}) collective-permute-start(bf16[144,128]{1,0:T(8,128)(2,1)S(1)} %get-tuple-element.81), channel_id=1, source_target_pairs={{0,3},{1,2},{2,1},{3,0},{4,7},{5,6},{6,5},{7,4},{8,11},{9,10},{10,... | collective-permute-start | bytes 110600 | tf_op jit(solution)/shard_map/ppermute | solution.py:96
  39.8 4.1 %collective-permute-start.16 = (bf16[144,128]{1,0:T(8,128)(2,1)S(1)}, bf16[144,128]{1,0:T(8,128)(2,1)S(1)}, u32[]{:S(2)}, u32[]{:S(2)}) collective-permute-start(bf16[144,128]{1,0:T(8,128)(2,1)S(1)} %get-tuple-element.82), channel_id=1, source_target_pairs={{0,2},{1,3},{2,0},{3,1},{4,6},{5,7},{6,4},{7,5},{8,10},{9,11},{10,... | collective-permute-start | bytes 110600 | tf_op jit(solution)/shard_map/ppermute | solution.py:96
  41.2 2.7 %collective-permute-start.17 = (bf16[144,128]{1,0:T(8,128)(2,1)S(1)}, bf16[144,128]{1,0:T(8,128)(2,1)S(1)}, u32[]{:S(2)}, u32[]{:S(2)}) collective-permute-start(bf16[144,128]{1,0:T(8,128)(2,1)S(1)} %get-tuple-element.83), channel_id=1, source_target_pairs={{0,1},{1,0},{2,3},{3,2},{4,5},{5,4},{6,7},{7,6},{8,9},{9,8},{10,11... | collective-permute-start | bytes 110600 | tf_op jit(solution)/shard_map/ppermute | solution.py:96
  44.0 6.4 %collective-permute-start.18 = (bf16[224,128]{1,0:T(8,128)(2,1)S(1)}, bf16[224,128]{1,0:T(8,128)(2,1)S(1)}, u32[]{:S(2)}, u32[]{:S(2)}) collective-permute-start(bf16[224,128]{1,0:T(8,128)(2,1)S(1)} %get-tuple-element.86), channel_id=1, source_target_pairs={{0,8},{4,12},{8,0},{12,4},{1,9},{5,13},{9,1},{13,5},{2,10},{6,14},... | collective-permute-start | bytes 172040 | tf_op jit(solution)/shard_map/ppermute | solution.py:96
  50.4 3.8 %collective-permute-start.21 = (bf16[144,128]{1,0:T(8,128)(2,1)S(1)}, bf16[144,128]{1,0:T(8,128)(2,1)S(1)}, u32[]{:S(2)}, u32[]{:S(2)}) collective-permute-start(bf16[144,128]{1,0:T(8,128)(2,1)S(1)} %get-tuple-element.89.refs_3_), channel_id=1, source_target_pairs={{0,3},{1,2},{2,1},{3,0},{4,7},{5,6},{6,5},{7,4},{8,11},{9,10},{10,... | collective-permute-start | bytes 110600 | tf_op jit(solution)/shard_map/ppermute | solution.py:96
  50.5 4.1 %collective-permute-start.20 = (bf16[144,128]{1,0:T(8,128)(2,1)S(1)}, bf16[144,128]{1,0:T(8,128)(2,1)S(1)}, u32[]{:S(2)}, u32[]{:S(2)}) collective-permute-start(bf16[144,128]{1,0:T(8,128)(2,1)S(1)} %get-tuple-element.89.refs_3_), channel_id=1, source_target_pairs={{0,2},{1,3},{2,0},{3,1},{4,6},{5,7},{6,4},{7,5},{8,10},{9,11},{10,... | collective-permute-start | bytes 110600 | tf_op jit(solution)/shard_map/ppermute | solution.py:96
  52.0 2.7 %collective-permute-start.19 = (bf16[144,128]{1,0:T(8,128)(2,1)S(1)}, bf16[144,128]{1,0:T(8,128)(2,1)S(1)}, u32[]{:S(2)}, u32[]{:S(2)}) collective-permute-start(bf16[144,128]{1,0:T(8,128)(2,1)S(1)} %get-tuple-element.89.refs_3_), channel_id=1, source_target_pairs={{0,1},{1,0},{2,3},{3,2},{4,5},{5,4},{6,7},{7,6},{8,9},{9,8},{10,11... | collective-permute-start | bytes 110600 | tf_op jit(solution)/shard_map/ppermute | solution.py:96
  56.1 6.0 %collective-permute-start.22 = (bf16[144,128]{1,0:T(8,128)(2,1)S(1)}, bf16[144,128]{1,0:T(8,128)(2,1)S(1)}, u32[]{:S(2)}, u32[]{:S(2)}) collective-permute-start(bf16[144,128]{1,0:T(8,128)(2,1)S(1)} %get-tuple-element.95), channel_id=1, source_target_pairs={{0,12},{4,8},{8,4},{12,0},{1,13},{5,9},{9,5},{13,1},{2,14},{6,10},... | collective-permute-start | bytes 110600 | tf_op jit(solution)/shard_map/ppermute | solution.py:96
  58.0 4.7 %collective-permute-start.23 = (bf16[144,128]{1,0:T(8,128)(2,1)S(1)}, bf16[144,128]{1,0:T(8,128)(2,1)S(1)}, u32[]{:S(2)}, u32[]{:S(2)}) collective-permute-start(bf16[144,128]{1,0:T(8,128)(2,1)S(1)} %get-tuple-element.96), channel_id=1, source_target_pairs={{0,4},{4,0},{8,12},{12,8},{1,5},{5,1},{9,13},{13,9},{2,6},{6,2},{1... | collective-permute-start | bytes 110600 | tf_op jit(solution)/shard_map/ppermute | solution.py:96
  58.0 5.3 %collective-permute-start.24 = (bf16[144,128]{1,0:T(8,128)(2,1)S(1)}, bf16[144,128]{1,0:T(8,128)(2,1)S(1)}, u32[]{:S(2)}, u32[]{:S(2)}) collective-permute-start(bf16[144,128]{1,0:T(8,128)(2,1)S(1)} %get-tuple-element.97), channel_id=1, source_target_pairs={{0,8},{4,12},{8,0},{12,4},{1,9},{5,13},{9,1},{13,5},{2,10},{6,14},... | collective-permute-start | bytes 110600 | tf_op jit(solution)/shard_map/ppermute | solution.py:96
  63.3 3.7 %collective-permute-start.27 = (bf16[144,128]{1,0:T(8,128)(2,1)S(1)}, bf16[144,128]{1,0:T(8,128)(2,1)S(1)}, u32[]{:S(2)}, u32[]{:S(2)}) collective-permute-start(bf16[144,128]{1,0:T(8,128)(2,1)S(1)} %get-tuple-element.99.refs_3_), channel_id=1, source_target_pairs={{0,3},{1,2},{2,1},{3,0},{4,7},{5,6},{6,5},{7,4},{8,11},{9,10},{10,... | collective-permute-start | bytes 110600 | tf_op jit(solution)/shard_map/ppermute | solution.py:96
  63.4 4.1 %collective-permute-start.26 = (bf16[144,128]{1,0:T(8,128)(2,1)S(1)}, bf16[144,128]{1,0:T(8,128)(2,1)S(1)}, u32[]{:S(2)}, u32[]{:S(2)}) collective-permute-start(bf16[144,128]{1,0:T(8,128)(2,1)S(1)} %get-tuple-element.99.refs_3_), channel_id=1, source_target_pairs={{0,2},{1,3},{2,0},{3,1},{4,6},{5,7},{6,4},{7,5},{8,10},{9,11},{10,... | collective-permute-start | bytes 110600 | tf_op jit(solution)/shard_map/ppermute | solution.py:96
  64.7 2.8 %collective-permute-start.25 = (bf16[144,128]{1,0:T(8,128)(2,1)S(1)}, bf16[144,128]{1,0:T(8,128)(2,1)S(1)}, u32[]{:S(2)}, u32[]{:S(2)}) collective-permute-start(bf16[144,128]{1,0:T(8,128)(2,1)S(1)} %get-tuple-element.99.refs_3_), channel_id=1, source_target_pairs={{0,1},{1,0},{2,3},{3,2},{4,5},{5,4},{6,7},{7,6},{8,9},{9,8},{10,11... | collective-permute-start | bytes 110600 | tf_op jit(solution)/shard_map/ppermute | solution.py:96
  69.0 5.9 %collective-permute-start.28 = (bf16[144,128]{1,0:T(8,128)(2,1)S(1)}, bf16[144,128]{1,0:T(8,128)(2,1)S(1)}, u32[]{:S(2)}, u32[]{:S(2)}) collective-permute-start(bf16[144,128]{1,0:T(8,128)(2,1)S(1)} %get-tuple-element.110), channel_id=1, source_target_pairs={{0,12},{4,8},{8,4},{12,0},{1,13},{5,9},{9,5},{13,1},{2,14},{6,10},... | collective-permute-start | bytes 110600 | tf_op jit(solution)/shard_map/ppermute | solution.py:96
  71.1 4.6 %collective-permute-start.29 = (bf16[144,128]{1,0:T(8,128)(2,1)S(1)}, bf16[144,128]{1,0:T(8,128)(2,1)S(1)}, u32[]{:S(2)}, u32[]{:S(2)}) collective-permute-start(bf16[144,128]{1,0:T(8,128)(2,1)S(1)} %get-tuple-element.111), channel_id=1, source_target_pairs={{0,4},{4,0},{8,12},{12,8},{1,5},{5,1},{9,13},{13,9},{2,6},{6,2},{1... | collective-permute-start | bytes 110600 | tf_op jit(solution)/shard_map/ppermute | solution.py:96
  71.9 4.9 %collective-permute-start.30 = (bf16[144,128]{1,0:T(8,128)(2,1)S(1)}, bf16[144,128]{1,0:T(8,128)(2,1)S(1)}, u32[]{:S(2)}, u32[]{:S(2)}) collective-permute-start(bf16[144,128]{1,0:T(8,128)(2,1)S(1)} %get-tuple-element.112), channel_id=1, source_target_pairs={{0,8},{4,12},{8,0},{12,4},{1,9},{5,13},{9,1},{13,5},{2,10},{6,14},... | collective-permute-start | bytes 110600 | tf_op jit(solution)/shard_map/ppermute | solution.py:96
  76.9 4.0 %collective-permute-start.33 = (bf16[176,128]{1,0:T(8,128)(2,1)S(1)}, bf16[176,128]{1,0:T(8,128)(2,1)S(1)}, u32[]{:S(2)}, u32[]{:S(2)}) collective-permute-start(bf16[176,128]{1,0:T(8,128)(2,1)S(1)} %shard_map.136.refs_3_.mine), channel_id=1, source_target_pairs={{0,3},{1,2},{2,1},{3,0},{4,7},{5,6},{6,5},{7,4},{8,11},{9,10},{10,... | collective-permute-start | bytes 135176 | tf_op jit(solution)/shard_map/ppermute | solution.py:96
  76.9 4.7 %collective-permute-start.32 = (bf16[176,128]{1,0:T(8,128)(2,1)S(1)}, bf16[176,128]{1,0:T(8,128)(2,1)S(1)}, u32[]{:S(2)}, u32[]{:S(2)}) collective-permute-start(bf16[176,128]{1,0:T(8,128)(2,1)S(1)} %shard_map.136.refs_3_.mine), channel_id=1, source_target_pairs={{0,2},{1,3},{2,0},{3,1},{4,6},{5,7},{6,4},{7,5},{8,10},{9,11},{10,... | collective-permute-start | bytes 135176 | tf_op jit(solution)/shard_map/ppermute | solution.py:96
  78.5 3.2 %collective-permute-start.31 = (bf16[176,128]{1,0:T(8,128)(2,1)S(1)}, bf16[176,128]{1,0:T(8,128)(2,1)S(1)}, u32[]{:S(2)}, u32[]{:S(2)}) collective-permute-start(bf16[176,128]{1,0:T(8,128)(2,1)S(1)} %shard_map.136.refs_3_.mine), channel_id=1, source_target_pairs={{0,1},{1,0},{2,3},{3,2},{4,5},{5,4},{6,7},{7,6},{8,9},{9,8},{10,11... | collective-permute-start | bytes 135176 | tf_op jit(solution)/shard_map/ppermute | solution.py:96
  82.2 4.5 %collective-permute-start.34 = (f32[64,128]{1,0:T(8,128)S(1)}, f32[64,128]{1,0:T(8,128)S(1)}, u32[]{:S(2)}, u32[]{:S(2)}) collective-permute-start(f32[64,128]{1,0:T(8,128)S(1)} %shard_map.138), channel_id=1, source_target_pairs={{0,4},{4,0},{8,12},{12,8},{1,5},{5,1},{9,13},{13,9},{2,6},{6,2},{1... | collective-permute-start | bytes 98312 | tf_op jit(solution)/shard_map/ppermute | solution.py:96

commit v12 on v11

--- a/solution.py
+++ b/solution.py
@@ -238,16 +238,14 @@
     near_ids, weights, mine = refs[:3]
     got = refs[3 : 3 + count]
     x, own = refs[3 + count : 5 + count]
-    parts, (sums, total, ids, sem) = refs[5 + count : -4], refs[-4:]
-    bring = pltpu.make_async_copy(near_ids, ids, sem)
-    bring.start()
+    parts, (sums, total) = refs[5 + count : -2], refs[-2:]
+    ids = near_ids[...]
     p, c = place()
     sums[...] = jnp.zeros_like(sums)
     for k in range(z.rows):
         ref = mine if k == 0 else away(got, "row", z.rows, p, k)
         z.add_blocks(sums, 0, p ^ k, ref[...].astype(F32)[0 : z.piece])
     x[...] = sums[...].astype(BF16)
-    bring.wait()
     multiply_forward(z, c, ids, weights, x, total, own, parts)
 
 
@@ -255,9 +253,8 @@
     near_ids, weights, kept, rates, gain, drive = refs[:6]
     got = refs[6 : 6 + count]
     new, act_pair, cur_pair, x, own = refs[6 + count : 11 + count]
-    parts, (sums, total, ids, sem) = refs[11 + count : -4], refs[-4:]
-    bring = pltpu.make_async_copy(near_ids, ids, sem)
-    bring.start()
+    parts, (sums, total) = refs[11 + count : -2], refs[-2:]
+    ids = near_ids[...]
     p, c = place()
     sums[...] = jnp.zeros_like(sums)
 
@@ -277,7 +274,6 @@
             cur_pair[at : at + z.piece] = current
         z.add_blocks(sums, 0, p ^ k, fresh)
     x[...] = sums[...].astype(BF16)
-    bring.wait()
     multiply_forward(z, c, ids, weights, x, total, own, parts)
 
 
@@ -332,13 +328,11 @@
     near_ids, weights, base, mine = refs[:4]
     got = refs[4 : 4 + count]
     d, own = refs[4 + count : 6 + count]
-    parts, (sums, total, ids, sem) = refs[6 + count : -4], refs[-4:]
-    bring = pltpu.make_async_copy(near_ids, ids, sem)
-    bring.start()
+    parts, (sums, total) = refs[6 + count : -2], refs[-2:]
+    ids = near_ids[...]
     p, c = place()
     gather_post(z, c, mine, got, sums, d)
     total[...] = jnp.zeros_like(total)
-    bring.wait()
     for s in range(z.slots):
         total[ids[0, z.slots + s]] += jnp.dot(d[ids[0, s]], weights[s], preferred_element_type=F32)
     pieces = [z.take_blocks(total, 0, p ^ k) for k in range(z.rows)]
@@ -538,7 +532,7 @@
     x, own, *parts = call(
         functools.partial(first_kernel, z, len(got)),
         [x_shape, *col_parts],
-        [pre_sums, post_sums, *held_ids],
+        [pre_sums, post_sums],
         [ids, turned, message, *got],
         flops=product_flops,
     )
@@ -572,7 +566,7 @@
         rates, act, cur, x, own, *parts = call(
             functools.partial(forward_kernel, z, t, len(got)),
             [shape(every), shape(pair), shape(pair), x_shape, *col_parts],
-            [pre_sums, post_sums, *held_ids],
+            [pre_sums, post_sums],
             [ids, turned, kept, rates, gain, drive, *got],
             flops=product_flops,
         )
@@ -598,7 +592,7 @@
         d, own, *parts = call(
             functools.partial(back_kernel, z, len(got)),
             [shape((2 * z.post, batch, BLOCK), BF16), shape(pair), *row_parts],
-            [post_sums, pre_sums, *held_ids],
+            [post_sums, pre_sums],
             [ids, weights, base, delta, *got],
             flops=product_flops,
         )

time: 87.6 us -> 85.3 us (0.974)
  Pallas kernels: 14.6 us -> 12.3 us
    pallas_call x17, Pallas kernels: 11.3 us -> 9.11 us  [call(): pl.pallas_call(body, out_shape=outs, in_specs=specs, out_specs=out_specs...]
where the time goes in v12:
time: 85.3 us; the launch traced here: 85.1 us
  starting transfers between devices  38.3 us (45%)
  waiting for transfers between devices  32.1 us (38%)
  Pallas kernels  12.3 us (14%)
    ppermute x35, starting transfers between devices, flip(): return lax.ppermute(x, axis, [(i, i ^ k) for i in range(count)])  38.3 us
    ppermute x35, waiting for transfers between devices, flip(): return lax.ppermute(x, axis, [(i, i ^ k) for i in range(count)])  32.1 us
    pallas_call x17, Pallas kernels, call(): pl.pallas_call(body, out_shape=outs, in_specs=specs, out_specs=out_specs...  9.11 us
    pallas_call x1, Pallas kernels, shards(): pl.pallas_call(functools.partial(grad_kernel, z, len(got), per_step), gri...  3.24 us
  transfers between devices with their start and end apart: 35, of which 28 were waited for; matrix products, arithmetic and copies ran while one was open for 0% of the time, Pallas kernels for 7%

profile of v12, /device:TPU:0, one launch (start us, length us, event | category | flops | bytes accessed | tf_op | source)
XLA Modules:
  0.0 85.1 jit_solution(10333597537789839912)
XLA Ops:
  0.7 0.6 copy-done.6
  1.6 5.1 %collective-permute-start.2 = (bf16[96,128]{1,0:T(8,128)(2,1)S(1)}, bf16[96,128]{1,0:T(8,128)(2,1)S(1)}, u32[]{:S(2)}, u32[]{:S(2)}) collective-permute-start(bf16[96,128]{1,0:T(8,128)(2,1)S(1)} %get-tuple-element.59.after.refs_2_.refs_0_.mine), channel_id=1, source_target_pairs={{0,12},{4,8},{8,4},{12,0},{1,13},{5,9},{9,5},{13,1},{2,14},{6,10},... | collective-permute-start | bytes 73736 | tf_op jit(solution)/shard_map/ppermute | solution.py:96
  6.7 0.6 collective-permute-start
  7.3 1.0 %shard_map.123.refs_1_ = bf16[64,128,128]{2,1,0:T(8,128)(2,1)S(1)} custom-call(bf16[96,128]{1,0:T(8,128)(2,1)S(1)} %get-tuple-element.59.after.refs_2_.refs_0_.mine, bf16[64,128,128]{2,1,0:T(8,128)(2,1)S(1)} %bitcast.6), custom_call_target="tpu_custom_call" | custom-call | bytes 4218880 | tf_op jit(solution)/shard_map/pallas_call | solution.py:78
  8.5 2.0 %collective-permute-done.1.refs_4_.refs_6_ = bf16[96,128]{1,0:T(8,128)(2,1)S(1)} collective-permute-done((bf16[96,128]{1,0:T(8,128)(2,1)S(1)}, bf16[96,128]{1,0:T(8,128)(2,1)S(1)}, u32[]{:S(2)}, u32[]{:S(2)}) %collective-permute-start.1) | collective-permute-done | bytes 24608 | tf_op jit(solution)/shard_map/ppermute | solution.py:96
  10.5 0.9 %collective-permute-done.refs_3_.refs_5_.partner = bf16[96,128]{1,0:T(8,128)(2,1)S(1)} collective-permute-done((bf16[96,128]{1,0:T(8,128)(2,1)S(1)}, bf16[96,128]{1,0:T(8,128)(2,1)S(1)}, u32[]{:S(2)}, u32[]{:S(2)}) %collective-permute-start) | collective-permute-done | bytes 24608 | tf_op jit(solution)/shard_map/ppermute | solution.py:96
  11.4 1.1 %shard_map.124 = (bf16[9,32,128]{2,1,0:T(8,128)(2,1)S(1)}, f32[144,128]{1,0:T(8,128)S(1)}, bf16[144,128]{1,0:T(8,128)(2,1)S(1)}, bf16[144,128]{1,0:T(8,128)(2,1)S(1)}, bf16[144,128]{1,0:T(8,128)(2,1)S(1)}) custom-call(s32[1,128]{1,0:T(1,128)S(1)} %get-tuple-element.58.refs_0_, bf16[64,128,128]{2,1,0:T(8,128)(2,1)S(1)} %shard_map.123.refs_1_, ...), custom_call_target="tpu_custom_call" | custom-call | flops 67108864 | bytes 2454016 | tf_op jit(solution)/shard_map/pallas_call | solution.py:78
  12.6 1.6 %collective-permute-start.4 = (bf16[144,128]{1,0:T(8,128)(2,1)S(1)}, bf16[144,128]{1,0:T(8,128)(2,1)S(1)}, u32[]{:S(2)}, u32[]{:S(2)}) collective-permute-start(bf16[144,128]{1,0:T(8,128)(2,1)S(1)} %get-tuple-element.63), channel_id=1, source_target_pairs={{0,2},{1,3},{2,0},{3,1},{4,6},{5,7},{6,4},{7,5},{8,10},{9,11},{10,... | collective-permute-start | bytes 110600 | tf_op jit(solution)/shard_map/ppermute | solution.py:96
  14.4 1.9 %collective-permute-done.3.refs_1_ = bf16[144,128]{1,0:T(8,128)(2,1)S(1)} collective-permute-done((bf16[144,128]{1,0:T(8,128)(2,1)S(1)}, bf16[144,128]{1,0:T(8,128)(2,1)S(1)}, u32[]{:S(2)}, u32[]{:S(2)}) %collective-permute-start.3) | collective-permute-done | bytes 36896 | tf_op jit(solution)/shard_map/ppermute | solution.py:96
  16.3 0.4 collective-permute-done.4.refs_2_
  16.7 1.7 %collective-permute-start.8 = (bf16[144,128]{1,0:T(8,128)(2,1)S(1)}, bf16[144,128]{1,0:T(8,128)(2,1)S(1)}, u32[]{:S(2)}, u32[]{:S(2)}) collective-permute-start(bf16[144,128]{1,0:T(8,128)(2,1)S(1)} %get-tuple-element.70), channel_id=1, source_target_pairs={{0,12},{4,8},{8,4},{12,0},{1,13},{5,9},{9,5},{13,1},{2,14},{6,10},... | collective-permute-start | bytes 110600 | tf_op jit(solution)/shard_map/ppermute | solution.py:96
  18.5 0.4 collective-permute-start.7
  18.9 2.3 %collective-permute-start.6 = (bf16[144,128]{1,0:T(8,128)(2,1)S(1)}, bf16[144,128]{1,0:T(8,128)(2,1)S(1)}, u32[]{:S(2)}, u32[]{:S(2)}) collective-permute-start(bf16[144,128]{1,0:T(8,128)(2,1)S(1)} %get-tuple-element.70), channel_id=1, source_target_pairs={{0,8},{4,12},{8,0},{12,4},{1,9},{5,13},{9,1},{13,5},{2,10},{6,14},... | collective-permute-start | bytes 110600 | tf_op jit(solution)/shard_map/ppermute | solution.py:96
  21.2 0.9 %shard_map.126 = (f32[288,128]{1,0:T(8,128)S(1)}, f32[288,128]{1,0:T(8,128)S(1)}, f32[3,288,128]{2,1,0:T(8,128)S(1)}, f32[3,72,128]{2,1,0:T(8,128)S(1)}) custom-call(bf16[96,128]{1,0:T(8,128)(2,1)S(1)} %get-tuple-element.59.after.refs_2_.refs_0_.mine, f32[72,128]{1,0:T(8,128)S(1)} %get-tuple-element.66.refs_1_, f32[3,32,288]{2,1,0:T(8,128)S(1)} %copy-done.1, ...), custom_call_target="tpu_custom_call" | custom-call | bytes 1224704 | tf_op jit(solution)/shard_map/pallas_call | solution.py:78
  22.1 0.8 collective-permute-done.8.refs_8_
  23.1 0.7 collective-permute-done.6.refs_6_
  23.8 1.1 %shard_map.127 = (f32[288,128]{1,0:T(8,128)S(1)}, f32[144,128]{1,0:T(8,128)S(1)}, f32[144,128]{1,0:T(8,128)S(1)}, bf16[9,32,128]{2,1,0:T(8,128)(2,1)S(1)}, f32[1...) custom-call(s32[1,128]{1,0:T(1,128)S(1)} %get-tuple-element.58.refs_, ...), custom_call_target="tpu_custom_call" | custom-call | flops 67108864 | bytes 3572224 | tf_op jit(solution)/shard_map/pallas_call | solution.py:78
  24.9 0.5 collective-permute-start.9
  25.4 1.0 %collective-permute-start.10 = (bf16[144,128]{1,0:T(8,128)(2,1)S(1)}, bf16[144,128]{1,0:T(8,128)(2,1)S(1)}, u32[]{:S(2)}, u32[]{:S(2)}) collective-permute-start(bf16[144,128]{1,0:T(8,128)(2,1)S(1)} %get-tuple-element.74), channel_id=1, source_target_pairs={{0,2},{1,3},{2,0},{3,1},{4,6},{5,7},{6,4},{7,5},{8,10},{9,11},{10,... | collective-permute-start | bytes 110600 | tf_op jit(solution)/shard_map/ppermute | solution.py:96
  26.5 0.4 collective-permute-start.11
  26.9 1.9 %collective-permute-done.9.refs_1_ = bf16[144,128]{1,0:T(8,128)(2,1)S(1)} collective-permute-done((bf16[144,128]{1,0:T(8,128)(2,1)S(1)}, bf16[144,128]{1,0:T(8,128)(2,1)S(1)}, u32[]{:S(2)}, u32[]{:S(2)}) %collective-permute-start.9) | collective-permute-done | bytes 36896 | tf_op jit(solution)/shard_map/ppermute | solution.py:96
  28.8 0.9 %collective-permute-done.10.refs_2_ = bf16[144,128]{1,0:T(8,128)(2,1)S(1)} collective-permute-done((bf16[144,128]{1,0:T(8,128)(2,1)S(1)}, bf16[144,128]{1,0:T(8,128)(2,1)S(1)}, u32[]{:S(2)}, u32[]{:S(2)}) %collective-permute-start.10) | collective-permute-done | bytes 36896 | tf_op jit(solution)/shard_map/ppermute | solution.py:96
  29.7 2.3 %collective-permute-start.14 = (bf16[144,128]{1,0:T(8,128)(2,1)S(1)}, bf16[144,128]{1,0:T(8,128)(2,1)S(1)}, u32[]{:S(2)}, u32[]{:S(2)}) collective-permute-start(bf16[144,128]{1,0:T(8,128)(2,1)S(1)} %get-tuple-element.78), channel_id=1, source_target_pairs={{0,12},{4,8},{8,4},{12,0},{1,13},{5,9},{9,5},{13,1},{2,14},{6,10},... | collective-permute-start | bytes 110600 | tf_op jit(solution)/shard_map/ppermute | solution.py:96
  32.1 2.1 %collective-permute-start.12 = (bf16[144,128]{1,0:T(8,128)(2,1)S(1)}, bf16[144,128]{1,0:T(8,128)(2,1)S(1)}, u32[]{:S(2)}, u32[]{:S(2)}) collective-permute-start(bf16[144,128]{1,0:T(8,128)(2,1)S(1)} %get-tuple-element.78), channel_id=1, source_target_pairs={{0,8},{4,12},{8,0},{12,4},{1,9},{5,13},{9,1},{13,5},{2,10},{6,14},... | collective-permute-start | bytes 110600 | tf_op jit(solution)/shard_map/ppermute | solution.py:96
  34.2 1.4 %collective-permute-done.14.refs_8_ = bf16[144,128]{1,0:T(8,128)(2,1)S(1)} collective-permute-done((bf16[144,128]{1,0:T(8,128)(2,1)S(1)}, bf16[144,128]{1,0:T(8,128)(2,1)S(1)}, u32[]{:S(2)}, u32[]{:S(2)}) %collective-permute-start.14) | collective-permute-done | bytes 36896 | tf_op jit(solution)/shard_map/ppermute | solution.py:96
  35.5 0.8 collective-permute-done.13.refs_7_
  36.3 1.0 %collective-permute-done.12.refs_6_ = bf16[144,128]{1,0:T(8,128)(2,1)S(1)} collective-permute-done((bf16[144,128]{1,0:T(8,128)(2,1)S(1)}, bf16[144,128]{1,0:T(8,128)(2,1)S(1)}, u32[]{:S(2)}, u32[]{:S(2)}) %collective-permute-start.12) | collective-permute-done | bytes 36896 | tf_op jit(solution)/shard_map/ppermute | solution.py:96
  37.3 1.1 %shard_map.129 = (f32[288,128]{1,0:T(8,128)S(1)}, f32[144,128]{1,0:T(8,128)S(1)}, f32[144,128]{1,0:T(8,128)S(1)}, bf16[9,32,128]{2,1,0:T(8,128)(2,1)S(1)}, f32[1...) custom-call(s32[1,128]{1,0:T(1,128)S(1)} %get-tuple-element.58.refs_, ...), custom_call_target="tpu_custom_call" | custom-call | flops 67108864 | bytes 3572224 | tf_op jit(solution)/shard_map/pallas_call | solution.py:78
  38.5 1.3 %collective-permute-start.16 = (bf16[144,128]{1,0:T(8,128)(2,1)S(1)}, bf16[144,128]{1,0:T(8,128)(2,1)S(1)}, u32[]{:S(2)}, u32[]{:S(2)}) collective-permute-start(bf16[144,128]{1,0:T(8,128)(2,1)S(1)} %get-tuple-element.82), channel_id=1, source_target_pairs={{0,2},{1,3},{2,0},{3,1},{4,6},{5,7},{6,4},{7,5},{8,10},{9,11},{10,... | collective-permute-start | bytes 110600 | tf_op jit(solution)/shard_map/ppermute | solution.py:96
  39.8 0.5 collective-permute-start.17
  40.3 1.7 %collective-permute-done.15.refs_1_ = bf16[144,128]{1,0:T(8,128)(2,1)S(1)} collective-permute-done((bf16[144,128]{1,0:T(8,128)(2,1)S(1)}, bf16[144,128]{1,0:T(8,128)(2,1)S(1)}, u32[]{:S(2)}, u32[]{:S(2)}) %collective-permute-start.15) | collective-permute-done | bytes 36896 | tf_op jit(solution)/shard_map/ppermute | solution.py:96
  42.1 0.5 collective-permute-done.16.refs_2_
  42.6 2.1 %collective-permute-start.18 = (bf16[224,128]{1,0:T(8,128)(2,1)S(1)}, bf16[224,128]{1,0:T(8,128)(2,1)S(1)}, u32[]{:S(2)}, u32[]{:S(2)}) collective-permute-start(bf16[224,128]{1,0:T(8,128)(2,1)S(1)} %get-tuple-element.86), channel_id=1, source_target_pairs={{0,8},{4,12},{8,0},{12,4},{1,9},{5,13},{9,1},{13,5},{2,10},{6,14},... | collective-permute-start | bytes 172040 | tf_op jit(solution)/shard_map/ppermute | solution.py:96
  44.7 4.3 %collective-permute-done.18.theirs = bf16[224,128]{1,0:T(8,128)(2,1)S(1)} collective-permute-done((bf16[224,128]{1,0:T(8,128)(2,1)S(1)}, bf16[224,128]{1,0:T(8,128)(2,1)S(1)}, u32[]{:S(2)}, u32[]{:S(2)}) %collective-permute-start.18) | collective-permute-done | bytes 57376 | tf_op jit(solution)/shard_map/ppermute | solution.py:96
  49.1 1.5 %collective-permute-start.20 = (bf16[144,128]{1,0:T(8,128)(2,1)S(1)}, bf16[144,128]{1,0:T(8,128)(2,1)S(1)}, u32[]{:S(2)}, u32[]{:S(2)}) collective-permute-start(bf16[144,128]{1,0:T(8,128)(2,1)S(1)} %get-tuple-element.89.refs_3_), channel_id=1, source_target_pairs={{0,2},{1,3},{2,0},{3,1},{4,6},{5,7},{6,4},{7,5},{8,10},{9,11},{10,... | collective-permute-start | bytes 110600 | tf_op jit(solution)/shard_map/ppermute | solution.py:96
  50.6 0.3 collective-permute-start.19
  51.0 1.9 %collective-permute-done.21.refs_6_ = bf16[144,128]{1,0:T(8,128)(2,1)S(1)} collective-permute-done((bf16[144,128]{1,0:T(8,128)(2,1)S(1)}, bf16[144,128]{1,0:T(8,128)(2,1)S(1)}, u32[]{:S(2)}, u32[]{:S(2)}) %collective-permute-start.21) | collective-permute-done | bytes 36896 | tf_op jit(solution)/shard_map/ppermute | solution.py:96
  52.9 0.4 collective-permute-done.20.refs_5_
  53.3 1.1 %shard_map.132 = (bf16[18,32,128]{2,1,0:T(8,128)(2,1)S(1)}, f32[144,128]{1,0:T(8,128)S(1)}, bf16[144,128]{1,0:T(8,128)(2,1)S(1)}, bf16[144,128]{1,0:T(8,128)(2,1)S(1)}, bf16[144,128]{1,0:T(8,128)(2,1)S(1)}) custom-call(s32[1,128]{1,0:T(1,128)S(1)} %get-tuple-element.58.refs_0_, bf16[64,128,128]{2,1,0:T(8,128)(2,1)S(1)} %bitcast.7, ...), custom_call_target="tpu_custom_call" | custom-call | flops 67108864 | bytes 2613760 | tf_op jit(solution)/shard_map/pallas_call | solution.py:78
  54.3 2.0 %collective-permute-start.22 = (bf16[144,128]{1,0:T(8,128)(2,1)S(1)}, bf16[144,128]{1,0:T(8,128)(2,1)S(1)}, u32[]{:S(2)}, u32[]{:S(2)}) collective-permute-start(bf16[144,128]{1,0:T(8,128)(2,1)S(1)} %get-tuple-element.95), channel_id=1, source_target_pairs={{0,12},{4,8},{8,4},{12,0},{1,13},{5,9},{9,5},{13,1},{2,14},{6,10},... | collective-permute-start | bytes 110600 | tf_op jit(solution)/shard_map/ppermute | solution.py:96
  56.3 2.5 %collective-permute-start.24 = (bf16[144,128]{1,0:T(8,128)(2,1)S(1)}, bf16[144,128]{1,0:T(8,128)(2,1)S(1)}, u32[]{:S(2)}, u32[]{:S(2)}) collective-permute-start(bf16[144,128]{1,0:T(8,128)(2,1)S(1)} %get-tuple-element.97), channel_id=1, source_target_pairs={{0,8},{4,12},{8,0},{12,4},{1,9},{5,13},{9,1},{13,5},{2,10},{6,14},... | collective-permute-start | bytes 110600 | tf_op jit(solution)/shard_map/ppermute | solution.py:96
  58.8 1.5 %collective-permute-done.22.refs_0_ = bf16[144,128]{1,0:T(8,128)(2,1)S(1)} collective-permute-done((bf16[144,128]{1,0:T(8,128)(2,1)S(1)}, bf16[144,128]{1,0:T(8,128)(2,1)S(1)}, u32[]{:S(2)}, u32[]{:S(2)}) %collective-permute-start.22) | collective-permute-done | bytes 36896 | tf_op jit(solution)/shard_map/ppermute | solution.py:96
  60.3 0.6 collective-permute-done.23.refs_1_
  60.9 0.6 collective-permute-done.24.refs_2_
  61.7 1.2 %collective-permute-start.26 = (bf16[144,128]{1,0:T(8,128)(2,1)S(1)}, bf16[144,128]{1,0:T(8,128)(2,1)S(1)}, u32[]{:S(2)}, u32[]{:S(2)}) collective-permute-start(bf16[144,128]{1,0:T(8,128)(2,1)S(1)} %get-tuple-element.99.refs_3_), channel_id=1, source_target_pairs={{0,2},{1,3},{2,0},{3,1},{4,6},{5,7},{6,4},{7,5},{8,10},{9,11},{10,... | collective-permute-start | bytes 110600 | tf_op jit(solution)/shard_map/ppermute | solution.py:96
  62.9 0.6 collective-permute-start.25
  63.5 1.6 %collective-permute-done.27.refs_6_ = bf16[144,128]{1,0:T(8,128)(2,1)S(1)} collective-permute-done((bf16[144,128]{1,0:T(8,128)(2,1)S(1)}, bf16[144,128]{1,0:T(8,128)(2,1)S(1)}, u32[]{:S(2)}, u32[]{:S(2)}) %collective-permute-start.27) | collective-permute-done | bytes 36896 | tf_op jit(solution)/shard_map/ppermute | solution.py:96
  65.1 0.7 collective-permute-done.26.refs_5_
  65.9 1.1 %shard_map.134 = (bf16[18,32,128]{2,1,0:T(8,128)(2,1)S(1)}, f32[144,128]{1,0:T(8,128)S(1)}, bf16[144,128]{1,0:T(8,128)(2,1)S(1)}, bf16[144,128]{1,0:T(8,128)(2,1)S(1)}, bf16[144,128]{1,0:T(8,128)(2,1)S(1)}) custom-call(s32[1,128]{1,0:T(1,128)S(1)} %get-tuple-element.58.refs_0_, bf16[64,128,128]{2,1,0:T(8,128)(2,1)S(1)} %bitcast.8, ...), custom_call_target="tpu_custom_call" | custom-call | flops 67108864 | bytes 2613760 | tf_op jit(solution)/shard_map/pallas_call | solution.py:78
  67.0 1.9 %collective-permute-start.28 = (bf16[144,128]{1,0:T(8,128)(2,1)S(1)}, bf16[144,128]{1,0:T(8,128)(2,1)S(1)}, u32[]{:S(2)}, u32[]{:S(2)}) collective-permute-start(bf16[144,128]{1,0:T(8,128)(2,1)S(1)} %get-tuple-element.110), channel_id=1, source_target_pairs={{0,12},{4,8},{8,4},{12,0},{1,13},{5,9},{9,5},{13,1},{2,14},{6,10},... | collective-permute-start | bytes 110600 | tf_op jit(solution)/shard_map/ppermute | solution.py:96
  68.8 0.8 collective-permute-start.29
  69.6 1.8 %collective-permute-start.30 = (bf16[144,128]{1,0:T(8,128)(2,1)S(1)}, bf16[144,128]{1,0:T(8,128)(2,1)S(1)}, u32[]{:S(2)}, u32[]{:S(2)}) collective-permute-start(bf16[144,128]{1,0:T(8,128)(2,1)S(1)} %get-tuple-element.112), channel_id=1, source_target_pairs={{0,8},{4,12},{8,0},{12,4},{1,9},{5,13},{9,1},{13,5},{2,10},{6,14},... | collective-permute-start | bytes 110600 | tf_op jit(solution)/shard_map/ppermute | solution.py:96
  71.4 1.4 %collective-permute-done.28.refs_0_ = bf16[144,128]{1,0:T(8,128)(2,1)S(1)} collective-permute-done((bf16[144,128]{1,0:T(8,128)(2,1)S(1)}, bf16[144,128]{1,0:T(8,128)(2,1)S(1)}, u32[]{:S(2)}, u32[]{:S(2)}) %collective-permute-start.28) | collective-permute-done | bytes 36896 | tf_op jit(solution)/shard_map/ppermute | solution.py:96
  72.8 0.8 collective-permute-done.29.refs_1_
  73.6 0.9 %collective-permute-done.30.refs_2_ = bf16[144,128]{1,0:T(8,128)(2,1)S(1)} collective-permute-done((bf16[144,128]{1,0:T(8,128)(2,1)S(1)}, bf16[144,128]{1,0:T(8,128)(2,1)S(1)}, u32[]{:S(2)}, u32[]{:S(2)}) %collective-permute-start.30) | collective-permute-done | bytes 36896 | tf_op jit(solution)/shard_map/ppermute | solution.py:96
  74.7 1.5 %collective-permute-start.32 = (bf16[176,128]{1,0:T(8,128)(2,1)S(1)}, bf16[176,128]{1,0:T(8,128)(2,1)S(1)}, u32[]{:S(2)}, u32[]{:S(2)}) collective-permute-start(bf16[176,128]{1,0:T(8,128)(2,1)S(1)} %shard_map.136.refs_3_.mine), channel_id=1, source_target_pairs={{0,2},{1,3},{2,0},{3,1},{4,6},{5,7},{6,4},{7,5},{8,10},{9,11},{10,... | collective-permute-start | bytes 135176 | tf_op jit(solution)/shard_map/ppermute | solution.py:96
  76.2 0.3 collective-permute-start.31
  76.5 0.8 shard_map.135
  77.4 1.3 %collective-permute-done.33.refs_6_.refs_2_ = bf16[176,128]{1,0:T(8,128)(2,1)S(1)} collective-permute-done((bf16[176,128]{1,0:T(8,128)(2,1)S(1)}, bf16[176,128]{1,0:T(8,128)(2,1)S(1)}, u32[]{:S(2)}, u32[]{:S(2)}) %collective-permute-start.33) | collective-permute-done | bytes 45088 | tf_op jit(solution)/shard_map/ppermute | solution.py:96
  78.6 0.7 collective-permute-done.32.refs_5_.refs_1_
  79.4 0.6 shard_map.138
  80.0 1.2 %collective-permute-start.34 = (f32[64,128]{1,0:T(8,128)S(1)}, f32[64,128]{1,0:T(8,128)S(1)}, u32[]{:S(2)}, u32[]{:S(2)}) collective-permute-start(f32[64,128]{1,0:T(8,128)S(1)} %shard_map.138), channel_id=1, source_target_pairs={{0,4},{4,0},{8,12},{12,8},{1,5},{5,1},{9,13},{13,9},{2,6},{6,2},{1... | collective-permute-start | bytes 98312 | tf_op jit(solution)/shard_map/ppermute | solution.py:96
  81.2 3.2 %shard_map.137 = bf16[64,128,128]{2,1,0:T(8,128)(2,1)} custom-call(s32[1,128]{1,0:T(1,128)S(1)} %get-tuple-element.58.refs_0_, bf16[9,128,128]{2,1,0:T(8,128)(2,1)S(1)} %get-tuple-element.104.refs_1_.right, bf16[18,128,128]{2,1,0:T(8,128)(2,1)S(1)} %get-tuple-element.105.refs_2_, bf16[176,128]{1,0:T(8,128)(2,1)S(1)} %shard_map.136.refs_3_.mine, ...), custom_call_target="tpu_custom_call" | custom-call | flops 268435456 | bytes 4194304 | tf_op jit(solution)/shard_map/pallas_call | solution.py:643
  84.5 0.6 add_bitcast_fusion
  (45 shorter events, 1.6 us)
Async XLA Ops:
  0.6 0.7 copy-start.6
  0.6 0.7 copy-start.5
  0.7 0.7 copy-start.9
  0.7 0.7 copy-start.8
  0.7 0.7 copy-start.7
  0.7 0.8 copy-start.3
  0.7 6.6 %copy-start = (bf16[1,1,64,128,128]{4,3,2,1,0:T(8,128)(2,1)S(1)}, bf16[1,1,64,128,128]{4,3,2,1,0:T(8,128)(2,1)}, u32[]{:S(2)}) copy-start(bf16[1,1,64,128,128]{4,3,2,1,0:T(8,128)(2,1)} %param.13) | copy-start | bytes 6291460
  1.6 6.9 %collective-permute-start.2 = (bf16[96,128]{1,0:T(8,128)(2,1)S(1)}, bf16[96,128]{1,0:T(8,128)(2,1)S(1)}, u32[]{:S(2)}, u32[]{:S(2)}) collective-permute-start(bf16[96,128]{1,0:T(8,128)(2,1)S(1)} %get-tuple-element.59.after.refs_2_.refs_0_.mine), channel_id=1, source_target_pairs={{0,12},{4,8},{8,4},{12,0},{1,13},{5,9},{9,5},{13,1},{2,14},{6,10},... | collective-permute-start | bytes 73736 | tf_op jit(solution)/shard_map/ppermute | solution.py:96
  6.6 3.8 %collective-permute-start.1 = (bf16[96,128]{1,0:T(8,128)(2,1)S(1)}, bf16[96,128]{1,0:T(8,128)(2,1)S(1)}, u32[]{:S(2)}, u32[]{:S(2)}) collective-permute-start(bf16[96,128]{1,0:T(8,128)(2,1)S(1)} %get-tuple-element.59.after.refs_2_.refs_0_.mine), channel_id=1, source_target_pairs={{0,4},{4,0},{8,12},{12,8},{1,5},{5,1},{9,13},{13,9},{2,6},{6,2},{1... | collective-permute-start | bytes 73736 | tf_op jit(solution)/shard_map/ppermute | solution.py:96
  6.7 4.8 %collective-permute-start = (bf16[96,128]{1,0:T(8,128)(2,1)S(1)}, bf16[96,128]{1,0:T(8,128)(2,1)S(1)}, u32[]{:S(2)}, u32[]{:S(2)}) collective-permute-start(bf16[96,128]{1,0:T(8,128)(2,1)S(1)} %get-tuple-element.59.after.refs_2_.refs_0_.mine), channel_id=1, source_target_pairs={{0,8},{4,12},{8,0},{12,4},{1,9},{5,13},{9,1},{13,5},{2,10},{6,14},... | collective-permute-start | bytes 73736 | tf_op jit(solution)/shard_map/ppermute | solution.py:96
  8.3 12.9 %copy-start.1 = (f32[3,32,288]{2,1,0:T(8,128)S(1)}, f32[3,32,288]{2,1,0:T(8,128)}, u32[]{:S(2)}) copy-start(f32[3,32,288]{2,1,0:T(8,128)} %refs_2_.1) | copy-start | bytes 331780
  8.3 12.9 %copy-start.2 = (bf16[3,32,512]{2,1,0:T(8,128)(2,1)S(1)}, bf16[3,32,512]{2,1,0:T(8,128)(2,1)}, u32[]{:S(2)}) copy-start(bf16[3,32,512]{2,1,0:T(8,128)(2,1)} %param.11) | copy-start | bytes 294916
  8.3 12.9 %copy-start.4 = (f32[8192]{0:T(1024)S(1)}, f32[8192]{0:T(1024)}, u32[]{:S(2)}) copy-start(f32[8192]{0:T(1024)} %param.18) | copy-start | bytes 98308
  12.5 3.8 %collective-permute-start.3 = (bf16[144,128]{1,0:T(8,128)(2,1)S(1)}, bf16[144,128]{1,0:T(8,128)(2,1)S(1)}, u32[]{:S(2)}, u32[]{:S(2)}) collective-permute-start(bf16[144,128]{1,0:T(8,128)(2,1)S(1)} %get-tuple-element.62), channel_id=1, source_target_pairs={{0,3},{1,2},{2,1},{3,0},{4,7},{5,6},{6,5},{7,4},{8,11},{9,10},{10,... | collective-permute-start | bytes 110600 | tf_op jit(solution)/shard_map/ppermute | solution.py:96
  12.6 4.2 %collective-permute-start.4 = (bf16[144,128]{1,0:T(8,128)(2,1)S(1)}, bf16[144,128]{1,0:T(8,128)(2,1)S(1)}, u32[]{:S(2)}, u32[]{:S(2)}) collective-permute-start(bf16[144,128]{1,0:T(8,128)(2,1)S(1)} %get-tuple-element.63), channel_id=1, source_target_pairs={{0,2},{1,3},{2,0},{3,1},{4,6},{5,7},{6,4},{7,5},{8,10},{9,11},{10,... | collective-permute-start | bytes 110600 | tf_op jit(solution)/shard_map/ppermute | solution.py:96
  14.1 2.6 %collective-permute-start.5 = (bf16[144,128]{1,0:T(8,128)(2,1)S(1)}, bf16[144,128]{1,0:T(8,128)(2,1)S(1)}, u32[]{:S(2)}, u32[]{:S(2)}) collective-permute-start(bf16[144,128]{1,0:T(8,128)(2,1)S(1)} %get-tuple-element.64), channel_id=1, source_target_pairs={{0,1},{1,0},{2,3},{3,2},{4,5},{5,4},{6,7},{7,6},{8,9},{9,8},{10,11... | collective-permute-start | bytes 110600 | tf_op jit(solution)/shard_map/ppermute | solution.py:96
  16.7 6.2 %collective-permute-start.8 = (bf16[144,128]{1,0:T(8,128)(2,1)S(1)}, bf16[144,128]{1,0:T(8,128)(2,1)S(1)}, u32[]{:S(2)}, u32[]{:S(2)}) collective-permute-start(bf16[144,128]{1,0:T(8,128)(2,1)S(1)} %get-tuple-element.70), channel_id=1, source_target_pairs={{0,12},{4,8},{8,4},{12,0},{1,13},{5,9},{9,5},{13,1},{2,14},{6,10},... | collective-permute-start | bytes 110600 | tf_op jit(solution)/shard_map/ppermute | solution.py:96
  18.5 4.7 %collective-permute-start.7 = (bf16[144,128]{1,0:T(8,128)(2,1)S(1)}, bf16[144,128]{1,0:T(8,128)(2,1)S(1)}, u32[]{:S(2)}, u32[]{:S(2)}) collective-permute-start(bf16[144,128]{1,0:T(8,128)(2,1)S(1)} %get-tuple-element.70), channel_id=1, source_target_pairs={{0,4},{4,0},{8,12},{12,8},{1,5},{5,1},{9,13},{13,9},{2,6},{6,2},{1... | collective-permute-start | bytes 110600 | tf_op jit(solution)/shard_map/ppermute | solution.py:96
  18.9 5.0 %collective-permute-start.6 = (bf16[144,128]{1,0:T(8,128)(2,1)S(1)}, bf16[144,128]{1,0:T(8,128)(2,1)S(1)}, u32[]{:S(2)}, u32[]{:S(2)}) collective-permute-start(bf16[144,128]{1,0:T(8,128)(2,1)S(1)} %get-tuple-element.70), channel_id=1, source_target_pairs={{0,8},{4,12},{8,0},{12,4},{1,9},{5,13},{9,1},{13,5},{2,10},{6,14},... | collective-permute-start | bytes 110600 | tf_op jit(solution)/shard_map/ppermute | solution.py:96
  24.9 3.8 %collective-permute-start.9 = (bf16[144,128]{1,0:T(8,128)(2,1)S(1)}, bf16[144,128]{1,0:T(8,128)(2,1)S(1)}, u32[]{:S(2)}, u32[]{:S(2)}) collective-permute-start(bf16[144,128]{1,0:T(8,128)(2,1)S(1)} %get-tuple-element.73), channel_id=1, source_target_pairs={{0,3},{1,2},{2,1},{3,0},{4,7},{5,6},{6,5},{7,4},{8,11},{9,10},{10,... | collective-permute-start | bytes 110600 | tf_op jit(solution)/shard_map/ppermute | solution.py:96
  25.4 4.2 %collective-permute-start.10 = (bf16[144,128]{1,0:T(8,128)(2,1)S(1)}, bf16[144,128]{1,0:T(8,128)(2,1)S(1)}, u32[]{:S(2)}, u32[]{:S(2)}) collective-permute-start(bf16[144,128]{1,0:T(8,128)(2,1)S(1)} %get-tuple-element.74), channel_id=1, source_target_pairs={{0,2},{1,3},{2,0},{3,1},{4,6},{5,7},{6,4},{7,5},{8,10},{9,11},{10,... | collective-permute-start | bytes 110600 | tf_op jit(solution)/shard_map/ppermute | solution.py:96
  26.5 3.2 %collective-permute-start.11 = (bf16[144,128]{1,0:T(8,128)(2,1)S(1)}, bf16[144,128]{1,0:T(8,128)(2,1)S(1)}, u32[]{:S(2)}, u32[]{:S(2)}) collective-permute-start(bf16[144,128]{1,0:T(8,128)(2,1)S(1)} %get-tuple-element.75), channel_id=1, source_target_pairs={{0,1},{1,0},{2,3},{3,2},{4,5},{5,4},{6,7},{7,6},{8,9},{9,8},{10,11... | collective-permute-start | bytes 110600 | tf_op jit(solution)/shard_map/ppermute | solution.py:96
  29.7 5.8 %collective-permute-start.14 = (bf16[144,128]{1,0:T(8,128)(2,1)S(1)}, bf16[144,128]{1,0:T(8,128)(2,1)S(1)}, u32[]{:S(2)}, u32[]{:S(2)}) collective-permute-start(bf16[144,128]{1,0:T(8,128)(2,1)S(1)} %get-tuple-element.78), channel_id=1, source_target_pairs={{0,12},{4,8},{8,4},{12,0},{1,13},{5,9},{9,5},{13,1},{2,14},{6,10},... | collective-permute-start | bytes 110600 | tf_op jit(solution)/shard_map/ppermute | solution.py:96
  32.0 4.3 %collective-permute-start.13 = (bf16[144,128]{1,0:T(8,128)(2,1)S(1)}, bf16[144,128]{1,0:T(8,128)(2,1)S(1)}, u32[]{:S(2)}, u32[]{:S(2)}) collective-permute-start(bf16[144,128]{1,0:T(8,128)(2,1)S(1)} %get-tuple-element.78), channel_id=1, source_target_pairs={{0,4},{4,0},{8,12},{12,8},{1,5},{5,1},{9,13},{13,9},{2,6},{6,2},{1... | collective-permute-start | bytes 110600 | tf_op jit(solution)/shard_map/ppermute | solution.py:96
  32.1 5.3 %collective-permute-start.12 = (bf16[144,128]{1,0:T(8,128)(2,1)S(1)}, bf16[144,128]{1,0:T(8,128)(2,1)S(1)}, u32[]{:S(2)}, u32[]{:S(2)}) collective-permute-start(bf16[144,128]{1,0:T(8,128)(2,1)S(1)} %get-tuple-element.78), channel_id=1, source_target_pairs={{0,8},{4,12},{8,0},{12,4},{1,9},{5,13},{9,1},{13,5},{2,10},{6,14},... | collective-permute-start | bytes 110600 | tf_op jit(solution)/shard_map/ppermute | solution.py:96
  38.4 3.7 %collective-permute-start.15 = (bf16[144,128]{1,0:T(8,128)(2,1)S(1)}, bf16[144,128]{1,0:T(8,128)(2,1)S(1)}, u32[]{:S(2)}, u32[]{:S(2)}) collective-permute-start(bf16[144,128]{1,0:T(8,128)(2,1)S(1)} %get-tuple-element.81), channel_id=1, source_target_pairs={{0,3},{1,2},{2,1},{3,0},{4,7},{5,6},{6,5},{7,4},{8,11},{9,10},{10,... | collective-permute-start | bytes 110600 | tf_op jit(solution)/shard_map/ppermute | solution.py:96
  38.5 4.1 %collective-permute-start.16 = (bf16[144,128]{1,0:T(8,128)(2,1)S(1)}, bf16[144,128]{1,0:T(8,128)(2,1)S(1)}, u32[]{:S(2)}, u32[]{:S(2)}) collective-permute-start(bf16[144,128]{1,0:T(8,128)(2,1)S(1)} %get-tuple-element.82), channel_id=1, source_target_pairs={{0,2},{1,3},{2,0},{3,1},{4,6},{5,7},{6,4},{7,5},{8,10},{9,11},{10,... | collective-permute-start | bytes 110600 | tf_op jit(solution)/shard_map/ppermute | solution.py:96
  39.8 2.7 %collective-permute-start.17 = (bf16[144,128]{1,0:T(8,128)(2,1)S(1)}, bf16[144,128]{1,0:T(8,128)(2,1)S(1)}, u32[]{:S(2)}, u32[]{:S(2)}) collective-permute-start(bf16[144,128]{1,0:T(8,128)(2,1)S(1)} %get-tuple-element.83), channel_id=1, source_target_pairs={{0,1},{1,0},{2,3},{3,2},{4,5},{5,4},{6,7},{7,6},{8,9},{9,8},{10,11... | collective-permute-start | bytes 110600 | tf_op jit(solution)/shard_map/ppermute | solution.py:96
  42.6 6.4 %collective-permute-start.18 = (bf16[224,128]{1,0:T(8,128)(2,1)S(1)}, bf16[224,128]{1,0:T(8,128)(2,1)S(1)}, u32[]{:S(2)}, u32[]{:S(2)}) collective-permute-start(bf16[224,128]{1,0:T(8,128)(2,1)S(1)} %get-tuple-element.86), channel_id=1, source_target_pairs={{0,8},{4,12},{8,0},{12,4},{1,9},{5,13},{9,1},{13,5},{2,10},{6,14},... | collective-permute-start | bytes 172040 | tf_op jit(solution)/shard_map/ppermute | solution.py:96
  49.0 3.8 %collective-permute-start.21 = (bf16[144,128]{1,0:T(8,128)(2,1)S(1)}, bf16[144,128]{1,0:T(8,128)(2,1)S(1)}, u32[]{:S(2)}, u32[]{:S(2)}) collective-permute-start(bf16[144,128]{1,0:T(8,128)(2,1)S(1)} %get-tuple-element.89.refs_3_), channel_id=1, source_target_pairs={{0,3},{1,2},{2,1},{3,0},{4,7},{5,6},{6,5},{7,4},{8,11},{9,10},{10,... | collective-permute-start | bytes 110600 | tf_op jit(solution)/shard_map/ppermute | solution.py:96
  49.1 4.1 %collective-permute-start.20 = (bf16[144,128]{1,0:T(8,128)(2,1)S(1)}, bf16[144,128]{1,0:T(8,128)(2,1)S(1)}, u32[]{:S(2)}, u32[]{:S(2)}) collective-permute-start(bf16[144,128]{1,0:T(8,128)(2,1)S(1)} %get-tuple-element.89.refs_3_), channel_id=1, source_target_pairs={{0,2},{1,3},{2,0},{3,1},{4,6},{5,7},{6,4},{7,5},{8,10},{9,11},{10,... | collective-permute-start | bytes 110600 | tf_op jit(solution)/shard_map/ppermute | solution.py:96
  50.6 2.7 %collective-permute-start.19 = (bf16[144,128]{1,0:T(8,128)(2,1)S(1)}, bf16[144,128]{1,0:T(8,128)(2,1)S(1)}, u32[]{:S(2)}, u32[]{:S(2)}) collective-permute-start(bf16[144,128]{1,0:T(8,128)(2,1)S(1)} %get-tuple-element.89.refs_3_), channel_id=1, source_target_pairs={{0,1},{1,0},{2,3},{3,2},{4,5},{5,4},{6,7},{7,6},{8,9},{9,8},{10,11... | collective-permute-start | bytes 110600 | tf_op jit(solution)/shard_map/ppermute | solution.py:96
  54.3 6.0 %collective-permute-start.22 = (bf16[144,128]{1,0:T(8,128)(2,1)S(1)}, bf16[144,128]{1,0:T(8,128)(2,1)S(1)}, u32[]{:S(2)}, u32[]{:S(2)}) collective-permute-start(bf16[144,128]{1,0:T(8,128)(2,1)S(1)} %get-tuple-element.95), channel_id=1, source_target_pairs={{0,12},{4,8},{8,4},{12,0},{1,13},{5,9},{9,5},{13,1},{2,14},{6,10},... | collective-permute-start | bytes 110600 | tf_op jit(solution)/shard_map/ppermute | solution.py:96
  56.3 4.7 %collective-permute-start.23 = (bf16[144,128]{1,0:T(8,128)(2,1)S(1)}, bf16[144,128]{1,0:T(8,128)(2,1)S(1)}, u32[]{:S(2)}, u32[]{:S(2)}) collective-permute-start(bf16[144,128]{1,0:T(8,128)(2,1)S(1)} %get-tuple-element.96), channel_id=1, source_target_pairs={{0,4},{4,0},{8,12},{12,8},{1,5},{5,1},{9,13},{13,9},{2,6},{6,2},{1... | collective-permute-start | bytes 110600 | tf_op jit(solution)/shard_map/ppermute | solution.py:96
  56.3 5.3 %collective-permute-start.24 = (bf16[144,128]{1,0:T(8,128)(2,1)S(1)}, bf16[144,128]{1,0:T(8,128)(2,1)S(1)}, u32[]{:S(2)}, u32[]{:S(2)}) collective-permute-start(bf16[144,128]{1,0:T(8,128)(2,1)S(1)} %get-tuple-element.97), channel_id=1, source_target_pairs={{0,8},{4,12},{8,0},{12,4},{1,9},{5,13},{9,1},{13,5},{2,10},{6,14},... | collective-permute-start | bytes 110600 | tf_op jit(solution)/shard_map/ppermute | solution.py:96
  61.6 3.5 %collective-permute-start.27 = (bf16[144,128]{1,0:T(8,128)(2,1)S(1)}, bf16[144,128]{1,0:T(8,128)(2,1)S(1)}, u32[]{:S(2)}, u32[]{:S(2)}) collective-permute-start(bf16[144,128]{1,0:T(8,128)(2,1)S(1)} %get-tuple-element.99.refs_3_), channel_id=1, source_target_pairs={{0,3},{1,2},{2,1},{3,0},{4,7},{5,6},{6,5},{7,4},{8,11},{9,10},{10,... | collective-permute-start | bytes 110600 | tf_op jit(solution)/shard_map/ppermute | solution.py:96
  61.7 4.2 %collective-permute-start.26 = (bf16[144,128]{1,0:T(8,128)(2,1)S(1)}, bf16[144,128]{1,0:T(8,128)(2,1)S(1)}, u32[]{:S(2)}, u32[]{:S(2)}) collective-permute-start(bf16[144,128]{1,0:T(8,128)(2,1)S(1)} %get-tuple-element.99.refs_3_), channel_id=1, source_target_pairs={{0,2},{1,3},{2,0},{3,1},{4,6},{5,7},{6,4},{7,5},{8,10},{9,11},{10,... | collective-permute-start | bytes 110600 | tf_op jit(solution)/shard_map/ppermute | solution.py:96
  62.9 3.0 %collective-permute-start.25 = (bf16[144,128]{1,0:T(8,128)(2,1)S(1)}, bf16[144,128]{1,0:T(8,128)(2,1)S(1)}, u32[]{:S(2)}, u32[]{:S(2)}) collective-permute-start(bf16[144,128]{1,0:T(8,128)(2,1)S(1)} %get-tuple-element.99.refs_3_), channel_id=1, source_target_pairs={{0,1},{1,0},{2,3},{3,2},{4,5},{5,4},{6,7},{7,6},{8,9},{9,8},{10,11... | collective-permute-start | bytes 110600 | tf_op jit(solution)/shard_map/ppermute | solution.py:96
  67.0 5.9 %collective-permute-start.28 = (bf16[144,128]{1,0:T(8,128)(2,1)S(1)}, bf16[144,128]{1,0:T(8,128)(2,1)S(1)}, u32[]{:S(2)}, u32[]{:S(2)}) collective-permute-start(bf16[144,128]{1,0:T(8,128)(2,1)S(1)} %get-tuple-element.110), channel_id=1, source_target_pairs={{0,12},{4,8},{8,4},{12,0},{1,13},{5,9},{9,5},{13,1},{2,14},{6,10},... | collective-permute-start | bytes 110600 | tf_op jit(solution)/shard_map/ppermute | solution.py:96
  68.8 4.7 %collective-permute-start.29 = (bf16[144,128]{1,0:T(8,128)(2,1)S(1)}, bf16[144,128]{1,0:T(8,128)(2,1)S(1)}, u32[]{:S(2)}, u32[]{:S(2)}) collective-permute-start(bf16[144,128]{1,0:T(8,128)(2,1)S(1)} %get-tuple-element.111), channel_id=1, source_target_pairs={{0,4},{4,0},{8,12},{12,8},{1,5},{5,1},{9,13},{13,9},{2,6},{6,2},{1... | collective-permute-start | bytes 110600 | tf_op jit(solution)/shard_map/ppermute | solution.py:96
  69.6 4.9 %collective-permute-start.30 = (bf16[144,128]{1,0:T(8,128)(2,1)S(1)}, bf16[144,128]{1,0:T(8,128)(2,1)S(1)}, u32[]{:S(2)}, u32[]{:S(2)}) collective-permute-start(bf16[144,128]{1,0:T(8,128)(2,1)S(1)} %get-tuple-element.112), channel_id=1, source_target_pairs={{0,8},{4,12},{8,0},{12,4},{1,9},{5,13},{9,1},{13,5},{2,10},{6,14},... | collective-permute-start | bytes 110600 | tf_op jit(solution)/shard_map/ppermute | solution.py:96
  74.6 4.0 %collective-permute-start.33 = (bf16[176,128]{1,0:T(8,128)(2,1)S(1)}, bf16[176,128]{1,0:T(8,128)(2,1)S(1)}, u32[]{:S(2)}, u32[]{:S(2)}) collective-permute-start(bf16[176,128]{1,0:T(8,128)(2,1)S(1)} %shard_map.136.refs_3_.mine), channel_id=1, source_target_pairs={{0,3},{1,2},{2,1},{3,0},{4,7},{5,6},{6,5},{7,4},{8,11},{9,10},{10,... | collective-permute-start | bytes 135176 | tf_op jit(solution)/shard_map/ppermute | solution.py:96
  74.7 4.7 %collective-permute-start.32 = (bf16[176,128]{1,0:T(8,128)(2,1)S(1)}, bf16[176,128]{1,0:T(8,128)(2,1)S(1)}, u32[]{:S(2)}, u32[]{:S(2)}) collective-permute-start(bf16[176,128]{1,0:T(8,128)(2,1)S(1)} %shard_map.136.refs_3_.mine), channel_id=1, source_target_pairs={{0,2},{1,3},{2,0},{3,1},{4,6},{5,7},{6,4},{7,5},{8,10},{9,11},{10,... | collective-permute-start | bytes 135176 | tf_op jit(solution)/shard_map/ppermute | solution.py:96
  76.2 3.2 %collective-permute-start.31 = (bf16[176,128]{1,0:T(8,128)(2,1)S(1)}, bf16[176,128]{1,0:T(8,128)(2,1)S(1)}, u32[]{:S(2)}, u32[]{:S(2)}) collective-permute-start(bf16[176,128]{1,0:T(8,128)(2,1)S(1)} %shard_map.136.refs_3_.mine), channel_id=1, source_target_pairs={{0,1},{1,0},{2,3},{3,2},{4,5},{5,4},{6,7},{7,6},{8,9},{9,8},{10,11... | collective-permute-start | bytes 135176 | tf_op jit(solution)/shard_map/ppermute | solution.py:96
  80.0 4.5 %collective-permute-start.34 = (f32[64,128]{1,0:T(8,128)S(1)}, f32[64,128]{1,0:T(8,128)S(1)}, u32[]{:S(2)}, u32[]{:S(2)}) collective-permute-start(f32[64,128]{1,0:T(8,128)S(1)} %shard_map.138), channel_id=1, source_target_pairs={{0,4},{4,0},{8,12},{12,8},{1,5},{5,1},{9,13},{13,9},{2,6},{6,2},{1... | collective-permute-start | bytes 98312 | tf_op jit(solution)/shard_map/ppermute | solution.py:96

commit v13 on v12

--- a/solution.py
+++ b/solution.py
@@ -445,14 +445,12 @@
 def grad_kernel(z, count, per_step, *refs):
     near_ids, right, later, mine = refs[:4]
     got = refs[4 : 4 + count]
-    out, left, sums, d0, ids, sem = refs[4 + count :]
+    out, left, sums, d0 = refs[4 + count :]
     n = z.batch
     deep = right.shape[1]
 
     @pl.when(pl.program_id(0) == 0)
     def _():
-        bring = pltpu.make_async_copy(near_ids, ids, sem)
-        bring.start()
         _, c = place()
         gather_post(z, c, mine, got, sums, d0)
         lanes = lax.broadcasted_iota(jnp.int32, (BLOCK, deep), 1)
@@ -463,9 +461,12 @@
             left[q] = jnp.where(lanes < n, turned, later[q].astype(F32)).astype(BF16)
 
         loop(2 * z.post, lay_left)
-        bring.wait()
-
-    products(z, pl.program_id(0) * per_step, per_step, ids, left, right, out)
+
+    for begin in range(0, z.slots, per_step):
+
+        @pl.when(pl.program_id(0) == begin // per_step)
+        def _(begin=begin):
+            products(z, begin, per_step, near_ids[...], left, right, out)
 
 
 def products(z, begin, count, ids, left, right, out):
@@ -519,7 +520,6 @@
         [],
         [message, weights],
     )
-    held_ids = [pltpu.SMEM((1, 2 * slots), jnp.int32), pltpu.SemaphoreType.DMA]
     if few(z.rows):
         partner_message = away(got, "row", z.rows, None, z.half)
     else:
@@ -650,7 +650,6 @@
             pltpu.VMEM(left_shape.shape, BF16),
             post_sums,
             pltpu.VMEM((2 * z.post, batch, BLOCK), BF16),
-            *held_ids,
         ],
         cost_estimate=cost,
         compiler_params=limit,

time: 85.3 us -> 85.2 us (level)
  no operation moved by 1% of the time
where the time goes in v13:
time: 85.2 us; the launch traced here: 85 us
  starting transfers between devices  38.3 us (45%)
  waiting for transfers between devices  32.1 us (38%)
  Pallas kernels  12.3 us (14%)
    ppermute x35, starting transfers between devices, flip(): return lax.ppermute(x, axis, [(i, i ^ k) for i in range(count)])  38.3 us
    ppermute x35, waiting for transfers between devices, flip(): return lax.ppermute(x, axis, [(i, i ^ k) for i in range(count)])  32.1 us
    pallas_call x17, Pallas kernels, call(): pl.pallas_call(body, out_shape=outs, in_specs=specs, out_specs=out_specs...  9.11 us
    pallas_call x1, Pallas kernels, shards(): pl.pallas_call(functools.partial(grad_kernel, z, len(got), per_step), gri...  3.2 us
  transfers between devices with their start and end apart: 35, of which 28 were waited for; matrix products, arithmetic and copies ran while one was open for 0% of the time, Pallas kernels for 7%

profile of v13, /device:TPU:0, one launch (start us, length us, event | category | flops | bytes accessed | tf_op | source)
XLA Modules:
  0.0 85.0 jit_solution(2372907857247148453)
XLA Ops:
  0.7 0.6 copy-done.6
  1.6 5.1 %collective-permute-start.2 = (bf16[96,128]{1,0:T(8,128)(2,1)S(1)}, bf16[96,128]{1,0:T(8,128)(2,1)S(1)}, u32[]{:S(2)}, u32[]{:S(2)}) collective-permute-start(bf16[96,128]{1,0:T(8,128)(2,1)S(1)} %get-tuple-element.59.after.refs_2_.refs_0_.mine), channel_id=1, source_target_pairs={{0,12},{4,8},{8,4},{12,0},{1,13},{5,9},{9,5},{13,1},{2,14},{6,10},... | collective-permute-start | bytes 73736 | tf_op jit(solution)/shard_map/ppermute | solution.py:96
  6.7 0.6 collective-permute-start
  7.3 1.0 %shard_map.123.refs_1_ = bf16[64,128,128]{2,1,0:T(8,128)(2,1)S(1)} custom-call(bf16[96,128]{1,0:T(8,128)(2,1)S(1)} %get-tuple-element.59.after.refs_2_.refs_0_.mine, bf16[64,128,128]{2,1,0:T(8,128)(2,1)S(1)} %bitcast.6), custom_call_target="tpu_custom_call" | custom-call | bytes 4218880 | tf_op jit(solution)/shard_map/pallas_call | solution.py:78
  8.5 2.0 %collective-permute-done.1.refs_4_.refs_6_ = bf16[96,128]{1,0:T(8,128)(2,1)S(1)} collective-permute-done((bf16[96,128]{1,0:T(8,128)(2,1)S(1)}, bf16[96,128]{1,0:T(8,128)(2,1)S(1)}, u32[]{:S(2)}, u32[]{:S(2)}) %collective-permute-start.1) | collective-permute-done | bytes 24608 | tf_op jit(solution)/shard_map/ppermute | solution.py:96
  10.5 0.9 %collective-permute-done.refs_3_.refs_5_.partner = bf16[96,128]{1,0:T(8,128)(2,1)S(1)} collective-permute-done((bf16[96,128]{1,0:T(8,128)(2,1)S(1)}, bf16[96,128]{1,0:T(8,128)(2,1)S(1)}, u32[]{:S(2)}, u32[]{:S(2)}) %collective-permute-start) | collective-permute-done | bytes 24608 | tf_op jit(solution)/shard_map/ppermute | solution.py:96
  11.4 1.1 %shard_map.124 = (bf16[9,32,128]{2,1,0:T(8,128)(2,1)S(1)}, f32[144,128]{1,0:T(8,128)S(1)}, bf16[144,128]{1,0:T(8,128)(2,1)S(1)}, bf16[144,128]{1,0:T(8,128)(2,1)S(1)}, bf16[144,128]{1,0:T(8,128)(2,1)S(1)}) custom-call(s32[1,128]{1,0:T(1,128)S(1)} %get-tuple-element.58.refs_0_, bf16[64,128,128]{2,1,0:T(8,128)(2,1)S(1)} %shard_map.123.refs_1_, ...), custom_call_target="tpu_custom_call" | custom-call | flops 67108864 | bytes 2454016 | tf_op jit(solution)/shard_map/pallas_call | solution.py:78
  12.6 1.6 %collective-permute-start.4 = (bf16[144,128]{1,0:T(8,128)(2,1)S(1)}, bf16[144,128]{1,0:T(8,128)(2,1)S(1)}, u32[]{:S(2)}, u32[]{:S(2)}) collective-permute-start(bf16[144,128]{1,0:T(8,128)(2,1)S(1)} %get-tuple-element.63), channel_id=1, source_target_pairs={{0,2},{1,3},{2,0},{3,1},{4,6},{5,7},{6,4},{7,5},{8,10},{9,11},{10,... | collective-permute-start | bytes 110600 | tf_op jit(solution)/shard_map/ppermute | solution.py:96
  14.4 1.9 %collective-permute-done.3.refs_1_ = bf16[144,128]{1,0:T(8,128)(2,1)S(1)} collective-permute-done((bf16[144,128]{1,0:T(8,128)(2,1)S(1)}, bf16[144,128]{1,0:T(8,128)(2,1)S(1)}, u32[]{:S(2)}, u32[]{:S(2)}) %collective-permute-start.3) | collective-permute-done | bytes 36896 | tf_op jit(solution)/shard_map/ppermute | solution.py:96
  16.3 0.4 collective-permute-done.4.refs_2_
  16.7 1.7 %collective-permute-start.8 = (bf16[144,128]{1,0:T(8,128)(2,1)S(1)}, bf16[144,128]{1,0:T(8,128)(2,1)S(1)}, u32[]{:S(2)}, u32[]{:S(2)}) collective-permute-start(bf16[144,128]{1,0:T(8,128)(2,1)S(1)} %get-tuple-element.70), channel_id=1, source_target_pairs={{0,12},{4,8},{8,4},{12,0},{1,13},{5,9},{9,5},{13,1},{2,14},{6,10},... | collective-permute-start | bytes 110600 | tf_op jit(solution)/shard_map/ppermute | solution.py:96
  18.5 0.4 collective-permute-start.7
  18.9 2.3 %collective-permute-start.6 = (bf16[144,128]{1,0:T(8,128)(2,1)S(1)}, bf16[144,128]{1,0:T(8,128)(2,1)S(1)}, u32[]{:S(2)}, u32[]{:S(2)}) collective-permute-start(bf16[144,128]{1,0:T(8,128)(2,1)S(1)} %get-tuple-element.70), channel_id=1, source_target_pairs={{0,8},{4,12},{8,0},{12,4},{1,9},{5,13},{9,1},{13,5},{2,10},{6,14},... | collective-permute-start | bytes 110600 | tf_op jit(solution)/shard_map/ppermute | solution.py:96
  21.2 0.9 %shard_map.126 = (f32[288,128]{1,0:T(8,128)S(1)}, f32[288,128]{1,0:T(8,128)S(1)}, f32[3,288,128]{2,1,0:T(8,128)S(1)}, f32[3,72,128]{2,1,0:T(8,128)S(1)}) custom-call(bf16[96,128]{1,0:T(8,128)(2,1)S(1)} %get-tuple-element.59.after.refs_2_.refs_0_.mine, f32[72,128]{1,0:T(8,128)S(1)} %get-tuple-element.66.refs_1_, f32[3,32,288]{2,1,0:T(8,128)S(1)} %copy-done.1, ...), custom_call_target="tpu_custom_call" | custom-call | bytes 1224704 | tf_op jit(solution)/shard_map/pallas_call | solution.py:78
  22.1 0.8 collective-permute-done.8.refs_8_
  23.1 0.7 collective-permute-done.6.refs_6_
  23.8 1.1 %shard_map.127 = (f32[288,128]{1,0:T(8,128)S(1)}, f32[144,128]{1,0:T(8,128)S(1)}, f32[144,128]{1,0:T(8,128)S(1)}, bf16[9,32,128]{2,1,0:T(8,128)(2,1)S(1)}, f32[1...) custom-call(s32[1,128]{1,0:T(1,128)S(1)} %get-tuple-element.58.refs_, ...), custom_call_target="tpu_custom_call" | custom-call | flops 67108864 | bytes 3572224 | tf_op jit(solution)/shard_map/pallas_call | solution.py:78
  24.9 0.5 collective-permute-start.9
  25.4 1.1 %collective-permute-start.10 = (bf16[144,128]{1,0:T(8,128)(2,1)S(1)}, bf16[144,128]{1,0:T(8,128)(2,1)S(1)}, u32[]{:S(2)}, u32[]{:S(2)}) collective-permute-start(bf16[144,128]{1,0:T(8,128)(2,1)S(1)} %get-tuple-element.74), channel_id=1, source_target_pairs={{0,2},{1,3},{2,0},{3,1},{4,6},{5,7},{6,4},{7,5},{8,10},{9,11},{10,... | collective-permute-start | bytes 110600 | tf_op jit(solution)/shard_map/ppermute | solution.py:96
  26.5 0.4 collective-permute-start.11
  26.8 1.9 %collective-permute-done.9.refs_1_ = bf16[144,128]{1,0:T(8,128)(2,1)S(1)} collective-permute-done((bf16[144,128]{1,0:T(8,128)(2,1)S(1)}, bf16[144,128]{1,0:T(8,128)(2,1)S(1)}, u32[]{:S(2)}, u32[]{:S(2)}) %collective-permute-start.9) | collective-permute-done | bytes 36896 | tf_op jit(solution)/shard_map/ppermute | solution.py:96
  28.8 0.9 %collective-permute-done.10.refs_2_ = bf16[144,128]{1,0:T(8,128)(2,1)S(1)} collective-permute-done((bf16[144,128]{1,0:T(8,128)(2,1)S(1)}, bf16[144,128]{1,0:T(8,128)(2,1)S(1)}, u32[]{:S(2)}, u32[]{:S(2)}) %collective-permute-start.10) | collective-permute-done | bytes 36896 | tf_op jit(solution)/shard_map/ppermute | solution.py:96
  29.7 2.3 %collective-permute-start.14 = (bf16[144,128]{1,0:T(8,128)(2,1)S(1)}, bf16[144,128]{1,0:T(8,128)(2,1)S(1)}, u32[]{:S(2)}, u32[]{:S(2)}) collective-permute-start(bf16[144,128]{1,0:T(8,128)(2,1)S(1)} %get-tuple-element.78), channel_id=1, source_target_pairs={{0,12},{4,8},{8,4},{12,0},{1,13},{5,9},{9,5},{13,1},{2,14},{6,10},... | collective-permute-start | bytes 110600 | tf_op jit(solution)/shard_map/ppermute | solution.py:96
  32.1 2.1 %collective-permute-start.12 = (bf16[144,128]{1,0:T(8,128)(2,1)S(1)}, bf16[144,128]{1,0:T(8,128)(2,1)S(1)}, u32[]{:S(2)}, u32[]{:S(2)}) collective-permute-start(bf16[144,128]{1,0:T(8,128)(2,1)S(1)} %get-tuple-element.78), channel_id=1, source_target_pairs={{0,8},{4,12},{8,0},{12,4},{1,9},{5,13},{9,1},{13,5},{2,10},{6,14},... | collective-permute-start | bytes 110600 | tf_op jit(solution)/shard_map/ppermute | solution.py:96
  34.2 1.4 %collective-permute-done.14.refs_8_ = bf16[144,128]{1,0:T(8,128)(2,1)S(1)} collective-permute-done((bf16[144,128]{1,0:T(8,128)(2,1)S(1)}, bf16[144,128]{1,0:T(8,128)(2,1)S(1)}, u32[]{:S(2)}, u32[]{:S(2)}) %collective-permute-start.14) | collective-permute-done | bytes 36896 | tf_op jit(solution)/shard_map/ppermute | solution.py:96
  35.5 0.8 collective-permute-done.13.refs_7_
  36.3 1.0 %collective-permute-done.12.refs_6_ = bf16[144,128]{1,0:T(8,128)(2,1)S(1)} collective-permute-done((bf16[144,128]{1,0:T(8,128)(2,1)S(1)}, bf16[144,128]{1,0:T(8,128)(2,1)S(1)}, u32[]{:S(2)}, u32[]{:S(2)}) %collective-permute-start.12) | collective-permute-done | bytes 36896 | tf_op jit(solution)/shard_map/ppermute | solution.py:96
  37.3 1.1 %shard_map.129 = (f32[288,128]{1,0:T(8,128)S(1)}, f32[144,128]{1,0:T(8,128)S(1)}, f32[144,128]{1,0:T(8,128)S(1)}, bf16[9,32,128]{2,1,0:T(8,128)(2,1)S(1)}, f32[1...) custom-call(s32[1,128]{1,0:T(1,128)S(1)} %get-tuple-element.58.refs_, ...), custom_call_target="tpu_custom_call" | custom-call | flops 67108864 | bytes 3572224 | tf_op jit(solution)/shard_map/pallas_call | solution.py:78
  38.5 1.3 %collective-permute-start.16 = (bf16[144,128]{1,0:T(8,128)(2,1)S(1)}, bf16[144,128]{1,0:T(8,128)(2,1)S(1)}, u32[]{:S(2)}, u32[]{:S(2)}) collective-permute-start(bf16[144,128]{1,0:T(8,128)(2,1)S(1)} %get-tuple-element.82), channel_id=1, source_target_pairs={{0,2},{1,3},{2,0},{3,1},{4,6},{5,7},{6,4},{7,5},{8,10},{9,11},{10,... | collective-permute-start | bytes 110600 | tf_op jit(solution)/shard_map/ppermute | solution.py:96
  39.8 0.5 collective-permute-start.17
  40.3 1.7 %collective-permute-done.15.refs_1_ = bf16[144,128]{1,0:T(8,128)(2,1)S(1)} collective-permute-done((bf16[144,128]{1,0:T(8,128)(2,1)S(1)}, bf16[144,128]{1,0:T(8,128)(2,1)S(1)}, u32[]{:S(2)}, u32[]{:S(2)}) %collective-permute-start.15) | collective-permute-done | bytes 36896 | tf_op jit(solution)/shard_map/ppermute | solution.py:96
  42.1 0.5 collective-permute-done.16.refs_2_
  42.6 2.1 %collective-permute-start.18 = (bf16[224,128]{1,0:T(8,128)(2,1)S(1)}, bf16[224,128]{1,0:T(8,128)(2,1)S(1)}, u32[]{:S(2)}, u32[]{:S(2)}) collective-permute-start(bf16[224,128]{1,0:T(8,128)(2,1)S(1)} %get-tuple-element.86), channel_id=1, source_target_pairs={{0,8},{4,12},{8,0},{12,4},{1,9},{5,13},{9,1},{13,5},{2,10},{6,14},... | collective-permute-start | bytes 172040 | tf_op jit(solution)/shard_map/ppermute | solution.py:96
  44.7 4.3 %collective-permute-done.18.theirs = bf16[224,128]{1,0:T(8,128)(2,1)S(1)} collective-permute-done((bf16[224,128]{1,0:T(8,128)(2,1)S(1)}, bf16[224,128]{1,0:T(8,128)(2,1)S(1)}, u32[]{:S(2)}, u32[]{:S(2)}) %collective-permute-start.18) | collective-permute-done | bytes 57376 | tf_op jit(solution)/shard_map/ppermute | solution.py:96
  49.1 1.5 %collective-permute-start.20 = (bf16[144,128]{1,0:T(8,128)(2,1)S(1)}, bf16[144,128]{1,0:T(8,128)(2,1)S(1)}, u32[]{:S(2)}, u32[]{:S(2)}) collective-permute-start(bf16[144,128]{1,0:T(8,128)(2,1)S(1)} %get-tuple-element.89.refs_3_), channel_id=1, source_target_pairs={{0,2},{1,3},{2,0},{3,1},{4,6},{5,7},{6,4},{7,5},{8,10},{9,11},{10,... | collective-permute-start | bytes 110600 | tf_op jit(solution)/shard_map/ppermute | solution.py:96
  50.6 0.3 collective-permute-start.19
  51.0 1.9 %collective-permute-done.21.refs_6_ = bf16[144,128]{1,0:T(8,128)(2,1)S(1)} collective-permute-done((bf16[144,128]{1,0:T(8,128)(2,1)S(1)}, bf16[144,128]{1,0:T(8,128)(2,1)S(1)}, u32[]{:S(2)}, u32[]{:S(2)}) %collective-permute-start.21) | collective-permute-done | bytes 36896 | tf_op jit(solution)/shard_map/ppermute | solution.py:96
  52.9 0.4 collective-permute-done.20.refs_5_
  53.3 1.1 %shard_map.132 = (bf16[18,32,128]{2,1,0:T(8,128)(2,1)S(1)}, f32[144,128]{1,0:T(8,128)S(1)}, bf16[144,128]{1,0:T(8,128)(2,1)S(1)}, bf16[144,128]{1,0:T(8,128)(2,1)S(1)}, bf16[144,128]{1,0:T(8,128)(2,1)S(1)}) custom-call(s32[1,128]{1,0:T(1,128)S(1)} %get-tuple-element.58.refs_0_, bf16[64,128,128]{2,1,0:T(8,128)(2,1)S(1)} %bitcast.7, ...), custom_call_target="tpu_custom_call" | custom-call | flops 67108864 | bytes 2613760 | tf_op jit(solution)/shard_map/pallas_call | solution.py:78
  54.3 2.0 %collective-permute-start.22 = (bf16[144,128]{1,0:T(8,128)(2,1)S(1)}, bf16[144,128]{1,0:T(8,128)(2,1)S(1)}, u32[]{:S(2)}, u32[]{:S(2)}) collective-permute-start(bf16[144,128]{1,0:T(8,128)(2,1)S(1)} %get-tuple-element.95), channel_id=1, source_target_pairs={{0,12},{4,8},{8,4},{12,0},{1,13},{5,9},{9,5},{13,1},{2,14},{6,10},... | collective-permute-start | bytes 110600 | tf_op jit(solution)/shard_map/ppermute | solution.py:96
  56.3 2.5 %collective-permute-start.24 = (bf16[144,128]{1,0:T(8,128)(2,1)S(1)}, bf16[144,128]{1,0:T(8,128)(2,1)S(1)}, u32[]{:S(2)}, u32[]{:S(2)}) collective-permute-start(bf16[144,128]{1,0:T(8,128)(2,1)S(1)} %get-tuple-element.97), channel_id=1, source_target_pairs={{0,8},{4,12},{8,0},{12,4},{1,9},{5,13},{9,1},{13,5},{2,10},{6,14},... | collective-permute-start | bytes 110600 | tf_op jit(solution)/shard_map/ppermute | solution.py:96
  58.8 1.5 %collective-permute-done.22.refs_0_ = bf16[144,128]{1,0:T(8,128)(2,1)S(1)} collective-permute-done((bf16[144,128]{1,0:T(8,128)(2,1)S(1)}, bf16[144,128]{1,0:T(8,128)(2,1)S(1)}, u32[]{:S(2)}, u32[]{:S(2)}) %collective-permute-start.22) | collective-permute-done | bytes 36896 | tf_op jit(solution)/shard_map/ppermute | solution.py:96
  60.3 0.6 collective-permute-done.23.refs_1_
  60.9 0.6 collective-permute-done.24.refs_2_
  61.7 1.2 %collective-permute-start.26 = (bf16[144,128]{1,0:T(8,128)(2,1)S(1)}, bf16[144,128]{1,0:T(8,128)(2,1)S(1)}, u32[]{:S(2)}, u32[]{:S(2)}) collective-permute-start(bf16[144,128]{1,0:T(8,128)(2,1)S(1)} %get-tuple-element.99.refs_3_), channel_id=1, source_target_pairs={{0,2},{1,3},{2,0},{3,1},{4,6},{5,7},{6,4},{7,5},{8,10},{9,11},{10,... | collective-permute-start | bytes 110600 | tf_op jit(solution)/shard_map/ppermute | solution.py:96
  62.9 0.6 collective-permute-start.25
  63.5 1.6 %collective-permute-done.27.refs_6_ = bf16[144,128]{1,0:T(8,128)(2,1)S(1)} collective-permute-done((bf16[144,128]{1,0:T(8,128)(2,1)S(1)}, bf16[144,128]{1,0:T(8,128)(2,1)S(1)}, u32[]{:S(2)}, u32[]{:S(2)}) %collective-permute-start.27) | collective-permute-done | bytes 36896 | tf_op jit(solution)/shard_map/ppermute | solution.py:96
  65.2 0.7 collective-permute-done.26.refs_5_
  65.9 1.1 %shard_map.134 = (bf16[18,32,128]{2,1,0:T(8,128)(2,1)S(1)}, f32[144,128]{1,0:T(8,128)S(1)}, bf16[144,128]{1,0:T(8,128)(2,1)S(1)}, bf16[144,128]{1,0:T(8,128)(2,1)S(1)}, bf16[144,128]{1,0:T(8,128)(2,1)S(1)}) custom-call(s32[1,128]{1,0:T(1,128)S(1)} %get-tuple-element.58.refs_0_, bf16[64,128,128]{2,1,0:T(8,128)(2,1)S(1)} %bitcast.8, ...), custom_call_target="tpu_custom_call" | custom-call | flops 67108864 | bytes 2613760 | tf_op jit(solution)/shard_map/pallas_call | solution.py:78
  66.9 1.9 %collective-permute-start.28 = (bf16[144,128]{1,0:T(8,128)(2,1)S(1)}, bf16[144,128]{1,0:T(8,128)(2,1)S(1)}, u32[]{:S(2)}, u32[]{:S(2)}) collective-permute-start(bf16[144,128]{1,0:T(8,128)(2,1)S(1)} %get-tuple-element.110), channel_id=1, source_target_pairs={{0,12},{4,8},{8,4},{12,0},{1,13},{5,9},{9,5},{13,1},{2,14},{6,10},... | collective-permute-start | bytes 110600 | tf_op jit(solution)/shard_map/ppermute | solution.py:96
  68.8 0.8 collective-permute-start.29
  69.6 1.8 %collective-permute-start.30 = (bf16[144,128]{1,0:T(8,128)(2,1)S(1)}, bf16[144,128]{1,0:T(8,128)(2,1)S(1)}, u32[]{:S(2)}, u32[]{:S(2)}) collective-permute-start(bf16[144,128]{1,0:T(8,128)(2,1)S(1)} %get-tuple-element.112), channel_id=1, source_target_pairs={{0,8},{4,12},{8,0},{12,4},{1,9},{5,13},{9,1},{13,5},{2,10},{6,14},... | collective-permute-start | bytes 110600 | tf_op jit(solution)/shard_map/ppermute | solution.py:96
  71.4 1.4 %collective-permute-done.28.refs_0_ = bf16[144,128]{1,0:T(8,128)(2,1)S(1)} collective-permute-done((bf16[144,128]{1,0:T(8,128)(2,1)S(1)}, bf16[144,128]{1,0:T(8,128)(2,1)S(1)}, u32[]{:S(2)}, u32[]{:S(2)}) %collective-permute-start.28) | collective-permute-done | bytes 36896 | tf_op jit(solution)/shard_map/ppermute | solution.py:96
  72.8 0.8 collective-permute-done.29.refs_1_
  73.6 0.9 %collective-permute-done.30.refs_2_ = bf16[144,128]{1,0:T(8,128)(2,1)S(1)} collective-permute-done((bf16[144,128]{1,0:T(8,128)(2,1)S(1)}, bf16[144,128]{1,0:T(8,128)(2,1)S(1)}, u32[]{:S(2)}, u32[]{:S(2)}) %collective-permute-start.30) | collective-permute-done | bytes 36896 | tf_op jit(solution)/shard_map/ppermute | solution.py:96
  74.7 1.5 %collective-permute-start.32 = (bf16[176,128]{1,0:T(8,128)(2,1)S(1)}, bf16[176,128]{1,0:T(8,128)(2,1)S(1)}, u32[]{:S(2)}, u32[]{:S(2)}) collective-permute-start(bf16[176,128]{1,0:T(8,128)(2,1)S(1)} %shard_map.136.refs_3_.mine), channel_id=1, source_target_pairs={{0,2},{1,3},{2,0},{3,1},{4,6},{5,7},{6,4},{7,5},{8,10},{9,11},{10,... | collective-permute-start | bytes 135176 | tf_op jit(solution)/shard_map/ppermute | solution.py:96
  76.2 0.3 collective-permute-start.31
  76.5 0.8 shard_map.135
  77.4 1.3 %collective-permute-done.33.refs_6_.refs_2_ = bf16[176,128]{1,0:T(8,128)(2,1)S(1)} collective-permute-done((bf16[176,128]{1,0:T(8,128)(2,1)S(1)}, bf16[176,128]{1,0:T(8,128)(2,1)S(1)}, u32[]{:S(2)}, u32[]{:S(2)}) %collective-permute-start.33) | collective-permute-done | bytes 45088 | tf_op jit(solution)/shard_map/ppermute | solution.py:96
  78.6 0.7 collective-permute-done.32.refs_5_.refs_1_
  79.4 0.6 shard_map.138
  80.0 1.2 %collective-permute-start.34 = (f32[64,128]{1,0:T(8,128)S(1)}, f32[64,128]{1,0:T(8,128)S(1)}, u32[]{:S(2)}, u32[]{:S(2)}) collective-permute-start(f32[64,128]{1,0:T(8,128)S(1)} %shard_map.138), channel_id=1, source_target_pairs={{0,4},{4,0},{8,12},{12,8},{1,5},{5,1},{9,13},{13,9},{2,6},{6,2},{1... | collective-permute-start | bytes 98312 | tf_op jit(solution)/shard_map/ppermute | solution.py:96
  81.2 3.2 %shard_map.137 = bf16[64,128,128]{2,1,0:T(8,128)(2,1)} custom-call(s32[1,128]{1,0:T(1,128)S(1)} %get-tuple-element.58.refs_0_, bf16[9,128,128]{2,1,0:T(8,128)(2,1)S(1)} %get-tuple-element.104.refs_1_.right, bf16[18,128,128]{2,1,0:T(8,128)(2,1)S(1)} %get-tuple-element.105.refs_2_, bf16[176,128]{1,0:T(8,128)(2,1)S(1)} %shard_map.136.refs_3_.mine, ...), custom_call_target="tpu_custom_call" | custom-call | flops 268435456 | bytes 4194304 | tf_op jit(solution)/shard_map/pallas_call | solution.py:643
  84.4 0.6 add_bitcast_fusion
  (45 shorter events, 1.6 us)
Async XLA Ops:
  0.6 0.7 copy-start.6
  0.6 0.7 copy-start.5
  0.7 0.7 copy-start.9
  0.7 0.7 copy-start.8
  0.7 0.7 copy-start.7
  0.7 0.8 copy-start.3
  0.7 6.6 %copy-start = (bf16[1,1,64,128,128]{4,3,2,1,0:T(8,128)(2,1)S(1)}, bf16[1,1,64,128,128]{4,3,2,1,0:T(8,128)(2,1)}, u32[]{:S(2)}) copy-start(bf16[1,1,64,128,128]{4,3,2,1,0:T(8,128)(2,1)} %param.13) | copy-start | bytes 6291460
  1.6 6.9 %collective-permute-start.2 = (bf16[96,128]{1,0:T(8,128)(2,1)S(1)}, bf16[96,128]{1,0:T(8,128)(2,1)S(1)}, u32[]{:S(2)}, u32[]{:S(2)}) collective-permute-start(bf16[96,128]{1,0:T(8,128)(2,1)S(1)} %get-tuple-element.59.after.refs_2_.refs_0_.mine), channel_id=1, source_target_pairs={{0,12},{4,8},{8,4},{12,0},{1,13},{5,9},{9,5},{13,1},{2,14},{6,10},... | collective-permute-start | bytes 73736 | tf_op jit(solution)/shard_map/ppermute | solution.py:96
  6.6 3.8 %collective-permute-start.1 = (bf16[96,128]{1,0:T(8,128)(2,1)S(1)}, bf16[96,128]{1,0:T(8,128)(2,1)S(1)}, u32[]{:S(2)}, u32[]{:S(2)}) collective-permute-start(bf16[96,128]{1,0:T(8,128)(2,1)S(1)} %get-tuple-element.59.after.refs_2_.refs_0_.mine), channel_id=1, source_target_pairs={{0,4},{4,0},{8,12},{12,8},{1,5},{5,1},{9,13},{13,9},{2,6},{6,2},{1... | collective-permute-start | bytes 73736 | tf_op jit(solution)/shard_map/ppermute | solution.py:96
  6.7 4.8 %collective-permute-start = (bf16[96,128]{1,0:T(8,128)(2,1)S(1)}, bf16[96,128]{1,0:T(8,128)(2,1)S(1)}, u32[]{:S(2)}, u32[]{:S(2)}) collective-permute-start(bf16[96,128]{1,0:T(8,128)(2,1)S(1)} %get-tuple-element.59.after.refs_2_.refs_0_.mine), channel_id=1, source_target_pairs={{0,8},{4,12},{8,0},{12,4},{1,9},{5,13},{9,1},{13,5},{2,10},{6,14},... | collective-permute-start | bytes 73736 | tf_op jit(solution)/shard_map/ppermute | solution.py:96
  8.3 12.9 %copy-start.1 = (f32[3,32,288]{2,1,0:T(8,128)S(1)}, f32[3,32,288]{2,1,0:T(8,128)}, u32[]{:S(2)}) copy-start(f32[3,32,288]{2,1,0:T(8,128)} %refs_2_.1) | copy-start | bytes 331780
  8.3 12.9 %copy-start.2 = (bf16[3,32,512]{2,1,0:T(8,128)(2,1)S(1)}, bf16[3,32,512]{2,1,0:T(8,128)(2,1)}, u32[]{:S(2)}) copy-start(bf16[3,32,512]{2,1,0:T(8,128)(2,1)} %param.11) | copy-start | bytes 294916
  8.3 12.9 %copy-start.4 = (f32[8192]{0:T(1024)S(1)}, f32[8192]{0:T(1024)}, u32[]{:S(2)}) copy-start(f32[8192]{0:T(1024)} %param.18) | copy-start | bytes 98308
  12.5 3.8 %collective-permute-start.3 = (bf16[144,128]{1,0:T(8,128)(2,1)S(1)}, bf16[144,128]{1,0:T(8,128)(2,1)S(1)}, u32[]{:S(2)}, u32[]{:S(2)}) collective-permute-start(bf16[144,128]{1,0:T(8,128)(2,1)S(1)} %get-tuple-element.62), channel_id=1, source_target_pairs={{0,3},{1,2},{2,1},{3,0},{4,7},{5,6},{6,5},{7,4},{8,11},{9,10},{10,... | collective-permute-start | bytes 110600 | tf_op jit(solution)/shard_map/ppermute | solution.py:96
  12.6 4.2 %collective-permute-start.4 = (bf16[144,128]{1,0:T(8,128)(2,1)S(1)}, bf16[144,128]{1,0:T(8,128)(2,1)S(1)}, u32[]{:S(2)}, u32[]{:S(2)}) collective-permute-start(bf16[144,128]{1,0:T(8,128)(2,1)S(1)} %get-tuple-element.63), channel_id=1, source_target_pairs={{0,2},{1,3},{2,0},{3,1},{4,6},{5,7},{6,4},{7,5},{8,10},{9,11},{10,... | collective-permute-start | bytes 110600 | tf_op jit(solution)/shard_map/ppermute | solution.py:96
  14.1 2.6 %collective-permute-start.5 = (bf16[144,128]{1,0:T(8,128)(2,1)S(1)}, bf16[144,128]{1,0:T(8,128)(2,1)S(1)}, u32[]{:S(2)}, u32[]{:S(2)}) collective-permute-start(bf16[144,128]{1,0:T(8,128)(2,1)S(1)} %get-tuple-element.64), channel_id=1, source_target_pairs={{0,1},{1,0},{2,3},{3,2},{4,5},{5,4},{6,7},{7,6},{8,9},{9,8},{10,11... | collective-permute-start | bytes 110600 | tf_op jit(solution)/shard_map/ppermute | solution.py:96
  16.7 6.2 %collective-permute-start.8 = (bf16[144,128]{1,0:T(8,128)(2,1)S(1)}, bf16[144,128]{1,0:T(8,128)(2,1)S(1)}, u32[]{:S(2)}, u32[]{:S(2)}) collective-permute-start(bf16[144,128]{1,0:T(8,128)(2,1)S(1)} %get-tuple-element.70), channel_id=1, source_target_pairs={{0,12},{4,8},{8,4},{12,0},{1,13},{5,9},{9,5},{13,1},{2,14},{6,10},... | collective-permute-start | bytes 110600 | tf_op jit(solution)/shard_map/ppermute | solution.py:96
  18.5 4.7 %collective-permute-start.7 = (bf16[144,128]{1,0:T(8,128)(2,1)S(1)}, bf16[144,128]{1,0:T(8,128)(2,1)S(1)}, u32[]{:S(2)}, u32[]{:S(2)}) collective-permute-start(bf16[144,128]{1,0:T(8,128)(2,1)S(1)} %get-tuple-element.70), channel_id=1, source_target_pairs={{0,4},{4,0},{8,12},{12,8},{1,5},{5,1},{9,13},{13,9},{2,6},{6,2},{1... | collective-permute-start | bytes 110600 | tf_op jit(solution)/shard_map/ppermute | solution.py:96
  18.9 5.0 %collective-permute-start.6 = (bf16[144,128]{1,0:T(8,128)(2,1)S(1)}, bf16[144,128]{1,0:T(8,128)(2,1)S(1)}, u32[]{:S(2)}, u32[]{:S(2)}) collective-permute-start(bf16[144,128]{1,0:T(8,128)(2,1)S(1)} %get-tuple-element.70), channel_id=1, source_target_pairs={{0,8},{4,12},{8,0},{12,4},{1,9},{5,13},{9,1},{13,5},{2,10},{6,14},... | collective-permute-start | bytes 110600 | tf_op jit(solution)/shard_map/ppermute | solution.py:96
  24.9 3.8 %collective-permute-start.9 = (bf16[144,128]{1,0:T(8,128)(2,1)S(1)}, bf16[144,128]{1,0:T(8,128)(2,1)S(1)}, u32[]{:S(2)}, u32[]{:S(2)}) collective-permute-start(bf16[144,128]{1,0:T(8,128)(2,1)S(1)} %get-tuple-element.73), channel_id=1, source_target_pairs={{0,3},{1,2},{2,1},{3,0},{4,7},{5,6},{6,5},{7,4},{8,11},{9,10},{10,... | collective-permute-start | bytes 110600 | tf_op jit(solution)/shard_map/ppermute | solution.py:96
  25.4 4.2 %collective-permute-start.10 = (bf16[144,128]{1,0:T(8,128)(2,1)S(1)}, bf16[144,128]{1,0:T(8,128)(2,1)S(1)}, u32[]{:S(2)}, u32[]{:S(2)}) collective-permute-start(bf16[144,128]{1,0:T(8,128)(2,1)S(1)} %get-tuple-element.74), channel_id=1, source_target_pairs={{0,2},{1,3},{2,0},{3,1},{4,6},{5,7},{6,4},{7,5},{8,10},{9,11},{10,... | collective-permute-start | bytes 110600 | tf_op jit(solution)/shard_map/ppermute | solution.py:96
  26.5 3.2 %collective-permute-start.11 = (bf16[144,128]{1,0:T(8,128)(2,1)S(1)}, bf16[144,128]{1,0:T(8,128)(2,1)S(1)}, u32[]{:S(2)}, u32[]{:S(2)}) collective-permute-start(bf16[144,128]{1,0:T(8,128)(2,1)S(1)} %get-tuple-element.75), channel_id=1, source_target_pairs={{0,1},{1,0},{2,3},{3,2},{4,5},{5,4},{6,7},{7,6},{8,9},{9,8},{10,11... | collective-permute-start | bytes 110600 | tf_op jit(solution)/shard_map/ppermute | solution.py:96
  29.7 5.8 %collective-permute-start.14 = (bf16[144,128]{1,0:T(8,128)(2,1)S(1)}, bf16[144,128]{1,0:T(8,128)(2,1)S(1)}, u32[]{:S(2)}, u32[]{:S(2)}) collective-permute-start(bf16[144,128]{1,0:T(8,128)(2,1)S(1)} %get-tuple-element.78), channel_id=1, source_target_pairs={{0,12},{4,8},{8,4},{12,0},{1,13},{5,9},{9,5},{13,1},{2,14},{6,10},... | collective-permute-start | bytes 110600 | tf_op jit(solution)/shard_map/ppermute | solution.py:96
  32.0 4.3 %collective-permute-start.13 = (bf16[144,128]{1,0:T(8,128)(2,1)S(1)}, bf16[144,128]{1,0:T(8,128)(2,1)S(1)}, u32[]{:S(2)}, u32[]{:S(2)}) collective-permute-start(bf16[144,128]{1,0:T(8,128)(2,1)S(1)} %get-tuple-element.78), channel_id=1, source_target_pairs={{0,4},{4,0},{8,12},{12,8},{1,5},{5,1},{9,13},{13,9},{2,6},{6,2},{1... | collective-permute-start | bytes 110600 | tf_op jit(solution)/shard_map/ppermute | solution.py:96
  32.1 5.3 %collective-permute-start.12 = (bf16[144,128]{1,0:T(8,128)(2,1)S(1)}, bf16[144,128]{1,0:T(8,128)(2,1)S(1)}, u32[]{:S(2)}, u32[]{:S(2)}) collective-permute-start(bf16[144,128]{1,0:T(8,128)(2,1)S(1)} %get-tuple-element.78), channel_id=1, source_target_pairs={{0,8},{4,12},{8,0},{12,4},{1,9},{5,13},{9,1},{13,5},{2,10},{6,14},... | collective-permute-start | bytes 110600 | tf_op jit(solution)/shard_map/ppermute | solution.py:96
  38.4 3.7 %collective-permute-start.15 = (bf16[144,128]{1,0:T(8,128)(2,1)S(1)}, bf16[144,128]{1,0:T(8,128)(2,1)S(1)}, u32[]{:S(2)}, u32[]{:S(2)}) collective-permute-start(bf16[144,128]{1,0:T(8,128)(2,1)S(1)} %get-tuple-element.81), channel_id=1, source_target_pairs={{0,3},{1,2},{2,1},{3,0},{4,7},{5,6},{6,5},{7,4},{8,11},{9,10},{10,... | collective-permute-start | bytes 110600 | tf_op jit(solution)/shard_map/ppermute | solution.py:96
  38.5 4.1 %collective-permute-start.16 = (bf16[144,128]{1,0:T(8,128)(2,1)S(1)}, bf16[144,128]{1,0:T(8,128)(2,1)S(1)}, u32[]{:S(2)}, u32[]{:S(2)}) collective-permute-start(bf16[144,128]{1,0:T(8,128)(2,1)S(1)} %get-tuple-element.82), channel_id=1, source_target_pairs={{0,2},{1,3},{2,0},{3,1},{4,6},{5,7},{6,4},{7,5},{8,10},{9,11},{10,... | collective-permute-start | bytes 110600 | tf_op jit(solution)/shard_map/ppermute | solution.py:96
  39.8 2.7 %collective-permute-start.17 = (bf16[144,128]{1,0:T(8,128)(2,1)S(1)}, bf16[144,128]{1,0:T(8,128)(2,1)S(1)}, u32[]{:S(2)}, u32[]{:S(2)}) collective-permute-start(bf16[144,128]{1,0:T(8,128)(2,1)S(1)} %get-tuple-element.83), channel_id=1, source_target_pairs={{0,1},{1,0},{2,3},{3,2},{4,5},{5,4},{6,7},{7,6},{8,9},{9,8},{10,11... | collective-permute-start | bytes 110600 | tf_op jit(solution)/shard_map/ppermute | solution.py:96
  42.6 6.4 %collective-permute-start.18 = (bf16[224,128]{1,0:T(8,128)(2,1)S(1)}, bf16[224,128]{1,0:T(8,128)(2,1)S(1)}, u32[]{:S(2)}, u32[]{:S(2)}) collective-permute-start(bf16[224,128]{1,0:T(8,128)(2,1)S(1)} %get-tuple-element.86), channel_id=1, source_target_pairs={{0,8},{4,12},{8,0},{12,4},{1,9},{5,13},{9,1},{13,5},{2,10},{6,14},... | collective-permute-start | bytes 172040 | tf_op jit(solution)/shard_map/ppermute | solution.py:96
  49.0 3.8 %collective-permute-start.21 = (bf16[144,128]{1,0:T(8,128)(2,1)S(1)}, bf16[144,128]{1,0:T(8,128)(2,1)S(1)}, u32[]{:S(2)}, u32[]{:S(2)}) collective-permute-start(bf16[144,128]{1,0:T(8,128)(2,1)S(1)} %get-tuple-element.89.refs_3_), channel_id=1, source_target_pairs={{0,3},{1,2},{2,1},{3,0},{4,7},{5,6},{6,5},{7,4},{8,11},{9,10},{10,... | collective-permute-start | bytes 110600 | tf_op jit(solution)/shard_map/ppermute | solution.py:96
  49.1 4.1 %collective-permute-start.20 = (bf16[144,128]{1,0:T(8,128)(2,1)S(1)}, bf16[144,128]{1,0:T(8,128)(2,1)S(1)}, u32[]{:S(2)}, u32[]{:S(2)}) collective-permute-start(bf16[144,128]{1,0:T(8,128)(2,1)S(1)} %get-tuple-element.89.refs_3_), channel_id=1, source_target_pairs={{0,2},{1,3},{2,0},{3,1},{4,6},{5,7},{6,4},{7,5},{8,10},{9,11},{10,... | collective-permute-start | bytes 110600 | tf_op jit(solution)/shard_map/ppermute | solution.py:96
  50.6 2.7 %collective-permute-start.19 = (bf16[144,128]{1,0:T(8,128)(2,1)S(1)}, bf16[144,128]{1,0:T(8,128)(2,1)S(1)}, u32[]{:S(2)}, u32[]{:S(2)}) collective-permute-start(bf16[144,128]{1,0:T(8,128)(2,1)S(1)} %get-tuple-element.89.refs_3_), channel_id=1, source_target_pairs={{0,1},{1,0},{2,3},{3,2},{4,5},{5,4},{6,7},{7,6},{8,9},{9,8},{10,11... | collective-permute-start | bytes 110600 | tf_op jit(solution)/shard_map/ppermute | solution.py:96
  54.3 6.0 %collective-permute-start.22 = (bf16[144,128]{1,0:T(8,128)(2,1)S(1)}, bf16[144,128]{1,0:T(8,128)(2,1)S(1)}, u32[]{:S(2)}, u32[]{:S(2)}) collective-permute-start(bf16[144,128]{1,0:T(8,128)(2,1)S(1)} %get-tuple-element.95), channel_id=1, source_target_pairs={{0,12},{4,8},{8,4},{12,0},{1,13},{5,9},{9,5},{13,1},{2,14},{6,10},... | collective-permute-start | bytes 110600 | tf_op jit(solution)/shard_map/ppermute | solution.py:96
  56.3 4.6 %collective-permute-start.23 = (bf16[144,128]{1,0:T(8,128)(2,1)S(1)}, bf16[144,128]{1,0:T(8,128)(2,1)S(1)}, u32[]{:S(2)}, u32[]{:S(2)}) collective-permute-start(bf16[144,128]{1,0:T(8,128)(2,1)S(1)} %get-tuple-element.96), channel_id=1, source_target_pairs={{0,4},{4,0},{8,12},{12,8},{1,5},{5,1},{9,13},{13,9},{2,6},{6,2},{1... | collective-permute-start | bytes 110600 | tf_op jit(solution)/shard_map/ppermute | solution.py:96
  56.3 5.3 %collective-permute-start.24 = (bf16[144,128]{1,0:T(8,128)(2,1)S(1)}, bf16[144,128]{1,0:T(8,128)(2,1)S(1)}, u32[]{:S(2)}, u32[]{:S(2)}) collective-permute-start(bf16[144,128]{1,0:T(8,128)(2,1)S(1)} %get-tuple-element.97), channel_id=1, source_target_pairs={{0,8},{4,12},{8,0},{12,4},{1,9},{5,13},{9,1},{13,5},{2,10},{6,14},... | collective-permute-start | bytes 110600 | tf_op jit(solution)/shard_map/ppermute | solution.py:96
  61.6 3.6 %collective-permute-start.27 = (bf16[144,128]{1,0:T(8,128)(2,1)S(1)}, bf16[144,128]{1,0:T(8,128)(2,1)S(1)}, u32[]{:S(2)}, u32[]{:S(2)}) collective-permute-start(bf16[144,128]{1,0:T(8,128)(2,1)S(1)} %get-tuple-element.99.refs_3_), channel_id=1, source_target_pairs={{0,3},{1,2},{2,1},{3,0},{4,7},{5,6},{6,5},{7,4},{8,11},{9,10},{10,... | collective-permute-start | bytes 110600 | tf_op jit(solution)/shard_map/ppermute | solution.py:96
  61.7 4.2 %collective-permute-start.26 = (bf16[144,128]{1,0:T(8,128)(2,1)S(1)}, bf16[144,128]{1,0:T(8,128)(2,1)S(1)}, u32[]{:S(2)}, u32[]{:S(2)}) collective-permute-start(bf16[144,128]{1,0:T(8,128)(2,1)S(1)} %get-tuple-element.99.refs_3_), channel_id=1, source_target_pairs={{0,2},{1,3},{2,0},{3,1},{4,6},{5,7},{6,4},{7,5},{8,10},{9,11},{10,... | collective-permute-start | bytes 110600 | tf_op jit(solution)/shard_map/ppermute | solution.py:96
  62.9 3.0 %collective-permute-start.25 = (bf16[144,128]{1,0:T(8,128)(2,1)S(1)}, bf16[144,128]{1,0:T(8,128)(2,1)S(1)}, u32[]{:S(2)}, u32[]{:S(2)}) collective-permute-start(bf16[144,128]{1,0:T(8,128)(2,1)S(1)} %get-tuple-element.99.refs_3_), channel_id=1, source_target_pairs={{0,1},{1,0},{2,3},{3,2},{4,5},{5,4},{6,7},{7,6},{8,9},{9,8},{10,11... | collective-permute-start | bytes 110600 | tf_op jit(solution)/shard_map/ppermute | solution.py:96
  66.9 5.9 %collective-permute-start.28 = (bf16[144,128]{1,0:T(8,128)(2,1)S(1)}, bf16[144,128]{1,0:T(8,128)(2,1)S(1)}, u32[]{:S(2)}, u32[]{:S(2)}) collective-permute-start(bf16[144,128]{1,0:T(8,128)(2,1)S(1)} %get-tuple-element.110), channel_id=1, source_target_pairs={{0,12},{4,8},{8,4},{12,0},{1,13},{5,9},{9,5},{13,1},{2,14},{6,10},... | collective-permute-start | bytes 110600 | tf_op jit(solution)/shard_map/ppermute | solution.py:96
  68.8 4.7 %collective-permute-start.29 = (bf16[144,128]{1,0:T(8,128)(2,1)S(1)}, bf16[144,128]{1,0:T(8,128)(2,1)S(1)}, u32[]{:S(2)}, u32[]{:S(2)}) collective-permute-start(bf16[144,128]{1,0:T(8,128)(2,1)S(1)} %get-tuple-element.111), channel_id=1, source_target_pairs={{0,4},{4,0},{8,12},{12,8},{1,5},{5,1},{9,13},{13,9},{2,6},{6,2},{1... | collective-permute-start | bytes 110600 | tf_op jit(solution)/shard_map/ppermute | solution.py:96
  69.6 4.9 %collective-permute-start.30 = (bf16[144,128]{1,0:T(8,128)(2,1)S(1)}, bf16[144,128]{1,0:T(8,128)(2,1)S(1)}, u32[]{:S(2)}, u32[]{:S(2)}) collective-permute-start(bf16[144,128]{1,0:T(8,128)(2,1)S(1)} %get-tuple-element.112), channel_id=1, source_target_pairs={{0,8},{4,12},{8,0},{12,4},{1,9},{5,13},{9,1},{13,5},{2,10},{6,14},... | collective-permute-start | bytes 110600 | tf_op jit(solution)/shard_map/ppermute | solution.py:96
  74.6 4.0 %collective-permute-start.33 = (bf16[176,128]{1,0:T(8,128)(2,1)S(1)}, bf16[176,128]{1,0:T(8,128)(2,1)S(1)}, u32[]{:S(2)}, u32[]{:S(2)}) collective-permute-start(bf16[176,128]{1,0:T(8,128)(2,1)S(1)} %shard_map.136.refs_3_.mine), channel_id=1, source_target_pairs={{0,3},{1,2},{2,1},{3,0},{4,7},{5,6},{6,5},{7,4},{8,11},{9,10},{10,... | collective-permute-start | bytes 135176 | tf_op jit(solution)/shard_map/ppermute | solution.py:96
  74.7 4.7 %collective-permute-start.32 = (bf16[176,128]{1,0:T(8,128)(2,1)S(1)}, bf16[176,128]{1,0:T(8,128)(2,1)S(1)}, u32[]{:S(2)}, u32[]{:S(2)}) collective-permute-start(bf16[176,128]{1,0:T(8,128)(2,1)S(1)} %shard_map.136.refs_3_.mine), channel_id=1, source_target_pairs={{0,2},{1,3},{2,0},{3,1},{4,6},{5,7},{6,4},{7,5},{8,10},{9,11},{10,... | collective-permute-start | bytes 135176 | tf_op jit(solution)/shard_map/ppermute | solution.py:96
  76.2 3.2 %collective-permute-start.31 = (bf16[176,128]{1,0:T(8,128)(2,1)S(1)}, bf16[176,128]{1,0:T(8,128)(2,1)S(1)}, u32[]{:S(2)}, u32[]{:S(2)}) collective-permute-start(bf16[176,128]{1,0:T(8,128)(2,1)S(1)} %shard_map.136.refs_3_.mine), channel_id=1, source_target_pairs={{0,1},{1,0},{2,3},{3,2},{4,5},{5,4},{6,7},{7,6},{8,9},{9,8},{10,11... | collective-permute-start | bytes 135176 | tf_op jit(solution)/shard_map/ppermute | solution.py:96
  80.0 4.4 %collective-permute-start.34 = (f32[64,128]{1,0:T(8,128)S(1)}, f32[64,128]{1,0:T(8,128)S(1)}, u32[]{:S(2)}, u32[]{:S(2)}) collective-permute-start(f32[64,128]{1,0:T(8,128)S(1)} %shard_map.138), channel_id=1, source_target_pairs={{0,4},{4,0},{8,12},{12,8},{1,5},{5,1},{9,13},{13,9},{2,6},{6,2},{1... | collective-permute-start | bytes 98312 | tf_op jit(solution)/shard_map/ppermute | solution.py:96
